TPU v7x, 32 devices: a whole 2x2x4 slice. The times are simulated.
32 devices in a mesh: groups: 2 (over x), blk: 16 (over z, y, core).
Axes of the slice: x: 2, y: 2, z: 4, core: 2. Of those that a mesh axis runs over, the one named last changes fastest.
Arguments:
- plus_start: bfloat16 [32, 512, 2048], P('groups', 'blk'), parts along dimension 0, may hold values from -6 to 6
- reflection: bfloat16 [2, 32, 2048, 2048], P(None, None, 'blk'), may hold values from -0.125 to 0.125
- onset_times: int32 [32, 2048], P('groups'), parts along dimension 0, may hold values from 128 to 511
Outputs:
- upgoing: bfloat16 [32, 512, 2048], P('groups', 'blk'), parts along dimension 0
- downgoing: bfloat16 [32, 512, 2048], P('groups', 'blk'), parts along dimension 0
There are 2 independent parts, one for each index of `groups`. A program takes and returns all parts, laid end to end along the dimension named above; an argument that names none is the same for every part. Nothing has to cross between parts.
All inputs are finite; a program needn't handle non-finite values.
Results may differ from a plain program's by a relative error of at most 0.035.
Values may be sent and summed in bfloat16 or wider, within the bound.
No kernel may reach another device: no remote copies, remote signals or barrier semaphores. Data moves between devices by JAX's collectives and lax.ppermute only.
A program may use at most 192 MiB of HBM per device.

v0:
```python
import math

import jax
import jax.numpy as jnp
from jax import lax
from jax.sharding import PartitionSpec as P

NT = 512
NFW = 32
FREQ0 = 16
ITERS = 2


def make_tables():
    freqs = FREQ0 + jnp.arange(NFW, dtype=jnp.int32)
    samples = jnp.arange(NT, dtype=jnp.int32)
    turns = freqs[:, None] * samples[None, :] % NT
    phase = turns.astype(jnp.float32) * (2.0 * math.pi / NT)
    basis = jnp.concatenate([jnp.cos(phase), -jnp.sin(phase)], axis=0)
    forward = (basis * (1.0 / math.sqrt(NT))).astype(jnp.bfloat16)
    inverse = (basis * math.sqrt(2.0 / NFW)).astype(jnp.bfloat16)
    return (forward, inverse)


def analyze(field, forward):
    total = jnp.einsum("kt,ptx->kpx", forward, field, preferred_element_type=jnp.float32)
    return total.reshape(2, NFW, field.shape[0], field.shape[2]).astype(jnp.bfloat16)


def synthesize(spectrum, inverse):
    flat = spectrum.reshape(2 * NFW, spectrum.shape[2], spectrum.shape[3])
    return jnp.einsum("kt,kpx->ptx", inverse, flat, preferred_element_type=jnp.float32)


def contract(form, left, right):
    return jnp.einsum(form, left, right, preferred_element_type=jnp.float32)


def local(plus_start, reflection, onset_times):
    forward, inverse = make_tables()
    local_plus = lax.all_to_all(plus_start, "blk", split_axis=2, concat_axis=1, tiled=True)
    focal = local_plus.shape[0]
    width = local_plus.shape[2]
    offset = lax.axis_index("blk") * width
    local_onset = lax.dynamic_slice_in_dim(onset_times, offset, width, 1)
    keep = jnp.arange(NT, dtype=jnp.int32)[None, :, None] < local_onset[:, None, :]
    spectrum_plus = analyze(local_plus, forward)
    upgoing_spec = None
    downgoing_spec = None
    upgoing = None
    downgoing = None
    for iteration in range(ITERS):
        current = spectrum_plus
        real_sum = contract("wrs,wpr->swp", reflection[0], current[0]) - contract(
            "wrs,wpr->swp", reflection[1], current[1]
        )
        imag_sum = contract("wrs,wpr->swp", reflection[0], current[1]) + contract(
            "wrs,wpr->swp", reflection[1], current[0]
        )
        summed = lax.psum_scatter(
            jnp.stack([real_sum, imag_sum], axis=1)
            .reshape(width * lax.axis_size("blk"), 2 * NFW * focal)
            .astype(jnp.bfloat16),
            "blk",
            scatter_dimension=0,
            tiled=True,
        ).astype(jnp.float32)
        upgoing_spec = jnp.transpose(
            summed.reshape(width, 2, NFW, focal).astype(jnp.bfloat16), (1, 2, 3, 0)
        )
        upgoing = jnp.where(keep, synthesize(upgoing_spec, inverse), 0.0).astype(jnp.bfloat16)
        spectrum_minus = analyze(upgoing, forward)
        piece = lax.all_gather(spectrum_minus, "blk", axis=3, tiled=True)
        add_real_sum = contract("wrs,wps->wpr", reflection[0], piece[0]) + contract(
            "wrs,wps->wpr", reflection[1], piece[1]
        )
        add_imag_sum = contract("wrs,wps->wpr", reflection[0], piece[1]) - contract(
            "wrs,wps->wpr", reflection[1], piece[0]
        )
        downgoing_spec = jnp.stack([add_real_sum, add_imag_sum]).astype(jnp.bfloat16)
        downgoing = (
            local_plus.astype(jnp.float32)
            + jnp.where(keep, synthesize(downgoing_spec, inverse), 0.0)
        ).astype(jnp.bfloat16)
        if iteration + 1 < ITERS:
            spectrum_plus = analyze(downgoing, forward)
    return (
        lax.all_to_all(upgoing, "blk", split_axis=1, concat_axis=2, tiled=True),
        lax.all_to_all(downgoing, "blk", split_axis=1, concat_axis=2, tiled=True),
    )


def solution(mesh):
    return jax.shard_map(
        local,
        mesh=mesh,
        in_specs=(P("groups", "blk", None), P(None, None, "blk", None), P("groups", None)),
        out_specs=(P("groups", "blk", None), P("groups", "blk", None)),
        check_vma=False,
    )
```

profile of v0, /device:TPU:15, one launch (start us, length us, event | category | flops | bytes accessed | tf_op | source)
XLA Modules:
  0.0 639.6 jit_solution(4668101289411605684)
XLA Ops:
  7.2 0.0 copy-start
  7.2 10.1 %copy.22 = bf16[16,32,2048]{1,0,2:T(8,128)(2,1)} copy(bf16[16,32,2048]{2,1,0:T(8,128)(2,1)} %param.3) | data formatting | bytes 4194304 | tf_op args[0]
  17.2 14.5 %reshape.59 = bf16[16,2,32768]{2,1,0:T(2,128)(2,1)} reshape(bf16[2048,16,32]{2,1,0:T(8,128)(2,1)} %bitcast.224) | data formatting | bytes 4194304
  31.7 6.6 %all-to-all-start = ((bf16[16,2,32768]{2,1,0:T(2,128)(2,1)}), bf16[16,2,32768]{2,1,0:T(2,128)(2,1)S(1)}, u32[]{:S(2)}, u32[]{:S(2)}) async-start(bf16[16,2,32768]{2,1,0:T(2,128)(2,1)} %reshape.59), calls=%async_computation | async-start | bytes 4194304 | tf_op jit(solution)/shard_map/all_to_all | solution.py:41
  38.3 0.0 reduce-scatter.7.cloned.1.call-start
  38.3 0.3 fusion.135
  38.7 47.0 %all-to-all-done = bf16[16,2,32768]{2,1,0:T(2,128)(2,1)S(1)} async-done(((bf16[16,2,32768]{2,1,0:T(2,128)(2,1)}), bf16[16,2,32768]{2,1,0:T(2,128)(2,1)S(1)}, u32[]{:S(2)}, u32[]{:S(2)}) %all-to-all-start) | async-done | bytes 2097184 | tf_op jit(solution)/shard_map/all_to_all | solution.py:41
  85.7 8.7 %reshape.60 = bf16[2048,16,32]{2,1,0:T(8,128)(2,1)} reshape(bf16[16,2,32768]{2,1,0:T(2,128)(2,1)S(1)} %all-to-all-done) | data formatting | bytes 4194304
  94.4 8.5 %copy.23 = bf16[16,32,16,128]{3,1,2,0:T(8,128)(2,1)S(1)} copy(bf16[16,32,16,128]{1,0,3,2:T(8,128)(2,1)} %bitcast.223) | data formatting | bytes 4194304 | tf_op jit(solution)/shard_map/all_to_all | solution.py:41
  102.9 0.5 convolution_convert_fusion.1
  103.4 7.0 %fusion.14 = f32[32,16,2048]{2,1,0:T(8,128)S(1)} fusion(bf16[2,32,128,2048]{3,2,1,0:T(8,128)(2,1)} %param.4, bf16[32,16,128]{2,0,1:T(8,128)(2,1)S(1)} %get-tuple-element.4), kind=kOutput, calls=%fused_computation.14 | convolution fusion | flops 268435456 | bytes 21102592 | tf_op jit(solution)/shard_map/wrs,wpr->swp/dot_general | solution.py:36
  110.4 7.0 %fusion.12 = f32[32,16,2048]{2,1,0:T(8,128)S(1)} fusion(bf16[2,32,128,2048]{3,2,1,0:T(8,128)(2,1)} %param.4, bf16[32,16,128]{2,0,1:T(8,128)(2,1)S(1)} %get-tuple-element.5), kind=kOutput, calls=%fused_computation.12 | convolution fusion | flops 268435456 | bytes 21102592 | tf_op jit(solution)/shard_map/wrs,wpr->swp/dot_general | solution.py:36
  117.4 9.4 %fusion.60 = bf16[2048,1,32,16]{0,3,2,1:T(8,128)(2,1)} fusion(f32[32,16,2048]{2,1,0:T(8,128)S(1)} %fusion.14, bf16[2,32,128,2048]{3,2,1,0:T(8,128)(2,1)} %param.4, bf16[32,16,128]{2,0,1:T(8,128)(2,1)S(1)} %get-tuple-element.5), kind=kOutput, calls=%fused_computation.65 | convolution fusion | flops 270532608 | bytes 23199744 | tf_op jit(solution)/shard_map/wrs,wpr->swp/dot_general | solution.py:36
  126.8 8.2 %fusion.63 = bf16[2048,1,32,16]{0,3,2,1:T(8,128)(2,1)S(1)} fusion(f32[32,16,2048]{2,1,0:T(8,128)S(1)} %fusion.12, bf16[2,32,128,2048]{3,2,1,0:T(8,128)(2,1)} %param.4, bf16[32,16,128]{2,0,1:T(8,128)(2,1)S(1)} %get-tuple-element.4), kind=kOutput, calls=%fused_computation.66 | convolution fusion | flops 270532608 | bytes 23199744 | tf_op jit(solution)/shard_map/wrs,wpr->swp/dot_general | solution.py:36
  135.1 2.4 pad_maximum_fusion
  137.4 6.4 copy.47
  143.8 0.0 reduce-scatter.7.cloned.1.call-update
  143.8 0.0 all-gather.3.cloned.1.call-start
  143.9 69.9 %reduce-scatter.7.cloned.1.call-done = bf16[128,1024]{1,0:T(8,128)(2,1)} async-done(((bf16[2048,1024]{1,0:T(8,128)(2,1)}), bf16[128,1024]{1,0:T(8,128)(2,1)}) %reduce-scatter.7.cloned.1.call-update) | async-done | bytes 262160
  213.8 1.1 copy.48
  214.9 1.3 fusion.75
  216.1 0.9 copy.28
  217.0 0.0 all-gather.3.cloned.1.call-update
  217.1 0.3 reduce-scatter.9.cloned.1.call-start
  217.4 51.9 %all-gather.3.cloned.1.call-done = bf16[2,32,16,2048]{3,2,1,0:T(8,128)(2,1)} async-done(((bf16[2,32,16,128]{3,2,1,0:T(8,128)(2,1)}), bf16[2,32,16,2048]{3,2,1,0:T(8,128)(2,1)}) %all-gather.3.cloned.1.call-update) | async-done | bytes 4194320 | tf_op jit(solution)/shard_map/all_gather | solution.py:73
  269.3 10.8 %fusion.8 = f32[32,16,128]{2,1,0:T(8,128)S(1)} fusion(bf16[2,32,128,2048]{3,2,1,0:T(8,128)(2,1)} %param.4, bf16[2,32,16,2048]{3,2,1,0:T(8,128)(2,1)} %all-gather.3.cloned.1.call-done), kind=kOutput, calls=%fused_computation.8 | convolution fusion | flops 268435456 | bytes 19136512 | tf_op jit(solution)/shard_map/wrs,wps->wpr/dot_general | solution.py:36
  280.1 10.9 %fusion.10 = f32[32,16,128]{2,1,0:T(8,128)S(1)} fusion(bf16[2,32,128,2048]{3,2,1,0:T(8,128)(2,1)} %param.4, bf16[2,32,16,2048]{3,2,1,0:T(8,128)(2,1)} %all-gather.3.cloned.1.call-done), kind=kOutput, calls=%fused_computation.10 | convolution fusion | flops 268435456 | bytes 19136512 | tf_op jit(solution)/shard_map/wrs,wps->wpr/dot_general | solution.py:36
  291.0 10.9 %fusion.103 = bf16[1,32,16,128]{3,2,1,0:T(8,128)(2,1)S(1)} fusion(f32[32,16,128]{2,1,0:T(8,128)S(1)} %fusion.8, bf16[2,32,128,2048]{3,2,1,0:T(8,128)(2,1)} %param.4, bf16[2,32,16,2048]{3,2,1,0:T(8,128)(2,1)} %all-gather.3.cloned.1.call-done), kind=kOutput, calls=%fused_computation.88 | convolution fusion | flops 268566528 | bytes 19267584 | tf_op jit(solution)/shard_map/wrs,wps->wpr/dot_general | solution.py:36
  301.8 21.3 %fusion.100 = bf16[1,32,16,128]{3,2,1,0:T(8,128)(2,1)S(1)} fusion(f32[32,16,128]{2,1,0:T(8,128)S(1)} %fusion.10, bf16[2,32,128,2048]{3,2,1,0:T(8,128)(2,1)} %param.4, bf16[2,32,16,2048]{3,2,1,0:T(8,128)(2,1)} %all-gather.3.cloned.1.call-done), kind=kOutput, calls=%fused_computation.87 | convolution fusion | flops 268566528 | bytes 19267584 | tf_op jit(solution)/shard_map/wrs,wps->wpr/dot_general | solution.py:36
  323.2 1.3 fusion.74
  324.6 7.0 %fusion.6 = f32[32,16,2048]{2,1,0:T(8,128)S(1)} fusion(bf16[2,32,128,2048]{3,2,1,0:T(8,128)(2,1)} %param.4, bf16[32,16,128]{2,0,1:T(8,128)(2,1)S(1)} %get-tuple-element.2), kind=kOutput, calls=%fused_computation.6 | convolution fusion | flops 268435456 | bytes 21102592 | tf_op jit(solution)/shard_map/wrs,wpr->swp/dot_general | solution.py:36
  331.6 7.0 %fusion.4 = f32[32,16,2048]{2,1,0:T(8,128)S(1)} fusion(bf16[2,32,128,2048]{3,2,1,0:T(8,128)(2,1)} %param.4, bf16[32,16,128]{2,0,1:T(8,128)(2,1)S(1)} %get-tuple-element.3), kind=kOutput, calls=%fused_computation.4 | convolution fusion | flops 268435456 | bytes 21102592 | tf_op jit(solution)/shard_map/wrs,wpr->swp/dot_general | solution.py:36
  338.6 9.4 %fusion.66 = bf16[2048,1,32,16]{0,3,2,1:T(8,128)(2,1)} fusion(f32[32,16,2048]{2,1,0:T(8,128)S(1)} %fusion.6, bf16[2,32,128,2048]{3,2,1,0:T(8,128)(2,1)} %param.4, bf16[32,16,128]{2,0,1:T(8,128)(2,1)S(1)} %get-tuple-element.3), kind=kOutput, calls=%fused_computation.67 | convolution fusion | flops 270532608 | bytes 23199744 | tf_op jit(solution)/shard_map/wrs,wpr->swp/dot_general | solution.py:36
  348.0 8.2 %fusion.69 = bf16[2048,1,32,16]{0,3,2,1:T(8,128)(2,1)S(1)} fusion(f32[32,16,2048]{2,1,0:T(8,128)S(1)} %fusion.4, bf16[2,32,128,2048]{3,2,1,0:T(8,128)(2,1)} %param.4, bf16[32,16,128]{2,0,1:T(8,128)(2,1)S(1)} %get-tuple-element.2), kind=kOutput, calls=%fused_computation.68 | convolution fusion | flops 270532608 | bytes 23199744 | tf_op jit(solution)/shard_map/wrs,wpr->swp/dot_general | solution.py:36
  356.2 2.4 pad_maximum_fusion.1
  358.6 6.4 copy.49
  365.0 0.0 reduce-scatter.9.cloned.1.call-update
  365.0 0.0 all-gather.5.cloned.1.call-start
  365.0 70.9 %reduce-scatter.9.cloned.1.call-done = bf16[128,1024]{1,0:T(8,128)(2,1)} async-done(((bf16[2048,1024]{1,0:T(8,128)(2,1)}), bf16[128,1024]{1,0:T(8,128)(2,1)}) %reduce-scatter.9.cloned.1.call-update) | async-done | bytes 262160
  435.9 1.1 copy.50
  437.0 0.1 copy.33
  437.1 0.8 fusion.34
  437.9 0.0 copy-start.2
  437.9 1.3 copy-done.2
  439.2 0.5 convolution_convert_fusion
  439.7 0.9 copy.37
  440.6 0.0 all-gather.5.cloned.1.call-update
  440.6 4.3 copy.35
  444.9 7.4 %all-to-all-start.1 = ((bf16[16,512,128]{2,0,1:T(8,128)(2,1)}), bf16[16,512,128]{2,0,1:T(8,128)(2,1)}, u32[]{:S(2)}, u32[]{:S(2)}) async-start(bf16[16,512,128]{2,0,1:T(8,128)(2,1)} %copy.35), calls=%async_computation.1 | async-start | bytes 4194304 | tf_op jit(solution)/shard_map/all_to_all | solution.py:88
  452.2 69.0 %all-gather.5.cloned.1.call-done = bf16[2,32,16,2048]{3,2,1,0:T(8,128)(2,1)} async-done(((bf16[2,32,16,128]{3,2,1,0:T(8,128)(2,1)}), bf16[2,32,16,2048]{3,2,1,0:T(8,128)(2,1)}) %all-gather.5.cloned.1.call-update) | async-done | bytes 4194320 | tf_op jit(solution)/shard_map/all_gather | solution.py:73
  521.2 10.8 %fusion = f32[32,16,128]{2,1,0:T(8,128)S(1)} fusion(bf16[2,32,128,2048]{3,2,1,0:T(8,128)(2,1)} %param.4, bf16[2,32,16,2048]{3,2,1,0:T(8,128)(2,1)} %all-gather.5.cloned.1.call-done), kind=kOutput, calls=%fused_computation | convolution fusion | flops 268435456 | bytes 19136512 | tf_op jit(solution)/shard_map/wrs,wps->wpr/dot_general | solution.py:36
  532.1 10.9 %fusion.2 = f32[32,16,128]{2,1,0:T(8,128)S(1)} fusion(bf16[2,32,128,2048]{3,2,1,0:T(8,128)(2,1)} %param.4, bf16[2,32,16,2048]{3,2,1,0:T(8,128)(2,1)} %all-gather.5.cloned.1.call-done), kind=kOutput, calls=%fused_computation.2 | convolution fusion | flops 268435456 | bytes 19136512 | tf_op jit(solution)/shard_map/wrs,wps->wpr/dot_general | solution.py:36
  542.9 10.9 %fusion.109 = bf16[1,32,16,128]{3,2,1,0:T(8,128)(2,1)S(1)} fusion(f32[32,16,128]{2,1,0:T(8,128)S(1)} %fusion, bf16[2,32,128,2048]{3,2,1,0:T(8,128)(2,1)} %param.4, bf16[2,32,16,2048]{3,2,1,0:T(8,128)(2,1)} %all-gather.5.cloned.1.call-done), kind=kOutput, calls=%fused_computation.90 | convolution fusion | flops 268566528 | bytes 19267584 | tf_op jit(solution)/shard_map/wrs,wps->wpr/dot_general | solution.py:36
  553.8 11.1 %fusion.106 = bf16[1,32,16,128]{3,2,1,0:T(8,128)(2,1)S(1)} fusion(f32[32,16,128]{2,1,0:T(8,128)S(1)} %fusion.2, bf16[2,32,128,2048]{3,2,1,0:T(8,128)(2,1)} %param.4, bf16[2,32,16,2048]{3,2,1,0:T(8,128)(2,1)} %all-gather.5.cloned.1.call-done), kind=kOutput, calls=%fused_computation.89 | convolution fusion | flops 268566528 | bytes 19267584 | tf_op jit(solution)/shard_map/wrs,wps->wpr/dot_general | solution.py:36
  565.0 1.1 fusion.33
  566.1 2.7 copy.40
  568.7 0.0 all-to-all-done.1
  568.8 9.6 %all-to-all-start.2 = ((bf16[16,512,128]{2,0,1:T(8,128)(2,1)}), bf16[16,512,128]{2,0,1:T(8,128)(2,1)S(1)}, u32[]{:S(2)}, u32[]{:S(2)}) async-start(bf16[16,512,128]{2,0,1:T(8,128)(2,1)} %copy.40), calls=%async_computation.2 | async-start | bytes 4194304 | tf_op jit(solution)/shard_map/all_to_all | solution.py:89
  578.3 4.3 copy.36
  582.6 4.2 all_to_all.46
  586.7 39.0 %all-to-all-done.2 = bf16[16,512,128]{2,0,1:T(8,128)(2,1)S(1)} async-done(((bf16[16,512,128]{2,0,1:T(8,128)(2,1)}), bf16[16,512,128]{2,0,1:T(8,128)(2,1)S(1)}, u32[]{:S(2)}, u32[]{:S(2)}) %all-to-all-start.2) | async-done | bytes 2097184 | tf_op jit(solution)/shard_map/all_to_all | solution.py:89
  625.8 2.7 copy.41
  628.4 4.2 all_to_all.50
  632.6 0.0 copy-done.1
  (13 shorter events, 0.2 us)
Async XLA Ops:
  7.2 136.7 %copy-start = (s32[16,2048]{1,0:T(8,128)S(1)}, s32[16,2048]{1,0:T(8,128)}, u32[]{:S(2)}) copy-start(s32[16,2048]{1,0:T(8,128)} %param.5) | copy-start | bytes 393220
  31.7 54.0 %all-to-all-start = ((bf16[16,2,32768]{2,1,0:T(2,128)(2,1)}), bf16[16,2,32768]{2,1,0:T(2,128)(2,1)S(1)}, u32[]{:S(2)}, u32[]{:S(2)}) async-start(bf16[16,2,32768]{2,1,0:T(2,128)(2,1)} %reshape.59), calls=%async_computation | async-start | bytes 4194304 | tf_op jit(solution)/shard_map/all_to_all | solution.py:41
  38.3 175.5 %reduce-scatter.7.cloned.1.call-start = ((), (), s32[]{:S(2)}) async-start(), calls=%async_computation.7 | async-start | bytes 4456448
  126.8 8.2 %copy-start.3 = (bf16[2048,1,32,16]{0,3,2,1:T(8,128)(2,1)S(1)}, bf16[2048,1,32,16]{0,3,2,1:T(8,128)(2,1)}, u32[]{:S(2)}) copy-start(bf16[2048,1,32,16]{0,3,2,1:T(8,128)(2,1)} %fusion.60) | copy-start | bytes 6291460
  143.8 125.4 %all-gather.3.cloned.1.call-start = ((), (), s32[]{:S(2)}) async-start(), calls=%async_computation.5 | async-start | bytes 4456448 | tf_op jit(solution)/shard_map/all_gather | solution.py:73
  217.1 218.8 %reduce-scatter.9.cloned.1.call-start = ((), (), s32[]{:S(2)}) async-start(), calls=%async_computation.8 | async-start | bytes 4456448
  348.0 8.2 %copy-start.4 = (bf16[2048,1,32,16]{0,3,2,1:T(8,128)(2,1)S(1)}, bf16[2048,1,32,16]{0,3,2,1:T(8,128)(2,1)}, u32[]{:S(2)}) copy-start(bf16[2048,1,32,16]{0,3,2,1:T(8,128)(2,1)} %fusion.66) | copy-start | bytes 6291460
  365.0 156.3 %all-gather.5.cloned.1.call-start = ((), (), s32[]{:S(2)}) async-start(), calls=%async_computation.6 | async-start | bytes 4456448 | tf_op jit(solution)/shard_map/all_gather | solution.py:73
  437.9 1.3 copy-start.2
  444.9 123.9 %all-to-all-start.1 = ((bf16[16,512,128]{2,0,1:T(8,128)(2,1)}), bf16[16,512,128]{2,0,1:T(8,128)(2,1)}, u32[]{:S(2)}, u32[]{:S(2)}) async-start(bf16[16,512,128]{2,0,1:T(8,128)(2,1)} %copy.35), calls=%async_computation.1 | async-start | bytes 4194304 | tf_op jit(solution)/shard_map/all_to_all | solution.py:88
  568.8 57.0 %all-to-all-start.2 = ((bf16[16,512,128]{2,0,1:T(8,128)(2,1)}), bf16[16,512,128]{2,0,1:T(8,128)(2,1)S(1)}, u32[]{:S(2)}, u32[]{:S(2)}) async-start(bf16[16,512,128]{2,0,1:T(8,128)(2,1)} %copy.40), calls=%async_computation.2 | async-start | bytes 4194304 | tf_op jit(solution)/shard_map/all_to_all | solution.py:89
  625.8 6.8 %copy-start.1 = (s32[16,2048]{1,0:T(8,128)S(1)}, s32[16,2048]{1,0:T(8,128)}, u32[]{:S(2)}) copy-start(s32[16,2048]{1,0:T(8,128)} %param.5) | copy-start | bytes 393220
Sparse Core Ops, SparseCore 0:
  143.9 69.7 reduce-scatter.6
  217.2 52.0 all-gather.2
  365.1 70.7 reduce-scatter.8
  440.7 80.4 all-gather.4
where the time goes:
time: 650 us; the launch traced here: 640 us
  waiting for transfers between devices  348 us (54%)
  matrix products  166 us (26%)
  local copies, waits for them, and re-layouts  82.2 us (13%)
  starting transfers between devices  23.9 us (4%)
  between operations  14.4 us (2%)
    dot_general x16, matrix products, contract(): return jnp.einsum(form, left, right, preferred_element_type=jnp.float32)  161 us
    unnamed x6, waiting for transfers between devices  141 us
    all_gather x2, waiting for transfers between devices, local(): piece = lax.all_gather(spectrum_minus, 'blk', axis=3, tiled=True)  121 us
    unnamed x17, local copies, waits for them, and re-layouts  49.6 us
    all_to_all x1, waiting for transfers between devices, local(): lax.all_to_all(plus_start, 'blk', split_axis=2, concat_axis=1, tiled=True)  47 us
    all_to_all x1, waiting for transfers between devices, local(): lax.all_to_all(downgoing, 'blk', split_axis=1, concat_axis=2, tiled=True)  39 us
  transfers between devices with their start and end apart: 7, of which 6 were waited for; matrix products, arithmetic and copies ran while one was open for 9% of the time, Pallas kernels for 0%

commit v1 on v0

v1 whole, which is shorter than its diff:
```python
import functools
import math

import jax
import jax.numpy as jnp
from jax import lax
from jax.experimental import pallas as pl
from jax.experimental.pallas import tpu as pltpu
from jax.sharding import PartitionSpec as P

NT = 512
NFW = 32
FREQ0 = 16
ITERS = 2
LANES = 128
F32 = jnp.float32
BF16 = jnp.bfloat16


def basis_of(samples):
    freqs = FREQ0 + jnp.arange(NFW, dtype=jnp.int32)
    turns = freqs[:, None] * samples[None, :] % NT
    phase = turns.astype(F32) * (2.0 * math.pi / NT)
    return jnp.stack([jnp.cos(phase), -jnp.sin(phase)], axis=1)


def tables_of(samples):
    basis = basis_of(samples).reshape(2 * NFW, samples.shape[0])
    forward = (basis * (1.0 / math.sqrt(NT))).astype(BF16)
    inverse = (basis * math.sqrt(2.0 / NFW)).astype(BF16)
    return forward, inverse.T


class Places:
    def __init__(self, axis, size):
        self.axis = axis
        self.size = size
        self.line = size // 4

    def core(self):
        return [(b, b ^ 1) for b in range(self.size)]

    def pair(self):
        return [(b, b ^ 2) for b in range(self.size)]

    def shift(self, step):
        return [(b, (b // 4 + step) % self.line * 4 + b % 4) for b in range(self.size)]

    def send(self, array, pairs):
        return lax.ppermute(array, self.axis, pairs)


def own_place(line):
    me = lax.axis_index("blk")
    return me, me // 4, (me // 2) % 2, me % 2


def chip_columns(line, ahead, flip, step):
    _, l, m, _ = own_place(line)
    other = lax.rem(l + step, line) if ahead else lax.rem(l - step + line, line)
    chip = other * 2 + (lax.rem(m + flip, 2))
    return pl.multiple_of(chip * (2 * LANES), 2 * LANES)


def relative(line):
    return [(flip, step) for flip in range(2) for step in range(line)]


def split_cores(core, block):
    low, high = block[:, :LANES], block[:, LANES:]
    first = core == 0
    return jnp.where(first, low, high), jnp.where(first, high, low)


def join_cores(core, own, other):
    first = core == 0
    return jnp.concatenate([jnp.where(first, own, other), jnp.where(first, other, own)], axis=1)


def analysis_kernel(line, rows, forward_ref, plus_ref, keep0, keep1, send0, send1):
    core = own_place(line)[3]
    keep, send = (keep0, keep1), (send0, send1)
    for p in range(rows):
        for flip, step in relative(line):
            columns = pl.ds(chip_columns(line, True, flip, step), 2 * LANES)
            block = jnp.dot(forward_ref[...], plus_ref[p, :, columns], preferred_element_type=F32)
            mine, theirs = split_cores(core, block.astype(BF16))
            keep[flip][step, p] = mine
            send[flip][step, p] = theirs


def first_analysis(plus_start, forward, line):
    focal, samples, width = plus_start.shape
    rows = 4
    out = jax.ShapeDtypeStruct((line, focal, 2 * NFW, LANES), BF16)
    out_spec = pl.BlockSpec((line, rows, 2 * NFW, LANES), lambda i: (0, i, 0, 0))
    return pl.pallas_call(
        functools.partial(analysis_kernel, line, rows),
        grid=(focal // rows,),
        in_specs=[
            pl.BlockSpec((2 * NFW, samples), lambda i: (0, 0)),
            pl.BlockSpec((rows, samples, width), lambda i: (i, 0, 0)),
        ],
        out_specs=[out_spec] * 4,
        out_shape=[out] * 4,
        compiler_params=pltpu.CompilerParams(vmem_limit_bytes=24 << 20),
        cost_estimate=pl.CostEstimate(
            flops=4 * NFW * focal * samples * width,
            bytes_accessed=2 * focal * samples * width + 4 * NFW * focal * width,
            transcendentals=0,
        ),
        name="first_analysis",
    )(forward, plus_start)


def convolve_kernel(line, rows, spec_ref, panel_ref, keep0, keep1, send0, send1):
    core = own_place(line)[3]
    keep, send = (keep0, keep1), (send0, send1)
    focal = spec_ref.shape[2]
    for w in range(rows):
        real, imag = spec_ref[w, 0], spec_ref[w, 1]
        left = jnp.concatenate(
            [jnp.concatenate([real, -imag], axis=1), jnp.concatenate([imag, real], axis=1)], axis=0
        )
        for flip, step in relative(line):
            columns = pl.ds(chip_columns(line, True, flip, step), 2 * LANES)
            panel = panel_ref[:, w, :, columns].reshape(2 * LANES, 2 * LANES)
            block = jnp.dot(left, panel, preferred_element_type=F32)
            mine, theirs = split_cores(core, block.astype(BF16))
            keep[flip][step, w] = mine.reshape(2, focal, LANES)
            send[flip][step, w] = theirs.reshape(2, focal, LANES)


def convolve(spectrum, reflection, line):
    focal = spectrum.shape[2]
    sources = reflection.shape[3]
    rows = 2
    out = jax.ShapeDtypeStruct((line, NFW, 2, focal, LANES), BF16)
    out_spec = pl.BlockSpec((line, rows, 2, focal, LANES), lambda i: (0, i, 0, 0, 0))
    return pl.pallas_call(
        functools.partial(convolve_kernel, line, rows),
        grid=(NFW // rows,),
        in_specs=[
            pl.BlockSpec((rows, 2, focal, LANES), lambda i: (i, 0, 0, 0)),
            pl.BlockSpec((2, rows, LANES, sources), lambda i: (0, i, 0, 0)),
        ],
        out_specs=[out_spec] * 4,
        out_shape=[out] * 4,
        compiler_params=pltpu.CompilerParams(vmem_limit_bytes=24 << 20),
        cost_estimate=pl.CostEstimate(
            flops=8 * NFW * focal * LANES * sources,
            bytes_accessed=4 * NFW * sources * (LANES + focal),
            transcendentals=0,
        ),
        name="convolve",
    )(spectrum, reflection)


def correlate_kernel(line, rows, *refs):
    core = own_place(line)[3]
    places = relative(line)
    own, other = refs[: len(places)], refs[len(places) : 2 * len(places)]
    panel_ref, out_ref = refs[2 * len(places) :]
    focal = out_ref.shape[2]
    for w in range(rows):
        total = jnp.zeros((2 * focal, 2 * LANES), F32)
        for at, (flip, step) in enumerate(places):
            columns = pl.ds(chip_columns(line, False, flip, step), 2 * LANES)
            panel = panel_ref[:, w, :, columns].reshape(2 * LANES, 2 * LANES)
            spec = join_cores(
                core, own[at][w].reshape(2 * focal, LANES), other[at][w].reshape(2 * focal, LANES)
            )
            total += lax.dot_general(spec, panel, (((1,), (1,)), ((), ())), preferred_element_type=F32)
        out_ref[w, 0] = total[:focal, :LANES] + total[focal:, LANES:]
        out_ref[w, 1] = total[focal:, :LANES] - total[:focal, LANES:]


def correlate(own, other, reflection, line):
    focal = own[0].shape[2]
    sources = reflection.shape[3]
    rows = 2
    spec_block = pl.BlockSpec((rows, 2, focal, LANES), lambda i: (i, 0, 0, 0))
    return pl.pallas_call(
        functools.partial(correlate_kernel, line, rows),
        grid=(NFW // rows,),
        in_specs=[spec_block] * (len(own) + len(other))
        + [pl.BlockSpec((2, rows, LANES, sources), lambda i: (0, i, 0, 0))],
        out_specs=spec_block,
        out_shape=jax.ShapeDtypeStruct((NFW, 2, focal, LANES), F32),
        compiler_params=pltpu.CompilerParams(vmem_limit_bytes=24 << 20),
        cost_estimate=pl.CostEstimate(
            flops=8 * NFW * focal * LANES * sources,
            bytes_accessed=4 * NFW * sources * (LANES + focal),
            transcendentals=0,
        ),
        name="correlate",
    )(*own, *other, reflection)


def window_kernel(parts, has_base, want_spec, *refs):
    refs = list(refs)
    forward_ref, inverse_ref, onset_ref = refs[:3]
    part_refs = refs[3 : 3 + parts]
    rest = refs[3 + parts :]
    base_ref = rest.pop(0) if has_base else None
    out_ref = rest.pop(0)
    spec_ref = rest.pop(0) if want_spec else None
    held, result = rest
    focal = out_ref.shape[2]
    k = 2 * NFW
    total = part_refs[0][...].astype(F32)
    for ref in part_refs[1:]:
        total += ref[...].astype(F32)
    held[...] = total.reshape(k * focal, LANES)
    me = lax.axis_index("blk")
    columns = pl.ds(pl.multiple_of(me * LANES, LANES), LANES)
    time = lax.broadcasted_iota(jnp.int32, (NT, 2 * LANES), 0)
    for p in range(0, focal, 2):
        pair = [held[pl.ds(p + q, k, stride=focal), :].astype(BF16) for q in range(2)]
        if spec_ref is not None:
            for q in range(2):
                spec_ref[p + q] = pair[q]
        field = jnp.dot(inverse_ref[...], jnp.concatenate(pair, axis=1), preferred_element_type=F32)
        onset = jnp.concatenate([onset_ref[p + q : p + q + 1, columns] for q in range(2)], axis=1)
        kept = jnp.where(time < onset, field, 0.0).astype(BF16)
        spectrum = jnp.dot(forward_ref[...], kept, preferred_element_type=F32)
        for q in range(2):
            result[pl.ds(p + q, k, stride=focal), :] = spectrum[:, q * LANES : (q + 1) * LANES]
    final = result[...].reshape(NFW, 2, focal, LANES)
    if base_ref is not None:
        final += base_ref[...].astype(F32)
    out_ref[...] = final.astype(BF16)


def window(parts, forward, inverse, onset_times, base=None, want_spec=False):
    focal = parts[0].shape[2]
    k = 2 * NFW
    operands = [forward, inverse, onset_times, *parts] + ([] if base is None else [base])
    whole = pl.BlockSpec(memory_space=pltpu.VMEM)
    out = [jax.ShapeDtypeStruct((NFW, 2, focal, LANES), BF16)]
    if want_spec:
        out.append(jax.ShapeDtypeStruct((focal, k, LANES), BF16))
    return pl.pallas_call(
        functools.partial(window_kernel, len(parts), base is not None, want_spec),
        in_specs=[whole] * len(operands),
        out_specs=[whole] * len(out),
        out_shape=out,
        scratch_shapes=[pltpu.VMEM((k * focal, LANES), F32)] * 2,
        compiler_params=pltpu.CompilerParams(vmem_limit_bytes=24 << 20),
        cost_estimate=pl.CostEstimate(
            flops=4 * k * NT * focal * LANES, bytes_accessed=2 * k * focal * LANES * 6, transcendentals=0
        ),
        name="window",
    )(*operands)


def field_kernel(line, rows, has_plus, *refs):
    core = own_place(line)[3]
    places = relative(line)
    inverse_ref, onset_ref = refs[:2]
    own, other = refs[2 : 2 + len(places)], refs[2 + len(places) : 2 + 2 * len(places)]
    rest = refs[2 + 2 * len(places) :]
    out_ref = rest[-1]
    samples = out_ref.shape[1]
    first = pl.program_id(0) * rows
    time = lax.axis_index("blk") * samples + lax.broadcasted_iota(jnp.int32, (samples, 2 * LANES), 0)
    for p in range(rows):
        for at, (flip, step) in enumerate(places):
            columns = pl.ds(chip_columns(line, False, flip, step), 2 * LANES)
            spec = join_cores(core, own[at][p], other[at][p])
            field = jnp.dot(inverse_ref[...], spec, preferred_element_type=F32)
            value = jnp.where(time < onset_ref[pl.ds(first + p, 1), columns], field, 0.0)
            if has_plus:
                value += rest[0][p, :, columns].astype(F32)
            out_ref[p, :, columns] = value.astype(BF16)


def field(own, other, inverse, onset_times, line, plus_start=None):
    focal, k, _ = own[0].shape
    samples = inverse.shape[0]
    width = onset_times.shape[1]
    rows = 4
    spec_block = pl.BlockSpec((rows, k, LANES), lambda i: (i, 0, 0))
    wide = pl.BlockSpec((rows, samples, width), lambda i: (i, 0, 0))
    plus = [] if plus_start is None else [plus_start]
    return pl.pallas_call(
        functools.partial(field_kernel, line, rows, bool(plus)),
        grid=(focal // rows,),
        in_specs=[
            pl.BlockSpec(inverse.shape, lambda i: (0, 0)),
            pl.BlockSpec(onset_times.shape, lambda i: (0, 0)),
        ]
        + [spec_block] * (len(own) + len(other))
        + [wide] * len(plus),
        out_specs=wide,
        out_shape=jax.ShapeDtypeStruct((focal, samples, width), BF16),
        compiler_params=pltpu.CompilerParams(vmem_limit_bytes=24 << 20),
        cost_estimate=pl.CostEstimate(
            flops=2 * k * focal * samples * width,
            bytes_accessed=2 * focal * width * (k + 2 * samples),
            transcendentals=0,
        ),
        name="field",
    )(inverse, onset_times, *own, *other, *plus)


def add(*parts):
    total = parts[0].astype(F32)
    for part in parts[1:]:
        total += part.astype(F32)
    return total


def reduce_scatter(places, keep0, keep1, send0, send1):
    got1 = places.send(send1, places.core())
    got0 = places.send(send0, places.core())
    order = list(range(1, places.line)) + [0]
    across = {}
    for step in order:
        across[step] = places.send(add(keep1[step], got1[step]).astype(BF16), places.pair())
    parts = [keep0[0], got0[0], across[0]]
    for step in order[:-1]:
        summed = add(keep0[step], got0[step], across[step]).astype(BF16)
        parts.append(places.send(summed, places.shift(step)))
    return parts


def all_gather(places, block):
    line = [block] + [places.send(block, places.shift(step)) for step in range(1, places.line)]
    own = line + [places.send(piece, places.pair()) for piece in line]
    other = [places.send(piece, places.core()) for piece in own]
    return own, other


def local(plus_start, reflection, onset_times):
    size = lax.axis_size("blk")
    places = Places("blk", size)
    line = places.line
    focal, samples, _ = plus_start.shape
    forward, inverse = tables_of(jnp.arange(NT, dtype=jnp.int32))
    own_samples = lax.axis_index("blk") * samples + jnp.arange(samples, dtype=jnp.int32)
    own_forward, own_inverse = tables_of(own_samples)

    parts = reduce_scatter(places, *first_analysis(plus_start, own_forward, line))
    start = add(*parts).astype(BF16)
    start = jnp.transpose(start, (1, 0, 2)).reshape(NFW, 2, focal, LANES)
    spectrum_plus = start
    for iteration in range(ITERS):
        last = iteration + 1 == ITERS
        parts = reduce_scatter(places, *convolve(spectrum_plus, reflection, line))
        windowed = window(parts, forward, inverse, onset_times, want_spec=last)
        gathered = all_gather(places, windowed[0])
        if last:
            upgoing_spec = all_gather(places, windowed[1])
        downgoing_spec = correlate(*gathered, reflection, line)
        if not last:
            (spectrum_plus,) = window([downgoing_spec], forward, inverse, onset_times, base=start)
    upgoing = field(*upgoing_spec, own_inverse, onset_times, line)
    final = jnp.transpose(
        downgoing_spec.astype(BF16).reshape(2 * NFW, focal, LANES), (1, 0, 2)
    )
    downgoing = field(*all_gather(places, final), own_inverse, onset_times, line, plus_start)
    return upgoing, downgoing


def analyze(values, forward):
    total = jnp.einsum("kt,ptx->kpx", forward, values, preferred_element_type=F32)
    return total.reshape(NFW, 2, values.shape[0], values.shape[2])


def synthesize(spectrum, inverse):
    flat = spectrum.reshape(2 * NFW, spectrum.shape[2], spectrum.shape[3])
    return jnp.einsum("tk,kpx->ptx", inverse, flat, preferred_element_type=F32)


def contract(form, left, right):
    return jnp.einsum(form, left, right, preferred_element_type=F32)


def local_any(plus_start, reflection, onset_times):
    samples = plus_start.shape[1]
    width = reflection.shape[2]
    me = lax.axis_index("blk")
    forward, inverse = tables_of(jnp.arange(NT, dtype=jnp.int32))
    own_forward, own_inverse = tables_of(me * samples + jnp.arange(samples, dtype=jnp.int32))
    onset = lax.dynamic_slice_in_dim(onset_times, me * width, width, 1)
    keep = jnp.arange(NT, dtype=jnp.int32)[None, :, None] < onset[:, None, :]
    time = me * samples + jnp.arange(samples, dtype=jnp.int32)
    own_keep = time[None, :, None] < onset_times[:, None, :]

    def scatter(partial):
        return lax.psum_scatter(partial.astype(BF16), "blk", scatter_dimension=3, tiled=True).astype(BF16)

    def gather(block):
        return lax.all_gather(block, "blk", axis=3, tiled=True)

    start = scatter(analyze(plus_start, own_forward))
    spectrum = start
    for iteration in range(ITERS):
        real = contract("wrs,wpr->wps", reflection[0], spectrum[:, 0]) - contract(
            "wrs,wpr->wps", reflection[1], spectrum[:, 1]
        )
        imag = contract("wrs,wpr->wps", reflection[0], spectrum[:, 1]) + contract(
            "wrs,wpr->wps", reflection[1], spectrum[:, 0]
        )
        upgoing_spec = scatter(jnp.stack([real, imag], axis=1))
        kept = jnp.where(keep, synthesize(upgoing_spec, inverse), 0.0).astype(BF16)
        minus = gather(analyze(kept, forward).astype(BF16))
        real = contract("wrs,wps->wpr", reflection[0], minus[:, 0]) + contract(
            "wrs,wps->wpr", reflection[1], minus[:, 1]
        )
        imag = contract("wrs,wps->wpr", reflection[0], minus[:, 1]) - contract(
            "wrs,wps->wpr", reflection[1], minus[:, 0]
        )
        downgoing_spec = jnp.stack([real, imag], axis=1).astype(BF16)
        if iteration + 1 < ITERS:
            kept = jnp.where(keep, synthesize(downgoing_spec, inverse), 0.0).astype(BF16)
            spectrum = (start.astype(F32) + analyze(kept, forward)).astype(BF16)
    upgoing = jnp.where(own_keep, synthesize(gather(upgoing_spec), own_inverse), 0.0).astype(BF16)
    change = jnp.where(own_keep, synthesize(gather(downgoing_spec), own_inverse), 0.0)
    return upgoing, (plus_start.astype(F32) + change).astype(BF16)


def solution(mesh):
    size = mesh.shape["blk"]

    def run(plus_start, reflection, onset_times):
        width = reflection.shape[2] // size
        fits = width == LANES and size % 4 == 0 and (plus_start.shape[1] // size) % 16 == 0
        return jax.shard_map(
            local if fits else local_any,
            mesh=mesh,
            in_specs=(P("groups", "blk", None), P(None, None, "blk", None), P("groups", None)),
            out_specs=(P("groups", "blk", None), P("groups", "blk", None)),
            check_vma=False,
        )(plus_start, reflection, onset_times)

    return run
```

time: 650 us -> 417 us (0.64)
  the two profiles are of different devices: /device:TPU:15 before, /device:TPU:0 now
where the time goes in v1:
time: 417 us; the launch traced here: 415 us
  waiting for transfers between devices  225 us (54%)
  Pallas kernels  94 us (23%)
  starting transfers between devices  73.7 us (18%)
  local copies, waits for them, and re-layouts  16.3 us (4%)
  other arithmetic  4.89 us (1%)
    ppermute x87, waiting for transfers between devices, send(): return lax.ppermute(array, self.axis, pairs)  225 us
    ppermute x87, starting transfers between devices, send(): return lax.ppermute(array, self.axis, pairs)  73.7 us
    pallas_call x2, Pallas kernels, correlate(): pl.pallas_call(functools.partial(correlate_kernel, line, rows), grid=(NFW...  40.6 us
    pallas_call x2, Pallas kernels, convolve(): pl.pallas_call(functools.partial(convolve_kernel, line, rows), grid=(NFW...  36.9 us
    unnamed x50, local copies, waits for them, and re-layouts  14.4 us
  transfers between devices with their start and end apart: 87, of which 39 were waited for; matrix products, arithmetic and copies ran while one was open for 1% of the time, Pallas kernels for 6%

profile of v1, /device:TPU:0, one launch (start us, length us, event | category | flops | bytes accessed | tf_op | source)
XLA Modules:
  0.0 415.1 jit_solution(2126125970140903870)
XLA Ops:
  0.9 1.6 copy-done
  2.4 2.1 first_analysis.1
  5.1 2.2 collective-permute-done.1
  7.7 3.0 collective-permute-start.7
  10.8 1.9 collective-permute-start.3
  12.8 5.0 %collective-permute-done.7 = bf16[16,64,128]{2,1,0:T(8,128)(2,1)S(1)} collective-permute-done((bf16[16,64,128]{2,1,0:T(8,128)(2,1)S(1)}, bf16[16,64,128]{2,1,0:T(8,128)(2,1)S(1)}, u32[]{:S(2)}, u32[]{:S(2)}) %collective-permute-start.7) | collective-permute-done | bytes 262176 | tf_op jit(solution)/shard_map/ppermute | solution.py:50
  17.8 5.6 %collective-permute-done.5 = bf16[16,64,128]{2,1,0:T(8,128)(2,1)S(1)} collective-permute-done((bf16[16,64,128]{2,1,0:T(8,128)(2,1)S(1)}, bf16[16,64,128]{2,1,0:T(8,128)(2,1)S(1)}, u32[]{:S(2)}, u32[]{:S(2)}) %collective-permute-start.5) | collective-permute-done | bytes 262176 | tf_op jit(solution)/shard_map/ppermute | solution.py:50
  23.4 5.6 %collective-permute-done.3 = bf16[16,64,128]{2,1,0:T(8,128)(2,1)S(1)} collective-permute-done((bf16[16,64,128]{2,1,0:T(8,128)(2,1)S(1)}, bf16[16,64,128]{2,1,0:T(8,128)(2,1)S(1)}, u32[]{:S(2)}, u32[]{:S(2)}) %collective-permute-start.3) | collective-permute-done | bytes 262176 | tf_op jit(solution)/shard_map/ppermute | solution.py:50
  29.4 2.2 collective-permute-start.4
  31.6 2.1 collective-permute-start.8
  34.6 6.2 %collective-permute-done.4 = bf16[16,64,128]{2,1,0:T(8,128)(2,1)S(1)} collective-permute-done((bf16[16,64,128]{2,1,0:T(8,128)(2,1)S(1)}, bf16[16,64,128]{2,1,0:T(8,128)(2,1)S(1)}, u32[]{:S(2)}, u32[]{:S(2)}) %collective-permute-start.4) | collective-permute-done | bytes 262176 | tf_op jit(solution)/shard_map/ppermute | solution.py:50
  40.9 3.2 collective-permute-done.8
  44.0 11.5 %collective-permute-done.6 = bf16[16,64,128]{2,1,0:T(8,128)(2,1)S(1)} collective-permute-done((bf16[16,64,128]{2,1,0:T(8,128)(2,1)S(1)}, bf16[16,64,128]{2,1,0:T(8,128)(2,1)S(1)}, u32[]{:S(2)}, u32[]{:S(2)}) %collective-permute-start.6) | collective-permute-done | bytes 262176 | tf_op jit(solution)/shard_map/ppermute | solution.py:50
  55.9 18.4 %convolve.2 = (bf16[4,32,2,16,128]{4,3,2,1,0:T(8,128)(2,1)S(1)}, bf16[4,32,2,16,128]{4,3,2,1,0:T(8,128)(2,1)S(1)}, bf16[4,32,2,16,128]{4,3,2,1,0:T(8,128)(2,1)S(1)}, bf16[4,32,2,16,128]{4,3,2,1,0:T(8,128)(2,1)S(1)}) custom-call(bf16[32,2,16,128]{3,2,1,0:T(8,128)(2,1)S(1)} %bitcast.90, bf16[2,32,128,2048]{3,2,1,0:T(8,128)(2,1)} %refs_16_.3), custom_call_target="tpu_custom_call" | custom-call | flops 1073741824 | bytes 37748736 | tf_op jit(solution)/shard_map/convolve/pallas_call | solution.py:140
  74.9 2.9 collective-permute-done.10
  83.7 4.5 %collective-permute-done.16 = bf16[32,2,16,128]{3,2,1,0:T(8,128)(2,1)S(1)} collective-permute-done((bf16[32,2,16,128]{3,2,1,0:T(8,128)(2,1)}, bf16[32,2,16,128]{3,2,1,0:T(8,128)(2,1)S(1)}, u32[]{:S(2)}, u32[]{:S(2)}) %collective-permute-start.16) | collective-permute-done | bytes 262176 | tf_op jit(solution)/shard_map/ppermute | solution.py:50
  88.2 5.7 %collective-permute-done.14 = bf16[32,2,16,128]{3,2,1,0:T(8,128)(2,1)} collective-permute-done((bf16[32,2,16,128]{3,2,1,0:T(8,128)(2,1)}, bf16[32,2,16,128]{3,2,1,0:T(8,128)(2,1)}, u32[]{:S(2)}, u32[]{:S(2)}) %collective-permute-start.14) | collective-permute-done | bytes 262176 | tf_op jit(solution)/shard_map/ppermute | solution.py:50
  93.9 5.6 %collective-permute-done.12 = bf16[32,2,16,128]{3,2,1,0:T(8,128)(2,1)} collective-permute-done((bf16[32,2,16,128]{3,2,1,0:T(8,128)(2,1)S(1)}, bf16[32,2,16,128]{3,2,1,0:T(8,128)(2,1)}, u32[]{:S(2)}, u32[]{:S(2)}) %collective-permute-start.12) | collective-permute-done | bytes 262176 | tf_op jit(solution)/shard_map/ppermute | solution.py:50
  99.6 1.6 fusion.3
  101.2 1.6 collective-permute-start.17
  104.5 5.2 %collective-permute-done.17.refs_8_ = bf16[32,2,16,128]{3,2,1,0:T(8,128)(2,1)S(1)} collective-permute-done((bf16[32,2,16,128]{3,2,1,0:T(8,128)(2,1)S(1)}, bf16[32,2,16,128]{3,2,1,0:T(8,128)(2,1)S(1)}, u32[]{:S(2)}, u32[]{:S(2)}) %collective-permute-start.17) | collective-permute-done | bytes 262176 | tf_op jit(solution)/shard_map/ppermute | solution.py:50
  109.6 13.4 %collective-permute-done.15.refs_7_ = bf16[32,2,16,128]{3,2,1,0:T(8,128)(2,1)S(1)} collective-permute-done((bf16[32,2,16,128]{3,2,1,0:T(8,128)(2,1)S(1)}, bf16[32,2,16,128]{3,2,1,0:T(8,128)(2,1)S(1)}, u32[]{:S(2)}, u32[]{:S(2)}) %collective-permute-start.15) | collective-permute-done | bytes 262176 | tf_op jit(solution)/shard_map/ppermute | solution.py:50
  123.0 2.5 window.3.refs_0_
  125.5 1.6 collective-permute-start.21
  127.1 3.5 collective-permute-start.19
  130.6 2.0 collective-permute-start.18
  134.5 18.2 %collective-permute-done.19.refs_2_ = bf16[32,2,16,128]{3,2,1,0:T(8,128)(2,1)S(1)} collective-permute-done((bf16[32,2,16,128]{3,2,1,0:T(8,128)(2,1)S(1)}, bf16[32,2,16,128]{3,2,1,0:T(8,128)(2,1)S(1)}, u32[]{:S(2)}, u32[]{:S(2)}) %collective-permute-start.19) | collective-permute-done | bytes 262176 | tf_op jit(solution)/shard_map/ppermute | solution.py:50
  153.3 1.5 collective-permute-start.22
  155.3 6.6 %collective-permute-done.23.refs_6_ = bf16[32,2,16,128]{3,2,1,0:T(8,128)(2,1)S(1)} collective-permute-done((bf16[32,2,16,128]{3,2,1,0:T(8,128)(2,1)S(1)}, bf16[32,2,16,128]{3,2,1,0:T(8,128)(2,1)S(1)}, u32[]{:S(2)}, u32[]{:S(2)}) %collective-permute-start.23) | collective-permute-done | bytes 262176 | tf_op jit(solution)/shard_map/ppermute | solution.py:50
  161.9 2.8 collective-permute-done.22.refs_5_
  164.8 1.5 collective-permute-done.30.refs_13_
  166.3 20.3 %correlate.2.refs_3_ = f32[32,2,16,128]{3,2,1,0:T(8,128)S(1)} custom-call(bf16[32,2,16,128]{3,2,1,0:T(8,128)(2,1)S(1)} %window.3.refs_0_, bf16[32,2,16,128]{3,2,1,0:T(8,128)(2,1)S(1)} %collective-permute-done.18.refs_1_, bf16[32,2,16,128]{3,2,1,0:T(8,128)(2,1)S(1)} %collective-permute-done.19.refs_2_, ...), custom_call_target="tpu_custom_call" | custom-call | flops 1073741824 | bytes 37748736 | tf_op jit(solution)/shard_map/correlate/pallas_call | solution.py:183
  186.6 2.4 window.4.spec_ref
  189.0 18.4 %convolve.3 = (bf16[4,32,2,16,128]{4,3,2,1,0:T(8,128)(2,1)S(1)}, bf16[4,32,2,16,128]{4,3,2,1,0:T(8,128)(2,1)S(1)}, bf16[4,32,2,16,128]{4,3,2,1,0:T(8,128)(2,1)S(1)}, bf16[4,32,2,16,128]{4,3,2,1,0:T(8,128)(2,1)S(1)}) custom-call(bf16[32,2,16,128]{3,2,1,0:T(8,128)(2,1)S(1)} %window.4.spec_ref, bf16[2,32,128,2048]{3,2,1,0:T(8,128)(2,1)} %refs_16_.3), custom_call_target="tpu_custom_call" | custom-call | flops 1073741824 | bytes 37748736 | tf_op jit(solution)/shard_map/convolve/pallas_call | solution.py:140
  208.0 2.1 collective-permute-done.34
  211.0 1.5 collective-permute-start.38
  213.1 1.5 collective-permute-start.35
  214.6 5.1 %collective-permute-done.40 = bf16[32,2,16,128]{3,2,1,0:T(8,128)(2,1)S(1)} collective-permute-done((bf16[32,2,16,128]{3,2,1,0:T(8,128)(2,1)S(1)}, bf16[32,2,16,128]{3,2,1,0:T(8,128)(2,1)S(1)}, u32[]{:S(2)}, u32[]{:S(2)}) %collective-permute-start.40) | collective-permute-done | bytes 262176 | tf_op jit(solution)/shard_map/ppermute | solution.py:50
  219.7 5.6 %collective-permute-done.38 = bf16[32,2,16,128]{3,2,1,0:T(8,128)(2,1)S(1)} collective-permute-done((bf16[32,2,16,128]{3,2,1,0:T(8,128)(2,1)S(1)}, bf16[32,2,16,128]{3,2,1,0:T(8,128)(2,1)S(1)}, u32[]{:S(2)}, u32[]{:S(2)}) %collective-permute-start.38) | collective-permute-done | bytes 262176 | tf_op jit(solution)/shard_map/ppermute | solution.py:50
  225.3 5.6 %collective-permute-done.36 = bf16[32,2,16,128]{3,2,1,0:T(8,128)(2,1)S(1)} collective-permute-done((bf16[32,2,16,128]{3,2,1,0:T(8,128)(2,1)S(1)}, bf16[32,2,16,128]{3,2,1,0:T(8,128)(2,1)S(1)}, u32[]{:S(2)}, u32[]{:S(2)}) %collective-permute-start.36) | collective-permute-done | bytes 262176 | tf_op jit(solution)/shard_map/ppermute | solution.py:50
  231.5 6.2 %collective-permute-start.39 = (bf16[32,2,16,128]{3,2,1,0:T(8,128)(2,1)S(1)}, bf16[32,2,16,128]{3,2,1,0:T(8,128)(2,1)S(1)}, u32[]{:S(2)}, u32[]{:S(2)}) collective-permute-start(bf16[32,2,16,128]{3,2,1,0:T(8,128)(2,1)S(1)} %get-tuple-element.31), channel_id=1, source_target_pairs={{0,8},{1,9},{2,10},{3,11},{4,12},{5,13},{6,14},{7,15},{8,0},{9,1},... | collective-permute-start | bytes 786440 | tf_op jit(solution)/shard_map/ppermute | solution.py:50
  237.7 3.5 collective-permute-done.41.refs_8_
  241.2 18.0 %collective-permute-done.39.refs_7_ = bf16[32,2,16,128]{3,2,1,0:T(8,128)(2,1)S(1)} collective-permute-done((bf16[32,2,16,128]{3,2,1,0:T(8,128)(2,1)S(1)}, bf16[32,2,16,128]{3,2,1,0:T(8,128)(2,1)S(1)}, u32[]{:S(2)}, u32[]{:S(2)}) %collective-permute-start.39) | collective-permute-done | bytes 262176 | tf_op jit(solution)/shard_map/ppermute | solution.py:50
  259.2 2.5 window.5
  262.4 2.0 collective-permute-start.42
  264.4 6.1 %collective-permute-done.45.refs_6_ = bf16[16,64,128]{2,1,0:T(8,128)(2,1)S(1)} collective-permute-done((bf16[16,64,128]{2,1,0:T(8,128)(2,1)S(1)}, bf16[16,64,128]{2,1,0:T(8,128)(2,1)S(1)}, u32[]{:S(2)}, u32[]{:S(2)}) %collective-permute-start.45) | collective-permute-done | bytes 262176 | tf_op jit(solution)/shard_map/ppermute | solution.py:50
  273.4 12.5 %collective-permute-done.43.refs_4_ = bf16[16,64,128]{2,1,0:T(8,128)(2,1)S(1)} collective-permute-done((bf16[16,64,128]{2,1,0:T(8,128)(2,1)S(1)}, bf16[16,64,128]{2,1,0:T(8,128)(2,1)S(1)}, u32[]{:S(2)}, u32[]{:S(2)}) %collective-permute-start.43) | collective-permute-done | bytes 262176 | tf_op jit(solution)/shard_map/ppermute | solution.py:50
  285.9 12.3 %collective-permute-start.57 = (bf16[32,2,16,128]{3,2,1,0:T(8,128)(2,1)S(1)}, bf16[32,2,16,128]{3,2,1,0:T(8,128)(2,1)S(1)}, u32[]{:S(2)}, u32[]{:S(2)}) collective-permute-start(bf16[32,2,16,128]{3,2,1,0:T(8,128)(2,1)S(1)} %get-tuple-element.29.refs_0_), channel_id=1, source_target_pairs={{0,4},{1,5},{2,6},{3,7},{4,8},{5,9},{6,10},{7,11},{8,12},{9,13},{1... | collective-permute-start | bytes 786440 | tf_op jit(solution)/shard_map/ppermute | solution.py:50
  300.2 7.7 %collective-permute-done.58.refs_2_ = bf16[32,2,16,128]{3,2,1,0:T(8,128)(2,1)S(1)} collective-permute-done((bf16[32,2,16,128]{3,2,1,0:T(8,128)(2,1)S(1)}, bf16[32,2,16,128]{3,2,1,0:T(8,128)(2,1)S(1)}, u32[]{:S(2)}, u32[]{:S(2)}) %collective-permute-start.58) | collective-permute-done | bytes 262176 | tf_op jit(solution)/shard_map/ppermute | solution.py:50
  312.0 5.2 %collective-permute-done.47.refs_8_ = bf16[16,64,128]{2,1,0:T(8,128)(2,1)S(1)} collective-permute-done((bf16[16,64,128]{2,1,0:T(8,128)(2,1)S(1)}, bf16[16,64,128]{2,1,0:T(8,128)(2,1)S(1)}, u32[]{:S(2)}, u32[]{:S(2)}) %collective-permute-start.47) | collective-permute-done | bytes 262176 | tf_op jit(solution)/shard_map/ppermute | solution.py:50
  318.6 4.2 %collective-permute-done.46.refs_7_ = bf16[16,64,128]{2,1,0:T(8,128)(2,1)S(1)} collective-permute-done((bf16[16,64,128]{2,1,0:T(8,128)(2,1)S(1)}, bf16[16,64,128]{2,1,0:T(8,128)(2,1)S(1)}, u32[]{:S(2)}, u32[]{:S(2)}) %collective-permute-start.46) | collective-permute-done | bytes 262176 | tf_op jit(solution)/shard_map/ppermute | solution.py:50
  324.8 3.6 collective-permute-done.63.refs_7_
  328.4 5.6 %collective-permute-done.62.refs_6_ = bf16[32,2,16,128]{3,2,1,0:T(8,128)(2,1)S(1)} collective-permute-done((bf16[32,2,16,128]{3,2,1,0:T(8,128)(2,1)S(1)}, bf16[32,2,16,128]{3,2,1,0:T(8,128)(2,1)S(1)}, u32[]{:S(2)}, u32[]{:S(2)}) %collective-permute-start.62) | collective-permute-done | bytes 262176 | tf_op jit(solution)/shard_map/ppermute | solution.py:50
  334.0 4.3 %collective-permute-done.61.refs_5_ = bf16[32,2,16,128]{3,2,1,0:T(8,128)(2,1)S(1)} collective-permute-done((bf16[32,2,16,128]{3,2,1,0:T(8,128)(2,1)S(1)}, bf16[32,2,16,128]{3,2,1,0:T(8,128)(2,1)S(1)}, u32[]{:S(2)}, u32[]{:S(2)}) %collective-permute-start.61) | collective-permute-done | bytes 262176 | tf_op jit(solution)/shard_map/ppermute | solution.py:50
  340.0 20.3 %correlate.3 = f32[32,2,16,128]{3,2,1,0:T(8,128)S(1)} custom-call(bf16[32,2,16,128]{3,2,1,0:T(8,128)(2,1)S(1)} %get-tuple-element.29.refs_0_, bf16[32,2,16,128]{3,2,1,0:T(8,128)(2,1)S(1)} %collective-permute-done.57.refs_1_, bf16[32,2,16,128]{3,2,1,0:T(8,128)(2,1)S(1)} %collective-permute-done.58.refs_2_, ...), custom_call_target="tpu_custom_call" | custom-call | flops 1073741824 | bytes 37748736 | tf_op jit(solution)/shard_map/correlate/pallas_call | solution.py:183
  361.3 1.5 collective-permute-start.75
  365.0 1.9 collective-permute-start.73
  367.7 2.2 collective-permute-done.75.refs_6_
  374.0 14.7 %collective-permute-done.73.refs_4_ = bf16[16,64,128]{2,1,0:T(8,128)(2,1)} collective-permute-done((bf16[16,64,128]{2,1,0:T(8,128)(2,1)S(1)}, bf16[16,64,128]{2,1,0:T(8,128)(2,1)}, u32[]{:S(2)}, u32[]{:S(2)}) %collective-permute-start.73) | collective-permute-done | bytes 262176 | tf_op jit(solution)/shard_map/ppermute | solution.py:50
  389.3 1.5 collective-permute-start.76
  392.7 5.6 %collective-permute-done.77.refs_8_ = bf16[16,64,128]{2,1,0:T(8,128)(2,1)} collective-permute-done((bf16[16,64,128]{2,1,0:T(8,128)(2,1)}, bf16[16,64,128]{2,1,0:T(8,128)(2,1)}, u32[]{:S(2)}, u32[]{:S(2)}) %collective-permute-start.77) | collective-permute-done | bytes 262176 | tf_op jit(solution)/shard_map/ppermute | solution.py:50
  398.3 3.8 collective-permute-done.76.refs_7_
  408.0 2.6 field.2
  410.6 4.5 %field.3 = bf16[16,32,2048]{2,1,0:T(8,128)(2,1)} custom-call(bf16[32,64]{1,0:T(8,128)(2,1)S(1)} %bitcast.102, s32[16,2048]{1,0:T(8,128)S(1)} %copy-done.2, bf16[16,64,128]{2,1,0:T(8,128)(2,1)S(1)} %bitcast.100, bf16[16,64,128]{2,1,0:T(8,128)(2,1)} %collective-permute-done.72.refs_3_, bf16[16,64,128]{2,1,0:T(8,128)(2,1)} %collective-permute-done.73.refs_4_, ...), custom_call_target="tpu_custom_call" | custom-call | flops 134217728 | bytes 8388608 | tf_op jit(solution)/shard_map/field/pallas_call | solution.py:286
  (197 shorter events, 48.0 us)
Async XLA Ops:
  7.7 10.0 %collective-permute-start.7 = (bf16[16,64,128]{2,1,0:T(8,128)(2,1)S(1)}, bf16[16,64,128]{2,1,0:T(8,128)(2,1)S(1)}, u32[]{:S(2)}, u32[]{:S(2)}) collective-permute-start(bf16[16,64,128]{2,1,0:T(8,128)(2,1)S(1)} %get-tuple-element.45), channel_id=1, source_target_pairs={{0,2},{1,3},{2,0},{3,1},{4,6},{5,7},{6,4},{7,5},{8,10},{9,11},{10,... | collective-permute-start | bytes 786440 | tf_op jit(solution)/shard_map/ppermute | solution.py:50
  10.7 12.7 %collective-permute-start.5 = (bf16[16,64,128]{2,1,0:T(8,128)(2,1)S(1)}, bf16[16,64,128]{2,1,0:T(8,128)(2,1)S(1)}, u32[]{:S(2)}, u32[]{:S(2)}) collective-permute-start(bf16[16,64,128]{2,1,0:T(8,128)(2,1)S(1)} %get-tuple-element.46), channel_id=1, source_target_pairs={{0,2},{1,3},{2,0},{3,1},{4,6},{5,7},{6,4},{7,5},{8,10},{9,11},{10,... | collective-permute-start | bytes 786440 | tf_op jit(solution)/shard_map/ppermute | solution.py:50
  10.8 18.2 %collective-permute-start.3 = (bf16[16,64,128]{2,1,0:T(8,128)(2,1)S(1)}, bf16[16,64,128]{2,1,0:T(8,128)(2,1)S(1)}, u32[]{:S(2)}, u32[]{:S(2)}) collective-permute-start(bf16[16,64,128]{2,1,0:T(8,128)(2,1)S(1)} %get-tuple-element.47), channel_id=1, source_target_pairs={{0,2},{1,3},{2,0},{3,1},{4,6},{5,7},{6,4},{7,5},{8,10},{9,11},{10,... | collective-permute-start | bytes 786440 | tf_op jit(solution)/shard_map/ppermute | solution.py:50
  12.7 21.9 %collective-permute-start.2 = (bf16[16,64,128]{2,1,0:T(8,128)(2,1)S(1)}, bf16[16,64,128]{2,1,0:T(8,128)(2,1)S(1)}, u32[]{:S(2)}, u32[]{:S(2)}) collective-permute-start(bf16[16,64,128]{2,1,0:T(8,128)(2,1)S(1)} %get-tuple-element.44), channel_id=1, source_target_pairs={{0,2},{1,3},{2,0},{3,1},{4,6},{5,7},{6,4},{7,5},{8,10},{9,11},{10,... | collective-permute-start | bytes 786440 | tf_op jit(solution)/shard_map/ppermute | solution.py:50
  29.4 11.4 %collective-permute-start.4 = (bf16[16,64,128]{2,1,0:T(8,128)(2,1)S(1)}, bf16[16,64,128]{2,1,0:T(8,128)(2,1)S(1)}, u32[]{:S(2)}, u32[]{:S(2)}) collective-permute-start(bf16[16,64,128]{2,1,0:T(8,128)(2,1)S(1)} %get-tuple-element.48), channel_id=1, source_target_pairs={{0,4},{1,5},{2,6},{3,7},{4,8},{5,9},{6,10},{7,11},{8,12},{9,13},{1... | collective-permute-start | bytes 786440 | tf_op jit(solution)/shard_map/ppermute | solution.py:50
  31.6 12.4 %collective-permute-start.8 = (bf16[16,64,128]{2,1,0:T(8,128)(2,1)S(1)}, bf16[16,64,128]{2,1,0:T(8,128)(2,1)S(1)}, u32[]{:S(2)}, u32[]{:S(2)}) collective-permute-start(bf16[16,64,128]{2,1,0:T(8,128)(2,1)S(1)} %get-tuple-element.49), channel_id=1, source_target_pairs={{0,12},{1,13},{2,14},{3,15},{4,0},{5,1},{6,2},{7,3},{8,4},{9,5},{1... | collective-permute-start | bytes 786440 | tf_op jit(solution)/shard_map/ppermute | solution.py:50
  33.7 21.8 %collective-permute-start.6 = (bf16[16,64,128]{2,1,0:T(8,128)(2,1)S(1)}, bf16[16,64,128]{2,1,0:T(8,128)(2,1)S(1)}, u32[]{:S(2)}, u32[]{:S(2)}) collective-permute-start(bf16[16,64,128]{2,1,0:T(8,128)(2,1)S(1)} %get-tuple-element.50), channel_id=1, source_target_pairs={{0,8},{1,9},{2,10},{3,11},{4,12},{5,13},{6,14},{7,15},{8,0},{9,1},... | collective-permute-start | bytes 786440 | tf_op jit(solution)/shard_map/ppermute | solution.py:50
  78.9 9.4 %collective-permute-start.16 = (bf16[32,2,16,128]{3,2,1,0:T(8,128)(2,1)}, bf16[32,2,16,128]{3,2,1,0:T(8,128)(2,1)S(1)}, u32[]{:S(2)}, u32[]{:S(2)}) collective-permute-start(bf16[32,2,16,128]{3,2,1,0:T(8,128)(2,1)} %get-tuple-element.40), channel_id=1, source_target_pairs={{0,2},{1,3},{2,0},{3,1},{4,6},{5,7},{6,4},{7,5},{8,10},{9,11},{10,... | collective-permute-start | bytes 786440 | tf_op jit(solution)/shard_map/ppermute | solution.py:50
  80.3 13.6 %collective-permute-start.14 = (bf16[32,2,16,128]{3,2,1,0:T(8,128)(2,1)}, bf16[32,2,16,128]{3,2,1,0:T(8,128)(2,1)}, u32[]{:S(2)}, u32[]{:S(2)}) collective-permute-start(bf16[32,2,16,128]{3,2,1,0:T(8,128)(2,1)} %get-tuple-element.41), channel_id=1, source_target_pairs={{0,2},{1,3},{2,0},{3,1},{4,6},{5,7},{6,4},{7,5},{8,10},{9,11},{10,... | collective-permute-start | bytes 786440 | tf_op jit(solution)/shard_map/ppermute | solution.py:50
  80.9 18.7 %collective-permute-start.12 = (bf16[32,2,16,128]{3,2,1,0:T(8,128)(2,1)S(1)}, bf16[32,2,16,128]{3,2,1,0:T(8,128)(2,1)}, u32[]{:S(2)}, u32[]{:S(2)}) collective-permute-start(bf16[32,2,16,128]{3,2,1,0:T(8,128)(2,1)S(1)} %get-tuple-element.42), channel_id=1, source_target_pairs={{0,2},{1,3},{2,0},{3,1},{4,6},{5,7},{6,4},{7,5},{8,10},{9,11},{10,... | collective-permute-start | bytes 786440 | tf_op jit(solution)/shard_map/ppermute | solution.py:50
  83.1 21.4 %collective-permute-start.11 = (bf16[32,2,16,128]{3,2,1,0:T(8,128)(2,1)S(1)}, bf16[32,2,16,128]{3,2,1,0:T(8,128)(2,1)S(1)}, u32[]{:S(2)}, u32[]{:S(2)}) collective-permute-start(bf16[32,2,16,128]{3,2,1,0:T(8,128)(2,1)S(1)} %get-tuple-element.43), channel_id=1, source_target_pairs={{0,2},{1,3},{2,0},{3,1},{4,6},{5,7},{6,4},{7,5},{8,10},{9,11},{10,... | collective-permute-start | bytes 786440 | tf_op jit(solution)/shard_map/ppermute | solution.py:50
  102.8 20.2 %collective-permute-start.15 = (bf16[32,2,16,128]{3,2,1,0:T(8,128)(2,1)S(1)}, bf16[32,2,16,128]{3,2,1,0:T(8,128)(2,1)S(1)}, u32[]{:S(2)}, u32[]{:S(2)}) collective-permute-start(bf16[32,2,16,128]{3,2,1,0:T(8,128)(2,1)S(1)} %get-tuple-element.38), channel_id=1, source_target_pairs={{0,8},{1,9},{2,10},{3,11},{4,12},{5,13},{6,14},{7,15},{8,0},{9,1},... | collective-permute-start | bytes 786440 | tf_op jit(solution)/shard_map/ppermute | solution.py:50
  102.8 20.2 %collective-permute-start.13 = (bf16[32,2,16,128]{3,2,1,0:T(8,128)(2,1)S(1)}, bf16[32,2,16,128]{3,2,1,0:T(8,128)(2,1)S(1)}, u32[]{:S(2)}, u32[]{:S(2)}) collective-permute-start(bf16[32,2,16,128]{3,2,1,0:T(8,128)(2,1)S(1)} %get-tuple-element.39), channel_id=1, source_target_pairs={{0,4},{1,5},{2,6},{3,7},{4,8},{5,9},{6,10},{7,11},{8,12},{9,13},{1... | collective-permute-start | bytes 786440 | tf_op jit(solution)/shard_map/ppermute | solution.py:50
  127.1 25.7 %collective-permute-start.19 = (bf16[32,2,16,128]{3,2,1,0:T(8,128)(2,1)S(1)}, bf16[32,2,16,128]{3,2,1,0:T(8,128)(2,1)S(1)}, u32[]{:S(2)}, u32[]{:S(2)}) collective-permute-start(bf16[32,2,16,128]{3,2,1,0:T(8,128)(2,1)S(1)} %window.3.refs_0_), channel_id=1, source_target_pairs={{0,8},{1,9},{2,10},{3,11},{4,12},{5,13},{6,14},{7,15},{8,0},{9,1},... | collective-permute-start | bytes 786440 | tf_op jit(solution)/shard_map/ppermute | solution.py:50
  130.6 22.7 %collective-permute-start.18 = (bf16[32,2,16,128]{3,2,1,0:T(8,128)(2,1)S(1)}, bf16[32,2,16,128]{3,2,1,0:T(8,128)(2,1)S(1)}, u32[]{:S(2)}, u32[]{:S(2)}) collective-permute-start(bf16[32,2,16,128]{3,2,1,0:T(8,128)(2,1)S(1)} %window.3.refs_0_), channel_id=1, source_target_pairs={{0,4},{1,5},{2,6},{3,7},{4,8},{5,9},{6,10},{7,11},{8,12},{9,13},{1... | collective-permute-start | bytes 786440 | tf_op jit(solution)/shard_map/ppermute | solution.py:50
  132.6 22.2 %collective-permute-start.29 = (bf16[32,2,16,128]{3,2,1,0:T(8,128)(2,1)S(1)}, bf16[32,2,16,128]{3,2,1,0:T(8,128)(2,1)S(1)}, u32[]{:S(2)}, u32[]{:S(2)}) collective-permute-start(bf16[32,2,16,128]{3,2,1,0:T(8,128)(2,1)S(1)} %collective-permute-done.21.refs_4_), channel_id=1, source_target_pairs={{0,1},{1,0},{2,3},{3,2},{4,5},{5,4},{6,7},{7,6},{8,9},{9,8},{10,11... | collective-permute-start | bytes 786440 | tf_op jit(solution)/shard_map/ppermute | solution.py:50
  133.9 20.8 %collective-permute-start.28 = (bf16[32,2,16,128]{3,2,1,0:T(8,128)(2,1)S(1)}, bf16[32,2,16,128]{3,2,1,0:T(8,128)(2,1)S(1)}, u32[]{:S(2)}, u32[]{:S(2)}) collective-permute-start(bf16[32,2,16,128]{3,2,1,0:T(8,128)(2,1)S(1)} %collective-permute-done.20.refs_3_), channel_id=1, source_target_pairs={{0,1},{1,0},{2,3},{3,2},{4,5},{5,4},{6,7},{7,6},{8,9},{9,8},{10,11... | collective-permute-start | bytes 786440 | tf_op jit(solution)/shard_map/ppermute | solution.py:50
  134.0 21.3 %collective-permute-start.24 = (bf16[32,2,16,128]{3,2,1,0:T(8,128)(2,1)S(1)}, bf16[32,2,16,128]{3,2,1,0:T(8,128)(2,1)S(1)}, u32[]{:S(2)}, u32[]{:S(2)}) collective-permute-start(bf16[32,2,16,128]{3,2,1,0:T(8,128)(2,1)S(1)} %collective-permute-done.20.refs_3_), channel_id=1, source_target_pairs={{0,2},{1,3},{2,0},{3,1},{4,6},{5,7},{6,4},{7,5},{8,10},{9,11},{10,... | collective-permute-start | bytes 786440 | tf_op jit(solution)/shard_map/ppermute | solution.py:50
  153.3 11.5 %collective-permute-start.22 = (bf16[32,2,16,128]{3,2,1,0:T(8,128)(2,1)S(1)}, bf16[32,2,16,128]{3,2,1,0:T(8,128)(2,1)S(1)}, u32[]{:S(2)}, u32[]{:S(2)}) collective-permute-start(bf16[32,2,16,128]{3,2,1,0:T(8,128)(2,1)S(1)} %collective-permute-done.18.refs_1_), channel_id=1, source_target_pairs={{0,2},{1,3},{2,0},{3,1},{4,6},{5,7},{6,4},{7,5},{8,10},{9,11},{10,... | collective-permute-start | bytes 786440 | tf_op jit(solution)/shard_map/ppermute | solution.py:50
  154.7 10.0 %collective-permute-start.27 = (bf16[32,2,16,128]{3,2,1,0:T(8,128)(2,1)S(1)}, bf16[32,2,16,128]{3,2,1,0:T(8,128)(2,1)S(1)}, u32[]{:S(2)}, u32[]{:S(2)}) collective-permute-start(bf16[32,2,16,128]{3,2,1,0:T(8,128)(2,1)S(1)} %collective-permute-done.19.refs_2_), channel_id=1, source_target_pairs={{0,1},{1,0},{2,3},{3,2},{4,5},{5,4},{6,7},{7,6},{8,9},{9,8},{10,11... | collective-permute-start | bytes 786440 | tf_op jit(solution)/shard_map/ppermute | solution.py:50
  154.8 10.0 %collective-permute-start.26 = (bf16[32,2,16,128]{3,2,1,0:T(8,128)(2,1)S(1)}, bf16[32,2,16,128]{3,2,1,0:T(8,128)(2,1)S(1)}, u32[]{:S(2)}, u32[]{:S(2)}) collective-permute-start(bf16[32,2,16,128]{3,2,1,0:T(8,128)(2,1)S(1)} %collective-permute-done.18.refs_1_), channel_id=1, source_target_pairs={{0,1},{1,0},{2,3},{3,2},{4,5},{5,4},{6,7},{7,6},{8,9},{9,8},{10,11... | collective-permute-start | bytes 786440 | tf_op jit(solution)/shard_map/ppermute | solution.py:50
  155.3 9.5 %collective-permute-start.32 = (bf16[32,2,16,128]{3,2,1,0:T(8,128)(2,1)S(1)}, bf16[32,2,16,128]{3,2,1,0:T(8,128)(2,1)S(1)}, u32[]{:S(2)}, u32[]{:S(2)}) collective-permute-start(bf16[32,2,16,128]{3,2,1,0:T(8,128)(2,1)S(1)} %collective-permute-done.24.refs_7_), channel_id=1, source_target_pairs={{0,1},{1,0},{2,3},{3,2},{4,5},{5,4},{6,7},{7,6},{8,9},{9,8},{10,11... | collective-permute-start | bytes 786440 | tf_op jit(solution)/shard_map/ppermute | solution.py:50
  211.0 14.3 %collective-permute-start.38 = (bf16[32,2,16,128]{3,2,1,0:T(8,128)(2,1)S(1)}, bf16[32,2,16,128]{3,2,1,0:T(8,128)(2,1)S(1)}, u32[]{:S(2)}, u32[]{:S(2)}) collective-permute-start(bf16[32,2,16,128]{3,2,1,0:T(8,128)(2,1)S(1)} %get-tuple-element.34), channel_id=1, source_target_pairs={{0,2},{1,3},{2,0},{3,1},{4,6},{5,7},{6,4},{7,5},{8,10},{9,11},{10,... | collective-permute-start | bytes 786440 | tf_op jit(solution)/shard_map/ppermute | solution.py:50
  212.6 18.4 %collective-permute-start.36 = (bf16[32,2,16,128]{3,2,1,0:T(8,128)(2,1)S(1)}, bf16[32,2,16,128]{3,2,1,0:T(8,128)(2,1)S(1)}, u32[]{:S(2)}, u32[]{:S(2)}) collective-permute-start(bf16[32,2,16,128]{3,2,1,0:T(8,128)(2,1)S(1)} %get-tuple-element.35), channel_id=1, source_target_pairs={{0,2},{1,3},{2,0},{3,1},{4,6},{5,7},{6,4},{7,5},{8,10},{9,11},{10,... | collective-permute-start | bytes 786440 | tf_op jit(solution)/shard_map/ppermute | solution.py:50
  213.1 24.6 %collective-permute-start.35 = (bf16[32,2,16,128]{3,2,1,0:T(8,128)(2,1)S(1)}, bf16[32,2,16,128]{3,2,1,0:T(8,128)(2,1)S(1)}, u32[]{:S(2)}, u32[]{:S(2)}) collective-permute-start(bf16[32,2,16,128]{3,2,1,0:T(8,128)(2,1)S(1)} %get-tuple-element.36), channel_id=1, source_target_pairs={{0,2},{1,3},{2,0},{3,1},{4,6},{5,7},{6,4},{7,5},{8,10},{9,11},{10,... | collective-permute-start | bytes 786440 | tf_op jit(solution)/shard_map/ppermute | solution.py:50
  231.2 9.9 %collective-permute-start.41 = (bf16[32,2,16,128]{3,2,1,0:T(8,128)(2,1)S(1)}, bf16[32,2,16,128]{3,2,1,0:T(8,128)(2,1)S(1)}, u32[]{:S(2)}, u32[]{:S(2)}) collective-permute-start(bf16[32,2,16,128]{3,2,1,0:T(8,128)(2,1)S(1)} %get-tuple-element.30), channel_id=1, source_target_pairs={{0,12},{1,13},{2,14},{3,15},{4,0},{5,1},{6,2},{7,3},{8,4},{9,5},{1... | collective-permute-start | bytes 786440 | tf_op jit(solution)/shard_map/ppermute | solution.py:50
  231.5 27.7 %collective-permute-start.39 = (bf16[32,2,16,128]{3,2,1,0:T(8,128)(2,1)S(1)}, bf16[32,2,16,128]{3,2,1,0:T(8,128)(2,1)S(1)}, u32[]{:S(2)}, u32[]{:S(2)}) collective-permute-start(bf16[32,2,16,128]{3,2,1,0:T(8,128)(2,1)S(1)} %get-tuple-element.31), channel_id=1, source_target_pairs={{0,8},{1,9},{2,10},{3,11},{4,12},{5,13},{6,14},{7,15},{8,0},{9,1},... | collective-permute-start | bytes 786440 | tf_op jit(solution)/shard_map/ppermute | solution.py:50
  237.6 21.5 %collective-permute-start.37 = (bf16[32,2,16,128]{3,2,1,0:T(8,128)(2,1)S(1)}, bf16[32,2,16,128]{3,2,1,0:T(8,128)(2,1)S(1)}, u32[]{:S(2)}, u32[]{:S(2)}) collective-permute-start(bf16[32,2,16,128]{3,2,1,0:T(8,128)(2,1)S(1)} %get-tuple-element.32), channel_id=1, source_target_pairs={{0,4},{1,5},{2,6},{3,7},{4,8},{5,9},{6,10},{7,11},{8,12},{9,13},{1... | collective-permute-start | bytes 786440 | tf_op jit(solution)/shard_map/ppermute | solution.py:50
  262.4 9.7 %collective-permute-start.44 = (bf16[16,64,128]{2,1,0:T(8,128)(2,1)S(1)}, bf16[16,64,128]{2,1,0:T(8,128)(2,1)S(1)}, u32[]{:S(2)}, u32[]{:S(2)}) collective-permute-start(bf16[16,64,128]{2,1,0:T(8,128)(2,1)S(1)} %get-tuple-element.28.refs_2_), channel_id=1, source_target_pairs={{0,12},{1,13},{2,14},{3,15},{4,0},{5,1},{6,2},{7,3},{8,4},{9,5},{1... | collective-permute-start | bytes 786440 | tf_op jit(solution)/shard_map/ppermute | solution.py:50
  262.4 23.5 %collective-permute-start.43 = (bf16[16,64,128]{2,1,0:T(8,128)(2,1)S(1)}, bf16[16,64,128]{2,1,0:T(8,128)(2,1)S(1)}, u32[]{:S(2)}, u32[]{:S(2)}) collective-permute-start(bf16[16,64,128]{2,1,0:T(8,128)(2,1)S(1)} %get-tuple-element.28.refs_2_), channel_id=1, source_target_pairs={{0,8},{1,9},{2,10},{3,11},{4,12},{5,13},{6,14},{7,15},{8,0},{9,1},... | collective-permute-start | bytes 786440 | tf_op jit(solution)/shard_map/ppermute | solution.py:50
  262.4 23.5 %collective-permute-start.42 = (bf16[16,64,128]{2,1,0:T(8,128)(2,1)S(1)}, bf16[16,64,128]{2,1,0:T(8,128)(2,1)S(1)}, u32[]{:S(2)}, u32[]{:S(2)}) collective-permute-start(bf16[16,64,128]{2,1,0:T(8,128)(2,1)S(1)} %get-tuple-element.28.refs_2_), channel_id=1, source_target_pairs={{0,4},{1,5},{2,6},{3,7},{4,8},{5,9},{6,10},{7,11},{8,12},{9,13},{1... | collective-permute-start | bytes 786440 | tf_op jit(solution)/shard_map/ppermute | solution.py:50
  264.4 33.8 %collective-permute-start.64 = (bf16[32,2,16,128]{3,2,1,0:T(8,128)(2,1)S(1)}, bf16[32,2,16,128]{3,2,1,0:T(8,128)(2,1)S(1)}, u32[]{:S(2)}, u32[]{:S(2)}) collective-permute-start(bf16[32,2,16,128]{3,2,1,0:T(8,128)(2,1)S(1)} %get-tuple-element.29.refs_0_), channel_id=1, source_target_pairs={{0,1},{1,0},{2,3},{3,2},{4,5},{5,4},{6,7},{7,6},{8,9},{9,8},{10,11... | collective-permute-start | bytes 786440 | tf_op jit(solution)/shard_map/ppermute | solution.py:50
  270.5 27.8 %collective-permute-start.60 = (bf16[32,2,16,128]{3,2,1,0:T(8,128)(2,1)S(1)}, bf16[32,2,16,128]{3,2,1,0:T(8,128)(2,1)S(1)}, u32[]{:S(2)}, u32[]{:S(2)}) collective-permute-start(bf16[32,2,16,128]{3,2,1,0:T(8,128)(2,1)S(1)} %get-tuple-element.29.refs_0_), channel_id=1, source_target_pairs={{0,2},{1,3},{2,0},{3,1},{4,6},{5,7},{6,4},{7,5},{8,10},{9,11},{10,... | collective-permute-start | bytes 786440 | tf_op jit(solution)/shard_map/ppermute | solution.py:50
  272.0 26.7 %collective-permute-start.59 = (bf16[32,2,16,128]{3,2,1,0:T(8,128)(2,1)S(1)}, bf16[32,2,16,128]{3,2,1,0:T(8,128)(2,1)S(1)}, u32[]{:S(2)}, u32[]{:S(2)}) collective-permute-start(bf16[32,2,16,128]{3,2,1,0:T(8,128)(2,1)S(1)} %get-tuple-element.29.refs_0_), channel_id=1, source_target_pairs={{0,12},{1,13},{2,14},{3,15},{4,0},{5,1},{6,2},{7,3},{8,4},{9,5},{1... | collective-permute-start | bytes 786440 | tf_op jit(solution)/shard_map/ppermute | solution.py:50
  285.9 22.0 %collective-permute-start.58 = (bf16[32,2,16,128]{3,2,1,0:T(8,128)(2,1)S(1)}, bf16[32,2,16,128]{3,2,1,0:T(8,128)(2,1)S(1)}, u32[]{:S(2)}, u32[]{:S(2)}) collective-permute-start(bf16[32,2,16,128]{3,2,1,0:T(8,128)(2,1)S(1)} %get-tuple-element.29.refs_0_), channel_id=1, source_target_pairs={{0,8},{1,9},{2,10},{3,11},{4,12},{5,13},{6,14},{7,15},{8,0},{9,1},... | collective-permute-start | bytes 786440 | tf_op jit(solution)/shard_map/ppermute | solution.py:50
  285.9 23.5 %collective-permute-start.57 = (bf16[32,2,16,128]{3,2,1,0:T(8,128)(2,1)S(1)}, bf16[32,2,16,128]{3,2,1,0:T(8,128)(2,1)S(1)}, u32[]{:S(2)}, u32[]{:S(2)}) collective-permute-start(bf16[32,2,16,128]{3,2,1,0:T(8,128)(2,1)S(1)} %get-tuple-element.29.refs_0_), channel_id=1, source_target_pairs={{0,4},{1,5},{2,6},{3,7},{4,8},{5,9},{6,10},{7,11},{8,12},{9,13},{1... | collective-permute-start | bytes 786440 | tf_op jit(solution)/shard_map/ppermute | solution.py:50
  298.2 11.7 %collective-permute-start.53 = (bf16[16,64,128]{2,1,0:T(8,128)(2,1)S(1)}, bf16[16,64,128]{2,1,0:T(8,128)(2,1)S(1)}, u32[]{:S(2)}, u32[]{:S(2)}) collective-permute-start(bf16[16,64,128]{2,1,0:T(8,128)(2,1)S(1)} %collective-permute-done.45.refs_6_), channel_id=1, source_target_pairs={{0,1},{1,0},{2,3},{3,2},{4,5},{5,4},{6,7},{7,6},{8,9},{9,8},{10,11... | collective-permute-start | bytes 786440 | tf_op jit(solution)/shard_map/ppermute | solution.py:50
  298.2 11.7 %collective-permute-start.52 = (bf16[16,64,128]{2,1,0:T(8,128)(2,1)S(1)}, bf16[16,64,128]{2,1,0:T(8,128)(2,1)S(1)}, u32[]{:S(2)}, u32[]{:S(2)}) collective-permute-start(bf16[16,64,128]{2,1,0:T(8,128)(2,1)S(1)} %collective-permute-done.44.refs_5_), channel_id=1, source_target_pairs={{0,1},{1,0},{2,3},{3,2},{4,5},{5,4},{6,7},{7,6},{8,9},{9,8},{10,11... | collective-permute-start | bytes 786440 | tf_op jit(solution)/shard_map/ppermute | solution.py:50
  298.8 11.7 %collective-permute-start.48 = (bf16[16,64,128]{2,1,0:T(8,128)(2,1)S(1)}, bf16[16,64,128]{2,1,0:T(8,128)(2,1)S(1)}, u32[]{:S(2)}, u32[]{:S(2)}) collective-permute-start(bf16[16,64,128]{2,1,0:T(8,128)(2,1)S(1)} %collective-permute-done.44.refs_5_), channel_id=1, source_target_pairs={{0,2},{1,3},{2,0},{3,1},{4,6},{5,7},{6,4},{7,5},{8,10},{9,11},{10,... | collective-permute-start | bytes 786440 | tf_op jit(solution)/shard_map/ppermute | solution.py:50
  309.4 13.4 %collective-permute-start.46 = (bf16[16,64,128]{2,1,0:T(8,128)(2,1)S(1)}, bf16[16,64,128]{2,1,0:T(8,128)(2,1)S(1)}, u32[]{:S(2)}, u32[]{:S(2)}) collective-permute-start(bf16[16,64,128]{2,1,0:T(8,128)(2,1)S(1)} %collective-permute-done.42.refs_3_), channel_id=1, source_target_pairs={{0,2},{1,3},{2,0},{3,1},{4,6},{5,7},{6,4},{7,5},{8,10},{9,11},{10,... | collective-permute-start | bytes 786440 | tf_op jit(solution)/shard_map/ppermute | solution.py:50
  310.0 14.3 %collective-permute-start.68 = (bf16[32,2,16,128]{3,2,1,0:T(8,128)(2,1)S(1)}, bf16[32,2,16,128]{3,2,1,0:T(8,128)(2,1)S(1)}, u32[]{:S(2)}, u32[]{:S(2)}) collective-permute-start(bf16[32,2,16,128]{3,2,1,0:T(8,128)(2,1)S(1)} %collective-permute-done.60.refs_4_), channel_id=1, source_target_pairs={{0,1},{1,0},{2,3},{3,2},{4,5},{5,4},{6,7},{7,6},{8,9},{9,8},{10,11... | collective-permute-start | bytes 786440 | tf_op jit(solution)/shard_map/ppermute | solution.py:50
  310.0 14.3 %collective-permute-start.67 = (bf16[32,2,16,128]{3,2,1,0:T(8,128)(2,1)S(1)}, bf16[32,2,16,128]{3,2,1,0:T(8,128)(2,1)S(1)}, u32[]{:S(2)}, u32[]{:S(2)}) collective-permute-start(bf16[32,2,16,128]{3,2,1,0:T(8,128)(2,1)S(1)} %collective-permute-done.59.refs_3_), channel_id=1, source_target_pairs={{0,1},{1,0},{2,3},{3,2},{4,5},{5,4},{6,7},{7,6},{8,9},{9,8},{10,11... | collective-permute-start | bytes 786440 | tf_op jit(solution)/shard_map/ppermute | solution.py:50
  310.5 17.9 %collective-permute-start.63 = (bf16[32,2,16,128]{3,2,1,0:T(8,128)(2,1)S(1)}, bf16[32,2,16,128]{3,2,1,0:T(8,128)(2,1)S(1)}, u32[]{:S(2)}, u32[]{:S(2)}) collective-permute-start(bf16[32,2,16,128]{3,2,1,0:T(8,128)(2,1)S(1)} %collective-permute-done.59.refs_3_), channel_id=1, source_target_pairs={{0,2},{1,3},{2,0},{3,1},{4,6},{5,7},{6,4},{7,5},{8,10},{9,11},{10,... | collective-permute-start | bytes 786440 | tf_op jit(solution)/shard_map/ppermute | solution.py:50
  317.2 16.9 %collective-permute-start.62 = (bf16[32,2,16,128]{3,2,1,0:T(8,128)(2,1)S(1)}, bf16[32,2,16,128]{3,2,1,0:T(8,128)(2,1)S(1)}, u32[]{:S(2)}, u32[]{:S(2)}) collective-permute-start(bf16[32,2,16,128]{3,2,1,0:T(8,128)(2,1)S(1)} %collective-permute-done.58.refs_2_), channel_id=1, source_target_pairs={{0,2},{1,3},{2,0},{3,1},{4,6},{5,7},{6,4},{7,5},{8,10},{9,11},{10,... | collective-permute-start | bytes 786440 | tf_op jit(solution)/shard_map/ppermute | solution.py:50
  322.8 15.5 %collective-permute-start.61 = (bf16[32,2,16,128]{3,2,1,0:T(8,128)(2,1)S(1)}, bf16[32,2,16,128]{3,2,1,0:T(8,128)(2,1)S(1)}, u32[]{:S(2)}, u32[]{:S(2)}) collective-permute-start(bf16[32,2,16,128]{3,2,1,0:T(8,128)(2,1)S(1)} %collective-permute-done.57.refs_1_), channel_id=1, source_target_pairs={{0,2},{1,3},{2,0},{3,1},{4,6},{5,7},{6,4},{7,5},{8,10},{9,11},{10,... | collective-permute-start | bytes 786440 | tf_op jit(solution)/shard_map/ppermute | solution.py:50
  324.2 14.1 %collective-permute-start.66 = (bf16[32,2,16,128]{3,2,1,0:T(8,128)(2,1)S(1)}, bf16[32,2,16,128]{3,2,1,0:T(8,128)(2,1)S(1)}, u32[]{:S(2)}, u32[]{:S(2)}) collective-permute-start(bf16[32,2,16,128]{3,2,1,0:T(8,128)(2,1)S(1)} %collective-permute-done.58.refs_2_), channel_id=1, source_target_pairs={{0,1},{1,0},{2,3},{3,2},{4,5},{5,4},{6,7},{7,6},{8,9},{9,8},{10,11... | collective-permute-start | bytes 786440 | tf_op jit(solution)/shard_map/ppermute | solution.py:50
  324.2 14.6 %collective-permute-start.65 = (bf16[32,2,16,128]{3,2,1,0:T(8,128)(2,1)S(1)}, bf16[32,2,16,128]{3,2,1,0:T(8,128)(2,1)S(1)}, u32[]{:S(2)}, u32[]{:S(2)}) collective-permute-start(bf16[32,2,16,128]{3,2,1,0:T(8,128)(2,1)S(1)} %collective-permute-done.57.refs_1_), channel_id=1, source_target_pairs={{0,1},{1,0},{2,3},{3,2},{4,5},{5,4},{6,7},{7,6},{8,9},{9,8},{10,11... | collective-permute-start | bytes 786440 | tf_op jit(solution)/shard_map/ppermute | solution.py:50
  328.4 10.5 %collective-permute-start.71 = (bf16[32,2,16,128]{3,2,1,0:T(8,128)(2,1)S(1)}, bf16[32,2,16,128]{3,2,1,0:T(8,128)(2,1)S(1)}, u32[]{:S(2)}, u32[]{:S(2)}) collective-permute-start(bf16[32,2,16,128]{3,2,1,0:T(8,128)(2,1)S(1)} %collective-permute-done.63.refs_7_), channel_id=1, source_target_pairs={{0,1},{1,0},{2,3},{3,2},{4,5},{5,4},{6,7},{7,6},{8,9},{9,8},{10,11... | collective-permute-start | bytes 786440 | tf_op jit(solution)/shard_map/ppermute | solution.py:50
  338.3 22.3 %collective-permute-start.51 = (bf16[16,64,128]{2,1,0:T(8,128)(2,1)S(1)}, bf16[16,64,128]{2,1,0:T(8,128)(2,1)S(1)}, u32[]{:S(2)}, u32[]{:S(2)}) collective-permute-start(bf16[16,64,128]{2,1,0:T(8,128)(2,1)S(1)} %collective-permute-done.43.refs_4_), channel_id=1, source_target_pairs={{0,1},{1,0},{2,3},{3,2},{4,5},{5,4},{6,7},{7,6},{8,9},{9,8},{10,11... | collective-permute-start | bytes 786440 | tf_op jit(solution)/shard_map/ppermute | solution.py:50
  338.8 24.0 %collective-permute-start.50 = (bf16[16,64,128]{2,1,0:T(8,128)(2,1)S(1)}, bf16[16,64,128]{2,1,0:T(8,128)(2,1)S(1)}, u32[]{:S(2)}, u32[]{:S(2)}) collective-permute-start(bf16[16,64,128]{2,1,0:T(8,128)(2,1)S(1)} %collective-permute-done.42.refs_3_), channel_id=1, source_target_pairs={{0,1},{1,0},{2,3},{3,2},{4,5},{5,4},{6,7},{7,6},{8,9},{9,8},{10,11... | collective-permute-start | bytes 786440 | tf_op jit(solution)/shard_map/ppermute | solution.py:50
  338.9 24.6 %collective-permute-start.56 = (bf16[16,64,128]{2,1,0:T(8,128)(2,1)S(1)}, bf16[16,64,128]{2,1,0:T(8,128)(2,1)S(1)}, u32[]{:S(2)}, u32[]{:S(2)}) collective-permute-start(bf16[16,64,128]{2,1,0:T(8,128)(2,1)S(1)} %collective-permute-done.48.refs_9_), channel_id=1, source_target_pairs={{0,1},{1,0},{2,3},{3,2},{4,5},{5,4},{6,7},{7,6},{8,9},{9,8},{10,11... | collective-permute-start | bytes 786440 | tf_op jit(solution)/shard_map/ppermute | solution.py:50
  339.3 25.0 %collective-permute-start.55 = (bf16[16,64,128]{2,1,0:T(8,128)(2,1)S(1)}, bf16[16,64,128]{2,1,0:T(8,128)(2,1)S(1)}, u32[]{:S(2)}, u32[]{:S(2)}) collective-permute-start(bf16[16,64,128]{2,1,0:T(8,128)(2,1)S(1)} %collective-permute-done.47.refs_8_), channel_id=1, source_target_pairs={{0,1},{1,0},{2,3},{3,2},{4,5},{5,4},{6,7},{7,6},{8,9},{9,8},{10,11... | collective-permute-start | bytes 786440 | tf_op jit(solution)/shard_map/ppermute | solution.py:50
  339.8 27.1 %collective-permute-start.54 = (bf16[16,64,128]{2,1,0:T(8,128)(2,1)S(1)}, bf16[16,64,128]{2,1,0:T(8,128)(2,1)S(1)}, u32[]{:S(2)}, u32[]{:S(2)}) collective-permute-start(bf16[16,64,128]{2,1,0:T(8,128)(2,1)S(1)} %collective-permute-done.46.refs_7_), channel_id=1, source_target_pairs={{0,1},{1,0},{2,3},{3,2},{4,5},{5,4},{6,7},{7,6},{8,9},{9,8},{10,11... | collective-permute-start | bytes 786440 | tf_op jit(solution)/shard_map/ppermute | solution.py:50
  365.0 23.7 %collective-permute-start.73 = (bf16[16,64,128]{2,1,0:T(8,128)(2,1)S(1)}, bf16[16,64,128]{2,1,0:T(8,128)(2,1)}, u32[]{:S(2)}, u32[]{:S(2)}) collective-permute-start(bf16[16,64,128]{2,1,0:T(8,128)(2,1)S(1)} %bitcast.98), channel_id=1, source_target_pairs={{0,8},{1,9},{2,10},{3,11},{4,12},{5,13},{6,14},{7,15},{8,0},{9,1},... | collective-permute-start | bytes 786440 | tf_op jit(solution)/shard_map/ppermute | solution.py:50
  367.7 21.6 %collective-permute-start.72 = (bf16[16,64,128]{2,1,0:T(8,128)(2,1)S(1)}, bf16[16,64,128]{2,1,0:T(8,128)(2,1)}, u32[]{:S(2)}, u32[]{:S(2)}) collective-permute-start(bf16[16,64,128]{2,1,0:T(8,128)(2,1)S(1)} %bitcast.99), channel_id=1, source_target_pairs={{0,4},{1,5},{2,6},{3,7},{4,8},{5,9},{6,10},{7,11},{8,12},{9,13},{1... | collective-permute-start | bytes 786440 | tf_op jit(solution)/shard_map/ppermute | solution.py:50
  369.9 20.9 %collective-permute-start.83 = (bf16[16,64,128]{2,1,0:T(8,128)(2,1)S(1)}, bf16[16,64,128]{2,1,0:T(8,128)(2,1)S(1)}, u32[]{:S(2)}, u32[]{:S(2)}) collective-permute-start(bf16[16,64,128]{2,1,0:T(8,128)(2,1)S(1)} %collective-permute-done.75.refs_6_), channel_id=1, source_target_pairs={{0,1},{1,0},{2,3},{3,2},{4,5},{5,4},{6,7},{7,6},{8,9},{9,8},{10,11... | collective-permute-start | bytes 786440 | tf_op jit(solution)/shard_map/ppermute | solution.py:50
  371.8 19.7 %collective-permute-start.82 = (bf16[16,64,128]{2,1,0:T(8,128)(2,1)S(1)}, bf16[16,64,128]{2,1,0:T(8,128)(2,1)S(1)}, u32[]{:S(2)}, u32[]{:S(2)}) collective-permute-start(bf16[16,64,128]{2,1,0:T(8,128)(2,1)S(1)} %collective-permute-done.74.refs_5_), channel_id=1, source_target_pairs={{0,1},{1,0},{2,3},{3,2},{4,5},{5,4},{6,7},{7,6},{8,9},{9,8},{10,11... | collective-permute-start | bytes 786440 | tf_op jit(solution)/shard_map/ppermute | solution.py:50
  372.5 20.2 %collective-permute-start.78 = (bf16[16,64,128]{2,1,0:T(8,128)(2,1)S(1)}, bf16[16,64,128]{2,1,0:T(8,128)(2,1)}, u32[]{:S(2)}, u32[]{:S(2)}) collective-permute-start(bf16[16,64,128]{2,1,0:T(8,128)(2,1)S(1)} %collective-permute-done.74.refs_5_), channel_id=1, source_target_pairs={{0,2},{1,3},{2,0},{3,1},{4,6},{5,7},{6,4},{7,5},{8,10},{9,11},{10,... | collective-permute-start | bytes 786440 | tf_op jit(solution)/shard_map/ppermute | solution.py:50
  388.7 9.6 %collective-permute-start.77 = (bf16[16,64,128]{2,1,0:T(8,128)(2,1)}, bf16[16,64,128]{2,1,0:T(8,128)(2,1)}, u32[]{:S(2)}, u32[]{:S(2)}) collective-permute-start(bf16[16,64,128]{2,1,0:T(8,128)(2,1)} %collective-permute-done.73.refs_4_), channel_id=1, source_target_pairs={{0,2},{1,3},{2,0},{3,1},{4,6},{5,7},{6,4},{7,5},{8,10},{9,11},{10,... | collective-permute-start | bytes 786440 | tf_op jit(solution)/shard_map/ppermute | solution.py:50
  389.3 12.8 %collective-permute-start.76 = (bf16[16,64,128]{2,1,0:T(8,128)(2,1)}, bf16[16,64,128]{2,1,0:T(8,128)(2,1)}, u32[]{:S(2)}, u32[]{:S(2)}) collective-permute-start(bf16[16,64,128]{2,1,0:T(8,128)(2,1)} %collective-permute-done.72.refs_3_), channel_id=1, source_target_pairs={{0,2},{1,3},{2,0},{3,1},{4,6},{5,7},{6,4},{7,5},{8,10},{9,11},{10,... | collective-permute-start | bytes 786440 | tf_op jit(solution)/shard_map/ppermute | solution.py:50
  391.5 19.1 %collective-permute-start.81 = (bf16[16,64,128]{2,1,0:T(8,128)(2,1)}, bf16[16,64,128]{2,1,0:T(8,128)(2,1)}, u32[]{:S(2)}, u32[]{:S(2)}) collective-permute-start(bf16[16,64,128]{2,1,0:T(8,128)(2,1)} %collective-permute-done.73.refs_4_), channel_id=1, source_target_pairs={{0,1},{1,0},{2,3},{3,2},{4,5},{5,4},{6,7},{7,6},{8,9},{9,8},{10,11... | collective-permute-start | bytes 786440 | tf_op jit(solution)/shard_map/ppermute | solution.py:50
  392.2 18.4 %collective-permute-start.80 = (bf16[16,64,128]{2,1,0:T(8,128)(2,1)}, bf16[16,64,128]{2,1,0:T(8,128)(2,1)}, u32[]{:S(2)}, u32[]{:S(2)}) collective-permute-start(bf16[16,64,128]{2,1,0:T(8,128)(2,1)} %collective-permute-done.72.refs_3_), channel_id=1, source_target_pairs={{0,1},{1,0},{2,3},{3,2},{4,5},{5,4},{6,7},{7,6},{8,9},{9,8},{10,11... | collective-permute-start | bytes 786440 | tf_op jit(solution)/shard_map/ppermute | solution.py:50
  392.7 17.9 %collective-permute-start.86 = (bf16[16,64,128]{2,1,0:T(8,128)(2,1)}, bf16[16,64,128]{2,1,0:T(8,128)(2,1)}, u32[]{:S(2)}, u32[]{:S(2)}) collective-permute-start(bf16[16,64,128]{2,1,0:T(8,128)(2,1)} %collective-permute-done.78.refs_9_), channel_id=1, source_target_pairs={{0,1},{1,0},{2,3},{3,2},{4,5},{5,4},{6,7},{7,6},{8,9},{9,8},{10,11... | collective-permute-start | bytes 786440 | tf_op jit(solution)/shard_map/ppermute | solution.py:50
  398.3 12.3 %collective-permute-start.85 = (bf16[16,64,128]{2,1,0:T(8,128)(2,1)}, bf16[16,64,128]{2,1,0:T(8,128)(2,1)}, u32[]{:S(2)}, u32[]{:S(2)}) collective-permute-start(bf16[16,64,128]{2,1,0:T(8,128)(2,1)} %collective-permute-done.77.refs_8_), channel_id=1, source_target_pairs={{0,1},{1,0},{2,3},{3,2},{4,5},{5,4},{6,7},{7,6},{8,9},{9,8},{10,11... | collective-permute-start | bytes 786440 | tf_op jit(solution)/shard_map/ppermute | solution.py:50
  (48 other events, 236.8 us)

commit v2 on v1

--- a/solution.py
+++ b/solution.py
@@ -113,79 +113,101 @@
     )(forward, plus_start)
 
 
-def convolve_kernel(line, rows, spec_ref, panel_ref, keep0, keep1, send0, send1):
+def convolve_kernel(line, rows, chips_ref, spec_ref, *refs):
     core = own_place(line)[3]
-    keep, send = (keep0, keep1), (send0, send1)
+    panels, (keep, send) = refs[:line], refs[line:]
     focal = spec_ref.shape[2]
     for w in range(rows):
         real, imag = spec_ref[w, 0], spec_ref[w, 1]
         left = jnp.concatenate(
             [jnp.concatenate([real, -imag], axis=1), jnp.concatenate([imag, real], axis=1)], axis=0
         )
-        for flip, step in relative(line):
-            columns = pl.ds(chip_columns(line, True, flip, step), 2 * LANES)
-            panel = panel_ref[:, w, :, columns].reshape(2 * LANES, 2 * LANES)
+        for step in range(line):
+            panel = panels[step][:, w].reshape(2 * LANES, 2 * LANES)
             block = jnp.dot(left, panel, preferred_element_type=F32)
             mine, theirs = split_cores(core, block.astype(BF16))
-            keep[flip][step, w] = mine.reshape(2, focal, LANES)
-            send[flip][step, w] = theirs.reshape(2, focal, LANES)
-
-
-def convolve(spectrum, reflection, line):
+            keep[step, w] = mine.reshape(2, focal, LANES)
+            send[step, w] = theirs.reshape(2, focal, LANES)
+
+
+def panel_specs(line, rows):
+    def block(step):
+        return pl.BlockSpec((2, rows, LANES, 2 * LANES), lambda i, chips: (0, i, 0, chips[step]))
+
+    return [block(step) for step in range(line)]
+
+
+def chips_of(line, ahead, flip):
+    _, l, m, _ = own_place(line)
+    steps = jnp.arange(line, dtype=jnp.int32)
+    other = (l + steps) % line if ahead else (l - steps + line) % line
+    return other * 2 + (m + flip) % 2
+
+
+def convolve(spectrum, reflection, line, flip):
     focal = spectrum.shape[2]
-    sources = reflection.shape[3]
-    rows = 2
+    sources = reflection.shape[3] // 2
+    rows = 4
     out = jax.ShapeDtypeStruct((line, NFW, 2, focal, LANES), BF16)
-    out_spec = pl.BlockSpec((line, rows, 2, focal, LANES), lambda i: (0, i, 0, 0, 0))
+    out_spec = pl.BlockSpec((line, rows, 2, focal, LANES), lambda i, chips: (0, i, 0, 0, 0))
     return pl.pallas_call(
         functools.partial(convolve_kernel, line, rows),
-        grid=(NFW // rows,),
-        in_specs=[
-            pl.BlockSpec((rows, 2, focal, LANES), lambda i: (i, 0, 0, 0)),
-            pl.BlockSpec((2, rows, LANES, sources), lambda i: (0, i, 0, 0)),
-        ],
-        out_specs=[out_spec] * 4,
-        out_shape=[out] * 4,
+        grid_spec=pltpu.PrefetchScalarGridSpec(
+            num_scalar_prefetch=1,
+            grid=(NFW // rows,),
+            in_specs=[pl.BlockSpec((rows, 2, focal, LANES), lambda i, chips: (i, 0, 0, 0))]
+            + panel_specs(line, rows),
+            out_specs=[out_spec] * 2,
+        ),
+        out_shape=[out] * 2,
         compiler_params=pltpu.CompilerParams(vmem_limit_bytes=24 << 20),
         cost_estimate=pl.CostEstimate(
             flops=8 * NFW * focal * LANES * sources,
             bytes_accessed=4 * NFW * sources * (LANES + focal),
             transcendentals=0,
         ),
-        name="convolve",
-    )(spectrum, reflection)
-
-
-def correlate_kernel(line, rows, *refs):
+        name=f"convolve{flip}",
+    )(chips_of(line, True, flip), spectrum, *[reflection] * line)
+
+
+def correlate_kernel(line, rows, has_base, chips_ref, *refs):
     core = own_place(line)[3]
-    places = relative(line)
-    own, other = refs[: len(places)], refs[len(places) : 2 * len(places)]
-    panel_ref, out_ref = refs[2 * len(places) :]
+    own, other, panels = refs[:line], refs[line : 2 * line], refs[2 * line : 3 * line]
+    base_ref = refs[3 * line] if has_base else None
+    out_ref = refs[-1]
     focal = out_ref.shape[2]
     for w in range(rows):
-        total = jnp.zeros((2 * focal, 2 * LANES), F32)
-        for at, (flip, step) in enumerate(places):
-            columns = pl.ds(chip_columns(line, False, flip, step), 2 * LANES)
-            panel = panel_ref[:, w, :, columns].reshape(2 * LANES, 2 * LANES)
+        total = jnp.zeros((2 * LANES, 2 * focal), F32)
+        for step in range(line):
+            panel = panels[step][:, w].reshape(2 * LANES, 2 * LANES)
             spec = join_cores(
-                core, own[at][w].reshape(2 * focal, LANES), other[at][w].reshape(2 * focal, LANES)
+                core, own[step][w].reshape(2 * focal, LANES), other[step][w].reshape(2 * focal, LANES)
             )
-            total += lax.dot_general(spec, panel, (((1,), (1,)), ((), ())), preferred_element_type=F32)
-        out_ref[w, 0] = total[:focal, :LANES] + total[focal:, LANES:]
-        out_ref[w, 1] = total[focal:, :LANES] - total[:focal, LANES:]
-
-
-def correlate(own, other, reflection, line):
+            total += lax.dot_general(panel, spec, (((1,), (1,)), ((), ())), preferred_element_type=F32)
+        total = total.T
+        real = total[:focal, :LANES] + total[focal:, LANES:]
+        imag = total[focal:, :LANES] - total[:focal, LANES:]
+        if has_base:
+            real += base_ref[w, 0]
+            imag += base_ref[w, 1]
+        out_ref[w, 0] = real
+        out_ref[w, 1] = imag
+
+
+def correlate(own, other, reflection, line, flip, base=None):
     focal = own[0].shape[2]
-    sources = reflection.shape[3]
-    rows = 2
-    spec_block = pl.BlockSpec((rows, 2, focal, LANES), lambda i: (i, 0, 0, 0))
+    sources = reflection.shape[3] // 2
+    rows = 4
+    spec_block = pl.BlockSpec((rows, 2, focal, LANES), lambda i, chips: (i, 0, 0, 0))
+    more = [] if base is None else [base]
     return pl.pallas_call(
-        functools.partial(correlate_kernel, line, rows),
-        grid=(NFW // rows,),
-        in_specs=[spec_block] * (len(own) + len(other))
-        + [pl.BlockSpec((2, rows, LANES, sources), lambda i: (0, i, 0, 0))],
-        out_specs=spec_block,
+        functools.partial(correlate_kernel, line, rows, bool(more)),
+        grid_spec=pltpu.PrefetchScalarGridSpec(
+            num_scalar_prefetch=1,
+            grid=(NFW // rows,),
+            in_specs=[spec_block] * (2 * line) + panel_specs(line, rows) + [spec_block] * len(more),
+            out_specs=spec_block,
+        ),
         out_shape=jax.ShapeDtypeStruct((NFW, 2, focal, LANES), F32),
         compiler_params=pltpu.CompilerParams(vmem_limit_bytes=24 << 20),
         cost_estimate=pl.CostEstimate(
@@ -193,8 +215,8 @@
             bytes_accessed=4 * NFW * sources * (LANES + focal),
             transcendentals=0,
         ),
-        name="correlate",
-    )(*own, *other, reflection)
+        name=f"correlate{flip}",
+    )(chips_of(line, False, flip), *own, *other, *[reflection] * line, *more)
 
 
 def window_kernel(parts, has_base, want_spec, *refs):
@@ -276,12 +298,13 @@
 
 
 def field(own, other, inverse, onset_times, line, plus_start=None):
-    focal, k, _ = own[0].shape
+    focal, k, _ = own[0][0].shape
     samples = inverse.shape[0]
     width = onset_times.shape[1]
     rows = 4
     spec_block = pl.BlockSpec((rows, k, LANES), lambda i: (i, 0, 0))
     wide = pl.BlockSpec((rows, samples, width), lambda i: (i, 0, 0))
+    own, other = sum(own, []), sum(other, [])
     plus = [] if plus_start is None else [plus_start]
     return pl.pallas_call(
         functools.partial(field_kernel, line, rows, bool(plus)),
@@ -311,24 +334,39 @@
     return total
 
 
+def after(value, *others):
+    return lax.optimization_barrier((value, *others))[0]
+
+
+def far_first(line):
+    return sorted(range(line), key=lambda step: -min(step, line - step))
+
+
 def reduce_scatter(places, keep0, keep1, send0, send1):
     got1 = places.send(send1, places.core())
     got0 = places.send(send0, places.core())
-    order = list(range(1, places.line)) + [0]
+    order = far_first(places.line)
     across = {}
+    ready = got1
     for step in order:
-        across[step] = places.send(add(keep1[step], got1[step]).astype(BF16), places.pair())
+        ready = add(keep1[step], after(got1, ready)[step]).astype(BF16)
+        across[step] = places.send(ready, places.pair())
     parts = [keep0[0], got0[0], across[0]]
+    ready = got0
     for step in order[:-1]:
-        summed = add(keep0[step], got0[step], across[step]).astype(BF16)
-        parts.append(places.send(summed, places.shift(step)))
+        ready = add(keep0[step], after(got0, ready)[step], across[step]).astype(BF16)
+        parts.append(places.send(ready, places.shift(step)))
     return parts
 
 
 def all_gather(places, block):
-    line = [block] + [places.send(block, places.shift(step)) for step in range(1, places.line)]
-    own = line + [places.send(piece, places.pair()) for piece in line]
-    other = [places.send(piece, places.core()) for piece in own]
+    near_first = far_first(places.line)[::-1]
+    line = {0: block}
+    for step in near_first[1:]:
+        line[step] = places.send(block, places.shift(step))
+    across = {step: places.send(line[step], places.pair()) for step in near_first}
+    own = [[side[step] for step in range(places.line)] for side in (line, across)]
+    other = [[places.send(piece, places.core()) for piece in side] for side in own]
     return own, other
 
 
@@ -347,12 +385,16 @@
     spectrum_plus = start
     for iteration in range(ITERS):
         last = iteration + 1 == ITERS
-        parts = reduce_scatter(places, *convolve(spectrum_plus, reflection, line))
+        keep1, send1 = convolve(spectrum_plus, reflection, line, 1)
+        keep0, send0 = convolve(after(spectrum_plus, keep1), reflection, line, 0)
+        parts = reduce_scatter(places, keep0, keep1, send0, send1)
         windowed = window(parts, forward, inverse, onset_times, want_spec=last)
         gathered = all_gather(places, windowed[0])
         if last:
             upgoing_spec = all_gather(places, windowed[1])
-        downgoing_spec = correlate(*gathered, reflection, line)
+        own, other = gathered
+        downgoing_spec = correlate(own[0], other[0], reflection, line, 0)
+        downgoing_spec = correlate(own[1], other[1], reflection, line, 1, downgoing_spec)
         if not last:
             (spectrum_plus,) = window([downgoing_spec], forward, inverse, onset_times, base=start)
     upgoing = field(*upgoing_spec, own_inverse, onset_times, line)

time: 417 us -> 401 us (0.962)
  waiting for transfers between devices: 225 us -> 203 us
  starting transfers between devices: 73.7 us -> 64.7 us
  Pallas kernels: 94 us -> 102 us
  other arithmetic: 4.89 us -> 12.1 us
    ppermute x87, waiting for transfers between devices: 225 us -> 203 us  [send(): return lax.ppermute(array, self.axis, pairs)]
    ppermute x87, starting transfers between devices: 73.7 us -> 64.7 us  [send(): return lax.ppermute(array, self.axis, pairs)]
    pallas_call x4 -> x8, Pallas kernels: 77.5 us -> 85.9 us  [the longest x4 44.4 us: correlate(): pl.pallas_call(functools.partial(correlate_kernel, line, rows, bool(more)...]
    convert_element_type x6 -> x21, other arithmetic: 4.07 us -> 10.7 us  [the longest x9 6.01 us: reduce_scatter(): add(keep0[step], after(got0, ready)[step], across[step]).astype(BF16)]
    unnamed x50 -> x48, local copies, waits for them, and re-layouts: 14.4 us -> 13.4 us
  transfers between devices with their start and end apart: 87 -> 87, of which waited for: 39 -> 36; matrix products, arithmetic and copies ran while one was open for 1% -> 3% of each run, Pallas kernels for 6% -> 14%
where the time goes in v2:
time: 401 us; the launch traced here: 399 us
  waiting for transfers between devices  203 us (51%)
  Pallas kernels  102 us (25%)
  starting transfers between devices  64.7 us (16%)
  local copies, waits for them, and re-layouts  15.3 us (4%)
  other arithmetic  12.1 us (3%)
    ppermute x87, waiting for transfers between devices, send(): return lax.ppermute(array, self.axis, pairs)  203 us
    ppermute x87, starting transfers between devices, send(): return lax.ppermute(array, self.axis, pairs)  64.7 us
    pallas_call x4, Pallas kernels, correlate(): pl.pallas_call(functools.partial(correlate_kernel, line, rows, bool(more)...  44.4 us
    pallas_call x4, Pallas kernels, convolve(): pl.pallas_call(functools.partial(convolve_kernel, line, rows), grid_spec=...  41.6 us
    unnamed x48, local copies, waits for them, and re-layouts  13.4 us
  transfers between devices with their start and end apart: 87, of which 36 were waited for; matrix products, arithmetic and copies ran while one was open for 3% of the time, Pallas kernels for 14%

profile of v2, /device:TPU:0, one launch (start us, length us, event | category | flops | bytes accessed | tf_op | source)
XLA Modules:
  0.0 398.8 jit_solution(3565808934677155557)
XLA Ops:
  1.4 1.6 copy-done
  3.0 2.1 first_analysis.1
  5.7 2.2 collective-permute-done.1
  8.0 3.0 collective-permute-start.3
  11.2 2.1 collective-permute-start.7
  13.4 4.6 %collective-permute-done.3 = bf16[16,64,128]{2,1,0:T(8,128)(2,1)S(1)} collective-permute-done((bf16[16,64,128]{2,1,0:T(8,128)(2,1)S(1)}, bf16[16,64,128]{2,1,0:T(8,128)(2,1)S(1)}, u32[]{:S(2)}, u32[]{:S(2)}) %collective-permute-start.3) | collective-permute-done | bytes 262176 | tf_op jit(solution)/shard_map/ppermute | solution.py:50
  18.9 4.8 %collective-permute-done.5 = bf16[16,64,128]{2,1,0:T(8,128)(2,1)S(1)} collective-permute-done((bf16[16,64,128]{2,1,0:T(8,128)(2,1)S(1)}, bf16[16,64,128]{2,1,0:T(8,128)(2,1)S(1)}, u32[]{:S(2)}, u32[]{:S(2)}) %collective-permute-start.5) | collective-permute-done | bytes 262176 | tf_op jit(solution)/shard_map/ppermute | solution.py:50
  24.5 4.8 %collective-permute-done.7 = bf16[16,64,128]{2,1,0:T(8,128)(2,1)S(1)} collective-permute-done((bf16[16,64,128]{2,1,0:T(8,128)(2,1)S(1)}, bf16[16,64,128]{2,1,0:T(8,128)(2,1)S(1)}, u32[]{:S(2)}, u32[]{:S(2)}) %collective-permute-start.7) | collective-permute-done | bytes 262176 | tf_op jit(solution)/shard_map/ppermute | solution.py:50
  30.1 4.1 %collective-permute-start.8 = (bf16[16,64,128]{2,1,0:T(8,128)(2,1)}, bf16[16,64,128]{2,1,0:T(8,128)(2,1)S(1)}, u32[]{:S(2)}, u32[]{:S(2)}) collective-permute-start(bf16[16,64,128]{2,1,0:T(8,128)(2,1)} %fusion.6), channel_id=1, source_target_pairs={{0,12},{1,13},{2,14},{3,15},{4,0},{5,1},{6,2},{7,3},{8,4},{9,5},{1... | collective-permute-start | bytes 786440 | tf_op jit(solution)/shard_map/ppermute | solution.py:50
  35.3 6.0 %collective-permute-done.8 = bf16[16,64,128]{2,1,0:T(8,128)(2,1)S(1)} collective-permute-done((bf16[16,64,128]{2,1,0:T(8,128)(2,1)}, bf16[16,64,128]{2,1,0:T(8,128)(2,1)S(1)}, u32[]{:S(2)}, u32[]{:S(2)}) %collective-permute-start.8) | collective-permute-done | bytes 262176 | tf_op jit(solution)/shard_map/ppermute | solution.py:50
  41.3 6.5 %collective-permute-done.6 = bf16[16,64,128]{2,1,0:T(8,128)(2,1)S(1)} collective-permute-done((bf16[16,64,128]{2,1,0:T(8,128)(2,1)}, bf16[16,64,128]{2,1,0:T(8,128)(2,1)S(1)}, u32[]{:S(2)}, u32[]{:S(2)}) %collective-permute-start.6) | collective-permute-done | bytes 262176 | tf_op jit(solution)/shard_map/ppermute | solution.py:50
  47.8 7.6 %collective-permute-done.4 = bf16[16,64,128]{2,1,0:T(8,128)(2,1)S(1)} collective-permute-done((bf16[16,64,128]{2,1,0:T(8,128)(2,1)}, bf16[16,64,128]{2,1,0:T(8,128)(2,1)S(1)}, u32[]{:S(2)}, u32[]{:S(2)}) %collective-permute-start.4) | collective-permute-done | bytes 262176 | tf_op jit(solution)/shard_map/ppermute | solution.py:50
  55.9 10.7 %convolve1.2 = (bf16[4,32,2,16,128]{4,3,2,1,0:T(8,128)(2,1)S(1)}, bf16[4,32,2,16,128]{4,3,2,1,0:T(8,128)(2,1)}) custom-call(s32[4]{0:T(128)S(1)} %get-tuple-element.86.chips_ref, bf16[32,2,16,128]{3,2,1,0:T(8,128)(2,1)S(1)} %bitcast.90, bf16[2,32,128,2048]{3,2,1,0:T(8,128)(2,1)} %refs_11_.7, bf16[2,32,128,2048]{3,2,1,0:T(8,128)(2,1)} %refs_11_.7, ...), custom_call_target="tpu_custom_call" | custom-call | flops 536870912 | bytes 18874368 | tf_op jit(solution)/shard_map/convolve1/pallas_call | solution.py:153
  66.9 10.7 %convolve0.2 = (bf16[4,32,2,16,128]{4,3,2,1,0:T(8,128)(2,1)S(1)}, bf16[4,32,2,16,128]{4,3,2,1,0:T(8,128)(2,1)}) custom-call(s32[4]{0:T(128)S(1)} %get-tuple-element.87.chips_ref, bf16[32,2,16,128]{3,2,1,0:T(8,128)(2,1)S(1)} %bitcast.91, bf16[2,32,128,2048]{3,2,1,0:T(8,128)(2,1)} %refs_11_.7, bf16[2,32,128,2048]{3,2,1,0:T(8,128)(2,1)} %refs_11_.7, ...), custom_call_target="tpu_custom_call" | custom-call | flops 536870912 | bytes 18874368 | tf_op jit(solution)/shard_map/convolve0/pallas_call | solution.py:153
  79.6 1.6 collective-permute-start.12
  83.8 1.6 collective-permute-start.16
  87.0 1.8 collective-permute-done.12
  90.0 4.4 %collective-permute-done.14 = bf16[32,2,16,128]{3,2,1,0:T(8,128)(2,1)S(1)} collective-permute-done((bf16[32,2,16,128]{3,2,1,0:T(8,128)(2,1)S(1)}, bf16[32,2,16,128]{3,2,1,0:T(8,128)(2,1)S(1)}, u32[]{:S(2)}, u32[]{:S(2)}) %collective-permute-start.14) | collective-permute-done | bytes 262176 | tf_op jit(solution)/shard_map/ppermute | solution.py:50
  95.6 4.5 %collective-permute-done.16 = bf16[32,2,16,128]{3,2,1,0:T(8,128)(2,1)S(1)} collective-permute-done((bf16[32,2,16,128]{3,2,1,0:T(8,128)(2,1)S(1)}, bf16[32,2,16,128]{3,2,1,0:T(8,128)(2,1)S(1)}, u32[]{:S(2)}, u32[]{:S(2)}) %collective-permute-start.16) | collective-permute-done | bytes 262176 | tf_op jit(solution)/shard_map/ppermute | solution.py:50
  101.1 2.7 collective-permute-start.17
  104.8 9.3 %collective-permute-done.17.refs_8_ = bf16[32,2,16,128]{3,2,1,0:T(8,128)(2,1)S(1)} collective-permute-done((bf16[32,2,16,128]{3,2,1,0:T(8,128)(2,1)S(1)}, bf16[32,2,16,128]{3,2,1,0:T(8,128)(2,1)S(1)}, u32[]{:S(2)}, u32[]{:S(2)}) %collective-permute-start.17) | collective-permute-done | bytes 262176 | tf_op jit(solution)/shard_map/ppermute | solution.py:50
  114.2 2.5 window.3.refs_0_
  120.6 4.6 %collective-permute-done.23.refs_3_ = bf16[32,2,16,128]{3,2,1,0:T(8,128)(2,1)S(1)} collective-permute-done((bf16[32,2,16,128]{3,2,1,0:T(8,128)(2,1)S(1)}, bf16[32,2,16,128]{3,2,1,0:T(8,128)(2,1)S(1)}, u32[]{:S(2)}, u32[]{:S(2)}) %collective-permute-start.23) | collective-permute-done | bytes 262176 | tf_op jit(solution)/shard_map/ppermute | solution.py:50
  125.2 1.5 collective-permute-start.24
  126.7 15.1 %collective-permute-done.21.refs_2_ = bf16[32,2,16,128]{3,2,1,0:T(8,128)(2,1)S(1)} collective-permute-done((bf16[32,2,16,128]{3,2,1,0:T(8,128)(2,1)S(1)}, bf16[32,2,16,128]{3,2,1,0:T(8,128)(2,1)S(1)}, u32[]{:S(2)}, u32[]{:S(2)}) %collective-permute-start.21) | collective-permute-done | bytes 262176 | tf_op jit(solution)/shard_map/ppermute | solution.py:50
  144.5 6.5 %collective-permute-done.22.refs_2_ = bf16[32,2,16,128]{3,2,1,0:T(8,128)(2,1)S(1)} collective-permute-done((bf16[32,2,16,128]{3,2,1,0:T(8,128)(2,1)S(1)}, bf16[32,2,16,128]{3,2,1,0:T(8,128)(2,1)S(1)}, u32[]{:S(2)}, u32[]{:S(2)}) %collective-permute-start.22) | collective-permute-done | bytes 262176 | tf_op jit(solution)/shard_map/ppermute | solution.py:50
  150.9 5.2 %collective-permute-done.20.refs_1_ = bf16[32,2,16,128]{3,2,1,0:T(8,128)(2,1)S(1)} collective-permute-done((bf16[32,2,16,128]{3,2,1,0:T(8,128)(2,1)S(1)}, bf16[32,2,16,128]{3,2,1,0:T(8,128)(2,1)S(1)}, u32[]{:S(2)}, u32[]{:S(2)}) %collective-permute-start.20) | collective-permute-done | bytes 262176 | tf_op jit(solution)/shard_map/ppermute | solution.py:50
  156.2 11.1 %correlate0.2.refs_12_ = f32[32,2,16,128]{3,2,1,0:T(8,128)S(1)} custom-call(s32[4]{0:T(128)S(1)} %broadcast_add_fusion.2.chips_ref, bf16[32,2,16,128]{3,2,1,0:T(8,128)(2,1)S(1)} %window.3.refs_0_, bf16[32,2,16,128]{3,2,1,0:T(8,128)(2,1)S(1)} %collective-permute-done.19.refs_1_, bf16[32,2,16,128]{3,2,1,0:T(8,128)(2,1)S(1)} %collective-permute-done.21.refs_2_, ...), custom_call_target="tpu_custom_call" | custom-call | flops 536870912 | bytes 18874368 | tf_op jit(solution)/shard_map/correlate0/pallas_call | solution.py:203
  167.4 11.1 %correlate1.2.refs_3_ = f32[32,2,16,128]{3,2,1,0:T(8,128)S(1)} custom-call(s32[4]{0:T(128)S(1)} %broadcast_add_fusion.1.chips_ref, bf16[32,2,16,128]{3,2,1,0:T(8,128)(2,1)S(1)} %collective-permute-done.18.refs_0_, bf16[32,2,16,128]{3,2,1,0:T(8,128)(2,1)S(1)} %collective-permute-done.20.refs_1_, bf16[32,2,16,128]{3,2,1,0:T(8,128)(2,1)S(1)} %collective-permute-done.22.refs_2_, ...), custom_call_target="tpu_custom_call" | custom-call | flops 536870912 | bytes 18874368 | tf_op jit(solution)/shard_map/correlate1/pallas_call | solution.py:203
  178.5 2.4 window.4.spec_ref
  180.9 10.0 %convolve1.3 = (bf16[4,32,2,16,128]{4,3,2,1,0:T(8,128)(2,1)S(1)}, bf16[4,32,2,16,128]{4,3,2,1,0:T(8,128)(2,1)S(1)}) custom-call(s32[4]{0:T(128)S(1)} %get-tuple-element.86.chips_ref, bf16[32,2,16,128]{3,2,1,0:T(8,128)(2,1)S(1)} %window.4.spec_ref, bf16[2,32,128,2048]{3,2,1,0:T(8,128)(2,1)} %refs_11_.7, bf16[2,32,128,2048]{3,2,1,0:T(8,128)(2,1)} %refs_11_.7, ...), custom_call_target="tpu_custom_call" | custom-call | flops 536870912 | bytes 18874368 | tf_op jit(solution)/shard_map/convolve1/pallas_call | solution.py:153
  191.5 10.0 %convolve0.3 = (bf16[4,32,2,16,128]{4,3,2,1,0:T(8,128)(2,1)S(1)}, bf16[4,32,2,16,128]{4,3,2,1,0:T(8,128)(2,1)S(1)}) custom-call(s32[4]{0:T(128)S(1)} %get-tuple-element.87.chips_ref, bf16[32,2,16,128]{3,2,1,0:T(8,128)(2,1)S(1)} %window.4.spec_ref, bf16[2,32,128,2048]{3,2,1,0:T(8,128)(2,1)} %refs_11_.7, bf16[2,32,128,2048]{3,2,1,0:T(8,128)(2,1)} %refs_11_.7, ...), custom_call_target="tpu_custom_call" | custom-call | flops 536870912 | bytes 18874368 | tf_op jit(solution)/shard_map/convolve0/pallas_call | solution.py:153
  201.7 1.6 collective-permute-start.36
  204.0 1.6 collective-permute-start.40
  206.2 4.6 %collective-permute-done.36 = bf16[32,2,16,128]{3,2,1,0:T(8,128)(2,1)S(1)} collective-permute-done((bf16[32,2,16,128]{3,2,1,0:T(8,128)(2,1)S(1)}, bf16[32,2,16,128]{3,2,1,0:T(8,128)(2,1)S(1)}, u32[]{:S(2)}, u32[]{:S(2)}) %collective-permute-start.36) | collective-permute-done | bytes 262176 | tf_op jit(solution)/shard_map/ppermute | solution.py:50
  211.0 1.7 collective-permute-start.37
  212.7 3.8 collective-permute-done.38
  216.6 1.6 collective-permute-start.39
  218.1 3.9 collective-permute-done.40
  222.3 5.0 %collective-permute-done.35.refs_5_ = bf16[32,2,16,128]{3,2,1,0:T(8,128)(2,1)S(1)} collective-permute-done((bf16[32,2,16,128]{3,2,1,0:T(8,128)(2,1)S(1)}, bf16[32,2,16,128]{3,2,1,0:T(8,128)(2,1)S(1)}, u32[]{:S(2)}, u32[]{:S(2)}) %collective-permute-start.35) | collective-permute-done | bytes 262176 | tf_op jit(solution)/shard_map/ppermute | solution.py:50
  227.3 9.0 %collective-permute-done.41.refs_8_ = bf16[32,2,16,128]{3,2,1,0:T(8,128)(2,1)S(1)} collective-permute-done((bf16[32,2,16,128]{3,2,1,0:T(8,128)(2,1)S(1)}, bf16[32,2,16,128]{3,2,1,0:T(8,128)(2,1)S(1)}, u32[]{:S(2)}, u32[]{:S(2)}) %collective-permute-start.41) | collective-permute-done | bytes 262176 | tf_op jit(solution)/shard_map/ppermute | solution.py:50
  236.3 2.5 window.5
  238.9 1.6 collective-permute-start.45
  240.5 2.1 collective-permute-start.43
  242.9 4.7 %collective-permute-done.45.refs_6_ = bf16[16,64,128]{2,1,0:T(8,128)(2,1)S(1)} collective-permute-done((bf16[16,64,128]{2,1,0:T(8,128)(2,1)S(1)}, bf16[16,64,128]{2,1,0:T(8,128)(2,1)S(1)}, u32[]{:S(2)}, u32[]{:S(2)}) %collective-permute-start.45) | collective-permute-done | bytes 262176 | tf_op jit(solution)/shard_map/ppermute | solution.py:50
  249.0 11.1 %collective-permute-start.60 = (bf16[32,2,16,128]{3,2,1,0:T(8,128)(2,1)S(1)}, bf16[32,2,16,128]{3,2,1,0:T(8,128)(2,1)S(1)}, u32[]{:S(2)}, u32[]{:S(2)}) collective-permute-start(bf16[32,2,16,128]{3,2,1,0:T(8,128)(2,1)S(1)} %get-tuple-element.75.refs_0_), channel_id=1, source_target_pairs={{0,8},{1,9},{2,10},{3,11},{4,12},{5,13},{6,14},{7,15},{8,0},{9,1},... | collective-permute-start | bytes 786440 | tf_op jit(solution)/shard_map/ppermute | solution.py:50
  260.2 14.8 %collective-permute-done.43.refs_4_ = bf16[16,64,128]{2,1,0:T(8,128)(2,1)S(1)} collective-permute-done((bf16[16,64,128]{2,1,0:T(8,128)(2,1)S(1)}, bf16[16,64,128]{2,1,0:T(8,128)(2,1)S(1)}, u32[]{:S(2)}, u32[]{:S(2)}) %collective-permute-start.43) | collective-permute-done | bytes 262176 | tf_op jit(solution)/shard_map/ppermute | solution.py:50
  276.0 12.2 %collective-permute-done.60.refs_2_ = bf16[32,2,16,128]{3,2,1,0:T(8,128)(2,1)S(1)} collective-permute-done((bf16[32,2,16,128]{3,2,1,0:T(8,128)(2,1)S(1)}, bf16[32,2,16,128]{3,2,1,0:T(8,128)(2,1)S(1)}, u32[]{:S(2)}, u32[]{:S(2)}) %collective-permute-start.60) | collective-permute-done | bytes 262176 | tf_op jit(solution)/shard_map/ppermute | solution.py:50
  290.8 1.6 collective-permute-start.63
  292.4 5.1 %collective-permute-done.48.refs_9_ = bf16[16,64,128]{2,1,0:T(8,128)(2,1)S(1)} collective-permute-done((bf16[16,64,128]{2,1,0:T(8,128)(2,1)S(1)}, bf16[16,64,128]{2,1,0:T(8,128)(2,1)S(1)}, u32[]{:S(2)}, u32[]{:S(2)}) %collective-permute-start.48) | collective-permute-done | bytes 262176 | tf_op jit(solution)/shard_map/ppermute | solution.py:50
  297.5 5.6 %collective-permute-done.47.refs_8_ = bf16[16,64,128]{2,1,0:T(8,128)(2,1)S(1)} collective-permute-done((bf16[16,64,128]{2,1,0:T(8,128)(2,1)S(1)}, bf16[16,64,128]{2,1,0:T(8,128)(2,1)S(1)}, u32[]{:S(2)}, u32[]{:S(2)}) %collective-permute-start.47) | collective-permute-done | bytes 262176 | tf_op jit(solution)/shard_map/ppermute | solution.py:50
  303.6 5.1 %collective-permute-done.46.refs_7_ = bf16[16,64,128]{2,1,0:T(8,128)(2,1)S(1)} collective-permute-done((bf16[16,64,128]{2,1,0:T(8,128)(2,1)S(1)}, bf16[16,64,128]{2,1,0:T(8,128)(2,1)S(1)}, u32[]{:S(2)}, u32[]{:S(2)}) %collective-permute-start.46) | collective-permute-done | bytes 262176 | tf_op jit(solution)/shard_map/ppermute | solution.py:50
  309.2 5.1 %collective-permute-done.63.refs_3_ = bf16[32,2,16,128]{3,2,1,0:T(8,128)(2,1)S(1)} collective-permute-done((bf16[32,2,16,128]{3,2,1,0:T(8,128)(2,1)S(1)}, bf16[32,2,16,128]{3,2,1,0:T(8,128)(2,1)S(1)}, u32[]{:S(2)}, u32[]{:S(2)}) %collective-permute-start.63) | collective-permute-done | bytes 262176 | tf_op jit(solution)/shard_map/ppermute | solution.py:50
  314.9 5.1 %collective-permute-done.61.refs_2_ = bf16[32,2,16,128]{3,2,1,0:T(8,128)(2,1)S(1)} collective-permute-done((bf16[32,2,16,128]{3,2,1,0:T(8,128)(2,1)S(1)}, bf16[32,2,16,128]{3,2,1,0:T(8,128)(2,1)S(1)}, u32[]{:S(2)}, u32[]{:S(2)}) %collective-permute-start.61) | collective-permute-done | bytes 262176 | tf_op jit(solution)/shard_map/ppermute | solution.py:50
  320.0 3.9 collective-permute-done.59.refs_1_
  325.5 11.1 %correlate0.3.refs_12_ = f32[32,2,16,128]{3,2,1,0:T(8,128)S(1)} custom-call(s32[4]{0:T(128)S(1)} %broadcast_add_fusion.2.chips_ref, bf16[32,2,16,128]{3,2,1,0:T(8,128)(2,1)S(1)} %get-tuple-element.75.refs_0_, bf16[32,2,16,128]{3,2,1,0:T(8,128)(2,1)S(1)} %collective-permute-done.58.refs_1_, bf16[32,2,16,128]{3,2,1,0:T(8,128)(2,1)S(1)} %collective-permute-done.60.refs_2_, ...), custom_call_target="tpu_custom_call" | custom-call | flops 536870912 | bytes 18874368 | tf_op jit(solution)/shard_map/correlate0/pallas_call | solution.py:203
  336.6 11.1 %correlate1.3 = f32[32,2,16,128]{3,2,1,0:T(8,128)S(1)} custom-call(s32[4]{0:T(128)S(1)} %broadcast_add_fusion.1.chips_ref, bf16[32,2,16,128]{3,2,1,0:T(8,128)(2,1)S(1)} %collective-permute-done.57.refs_0_, bf16[32,2,16,128]{3,2,1,0:T(8,128)(2,1)S(1)} %collective-permute-done.59.refs_1_, bf16[32,2,16,128]{3,2,1,0:T(8,128)(2,1)S(1)} %collective-permute-done.61.refs_2_, ...), custom_call_target="tpu_custom_call" | custom-call | flops 536870912 | bytes 18874368 | tf_op jit(solution)/shard_map/correlate1/pallas_call | solution.py:203
  352.2 2.0 collective-permute-start.72
  354.2 3.2 collective-permute-done.75.refs_6_
  362.5 10.5 %collective-permute-done.73.refs_4_ = bf16[16,64,128]{2,1,0:T(8,128)(2,1)} collective-permute-done((bf16[16,64,128]{2,1,0:T(8,128)(2,1)S(1)}, bf16[16,64,128]{2,1,0:T(8,128)(2,1)}, u32[]{:S(2)}, u32[]{:S(2)}) %collective-permute-start.73) | collective-permute-done | bytes 262176 | tf_op jit(solution)/shard_map/ppermute | solution.py:50
  377.0 5.6 %collective-permute-done.77.refs_8_ = bf16[16,64,128]{2,1,0:T(8,128)(2,1)} collective-permute-done((bf16[16,64,128]{2,1,0:T(8,128)(2,1)}, bf16[16,64,128]{2,1,0:T(8,128)(2,1)}, u32[]{:S(2)}, u32[]{:S(2)}) %collective-permute-start.77) | collective-permute-done | bytes 262176 | tf_op jit(solution)/shard_map/ppermute | solution.py:50
  382.6 4.2 %collective-permute-done.76.refs_7_ = bf16[16,64,128]{2,1,0:T(8,128)(2,1)} collective-permute-done((bf16[16,64,128]{2,1,0:T(8,128)(2,1)}, bf16[16,64,128]{2,1,0:T(8,128)(2,1)}, u32[]{:S(2)}, u32[]{:S(2)}) %collective-permute-start.76) | collective-permute-done | bytes 262176 | tf_op jit(solution)/shard_map/ppermute | solution.py:50
  391.7 2.6 field.2
  394.3 4.5 %field.3 = bf16[16,32,2048]{2,1,0:T(8,128)(2,1)} custom-call(bf16[32,64]{1,0:T(8,128)(2,1)S(1)} %bitcast.103, s32[16,2048]{1,0:T(8,128)S(1)} %copy-done.2, bf16[16,64,128]{2,1,0:T(8,128)(2,1)S(1)} %bitcast.101, bf16[16,64,128]{2,1,0:T(8,128)(2,1)} %collective-permute-done.72.refs_3_, bf16[16,64,128]{2,1,0:T(8,128)(2,1)} %collective-permute-done.73.refs_4_, ...), custom_call_target="tpu_custom_call" | custom-call | flops 134217728 | bytes 8388608 | tf_op jit(solution)/shard_map/field/pallas_call | solution.py:309
  (217 shorter events, 52.7 us)
Async XLA Ops:
  11.0 12.6 %collective-permute-start.5 = (bf16[16,64,128]{2,1,0:T(8,128)(2,1)S(1)}, bf16[16,64,128]{2,1,0:T(8,128)(2,1)S(1)}, u32[]{:S(2)}, u32[]{:S(2)}) collective-permute-start(bf16[16,64,128]{2,1,0:T(8,128)(2,1)S(1)} %fusion.14), channel_id=1, source_target_pairs={{0,2},{1,3},{2,0},{3,1},{4,6},{5,7},{6,4},{7,5},{8,10},{9,11},{10,... | collective-permute-start | bytes 786440 | tf_op jit(solution)/shard_map/ppermute | solution.py:50
  11.2 18.1 %collective-permute-start.7 = (bf16[16,64,128]{2,1,0:T(8,128)(2,1)S(1)}, bf16[16,64,128]{2,1,0:T(8,128)(2,1)S(1)}, u32[]{:S(2)}, u32[]{:S(2)}) collective-permute-start(bf16[16,64,128]{2,1,0:T(8,128)(2,1)S(1)} %fusion.15), channel_id=1, source_target_pairs={{0,2},{1,3},{2,0},{3,1},{4,6},{5,7},{6,4},{7,5},{8,10},{9,11},{10,... | collective-permute-start | bytes 786440 | tf_op jit(solution)/shard_map/ppermute | solution.py:50
  13.3 21.9 %collective-permute-start.2 = (bf16[16,64,128]{2,1,0:T(8,128)(2,1)S(1)}, bf16[16,64,128]{2,1,0:T(8,128)(2,1)S(1)}, u32[]{:S(2)}, u32[]{:S(2)}) collective-permute-start(bf16[16,64,128]{2,1,0:T(8,128)(2,1)S(1)} %fusion.16), channel_id=1, source_target_pairs={{0,2},{1,3},{2,0},{3,1},{4,6},{5,7},{6,4},{7,5},{8,10},{9,11},{10,... | collective-permute-start | bytes 786440 | tf_op jit(solution)/shard_map/ppermute | solution.py:50
  30.1 11.2 %collective-permute-start.8 = (bf16[16,64,128]{2,1,0:T(8,128)(2,1)}, bf16[16,64,128]{2,1,0:T(8,128)(2,1)S(1)}, u32[]{:S(2)}, u32[]{:S(2)}) collective-permute-start(bf16[16,64,128]{2,1,0:T(8,128)(2,1)} %fusion.6), channel_id=1, source_target_pairs={{0,12},{1,13},{2,14},{3,15},{4,0},{5,1},{6,2},{7,3},{8,4},{9,5},{1... | collective-permute-start | bytes 786440 | tf_op jit(solution)/shard_map/ppermute | solution.py:50
  34.2 13.6 %collective-permute-start.6 = (bf16[16,64,128]{2,1,0:T(8,128)(2,1)}, bf16[16,64,128]{2,1,0:T(8,128)(2,1)S(1)}, u32[]{:S(2)}, u32[]{:S(2)}) collective-permute-start(bf16[16,64,128]{2,1,0:T(8,128)(2,1)} %fusion.7), channel_id=1, source_target_pairs={{0,4},{1,5},{2,6},{3,7},{4,8},{5,9},{6,10},{7,11},{8,12},{9,13},{1... | collective-permute-start | bytes 786440 | tf_op jit(solution)/shard_map/ppermute | solution.py:50
  34.2 21.2 %collective-permute-start.4 = (bf16[16,64,128]{2,1,0:T(8,128)(2,1)}, bf16[16,64,128]{2,1,0:T(8,128)(2,1)S(1)}, u32[]{:S(2)}, u32[]{:S(2)}) collective-permute-start(bf16[16,64,128]{2,1,0:T(8,128)(2,1)} %fusion.8), channel_id=1, source_target_pairs={{0,8},{1,9},{2,10},{3,11},{4,12},{5,13},{6,14},{7,15},{8,0},{9,1},... | collective-permute-start | bytes 786440 | tf_op jit(solution)/shard_map/ppermute | solution.py:50
  66.6 12.0 %collective-permute-start.10 = (bf16[4,32,2,16,128]{4,3,2,1,0:T(8,128)(2,1)}, bf16[4,32,2,16,128]{4,3,2,1,0:T(8,128)(2,1)}, u32[]{:S(2)}, u32[]{:S(2)}) collective-permute-start(bf16[4,32,2,16,128]{4,3,2,1,0:T(8,128)(2,1)} %get-tuple-element.54), channel_id=1, source_target_pairs={{0,1},{1,0},{2,3},{3,2},{4,5},{5,4},{6,7},{7,6},{8,9},{9,8},{10,11... | collective-permute-start | bytes 3145736 | tf_op jit(solution)/shard_map/ppermute | solution.py:50
  82.2 12.2 %collective-permute-start.14 = (bf16[32,2,16,128]{3,2,1,0:T(8,128)(2,1)S(1)}, bf16[32,2,16,128]{3,2,1,0:T(8,128)(2,1)S(1)}, u32[]{:S(2)}, u32[]{:S(2)}) collective-permute-start(bf16[32,2,16,128]{3,2,1,0:T(8,128)(2,1)S(1)} %fusion.18), channel_id=1, source_target_pairs={{0,2},{1,3},{2,0},{3,1},{4,6},{5,7},{6,4},{7,5},{8,10},{9,11},{10,... | collective-permute-start | bytes 786440 | tf_op jit(solution)/shard_map/ppermute | solution.py:50
  83.8 16.3 %collective-permute-start.16 = (bf16[32,2,16,128]{3,2,1,0:T(8,128)(2,1)S(1)}, bf16[32,2,16,128]{3,2,1,0:T(8,128)(2,1)S(1)}, u32[]{:S(2)}, u32[]{:S(2)}) collective-permute-start(bf16[32,2,16,128]{3,2,1,0:T(8,128)(2,1)S(1)} %fusion.19), channel_id=1, source_target_pairs={{0,2},{1,3},{2,0},{3,1},{4,6},{5,7},{6,4},{7,5},{8,10},{9,11},{10,... | collective-permute-start | bytes 786440 | tf_op jit(solution)/shard_map/ppermute | solution.py:50
  86.4 18.4 %collective-permute-start.11 = (bf16[32,2,16,128]{3,2,1,0:T(8,128)(2,1)S(1)}, bf16[32,2,16,128]{3,2,1,0:T(8,128)(2,1)S(1)}, u32[]{:S(2)}, u32[]{:S(2)}) collective-permute-start(bf16[32,2,16,128]{3,2,1,0:T(8,128)(2,1)S(1)} %fusion.20), channel_id=1, source_target_pairs={{0,2},{1,3},{2,0},{3,1},{4,6},{5,7},{6,4},{7,5},{8,10},{9,11},{10,... | collective-permute-start | bytes 786440 | tf_op jit(solution)/shard_map/ppermute | solution.py:50
  89.9 24.2 %collective-permute-start.13 = (bf16[32,2,16,128]{3,2,1,0:T(8,128)(2,1)S(1)}, bf16[32,2,16,128]{3,2,1,0:T(8,128)(2,1)S(1)}, u32[]{:S(2)}, u32[]{:S(2)}) collective-permute-start(bf16[32,2,16,128]{3,2,1,0:T(8,128)(2,1)S(1)} %fusion.5), channel_id=1, source_target_pairs={{0,8},{1,9},{2,10},{3,11},{4,12},{5,13},{6,14},{7,15},{8,0},{9,1},... | collective-permute-start | bytes 786440 | tf_op jit(solution)/shard_map/ppermute | solution.py:50
  95.5 18.7 %collective-permute-start.15 = (bf16[32,2,16,128]{3,2,1,0:T(8,128)(2,1)S(1)}, bf16[32,2,16,128]{3,2,1,0:T(8,128)(2,1)S(1)}, u32[]{:S(2)}, u32[]{:S(2)}) collective-permute-start(bf16[32,2,16,128]{3,2,1,0:T(8,128)(2,1)S(1)} %fusion.4), channel_id=1, source_target_pairs={{0,4},{1,5},{2,6},{3,7},{4,8},{5,9},{6,10},{7,11},{8,12},{9,13},{1... | collective-permute-start | bytes 786440 | tf_op jit(solution)/shard_map/ppermute | solution.py:50
  101.1 13.0 %collective-permute-start.17 = (bf16[32,2,16,128]{3,2,1,0:T(8,128)(2,1)S(1)}, bf16[32,2,16,128]{3,2,1,0:T(8,128)(2,1)S(1)}, u32[]{:S(2)}, u32[]{:S(2)}) collective-permute-start(bf16[32,2,16,128]{3,2,1,0:T(8,128)(2,1)S(1)} %fusion.3), channel_id=1, source_target_pairs={{0,12},{1,13},{2,14},{3,15},{4,0},{5,1},{6,2},{7,3},{8,4},{9,5},{1... | collective-permute-start | bytes 786440 | tf_op jit(solution)/shard_map/ppermute | solution.py:50
  117.9 23.9 %collective-permute-start.21 = (bf16[32,2,16,128]{3,2,1,0:T(8,128)(2,1)S(1)}, bf16[32,2,16,128]{3,2,1,0:T(8,128)(2,1)S(1)}, u32[]{:S(2)}, u32[]{:S(2)}) collective-permute-start(bf16[32,2,16,128]{3,2,1,0:T(8,128)(2,1)S(1)} %window.3.refs_0_), channel_id=1, source_target_pairs={{0,8},{1,9},{2,10},{3,11},{4,12},{5,13},{6,14},{7,15},{8,0},{9,1},... | collective-permute-start | bytes 786440 | tf_op jit(solution)/shard_map/ppermute | solution.py:50
  118.8 23.1 %collective-permute-start.19 = (bf16[32,2,16,128]{3,2,1,0:T(8,128)(2,1)S(1)}, bf16[32,2,16,128]{3,2,1,0:T(8,128)(2,1)S(1)}, u32[]{:S(2)}, u32[]{:S(2)}) collective-permute-start(bf16[32,2,16,128]{3,2,1,0:T(8,128)(2,1)S(1)} %window.3.refs_0_), channel_id=1, source_target_pairs={{0,4},{1,5},{2,6},{3,7},{4,8},{5,9},{6,10},{7,11},{8,12},{9,13},{1... | collective-permute-start | bytes 786440 | tf_op jit(solution)/shard_map/ppermute | solution.py:50
  119.1 24.3 %collective-permute-start.18 = (bf16[32,2,16,128]{3,2,1,0:T(8,128)(2,1)S(1)}, bf16[32,2,16,128]{3,2,1,0:T(8,128)(2,1)S(1)}, u32[]{:S(2)}, u32[]{:S(2)}) collective-permute-start(bf16[32,2,16,128]{3,2,1,0:T(8,128)(2,1)S(1)} %window.3.refs_0_), channel_id=1, source_target_pairs={{0,2},{1,3},{2,0},{3,1},{4,6},{5,7},{6,4},{7,5},{8,10},{9,11},{10,... | collective-permute-start | bytes 786440 | tf_op jit(solution)/shard_map/ppermute | solution.py:50
  125.2 18.7 %collective-permute-start.32 = (bf16[32,2,16,128]{3,2,1,0:T(8,128)(2,1)S(1)}, bf16[32,2,16,128]{3,2,1,0:T(8,128)(2,1)S(1)}, u32[]{:S(2)}, u32[]{:S(2)}) collective-permute-start(bf16[32,2,16,128]{3,2,1,0:T(8,128)(2,1)S(1)} %collective-permute-done.23.refs_3_), channel_id=1, source_target_pairs={{0,1},{1,0},{2,3},{3,2},{4,5},{5,4},{6,7},{7,6},{8,9},{9,8},{10,11... | collective-permute-start | bytes 786440 | tf_op jit(solution)/shard_map/ppermute | solution.py:50
  125.2 18.7 %collective-permute-start.24 = (bf16[32,2,16,128]{3,2,1,0:T(8,128)(2,1)S(1)}, bf16[32,2,16,128]{3,2,1,0:T(8,128)(2,1)S(1)}, u32[]{:S(2)}, u32[]{:S(2)}) collective-permute-start(bf16[32,2,16,128]{3,2,1,0:T(8,128)(2,1)S(1)} %collective-permute-done.23.refs_3_), channel_id=1, source_target_pairs={{0,2},{1,3},{2,0},{3,1},{4,6},{5,7},{6,4},{7,5},{8,10},{9,11},{10,... | collective-permute-start | bytes 786440 | tf_op jit(solution)/shard_map/ppermute | solution.py:50
  143.4 12.8 %collective-permute-start.20 = (bf16[32,2,16,128]{3,2,1,0:T(8,128)(2,1)S(1)}, bf16[32,2,16,128]{3,2,1,0:T(8,128)(2,1)S(1)}, u32[]{:S(2)}, u32[]{:S(2)}) collective-permute-start(bf16[32,2,16,128]{3,2,1,0:T(8,128)(2,1)S(1)} %collective-permute-done.19.refs_1_), channel_id=1, source_target_pairs={{0,2},{1,3},{2,0},{3,1},{4,6},{5,7},{6,4},{7,5},{8,10},{9,11},{10,... | collective-permute-start | bytes 786440 | tf_op jit(solution)/shard_map/ppermute | solution.py:50
  143.9 12.3 %collective-permute-start.30 = (bf16[32,2,16,128]{3,2,1,0:T(8,128)(2,1)S(1)}, bf16[32,2,16,128]{3,2,1,0:T(8,128)(2,1)S(1)}, u32[]{:S(2)}, u32[]{:S(2)}) collective-permute-start(bf16[32,2,16,128]{3,2,1,0:T(8,128)(2,1)S(1)} %collective-permute-done.19.refs_1_), channel_id=1, source_target_pairs={{0,1},{1,0},{2,3},{3,2},{4,5},{5,4},{6,7},{7,6},{8,9},{9,8},{10,11... | collective-permute-start | bytes 786440 | tf_op jit(solution)/shard_map/ppermute | solution.py:50
  143.9 23.4 %collective-permute-start.25 = (bf16[32,2,16,128]{3,2,1,0:T(8,128)(2,1)S(1)}, bf16[32,2,16,128]{3,2,1,0:T(8,128)(2,1)S(1)}, u32[]{:S(2)}, u32[]{:S(2)}) collective-permute-start(bf16[32,2,16,128]{3,2,1,0:T(8,128)(2,1)S(1)} %collective-permute-done.18.refs_0_), channel_id=1, source_target_pairs={{0,1},{1,0},{2,3},{3,2},{4,5},{5,4},{6,7},{7,6},{8,9},{9,8},{10,11... | collective-permute-start | bytes 786440 | tf_op jit(solution)/shard_map/ppermute | solution.py:50
  144.4 23.0 %collective-permute-start.28 = (bf16[32,2,16,128]{3,2,1,0:T(8,128)(2,1)S(1)}, bf16[32,2,16,128]{3,2,1,0:T(8,128)(2,1)S(1)}, u32[]{:S(2)}, u32[]{:S(2)}) collective-permute-start(bf16[32,2,16,128]{3,2,1,0:T(8,128)(2,1)S(1)} %collective-permute-done.24.refs_3_), channel_id=1, source_target_pairs={{0,1},{1,0},{2,3},{3,2},{4,5},{5,4},{6,7},{7,6},{8,9},{9,8},{10,11... | collective-permute-start | bytes 786440 | tf_op jit(solution)/shard_map/ppermute | solution.py:50
  150.9 16.4 %collective-permute-start.27 = (bf16[32,2,16,128]{3,2,1,0:T(8,128)(2,1)S(1)}, bf16[32,2,16,128]{3,2,1,0:T(8,128)(2,1)S(1)}, u32[]{:S(2)}, u32[]{:S(2)}) collective-permute-start(bf16[32,2,16,128]{3,2,1,0:T(8,128)(2,1)S(1)} %collective-permute-done.22.refs_2_), channel_id=1, source_target_pairs={{0,1},{1,0},{2,3},{3,2},{4,5},{5,4},{6,7},{7,6},{8,9},{9,8},{10,11... | collective-permute-start | bytes 786440 | tf_op jit(solution)/shard_map/ppermute | solution.py:50
  156.2 11.2 %collective-permute-start.26 = (bf16[32,2,16,128]{3,2,1,0:T(8,128)(2,1)S(1)}, bf16[32,2,16,128]{3,2,1,0:T(8,128)(2,1)S(1)}, u32[]{:S(2)}, u32[]{:S(2)}) collective-permute-start(bf16[32,2,16,128]{3,2,1,0:T(8,128)(2,1)S(1)} %collective-permute-done.20.refs_1_), channel_id=1, source_target_pairs={{0,1},{1,0},{2,3},{3,2},{4,5},{5,4},{6,7},{7,6},{8,9},{9,8},{10,11... | collective-permute-start | bytes 786440 | tf_op jit(solution)/shard_map/ppermute | solution.py:50
  190.9 10.7 %collective-permute-start.34 = (bf16[4,32,2,16,128]{4,3,2,1,0:T(8,128)(2,1)S(1)}, bf16[4,32,2,16,128]{4,3,2,1,0:T(8,128)(2,1)S(1)}, u32[]{:S(2)}, u32[]{:S(2)}) collective-permute-start(bf16[4,32,2,16,128]{4,3,2,1,0:T(8,128)(2,1)S(1)} %get-tuple-element.66), channel_id=1, source_target_pairs={{0,1},{1,0},{2,3},{3,2},{4,5},{5,4},{6,7},{7,6},{8,9},{9,8},{10,11... | collective-permute-start | bytes 3145736 | tf_op jit(solution)/shard_map/ppermute | solution.py:50
  203.3 13.1 %collective-permute-start.38 = (bf16[32,2,16,128]{3,2,1,0:T(8,128)(2,1)S(1)}, bf16[32,2,16,128]{3,2,1,0:T(8,128)(2,1)S(1)}, u32[]{:S(2)}, u32[]{:S(2)}) collective-permute-start(bf16[32,2,16,128]{3,2,1,0:T(8,128)(2,1)S(1)} %fusion.22), channel_id=1, source_target_pairs={{0,2},{1,3},{2,0},{3,1},{4,6},{5,7},{6,4},{7,5},{8,10},{9,11},{10,... | collective-permute-start | bytes 786440 | tf_op jit(solution)/shard_map/ppermute | solution.py:50
  204.0 18.1 %collective-permute-start.40 = (bf16[32,2,16,128]{3,2,1,0:T(8,128)(2,1)S(1)}, bf16[32,2,16,128]{3,2,1,0:T(8,128)(2,1)S(1)}, u32[]{:S(2)}, u32[]{:S(2)}) collective-permute-start(bf16[32,2,16,128]{3,2,1,0:T(8,128)(2,1)S(1)} %fusion.23), channel_id=1, source_target_pairs={{0,2},{1,3},{2,0},{3,1},{4,6},{5,7},{6,4},{7,5},{8,10},{9,11},{10,... | collective-permute-start | bytes 786440 | tf_op jit(solution)/shard_map/ppermute | solution.py:50
  205.7 21.6 %collective-permute-start.35 = (bf16[32,2,16,128]{3,2,1,0:T(8,128)(2,1)S(1)}, bf16[32,2,16,128]{3,2,1,0:T(8,128)(2,1)S(1)}, u32[]{:S(2)}, u32[]{:S(2)}) collective-permute-start(bf16[32,2,16,128]{3,2,1,0:T(8,128)(2,1)S(1)} %fusion.24), channel_id=1, source_target_pairs={{0,2},{1,3},{2,0},{3,1},{4,6},{5,7},{6,4},{7,5},{8,10},{9,11},{10,... | collective-permute-start | bytes 786440 | tf_op jit(solution)/shard_map/ppermute | solution.py:50
  211.0 25.3 %collective-permute-start.37 = (bf16[32,2,16,128]{3,2,1,0:T(8,128)(2,1)S(1)}, bf16[32,2,16,128]{3,2,1,0:T(8,128)(2,1)S(1)}, u32[]{:S(2)}, u32[]{:S(2)}) collective-permute-start(bf16[32,2,16,128]{3,2,1,0:T(8,128)(2,1)S(1)} %fusion.2), channel_id=1, source_target_pairs={{0,8},{1,9},{2,10},{3,11},{4,12},{5,13},{6,14},{7,15},{8,0},{9,1},... | collective-permute-start | bytes 786440 | tf_op jit(solution)/shard_map/ppermute | solution.py:50
  216.6 19.7 %collective-permute-start.39 = (bf16[32,2,16,128]{3,2,1,0:T(8,128)(2,1)S(1)}, bf16[32,2,16,128]{3,2,1,0:T(8,128)(2,1)S(1)}, u32[]{:S(2)}, u32[]{:S(2)}) collective-permute-start(bf16[32,2,16,128]{3,2,1,0:T(8,128)(2,1)S(1)} %fusion.1), channel_id=1, source_target_pairs={{0,4},{1,5},{2,6},{3,7},{4,8},{5,9},{6,10},{7,11},{8,12},{9,13},{1... | collective-permute-start | bytes 786440 | tf_op jit(solution)/shard_map/ppermute | solution.py:50
  222.2 14.1 %collective-permute-start.41 = (bf16[32,2,16,128]{3,2,1,0:T(8,128)(2,1)S(1)}, bf16[32,2,16,128]{3,2,1,0:T(8,128)(2,1)S(1)}, u32[]{:S(2)}, u32[]{:S(2)}) collective-permute-start(bf16[32,2,16,128]{3,2,1,0:T(8,128)(2,1)S(1)} %fusion), channel_id=1, source_target_pairs={{0,12},{1,13},{2,14},{3,15},{4,0},{5,1},{6,2},{7,3},{8,4},{9,5},{1... | collective-permute-start | bytes 786440 | tf_op jit(solution)/shard_map/ppermute | solution.py:50
  240.5 34.5 %collective-permute-start.43 = (bf16[16,64,128]{2,1,0:T(8,128)(2,1)S(1)}, bf16[16,64,128]{2,1,0:T(8,128)(2,1)S(1)}, u32[]{:S(2)}, u32[]{:S(2)}) collective-permute-start(bf16[16,64,128]{2,1,0:T(8,128)(2,1)S(1)} %get-tuple-element.74.refs_2_), channel_id=1, source_target_pairs={{0,8},{1,9},{2,10},{3,11},{4,12},{5,13},{6,14},{7,15},{8,0},{9,1},... | collective-permute-start | bytes 786440 | tf_op jit(solution)/shard_map/ppermute | solution.py:50
  242.5 32.4 %collective-permute-start.42 = (bf16[16,64,128]{2,1,0:T(8,128)(2,1)S(1)}, bf16[16,64,128]{2,1,0:T(8,128)(2,1)S(1)}, u32[]{:S(2)}, u32[]{:S(2)}) collective-permute-start(bf16[16,64,128]{2,1,0:T(8,128)(2,1)S(1)} %get-tuple-element.74.refs_2_), channel_id=1, source_target_pairs={{0,4},{1,5},{2,6},{3,7},{4,8},{5,9},{6,10},{7,11},{8,12},{9,13},{1... | collective-permute-start | bytes 786440 | tf_op jit(solution)/shard_map/ppermute | solution.py:50
  242.9 32.6 %collective-permute-start.68 = (bf16[32,2,16,128]{3,2,1,0:T(8,128)(2,1)S(1)}, bf16[32,2,16,128]{3,2,1,0:T(8,128)(2,1)S(1)}, u32[]{:S(2)}, u32[]{:S(2)}) collective-permute-start(bf16[32,2,16,128]{3,2,1,0:T(8,128)(2,1)S(1)} %get-tuple-element.75.refs_0_), channel_id=1, source_target_pairs={{0,1},{1,0},{2,3},{3,2},{4,5},{5,4},{6,7},{7,6},{8,9},{9,8},{10,11... | collective-permute-start | bytes 786440 | tf_op jit(solution)/shard_map/ppermute | solution.py:50
  247.6 27.9 %collective-permute-start.62 = (bf16[32,2,16,128]{3,2,1,0:T(8,128)(2,1)S(1)}, bf16[32,2,16,128]{3,2,1,0:T(8,128)(2,1)S(1)}, u32[]{:S(2)}, u32[]{:S(2)}) collective-permute-start(bf16[32,2,16,128]{3,2,1,0:T(8,128)(2,1)S(1)} %get-tuple-element.75.refs_0_), channel_id=1, source_target_pairs={{0,12},{1,13},{2,14},{3,15},{4,0},{5,1},{6,2},{7,3},{8,4},{9,5},{1... | collective-permute-start | bytes 786440 | tf_op jit(solution)/shard_map/ppermute | solution.py:50
  249.0 39.2 %collective-permute-start.60 = (bf16[32,2,16,128]{3,2,1,0:T(8,128)(2,1)S(1)}, bf16[32,2,16,128]{3,2,1,0:T(8,128)(2,1)S(1)}, u32[]{:S(2)}, u32[]{:S(2)}) collective-permute-start(bf16[32,2,16,128]{3,2,1,0:T(8,128)(2,1)S(1)} %get-tuple-element.75.refs_0_), channel_id=1, source_target_pairs={{0,8},{1,9},{2,10},{3,11},{4,12},{5,13},{6,14},{7,15},{8,0},{9,1},... | collective-permute-start | bytes 786440 | tf_op jit(solution)/shard_map/ppermute | solution.py:50
  275.0 13.8 %collective-permute-start.58 = (bf16[32,2,16,128]{3,2,1,0:T(8,128)(2,1)S(1)}, bf16[32,2,16,128]{3,2,1,0:T(8,128)(2,1)S(1)}, u32[]{:S(2)}, u32[]{:S(2)}) collective-permute-start(bf16[32,2,16,128]{3,2,1,0:T(8,128)(2,1)S(1)} %get-tuple-element.75.refs_0_), channel_id=1, source_target_pairs={{0,4},{1,5},{2,6},{3,7},{4,8},{5,9},{6,10},{7,11},{8,12},{9,13},{1... | collective-permute-start | bytes 786440 | tf_op jit(solution)/shard_map/ppermute | solution.py:50
  275.0 15.3 %collective-permute-start.57 = (bf16[32,2,16,128]{3,2,1,0:T(8,128)(2,1)S(1)}, bf16[32,2,16,128]{3,2,1,0:T(8,128)(2,1)S(1)}, u32[]{:S(2)}, u32[]{:S(2)}) collective-permute-start(bf16[32,2,16,128]{3,2,1,0:T(8,128)(2,1)S(1)} %get-tuple-element.75.refs_0_), channel_id=1, source_target_pairs={{0,2},{1,3},{2,0},{3,1},{4,6},{5,7},{6,4},{7,5},{8,10},{9,11},{10,... | collective-permute-start | bytes 786440 | tf_op jit(solution)/shard_map/ppermute | solution.py:50
  275.5 15.3 %collective-permute-start.53 = (bf16[16,64,128]{2,1,0:T(8,128)(2,1)S(1)}, bf16[16,64,128]{2,1,0:T(8,128)(2,1)S(1)}, u32[]{:S(2)}, u32[]{:S(2)}) collective-permute-start(bf16[16,64,128]{2,1,0:T(8,128)(2,1)S(1)} %collective-permute-done.45.refs_6_), channel_id=1, source_target_pairs={{0,1},{1,0},{2,3},{3,2},{4,5},{5,4},{6,7},{7,6},{8,9},{9,8},{10,11... | collective-permute-start | bytes 786440 | tf_op jit(solution)/shard_map/ppermute | solution.py:50
  275.5 15.3 %collective-permute-start.52 = (bf16[16,64,128]{2,1,0:T(8,128)(2,1)S(1)}, bf16[16,64,128]{2,1,0:T(8,128)(2,1)S(1)}, u32[]{:S(2)}, u32[]{:S(2)}) collective-permute-start(bf16[16,64,128]{2,1,0:T(8,128)(2,1)S(1)} %collective-permute-done.44.refs_5_), channel_id=1, source_target_pairs={{0,1},{1,0},{2,3},{3,2},{4,5},{5,4},{6,7},{7,6},{8,9},{9,8},{10,11... | collective-permute-start | bytes 786440 | tf_op jit(solution)/shard_map/ppermute | solution.py:50
  288.8 14.3 %collective-permute-start.47 = (bf16[16,64,128]{2,1,0:T(8,128)(2,1)S(1)}, bf16[16,64,128]{2,1,0:T(8,128)(2,1)S(1)}, u32[]{:S(2)}, u32[]{:S(2)}) collective-permute-start(bf16[16,64,128]{2,1,0:T(8,128)(2,1)S(1)} %collective-permute-done.43.refs_4_), channel_id=1, source_target_pairs={{0,2},{1,3},{2,0},{3,1},{4,6},{5,7},{6,4},{7,5},{8,10},{9,11},{10,... | collective-permute-start | bytes 786440 | tf_op jit(solution)/shard_map/ppermute | solution.py:50
  290.3 18.4 %collective-permute-start.46 = (bf16[16,64,128]{2,1,0:T(8,128)(2,1)S(1)}, bf16[16,64,128]{2,1,0:T(8,128)(2,1)S(1)}, u32[]{:S(2)}, u32[]{:S(2)}) collective-permute-start(bf16[16,64,128]{2,1,0:T(8,128)(2,1)S(1)} %collective-permute-done.42.refs_3_), channel_id=1, source_target_pairs={{0,2},{1,3},{2,0},{3,1},{4,6},{5,7},{6,4},{7,5},{8,10},{9,11},{10,... | collective-permute-start | bytes 786440 | tf_op jit(solution)/shard_map/ppermute | solution.py:50
  290.8 18.4 %collective-permute-start.71 = (bf16[32,2,16,128]{3,2,1,0:T(8,128)(2,1)S(1)}, bf16[32,2,16,128]{3,2,1,0:T(8,128)(2,1)S(1)}, u32[]{:S(2)}, u32[]{:S(2)}) collective-permute-start(bf16[32,2,16,128]{3,2,1,0:T(8,128)(2,1)S(1)} %collective-permute-done.62.refs_3_), channel_id=1, source_target_pairs={{0,1},{1,0},{2,3},{3,2},{4,5},{5,4},{6,7},{7,6},{8,9},{9,8},{10,11... | collective-permute-start | bytes 786440 | tf_op jit(solution)/shard_map/ppermute | solution.py:50
  290.8 23.5 %collective-permute-start.63 = (bf16[32,2,16,128]{3,2,1,0:T(8,128)(2,1)S(1)}, bf16[32,2,16,128]{3,2,1,0:T(8,128)(2,1)S(1)}, u32[]{:S(2)}, u32[]{:S(2)}) collective-permute-start(bf16[32,2,16,128]{3,2,1,0:T(8,128)(2,1)S(1)} %collective-permute-done.62.refs_3_), channel_id=1, source_target_pairs={{0,2},{1,3},{2,0},{3,1},{4,6},{5,7},{6,4},{7,5},{8,10},{9,11},{10,... | collective-permute-start | bytes 786440 | tf_op jit(solution)/shard_map/ppermute | solution.py:50
  297.5 16.9 %collective-permute-start.70 = (bf16[32,2,16,128]{3,2,1,0:T(8,128)(2,1)S(1)}, bf16[32,2,16,128]{3,2,1,0:T(8,128)(2,1)S(1)}, u32[]{:S(2)}, u32[]{:S(2)}) collective-permute-start(bf16[32,2,16,128]{3,2,1,0:T(8,128)(2,1)S(1)} %collective-permute-done.60.refs_2_), channel_id=1, source_target_pairs={{0,1},{1,0},{2,3},{3,2},{4,5},{5,4},{6,7},{7,6},{8,9},{9,8},{10,11... | collective-permute-start | bytes 786440 | tf_op jit(solution)/shard_map/ppermute | solution.py:50
  303.1 16.9 %collective-permute-start.61 = (bf16[32,2,16,128]{3,2,1,0:T(8,128)(2,1)S(1)}, bf16[32,2,16,128]{3,2,1,0:T(8,128)(2,1)S(1)}, u32[]{:S(2)}, u32[]{:S(2)}) collective-permute-start(bf16[32,2,16,128]{3,2,1,0:T(8,128)(2,1)S(1)} %collective-permute-done.60.refs_2_), channel_id=1, source_target_pairs={{0,2},{1,3},{2,0},{3,1},{4,6},{5,7},{6,4},{7,5},{8,10},{9,11},{10,... | collective-permute-start | bytes 786440 | tf_op jit(solution)/shard_map/ppermute | solution.py:50
  308.7 15.2 %collective-permute-start.59 = (bf16[32,2,16,128]{3,2,1,0:T(8,128)(2,1)S(1)}, bf16[32,2,16,128]{3,2,1,0:T(8,128)(2,1)S(1)}, u32[]{:S(2)}, u32[]{:S(2)}) collective-permute-start(bf16[32,2,16,128]{3,2,1,0:T(8,128)(2,1)S(1)} %collective-permute-done.58.refs_1_), channel_id=1, source_target_pairs={{0,2},{1,3},{2,0},{3,1},{4,6},{5,7},{6,4},{7,5},{8,10},{9,11},{10,... | collective-permute-start | bytes 786440 | tf_op jit(solution)/shard_map/ppermute | solution.py:50
  309.2 14.7 %collective-permute-start.69 = (bf16[32,2,16,128]{3,2,1,0:T(8,128)(2,1)S(1)}, bf16[32,2,16,128]{3,2,1,0:T(8,128)(2,1)S(1)}, u32[]{:S(2)}, u32[]{:S(2)}) collective-permute-start(bf16[32,2,16,128]{3,2,1,0:T(8,128)(2,1)S(1)} %collective-permute-done.58.refs_1_), channel_id=1, source_target_pairs={{0,1},{1,0},{2,3},{3,2},{4,5},{5,4},{6,7},{7,6},{8,9},{9,8},{10,11... | collective-permute-start | bytes 786440 | tf_op jit(solution)/shard_map/ppermute | solution.py:50
  314.3 10.1 %collective-permute-start.67 = (bf16[32,2,16,128]{3,2,1,0:T(8,128)(2,1)S(1)}, bf16[32,2,16,128]{3,2,1,0:T(8,128)(2,1)S(1)}, u32[]{:S(2)}, u32[]{:S(2)}) collective-permute-start(bf16[32,2,16,128]{3,2,1,0:T(8,128)(2,1)S(1)} %collective-permute-done.63.refs_3_), channel_id=1, source_target_pairs={{0,1},{1,0},{2,3},{3,2},{4,5},{5,4},{6,7},{7,6},{8,9},{9,8},{10,11... | collective-permute-start | bytes 786440 | tf_op jit(solution)/shard_map/ppermute | solution.py:50
  323.9 24.2 %collective-permute-start.51 = (bf16[16,64,128]{2,1,0:T(8,128)(2,1)S(1)}, bf16[16,64,128]{2,1,0:T(8,128)(2,1)S(1)}, u32[]{:S(2)}, u32[]{:S(2)}) collective-permute-start(bf16[16,64,128]{2,1,0:T(8,128)(2,1)S(1)} %collective-permute-done.43.refs_4_), channel_id=1, source_target_pairs={{0,1},{1,0},{2,3},{3,2},{4,5},{5,4},{6,7},{7,6},{8,9},{9,8},{10,11... | collective-permute-start | bytes 786440 | tf_op jit(solution)/shard_map/ppermute | solution.py:50
  324.4 24.9 %collective-permute-start.50 = (bf16[16,64,128]{2,1,0:T(8,128)(2,1)S(1)}, bf16[16,64,128]{2,1,0:T(8,128)(2,1)S(1)}, u32[]{:S(2)}, u32[]{:S(2)}) collective-permute-start(bf16[16,64,128]{2,1,0:T(8,128)(2,1)S(1)} %collective-permute-done.42.refs_3_), channel_id=1, source_target_pairs={{0,1},{1,0},{2,3},{3,2},{4,5},{5,4},{6,7},{7,6},{8,9},{9,8},{10,11... | collective-permute-start | bytes 786440 | tf_op jit(solution)/shard_map/ppermute | solution.py:50
  324.5 25.6 %collective-permute-start.56 = (bf16[16,64,128]{2,1,0:T(8,128)(2,1)S(1)}, bf16[16,64,128]{2,1,0:T(8,128)(2,1)S(1)}, u32[]{:S(2)}, u32[]{:S(2)}) collective-permute-start(bf16[16,64,128]{2,1,0:T(8,128)(2,1)S(1)} %collective-permute-done.48.refs_9_), channel_id=1, source_target_pairs={{0,1},{1,0},{2,3},{3,2},{4,5},{5,4},{6,7},{7,6},{8,9},{9,8},{10,11... | collective-permute-start | bytes 786440 | tf_op jit(solution)/shard_map/ppermute | solution.py:50
  324.9 25.9 %collective-permute-start.55 = (bf16[16,64,128]{2,1,0:T(8,128)(2,1)S(1)}, bf16[16,64,128]{2,1,0:T(8,128)(2,1)S(1)}, u32[]{:S(2)}, u32[]{:S(2)}) collective-permute-start(bf16[16,64,128]{2,1,0:T(8,128)(2,1)S(1)} %collective-permute-done.47.refs_8_), channel_id=1, source_target_pairs={{0,1},{1,0},{2,3},{3,2},{4,5},{5,4},{6,7},{7,6},{8,9},{9,8},{10,11... | collective-permute-start | bytes 786440 | tf_op jit(solution)/shard_map/ppermute | solution.py:50
  325.4 26.1 %collective-permute-start.54 = (bf16[16,64,128]{2,1,0:T(8,128)(2,1)S(1)}, bf16[16,64,128]{2,1,0:T(8,128)(2,1)S(1)}, u32[]{:S(2)}, u32[]{:S(2)}) collective-permute-start(bf16[16,64,128]{2,1,0:T(8,128)(2,1)S(1)} %collective-permute-done.46.refs_7_), channel_id=1, source_target_pairs={{0,1},{1,0},{2,3},{3,2},{4,5},{5,4},{6,7},{7,6},{8,9},{9,8},{10,11... | collective-permute-start | bytes 786440 | tf_op jit(solution)/shard_map/ppermute | solution.py:50
  351.5 21.5 %collective-permute-start.73 = (bf16[16,64,128]{2,1,0:T(8,128)(2,1)S(1)}, bf16[16,64,128]{2,1,0:T(8,128)(2,1)}, u32[]{:S(2)}, u32[]{:S(2)}) collective-permute-start(bf16[16,64,128]{2,1,0:T(8,128)(2,1)S(1)} %bitcast.99), channel_id=1, source_target_pairs={{0,8},{1,9},{2,10},{3,11},{4,12},{5,13},{6,14},{7,15},{8,0},{9,1},... | collective-permute-start | bytes 786440 | tf_op jit(solution)/shard_map/ppermute | solution.py:50
  352.2 22.4 %collective-permute-start.72 = (bf16[16,64,128]{2,1,0:T(8,128)(2,1)S(1)}, bf16[16,64,128]{2,1,0:T(8,128)(2,1)}, u32[]{:S(2)}, u32[]{:S(2)}) collective-permute-start(bf16[16,64,128]{2,1,0:T(8,128)(2,1)S(1)} %bitcast.100), channel_id=1, source_target_pairs={{0,4},{1,5},{2,6},{3,7},{4,8},{5,9},{6,10},{7,11},{8,12},{9,13},{1... | collective-permute-start | bytes 786440 | tf_op jit(solution)/shard_map/ppermute | solution.py:50
  357.4 17.7 %collective-permute-start.83 = (bf16[16,64,128]{2,1,0:T(8,128)(2,1)S(1)}, bf16[16,64,128]{2,1,0:T(8,128)(2,1)S(1)}, u32[]{:S(2)}, u32[]{:S(2)}) collective-permute-start(bf16[16,64,128]{2,1,0:T(8,128)(2,1)S(1)} %collective-permute-done.75.refs_6_), channel_id=1, source_target_pairs={{0,1},{1,0},{2,3},{3,2},{4,5},{5,4},{6,7},{7,6},{8,9},{9,8},{10,11... | collective-permute-start | bytes 786440 | tf_op jit(solution)/shard_map/ppermute | solution.py:50
  359.6 16.2 %collective-permute-start.82 = (bf16[16,64,128]{2,1,0:T(8,128)(2,1)S(1)}, bf16[16,64,128]{2,1,0:T(8,128)(2,1)S(1)}, u32[]{:S(2)}, u32[]{:S(2)}) collective-permute-start(bf16[16,64,128]{2,1,0:T(8,128)(2,1)S(1)} %collective-permute-done.74.refs_5_), channel_id=1, source_target_pairs={{0,1},{1,0},{2,3},{3,2},{4,5},{5,4},{6,7},{7,6},{8,9},{9,8},{10,11... | collective-permute-start | bytes 786440 | tf_op jit(solution)/shard_map/ppermute | solution.py:50
  360.3 16.7 %collective-permute-start.78 = (bf16[16,64,128]{2,1,0:T(8,128)(2,1)S(1)}, bf16[16,64,128]{2,1,0:T(8,128)(2,1)}, u32[]{:S(2)}, u32[]{:S(2)}) collective-permute-start(bf16[16,64,128]{2,1,0:T(8,128)(2,1)S(1)} %collective-permute-done.74.refs_5_), channel_id=1, source_target_pairs={{0,2},{1,3},{2,0},{3,1},{4,6},{5,7},{6,4},{7,5},{8,10},{9,11},{10,... | collective-permute-start | bytes 786440 | tf_op jit(solution)/shard_map/ppermute | solution.py:50
  374.6 12.2 %collective-permute-start.76 = (bf16[16,64,128]{2,1,0:T(8,128)(2,1)}, bf16[16,64,128]{2,1,0:T(8,128)(2,1)}, u32[]{:S(2)}, u32[]{:S(2)}) collective-permute-start(bf16[16,64,128]{2,1,0:T(8,128)(2,1)} %collective-permute-done.72.refs_3_), channel_id=1, source_target_pairs={{0,2},{1,3},{2,0},{3,1},{4,6},{5,7},{6,4},{7,5},{8,10},{9,11},{10,... | collective-permute-start | bytes 786440 | tf_op jit(solution)/shard_map/ppermute | solution.py:50
  375.8 18.4 %collective-permute-start.81 = (bf16[16,64,128]{2,1,0:T(8,128)(2,1)}, bf16[16,64,128]{2,1,0:T(8,128)(2,1)}, u32[]{:S(2)}, u32[]{:S(2)}) collective-permute-start(bf16[16,64,128]{2,1,0:T(8,128)(2,1)} %collective-permute-done.73.refs_4_), channel_id=1, source_target_pairs={{0,1},{1,0},{2,3},{3,2},{4,5},{5,4},{6,7},{7,6},{8,9},{9,8},{10,11... | collective-permute-start | bytes 786440 | tf_op jit(solution)/shard_map/ppermute | solution.py:50
  376.5 17.7 %collective-permute-start.80 = (bf16[16,64,128]{2,1,0:T(8,128)(2,1)}, bf16[16,64,128]{2,1,0:T(8,128)(2,1)}, u32[]{:S(2)}, u32[]{:S(2)}) collective-permute-start(bf16[16,64,128]{2,1,0:T(8,128)(2,1)} %collective-permute-done.72.refs_3_), channel_id=1, source_target_pairs={{0,1},{1,0},{2,3},{3,2},{4,5},{5,4},{6,7},{7,6},{8,9},{9,8},{10,11... | collective-permute-start | bytes 786440 | tf_op jit(solution)/shard_map/ppermute | solution.py:50
  377.0 17.2 %collective-permute-start.86 = (bf16[16,64,128]{2,1,0:T(8,128)(2,1)}, bf16[16,64,128]{2,1,0:T(8,128)(2,1)}, u32[]{:S(2)}, u32[]{:S(2)}) collective-permute-start(bf16[16,64,128]{2,1,0:T(8,128)(2,1)} %collective-permute-done.78.refs_9_), channel_id=1, source_target_pairs={{0,1},{1,0},{2,3},{3,2},{4,5},{5,4},{6,7},{7,6},{8,9},{9,8},{10,11... | collective-permute-start | bytes 786440 | tf_op jit(solution)/shard_map/ppermute | solution.py:50
  382.6 11.6 %collective-permute-start.85 = (bf16[16,64,128]{2,1,0:T(8,128)(2,1)}, bf16[16,64,128]{2,1,0:T(8,128)(2,1)}, u32[]{:S(2)}, u32[]{:S(2)}) collective-permute-start(bf16[16,64,128]{2,1,0:T(8,128)(2,1)} %collective-permute-done.77.refs_8_), channel_id=1, source_target_pairs={{0,1},{1,0},{2,3},{3,2},{4,5},{5,4},{6,7},{7,6},{8,9},{9,8},{10,11... | collective-permute-start | bytes 786440 | tf_op jit(solution)/shard_map/ppermute | solution.py:50
  (47 other events, 276.5 us)

commit v3 on v2

--- a/solution.py
+++ b/solution.py
@@ -103,7 +103,7 @@
         ],
         out_specs=[out_spec] * 4,
         out_shape=[out] * 4,
-        compiler_params=pltpu.CompilerParams(vmem_limit_bytes=24 << 20),
+        compiler_params=pltpu.CompilerParams(vmem_limit_bytes=16 << 20),
         cost_estimate=pl.CostEstimate(
             flops=4 * NFW * focal * samples * width,
             bytes_accessed=2 * focal * samples * width + 4 * NFW * focal * width,
@@ -113,73 +113,93 @@
     )(forward, plus_start)
 
 
-def convolve_kernel(line, rows, chips_ref, spec_ref, *refs):
+def convolve_kernel(line, flip, spec_ref, panel_ref, keep, send):
     core = own_place(line)[3]
-    panels, (keep, send) = refs[:line], refs[line:]
     focal = spec_ref.shape[2]
-    for w in range(rows):
+
+    def body(w, carry):
         real, imag = spec_ref[w, 0], spec_ref[w, 1]
         left = jnp.concatenate(
             [jnp.concatenate([real, -imag], axis=1), jnp.concatenate([imag, real], axis=1)], axis=0
         )
         for step in range(line):
-            panel = panels[step][:, w].reshape(2 * LANES, 2 * LANES)
+            columns = pl.ds(chip_columns(line, True, flip, step), 2 * LANES)
+            panel = panel_ref[:, w, :, columns].reshape(2 * LANES, 2 * LANES)
             block = jnp.dot(left, panel, preferred_element_type=F32)
             mine, theirs = split_cores(core, block.astype(BF16))
             keep[step, w] = mine.reshape(2, focal, LANES)
             send[step, w] = theirs.reshape(2, focal, LANES)
-
-
-def panel_specs(line, rows):
-    def block(step):
-        return pl.BlockSpec((2, rows, LANES, 2 * LANES), lambda i, chips: (0, i, 0, chips[step]))
-
-    return [block(step) for step in range(line)]
-
-
-def chips_of(line, ahead, flip):
-    _, l, m, _ = own_place(line)
-    steps = jnp.arange(line, dtype=jnp.int32)
-    other = (l + steps) % line if ahead else (l - steps + line) % line
-    return other * 2 + (m + flip) % 2
+        return carry
+
+    lax.fori_loop(0, NFW, body, 0, unroll=2)
+
+
+VMEM = pl.BlockSpec(memory_space=pltpu.VMEM)
+SMALL = pltpu.CompilerParams(vmem_limit_bytes=12 << 20)
+
+
+def hold_kernel(parts, source, target, sems):
+    depth = source.shape[1] // parts
+    copies = [
+        pltpu.make_async_copy(
+            source.at[:, pl.ds(i * depth, depth)], target.at[:, pl.ds(i * depth, depth)], sems.at[i]
+        )
+        for i in range(parts)
+    ]
+    for copy in copies:
+        copy.start()
+    for copy in copies:
+        copy.wait()
+
+
+def hold(reflection):
+    parts = 8
+    return pl.pallas_call(
+        functools.partial(hold_kernel, parts),
+        in_specs=[pl.BlockSpec(memory_space=pl.ANY)],
+        out_specs=VMEM,
+        out_shape=jax.ShapeDtypeStruct(reflection.shape, reflection.dtype),
+        scratch_shapes=[pltpu.SemaphoreType.DMA((parts,))],
+        compiler_params=SMALL,
+        cost_estimate=pl.CostEstimate(flops=0, bytes_accessed=2 * reflection.size, transcendentals=0),
+        name="hold",
+    )(reflection)
+
+
+def panel_cost(focal, sources):
+    return pl.CostEstimate(
+        flops=8 * NFW * focal * LANES * sources,
+        bytes_accessed=4 * NFW * sources * (LANES + focal),
+        transcendentals=0,
+    )
 
 
 def convolve(spectrum, reflection, line, flip):
     focal = spectrum.shape[2]
-    sources = reflection.shape[3] // 2
-    rows = 4
     out = jax.ShapeDtypeStruct((line, NFW, 2, focal, LANES), BF16)
-    out_spec = pl.BlockSpec((line, rows, 2, focal, LANES), lambda i, chips: (0, i, 0, 0, 0))
-    return pl.pallas_call(
-        functools.partial(convolve_kernel, line, rows),
-        grid_spec=pltpu.PrefetchScalarGridSpec(
-            num_scalar_prefetch=1,
-            grid=(NFW // rows,),
-            in_specs=[pl.BlockSpec((rows, 2, focal, LANES), lambda i, chips: (i, 0, 0, 0))]
-            + panel_specs(line, rows),
-            out_specs=[out_spec] * 2,
-        ),
+    return pl.pallas_call(
+        functools.partial(convolve_kernel, line, flip),
+        in_specs=[VMEM] * 2,
+        out_specs=[VMEM] * 2,
         out_shape=[out] * 2,
-        compiler_params=pltpu.CompilerParams(vmem_limit_bytes=24 << 20),
-        cost_estimate=pl.CostEstimate(
-            flops=8 * NFW * focal * LANES * sources,
-            bytes_accessed=4 * NFW * sources * (LANES + focal),
-            transcendentals=0,
-        ),
+        compiler_params=SMALL,
+        cost_estimate=panel_cost(focal, reflection.shape[3] // 2),
         name=f"convolve{flip}",
-    )(chips_of(line, True, flip), spectrum, *[reflection] * line)
-
-
-def correlate_kernel(line, rows, has_base, chips_ref, *refs):
+    )(spectrum, reflection)
+
+
+def correlate_kernel(line, flip, has_base, *refs):
     core = own_place(line)[3]
-    own, other, panels = refs[:line], refs[line : 2 * line], refs[2 * line : 3 * line]
-    base_ref = refs[3 * line] if has_base else None
+    own, other, panel_ref = refs[:line], refs[line : 2 * line], refs[2 * line]
+    base_ref = refs[2 * line + 1] if has_base else None
     out_ref = refs[-1]
     focal = out_ref.shape[2]
-    for w in range(rows):
+
+    def body(w, carry):
         total = jnp.zeros((2 * LANES, 2 * focal), F32)
         for step in range(line):
-            panel = panels[step][:, w].reshape(2 * LANES, 2 * LANES)
+            columns = pl.ds(chip_columns(line, False, flip, step), 2 * LANES)
+            panel = panel_ref[:, w, :, columns].reshape(2 * LANES, 2 * LANES)
             spec = join_cores(
                 core, own[step][w].reshape(2 * focal, LANES), other[step][w].reshape(2 * focal, LANES)
             )
@@ -192,31 +212,23 @@
             imag += base_ref[w, 1]
         out_ref[w, 0] = real
         out_ref[w, 1] = imag
+        return carry
+
+    lax.fori_loop(0, NFW, body, 0, unroll=2)
 
 
 def correlate(own, other, reflection, line, flip, base=None):
     focal = own[0].shape[2]
-    sources = reflection.shape[3] // 2
-    rows = 4
-    spec_block = pl.BlockSpec((rows, 2, focal, LANES), lambda i, chips: (i, 0, 0, 0))
     more = [] if base is None else [base]
     return pl.pallas_call(
-        functools.partial(correlate_kernel, line, rows, bool(more)),
-        grid_spec=pltpu.PrefetchScalarGridSpec(
-            num_scalar_prefetch=1,
-            grid=(NFW // rows,),
-            in_specs=[spec_block] * (2 * line) + panel_specs(line, rows) + [spec_block] * len(more),
-            out_specs=spec_block,
-        ),
+        functools.partial(correlate_kernel, line, flip, bool(more)),
+        in_specs=[VMEM] * (2 * line + 1 + len(more)),
+        out_specs=VMEM,
         out_shape=jax.ShapeDtypeStruct((NFW, 2, focal, LANES), F32),
-        compiler_params=pltpu.CompilerParams(vmem_limit_bytes=24 << 20),
-        cost_estimate=pl.CostEstimate(
-            flops=8 * NFW * focal * LANES * sources,
-            bytes_accessed=4 * NFW * sources * (LANES + focal),
-            transcendentals=0,
-        ),
+        compiler_params=SMALL,
+        cost_estimate=panel_cost(focal, reflection.shape[3] // 2),
         name=f"correlate{flip}",
-    )(chips_of(line, False, flip), *own, *other, *[reflection] * line, *more)
+    )(*own, *other, reflection, *more)
 
 
 def window_kernel(parts, has_base, want_spec, *refs):
@@ -268,7 +280,7 @@
         out_specs=[whole] * len(out),
         out_shape=out,
         scratch_shapes=[pltpu.VMEM((k * focal, LANES), F32)] * 2,
-        compiler_params=pltpu.CompilerParams(vmem_limit_bytes=24 << 20),
+        compiler_params=pltpu.CompilerParams(vmem_limit_bytes=16 << 20),
         cost_estimate=pl.CostEstimate(
             flops=4 * k * NT * focal * LANES, bytes_accessed=2 * k * focal * LANES * 6, transcendentals=0
         ),
@@ -317,7 +329,7 @@
         + [wide] * len(plus),
         out_specs=wide,
         out_shape=jax.ShapeDtypeStruct((focal, samples, width), BF16),
-        compiler_params=pltpu.CompilerParams(vmem_limit_bytes=24 << 20),
+        compiler_params=pltpu.CompilerParams(vmem_limit_bytes=16 << 20),
         cost_estimate=pl.CostEstimate(
             flops=2 * k * focal * samples * width,
             bytes_accessed=2 * focal * width * (k + 2 * samples),
@@ -383,6 +395,7 @@
     start = add(*parts).astype(BF16)
     start = jnp.transpose(start, (1, 0, 2)).reshape(NFW, 2, focal, LANES)
     spectrum_plus = start
+    reflection = hold(reflection)
     for iteration in range(ITERS):
         last = iteration + 1 == ITERS
         keep1, send1 = convolve(spectrum_plus, reflection, line, 1)

time: 401 us -> 413 us (1.030)
  waiting for transfers between devices: 203 us -> 141 us
  local copies, waits for them, and re-layouts: 15.3 us -> 68.5 us
  starting transfers between devices: 64.7 us -> 109 us
  Pallas kernels: 102 us -> 80.5 us
    ppermute x87, waiting for transfers between devices: 203 us -> 141 us  [send(): return lax.ppermute(array, self.axis, pairs)]
    unnamed x48 -> x56, local copies, waits for them, and re-layouts: 13.4 us -> 66.6 us
    ppermute x87, starting transfers between devices: 64.7 us -> 109 us  [send(): return lax.ppermute(array, self.axis, pairs)]
    pallas_call x8 -> x9, Pallas kernels: 85.9 us -> 64 us  [the longest x4 31.8 us: correlate(): pl.pallas_call(functools.partial(correlate_kernel, line, flip, bool(more)...]
  transfers between devices with their start and end apart: 87 -> 87, of which waited for: 36 -> 32; matrix products, arithmetic and copies ran while one was open for 3% -> 3% of each run, Pallas kernels for 14% -> 12%
where the time goes in v3:
time: 413 us; the launch traced here: 410 us
  waiting for transfers between devices  141 us (34%)
  starting transfers between devices  109 us (26%)
  Pallas kernels  80.5 us (19%)
  local copies, waits for them, and re-layouts  68.5 us (17%)
  other arithmetic  9.39 us (2%)
    ppermute x87, waiting for transfers between devices, send(): return lax.ppermute(array, self.axis, pairs)  141 us
    ppermute x87, starting transfers between devices, send(): return lax.ppermute(array, self.axis, pairs)  109 us
    unnamed x56, local copies, waits for them, and re-layouts  66.6 us
    pallas_call x4, Pallas kernels, correlate(): pl.pallas_call(functools.partial(correlate_kernel, line, flip, bool(more)...  31.8 us
    pallas_call x4, Pallas kernels, convolve(): pl.pallas_call(functools.partial(convolve_kernel, line, flip), in_specs=[...  21.5 us
    pallas_call x1, Pallas kernels, hold(): pl.pallas_call(functools.partial(hold_kernel, parts), in_specs=[pl.BlockS...  10.7 us
  transfers between devices with their start and end apart: 87, of which 32 were waited for; matrix products, arithmetic and copies ran while one was open for 3% of the time, Pallas kernels for 12%

profile of v3, /device:TPU:0, one launch (start us, length us, event | category | flops | bytes accessed | tf_op | source)
XLA Modules:
  0.0 409.6 jit_solution(13876977295633031614)
XLA Ops:
  2.4 2.1 first_analysis.1
  5.1 2.2 collective-permute-done.1
  7.4 3.0 collective-permute-start.3
  10.6 2.1 collective-permute-start.7
  12.8 4.6 %collective-permute-done.3 = bf16[16,64,128]{2,1,0:T(8,128)(2,1)S(1)} collective-permute-done((bf16[16,64,128]{2,1,0:T(8,128)(2,1)S(1)}, bf16[16,64,128]{2,1,0:T(8,128)(2,1)S(1)}, u32[]{:S(2)}, u32[]{:S(2)}) %collective-permute-start.3) | collective-permute-done | bytes 262176 | tf_op jit(solution)/shard_map/ppermute | solution.py:50
  17.6 5.5 %collective-permute-done.5 = bf16[16,64,128]{2,1,0:T(8,128)(2,1)S(1)} collective-permute-done((bf16[16,64,128]{2,1,0:T(8,128)(2,1)S(1)}, bf16[16,64,128]{2,1,0:T(8,128)(2,1)S(1)}, u32[]{:S(2)}, u32[]{:S(2)}) %collective-permute-start.5) | collective-permute-done | bytes 262176 | tf_op jit(solution)/shard_map/ppermute | solution.py:50
  23.2 5.5 %collective-permute-done.7 = bf16[16,64,128]{2,1,0:T(8,128)(2,1)S(1)} collective-permute-done((bf16[16,64,128]{2,1,0:T(8,128)(2,1)S(1)}, bf16[16,64,128]{2,1,0:T(8,128)(2,1)S(1)}, u32[]{:S(2)}, u32[]{:S(2)}) %collective-permute-start.7) | collective-permute-done | bytes 262176 | tf_op jit(solution)/shard_map/ppermute | solution.py:50
  28.8 4.2 %collective-permute-start.8 = (bf16[16,64,128]{2,1,0:T(8,128)(2,1)S(1)}, bf16[16,64,128]{2,1,0:T(8,128)(2,1)S(1)}, u32[]{:S(2)}, u32[]{:S(2)}) collective-permute-start(bf16[16,64,128]{2,1,0:T(8,128)(2,1)S(1)} %fusion.6), channel_id=1, source_target_pairs={{0,12},{1,13},{2,14},{3,15},{4,0},{5,1},{6,2},{7,3},{8,4},{9,5},{1... | collective-permute-start | bytes 786440 | tf_op jit(solution)/shard_map/ppermute | solution.py:50
  34.0 10.7 %hold.1.panel_ref.refs_8_ = bf16[2,32,128,2048]{3,2,1,0:T(8,128)(2,1)S(1)} custom-call(bf16[2,32,128,2048]{3,2,1,0:T(8,128)(2,1)} %source.1), custom_call_target="tpu_custom_call" | custom-call | bytes 33554432 | tf_op jit(solution)/shard_map/hold/pallas_call | solution.py:157
  44.7 11.1 %copy-done = bf16[2,32,128,2048]{3,2,1,0:T(8,128)(2,1)} copy-done((bf16[2,32,128,2048]{3,2,1,0:T(8,128)(2,1)}, bf16[2,32,128,2048]{3,2,1,0:T(8,128)(2,1)S(1)}, u32[]{:S(2)}) %copy-start) | copy-done | bytes 33554456
  56.2 10.5 %copy-done.1 = bf16[2,32,128,2048]{3,2,1,0:T(8,128)(2,1)S(1)} copy-done((bf16[2,32,128,2048]{3,2,1,0:T(8,128)(2,1)S(1)}, bf16[2,32,128,2048]{3,2,1,0:T(8,128)(2,1)}, u32[]{:S(2)}) %copy-start.1) | copy-done | bytes 33554456
  66.8 5.9 %convolve1.2 = (bf16[4,32,2,16,128]{4,3,2,1,0:T(8,128)(2,1)S(1)}, bf16[4,32,2,16,128]{4,3,2,1,0:T(8,128)(2,1)}) custom-call(bf16[32,2,16,128]{3,2,1,0:T(8,128)(2,1)S(1)} %bitcast.90, bf16[2,32,128,2048]{3,2,1,0:T(8,128)(2,1)S(1)} %copy-done.1), custom_call_target="tpu_custom_call" | custom-call | flops 536870912 | bytes 18874368 | tf_op jit(solution)/shard_map/convolve1/pallas_call | solution.py:180
  73.0 5.9 %convolve0.2 = (bf16[4,32,2,16,128]{4,3,2,1,0:T(8,128)(2,1)S(1)}, bf16[4,32,2,16,128]{4,3,2,1,0:T(8,128)(2,1)}) custom-call(bf16[32,2,16,128]{3,2,1,0:T(8,128)(2,1)S(1)} %bitcast.91, bf16[2,32,128,2048]{3,2,1,0:T(8,128)(2,1)S(1)} %copy-done.1), custom_call_target="tpu_custom_call" | custom-call | flops 536870912 | bytes 18874368 | tf_op jit(solution)/shard_map/convolve0/pallas_call | solution.py:180
  88.2 1.8 collective-permute-done.12
  91.1 2.0 collective-permute-start.13
  93.1 2.5 collective-permute-done.14
  96.7 3.4 collective-permute-start.15
  102.3 2.9 collective-permute-start.17
  106.2 9.1 %collective-permute-done.17.refs_8_ = bf16[32,2,16,128]{3,2,1,0:T(8,128)(2,1)S(1)} collective-permute-done((bf16[32,2,16,128]{3,2,1,0:T(8,128)(2,1)S(1)}, bf16[32,2,16,128]{3,2,1,0:T(8,128)(2,1)S(1)}, u32[]{:S(2)}, u32[]{:S(2)}) %collective-permute-start.17) | collective-permute-done | bytes 262176 | tf_op jit(solution)/shard_map/ppermute | solution.py:50
  115.4 2.5 window.3.refs_0_
  118.5 1.8 collective-permute-start.21
  120.3 2.5 collective-permute-start.23
  124.3 4.7 %collective-permute-done.19.refs_1_ = bf16[32,2,16,128]{3,2,1,0:T(8,128)(2,1)S(1)} collective-permute-done((bf16[32,2,16,128]{3,2,1,0:T(8,128)(2,1)S(1)}, bf16[32,2,16,128]{3,2,1,0:T(8,128)(2,1)S(1)}, u32[]{:S(2)}, u32[]{:S(2)}) %collective-permute-start.19) | collective-permute-done | bytes 262176 | tf_op jit(solution)/shard_map/ppermute | solution.py:50
  129.0 10.2 %collective-permute-done.21.refs_2_ = bf16[32,2,16,128]{3,2,1,0:T(8,128)(2,1)S(1)} collective-permute-done((bf16[32,2,16,128]{3,2,1,0:T(8,128)(2,1)S(1)}, bf16[32,2,16,128]{3,2,1,0:T(8,128)(2,1)S(1)}, u32[]{:S(2)}, u32[]{:S(2)}) %collective-permute-start.21) | collective-permute-done | bytes 262176 | tf_op jit(solution)/shard_map/ppermute | solution.py:50
  143.3 5.0 %collective-permute-done.20.refs_1_ = bf16[32,2,16,128]{3,2,1,0:T(8,128)(2,1)S(1)} collective-permute-done((bf16[32,2,16,128]{3,2,1,0:T(8,128)(2,1)S(1)}, bf16[32,2,16,128]{3,2,1,0:T(8,128)(2,1)S(1)}, u32[]{:S(2)}, u32[]{:S(2)}) %collective-permute-start.20) | collective-permute-done | bytes 262176 | tf_op jit(solution)/shard_map/ppermute | solution.py:50
  148.3 5.6 %collective-permute-done.22.refs_2_ = bf16[32,2,16,128]{3,2,1,0:T(8,128)(2,1)S(1)} collective-permute-done((bf16[32,2,16,128]{3,2,1,0:T(8,128)(2,1)S(1)}, bf16[32,2,16,128]{3,2,1,0:T(8,128)(2,1)S(1)}, u32[]{:S(2)}, u32[]{:S(2)}) %collective-permute-start.22) | collective-permute-done | bytes 262176 | tf_op jit(solution)/shard_map/ppermute | solution.py:50
  153.9 5.2 %collective-permute-done.24.refs_3_ = bf16[32,2,16,128]{3,2,1,0:T(8,128)(2,1)S(1)} collective-permute-done((bf16[32,2,16,128]{3,2,1,0:T(8,128)(2,1)S(1)}, bf16[32,2,16,128]{3,2,1,0:T(8,128)(2,1)S(1)}, u32[]{:S(2)}, u32[]{:S(2)}) %collective-permute-start.24) | collective-permute-done | bytes 262176 | tf_op jit(solution)/shard_map/ppermute | solution.py:50
  159.2 10.5 %copy-done.2 = bf16[2,32,128,2048]{3,2,1,0:T(8,128)(2,1)S(1)} copy-done((bf16[2,32,128,2048]{3,2,1,0:T(8,128)(2,1)S(1)}, bf16[2,32,128,2048]{3,2,1,0:T(8,128)(2,1)}, u32[]{:S(2)}) %copy-start.2) | copy-done | bytes 33554456
  169.7 7.9 %correlate0.2.refs_9_ = f32[32,2,16,128]{3,2,1,0:T(8,128)S(1)} custom-call(bf16[32,2,16,128]{3,2,1,0:T(8,128)(2,1)S(1)} %window.3.refs_0_, bf16[32,2,16,128]{3,2,1,0:T(8,128)(2,1)S(1)} %collective-permute-done.19.refs_1_, bf16[32,2,16,128]{3,2,1,0:T(8,128)(2,1)S(1)} %collective-permute-done.21.refs_2_, ...), custom_call_target="tpu_custom_call" | custom-call | flops 536870912 | bytes 18874368 | tf_op jit(solution)/shard_map/correlate0/pallas_call | solution.py:223
  177.7 8.0 %correlate1.2.refs_3_ = f32[32,2,16,128]{3,2,1,0:T(8,128)S(1)} custom-call(bf16[32,2,16,128]{3,2,1,0:T(8,128)(2,1)S(1)} %collective-permute-done.18.refs_0_, bf16[32,2,16,128]{3,2,1,0:T(8,128)(2,1)S(1)} %collective-permute-done.20.refs_1_, bf16[32,2,16,128]{3,2,1,0:T(8,128)(2,1)S(1)} %collective-permute-done.22.refs_2_, ...), custom_call_target="tpu_custom_call" | custom-call | flops 536870912 | bytes 18874368 | tf_op jit(solution)/shard_map/correlate1/pallas_call | solution.py:223
  185.7 2.4 window.4.spec_ref
  188.1 10.5 %copy-done.3 = bf16[2,32,128,2048]{3,2,1,0:T(8,128)(2,1)S(1)} copy-done((bf16[2,32,128,2048]{3,2,1,0:T(8,128)(2,1)S(1)}, bf16[2,32,128,2048]{3,2,1,0:T(8,128)(2,1)}, u32[]{:S(2)}) %copy-start.3) | copy-done | bytes 33554456
  198.6 4.9 %convolve1.3 = (bf16[4,32,2,16,128]{4,3,2,1,0:T(8,128)(2,1)S(1)}, bf16[4,32,2,16,128]{4,3,2,1,0:T(8,128)(2,1)S(1)}) custom-call(bf16[32,2,16,128]{3,2,1,0:T(8,128)(2,1)S(1)} %window.4.spec_ref, bf16[2,32,128,2048]{3,2,1,0:T(8,128)(2,1)S(1)} %copy-done.3), custom_call_target="tpu_custom_call" | custom-call | flops 536870912 | bytes 18874368 | tf_op jit(solution)/shard_map/convolve1/pallas_call | solution.py:180
  204.0 4.9 %convolve0.3 = (bf16[4,32,2,16,128]{4,3,2,1,0:T(8,128)(2,1)S(1)}, bf16[4,32,2,16,128]{4,3,2,1,0:T(8,128)(2,1)S(1)}) custom-call(bf16[32,2,16,128]{3,2,1,0:T(8,128)(2,1)S(1)} %window.4.spec_ref, bf16[2,32,128,2048]{3,2,1,0:T(8,128)(2,1)S(1)} %copy-done.3), custom_call_target="tpu_custom_call" | custom-call | flops 536870912 | bytes 18874368 | tf_op jit(solution)/shard_map/convolve0/pallas_call | solution.py:180
  213.7 4.6 %collective-permute-done.36 = bf16[32,2,16,128]{3,2,1,0:T(8,128)(2,1)S(1)} collective-permute-done((bf16[32,2,16,128]{3,2,1,0:T(8,128)(2,1)S(1)}, bf16[32,2,16,128]{3,2,1,0:T(8,128)(2,1)S(1)}, u32[]{:S(2)}, u32[]{:S(2)}) %collective-permute-start.36) | collective-permute-done | bytes 262176 | tf_op jit(solution)/shard_map/ppermute | solution.py:50
  218.4 2.9 collective-permute-start.37
  221.3 2.6 collective-permute-done.38
  224.0 3.9 collective-permute-start.39
  229.6 6.7 %collective-permute-start.41 = (bf16[32,2,16,128]{3,2,1,0:T(8,128)(2,1)S(1)}, bf16[32,2,16,128]{3,2,1,0:T(8,128)(2,1)S(1)}, u32[]{:S(2)}, u32[]{:S(2)}) collective-permute-start(bf16[32,2,16,128]{3,2,1,0:T(8,128)(2,1)S(1)} %fusion), channel_id=1, source_target_pairs={{0,12},{1,13},{2,14},{3,15},{4,0},{5,1},{6,2},{7,3},{8,4},{9,5},{1... | collective-permute-start | bytes 786440 | tf_op jit(solution)/shard_map/ppermute | solution.py:50
  236.4 7.4 %collective-permute-done.41.refs_8_ = bf16[32,2,16,128]{3,2,1,0:T(8,128)(2,1)S(1)} collective-permute-done((bf16[32,2,16,128]{3,2,1,0:T(8,128)(2,1)S(1)}, bf16[32,2,16,128]{3,2,1,0:T(8,128)(2,1)S(1)}, u32[]{:S(2)}, u32[]{:S(2)}) %collective-permute-start.41) | collective-permute-done | bytes 262176 | tf_op jit(solution)/shard_map/ppermute | solution.py:50
  243.9 2.5 window.5
  247.2 3.3 collective-permute-start.60
  253.5 4.0 collective-permute-done.58.refs_1_
  257.5 10.1 %collective-permute-start.42 = (bf16[16,64,128]{2,1,0:T(8,128)(2,1)S(1)}, bf16[16,64,128]{2,1,0:T(8,128)(2,1)S(1)}, u32[]{:S(2)}, u32[]{:S(2)}) collective-permute-start(bf16[16,64,128]{2,1,0:T(8,128)(2,1)S(1)} %get-tuple-element.74.refs_2_), channel_id=1, source_target_pairs={{0,4},{1,5},{2,6},{3,7},{4,8},{5,9},{6,10},{7,11},{8,12},{9,13},{1... | collective-permute-start | bytes 786440 | tf_op jit(solution)/shard_map/ppermute | solution.py:50
  269.5 14.9 %collective-permute-start.44 = (bf16[16,64,128]{2,1,0:T(8,128)(2,1)S(1)}, bf16[16,64,128]{2,1,0:T(8,128)(2,1)S(1)}, u32[]{:S(2)}, u32[]{:S(2)}) collective-permute-start(bf16[16,64,128]{2,1,0:T(8,128)(2,1)S(1)} %get-tuple-element.74.refs_2_), channel_id=1, source_target_pairs={{0,12},{1,13},{2,14},{3,15},{4,0},{5,1},{6,2},{7,3},{8,4},{9,5},{1... | collective-permute-start | bytes 786440 | tf_op jit(solution)/shard_map/ppermute | solution.py:50
  286.5 3.9 collective-permute-done.43.refs_4_
  290.4 2.6 collective-permute-done.44.refs_5_
  297.1 5.0 %collective-permute-done.59.refs_1_ = bf16[32,2,16,128]{3,2,1,0:T(8,128)(2,1)S(1)} collective-permute-done((bf16[32,2,16,128]{3,2,1,0:T(8,128)(2,1)S(1)}, bf16[32,2,16,128]{3,2,1,0:T(8,128)(2,1)S(1)}, u32[]{:S(2)}, u32[]{:S(2)}) %collective-permute-start.59) | collective-permute-done | bytes 262176 | tf_op jit(solution)/shard_map/ppermute | solution.py:50
  303.6 4.1 %collective-permute-done.61.refs_2_ = bf16[32,2,16,128]{3,2,1,0:T(8,128)(2,1)S(1)} collective-permute-done((bf16[32,2,16,128]{3,2,1,0:T(8,128)(2,1)S(1)}, bf16[32,2,16,128]{3,2,1,0:T(8,128)(2,1)S(1)}, u32[]{:S(2)}, u32[]{:S(2)}) %collective-permute-start.61) | collective-permute-done | bytes 262176 | tf_op jit(solution)/shard_map/ppermute | solution.py:50
  309.2 4.1 %collective-permute-done.63.refs_3_ = bf16[32,2,16,128]{3,2,1,0:T(8,128)(2,1)S(1)} collective-permute-done((bf16[32,2,16,128]{3,2,1,0:T(8,128)(2,1)S(1)}, bf16[32,2,16,128]{3,2,1,0:T(8,128)(2,1)S(1)}, u32[]{:S(2)}, u32[]{:S(2)}) %collective-permute-start.63) | collective-permute-done | bytes 262176 | tf_op jit(solution)/shard_map/ppermute | solution.py:50
  313.9 5.1 %collective-permute-done.46.refs_7_ = bf16[16,64,128]{2,1,0:T(8,128)(2,1)S(1)} collective-permute-done((bf16[16,64,128]{2,1,0:T(8,128)(2,1)S(1)}, bf16[16,64,128]{2,1,0:T(8,128)(2,1)S(1)}, u32[]{:S(2)}, u32[]{:S(2)}) %collective-permute-start.46) | collective-permute-done | bytes 262176 | tf_op jit(solution)/shard_map/ppermute | solution.py:50
  319.0 5.6 %collective-permute-done.47.refs_8_ = bf16[16,64,128]{2,1,0:T(8,128)(2,1)S(1)} collective-permute-done((bf16[16,64,128]{2,1,0:T(8,128)(2,1)S(1)}, bf16[16,64,128]{2,1,0:T(8,128)(2,1)S(1)}, u32[]{:S(2)}, u32[]{:S(2)}) %collective-permute-start.47) | collective-permute-done | bytes 262176 | tf_op jit(solution)/shard_map/ppermute | solution.py:50
  324.6 5.2 %collective-permute-done.48.refs_9_ = bf16[16,64,128]{2,1,0:T(8,128)(2,1)S(1)} collective-permute-done((bf16[16,64,128]{2,1,0:T(8,128)(2,1)S(1)}, bf16[16,64,128]{2,1,0:T(8,128)(2,1)S(1)}, u32[]{:S(2)}, u32[]{:S(2)}) %collective-permute-start.48) | collective-permute-done | bytes 262176 | tf_op jit(solution)/shard_map/ppermute | solution.py:50
  331.5 10.5 %copy-done.4 = bf16[2,32,128,2048]{3,2,1,0:T(8,128)(2,1)S(1)} copy-done((bf16[2,32,128,2048]{3,2,1,0:T(8,128)(2,1)S(1)}, bf16[2,32,128,2048]{3,2,1,0:T(8,128)(2,1)}, u32[]{:S(2)}) %copy-start.4) | copy-done | bytes 33554456
  342.0 7.9 %correlate0.3.refs_9_ = f32[32,2,16,128]{3,2,1,0:T(8,128)S(1)} custom-call(bf16[32,2,16,128]{3,2,1,0:T(8,128)(2,1)S(1)} %get-tuple-element.75.refs_0_, bf16[32,2,16,128]{3,2,1,0:T(8,128)(2,1)S(1)} %collective-permute-done.58.refs_1_, bf16[32,2,16,128]{3,2,1,0:T(8,128)(2,1)S(1)} %collective-permute-done.60.refs_2_, ...), custom_call_target="tpu_custom_call" | custom-call | flops 536870912 | bytes 18874368 | tf_op jit(solution)/shard_map/correlate0/pallas_call | solution.py:223
  350.0 8.0 %correlate1.3 = f32[32,2,16,128]{3,2,1,0:T(8,128)S(1)} custom-call(bf16[32,2,16,128]{3,2,1,0:T(8,128)(2,1)S(1)} %collective-permute-done.57.refs_0_, bf16[32,2,16,128]{3,2,1,0:T(8,128)(2,1)S(1)} %collective-permute-done.59.refs_1_, bf16[32,2,16,128]{3,2,1,0:T(8,128)(2,1)S(1)} %collective-permute-done.61.refs_2_, ...), custom_call_target="tpu_custom_call" | custom-call | flops 536870912 | bytes 18874368 | tf_op jit(solution)/shard_map/correlate1/pallas_call | solution.py:223
  359.0 3.5 collective-permute-start.72
  363.2 1.7 collective-permute-start.73
  369.2 1.7 collective-permute-done.72.refs_3_
  372.4 9.4 %collective-permute-done.73.refs_4_ = bf16[16,64,128]{2,1,0:T(8,128)(2,1)S(1)} collective-permute-done((bf16[16,64,128]{2,1,0:T(8,128)(2,1)S(1)}, bf16[16,64,128]{2,1,0:T(8,128)(2,1)S(1)}, u32[]{:S(2)}, u32[]{:S(2)}) %collective-permute-start.73) | collective-permute-done | bytes 262176 | tf_op jit(solution)/shard_map/ppermute | solution.py:50
  386.5 4.6 %collective-permute-done.77.refs_8_ = bf16[16,64,128]{2,1,0:T(8,128)(2,1)} collective-permute-done((bf16[16,64,128]{2,1,0:T(8,128)(2,1)S(1)}, bf16[16,64,128]{2,1,0:T(8,128)(2,1)}, u32[]{:S(2)}, u32[]{:S(2)}) %collective-permute-start.77) | collective-permute-done | bytes 262176 | tf_op jit(solution)/shard_map/ppermute | solution.py:50
  391.1 4.6 %collective-permute-done.78.refs_9_ = bf16[16,64,128]{2,1,0:T(8,128)(2,1)} collective-permute-done((bf16[16,64,128]{2,1,0:T(8,128)(2,1)}, bf16[16,64,128]{2,1,0:T(8,128)(2,1)}, u32[]{:S(2)}, u32[]{:S(2)}) %collective-permute-start.78) | collective-permute-done | bytes 262176 | tf_op jit(solution)/shard_map/ppermute | solution.py:50
  402.5 2.6 field.2
  405.2 4.5 %field.3 = bf16[16,32,2048]{2,1,0:T(8,128)(2,1)} custom-call(bf16[32,64]{1,0:T(8,128)(2,1)S(1)} %bitcast.103, s32[16,2048]{1,0:T(8,128)S(1)} %copy-done.7, bf16[16,64,128]{2,1,0:T(8,128)(2,1)S(1)} %bitcast.101, bf16[16,64,128]{2,1,0:T(8,128)(2,1)S(1)} %copy-done.19, bf16[16,64,128]{2,1,0:T(8,128)(2,1)S(1)} %copy-done.21, ...), custom_call_target="tpu_custom_call" | custom-call | flops 134217728 | bytes 8388608 | tf_op jit(solution)/shard_map/field/pallas_call | solution.py:321
  (223 shorter events, 69.1 us)
Async XLA Ops:
  10.4 12.6 %collective-permute-start.5 = (bf16[16,64,128]{2,1,0:T(8,128)(2,1)S(1)}, bf16[16,64,128]{2,1,0:T(8,128)(2,1)S(1)}, u32[]{:S(2)}, u32[]{:S(2)}) collective-permute-start(bf16[16,64,128]{2,1,0:T(8,128)(2,1)S(1)} %fusion.14), channel_id=1, source_target_pairs={{0,2},{1,3},{2,0},{3,1},{4,6},{5,7},{6,4},{7,5},{8,10},{9,11},{10,... | collective-permute-start | bytes 786440 | tf_op jit(solution)/shard_map/ppermute | solution.py:50
  10.6 18.1 %collective-permute-start.7 = (bf16[16,64,128]{2,1,0:T(8,128)(2,1)S(1)}, bf16[16,64,128]{2,1,0:T(8,128)(2,1)S(1)}, u32[]{:S(2)}, u32[]{:S(2)}) collective-permute-start(bf16[16,64,128]{2,1,0:T(8,128)(2,1)S(1)} %fusion.15), channel_id=1, source_target_pairs={{0,2},{1,3},{2,0},{3,1},{4,6},{5,7},{6,4},{7,5},{8,10},{9,11},{10,... | collective-permute-start | bytes 786440 | tf_op jit(solution)/shard_map/ppermute | solution.py:50
  12.8 43.0 %collective-permute-start.2 = (bf16[16,64,128]{2,1,0:T(8,128)(2,1)S(1)}, bf16[16,64,128]{2,1,0:T(8,128)(2,1)S(1)}, u32[]{:S(2)}, u32[]{:S(2)}) collective-permute-start(bf16[16,64,128]{2,1,0:T(8,128)(2,1)S(1)} %fusion.16), channel_id=1, source_target_pairs={{0,2},{1,3},{2,0},{3,1},{4,6},{5,7},{6,4},{7,5},{8,10},{9,11},{10,... | collective-permute-start | bytes 786440 | tf_op jit(solution)/shard_map/ppermute | solution.py:50
  28.8 27.0 %collective-permute-start.8 = (bf16[16,64,128]{2,1,0:T(8,128)(2,1)S(1)}, bf16[16,64,128]{2,1,0:T(8,128)(2,1)S(1)}, u32[]{:S(2)}, u32[]{:S(2)}) collective-permute-start(bf16[16,64,128]{2,1,0:T(8,128)(2,1)S(1)} %fusion.6), channel_id=1, source_target_pairs={{0,12},{1,13},{2,14},{3,15},{4,0},{5,1},{6,2},{7,3},{8,4},{9,5},{1... | collective-permute-start | bytes 786440 | tf_op jit(solution)/shard_map/ppermute | solution.py:50
  33.0 22.8 %collective-permute-start.6 = (bf16[16,64,128]{2,1,0:T(8,128)(2,1)S(1)}, bf16[16,64,128]{2,1,0:T(8,128)(2,1)S(1)}, u32[]{:S(2)}, u32[]{:S(2)}) collective-permute-start(bf16[16,64,128]{2,1,0:T(8,128)(2,1)S(1)} %fusion.7), channel_id=1, source_target_pairs={{0,4},{1,5},{2,6},{3,7},{4,8},{5,9},{6,10},{7,11},{8,12},{9,13},{1... | collective-permute-start | bytes 786440 | tf_op jit(solution)/shard_map/ppermute | solution.py:50
  33.0 22.8 %collective-permute-start.4 = (bf16[16,64,128]{2,1,0:T(8,128)(2,1)S(1)}, bf16[16,64,128]{2,1,0:T(8,128)(2,1)S(1)}, u32[]{:S(2)}, u32[]{:S(2)}) collective-permute-start(bf16[16,64,128]{2,1,0:T(8,128)(2,1)S(1)} %fusion.8), channel_id=1, source_target_pairs={{0,8},{1,9},{2,10},{3,11},{4,12},{5,13},{6,14},{7,15},{8,0},{9,1},... | collective-permute-start | bytes 786440 | tf_op jit(solution)/shard_map/ppermute | solution.py:50
  83.4 12.2 %collective-permute-start.14 = (bf16[32,2,16,128]{3,2,1,0:T(8,128)(2,1)S(1)}, bf16[32,2,16,128]{3,2,1,0:T(8,128)(2,1)S(1)}, u32[]{:S(2)}, u32[]{:S(2)}) collective-permute-start(bf16[32,2,16,128]{3,2,1,0:T(8,128)(2,1)S(1)} %fusion.18), channel_id=1, source_target_pairs={{0,2},{1,3},{2,0},{3,1},{4,6},{5,7},{6,4},{7,5},{8,10},{9,11},{10,... | collective-permute-start | bytes 786440 | tf_op jit(solution)/shard_map/ppermute | solution.py:50
  85.0 16.3 %collective-permute-start.16 = (bf16[32,2,16,128]{3,2,1,0:T(8,128)(2,1)S(1)}, bf16[32,2,16,128]{3,2,1,0:T(8,128)(2,1)S(1)}, u32[]{:S(2)}, u32[]{:S(2)}) collective-permute-start(bf16[32,2,16,128]{3,2,1,0:T(8,128)(2,1)S(1)} %fusion.19), channel_id=1, source_target_pairs={{0,2},{1,3},{2,0},{3,1},{4,6},{5,7},{6,4},{7,5},{8,10},{9,11},{10,... | collective-permute-start | bytes 786440 | tf_op jit(solution)/shard_map/ppermute | solution.py:50
  87.6 18.6 %collective-permute-start.11 = (bf16[32,2,16,128]{3,2,1,0:T(8,128)(2,1)S(1)}, bf16[32,2,16,128]{3,2,1,0:T(8,128)(2,1)S(1)}, u32[]{:S(2)}, u32[]{:S(2)}) collective-permute-start(bf16[32,2,16,128]{3,2,1,0:T(8,128)(2,1)S(1)} %fusion.20), channel_id=1, source_target_pairs={{0,2},{1,3},{2,0},{3,1},{4,6},{5,7},{6,4},{7,5},{8,10},{9,11},{10,... | collective-permute-start | bytes 786440 | tf_op jit(solution)/shard_map/ppermute | solution.py:50
  91.1 24.2 %collective-permute-start.13 = (bf16[32,2,16,128]{3,2,1,0:T(8,128)(2,1)S(1)}, bf16[32,2,16,128]{3,2,1,0:T(8,128)(2,1)S(1)}, u32[]{:S(2)}, u32[]{:S(2)}) collective-permute-start(bf16[32,2,16,128]{3,2,1,0:T(8,128)(2,1)S(1)} %fusion.5), channel_id=1, source_target_pairs={{0,8},{1,9},{2,10},{3,11},{4,12},{5,13},{6,14},{7,15},{8,0},{9,1},... | collective-permute-start | bytes 786440 | tf_op jit(solution)/shard_map/ppermute | solution.py:50
  96.7 18.6 %collective-permute-start.15 = (bf16[32,2,16,128]{3,2,1,0:T(8,128)(2,1)S(1)}, bf16[32,2,16,128]{3,2,1,0:T(8,128)(2,1)S(1)}, u32[]{:S(2)}, u32[]{:S(2)}) collective-permute-start(bf16[32,2,16,128]{3,2,1,0:T(8,128)(2,1)S(1)} %fusion.4), channel_id=1, source_target_pairs={{0,4},{1,5},{2,6},{3,7},{4,8},{5,9},{6,10},{7,11},{8,12},{9,13},{1... | collective-permute-start | bytes 786440 | tf_op jit(solution)/shard_map/ppermute | solution.py:50
  102.3 13.0 %collective-permute-start.17 = (bf16[32,2,16,128]{3,2,1,0:T(8,128)(2,1)S(1)}, bf16[32,2,16,128]{3,2,1,0:T(8,128)(2,1)S(1)}, u32[]{:S(2)}, u32[]{:S(2)}) collective-permute-start(bf16[32,2,16,128]{3,2,1,0:T(8,128)(2,1)S(1)} %fusion.3), channel_id=1, source_target_pairs={{0,12},{1,13},{2,14},{3,15},{4,0},{5,1},{6,2},{7,3},{8,4},{9,5},{1... | collective-permute-start | bytes 786440 | tf_op jit(solution)/shard_map/ppermute | solution.py:50
  117.9 11.1 %collective-permute-start.19 = (bf16[32,2,16,128]{3,2,1,0:T(8,128)(2,1)S(1)}, bf16[32,2,16,128]{3,2,1,0:T(8,128)(2,1)S(1)}, u32[]{:S(2)}, u32[]{:S(2)}) collective-permute-start(bf16[32,2,16,128]{3,2,1,0:T(8,128)(2,1)S(1)} %window.3.refs_0_), channel_id=1, source_target_pairs={{0,4},{1,5},{2,6},{3,7},{4,8},{5,9},{6,10},{7,11},{8,12},{9,13},{1... | collective-permute-start | bytes 786440 | tf_op jit(solution)/shard_map/ppermute | solution.py:50
  118.5 20.7 %collective-permute-start.21 = (bf16[32,2,16,128]{3,2,1,0:T(8,128)(2,1)S(1)}, bf16[32,2,16,128]{3,2,1,0:T(8,128)(2,1)S(1)}, u32[]{:S(2)}, u32[]{:S(2)}) collective-permute-start(bf16[32,2,16,128]{3,2,1,0:T(8,128)(2,1)S(1)} %window.3.refs_0_), channel_id=1, source_target_pairs={{0,8},{1,9},{2,10},{3,11},{4,12},{5,13},{6,14},{7,15},{8,0},{9,1},... | collective-permute-start | bytes 786440 | tf_op jit(solution)/shard_map/ppermute | solution.py:50
  120.3 18.9 %collective-permute-start.23 = (bf16[32,2,16,128]{3,2,1,0:T(8,128)(2,1)S(1)}, bf16[32,2,16,128]{3,2,1,0:T(8,128)(2,1)S(1)}, u32[]{:S(2)}, u32[]{:S(2)}) collective-permute-start(bf16[32,2,16,128]{3,2,1,0:T(8,128)(2,1)S(1)} %window.3.refs_0_), channel_id=1, source_target_pairs={{0,12},{1,13},{2,14},{3,15},{4,0},{5,1},{6,2},{7,3},{8,4},{9,5},{1... | collective-permute-start | bytes 786440 | tf_op jit(solution)/shard_map/ppermute | solution.py:50
  122.8 17.9 %collective-permute-start.29 = (bf16[32,2,16,128]{3,2,1,0:T(8,128)(2,1)S(1)}, bf16[32,2,16,128]{3,2,1,0:T(8,128)(2,1)S(1)}, u32[]{:S(2)}, u32[]{:S(2)}) collective-permute-start(bf16[32,2,16,128]{3,2,1,0:T(8,128)(2,1)S(1)} %window.3.refs_0_), channel_id=1, source_target_pairs={{0,1},{1,0},{2,3},{3,2},{4,5},{5,4},{6,7},{7,6},{8,9},{9,8},{10,11... | collective-permute-start | bytes 786440 | tf_op jit(solution)/shard_map/ppermute | solution.py:50
  122.8 18.4 %collective-permute-start.18 = (bf16[32,2,16,128]{3,2,1,0:T(8,128)(2,1)S(1)}, bf16[32,2,16,128]{3,2,1,0:T(8,128)(2,1)S(1)}, u32[]{:S(2)}, u32[]{:S(2)}) collective-permute-start(bf16[32,2,16,128]{3,2,1,0:T(8,128)(2,1)S(1)} %window.3.refs_0_), channel_id=1, source_target_pairs={{0,2},{1,3},{2,0},{3,1},{4,6},{5,7},{6,4},{7,5},{8,10},{9,11},{10,... | collective-permute-start | bytes 786440 | tf_op jit(solution)/shard_map/ppermute | solution.py:50
  129.0 13.8 %collective-permute-start.30 = (bf16[32,2,16,128]{3,2,1,0:T(8,128)(2,1)S(1)}, bf16[32,2,16,128]{3,2,1,0:T(8,128)(2,1)S(1)}, u32[]{:S(2)}, u32[]{:S(2)}) collective-permute-start(bf16[32,2,16,128]{3,2,1,0:T(8,128)(2,1)S(1)} %collective-permute-done.19.refs_1_), channel_id=1, source_target_pairs={{0,1},{1,0},{2,3},{3,2},{4,5},{5,4},{6,7},{7,6},{8,9},{9,8},{10,11... | collective-permute-start | bytes 786440 | tf_op jit(solution)/shard_map/ppermute | solution.py:50
  140.7 13.2 %collective-permute-start.22 = (bf16[32,2,16,128]{3,2,1,0:T(8,128)(2,1)S(1)}, bf16[32,2,16,128]{3,2,1,0:T(8,128)(2,1)S(1)}, u32[]{:S(2)}, u32[]{:S(2)}) collective-permute-start(bf16[32,2,16,128]{3,2,1,0:T(8,128)(2,1)S(1)} %collective-permute-done.21.refs_2_), channel_id=1, source_target_pairs={{0,2},{1,3},{2,0},{3,1},{4,6},{5,7},{6,4},{7,5},{8,10},{9,11},{10,... | collective-permute-start | bytes 786440 | tf_op jit(solution)/shard_map/ppermute | solution.py:50
  141.2 17.9 %collective-permute-start.24 = (bf16[32,2,16,128]{3,2,1,0:T(8,128)(2,1)S(1)}, bf16[32,2,16,128]{3,2,1,0:T(8,128)(2,1)S(1)}, u32[]{:S(2)}, u32[]{:S(2)}) collective-permute-start(bf16[32,2,16,128]{3,2,1,0:T(8,128)(2,1)S(1)} %collective-permute-done.23.refs_3_), channel_id=1, source_target_pairs={{0,2},{1,3},{2,0},{3,1},{4,6},{5,7},{6,4},{7,5},{8,10},{9,11},{10,... | collective-permute-start | bytes 786440 | tf_op jit(solution)/shard_map/ppermute | solution.py:50
  142.8 16.4 %collective-permute-start.32 = (bf16[32,2,16,128]{3,2,1,0:T(8,128)(2,1)S(1)}, bf16[32,2,16,128]{3,2,1,0:T(8,128)(2,1)S(1)}, u32[]{:S(2)}, u32[]{:S(2)}) collective-permute-start(bf16[32,2,16,128]{3,2,1,0:T(8,128)(2,1)S(1)} %collective-permute-done.23.refs_3_), channel_id=1, source_target_pairs={{0,1},{1,0},{2,3},{3,2},{4,5},{5,4},{6,7},{7,6},{8,9},{9,8},{10,11... | collective-permute-start | bytes 786440 | tf_op jit(solution)/shard_map/ppermute | solution.py:50
  142.8 34.9 %collective-permute-start.25 = (bf16[32,2,16,128]{3,2,1,0:T(8,128)(2,1)S(1)}, bf16[32,2,16,128]{3,2,1,0:T(8,128)(2,1)S(1)}, u32[]{:S(2)}, u32[]{:S(2)}) collective-permute-start(bf16[32,2,16,128]{3,2,1,0:T(8,128)(2,1)S(1)} %collective-permute-done.18.refs_0_), channel_id=1, source_target_pairs={{0,1},{1,0},{2,3},{3,2},{4,5},{5,4},{6,7},{7,6},{8,9},{9,8},{10,11... | collective-permute-start | bytes 786440 | tf_op jit(solution)/shard_map/ppermute | solution.py:50
  148.3 29.3 %collective-permute-start.26 = (bf16[32,2,16,128]{3,2,1,0:T(8,128)(2,1)S(1)}, bf16[32,2,16,128]{3,2,1,0:T(8,128)(2,1)S(1)}, u32[]{:S(2)}, u32[]{:S(2)}) collective-permute-start(bf16[32,2,16,128]{3,2,1,0:T(8,128)(2,1)S(1)} %collective-permute-done.20.refs_1_), channel_id=1, source_target_pairs={{0,1},{1,0},{2,3},{3,2},{4,5},{5,4},{6,7},{7,6},{8,9},{9,8},{10,11... | collective-permute-start | bytes 786440 | tf_op jit(solution)/shard_map/ppermute | solution.py:50
  153.9 23.7 %collective-permute-start.27 = (bf16[32,2,16,128]{3,2,1,0:T(8,128)(2,1)S(1)}, bf16[32,2,16,128]{3,2,1,0:T(8,128)(2,1)S(1)}, u32[]{:S(2)}, u32[]{:S(2)}) collective-permute-start(bf16[32,2,16,128]{3,2,1,0:T(8,128)(2,1)S(1)} %collective-permute-done.22.refs_2_), channel_id=1, source_target_pairs={{0,1},{1,0},{2,3},{3,2},{4,5},{5,4},{6,7},{7,6},{8,9},{9,8},{10,11... | collective-permute-start | bytes 786440 | tf_op jit(solution)/shard_map/ppermute | solution.py:50
  159.1 18.5 %collective-permute-start.28 = (bf16[32,2,16,128]{3,2,1,0:T(8,128)(2,1)S(1)}, bf16[32,2,16,128]{3,2,1,0:T(8,128)(2,1)S(1)}, u32[]{:S(2)}, u32[]{:S(2)}) collective-permute-start(bf16[32,2,16,128]{3,2,1,0:T(8,128)(2,1)S(1)} %collective-permute-done.24.refs_3_), channel_id=1, source_target_pairs={{0,1},{1,0},{2,3},{3,2},{4,5},{5,4},{6,7},{7,6},{8,9},{9,8},{10,11... | collective-permute-start | bytes 786440 | tf_op jit(solution)/shard_map/ppermute | solution.py:50
  210.8 13.1 %collective-permute-start.38 = (bf16[32,2,16,128]{3,2,1,0:T(8,128)(2,1)S(1)}, bf16[32,2,16,128]{3,2,1,0:T(8,128)(2,1)S(1)}, u32[]{:S(2)}, u32[]{:S(2)}) collective-permute-start(bf16[32,2,16,128]{3,2,1,0:T(8,128)(2,1)S(1)} %fusion.22), channel_id=1, source_target_pairs={{0,2},{1,3},{2,0},{3,1},{4,6},{5,7},{6,4},{7,5},{8,10},{9,11},{10,... | collective-permute-start | bytes 786440 | tf_op jit(solution)/shard_map/ppermute | solution.py:50
  211.4 18.1 %collective-permute-start.40 = (bf16[32,2,16,128]{3,2,1,0:T(8,128)(2,1)S(1)}, bf16[32,2,16,128]{3,2,1,0:T(8,128)(2,1)S(1)}, u32[]{:S(2)}, u32[]{:S(2)}) collective-permute-start(bf16[32,2,16,128]{3,2,1,0:T(8,128)(2,1)S(1)} %fusion.23), channel_id=1, source_target_pairs={{0,2},{1,3},{2,0},{3,1},{4,6},{5,7},{6,4},{7,5},{8,10},{9,11},{10,... | collective-permute-start | bytes 786440 | tf_op jit(solution)/shard_map/ppermute | solution.py:50
  213.1 23.3 %collective-permute-start.35 = (bf16[32,2,16,128]{3,2,1,0:T(8,128)(2,1)S(1)}, bf16[32,2,16,128]{3,2,1,0:T(8,128)(2,1)S(1)}, u32[]{:S(2)}, u32[]{:S(2)}) collective-permute-start(bf16[32,2,16,128]{3,2,1,0:T(8,128)(2,1)S(1)} %fusion.24), channel_id=1, source_target_pairs={{0,2},{1,3},{2,0},{3,1},{4,6},{5,7},{6,4},{7,5},{8,10},{9,11},{10,... | collective-permute-start | bytes 786440 | tf_op jit(solution)/shard_map/ppermute | solution.py:50
  218.4 25.5 %collective-permute-start.37 = (bf16[32,2,16,128]{3,2,1,0:T(8,128)(2,1)S(1)}, bf16[32,2,16,128]{3,2,1,0:T(8,128)(2,1)S(1)}, u32[]{:S(2)}, u32[]{:S(2)}) collective-permute-start(bf16[32,2,16,128]{3,2,1,0:T(8,128)(2,1)S(1)} %fusion.2), channel_id=1, source_target_pairs={{0,8},{1,9},{2,10},{3,11},{4,12},{5,13},{6,14},{7,15},{8,0},{9,1},... | collective-permute-start | bytes 786440 | tf_op jit(solution)/shard_map/ppermute | solution.py:50
  224.0 19.8 %collective-permute-start.39 = (bf16[32,2,16,128]{3,2,1,0:T(8,128)(2,1)S(1)}, bf16[32,2,16,128]{3,2,1,0:T(8,128)(2,1)S(1)}, u32[]{:S(2)}, u32[]{:S(2)}) collective-permute-start(bf16[32,2,16,128]{3,2,1,0:T(8,128)(2,1)S(1)} %fusion.1), channel_id=1, source_target_pairs={{0,4},{1,5},{2,6},{3,7},{4,8},{5,9},{6,10},{7,11},{8,12},{9,13},{1... | collective-permute-start | bytes 786440 | tf_op jit(solution)/shard_map/ppermute | solution.py:50
  229.6 14.2 %collective-permute-start.41 = (bf16[32,2,16,128]{3,2,1,0:T(8,128)(2,1)S(1)}, bf16[32,2,16,128]{3,2,1,0:T(8,128)(2,1)S(1)}, u32[]{:S(2)}, u32[]{:S(2)}) collective-permute-start(bf16[32,2,16,128]{3,2,1,0:T(8,128)(2,1)S(1)} %fusion), channel_id=1, source_target_pairs={{0,12},{1,13},{2,14},{3,15},{4,0},{5,1},{6,2},{7,3},{8,4},{9,5},{1... | collective-permute-start | bytes 786440 | tf_op jit(solution)/shard_map/ppermute | solution.py:50
  246.4 11.2 %collective-permute-start.58 = (bf16[32,2,16,128]{3,2,1,0:T(8,128)(2,1)S(1)}, bf16[32,2,16,128]{3,2,1,0:T(8,128)(2,1)S(1)}, u32[]{:S(2)}, u32[]{:S(2)}) collective-permute-start(bf16[32,2,16,128]{3,2,1,0:T(8,128)(2,1)S(1)} %get-tuple-element.75.refs_0_), channel_id=1, source_target_pairs={{0,4},{1,5},{2,6},{3,7},{4,8},{5,9},{6,10},{7,11},{8,12},{9,13},{1... | collective-permute-start | bytes 786440 | tf_op jit(solution)/shard_map/ppermute | solution.py:50
  247.2 21.6 %collective-permute-start.60 = (bf16[32,2,16,128]{3,2,1,0:T(8,128)(2,1)S(1)}, bf16[32,2,16,128]{3,2,1,0:T(8,128)(2,1)S(1)}, u32[]{:S(2)}, u32[]{:S(2)}) collective-permute-start(bf16[32,2,16,128]{3,2,1,0:T(8,128)(2,1)S(1)} %get-tuple-element.75.refs_0_), channel_id=1, source_target_pairs={{0,8},{1,9},{2,10},{3,11},{4,12},{5,13},{6,14},{7,15},{8,0},{9,1},... | collective-permute-start | bytes 786440 | tf_op jit(solution)/shard_map/ppermute | solution.py:50
  250.5 19.0 %collective-permute-start.62 = (bf16[32,2,16,128]{3,2,1,0:T(8,128)(2,1)S(1)}, bf16[32,2,16,128]{3,2,1,0:T(8,128)(2,1)S(1)}, u32[]{:S(2)}, u32[]{:S(2)}) collective-permute-start(bf16[32,2,16,128]{3,2,1,0:T(8,128)(2,1)S(1)} %get-tuple-element.75.refs_0_), channel_id=1, source_target_pairs={{0,12},{1,13},{2,14},{3,15},{4,0},{5,1},{6,2},{7,3},{8,4},{9,5},{1... | collective-permute-start | bytes 786440 | tf_op jit(solution)/shard_map/ppermute | solution.py:50
  252.0 32.4 %collective-permute-start.68 = (bf16[32,2,16,128]{3,2,1,0:T(8,128)(2,1)S(1)}, bf16[32,2,16,128]{3,2,1,0:T(8,128)(2,1)S(1)}, u32[]{:S(2)}, u32[]{:S(2)}) collective-permute-start(bf16[32,2,16,128]{3,2,1,0:T(8,128)(2,1)S(1)} %get-tuple-element.75.refs_0_), channel_id=1, source_target_pairs={{0,1},{1,0},{2,3},{3,2},{4,5},{5,4},{6,7},{7,6},{8,9},{9,8},{10,11... | collective-permute-start | bytes 786440 | tf_op jit(solution)/shard_map/ppermute | solution.py:50
  252.0 33.9 %collective-permute-start.57 = (bf16[32,2,16,128]{3,2,1,0:T(8,128)(2,1)S(1)}, bf16[32,2,16,128]{3,2,1,0:T(8,128)(2,1)S(1)}, u32[]{:S(2)}, u32[]{:S(2)}) collective-permute-start(bf16[32,2,16,128]{3,2,1,0:T(8,128)(2,1)S(1)} %get-tuple-element.75.refs_0_), channel_id=1, source_target_pairs={{0,2},{1,3},{2,0},{3,1},{4,6},{5,7},{6,4},{7,5},{8,10},{9,11},{10,... | collective-permute-start | bytes 786440 | tf_op jit(solution)/shard_map/ppermute | solution.py:50
  257.5 28.4 %collective-permute-start.42 = (bf16[16,64,128]{2,1,0:T(8,128)(2,1)S(1)}, bf16[16,64,128]{2,1,0:T(8,128)(2,1)S(1)}, u32[]{:S(2)}, u32[]{:S(2)}) collective-permute-start(bf16[16,64,128]{2,1,0:T(8,128)(2,1)S(1)} %get-tuple-element.74.refs_2_), channel_id=1, source_target_pairs={{0,4},{1,5},{2,6},{3,7},{4,8},{5,9},{6,10},{7,11},{8,12},{9,13},{1... | collective-permute-start | bytes 786440 | tf_op jit(solution)/shard_map/ppermute | solution.py:50
  268.8 21.6 %collective-permute-start.43 = (bf16[16,64,128]{2,1,0:T(8,128)(2,1)S(1)}, bf16[16,64,128]{2,1,0:T(8,128)(2,1)S(1)}, u32[]{:S(2)}, u32[]{:S(2)}) collective-permute-start(bf16[16,64,128]{2,1,0:T(8,128)(2,1)S(1)} %get-tuple-element.74.refs_2_), channel_id=1, source_target_pairs={{0,8},{1,9},{2,10},{3,11},{4,12},{5,13},{6,14},{7,15},{8,0},{9,1},... | collective-permute-start | bytes 786440 | tf_op jit(solution)/shard_map/ppermute | solution.py:50
  269.5 23.5 %collective-permute-start.44 = (bf16[16,64,128]{2,1,0:T(8,128)(2,1)S(1)}, bf16[16,64,128]{2,1,0:T(8,128)(2,1)S(1)}, u32[]{:S(2)}, u32[]{:S(2)}) collective-permute-start(bf16[16,64,128]{2,1,0:T(8,128)(2,1)S(1)} %get-tuple-element.74.refs_2_), channel_id=1, source_target_pairs={{0,12},{1,13},{2,14},{3,15},{4,0},{5,1},{6,2},{7,3},{8,4},{9,5},{1... | collective-permute-start | bytes 786440 | tf_op jit(solution)/shard_map/ppermute | solution.py:50
  294.5 13.2 %collective-permute-start.61 = (bf16[32,2,16,128]{3,2,1,0:T(8,128)(2,1)S(1)}, bf16[32,2,16,128]{3,2,1,0:T(8,128)(2,1)S(1)}, u32[]{:S(2)}, u32[]{:S(2)}) collective-permute-start(bf16[32,2,16,128]{3,2,1,0:T(8,128)(2,1)S(1)} %collective-permute-done.60.refs_2_), channel_id=1, source_target_pairs={{0,2},{1,3},{2,0},{3,1},{4,6},{5,7},{6,4},{7,5},{8,10},{9,11},{10,... | collective-permute-start | bytes 786440 | tf_op jit(solution)/shard_map/ppermute | solution.py:50
  295.0 18.3 %collective-permute-start.63 = (bf16[32,2,16,128]{3,2,1,0:T(8,128)(2,1)S(1)}, bf16[32,2,16,128]{3,2,1,0:T(8,128)(2,1)S(1)}, u32[]{:S(2)}, u32[]{:S(2)}) collective-permute-start(bf16[32,2,16,128]{3,2,1,0:T(8,128)(2,1)S(1)} %collective-permute-done.62.refs_3_), channel_id=1, source_target_pairs={{0,2},{1,3},{2,0},{3,1},{4,6},{5,7},{6,4},{7,5},{8,10},{9,11},{10,... | collective-permute-start | bytes 786440 | tf_op jit(solution)/shard_map/ppermute | solution.py:50
  296.5 16.8 %collective-permute-start.64 = (bf16[32,2,16,128]{3,2,1,0:T(8,128)(2,1)S(1)}, bf16[32,2,16,128]{3,2,1,0:T(8,128)(2,1)S(1)}, u32[]{:S(2)}, u32[]{:S(2)}) collective-permute-start(bf16[32,2,16,128]{3,2,1,0:T(8,128)(2,1)S(1)} %collective-permute-done.57.refs_0_), channel_id=1, source_target_pairs={{0,1},{1,0},{2,3},{3,2},{4,5},{5,4},{6,7},{7,6},{8,9},{9,8},{10,11... | collective-permute-start | bytes 786440 | tf_op jit(solution)/shard_map/ppermute | solution.py:50
  296.5 22.4 %collective-permute-start.46 = (bf16[16,64,128]{2,1,0:T(8,128)(2,1)S(1)}, bf16[16,64,128]{2,1,0:T(8,128)(2,1)S(1)}, u32[]{:S(2)}, u32[]{:S(2)}) collective-permute-start(bf16[16,64,128]{2,1,0:T(8,128)(2,1)S(1)} %collective-permute-done.42.refs_3_), channel_id=1, source_target_pairs={{0,2},{1,3},{2,0},{3,1},{4,6},{5,7},{6,4},{7,5},{8,10},{9,11},{10,... | collective-permute-start | bytes 786440 | tf_op jit(solution)/shard_map/ppermute | solution.py:50
  302.1 22.5 %collective-permute-start.47 = (bf16[16,64,128]{2,1,0:T(8,128)(2,1)S(1)}, bf16[16,64,128]{2,1,0:T(8,128)(2,1)S(1)}, u32[]{:S(2)}, u32[]{:S(2)}) collective-permute-start(bf16[16,64,128]{2,1,0:T(8,128)(2,1)S(1)} %collective-permute-done.43.refs_4_), channel_id=1, source_target_pairs={{0,2},{1,3},{2,0},{3,1},{4,6},{5,7},{6,4},{7,5},{8,10},{9,11},{10,... | collective-permute-start | bytes 786440 | tf_op jit(solution)/shard_map/ppermute | solution.py:50
  307.7 22.1 %collective-permute-start.48 = (bf16[16,64,128]{2,1,0:T(8,128)(2,1)S(1)}, bf16[16,64,128]{2,1,0:T(8,128)(2,1)S(1)}, u32[]{:S(2)}, u32[]{:S(2)}) collective-permute-start(bf16[16,64,128]{2,1,0:T(8,128)(2,1)S(1)} %collective-permute-done.44.refs_5_), channel_id=1, source_target_pairs={{0,2},{1,3},{2,0},{3,1},{4,6},{5,7},{6,4},{7,5},{8,10},{9,11},{10,... | collective-permute-start | bytes 786440 | tf_op jit(solution)/shard_map/ppermute | solution.py:50
  313.3 16.5 %collective-permute-start.50 = (bf16[16,64,128]{2,1,0:T(8,128)(2,1)S(1)}, bf16[16,64,128]{2,1,0:T(8,128)(2,1)S(1)}, u32[]{:S(2)}, u32[]{:S(2)}) collective-permute-start(bf16[16,64,128]{2,1,0:T(8,128)(2,1)S(1)} %collective-permute-done.42.refs_3_), channel_id=1, source_target_pairs={{0,1},{1,0},{2,3},{3,2},{4,5},{5,4},{6,7},{7,6},{8,9},{9,8},{10,11... | collective-permute-start | bytes 786440 | tf_op jit(solution)/shard_map/ppermute | solution.py:50
  313.3 17.0 %collective-permute-start.51 = (bf16[16,64,128]{2,1,0:T(8,128)(2,1)S(1)}, bf16[16,64,128]{2,1,0:T(8,128)(2,1)S(1)}, u32[]{:S(2)}, u32[]{:S(2)}) collective-permute-start(bf16[16,64,128]{2,1,0:T(8,128)(2,1)S(1)} %collective-permute-done.43.refs_4_), channel_id=1, source_target_pairs={{0,1},{1,0},{2,3},{3,2},{4,5},{5,4},{6,7},{7,6},{8,9},{9,8},{10,11... | collective-permute-start | bytes 786440 | tf_op jit(solution)/shard_map/ppermute | solution.py:50
  319.0 11.4 %collective-permute-start.65 = (bf16[32,2,16,128]{3,2,1,0:T(8,128)(2,1)S(1)}, bf16[32,2,16,128]{3,2,1,0:T(8,128)(2,1)S(1)}, u32[]{:S(2)}, u32[]{:S(2)}) collective-permute-start(bf16[32,2,16,128]{3,2,1,0:T(8,128)(2,1)S(1)} %collective-permute-done.59.refs_1_), channel_id=1, source_target_pairs={{0,1},{1,0},{2,3},{3,2},{4,5},{5,4},{6,7},{7,6},{8,9},{9,8},{10,11... | collective-permute-start | bytes 786440 | tf_op jit(solution)/shard_map/ppermute | solution.py:50
  329.8 28.4 %collective-permute-start.52 = (bf16[16,64,128]{2,1,0:T(8,128)(2,1)S(1)}, bf16[16,64,128]{2,1,0:T(8,128)(2,1)S(1)}, u32[]{:S(2)}, u32[]{:S(2)}) collective-permute-start(bf16[16,64,128]{2,1,0:T(8,128)(2,1)S(1)} %collective-permute-done.44.refs_5_), channel_id=1, source_target_pairs={{0,1},{1,0},{2,3},{3,2},{4,5},{5,4},{6,7},{7,6},{8,9},{9,8},{10,11... | collective-permute-start | bytes 786440 | tf_op jit(solution)/shard_map/ppermute | solution.py:50
  330.3 32.1 %collective-permute-start.53 = (bf16[16,64,128]{2,1,0:T(8,128)(2,1)S(1)}, bf16[16,64,128]{2,1,0:T(8,128)(2,1)S(1)}, u32[]{:S(2)}, u32[]{:S(2)}) collective-permute-start(bf16[16,64,128]{2,1,0:T(8,128)(2,1)S(1)} %collective-permute-done.45.refs_6_), channel_id=1, source_target_pairs={{0,1},{1,0},{2,3},{3,2},{4,5},{5,4},{6,7},{7,6},{8,9},{9,8},{10,11... | collective-permute-start | bytes 786440 | tf_op jit(solution)/shard_map/ppermute | solution.py:50
  330.4 34.5 %collective-permute-start.54 = (bf16[16,64,128]{2,1,0:T(8,128)(2,1)S(1)}, bf16[16,64,128]{2,1,0:T(8,128)(2,1)S(1)}, u32[]{:S(2)}, u32[]{:S(2)}) collective-permute-start(bf16[16,64,128]{2,1,0:T(8,128)(2,1)S(1)} %collective-permute-done.46.refs_7_), channel_id=1, source_target_pairs={{0,1},{1,0},{2,3},{3,2},{4,5},{5,4},{6,7},{7,6},{8,9},{9,8},{10,11... | collective-permute-start | bytes 786440 | tf_op jit(solution)/shard_map/ppermute | solution.py:50
  330.8 35.4 %collective-permute-start.55 = (bf16[16,64,128]{2,1,0:T(8,128)(2,1)S(1)}, bf16[16,64,128]{2,1,0:T(8,128)(2,1)S(1)}, u32[]{:S(2)}, u32[]{:S(2)}) collective-permute-start(bf16[16,64,128]{2,1,0:T(8,128)(2,1)S(1)} %collective-permute-done.47.refs_8_), channel_id=1, source_target_pairs={{0,1},{1,0},{2,3},{3,2},{4,5},{5,4},{6,7},{7,6},{8,9},{9,8},{10,11... | collective-permute-start | bytes 786440 | tf_op jit(solution)/shard_map/ppermute | solution.py:50
  331.3 37.1 %collective-permute-start.56 = (bf16[16,64,128]{2,1,0:T(8,128)(2,1)S(1)}, bf16[16,64,128]{2,1,0:T(8,128)(2,1)S(1)}, u32[]{:S(2)}, u32[]{:S(2)}) collective-permute-start(bf16[16,64,128]{2,1,0:T(8,128)(2,1)S(1)} %collective-permute-done.48.refs_9_), channel_id=1, source_target_pairs={{0,1},{1,0},{2,3},{3,2},{4,5},{5,4},{6,7},{7,6},{8,9},{9,8},{10,11... | collective-permute-start | bytes 786440 | tf_op jit(solution)/shard_map/ppermute | solution.py:50
  359.0 11.9 %collective-permute-start.72 = (bf16[16,64,128]{2,1,0:T(8,128)(2,1)S(1)}, bf16[16,64,128]{2,1,0:T(8,128)(2,1)S(1)}, u32[]{:S(2)}, u32[]{:S(2)}) collective-permute-start(bf16[16,64,128]{2,1,0:T(8,128)(2,1)S(1)} %bitcast.96), channel_id=1, source_target_pairs={{0,4},{1,5},{2,6},{3,7},{4,8},{5,9},{6,10},{7,11},{8,12},{9,13},{1... | collective-permute-start | bytes 786440 | tf_op jit(solution)/shard_map/ppermute | solution.py:50
  363.2 18.6 %collective-permute-start.73 = (bf16[16,64,128]{2,1,0:T(8,128)(2,1)S(1)}, bf16[16,64,128]{2,1,0:T(8,128)(2,1)S(1)}, u32[]{:S(2)}, u32[]{:S(2)}) collective-permute-start(bf16[16,64,128]{2,1,0:T(8,128)(2,1)S(1)} %bitcast.97), channel_id=1, source_target_pairs={{0,8},{1,9},{2,10},{3,11},{4,12},{5,13},{6,14},{7,15},{8,0},{9,1},... | collective-permute-start | bytes 786440 | tf_op jit(solution)/shard_map/ppermute | solution.py:50
  365.6 17.7 %collective-permute-start.74 = (bf16[16,64,128]{2,1,0:T(8,128)(2,1)S(1)}, bf16[16,64,128]{2,1,0:T(8,128)(2,1)}, u32[]{:S(2)}, u32[]{:S(2)}) collective-permute-start(bf16[16,64,128]{2,1,0:T(8,128)(2,1)S(1)} %bitcast.98), channel_id=1, source_target_pairs={{0,12},{1,13},{2,14},{3,15},{4,0},{5,1},{6,2},{7,3},{8,4},{9,5},{1... | collective-permute-start | bytes 786440 | tf_op jit(solution)/shard_map/ppermute | solution.py:50
  366.9 16.9 %collective-permute-start.75 = (bf16[16,64,128]{2,1,0:T(8,128)(2,1)S(1)}, bf16[16,64,128]{2,1,0:T(8,128)(2,1)}, u32[]{:S(2)}, u32[]{:S(2)}) collective-permute-start(bf16[16,64,128]{2,1,0:T(8,128)(2,1)S(1)} %bitcast.99), channel_id=1, source_target_pairs={{0,2},{1,3},{2,0},{3,1},{4,6},{5,7},{6,4},{7,5},{8,10},{9,11},{10,... | collective-permute-start | bytes 786440 | tf_op jit(solution)/shard_map/ppermute | solution.py:50
  369.2 15.4 %collective-permute-start.79 = (bf16[16,64,128]{2,1,0:T(8,128)(2,1)S(1)}, bf16[16,64,128]{2,1,0:T(8,128)(2,1)S(1)}, u32[]{:S(2)}, u32[]{:S(2)}) collective-permute-start(bf16[16,64,128]{2,1,0:T(8,128)(2,1)S(1)} %bitcast.100), channel_id=1, source_target_pairs={{0,1},{1,0},{2,3},{3,2},{4,5},{5,4},{6,7},{7,6},{8,9},{9,8},{10,11... | collective-permute-start | bytes 786440 | tf_op jit(solution)/shard_map/ppermute | solution.py:50
  370.9 15.6 %collective-permute-start.76 = (bf16[16,64,128]{2,1,0:T(8,128)(2,1)S(1)}, bf16[16,64,128]{2,1,0:T(8,128)(2,1)}, u32[]{:S(2)}, u32[]{:S(2)}) collective-permute-start(bf16[16,64,128]{2,1,0:T(8,128)(2,1)S(1)} %collective-permute-done.72.refs_3_), channel_id=1, source_target_pairs={{0,2},{1,3},{2,0},{3,1},{4,6},{5,7},{6,4},{7,5},{8,10},{9,11},{10,... | collective-permute-start | bytes 786440 | tf_op jit(solution)/shard_map/ppermute | solution.py:50
  383.3 12.4 %collective-permute-start.78 = (bf16[16,64,128]{2,1,0:T(8,128)(2,1)}, bf16[16,64,128]{2,1,0:T(8,128)(2,1)}, u32[]{:S(2)}, u32[]{:S(2)}) collective-permute-start(bf16[16,64,128]{2,1,0:T(8,128)(2,1)} %collective-permute-done.74.refs_5_), channel_id=1, source_target_pairs={{0,2},{1,3},{2,0},{3,1},{4,6},{5,7},{6,4},{7,5},{8,10},{9,11},{10,... | collective-permute-start | bytes 786440 | tf_op jit(solution)/shard_map/ppermute | solution.py:50
  383.8 11.9 %collective-permute-start.80 = (bf16[16,64,128]{2,1,0:T(8,128)(2,1)S(1)}, bf16[16,64,128]{2,1,0:T(8,128)(2,1)S(1)}, u32[]{:S(2)}, u32[]{:S(2)}) collective-permute-start(bf16[16,64,128]{2,1,0:T(8,128)(2,1)S(1)} %collective-permute-done.72.refs_3_), channel_id=1, source_target_pairs={{0,1},{1,0},{2,3},{3,2},{4,5},{5,4},{6,7},{7,6},{8,9},{9,8},{10,11... | collective-permute-start | bytes 786440 | tf_op jit(solution)/shard_map/ppermute | solution.py:50
  385.3 11.6 %collective-permute-start.81 = (bf16[16,64,128]{2,1,0:T(8,128)(2,1)S(1)}, bf16[16,64,128]{2,1,0:T(8,128)(2,1)S(1)}, u32[]{:S(2)}, u32[]{:S(2)}) collective-permute-start(bf16[16,64,128]{2,1,0:T(8,128)(2,1)S(1)} %collective-permute-done.73.refs_4_), channel_id=1, source_target_pairs={{0,1},{1,0},{2,3},{3,2},{4,5},{5,4},{6,7},{7,6},{8,9},{9,8},{10,11... | collective-permute-start | bytes 786440 | tf_op jit(solution)/shard_map/ppermute | solution.py:50
  386.5 18.6 %collective-permute-start.82 = (bf16[16,64,128]{2,1,0:T(8,128)(2,1)}, bf16[16,64,128]{2,1,0:T(8,128)(2,1)}, u32[]{:S(2)}, u32[]{:S(2)}) collective-permute-start(bf16[16,64,128]{2,1,0:T(8,128)(2,1)} %collective-permute-done.74.refs_5_), channel_id=1, source_target_pairs={{0,1},{1,0},{2,3},{3,2},{4,5},{5,4},{6,7},{7,6},{8,9},{9,8},{10,11... | collective-permute-start | bytes 786440 | tf_op jit(solution)/shard_map/ppermute | solution.py:50
  391.1 14.0 %collective-permute-start.83 = (bf16[16,64,128]{2,1,0:T(8,128)(2,1)}, bf16[16,64,128]{2,1,0:T(8,128)(2,1)}, u32[]{:S(2)}, u32[]{:S(2)}) collective-permute-start(bf16[16,64,128]{2,1,0:T(8,128)(2,1)} %collective-permute-done.75.refs_6_), channel_id=1, source_target_pairs={{0,1},{1,0},{2,3},{3,2},{4,5},{5,4},{6,7},{7,6},{8,9},{9,8},{10,11... | collective-permute-start | bytes 786440 | tf_op jit(solution)/shard_map/ppermute | solution.py:50
  (51 other events, 272.8 us)

commit v4 on v3

--- a/solution.py
+++ b/solution.py
@@ -113,57 +113,64 @@
     )(forward, plus_start)
 
 
-def convolve_kernel(line, flip, spec_ref, panel_ref, keep, send):
+def fetch_panels(line, ahead, flip, panel_ref, held, sems):
+    chunks, _, _, rows = held.shape[:4]
+
+    def copy(chunk, step):
+        columns = pl.ds(chip_columns(line, ahead, flip, step), 2 * LANES)
+        source = panel_ref.at[:, pl.ds(chunk * rows, rows), :, columns]
+        return pltpu.make_async_copy(source, held.at[chunk, step], sems.at[chunk, step])
+
+    for chunk in range(chunks):
+        for step in range(line):
+            copy(chunk, step).start()
+
+    def wait(chunk):
+        for step in range(line):
+            copy(chunk, step).wait()
+
+    return wait
+
+
+CHUNKS = 8
+
+
+def panel_scratch(line):
+    rows = NFW // CHUNKS
+    return [
+        pltpu.VMEM((CHUNKS, line, 2, rows, LANES, 2 * LANES), BF16),
+        pltpu.SemaphoreType.DMA((CHUNKS, line)),
+    ]
+
+
+def convolve_kernel(line, flip, spec_ref, panel_ref, keep, send, held, sems):
     core = own_place(line)[3]
     focal = spec_ref.shape[2]
-
-    def body(w, carry):
-        real, imag = spec_ref[w, 0], spec_ref[w, 1]
-        left = jnp.concatenate(
-            [jnp.concatenate([real, -imag], axis=1), jnp.concatenate([imag, real], axis=1)], axis=0
-        )
-        for step in range(line):
-            columns = pl.ds(chip_columns(line, True, flip, step), 2 * LANES)
-            panel = panel_ref[:, w, :, columns].reshape(2 * LANES, 2 * LANES)
-            block = jnp.dot(left, panel, preferred_element_type=F32)
-            mine, theirs = split_cores(core, block.astype(BF16))
-            keep[step, w] = mine.reshape(2, focal, LANES)
-            send[step, w] = theirs.reshape(2, focal, LANES)
+    rows = held.shape[3]
+    wait = fetch_panels(line, True, flip, panel_ref, held, sems)
+
+    def body(chunk, carry):
+        wait(chunk)
+        for row in range(rows):
+            w = chunk * rows + row
+            real, imag = spec_ref[w, 0], spec_ref[w, 1]
+            left = jnp.concatenate(
+                [jnp.concatenate([real, -imag], axis=1), jnp.concatenate([imag, real], axis=1)], axis=0
+            )
+            for step in range(line):
+                panel = held[chunk, step, :, row].reshape(2 * LANES, 2 * LANES)
+                block = jnp.dot(left, panel, preferred_element_type=F32)
+                mine, theirs = split_cores(core, block.astype(BF16))
+                keep[step, w] = mine.reshape(2, focal, LANES)
+                send[step, w] = theirs.reshape(2, focal, LANES)
         return carry
 
-    lax.fori_loop(0, NFW, body, 0, unroll=2)
+    lax.fori_loop(0, CHUNKS, body, 0)
 
 
 VMEM = pl.BlockSpec(memory_space=pltpu.VMEM)
-SMALL = pltpu.CompilerParams(vmem_limit_bytes=12 << 20)
-
-
-def hold_kernel(parts, source, target, sems):
-    depth = source.shape[1] // parts
-    copies = [
-        pltpu.make_async_copy(
-            source.at[:, pl.ds(i * depth, depth)], target.at[:, pl.ds(i * depth, depth)], sems.at[i]
-        )
-        for i in range(parts)
-    ]
-    for copy in copies:
-        copy.start()
-    for copy in copies:
-        copy.wait()
-
-
-def hold(reflection):
-    parts = 8
-    return pl.pallas_call(
-        functools.partial(hold_kernel, parts),
-        in_specs=[pl.BlockSpec(memory_space=pl.ANY)],
-        out_specs=VMEM,
-        out_shape=jax.ShapeDtypeStruct(reflection.shape, reflection.dtype),
-        scratch_shapes=[pltpu.SemaphoreType.DMA((parts,))],
-        compiler_params=SMALL,
-        cost_estimate=pl.CostEstimate(flops=0, bytes_accessed=2 * reflection.size, transcendentals=0),
-        name="hold",
-    )(reflection)
+ANY = pl.BlockSpec(memory_space=pl.ANY)
+MEDIUM = pltpu.CompilerParams(vmem_limit_bytes=24 << 20)
 
 
 def panel_cost(focal, sources):
@@ -179,56 +186,79 @@
     out = jax.ShapeDtypeStruct((line, NFW, 2, focal, LANES), BF16)
     return pl.pallas_call(
         functools.partial(convolve_kernel, line, flip),
-        in_specs=[VMEM] * 2,
+        in_specs=[VMEM, ANY],
         out_specs=[VMEM] * 2,
         out_shape=[out] * 2,
-        compiler_params=SMALL,
+        scratch_shapes=panel_scratch(line),
+        compiler_params=MEDIUM,
         cost_estimate=panel_cost(focal, reflection.shape[3] // 2),
         name=f"convolve{flip}",
     )(spectrum, reflection)
 
 
-def correlate_kernel(line, flip, has_base, *refs):
+def correlate_kernel(line, flip, has_base, final, *refs):
     core = own_place(line)[3]
     own, other, panel_ref = refs[:line], refs[line : 2 * line], refs[2 * line]
     base_ref = refs[2 * line + 1] if has_base else None
-    out_ref = refs[-1]
-    focal = out_ref.shape[2]
-
-    def body(w, carry):
-        total = jnp.zeros((2 * LANES, 2 * focal), F32)
-        for step in range(line):
-            columns = pl.ds(chip_columns(line, False, flip, step), 2 * LANES)
-            panel = panel_ref[:, w, :, columns].reshape(2 * LANES, 2 * LANES)
-            spec = join_cores(
-                core, own[step][w].reshape(2 * focal, LANES), other[step][w].reshape(2 * focal, LANES)
-            )
-            total += lax.dot_general(panel, spec, (((1,), (1,)), ((), ())), preferred_element_type=F32)
-        total = total.T
-        real = total[:focal, :LANES] + total[focal:, LANES:]
-        imag = total[focal:, :LANES] - total[:focal, LANES:]
-        if has_base:
-            real += base_ref[w, 0]
-            imag += base_ref[w, 1]
-        out_ref[w, 0] = real
-        out_ref[w, 1] = imag
+    out_ref, held, sems, *spare = refs[2 * line + 1 + has_base :]
+    focal = own[0].shape[2]
+    rows = held.shape[3]
+    wait = fetch_panels(line, False, flip, panel_ref, held, sems)
+
+    def body(chunk, carry):
+        wait(chunk)
+        for row in range(rows):
+            w = chunk * rows + row
+            total = jnp.zeros((2 * focal, 2 * LANES), F32)
+            for step in range(line):
+                panel = held[chunk, step, :, row].reshape(2 * LANES, 2 * LANES)
+                spec = join_cores(
+                    core, own[step][w].reshape(2 * focal, LANES), other[step][w].reshape(2 * focal, LANES)
+                )
+                total += lax.dot_general(spec, panel, (((1,), (1,)), ((), ())), preferred_element_type=F32)
+            real = total[:focal, :LANES] + total[focal:, LANES:]
+            imag = total[focal:, :LANES] - total[:focal, LANES:]
+            if has_base:
+                real += base_ref[w, 0]
+                imag += base_ref[w, 1]
+            if final:
+                spare[0][pl.ds(2 * w * focal, focal), :] = real
+                spare[0][pl.ds((2 * w + 1) * focal, focal), :] = imag
+            else:
+                out_ref[w, 0] = real
+                out_ref[w, 1] = imag
         return carry
 
-    lax.fori_loop(0, NFW, body, 0, unroll=2)
-
-
-def correlate(own, other, reflection, line, flip, base=None):
+    lax.fori_loop(0, CHUNKS, body, 0)
+    if final:
+        for p in range(focal):
+            out_ref[p] = spare[0][pl.ds(p, 2 * NFW, stride=focal), :].astype(BF16)
+
+
+def correlate(own, other, reflection, line, flip, base=None, final=False):
     focal = own[0].shape[2]
     more = [] if base is None else [base]
+    shape = jax.ShapeDtypeStruct((NFW, 2, focal, LANES), F32)
+    if final:
+        shape = jax.ShapeDtypeStruct((focal, 2 * NFW, LANES), BF16)
+    spare = [pltpu.VMEM((2 * NFW * focal, LANES), F32)] if final else []
     return pl.pallas_call(
-        functools.partial(correlate_kernel, line, flip, bool(more)),
-        in_specs=[VMEM] * (2 * line + 1 + len(more)),
+        functools.partial(correlate_kernel, line, flip, bool(more), final),
+        in_specs=[VMEM] * (2 * line) + [ANY] + [VMEM] * len(more),
         out_specs=VMEM,
-        out_shape=jax.ShapeDtypeStruct((NFW, 2, focal, LANES), F32),
-        compiler_params=SMALL,
+        out_shape=shape,
+        scratch_shapes=panel_scratch(line) + spare,
+        compiler_params=MEDIUM,
         cost_estimate=panel_cost(focal, reflection.shape[3] // 2),
         name=f"correlate{flip}",
     )(*own, *other, reflection, *more)
+
+
+def windowed_spectrum(pair, onset, forward, inverse):
+    time = lax.broadcasted_iota(jnp.int32, (NT, 2 * LANES), 0)
+    values = jnp.dot(inverse, jnp.concatenate(pair, axis=1), preferred_element_type=F32)
+    kept = jnp.where(time < jnp.concatenate(onset, axis=1), values, 0.0).astype(BF16)
+    return jnp.dot(forward, kept, preferred_element_type=F32)
 
 
 def window_kernel(parts, has_base, want_spec, *refs):
@@ -238,9 +268,8 @@
     rest = refs[3 + parts :]
     base_ref = rest.pop(0) if has_base else None
     out_ref = rest.pop(0)
-    spec_ref = rest.pop(0) if want_spec else None
     held, result = rest
-    focal = out_ref.shape[2]
+    focal = part_refs[0].shape[2]
     k = 2 * NFW
     total = part_refs[0][...].astype(F32)
     for ref in part_refs[1:]:
@@ -248,16 +277,14 @@
     held[...] = total.reshape(k * focal, LANES)
     me = lax.axis_index("blk")
     columns = pl.ds(pl.multiple_of(me * LANES, LANES), LANES)
-    time = lax.broadcasted_iota(jnp.int32, (NT, 2 * LANES), 0)
+    if want_spec:
+        for p in range(focal):
+            out_ref[p] = held[pl.ds(p, k, stride=focal), :].astype(BF16)
+        return
     for p in range(0, focal, 2):
         pair = [held[pl.ds(p + q, k, stride=focal), :].astype(BF16) for q in range(2)]
-        if spec_ref is not None:
-            for q in range(2):
-                spec_ref[p + q] = pair[q]
-        field = jnp.dot(inverse_ref[...], jnp.concatenate(pair, axis=1), preferred_element_type=F32)
-        onset = jnp.concatenate([onset_ref[p + q : p + q + 1, columns] for q in range(2)], axis=1)
-        kept = jnp.where(time < onset, field, 0.0).astype(BF16)
-        spectrum = jnp.dot(forward_ref[...], kept, preferred_element_type=F32)
+        onset = [onset_ref[p + q : p + q + 1, columns] for q in range(2)]
+        spectrum = windowed_spectrum(pair, onset, forward_ref[...], inverse_ref[...])
         for q in range(2):
             result[pl.ds(p + q, k, stride=focal), :] = spectrum[:, q * LANES : (q + 1) * LANES]
     final = result[...].reshape(NFW, 2, focal, LANES)
@@ -270,14 +297,13 @@
     focal = parts[0].shape[2]
     k = 2 * NFW
     operands = [forward, inverse, onset_times, *parts] + ([] if base is None else [base])
-    whole = pl.BlockSpec(memory_space=pltpu.VMEM)
-    out = [jax.ShapeDtypeStruct((NFW, 2, focal, LANES), BF16)]
+    out = jax.ShapeDtypeStruct((NFW, 2, focal, LANES), BF16)
     if want_spec:
-        out.append(jax.ShapeDtypeStruct((focal, k, LANES), BF16))
+        out = jax.ShapeDtypeStruct((focal, k, LANES), BF16)
     return pl.pallas_call(
         functools.partial(window_kernel, len(parts), base is not None, want_spec),
-        in_specs=[whole] * len(operands),
-        out_specs=[whole] * len(out),
+        in_specs=[VMEM] * len(operands),
+        out_specs=VMEM,
         out_shape=out,
         scratch_shapes=[pltpu.VMEM((k * focal, LANES), F32)] * 2,
         compiler_params=pltpu.CompilerParams(vmem_limit_bytes=16 << 20),
@@ -286,6 +312,36 @@
         ),
         name="window",
     )(*operands)
+
+
+def window_at_kernel(line, flip, step, forward_ref, inverse_ref, onset_ref, spec_ref, out_ref, result):
+    core = own_place(line)[3]
+    focal, k, _ = spec_ref.shape
+    start = chip_columns(line, False, flip, step) + core * LANES
+    columns = pl.ds(pl.multiple_of(start, LANES), LANES)
+    for p in range(0, focal, 2):
+        onset = [onset_ref[p + q : p + q + 1, columns] for q in range(2)]
+        pair = [spec_ref[p + q] for q in range(2)]
+        spectrum = windowed_spectrum(pair, onset, forward_ref[...], inverse_ref[...])
+        for q in range(2):
+            result[pl.ds(p + q, k, stride=focal), :] = spectrum[:, q * LANES : (q + 1) * LANES]
+    out_ref[...] = result[...].reshape(NFW, 2, focal, LANES).astype(BF16)
+
+
+def window_at(spec, forward, inverse, onset_times, line, flip, step):
+    focal, k, _ = spec.shape
+    return pl.pallas_call(
+        functools.partial(window_at_kernel, line, flip, step),
+        in_specs=[VMEM] * 4,
+        out_specs=VMEM,
+        out_shape=jax.ShapeDtypeStruct((NFW, 2, focal, LANES), BF16),
+        scratch_shapes=[pltpu.VMEM((k * focal, LANES), F32)],
+        compiler_params=pltpu.CompilerParams(vmem_limit_bytes=16 << 20),
+        cost_estimate=pl.CostEstimate(
+            flops=4 * k * NT * focal * LANES, bytes_accessed=2 * k * focal * LANES * 6, transcendentals=0
+        ),
+        name="window_at",
+    )(forward, inverse, onset_times, spec)
 
 
 def field_kernel(line, rows, has_plus, *refs):
@@ -329,7 +385,7 @@
         + [wide] * len(plus),
         out_specs=wide,
         out_shape=jax.ShapeDtypeStruct((focal, samples, width), BF16),
-        compiler_params=pltpu.CompilerParams(vmem_limit_bytes=16 << 20),
+        compiler_params=pltpu.CompilerParams(vmem_limit_bytes=40 << 20),
         cost_estimate=pl.CostEstimate(
             flops=2 * k * focal * samples * width,
             bytes_accessed=2 * focal * width * (k + 2 * samples),
@@ -354,32 +410,39 @@
     return sorted(range(line), key=lambda step: -min(step, line - step))
 
 
-def reduce_scatter(places, keep0, keep1, send0, send1):
-    got1 = places.send(send1, places.core())
-    got0 = places.send(send0, places.core())
-    order = far_first(places.line)
+def across_pair(places, keep, send):
+    got = places.send(send, places.core())
     across = {}
-    ready = got1
-    for step in order:
-        ready = add(keep1[step], after(got1, ready)[step]).astype(BF16)
-        across[step] = places.send(ready, places.pair())
-    parts = [keep0[0], got0[0], across[0]]
-    ready = got0
-    for step in order[:-1]:
-        ready = add(keep0[step], after(got0, ready)[step], across[step]).astype(BF16)
+    for step in far_first(places.line):
+        across[step] = places.send(add(keep[step], got[step]).astype(BF16), places.pair())
+    return got, across
+
+
+def along_line(places, keep, send, across):
+    got = places.send(send, places.core())
+    parts = [keep[0], got[0], across[0]]
+    ready = got
+    for step in far_first(places.line)[:-1]:
+        ready = add(keep[step], after(got, ready)[step], across[step]).astype(BF16)
         parts.append(places.send(ready, places.shift(step)))
     return parts
 
 
-def all_gather(places, block):
+def gather_chips(places, block):
     near_first = far_first(places.line)[::-1]
-    line = {0: block}
+    line, across = {0: block}, {}
+    ready = block
     for step in near_first[1:]:
-        line[step] = places.send(block, places.shift(step))
-    across = {step: places.send(line[step], places.pair()) for step in near_first}
-    own = [[side[step] for step in range(places.line)] for side in (line, across)]
-    other = [[places.send(piece, places.core()) for piece in side] for side in own]
-    return own, other
+        away = min(step, places.line - step)
+        ready = block if away == 1 else after(block, line[near_first[1]])
+        line[step] = places.send(ready, places.shift(step))
+    for step in near_first:
+        across[step] = places.send(line[step], places.pair())
+    return [[side[step] for step in range(places.line)] for side in (line, across)]
+
+
+def other_cores(places, sides):
+    return [[places.send(piece, places.core()) for piece in side] for side in sides]
 
 
 def local(plus_start, reflection, onset_times):
@@ -391,30 +454,39 @@
     own_samples = lax.axis_index("blk") * samples + jnp.arange(samples, dtype=jnp.int32)
     own_forward, own_inverse = tables_of(own_samples)
 
-    parts = reduce_scatter(places, *first_analysis(plus_start, own_forward, line))
-    start = add(*parts).astype(BF16)
+    keep0, keep1, send0, send1 = first_analysis(plus_start, own_forward, line)
+    _, across = across_pair(places, keep1, send1)
+    start = add(*along_line(places, keep0, send0, across)).astype(BF16)
     start = jnp.transpose(start, (1, 0, 2)).reshape(NFW, 2, focal, LANES)
     spectrum_plus = start
-    reflection = hold(reflection)
     for iteration in range(ITERS):
         last = iteration + 1 == ITERS
         keep1, send1 = convolve(spectrum_plus, reflection, line, 1)
-        keep0, send0 = convolve(after(spectrum_plus, keep1), reflection, line, 0)
-        parts = reduce_scatter(places, keep0, keep1, send0, send1)
-        windowed = window(parts, forward, inverse, onset_times, want_spec=last)
-        gathered = all_gather(places, windowed[0])
+        got1, across = across_pair(places, keep1, send1)
+        keep0, send0 = convolve(after(spectrum_plus, got1), reflection, line, 0)
+        parts = along_line(places, keep0, send0, across)
         if last:
-            upgoing_spec = all_gather(places, windowed[1])
-        own, other = gathered
+            upgoing_spec = gather_chips(
+                places, window(parts, forward, inverse, onset_times, want_spec=True)
+            )
+            own = [
+                [
+                    window_at(piece, forward, inverse, onset_times, line, flip, step)
+                    for step, piece in enumerate(side)
+                ]
+                for flip, side in enumerate(upgoing_spec)
+            ]
+        else:
+            own = gather_chips(places, window(parts, forward, inverse, onset_times))
+        other = other_cores(places, own)
         downgoing_spec = correlate(own[0], other[0], reflection, line, 0)
-        downgoing_spec = correlate(own[1], other[1], reflection, line, 1, downgoing_spec)
+        downgoing_spec = correlate(own[1], other[1], reflection, line, 1, downgoing_spec, last)
         if not last:
-            (spectrum_plus,) = window([downgoing_spec], forward, inverse, onset_times, base=start)
-    upgoing = field(*upgoing_spec, own_inverse, onset_times, line)
-    final = jnp.transpose(
-        downgoing_spec.astype(BF16).reshape(2 * NFW, focal, LANES), (1, 0, 2)
-    )
-    downgoing = field(*all_gather(places, final), own_inverse, onset_times, line, plus_start)
+            spectrum_plus = window([downgoing_spec], forward, inverse, onset_times, base=start)
+    other = other_cores(places, upgoing_spec)
+    upgoing = field(upgoing_spec, other, own_inverse, onset_times, line)
+    own = gather_chips(places, downgoing_spec)
+    downgoing = field(own, other_cores(places, own), own_inverse, onset_times, line, plus_start)
     return upgoing, downgoing
 
 

time: 413 us -> 331 us (0.80)
  local copies, waits for them, and re-layouts: 68.5 us -> 16 us
  starting transfers between devices: 109 us -> 61.6 us
  waiting for transfers between devices: 141 us -> 153 us
  Pallas kernels: 80.5 us -> 91.4 us
    unnamed x56 -> x46, local copies, waits for them, and re-layouts: 66.6 us -> 14.4 us
    ppermute x87 -> x80, starting transfers between devices: 109 us -> 61.6 us  [send(): return lax.ppermute(array, self.axis, pairs)]
    ppermute x87 -> x80, waiting for transfers between devices: 141 us -> 153 us  [send(): return lax.ppermute(array, self.axis, pairs)]
    pallas_call x1 -> x8, Pallas kernels: 10.7 us -> 18.9 us  [window_at(): pl.pallas_call(functools.partial(window_at_kernel, line, flip, step), in_...]
    pallas_call x4, Pallas kernels: 21.5 us -> 27.3 us  [convolve(): pl.pallas_call(functools.partial(convolve_kernel, line, flip), in_specs=[...]
    convert_element_type x22 -> x12, other arithmetic: 8.6 us -> 5.71 us  [the longest x9 4.02 us: along_line(): ready = add(keep[step], after(got, ready)[step], across[step]).astype(BF16)]
  transfers between devices with their start and end apart: 87 -> 80, of which waited for: 32 -> 32; matrix products, arithmetic and copies ran while one was open for 3% -> 2% of each run, Pallas kernels for 12% -> 13%
where the time goes in v4:
time: 331 us; the launch traced here: 330 us
  waiting for transfers between devices  153 us (46%)
  Pallas kernels  91.4 us (28%)
  starting transfers between devices  61.6 us (19%)
  local copies, waits for them, and re-layouts  16 us (5%)
  other arithmetic  6.49 us (2%)
    ppermute x80, waiting for transfers between devices, send(): return lax.ppermute(array, self.axis, pairs)  153 us
    ppermute x80, starting transfers between devices, send(): return lax.ppermute(array, self.axis, pairs)  61.6 us
    pallas_call x4, Pallas kernels, correlate(): pl.pallas_call(functools.partial(correlate_kernel, line, flip, bool(more)...  30.8 us
    pallas_call x4, Pallas kernels, convolve(): pl.pallas_call(functools.partial(convolve_kernel, line, flip), in_specs=[...  27.3 us
    pallas_call x8, Pallas kernels, window_at(): pl.pallas_call(functools.partial(window_at_kernel, line, flip, step), in_...  18.9 us
    unnamed x46, local copies, waits for them, and re-layouts  14.4 us
    pallas_call x2, Pallas kernels, field(): pl.pallas_call(functools.partial(field_kernel, line, rows, bool(plus)), g...  7.05 us
  transfers between devices with their start and end apart: 80, of which 32 were waited for; matrix products, arithmetic and copies ran while one was open for 2% of the time, Pallas kernels for 13%

profile of v4, /device:TPU:0, one launch (start us, length us, event | category | flops | bytes accessed | tf_op | source)
XLA Modules:
  0.0 330.2 jit_solution(18435975093564179258)
XLA Ops:
  0.9 1.6 copy-done
  2.4 2.1 first_analysis.1
  5.1 2.2 collective-permute-done.1
  7.7 3.0 collective-permute-start.3
  10.7 1.9 collective-permute-start.7
  12.8 5.0 %collective-permute-done.3 = bf16[16,64,128]{2,1,0:T(8,128)(2,1)S(1)} collective-permute-done((bf16[16,64,128]{2,1,0:T(8,128)(2,1)S(1)}, bf16[16,64,128]{2,1,0:T(8,128)(2,1)S(1)}, u32[]{:S(2)}, u32[]{:S(2)}) %collective-permute-start.3) | collective-permute-done | bytes 262176 | tf_op jit(solution)/shard_map/ppermute | solution.py:50
  17.9 5.5 %collective-permute-done.5 = bf16[16,64,128]{2,1,0:T(8,128)(2,1)S(1)} collective-permute-done((bf16[16,64,128]{2,1,0:T(8,128)(2,1)S(1)}, bf16[16,64,128]{2,1,0:T(8,128)(2,1)S(1)}, u32[]{:S(2)}, u32[]{:S(2)}) %collective-permute-start.5) | collective-permute-done | bytes 262176 | tf_op jit(solution)/shard_map/ppermute | solution.py:50
  23.5 5.5 %collective-permute-done.7 = bf16[16,64,128]{2,1,0:T(8,128)(2,1)S(1)} collective-permute-done((bf16[16,64,128]{2,1,0:T(8,128)(2,1)S(1)}, bf16[16,64,128]{2,1,0:T(8,128)(2,1)S(1)}, u32[]{:S(2)}, u32[]{:S(2)}) %collective-permute-start.7) | collective-permute-done | bytes 262176 | tf_op jit(solution)/shard_map/ppermute | solution.py:50
  29.1 4.2 %collective-permute-start.8 = (bf16[16,64,128]{2,1,0:T(8,128)(2,1)S(1)}, bf16[16,64,128]{2,1,0:T(8,128)(2,1)S(1)}, u32[]{:S(2)}, u32[]{:S(2)}) collective-permute-start(bf16[16,64,128]{2,1,0:T(8,128)(2,1)S(1)} %fusion.6), channel_id=1, source_target_pairs={{0,12},{1,13},{2,14},{3,15},{4,0},{5,1},{6,2},{7,3},{8,4},{9,5},{1... | collective-permute-start | bytes 786440 | tf_op jit(solution)/shard_map/ppermute | solution.py:50
  34.3 5.8 %collective-permute-done.8 = bf16[16,64,128]{2,1,0:T(8,128)(2,1)S(1)} collective-permute-done((bf16[16,64,128]{2,1,0:T(8,128)(2,1)S(1)}, bf16[16,64,128]{2,1,0:T(8,128)(2,1)S(1)}, u32[]{:S(2)}, u32[]{:S(2)}) %collective-permute-start.8) | collective-permute-done | bytes 262176 | tf_op jit(solution)/shard_map/ppermute | solution.py:50
  40.1 6.5 %collective-permute-done.6 = bf16[16,64,128]{2,1,0:T(8,128)(2,1)S(1)} collective-permute-done((bf16[16,64,128]{2,1,0:T(8,128)(2,1)S(1)}, bf16[16,64,128]{2,1,0:T(8,128)(2,1)S(1)}, u32[]{:S(2)}, u32[]{:S(2)}) %collective-permute-start.6) | collective-permute-done | bytes 262176 | tf_op jit(solution)/shard_map/ppermute | solution.py:50
  46.7 7.6 %collective-permute-done.4 = bf16[16,64,128]{2,1,0:T(8,128)(2,1)S(1)} collective-permute-done((bf16[16,64,128]{2,1,0:T(8,128)(2,1)S(1)}, bf16[16,64,128]{2,1,0:T(8,128)(2,1)S(1)}, u32[]{:S(2)}, u32[]{:S(2)}) %collective-permute-start.4) | collective-permute-done | bytes 262176 | tf_op jit(solution)/shard_map/ppermute | solution.py:50
  54.7 6.8 %convolve1.2 = (bf16[4,32,2,16,128]{4,3,2,1,0:T(8,128)(2,1)S(1)}, bf16[4,32,2,16,128]{4,3,2,1,0:T(8,128)(2,1)S(1)}) custom-call(bf16[32,2,16,128]{3,2,1,0:T(8,128)(2,1)S(1)} %bitcast.87, bf16[2,32,128,2048]{3,2,1,0:T(8,128)(2,1)} %refs_8_.7), custom_call_target="tpu_custom_call" | custom-call | flops 536870912 | bytes 18874368 | tf_op jit(solution)/shard_map/convolve1/pallas_call | solution.py:187
  61.6 2.6 collective-permute-done.9
  64.3 6.8 %convolve0.2 = (bf16[4,32,2,16,128]{4,3,2,1,0:T(8,128)(2,1)S(1)}, bf16[4,32,2,16,128]{4,3,2,1,0:T(8,128)(2,1)S(1)}) custom-call(bf16[32,2,16,128]{3,2,1,0:T(8,128)(2,1)S(1)} %bitcast.88, bf16[2,32,128,2048]{3,2,1,0:T(8,128)(2,1)} %refs_8_.7), custom_call_target="tpu_custom_call" | custom-call | flops 536870912 | bytes 18874368 | tf_op jit(solution)/shard_map/convolve0/pallas_call | solution.py:187
  77.2 4.5 %collective-permute-done.12 = bf16[32,2,16,128]{3,2,1,0:T(8,128)(2,1)} collective-permute-done((bf16[32,2,16,128]{3,2,1,0:T(8,128)(2,1)}, bf16[32,2,16,128]{3,2,1,0:T(8,128)(2,1)}, u32[]{:S(2)}, u32[]{:S(2)}) %collective-permute-start.12) | collective-permute-done | bytes 262176 | tf_op jit(solution)/shard_map/ppermute | solution.py:50
  83.0 4.4 %collective-permute-done.14 = bf16[32,2,16,128]{3,2,1,0:T(8,128)(2,1)} collective-permute-done((bf16[32,2,16,128]{3,2,1,0:T(8,128)(2,1)S(1)}, bf16[32,2,16,128]{3,2,1,0:T(8,128)(2,1)}, u32[]{:S(2)}, u32[]{:S(2)}) %collective-permute-start.14) | collective-permute-done | bytes 262176 | tf_op jit(solution)/shard_map/ppermute | solution.py:50
  88.6 4.3 %collective-permute-done.16 = bf16[32,2,16,128]{3,2,1,0:T(8,128)(2,1)S(1)} collective-permute-done((bf16[32,2,16,128]{3,2,1,0:T(8,128)(2,1)S(1)}, bf16[32,2,16,128]{3,2,1,0:T(8,128)(2,1)S(1)}, u32[]{:S(2)}, u32[]{:S(2)}) %collective-permute-start.16) | collective-permute-done | bytes 262176 | tf_op jit(solution)/shard_map/ppermute | solution.py:50
  93.9 2.7 collective-permute-start.17
  98.0 10.0 %collective-permute-done.17.refs_8_ = bf16[32,2,16,128]{3,2,1,0:T(8,128)(2,1)S(1)} collective-permute-done((bf16[32,2,16,128]{3,2,1,0:T(8,128)(2,1)S(1)}, bf16[32,2,16,128]{3,2,1,0:T(8,128)(2,1)S(1)}, u32[]{:S(2)}, u32[]{:S(2)}) %collective-permute-start.17) | collective-permute-done | bytes 262176 | tf_op jit(solution)/shard_map/ppermute | solution.py:50
  108.0 2.5 window.3.refs_0_
  114.1 9.5 %collective-permute-done.21.refs_3_ = bf16[32,2,16,128]{3,2,1,0:T(8,128)(2,1)S(1)} collective-permute-done((bf16[32,2,16,128]{3,2,1,0:T(8,128)(2,1)S(1)}, bf16[32,2,16,128]{3,2,1,0:T(8,128)(2,1)S(1)}, u32[]{:S(2)}, u32[]{:S(2)}) %collective-permute-start.21) | collective-permute-done | bytes 262176 | tf_op jit(solution)/shard_map/ppermute | solution.py:50
  123.6 1.6 collective-permute-done.19.refs_1_
  125.7 3.1 collective-permute-start.20
  128.9 6.8 %collective-permute-done.22.refs_2_ = bf16[32,2,16,128]{3,2,1,0:T(8,128)(2,1)S(1)} collective-permute-done((bf16[32,2,16,128]{3,2,1,0:T(8,128)(2,1)S(1)}, bf16[32,2,16,128]{3,2,1,0:T(8,128)(2,1)S(1)}, u32[]{:S(2)}, u32[]{:S(2)}) %collective-permute-start.22) | collective-permute-done | bytes 262176 | tf_op jit(solution)/shard_map/ppermute | solution.py:50
  137.7 3.8 %collective-permute-done.24.refs_3_ = bf16[32,2,16,128]{3,2,1,0:T(8,128)(2,1)S(1)} collective-permute-done((bf16[32,2,16,128]{3,2,1,0:T(8,128)(2,1)S(1)}, bf16[32,2,16,128]{3,2,1,0:T(8,128)(2,1)S(1)}, u32[]{:S(2)}, u32[]{:S(2)}) %collective-permute-start.24) | collective-permute-done | bytes 262176 | tf_op jit(solution)/shard_map/ppermute | solution.py:50
  141.6 5.0 %collective-permute-done.23.refs_2_ = bf16[32,2,16,128]{3,2,1,0:T(8,128)(2,1)S(1)} collective-permute-done((bf16[32,2,16,128]{3,2,1,0:T(8,128)(2,1)S(1)}, bf16[32,2,16,128]{3,2,1,0:T(8,128)(2,1)S(1)}, u32[]{:S(2)}, u32[]{:S(2)}) %collective-permute-start.23) | collective-permute-done | bytes 262176 | tf_op jit(solution)/shard_map/ppermute | solution.py:50
  146.5 7.6 %correlate0.2.refs_9_ = f32[32,2,16,128]{3,2,1,0:T(8,128)S(1)} custom-call(bf16[32,2,16,128]{3,2,1,0:T(8,128)(2,1)S(1)} %window.3.refs_0_, bf16[32,2,16,128]{3,2,1,0:T(8,128)(2,1)S(1)} %collective-permute-done.19.refs_1_, bf16[32,2,16,128]{3,2,1,0:T(8,128)(2,1)S(1)} %collective-permute-done.22.refs_2_, ...), custom_call_target="tpu_custom_call" | custom-call | flops 536870912 | bytes 18874368 | tf_op jit(solution)/shard_map/correlate0/pallas_call | solution.py:245
  154.2 7.7 %correlate1.2.refs_3_ = f32[32,2,16,128]{3,2,1,0:T(8,128)S(1)} custom-call(bf16[32,2,16,128]{3,2,1,0:T(8,128)(2,1)S(1)} %collective-permute-done.18.refs_0_, bf16[32,2,16,128]{3,2,1,0:T(8,128)(2,1)S(1)} %collective-permute-done.20.refs_1_, bf16[32,2,16,128]{3,2,1,0:T(8,128)(2,1)S(1)} %collective-permute-done.23.refs_2_, ...), custom_call_target="tpu_custom_call" | custom-call | flops 536870912 | bytes 18874368 | tf_op jit(solution)/shard_map/correlate1/pallas_call | solution.py:245
  161.9 2.3 window.4.spec_ref
  164.3 6.8 %convolve1.3 = (bf16[4,32,2,16,128]{4,3,2,1,0:T(8,128)(2,1)S(1)}, bf16[4,32,2,16,128]{4,3,2,1,0:T(8,128)(2,1)S(1)}) custom-call(bf16[32,2,16,128]{3,2,1,0:T(8,128)(2,1)S(1)} %window.4.spec_ref, bf16[2,32,128,2048]{3,2,1,0:T(8,128)(2,1)} %refs_8_.7), custom_call_target="tpu_custom_call" | custom-call | flops 536870912 | bytes 18874368 | tf_op jit(solution)/shard_map/convolve1/pallas_call | solution.py:187
  171.7 2.3 collective-permute-done.33
  174.0 6.8 %convolve0.3 = (bf16[4,32,2,16,128]{4,3,2,1,0:T(8,128)(2,1)S(1)}, bf16[4,32,2,16,128]{4,3,2,1,0:T(8,128)(2,1)S(1)}) custom-call(bf16[32,2,16,128]{3,2,1,0:T(8,128)(2,1)S(1)} %window.4.spec_ref, bf16[2,32,128,2048]{3,2,1,0:T(8,128)(2,1)} %refs_8_.7), custom_call_target="tpu_custom_call" | custom-call | flops 536870912 | bytes 18874368 | tf_op jit(solution)/shard_map/convolve0/pallas_call | solution.py:187
  181.6 1.8 collective-permute-start.36
  183.6 1.7 collective-permute-start.40
  185.7 5.1 %collective-permute-done.36 = bf16[32,2,16,128]{3,2,1,0:T(8,128)(2,1)S(1)} collective-permute-done((bf16[32,2,16,128]{3,2,1,0:T(8,128)(2,1)S(1)}, bf16[32,2,16,128]{3,2,1,0:T(8,128)(2,1)S(1)}, u32[]{:S(2)}, u32[]{:S(2)}) %collective-permute-start.36) | collective-permute-done | bytes 262176 | tf_op jit(solution)/shard_map/ppermute | solution.py:50
  191.9 4.5 %collective-permute-done.38 = bf16[32,2,16,128]{3,2,1,0:T(8,128)(2,1)S(1)} collective-permute-done((bf16[32,2,16,128]{3,2,1,0:T(8,128)(2,1)S(1)}, bf16[32,2,16,128]{3,2,1,0:T(8,128)(2,1)S(1)}, u32[]{:S(2)}, u32[]{:S(2)}) %collective-permute-start.38) | collective-permute-done | bytes 262176 | tf_op jit(solution)/shard_map/ppermute | solution.py:50
  198.0 4.0 %collective-permute-done.40 = bf16[32,2,16,128]{3,2,1,0:T(8,128)(2,1)S(1)} collective-permute-done((bf16[32,2,16,128]{3,2,1,0:T(8,128)(2,1)S(1)}, bf16[32,2,16,128]{3,2,1,0:T(8,128)(2,1)S(1)}, u32[]{:S(2)}, u32[]{:S(2)}) %collective-permute-start.40) | collective-permute-done | bytes 262176 | tf_op jit(solution)/shard_map/ppermute | solution.py:50
  202.1 3.8 %collective-permute-start.41 = (bf16[32,2,16,128]{3,2,1,0:T(8,128)(2,1)S(1)}, bf16[32,2,16,128]{3,2,1,0:T(8,128)(2,1)S(1)}, u32[]{:S(2)}, u32[]{:S(2)}) collective-permute-start(bf16[32,2,16,128]{3,2,1,0:T(8,128)(2,1)S(1)} %fusion), channel_id=1, source_target_pairs={{0,12},{1,13},{2,14},{3,15},{4,0},{5,1},{6,2},{7,3},{8,4},{9,5},{1... | collective-permute-start | bytes 786440 | tf_op jit(solution)/shard_map/ppermute | solution.py:50
  206.8 8.6 %collective-permute-done.41.refs_8_ = bf16[32,2,16,128]{3,2,1,0:T(8,128)(2,1)S(1)} collective-permute-done((bf16[32,2,16,128]{3,2,1,0:T(8,128)(2,1)S(1)}, bf16[32,2,16,128]{3,2,1,0:T(8,128)(2,1)S(1)}, u32[]{:S(2)}, u32[]{:S(2)}) %collective-permute-start.41) | collective-permute-done | bytes 262176 | tf_op jit(solution)/shard_map/ppermute | solution.py:50
  215.9 1.9 collective-permute-start.43
  218.0 6.7 %collective-permute-done.43.refs_5_.spec_ref = bf16[16,64,128]{2,1,0:T(8,128)(2,1)S(1)} collective-permute-done((bf16[16,64,128]{2,1,0:T(8,128)(2,1)S(1)}, bf16[16,64,128]{2,1,0:T(8,128)(2,1)S(1)}, u32[]{:S(2)}, u32[]{:S(2)}) %collective-permute-start.43) | collective-permute-done | bytes 262176 | tf_op jit(solution)/shard_map/ppermute | solution.py:50
  227.6 3.7 %collective-permute-done.42.refs_3_.spec_ref = bf16[16,64,128]{2,1,0:T(8,128)(2,1)S(1)} collective-permute-done((bf16[16,64,128]{2,1,0:T(8,128)(2,1)S(1)}, bf16[16,64,128]{2,1,0:T(8,128)(2,1)S(1)}, u32[]{:S(2)}, u32[]{:S(2)}) %collective-permute-start.42) | collective-permute-done | bytes 262176 | tf_op jit(solution)/shard_map/ppermute | solution.py:50
  233.3 2.3 window_at.12.refs_0_
  235.7 5.8 %collective-permute-done.44.refs_4_.spec_ref = bf16[16,64,128]{2,1,0:T(8,128)(2,1)S(1)} collective-permute-done((bf16[16,64,128]{2,1,0:T(8,128)(2,1)S(1)}, bf16[16,64,128]{2,1,0:T(8,128)(2,1)S(1)}, u32[]{:S(2)}, u32[]{:S(2)}) %collective-permute-start.44) | collective-permute-done | bytes 262176 | tf_op jit(solution)/shard_map/ppermute | solution.py:50
  242.9 2.3 window_at.13.refs_1_
  245.3 2.3 window_at.15.refs_3_
  248.2 2.3 window_at.8.refs_0_
  250.5 2.3 window_at.14.refs_2_
  252.9 2.3 window_at.9.refs_1_
  255.4 2.3 window_at.11.refs_3_
  258.2 2.6 window_at.10.refs_2_
  261.9 7.6 %correlate0.3.refs_9_ = f32[32,2,16,128]{3,2,1,0:T(8,128)S(1)} custom-call(bf16[32,2,16,128]{3,2,1,0:T(8,128)(2,1)S(1)} %window_at.12.refs_0_, bf16[32,2,16,128]{3,2,1,0:T(8,128)(2,1)S(1)} %window_at.13.refs_1_, bf16[32,2,16,128]{3,2,1,0:T(8,128)(2,1)S(1)} %window_at.14.refs_2_, bf16[32,2,16,128]{3,2,1,0:T(8,128)(2,1)S(1)} %window_at.15.refs_3_, ...), custom_call_target="tpu_custom_call" | custom-call | flops 536870912 | bytes 18874368 | tf_op jit(solution)/shard_map/correlate0/pallas_call | solution.py:245
  269.7 7.8 %correlate1.3.refs_2_ = bf16[16,64,128]{2,1,0:T(8,128)(2,1)S(1)} custom-call(bf16[32,2,16,128]{3,2,1,0:T(8,128)(2,1)S(1)} %window_at.8.refs_0_, bf16[32,2,16,128]{3,2,1,0:T(8,128)(2,1)S(1)} %window_at.9.refs_1_, bf16[32,2,16,128]{3,2,1,0:T(8,128)(2,1)S(1)} %window_at.10.refs_2_, bf16[32,2,16,128]{3,2,1,0:T(8,128)(2,1)S(1)} %window_at.11.refs_3_, ...), custom_call_target="tpu_custom_call" | custom-call | flops 536870912 | bytes 18874368 | tf_op jit(solution)/shard_map/correlate1/pallas_call | solution.py:245
  277.5 2.2 collective-permute-start.66
  281.5 4.7 %collective-permute-done.66.refs_5_ = bf16[16,64,128]{2,1,0:T(8,128)(2,1)S(1)} collective-permute-done((bf16[16,64,128]{2,1,0:T(8,128)(2,1)S(1)}, bf16[16,64,128]{2,1,0:T(8,128)(2,1)S(1)}, u32[]{:S(2)}, u32[]{:S(2)}) %collective-permute-start.66) | collective-permute-done | bytes 262176 | tf_op jit(solution)/shard_map/ppermute | solution.py:50
  290.2 4.0 %collective-permute-start.67 = (bf16[16,64,128]{2,1,0:T(8,128)(2,1)S(1)}, bf16[16,64,128]{2,1,0:T(8,128)(2,1)}, u32[]{:S(2)}, u32[]{:S(2)}) collective-permute-start(bf16[16,64,128]{2,1,0:T(8,128)(2,1)S(1)} %correlate1.3.refs_2_), channel_id=1, source_target_pairs={{0,8},{1,9},{2,10},{3,11},{4,12},{5,13},{6,14},{7,15},{8,0},{9,1},... | collective-permute-start | bytes 786440 | tf_op jit(solution)/shard_map/ppermute | solution.py:50
  294.2 3.3 %collective-permute-done.65.refs_3_ = bf16[16,64,128]{2,1,0:T(8,128)(2,1)S(1)} collective-permute-done((bf16[16,64,128]{2,1,0:T(8,128)(2,1)S(1)}, bf16[16,64,128]{2,1,0:T(8,128)(2,1)S(1)}, u32[]{:S(2)}, u32[]{:S(2)}) %collective-permute-start.65) | collective-permute-done | bytes 262176 | tf_op jit(solution)/shard_map/ppermute | solution.py:50
  298.5 1.7 collective-permute-start.71
  302.2 6.4 %collective-permute-done.67.refs_4_ = bf16[16,64,128]{2,1,0:T(8,128)(2,1)} collective-permute-done((bf16[16,64,128]{2,1,0:T(8,128)(2,1)S(1)}, bf16[16,64,128]{2,1,0:T(8,128)(2,1)}, u32[]{:S(2)}, u32[]{:S(2)}) %collective-permute-start.67) | collective-permute-done | bytes 262176 | tf_op jit(solution)/shard_map/ppermute | solution.py:50
  308.9 2.2 collective-permute-done.71.refs_9_
  313.0 4.2 %collective-permute-done.70.refs_8_ = bf16[16,64,128]{2,1,0:T(8,128)(2,1)} collective-permute-done((bf16[16,64,128]{2,1,0:T(8,128)(2,1)}, bf16[16,64,128]{2,1,0:T(8,128)(2,1)}, u32[]{:S(2)}, u32[]{:S(2)}) %collective-permute-start.70) | collective-permute-done | bytes 262176 | tf_op jit(solution)/shard_map/ppermute | solution.py:50
  323.0 2.6 field.2
  325.7 4.5 %field.3 = bf16[16,32,2048]{2,1,0:T(8,128)(2,1)} custom-call(bf16[32,64]{1,0:T(8,128)(2,1)S(1)} %bitcast.102, s32[16,2048]{1,0:T(8,128)S(1)} %copy-done.2, bf16[16,64,128]{2,1,0:T(8,128)(2,1)S(1)} %correlate1.3.refs_2_, bf16[16,64,128]{2,1,0:T(8,128)(2,1)S(1)} %copy-done.8, bf16[16,64,128]{2,1,0:T(8,128)(2,1)} %collective-permute-done.67.refs_4_, ...), custom_call_target="tpu_custom_call" | custom-call | flops 134217728 | bytes 8388608 | tf_op jit(solution)/shard_map/field/pallas_call | solution.py:377
  (195 shorter events, 52.2 us)
Async XLA Ops:
  7.7 10.0 %collective-permute-start.3 = (bf16[16,64,128]{2,1,0:T(8,128)(2,1)S(1)}, bf16[16,64,128]{2,1,0:T(8,128)(2,1)S(1)}, u32[]{:S(2)}, u32[]{:S(2)}) collective-permute-start(bf16[16,64,128]{2,1,0:T(8,128)(2,1)S(1)} %get-tuple-element.65), channel_id=1, source_target_pairs={{0,2},{1,3},{2,0},{3,1},{4,6},{5,7},{6,4},{7,5},{8,10},{9,11},{10,... | collective-permute-start | bytes 786440 | tf_op jit(solution)/shard_map/ppermute | solution.py:50
  10.6 12.7 %collective-permute-start.5 = (bf16[16,64,128]{2,1,0:T(8,128)(2,1)S(1)}, bf16[16,64,128]{2,1,0:T(8,128)(2,1)S(1)}, u32[]{:S(2)}, u32[]{:S(2)}) collective-permute-start(bf16[16,64,128]{2,1,0:T(8,128)(2,1)S(1)} %get-tuple-element.64), channel_id=1, source_target_pairs={{0,2},{1,3},{2,0},{3,1},{4,6},{5,7},{6,4},{7,5},{8,10},{9,11},{10,... | collective-permute-start | bytes 786440 | tf_op jit(solution)/shard_map/ppermute | solution.py:50
  10.7 18.2 %collective-permute-start.7 = (bf16[16,64,128]{2,1,0:T(8,128)(2,1)S(1)}, bf16[16,64,128]{2,1,0:T(8,128)(2,1)S(1)}, u32[]{:S(2)}, u32[]{:S(2)}) collective-permute-start(bf16[16,64,128]{2,1,0:T(8,128)(2,1)S(1)} %get-tuple-element.63), channel_id=1, source_target_pairs={{0,2},{1,3},{2,0},{3,1},{4,6},{5,7},{6,4},{7,5},{8,10},{9,11},{10,... | collective-permute-start | bytes 786440 | tf_op jit(solution)/shard_map/ppermute | solution.py:50
  12.7 21.6 %collective-permute-start.2 = (bf16[16,64,128]{2,1,0:T(8,128)(2,1)S(1)}, bf16[16,64,128]{2,1,0:T(8,128)(2,1)S(1)}, u32[]{:S(2)}, u32[]{:S(2)}) collective-permute-start(bf16[16,64,128]{2,1,0:T(8,128)(2,1)S(1)} %get-tuple-element.62), channel_id=1, source_target_pairs={{0,2},{1,3},{2,0},{3,1},{4,6},{5,7},{6,4},{7,5},{8,10},{9,11},{10,... | collective-permute-start | bytes 786440 | tf_op jit(solution)/shard_map/ppermute | solution.py:50
  29.1 11.0 %collective-permute-start.8 = (bf16[16,64,128]{2,1,0:T(8,128)(2,1)S(1)}, bf16[16,64,128]{2,1,0:T(8,128)(2,1)S(1)}, u32[]{:S(2)}, u32[]{:S(2)}) collective-permute-start(bf16[16,64,128]{2,1,0:T(8,128)(2,1)S(1)} %fusion.6), channel_id=1, source_target_pairs={{0,12},{1,13},{2,14},{3,15},{4,0},{5,1},{6,2},{7,3},{8,4},{9,5},{1... | collective-permute-start | bytes 786440 | tf_op jit(solution)/shard_map/ppermute | solution.py:50
  33.3 13.4 %collective-permute-start.6 = (bf16[16,64,128]{2,1,0:T(8,128)(2,1)S(1)}, bf16[16,64,128]{2,1,0:T(8,128)(2,1)S(1)}, u32[]{:S(2)}, u32[]{:S(2)}) collective-permute-start(bf16[16,64,128]{2,1,0:T(8,128)(2,1)S(1)} %fusion.7), channel_id=1, source_target_pairs={{0,4},{1,5},{2,6},{3,7},{4,8},{5,9},{6,10},{7,11},{8,12},{9,13},{1... | collective-permute-start | bytes 786440 | tf_op jit(solution)/shard_map/ppermute | solution.py:50
  33.3 21.0 %collective-permute-start.4 = (bf16[16,64,128]{2,1,0:T(8,128)(2,1)S(1)}, bf16[16,64,128]{2,1,0:T(8,128)(2,1)S(1)}, u32[]{:S(2)}, u32[]{:S(2)}) collective-permute-start(bf16[16,64,128]{2,1,0:T(8,128)(2,1)S(1)} %fusion.8), channel_id=1, source_target_pairs={{0,8},{1,9},{2,10},{3,11},{4,12},{5,13},{6,14},{7,15},{8,0},{9,1},... | collective-permute-start | bytes 786440 | tf_op jit(solution)/shard_map/ppermute | solution.py:50
  72.3 9.5 %collective-permute-start.12 = (bf16[32,2,16,128]{3,2,1,0:T(8,128)(2,1)}, bf16[32,2,16,128]{3,2,1,0:T(8,128)(2,1)}, u32[]{:S(2)}, u32[]{:S(2)}) collective-permute-start(bf16[32,2,16,128]{3,2,1,0:T(8,128)(2,1)} %get-tuple-element.60), channel_id=1, source_target_pairs={{0,2},{1,3},{2,0},{3,1},{4,6},{5,7},{6,4},{7,5},{8,10},{9,11},{10,... | collective-permute-start | bytes 786440 | tf_op jit(solution)/shard_map/ppermute | solution.py:50
  74.2 13.2 %collective-permute-start.14 = (bf16[32,2,16,128]{3,2,1,0:T(8,128)(2,1)S(1)}, bf16[32,2,16,128]{3,2,1,0:T(8,128)(2,1)}, u32[]{:S(2)}, u32[]{:S(2)}) collective-permute-start(bf16[32,2,16,128]{3,2,1,0:T(8,128)(2,1)S(1)} %get-tuple-element.59), channel_id=1, source_target_pairs={{0,2},{1,3},{2,0},{3,1},{4,6},{5,7},{6,4},{7,5},{8,10},{9,11},{10,... | collective-permute-start | bytes 786440 | tf_op jit(solution)/shard_map/ppermute | solution.py:50
  75.1 17.8 %collective-permute-start.16 = (bf16[32,2,16,128]{3,2,1,0:T(8,128)(2,1)S(1)}, bf16[32,2,16,128]{3,2,1,0:T(8,128)(2,1)S(1)}, u32[]{:S(2)}, u32[]{:S(2)}) collective-permute-start(bf16[32,2,16,128]{3,2,1,0:T(8,128)(2,1)S(1)} %get-tuple-element.58), channel_id=1, source_target_pairs={{0,2},{1,3},{2,0},{3,1},{4,6},{5,7},{6,4},{7,5},{8,10},{9,11},{10,... | collective-permute-start | bytes 786440 | tf_op jit(solution)/shard_map/ppermute | solution.py:50
  76.7 21.3 %collective-permute-start.11 = (bf16[32,2,16,128]{3,2,1,0:T(8,128)(2,1)S(1)}, bf16[32,2,16,128]{3,2,1,0:T(8,128)(2,1)S(1)}, u32[]{:S(2)}, u32[]{:S(2)}) collective-permute-start(bf16[32,2,16,128]{3,2,1,0:T(8,128)(2,1)S(1)} %get-tuple-element.61), channel_id=1, source_target_pairs={{0,2},{1,3},{2,0},{3,1},{4,6},{5,7},{6,4},{7,5},{8,10},{9,11},{10,... | collective-permute-start | bytes 786440 | tf_op jit(solution)/shard_map/ppermute | solution.py:50
  82.9 25.0 %collective-permute-start.13 = (bf16[32,2,16,128]{3,2,1,0:T(8,128)(2,1)S(1)}, bf16[32,2,16,128]{3,2,1,0:T(8,128)(2,1)S(1)}, u32[]{:S(2)}, u32[]{:S(2)}) collective-permute-start(bf16[32,2,16,128]{3,2,1,0:T(8,128)(2,1)S(1)} %fusion.5), channel_id=1, source_target_pairs={{0,8},{1,9},{2,10},{3,11},{4,12},{5,13},{6,14},{7,15},{8,0},{9,1},... | collective-permute-start | bytes 786440 | tf_op jit(solution)/shard_map/ppermute | solution.py:50
  88.5 19.5 %collective-permute-start.15 = (bf16[32,2,16,128]{3,2,1,0:T(8,128)(2,1)S(1)}, bf16[32,2,16,128]{3,2,1,0:T(8,128)(2,1)S(1)}, u32[]{:S(2)}, u32[]{:S(2)}) collective-permute-start(bf16[32,2,16,128]{3,2,1,0:T(8,128)(2,1)S(1)} %fusion.4), channel_id=1, source_target_pairs={{0,4},{1,5},{2,6},{3,7},{4,8},{5,9},{6,10},{7,11},{8,12},{9,13},{1... | collective-permute-start | bytes 786440 | tf_op jit(solution)/shard_map/ppermute | solution.py:50
  93.9 14.0 %collective-permute-start.17 = (bf16[32,2,16,128]{3,2,1,0:T(8,128)(2,1)S(1)}, bf16[32,2,16,128]{3,2,1,0:T(8,128)(2,1)S(1)}, u32[]{:S(2)}, u32[]{:S(2)}) collective-permute-start(bf16[32,2,16,128]{3,2,1,0:T(8,128)(2,1)S(1)} %fusion.3), channel_id=1, source_target_pairs={{0,12},{1,13},{2,14},{3,15},{4,0},{5,1},{6,2},{7,3},{8,4},{9,5},{1... | collective-permute-start | bytes 786440 | tf_op jit(solution)/shard_map/ppermute | solution.py:50
  110.5 13.1 %collective-permute-start.21 = (bf16[32,2,16,128]{3,2,1,0:T(8,128)(2,1)S(1)}, bf16[32,2,16,128]{3,2,1,0:T(8,128)(2,1)S(1)}, u32[]{:S(2)}, u32[]{:S(2)}) collective-permute-start(bf16[32,2,16,128]{3,2,1,0:T(8,128)(2,1)S(1)} %window.3.refs_0_), channel_id=1, source_target_pairs={{0,12},{1,13},{2,14},{3,15},{4,0},{5,1},{6,2},{7,3},{8,4},{9,5},{1... | collective-permute-start | bytes 786440 | tf_op jit(solution)/shard_map/ppermute | solution.py:50
  111.7 13.5 %collective-permute-start.19 = (bf16[32,2,16,128]{3,2,1,0:T(8,128)(2,1)S(1)}, bf16[32,2,16,128]{3,2,1,0:T(8,128)(2,1)S(1)}, u32[]{:S(2)}, u32[]{:S(2)}) collective-permute-start(bf16[32,2,16,128]{3,2,1,0:T(8,128)(2,1)S(1)} %window.3.refs_0_), channel_id=1, source_target_pairs={{0,4},{1,5},{2,6},{3,7},{4,8},{5,9},{6,10},{7,11},{8,12},{9,13},{1... | collective-permute-start | bytes 786440 | tf_op jit(solution)/shard_map/ppermute | solution.py:50
  112.6 13.1 %collective-permute-start.29 = (bf16[32,2,16,128]{3,2,1,0:T(8,128)(2,1)S(1)}, bf16[32,2,16,128]{3,2,1,0:T(8,128)(2,1)S(1)}, u32[]{:S(2)}, u32[]{:S(2)}) collective-permute-start(bf16[32,2,16,128]{3,2,1,0:T(8,128)(2,1)S(1)} %window.3.refs_0_), channel_id=1, source_target_pairs={{0,1},{1,0},{2,3},{3,2},{4,5},{5,4},{6,7},{7,6},{8,9},{9,8},{10,11... | collective-permute-start | bytes 786440 | tf_op jit(solution)/shard_map/ppermute | solution.py:50
  112.6 16.3 %collective-permute-start.18 = (bf16[32,2,16,128]{3,2,1,0:T(8,128)(2,1)S(1)}, bf16[32,2,16,128]{3,2,1,0:T(8,128)(2,1)S(1)}, u32[]{:S(2)}, u32[]{:S(2)}) collective-permute-start(bf16[32,2,16,128]{3,2,1,0:T(8,128)(2,1)S(1)} %window.3.refs_0_), channel_id=1, source_target_pairs={{0,2},{1,3},{2,0},{3,1},{4,6},{5,7},{6,4},{7,5},{8,10},{9,11},{10,... | collective-permute-start | bytes 786440 | tf_op jit(solution)/shard_map/ppermute | solution.py:50
  123.6 12.1 %collective-permute-start.22 = (bf16[32,2,16,128]{3,2,1,0:T(8,128)(2,1)S(1)}, bf16[32,2,16,128]{3,2,1,0:T(8,128)(2,1)S(1)}, u32[]{:S(2)}, u32[]{:S(2)}) collective-permute-start(bf16[32,2,16,128]{3,2,1,0:T(8,128)(2,1)S(1)} %window.3.refs_0_), channel_id=1, source_target_pairs={{0,8},{1,9},{2,10},{3,11},{4,12},{5,13},{6,14},{7,15},{8,0},{9,1},... | collective-permute-start | bytes 786440 | tf_op jit(solution)/shard_map/ppermute | solution.py:50
  125.2 12.0 %collective-permute-start.30 = (bf16[32,2,16,128]{3,2,1,0:T(8,128)(2,1)S(1)}, bf16[32,2,16,128]{3,2,1,0:T(8,128)(2,1)S(1)}, u32[]{:S(2)}, u32[]{:S(2)}) collective-permute-start(bf16[32,2,16,128]{3,2,1,0:T(8,128)(2,1)S(1)} %collective-permute-done.19.refs_1_), channel_id=1, source_target_pairs={{0,1},{1,0},{2,3},{3,2},{4,5},{5,4},{6,7},{7,6},{8,9},{9,8},{10,11... | collective-permute-start | bytes 786440 | tf_op jit(solution)/shard_map/ppermute | solution.py:50
  125.2 12.0 %collective-permute-start.32 = (bf16[32,2,16,128]{3,2,1,0:T(8,128)(2,1)S(1)}, bf16[32,2,16,128]{3,2,1,0:T(8,128)(2,1)S(1)}, u32[]{:S(2)}, u32[]{:S(2)}) collective-permute-start(bf16[32,2,16,128]{3,2,1,0:T(8,128)(2,1)S(1)} %collective-permute-done.21.refs_3_), channel_id=1, source_target_pairs={{0,1},{1,0},{2,3},{3,2},{4,5},{5,4},{6,7},{7,6},{8,9},{9,8},{10,11... | collective-permute-start | bytes 786440 | tf_op jit(solution)/shard_map/ppermute | solution.py:50
  125.7 12.0 %collective-permute-start.20 = (bf16[32,2,16,128]{3,2,1,0:T(8,128)(2,1)S(1)}, bf16[32,2,16,128]{3,2,1,0:T(8,128)(2,1)S(1)}, u32[]{:S(2)}, u32[]{:S(2)}) collective-permute-start(bf16[32,2,16,128]{3,2,1,0:T(8,128)(2,1)S(1)} %collective-permute-done.19.refs_1_), channel_id=1, source_target_pairs={{0,2},{1,3},{2,0},{3,1},{4,6},{5,7},{6,4},{7,5},{8,10},{9,11},{10,... | collective-permute-start | bytes 786440 | tf_op jit(solution)/shard_map/ppermute | solution.py:50
  128.8 12.7 %collective-permute-start.24 = (bf16[32,2,16,128]{3,2,1,0:T(8,128)(2,1)S(1)}, bf16[32,2,16,128]{3,2,1,0:T(8,128)(2,1)S(1)}, u32[]{:S(2)}, u32[]{:S(2)}) collective-permute-start(bf16[32,2,16,128]{3,2,1,0:T(8,128)(2,1)S(1)} %collective-permute-done.21.refs_3_), channel_id=1, source_target_pairs={{0,2},{1,3},{2,0},{3,1},{4,6},{5,7},{6,4},{7,5},{8,10},{9,11},{10,... | collective-permute-start | bytes 786440 | tf_op jit(solution)/shard_map/ppermute | solution.py:50
  135.6 10.9 %collective-permute-start.23 = (bf16[32,2,16,128]{3,2,1,0:T(8,128)(2,1)S(1)}, bf16[32,2,16,128]{3,2,1,0:T(8,128)(2,1)S(1)}, u32[]{:S(2)}, u32[]{:S(2)}) collective-permute-start(bf16[32,2,16,128]{3,2,1,0:T(8,128)(2,1)S(1)} %collective-permute-done.22.refs_2_), channel_id=1, source_target_pairs={{0,2},{1,3},{2,0},{3,1},{4,6},{5,7},{6,4},{7,5},{8,10},{9,11},{10,... | collective-permute-start | bytes 786440 | tf_op jit(solution)/shard_map/ppermute | solution.py:50
  137.2 9.4 %collective-permute-start.31 = (bf16[32,2,16,128]{3,2,1,0:T(8,128)(2,1)S(1)}, bf16[32,2,16,128]{3,2,1,0:T(8,128)(2,1)S(1)}, u32[]{:S(2)}, u32[]{:S(2)}) collective-permute-start(bf16[32,2,16,128]{3,2,1,0:T(8,128)(2,1)S(1)} %collective-permute-done.22.refs_2_), channel_id=1, source_target_pairs={{0,1},{1,0},{2,3},{3,2},{4,5},{5,4},{6,7},{7,6},{8,9},{9,8},{10,11... | collective-permute-start | bytes 786440 | tf_op jit(solution)/shard_map/ppermute | solution.py:50
  137.2 17.0 %collective-permute-start.25 = (bf16[32,2,16,128]{3,2,1,0:T(8,128)(2,1)S(1)}, bf16[32,2,16,128]{3,2,1,0:T(8,128)(2,1)S(1)}, u32[]{:S(2)}, u32[]{:S(2)}) collective-permute-start(bf16[32,2,16,128]{3,2,1,0:T(8,128)(2,1)S(1)} %collective-permute-done.18.refs_0_), channel_id=1, source_target_pairs={{0,1},{1,0},{2,3},{3,2},{4,5},{5,4},{6,7},{7,6},{8,9},{9,8},{10,11... | collective-permute-start | bytes 786440 | tf_op jit(solution)/shard_map/ppermute | solution.py:50
  137.7 16.5 %collective-permute-start.26 = (bf16[32,2,16,128]{3,2,1,0:T(8,128)(2,1)S(1)}, bf16[32,2,16,128]{3,2,1,0:T(8,128)(2,1)S(1)}, u32[]{:S(2)}, u32[]{:S(2)}) collective-permute-start(bf16[32,2,16,128]{3,2,1,0:T(8,128)(2,1)S(1)} %collective-permute-done.20.refs_1_), channel_id=1, source_target_pairs={{0,1},{1,0},{2,3},{3,2},{4,5},{5,4},{6,7},{7,6},{8,9},{9,8},{10,11... | collective-permute-start | bytes 786440 | tf_op jit(solution)/shard_map/ppermute | solution.py:50
  141.5 12.7 %collective-permute-start.28 = (bf16[32,2,16,128]{3,2,1,0:T(8,128)(2,1)S(1)}, bf16[32,2,16,128]{3,2,1,0:T(8,128)(2,1)S(1)}, u32[]{:S(2)}, u32[]{:S(2)}) collective-permute-start(bf16[32,2,16,128]{3,2,1,0:T(8,128)(2,1)S(1)} %collective-permute-done.24.refs_3_), channel_id=1, source_target_pairs={{0,1},{1,0},{2,3},{3,2},{4,5},{5,4},{6,7},{7,6},{8,9},{9,8},{10,11... | collective-permute-start | bytes 786440 | tf_op jit(solution)/shard_map/ppermute | solution.py:50
  181.6 9.2 %collective-permute-start.36 = (bf16[32,2,16,128]{3,2,1,0:T(8,128)(2,1)S(1)}, bf16[32,2,16,128]{3,2,1,0:T(8,128)(2,1)S(1)}, u32[]{:S(2)}, u32[]{:S(2)}) collective-permute-start(bf16[32,2,16,128]{3,2,1,0:T(8,128)(2,1)S(1)} %get-tuple-element.56), channel_id=1, source_target_pairs={{0,2},{1,3},{2,0},{3,1},{4,6},{5,7},{6,4},{7,5},{8,10},{9,11},{10,... | collective-permute-start | bytes 786440 | tf_op jit(solution)/shard_map/ppermute | solution.py:50
  183.4 13.0 %collective-permute-start.38 = (bf16[32,2,16,128]{3,2,1,0:T(8,128)(2,1)S(1)}, bf16[32,2,16,128]{3,2,1,0:T(8,128)(2,1)S(1)}, u32[]{:S(2)}, u32[]{:S(2)}) collective-permute-start(bf16[32,2,16,128]{3,2,1,0:T(8,128)(2,1)S(1)} %get-tuple-element.55), channel_id=1, source_target_pairs={{0,2},{1,3},{2,0},{3,1},{4,6},{5,7},{6,4},{7,5},{8,10},{9,11},{10,... | collective-permute-start | bytes 786440 | tf_op jit(solution)/shard_map/ppermute | solution.py:50
  183.6 18.4 %collective-permute-start.40 = (bf16[32,2,16,128]{3,2,1,0:T(8,128)(2,1)S(1)}, bf16[32,2,16,128]{3,2,1,0:T(8,128)(2,1)S(1)}, u32[]{:S(2)}, u32[]{:S(2)}) collective-permute-start(bf16[32,2,16,128]{3,2,1,0:T(8,128)(2,1)S(1)} %get-tuple-element.54), channel_id=1, source_target_pairs={{0,2},{1,3},{2,0},{3,1},{4,6},{5,7},{6,4},{7,5},{8,10},{9,11},{10,... | collective-permute-start | bytes 786440 | tf_op jit(solution)/shard_map/ppermute | solution.py:50
  185.4 21.4 %collective-permute-start.35 = (bf16[32,2,16,128]{3,2,1,0:T(8,128)(2,1)S(1)}, bf16[32,2,16,128]{3,2,1,0:T(8,128)(2,1)S(1)}, u32[]{:S(2)}, u32[]{:S(2)}) collective-permute-start(bf16[32,2,16,128]{3,2,1,0:T(8,128)(2,1)S(1)} %get-tuple-element.57), channel_id=1, source_target_pairs={{0,2},{1,3},{2,0},{3,1},{4,6},{5,7},{6,4},{7,5},{8,10},{9,11},{10,... | collective-permute-start | bytes 786440 | tf_op jit(solution)/shard_map/ppermute | solution.py:50
  190.9 24.5 %collective-permute-start.37 = (bf16[32,2,16,128]{3,2,1,0:T(8,128)(2,1)S(1)}, bf16[32,2,16,128]{3,2,1,0:T(8,128)(2,1)S(1)}, u32[]{:S(2)}, u32[]{:S(2)}) collective-permute-start(bf16[32,2,16,128]{3,2,1,0:T(8,128)(2,1)S(1)} %fusion.2), channel_id=1, source_target_pairs={{0,8},{1,9},{2,10},{3,11},{4,12},{5,13},{6,14},{7,15},{8,0},{9,1},... | collective-permute-start | bytes 786440 | tf_op jit(solution)/shard_map/ppermute | solution.py:50
  196.5 18.9 %collective-permute-start.39 = (bf16[32,2,16,128]{3,2,1,0:T(8,128)(2,1)S(1)}, bf16[32,2,16,128]{3,2,1,0:T(8,128)(2,1)S(1)}, u32[]{:S(2)}, u32[]{:S(2)}) collective-permute-start(bf16[32,2,16,128]{3,2,1,0:T(8,128)(2,1)S(1)} %fusion.1), channel_id=1, source_target_pairs={{0,4},{1,5},{2,6},{3,7},{4,8},{5,9},{6,10},{7,11},{8,12},{9,13},{1... | collective-permute-start | bytes 786440 | tf_op jit(solution)/shard_map/ppermute | solution.py:50
  202.1 13.3 %collective-permute-start.41 = (bf16[32,2,16,128]{3,2,1,0:T(8,128)(2,1)S(1)}, bf16[32,2,16,128]{3,2,1,0:T(8,128)(2,1)S(1)}, u32[]{:S(2)}, u32[]{:S(2)}) collective-permute-start(bf16[32,2,16,128]{3,2,1,0:T(8,128)(2,1)S(1)} %fusion), channel_id=1, source_target_pairs={{0,12},{1,13},{2,14},{3,15},{4,0},{5,1},{6,2},{7,3},{8,4},{9,5},{1... | collective-permute-start | bytes 786440 | tf_op jit(solution)/shard_map/ppermute | solution.py:50
  215.9 8.8 %collective-permute-start.43 = (bf16[16,64,128]{2,1,0:T(8,128)(2,1)S(1)}, bf16[16,64,128]{2,1,0:T(8,128)(2,1)S(1)}, u32[]{:S(2)}, u32[]{:S(2)}) collective-permute-start(bf16[16,64,128]{2,1,0:T(8,128)(2,1)S(1)} %window.5.refs_2_.spec_ref), channel_id=1, source_target_pairs={{0,12},{1,13},{2,14},{3,15},{4,0},{5,1},{6,2},{7,3},{8,4},{9,5},{1... | collective-permute-start | bytes 786440 | tf_op jit(solution)/shard_map/ppermute | solution.py:50
  217.8 13.5 %collective-permute-start.42 = (bf16[16,64,128]{2,1,0:T(8,128)(2,1)S(1)}, bf16[16,64,128]{2,1,0:T(8,128)(2,1)S(1)}, u32[]{:S(2)}, u32[]{:S(2)}) collective-permute-start(bf16[16,64,128]{2,1,0:T(8,128)(2,1)S(1)} %window.5.refs_2_.spec_ref), channel_id=1, source_target_pairs={{0,4},{1,5},{2,6},{3,7},{4,8},{5,9},{6,10},{7,11},{8,12},{9,13},{1... | collective-permute-start | bytes 786440 | tf_op jit(solution)/shard_map/ppermute | solution.py:50
  224.7 16.8 %collective-permute-start.44 = (bf16[16,64,128]{2,1,0:T(8,128)(2,1)S(1)}, bf16[16,64,128]{2,1,0:T(8,128)(2,1)S(1)}, u32[]{:S(2)}, u32[]{:S(2)}) collective-permute-start(bf16[16,64,128]{2,1,0:T(8,128)(2,1)S(1)} %window.5.refs_2_.spec_ref), channel_id=1, source_target_pairs={{0,8},{1,9},{2,10},{3,11},{4,12},{5,13},{6,14},{7,15},{8,0},{9,1},... | collective-permute-start | bytes 786440 | tf_op jit(solution)/shard_map/ppermute | solution.py:50
  226.1 21.5 %collective-permute-start.45 = (bf16[16,64,128]{2,1,0:T(8,128)(2,1)S(1)}, bf16[16,64,128]{2,1,0:T(8,128)(2,1)S(1)}, u32[]{:S(2)}, u32[]{:S(2)}) collective-permute-start(bf16[16,64,128]{2,1,0:T(8,128)(2,1)S(1)} %window.5.refs_2_.spec_ref), channel_id=1, source_target_pairs={{0,2},{1,3},{2,0},{3,1},{4,6},{5,7},{6,4},{7,5},{8,10},{9,11},{10,... | collective-permute-start | bytes 786440 | tf_op jit(solution)/shard_map/ppermute | solution.py:50
  231.2 16.4 %collective-permute-start.46 = (bf16[16,64,128]{2,1,0:T(8,128)(2,1)S(1)}, bf16[16,64,128]{2,1,0:T(8,128)(2,1)S(1)}, u32[]{:S(2)}, u32[]{:S(2)}) collective-permute-start(bf16[16,64,128]{2,1,0:T(8,128)(2,1)S(1)} %collective-permute-done.42.refs_3_.spec_ref), channel_id=1, source_target_pairs={{0,2},{1,3},{2,0},{3,1},{4,6},{5,7},{6,4},{7,5},{8,10},{9,11},{10,... | collective-permute-start | bytes 786440 | tf_op jit(solution)/shard_map/ppermute | solution.py:50
  232.7 22.5 %collective-permute-start.48 = (bf16[16,64,128]{2,1,0:T(8,128)(2,1)S(1)}, bf16[16,64,128]{2,1,0:T(8,128)(2,1)S(1)}, u32[]{:S(2)}, u32[]{:S(2)}) collective-permute-start(bf16[16,64,128]{2,1,0:T(8,128)(2,1)S(1)} %collective-permute-done.43.refs_5_.spec_ref), channel_id=1, source_target_pairs={{0,2},{1,3},{2,0},{3,1},{4,6},{5,7},{6,4},{7,5},{8,10},{9,11},{10,... | collective-permute-start | bytes 786440 | tf_op jit(solution)/shard_map/ppermute | solution.py:50
  235.6 25.2 %collective-permute-start.61 = (bf16[32,2,16,128]{3,2,1,0:T(8,128)(2,1)S(1)}, bf16[32,2,16,128]{3,2,1,0:T(8,128)(2,1)S(1)}, u32[]{:S(2)}, u32[]{:S(2)}) collective-permute-start(bf16[32,2,16,128]{3,2,1,0:T(8,128)(2,1)S(1)} %window_at.12.refs_0_), channel_id=1, source_target_pairs={{0,1},{1,0},{2,3},{3,2},{4,5},{5,4},{6,7},{7,6},{8,9},{9,8},{10,11... | collective-permute-start | bytes 786440 | tf_op jit(solution)/shard_map/ppermute | solution.py:50
  241.4 16.3 %collective-permute-start.47 = (bf16[16,64,128]{2,1,0:T(8,128)(2,1)S(1)}, bf16[16,64,128]{2,1,0:T(8,128)(2,1)S(1)}, u32[]{:S(2)}, u32[]{:S(2)}) collective-permute-start(bf16[16,64,128]{2,1,0:T(8,128)(2,1)S(1)} %collective-permute-done.44.refs_4_.spec_ref), channel_id=1, source_target_pairs={{0,2},{1,3},{2,0},{3,1},{4,6},{5,7},{6,4},{7,5},{8,10},{9,11},{10,... | collective-permute-start | bytes 786440 | tf_op jit(solution)/shard_map/ppermute | solution.py:50
  247.6 13.3 %collective-permute-start.62 = (bf16[32,2,16,128]{3,2,1,0:T(8,128)(2,1)S(1)}, bf16[32,2,16,128]{3,2,1,0:T(8,128)(2,1)S(1)}, u32[]{:S(2)}, u32[]{:S(2)}) collective-permute-start(bf16[32,2,16,128]{3,2,1,0:T(8,128)(2,1)S(1)} %window_at.13.refs_1_), channel_id=1, source_target_pairs={{0,1},{1,0},{2,3},{3,2},{4,5},{5,4},{6,7},{7,6},{8,9},{9,8},{10,11... | collective-permute-start | bytes 786440 | tf_op jit(solution)/shard_map/ppermute | solution.py:50
  247.7 13.7 %collective-permute-start.64 = (bf16[32,2,16,128]{3,2,1,0:T(8,128)(2,1)S(1)}, bf16[32,2,16,128]{3,2,1,0:T(8,128)(2,1)S(1)}, u32[]{:S(2)}, u32[]{:S(2)}) collective-permute-start(bf16[32,2,16,128]{3,2,1,0:T(8,128)(2,1)S(1)} %window_at.15.refs_3_), channel_id=1, source_target_pairs={{0,1},{1,0},{2,3},{3,2},{4,5},{5,4},{6,7},{7,6},{8,9},{9,8},{10,11... | collective-permute-start | bytes 786440 | tf_op jit(solution)/shard_map/ppermute | solution.py:50
  257.7 11.8 %collective-permute-start.57 = (bf16[32,2,16,128]{3,2,1,0:T(8,128)(2,1)S(1)}, bf16[32,2,16,128]{3,2,1,0:T(8,128)(2,1)S(1)}, u32[]{:S(2)}, u32[]{:S(2)}) collective-permute-start(bf16[32,2,16,128]{3,2,1,0:T(8,128)(2,1)S(1)} %window_at.8.refs_0_), channel_id=1, source_target_pairs={{0,1},{1,0},{2,3},{3,2},{4,5},{5,4},{6,7},{7,6},{8,9},{9,8},{10,11... | collective-permute-start | bytes 786440 | tf_op jit(solution)/shard_map/ppermute | solution.py:50
  260.8 8.9 %collective-permute-start.58 = (bf16[32,2,16,128]{3,2,1,0:T(8,128)(2,1)S(1)}, bf16[32,2,16,128]{3,2,1,0:T(8,128)(2,1)S(1)}, u32[]{:S(2)}, u32[]{:S(2)}) collective-permute-start(bf16[32,2,16,128]{3,2,1,0:T(8,128)(2,1)S(1)} %window_at.9.refs_1_), channel_id=1, source_target_pairs={{0,1},{1,0},{2,3},{3,2},{4,5},{5,4},{6,7},{7,6},{8,9},{9,8},{10,11... | collective-permute-start | bytes 786440 | tf_op jit(solution)/shard_map/ppermute | solution.py:50
  260.9 8.8 %collective-permute-start.60 = (bf16[32,2,16,128]{3,2,1,0:T(8,128)(2,1)S(1)}, bf16[32,2,16,128]{3,2,1,0:T(8,128)(2,1)S(1)}, u32[]{:S(2)}, u32[]{:S(2)}) collective-permute-start(bf16[32,2,16,128]{3,2,1,0:T(8,128)(2,1)S(1)} %window_at.11.refs_3_), channel_id=1, source_target_pairs={{0,1},{1,0},{2,3},{3,2},{4,5},{5,4},{6,7},{7,6},{8,9},{9,8},{10,11... | collective-permute-start | bytes 786440 | tf_op jit(solution)/shard_map/ppermute | solution.py:50
  261.4 18.9 %collective-permute-start.49 = (bf16[16,64,128]{2,1,0:T(8,128)(2,1)S(1)}, bf16[16,64,128]{2,1,0:T(8,128)(2,1)S(1)}, u32[]{:S(2)}, u32[]{:S(2)}) collective-permute-start(bf16[16,64,128]{2,1,0:T(8,128)(2,1)S(1)} %window.5.refs_2_.spec_ref), channel_id=1, source_target_pairs={{0,1},{1,0},{2,3},{3,2},{4,5},{5,4},{6,7},{7,6},{8,9},{9,8},{10,11... | collective-permute-start | bytes 786440 | tf_op jit(solution)/shard_map/ppermute | solution.py:50
  269.5 11.6 %collective-permute-start.50 = (bf16[16,64,128]{2,1,0:T(8,128)(2,1)S(1)}, bf16[16,64,128]{2,1,0:T(8,128)(2,1)S(1)}, u32[]{:S(2)}, u32[]{:S(2)}) collective-permute-start(bf16[16,64,128]{2,1,0:T(8,128)(2,1)S(1)} %collective-permute-done.42.refs_3_.spec_ref), channel_id=1, source_target_pairs={{0,1},{1,0},{2,3},{3,2},{4,5},{5,4},{6,7},{7,6},{8,9},{9,8},{10,11... | collective-permute-start | bytes 786440 | tf_op jit(solution)/shard_map/ppermute | solution.py:50
  277.5 8.7 %collective-permute-start.66 = (bf16[16,64,128]{2,1,0:T(8,128)(2,1)S(1)}, bf16[16,64,128]{2,1,0:T(8,128)(2,1)S(1)}, u32[]{:S(2)}, u32[]{:S(2)}) collective-permute-start(bf16[16,64,128]{2,1,0:T(8,128)(2,1)S(1)} %correlate1.3.refs_2_), channel_id=1, source_target_pairs={{0,12},{1,13},{2,14},{3,15},{4,0},{5,1},{6,2},{7,3},{8,4},{9,5},{1... | collective-permute-start | bytes 786440 | tf_op jit(solution)/shard_map/ppermute | solution.py:50
  286.3 11.2 %collective-permute-start.65 = (bf16[16,64,128]{2,1,0:T(8,128)(2,1)S(1)}, bf16[16,64,128]{2,1,0:T(8,128)(2,1)S(1)}, u32[]{:S(2)}, u32[]{:S(2)}) collective-permute-start(bf16[16,64,128]{2,1,0:T(8,128)(2,1)S(1)} %correlate1.3.refs_2_), channel_id=1, source_target_pairs={{0,4},{1,5},{2,6},{3,7},{4,8},{5,9},{6,10},{7,11},{8,12},{9,13},{1... | collective-permute-start | bytes 786440 | tf_op jit(solution)/shard_map/ppermute | solution.py:50
  287.2 10.7 %collective-permute-start.55 = (bf16[16,64,128]{2,1,0:T(8,128)(2,1)S(1)}, bf16[16,64,128]{2,1,0:T(8,128)(2,1)S(1)}, u32[]{:S(2)}, u32[]{:S(2)}) collective-permute-start(bf16[16,64,128]{2,1,0:T(8,128)(2,1)S(1)} %collective-permute-done.47.refs_8_.spec_ref), channel_id=1, source_target_pairs={{0,1},{1,0},{2,3},{3,2},{4,5},{5,4},{6,7},{7,6},{8,9},{9,8},{10,11... | collective-permute-start | bytes 786440 | tf_op jit(solution)/shard_map/ppermute | solution.py:50
  288.2 12.0 %collective-permute-start.68 = (bf16[16,64,128]{2,1,0:T(8,128)(2,1)S(1)}, bf16[16,64,128]{2,1,0:T(8,128)(2,1)}, u32[]{:S(2)}, u32[]{:S(2)}) collective-permute-start(bf16[16,64,128]{2,1,0:T(8,128)(2,1)S(1)} %correlate1.3.refs_2_), channel_id=1, source_target_pairs={{0,2},{1,3},{2,0},{3,1},{4,6},{5,7},{6,4},{7,5},{8,10},{9,11},{10,... | collective-permute-start | bytes 786440 | tf_op jit(solution)/shard_map/ppermute | solution.py:50
  289.4 11.5 %collective-permute-start.72 = (bf16[16,64,128]{2,1,0:T(8,128)(2,1)S(1)}, bf16[16,64,128]{2,1,0:T(8,128)(2,1)S(1)}, u32[]{:S(2)}, u32[]{:S(2)}) collective-permute-start(bf16[16,64,128]{2,1,0:T(8,128)(2,1)S(1)} %correlate1.3.refs_2_), channel_id=1, source_target_pairs={{0,1},{1,0},{2,3},{3,2},{4,5},{5,4},{6,7},{7,6},{8,9},{9,8},{10,11... | collective-permute-start | bytes 786440 | tf_op jit(solution)/shard_map/ppermute | solution.py:50
  290.2 18.4 %collective-permute-start.67 = (bf16[16,64,128]{2,1,0:T(8,128)(2,1)S(1)}, bf16[16,64,128]{2,1,0:T(8,128)(2,1)}, u32[]{:S(2)}, u32[]{:S(2)}) collective-permute-start(bf16[16,64,128]{2,1,0:T(8,128)(2,1)S(1)} %correlate1.3.refs_2_), channel_id=1, source_target_pairs={{0,8},{1,9},{2,10},{3,11},{4,12},{5,13},{6,14},{7,15},{8,0},{9,1},... | collective-permute-start | bytes 786440 | tf_op jit(solution)/shard_map/ppermute | solution.py:50
  297.5 11.3 %collective-permute-start.69 = (bf16[16,64,128]{2,1,0:T(8,128)(2,1)S(1)}, bf16[16,64,128]{2,1,0:T(8,128)(2,1)}, u32[]{:S(2)}, u32[]{:S(2)}) collective-permute-start(bf16[16,64,128]{2,1,0:T(8,128)(2,1)S(1)} %collective-permute-done.65.refs_3_), channel_id=1, source_target_pairs={{0,2},{1,3},{2,0},{3,1},{4,6},{5,7},{6,4},{7,5},{8,10},{9,11},{10,... | collective-permute-start | bytes 786440 | tf_op jit(solution)/shard_map/ppermute | solution.py:50
  298.5 12.6 %collective-permute-start.71 = (bf16[16,64,128]{2,1,0:T(8,128)(2,1)S(1)}, bf16[16,64,128]{2,1,0:T(8,128)(2,1)}, u32[]{:S(2)}, u32[]{:S(2)}) collective-permute-start(bf16[16,64,128]{2,1,0:T(8,128)(2,1)S(1)} %collective-permute-done.66.refs_5_), channel_id=1, source_target_pairs={{0,2},{1,3},{2,0},{3,1},{4,6},{5,7},{6,4},{7,5},{8,10},{9,11},{10,... | collective-permute-start | bytes 786440 | tf_op jit(solution)/shard_map/ppermute | solution.py:50
  300.2 10.9 %collective-permute-start.73 = (bf16[16,64,128]{2,1,0:T(8,128)(2,1)S(1)}, bf16[16,64,128]{2,1,0:T(8,128)(2,1)S(1)}, u32[]{:S(2)}, u32[]{:S(2)}) collective-permute-start(bf16[16,64,128]{2,1,0:T(8,128)(2,1)S(1)} %collective-permute-done.65.refs_3_), channel_id=1, source_target_pairs={{0,1},{1,0},{2,3},{3,2},{4,5},{5,4},{6,7},{7,6},{8,9},{9,8},{10,11... | collective-permute-start | bytes 786440 | tf_op jit(solution)/shard_map/ppermute | solution.py:50
  301.7 10.6 %collective-permute-start.75 = (bf16[16,64,128]{2,1,0:T(8,128)(2,1)S(1)}, bf16[16,64,128]{2,1,0:T(8,128)(2,1)S(1)}, u32[]{:S(2)}, u32[]{:S(2)}) collective-permute-start(bf16[16,64,128]{2,1,0:T(8,128)(2,1)S(1)} %collective-permute-done.66.refs_5_), channel_id=1, source_target_pairs={{0,1},{1,0},{2,3},{3,2},{4,5},{5,4},{6,7},{7,6},{8,9},{9,8},{10,11... | collective-permute-start | bytes 786440 | tf_op jit(solution)/shard_map/ppermute | solution.py:50
  308.8 16.7 %collective-permute-start.76 = (bf16[16,64,128]{2,1,0:T(8,128)(2,1)}, bf16[16,64,128]{2,1,0:T(8,128)(2,1)}, u32[]{:S(2)}, u32[]{:S(2)}) collective-permute-start(bf16[16,64,128]{2,1,0:T(8,128)(2,1)} %collective-permute-done.68.refs_6_), channel_id=1, source_target_pairs={{0,1},{1,0},{2,3},{3,2},{4,5},{5,4},{6,7},{7,6},{8,9},{9,8},{10,11... | collective-permute-start | bytes 786440 | tf_op jit(solution)/shard_map/ppermute | solution.py:50
  311.1 14.5 %collective-permute-start.74 = (bf16[16,64,128]{2,1,0:T(8,128)(2,1)}, bf16[16,64,128]{2,1,0:T(8,128)(2,1)}, u32[]{:S(2)}, u32[]{:S(2)}) collective-permute-start(bf16[16,64,128]{2,1,0:T(8,128)(2,1)} %collective-permute-done.67.refs_4_), channel_id=1, source_target_pairs={{0,1},{1,0},{2,3},{3,2},{4,5},{5,4},{6,7},{7,6},{8,9},{9,8},{10,11... | collective-permute-start | bytes 786440 | tf_op jit(solution)/shard_map/ppermute | solution.py:50
  311.8 13.8 %collective-permute-start.77 = (bf16[16,64,128]{2,1,0:T(8,128)(2,1)}, bf16[16,64,128]{2,1,0:T(8,128)(2,1)}, u32[]{:S(2)}, u32[]{:S(2)}) collective-permute-start(bf16[16,64,128]{2,1,0:T(8,128)(2,1)} %collective-permute-done.69.refs_7_), channel_id=1, source_target_pairs={{0,1},{1,0},{2,3},{3,2},{4,5},{5,4},{6,7},{7,6},{8,9},{9,8},{10,11... | collective-permute-start | bytes 786440 | tf_op jit(solution)/shard_map/ppermute | solution.py:50
  313.0 12.6 %collective-permute-start.79 = (bf16[16,64,128]{2,1,0:T(8,128)(2,1)}, bf16[16,64,128]{2,1,0:T(8,128)(2,1)}, u32[]{:S(2)}, u32[]{:S(2)}) collective-permute-start(bf16[16,64,128]{2,1,0:T(8,128)(2,1)} %collective-permute-done.71.refs_9_), channel_id=1, source_target_pairs={{0,1},{1,0},{2,3},{3,2},{4,5},{5,4},{6,7},{7,6},{8,9},{9,8},{10,11... | collective-permute-start | bytes 786440 | tf_op jit(solution)/shard_map/ppermute | solution.py:50
  (39 other events, 148.5 us)

commit v5 on v4

--- a/solution.py
+++ b/solution.py
@@ -77,33 +77,58 @@
     return jnp.concatenate([jnp.where(first, own, other), jnp.where(first, other, own)], axis=1)
 
 
-def analysis_kernel(line, rows, forward_ref, plus_ref, keep0, keep1, send0, send1):
+VMEM = pl.BlockSpec(memory_space=pltpu.VMEM)
+ANY = pl.BlockSpec(memory_space=pl.ANY)
+CHUNKS = 8
+STRIPS = 4
+
+
+def limit(mebibytes):
+    return pltpu.CompilerParams(vmem_limit_bytes=mebibytes << 20)
+
+
+def strip_copies(source, target, sems, strips):
+    rows = source.shape[0] // strips
+
+    def copy(strip):
+        part = pl.ds(strip * rows, rows)
+        return pltpu.make_async_copy(source.at[part], target.at[part], sems.at[strip])
+
+    return copy, rows
+
+
+def analysis_kernel(line, forward_ref, plus_ref, keep0, keep1, send0, send1, held, sems):
     core = own_place(line)[3]
     keep, send = (keep0, keep1), (send0, send1)
-    for p in range(rows):
-        for flip, step in relative(line):
-            columns = pl.ds(chip_columns(line, True, flip, step), 2 * LANES)
-            block = jnp.dot(forward_ref[...], plus_ref[p, :, columns], preferred_element_type=F32)
-            mine, theirs = split_cores(core, block.astype(BF16))
-            keep[flip][step, p] = mine
-            send[flip][step, p] = theirs
+    copy, rows = strip_copies(plus_ref, held, sems, STRIPS)
+    for strip in range(STRIPS):
+        copy(strip).start()
+
+    def body(strip, carry):
+        copy(strip).wait()
+        for row in range(rows):
+            p = strip * rows + row
+            for flip, step in relative(line):
+                columns = pl.ds(chip_columns(line, True, flip, step), 2 * LANES)
+                block = jnp.dot(forward_ref[...], held[p, :, columns], preferred_element_type=F32)
+                mine, theirs = split_cores(core, block.astype(BF16))
+                keep[flip][step, p] = mine
+                send[flip][step, p] = theirs
+        return carry
+
+    lax.fori_loop(0, STRIPS, body, 0)
 
 
 def first_analysis(plus_start, forward, line):
     focal, samples, width = plus_start.shape
-    rows = 4
     out = jax.ShapeDtypeStruct((line, focal, 2 * NFW, LANES), BF16)
-    out_spec = pl.BlockSpec((line, rows, 2 * NFW, LANES), lambda i: (0, i, 0, 0))
     return pl.pallas_call(
-        functools.partial(analysis_kernel, line, rows),
-        grid=(focal // rows,),
-        in_specs=[
-            pl.BlockSpec((2 * NFW, samples), lambda i: (0, 0)),
-            pl.BlockSpec((rows, samples, width), lambda i: (i, 0, 0)),
-        ],
-        out_specs=[out_spec] * 4,
+        functools.partial(analysis_kernel, line),
+        in_specs=[VMEM, ANY],
+        out_specs=[VMEM] * 4,
         out_shape=[out] * 4,
-        compiler_params=pltpu.CompilerParams(vmem_limit_bytes=16 << 20),
+        scratch_shapes=[pltpu.VMEM(plus_start.shape, BF16), pltpu.SemaphoreType.DMA((STRIPS,))],
+        compiler_params=limit(8),
         cost_estimate=pl.CostEstimate(
             flops=4 * NFW * focal * samples * width,
             bytes_accessed=2 * focal * samples * width + 4 * NFW * focal * width,
@@ -132,9 +157,6 @@
     return wait
 
 
-CHUNKS = 8
-
-
 def panel_scratch(line):
     rows = NFW // CHUNKS
     return [
@@ -143,34 +165,37 @@
     ]
 
 
-def convolve_kernel(line, flip, spec_ref, panel_ref, keep, send, held, sems):
+def convolve_kernel(line, spec_ref, panel_ref, keep0, keep1, send0, send1, held, sems):
     core = own_place(line)[3]
+    keep, send = (keep0, keep1), (send0, send1)
     focal = spec_ref.shape[2]
-    rows = held.shape[3]
-    wait = fetch_panels(line, True, flip, panel_ref, held, sems)
+    rows = NFW // CHUNKS
+
+    def copy(chunk):
+        part = pl.ds(chunk * rows, rows)
+        return pltpu.make_async_copy(panel_ref.at[:, part], held.at[:, part], sems.at[chunk])
+
+    for chunk in range(CHUNKS):
+        copy(chunk).start()
 
     def body(chunk, carry):
-        wait(chunk)
+        copy(chunk).wait()
         for row in range(rows):
             w = chunk * rows + row
             real, imag = spec_ref[w, 0], spec_ref[w, 1]
             left = jnp.concatenate(
                 [jnp.concatenate([real, -imag], axis=1), jnp.concatenate([imag, real], axis=1)], axis=0
             )
-            for step in range(line):
-                panel = held[chunk, step, :, row].reshape(2 * LANES, 2 * LANES)
+            for flip, step in relative(line):
+                columns = pl.ds(chip_columns(line, True, flip, step), 2 * LANES)
+                panel = held[:, w, :, columns].reshape(2 * LANES, 2 * LANES)
                 block = jnp.dot(left, panel, preferred_element_type=F32)
                 mine, theirs = split_cores(core, block.astype(BF16))
-                keep[step, w] = mine.reshape(2, focal, LANES)
-                send[step, w] = theirs.reshape(2, focal, LANES)
+                keep[flip][step, w] = mine.reshape(2, focal, LANES)
+                send[flip][step, w] = theirs.reshape(2, focal, LANES)
         return carry
 
     lax.fori_loop(0, CHUNKS, body, 0)
-
-
-VMEM = pl.BlockSpec(memory_space=pltpu.VMEM)
-ANY = pl.BlockSpec(memory_space=pl.ANY)
-MEDIUM = pltpu.CompilerParams(vmem_limit_bytes=24 << 20)
 
 
 def panel_cost(focal, sources):
@@ -181,18 +206,18 @@
     )
 
 
-def convolve(spectrum, reflection, line, flip):
+def convolve(spectrum, reflection, line):
     focal = spectrum.shape[2]
     out = jax.ShapeDtypeStruct((line, NFW, 2, focal, LANES), BF16)
     return pl.pallas_call(
-        functools.partial(convolve_kernel, line, flip),
+        functools.partial(convolve_kernel, line),
         in_specs=[VMEM, ANY],
-        out_specs=[VMEM] * 2,
-        out_shape=[out] * 2,
-        scratch_shapes=panel_scratch(line),
-        compiler_params=MEDIUM,
-        cost_estimate=panel_cost(focal, reflection.shape[3] // 2),
-        name=f"convolve{flip}",
+        out_specs=[VMEM] * 4,
+        out_shape=[out] * 4,
+        scratch_shapes=[pltpu.VMEM(reflection.shape, BF16), pltpu.SemaphoreType.DMA((CHUNKS,))],
+        compiler_params=limit(36),
+        cost_estimate=panel_cost(focal, reflection.shape[3]),
+        name="convolve",
     )(spectrum, reflection)
 
 
@@ -248,7 +273,7 @@
         out_specs=VMEM,
         out_shape=shape,
         scratch_shapes=panel_scratch(line) + spare,
-        compiler_params=MEDIUM,
+        compiler_params=limit(24),
         cost_estimate=panel_cost(focal, reflection.shape[3] // 2),
         name=f"correlate{flip}",
     )(*own, *other, reflection, *more)
@@ -306,7 +331,7 @@
         out_specs=VMEM,
         out_shape=out,
         scratch_shapes=[pltpu.VMEM((k * focal, LANES), F32)] * 2,
-        compiler_params=pltpu.CompilerParams(vmem_limit_bytes=16 << 20),
+        compiler_params=limit(8),
         cost_estimate=pl.CostEstimate(
             flops=4 * k * NT * focal * LANES, bytes_accessed=2 * k * focal * LANES * 6, transcendentals=0
         ),
@@ -336,7 +361,7 @@
         out_specs=VMEM,
         out_shape=jax.ShapeDtypeStruct((NFW, 2, focal, LANES), BF16),
         scratch_shapes=[pltpu.VMEM((k * focal, LANES), F32)],
-        compiler_params=pltpu.CompilerParams(vmem_limit_bytes=16 << 20),
+        compiler_params=limit(8),
         cost_estimate=pl.CostEstimate(
             flops=4 * k * NT * focal * LANES, bytes_accessed=2 * k * focal * LANES * 6, transcendentals=0
         ),
@@ -344,51 +369,60 @@
     )(forward, inverse, onset_times, spec)
 
 
-def field_kernel(line, rows, has_plus, *refs):
+def field_kernel(line, has_plus, inverse_ref, onset_ref, *refs):
     core = own_place(line)[3]
     places = relative(line)
-    inverse_ref, onset_ref = refs[:2]
-    own, other = refs[2 : 2 + len(places)], refs[2 + len(places) : 2 + 2 * len(places)]
-    rest = refs[2 + 2 * len(places) :]
-    out_ref = rest[-1]
+    own, other = refs[: len(places)], refs[len(places) : 2 * len(places)]
+    rest = list(refs[2 * len(places) :])
+    plus_ref = rest.pop(0) if has_plus else None
+    out_ref, made, out_sems, *spare = rest
     samples = out_ref.shape[1]
-    first = pl.program_id(0) * rows
+    out_copy, rows = strip_copies(made, out_ref, out_sems, STRIPS)
+    if has_plus:
+        plus, plus_sems = spare
+        plus_copy, _ = strip_copies(plus_ref, plus, plus_sems, STRIPS)
+        for strip in range(STRIPS):
+            plus_copy(strip).start()
     time = lax.axis_index("blk") * samples + lax.broadcasted_iota(jnp.int32, (samples, 2 * LANES), 0)
-    for p in range(rows):
-        for at, (flip, step) in enumerate(places):
-            columns = pl.ds(chip_columns(line, False, flip, step), 2 * LANES)
-            spec = join_cores(core, own[at][p], other[at][p])
-            field = jnp.dot(inverse_ref[...], spec, preferred_element_type=F32)
-            value = jnp.where(time < onset_ref[pl.ds(first + p, 1), columns], field, 0.0)
-            if has_plus:
-                value += rest[0][p, :, columns].astype(F32)
-            out_ref[p, :, columns] = value.astype(BF16)
+
+    def body(strip, carry):
+        if has_plus:
+            plus_copy(strip).wait()
+        for row in range(rows):
+            p = strip * rows + row
+            for at, (flip, step) in enumerate(places):
+                columns = pl.ds(chip_columns(line, False, flip, step), 2 * LANES)
+                spec = join_cores(core, own[at][p], other[at][p])
+                values = jnp.dot(inverse_ref[...], spec, preferred_element_type=F32)
+                values = jnp.where(time < onset_ref[pl.ds(p, 1), columns], values, 0.0)
+                if has_plus:
+                    values += plus[p, :, columns].astype(F32)
+                made[p, :, columns] = values.astype(BF16)
+        out_copy(strip).start()
+        return carry
+
+    lax.fori_loop(0, STRIPS, body, 0)
+    for strip in range(STRIPS):
+        out_copy(strip).wait()
 
 
 def field(own, other, inverse, onset_times, line, plus_start=None):
-    focal, k, _ = own[0][0].shape
+    own, other = sum(own, []), sum(other, [])
+    focal, k, _ = own[0].shape
     samples = inverse.shape[0]
-    width = onset_times.shape[1]
-    rows = 4
-    spec_block = pl.BlockSpec((rows, k, LANES), lambda i: (i, 0, 0))
-    wide = pl.BlockSpec((rows, samples, width), lambda i: (i, 0, 0))
-    own, other = sum(own, []), sum(other, [])
+    shape = (focal, samples, onset_times.shape[1])
     plus = [] if plus_start is None else [plus_start]
+    moved = [pltpu.VMEM(shape, BF16), pltpu.SemaphoreType.DMA((STRIPS,))]
     return pl.pallas_call(
-        functools.partial(field_kernel, line, rows, bool(plus)),
-        grid=(focal // rows,),
-        in_specs=[
-            pl.BlockSpec(inverse.shape, lambda i: (0, 0)),
-            pl.BlockSpec(onset_times.shape, lambda i: (0, 0)),
-        ]
-        + [spec_block] * (len(own) + len(other))
-        + [wide] * len(plus),
-        out_specs=wide,
-        out_shape=jax.ShapeDtypeStruct((focal, samples, width), BF16),
-        compiler_params=pltpu.CompilerParams(vmem_limit_bytes=40 << 20),
+        functools.partial(field_kernel, line, bool(plus)),
+        in_specs=[VMEM] * (2 + len(own) + len(other)) + [ANY] * len(plus),
+        out_specs=ANY,
+        out_shape=jax.ShapeDtypeStruct(shape, BF16),
+        scratch_shapes=moved * (1 + len(plus)),
+        compiler_params=limit(12),
         cost_estimate=pl.CostEstimate(
-            flops=2 * k * focal * samples * width,
-            bytes_accessed=2 * focal * width * (k + 2 * samples),
+            flops=2 * k * math.prod(shape),
+            bytes_accessed=4 * math.prod(shape) + 2 * k * focal * shape[2],
             transcendentals=0,
         ),
         name="field",
@@ -403,46 +437,68 @@
 
 
 def after(value, *others):
-    return lax.optimization_barrier((value, *others))[0]
-
-
-def far_first(line):
-    return sorted(range(line), key=lambda step: -min(step, line - step))
-
-
-def across_pair(places, keep, send):
-    got = places.send(send, places.core())
-    across = {}
-    for step in far_first(places.line):
-        across[step] = places.send(add(keep[step], got[step]).astype(BF16), places.pair())
-    return got, across
-
-
-def along_line(places, keep, send, across):
-    got = places.send(send, places.core())
-    parts = [keep[0], got[0], across[0]]
-    ready = got
-    for step in far_first(places.line)[:-1]:
-        ready = add(keep[step], after(got, ready)[step], across[step]).astype(BF16)
+    return lax.optimization_barrier((value, *others))[0] if others else value
+
+
+def reduce_scatter(places, keep0, keep1, send0, send1):
+    got1 = places.send(send1, places.core())
+    got0 = places.send(send0, places.core())
+    far = [add(keep, got).astype(BF16) for keep, got in zip(keep1, got1)]
+    beside = {}
+    if places.line > 1:
+        beside[1] = places.send(far[1], places.shift(1))
+    across = {step: places.send(far[step], places.pair()) for step in range(2, places.line)}
+    across[0] = places.send(add(keep1[0], got1[0], *beside.values()).astype(BF16), places.pair())
+    parts = [keep0[0], got0[0], across[0]]
+    first = []
+    for step in range(1, places.line):
+        terms = [keep0[step], got0[step]] + ([across[step]] if step in across else [])
+        ready = add(*terms).astype(BF16)
+        if step > 2:
+            ready = after(ready, *first)
         parts.append(places.send(ready, places.shift(step)))
+        if step == 1:
+            first = [parts[-1]]
     return parts
 
 
-def gather_chips(places, block):
-    near_first = far_first(places.line)[::-1]
-    line, across = {0: block}, {}
-    ready = block
-    for step in near_first[1:]:
-        away = min(step, places.line - step)
-        ready = block if away == 1 else after(block, line[near_first[1]])
-        line[step] = places.send(ready, places.shift(step))
-    for step in near_first:
-        across[step] = places.send(line[step], places.pair())
-    return [[side[step] for step in range(places.line)] for side in (line, across)]
-
-
-def other_cores(places, sides):
-    return [[places.send(piece, places.core()) for piece in side] for side in sides]
+def gather_chips(places, block, work=None):
+    size = places.line
+    near = [1, size - 1] if size > 2 else [1] if size > 1 else []
+    far = list(range(2, size - 1))
+    made = {}
+
+    def run(flip, steps, pieces, *others):
+        if work is None:
+            return []
+        for step in steps:
+            made[flip, step] = work(after(pieces[step], *others), flip, step)
+        return [made[flip, step] for step in steps]
+
+    line = {0: block}
+    for step in near:
+        line[step] = places.send(block, places.shift(step))
+    across = {0: places.send(block, places.pair())}
+    own = run(0, [0], line)
+    for step in far:
+        line[step] = places.send(after(block, line[1], *own), places.shift(step))
+    for step in near:
+        if step == 1:
+            across[step] = places.send(across[0], places.shift(1))
+        else:
+            across[step] = places.send(line[step], places.pair())
+    middle = run(1, [0], across) + run(0, near, line)
+    for step in far:
+        across[step] = places.send(after(line[step], *middle), places.pair())
+    late = run(0, far, line) + run(1, near, across)
+    run(1, far, across, *late)
+    pieces = [[side[step] for step in range(size)] for side in (line, across)]
+    results = [[made[flip, step] for step in range(size)] for flip in range(2)] if work else None
+    return pieces, results
+
+
+def swap_cores(places, pieces):
+    return [places.send(piece, places.core()) for piece in pieces]
 
 
 def local(plus_start, reflection, onset_times):
@@ -454,39 +510,35 @@
     own_samples = lax.axis_index("blk") * samples + jnp.arange(samples, dtype=jnp.int32)
     own_forward, own_inverse = tables_of(own_samples)
 
-    keep0, keep1, send0, send1 = first_analysis(plus_start, own_forward, line)
-    _, across = across_pair(places, keep1, send1)
-    start = add(*along_line(places, keep0, send0, across)).astype(BF16)
+    def window_piece(piece, flip, step):
+        return window_at(piece, forward, inverse, onset_times, line, flip, step)
+
+    parts = reduce_scatter(places, *first_analysis(plus_start, own_forward, line))
+    start = add(*parts).astype(BF16)
     start = jnp.transpose(start, (1, 0, 2)).reshape(NFW, 2, focal, LANES)
     spectrum_plus = start
     for iteration in range(ITERS):
         last = iteration + 1 == ITERS
-        keep1, send1 = convolve(spectrum_plus, reflection, line, 1)
-        got1, across = across_pair(places, keep1, send1)
-        keep0, send0 = convolve(after(spectrum_plus, got1), reflection, line, 0)
-        parts = along_line(places, keep0, send0, across)
+        parts = reduce_scatter(places, *convolve(spectrum_plus, reflection, line))
+        windowed = window(parts, forward, inverse, onset_times, want_spec=last)
         if last:
-            upgoing_spec = gather_chips(
-                places, window(parts, forward, inverse, onset_times, want_spec=True)
-            )
-            own = [
-                [
-                    window_at(piece, forward, inverse, onset_times, line, flip, step)
-                    for step, piece in enumerate(side)
-                ]
-                for flip, side in enumerate(upgoing_spec)
-            ]
+            upgoing_spec, own = gather_chips(places, windowed, window_piece)
         else:
-            own = gather_chips(places, window(parts, forward, inverse, onset_times))
-        other = other_cores(places, own)
-        downgoing_spec = correlate(own[0], other[0], reflection, line, 0)
-        downgoing_spec = correlate(own[1], other[1], reflection, line, 1, downgoing_spec, last)
+            own, _ = gather_chips(places, windowed)
+        half = correlate(own[0], swap_cores(places, own[0]), reflection, line, 0)
+        across = [own[1][step] if step in (0, line - 1) else after(own[1][step], half) for step in range(line)]
+        downgoing_spec = correlate(own[1], swap_cores(places, across), reflection, line, 1, half, last)
         if not last:
             spectrum_plus = window([downgoing_spec], forward, inverse, onset_times, base=start)
-    other = other_cores(places, upgoing_spec)
+    other = [swap_cores(places, side) for side in upgoing_spec]
     upgoing = field(upgoing_spec, other, own_inverse, onset_times, line)
-    own = gather_chips(places, downgoing_spec)
-    downgoing = field(own, other_cores(places, own), own_inverse, onset_times, line, plus_start)
+
+    def before_far(piece, flip, step):
+        return upgoing if (flip, step) == (0, 0) else piece
+
+    own, _ = gather_chips(places, downgoing_spec, before_far)
+    other = [swap_cores(places, side) for side in own]
+    downgoing = field(own, other, own_inverse, onset_times, line, plus_start)
     return upgoing, downgoing
 
 

time: 331 us -> 306 us (0.924)
  local copies, waits for them, and re-layouts: 16 us -> 7.74 us
  waiting for transfers between devices: 153 us -> 145 us
  Pallas kernels: 91.4 us -> 86.1 us
    ppermute x80, waiting for transfers between devices: 153 us -> 145 us  [send(): return lax.ppermute(array, self.axis, pairs)]
    unnamed x46 -> x20, local copies, waits for them, and re-layouts: 14.4 us -> 6.12 us
    pallas_call x7 -> x5, Pallas kernels: 36.4 us -> 31.4 us  [the longest x2 23.9 us: convolve(): pl.pallas_call(functools.partial(convolve_kernel, line), in_specs=[VMEM,...]
  transfers between devices with their start and end apart: 80 -> 80, of which waited for: 32 -> 28; matrix products, arithmetic and copies ran while one was open for 2% -> 2% of each run, Pallas kernels for 13% -> 15%
where the time goes in v5:
time: 306 us
  waiting for transfers between devices  145 us (47%)
  Pallas kernels  86.1 us (28%)
  starting transfers between devices  60.1 us (20%)
  local copies, waits for them, and re-layouts  7.74 us (3%)
  other arithmetic  5.82 us (2%)
    ppermute x80, waiting for transfers between devices, send(): return lax.ppermute(array, self.axis, pairs)  145 us
    ppermute x80, starting transfers between devices, send(): return lax.ppermute(array, self.axis, pairs)  60.1 us
    pallas_call x4, Pallas kernels, correlate(): pl.pallas_call(functools.partial(correlate_kernel, line, flip, bool(more)...  30.7 us
    pallas_call x2, Pallas kernels, convolve(): pl.pallas_call(functools.partial(convolve_kernel, line), in_specs=[VMEM,...  23.9 us
    pallas_call x8, Pallas kernels, window_at(): pl.pallas_call(functools.partial(window_at_kernel, line, flip, step), in_...  18.6 us
  transfers between devices with their start and end apart: 80, of which 28 were waited for; matrix products, arithmetic and copies ran while one was open for 2% of the time, Pallas kernels for 15%

profile of v5, /device:TPU:0, one launch (start us, length us, event | category | flops | bytes accessed | tf_op | source)
XLA Modules:
  0.0 305.8 jit_solution(2665099777822611804)
XLA Ops:
  0.9 1.6 copy-done
  2.4 1.9 first_analysis.1
  4.9 2.2 collective-permute-done.1
  7.5 3.0 collective-permute-start.5
  10.6 2.1 collective-permute-start.4
  12.7 1.6 collective-permute-start.2
  14.2 3.3 %collective-permute-done.5 = bf16[16,64,128]{2,1,0:T(8,128)(2,1)S(1)} collective-permute-done((bf16[16,64,128]{2,1,0:T(8,128)(2,1)S(1)}, bf16[16,64,128]{2,1,0:T(8,128)(2,1)S(1)}, u32[]{:S(2)}, u32[]{:S(2)}) %collective-permute-start.5) | collective-permute-done | bytes 262176 | tf_op jit(solution)/shard_map/ppermute | solution.py:50
  17.5 5.1 %collective-permute-done.7 = bf16[16,64,128]{2,1,0:T(8,128)(2,1)S(1)} collective-permute-done((bf16[16,64,128]{2,1,0:T(8,128)(2,1)S(1)}, bf16[16,64,128]{2,1,0:T(8,128)(2,1)S(1)}, u32[]{:S(2)}, u32[]{:S(2)}) %collective-permute-start.7) | collective-permute-done | bytes 262176 | tf_op jit(solution)/shard_map/ppermute | solution.py:50
  22.9 3.9 %collective-permute-start.8 = (bf16[16,64,128]{2,1,0:T(8,128)(2,1)S(1)}, bf16[16,64,128]{2,1,0:T(8,128)(2,1)S(1)}, u32[]{:S(2)}, u32[]{:S(2)}) collective-permute-start(bf16[16,64,128]{2,1,0:T(8,128)(2,1)S(1)} %get-tuple-element.31), channel_id=1, source_target_pairs={{0,12},{1,13},{2,14},{3,15},{4,0},{5,1},{6,2},{7,3},{8,4},{9,5},{1... | collective-permute-start | bytes 786440 | tf_op jit(solution)/shard_map/ppermute | solution.py:50
  26.9 1.6 collective-permute-start.3
  28.5 5.1 %collective-permute-done.8 = bf16[16,64,128]{2,1,0:T(8,128)(2,1)S(1)} collective-permute-done((bf16[16,64,128]{2,1,0:T(8,128)(2,1)S(1)}, bf16[16,64,128]{2,1,0:T(8,128)(2,1)S(1)}, u32[]{:S(2)}, u32[]{:S(2)}) %collective-permute-start.8) | collective-permute-done | bytes 262176 | tf_op jit(solution)/shard_map/ppermute | solution.py:50
  33.6 9.6 %collective-permute-done.6 = bf16[16,64,128]{2,1,0:T(8,128)(2,1)S(1)} collective-permute-done((bf16[16,64,128]{2,1,0:T(8,128)(2,1)S(1)}, bf16[16,64,128]{2,1,0:T(8,128)(2,1)S(1)}, u32[]{:S(2)}, u32[]{:S(2)}) %collective-permute-start.6) | collective-permute-done | bytes 262176 | tf_op jit(solution)/shard_map/ppermute | solution.py:50
  43.6 12.4 %convolve.2 = (bf16[4,32,2,16,128]{4,3,2,1,0:T(8,128)(2,1)S(1)}, bf16[4,32,2,16,128]{4,3,2,1,0:T(8,128)(2,1)S(1)}, bf16[4,32,2,16,128]{4,3,2,1,0:T(8,128)(2,1)}, bf16[4,32,2,16,128]{4,3,2,1,0:T(8,128)(2,1)S(1)}) custom-call(bf16[32,2,16,128]{3,2,1,0:T(8,128)(2,1)S(1)} %bitcast.87, bf16[2,32,128,2048]{3,2,1,0:T(8,128)(2,1)} %refs_8_.7), custom_call_target="tpu_custom_call" | custom-call | flops 1073741824 | bytes 37748736 | tf_op jit(solution)/shard_map/convolve/pallas_call | solution.py:212
  57.0 2.5 collective-permute-done.10
  60.7 1.6 collective-permute-start.14
  64.9 5.1 %collective-permute-done.14 = bf16[32,2,16,128]{3,2,1,0:T(8,128)(2,1)} collective-permute-done((bf16[32,2,16,128]{3,2,1,0:T(8,128)(2,1)S(1)}, bf16[32,2,16,128]{3,2,1,0:T(8,128)(2,1)}, u32[]{:S(2)}, u32[]{:S(2)}) %collective-permute-start.14) | collective-permute-done | bytes 262176 | tf_op jit(solution)/shard_map/ppermute | solution.py:50
  70.0 4.8 %collective-permute-done.16 = bf16[32,2,16,128]{3,2,1,0:T(8,128)(2,1)} collective-permute-done((bf16[32,2,16,128]{3,2,1,0:T(8,128)(2,1)S(1)}, bf16[32,2,16,128]{3,2,1,0:T(8,128)(2,1)}, u32[]{:S(2)}, u32[]{:S(2)}) %collective-permute-start.16) | collective-permute-done | bytes 262176 | tf_op jit(solution)/shard_map/ppermute | solution.py:50
  74.8 1.4 fusion.3
  76.2 3.5 %collective-permute-start.17 = (bf16[32,2,16,128]{3,2,1,0:T(8,128)(2,1)S(1)}, bf16[32,2,16,128]{3,2,1,0:T(8,128)(2,1)S(1)}, u32[]{:S(2)}, u32[]{:S(2)}) collective-permute-start(bf16[32,2,16,128]{3,2,1,0:T(8,128)(2,1)S(1)} %get-tuple-element.36), channel_id=1, source_target_pairs={{0,12},{1,13},{2,14},{3,15},{4,0},{5,1},{6,2},{7,3},{8,4},{9,5},{1... | collective-permute-start | bytes 786440 | tf_op jit(solution)/shard_map/ppermute | solution.py:50
  80.8 1.6 collective-permute-start.12
  83.3 3.1 %collective-permute-done.17.refs_8_ = bf16[32,2,16,128]{3,2,1,0:T(8,128)(2,1)S(1)} collective-permute-done((bf16[32,2,16,128]{3,2,1,0:T(8,128)(2,1)S(1)}, bf16[32,2,16,128]{3,2,1,0:T(8,128)(2,1)S(1)}, u32[]{:S(2)}, u32[]{:S(2)}) %collective-permute-start.17) | collective-permute-done | bytes 262176 | tf_op jit(solution)/shard_map/ppermute | solution.py:50
  86.4 9.8 %collective-permute-done.15.refs_7_ = bf16[32,2,16,128]{3,2,1,0:T(8,128)(2,1)S(1)} collective-permute-done((bf16[32,2,16,128]{3,2,1,0:T(8,128)(2,1)S(1)}, bf16[32,2,16,128]{3,2,1,0:T(8,128)(2,1)S(1)}, u32[]{:S(2)}, u32[]{:S(2)}) %collective-permute-start.15) | collective-permute-done | bytes 262176 | tf_op jit(solution)/shard_map/ppermute | solution.py:50
  96.3 2.5 window.3.refs_0_
  99.1 3.5 %collective-permute-start.23 = (bf16[32,2,16,128]{3,2,1,0:T(8,128)(2,1)S(1)}, bf16[32,2,16,128]{3,2,1,0:T(8,128)(2,1)S(1)}, u32[]{:S(2)}, u32[]{:S(2)}) collective-permute-start(bf16[32,2,16,128]{3,2,1,0:T(8,128)(2,1)S(1)} %window.3.refs_0_), channel_id=1, source_target_pairs={{0,12},{1,13},{2,14},{3,15},{4,0},{5,1},{6,2},{7,3},{8,4},{9,5},{1... | collective-permute-start | bytes 786440 | tf_op jit(solution)/shard_map/ppermute | solution.py:50
  102.6 7.2 %collective-permute-done.20.refs_1_ = bf16[32,2,16,128]{3,2,1,0:T(8,128)(2,1)S(1)} collective-permute-done((bf16[32,2,16,128]{3,2,1,0:T(8,128)(2,1)S(1)}, bf16[32,2,16,128]{3,2,1,0:T(8,128)(2,1)S(1)}, u32[]{:S(2)}, u32[]{:S(2)}) %collective-permute-start.20) | collective-permute-done | bytes 262176 | tf_op jit(solution)/shard_map/ppermute | solution.py:50
  109.8 2.2 collective-permute-start.21
  112.1 1.4 collective-permute-start.18
  114.6 10.1 %collective-permute-done.21.refs_2_ = bf16[32,2,16,128]{3,2,1,0:T(8,128)(2,1)S(1)} collective-permute-done((bf16[32,2,16,128]{3,2,1,0:T(8,128)(2,1)S(1)}, bf16[32,2,16,128]{3,2,1,0:T(8,128)(2,1)S(1)}, u32[]{:S(2)}, u32[]{:S(2)}) %collective-permute-start.21) | collective-permute-done | bytes 262176 | tf_op jit(solution)/shard_map/ppermute | solution.py:50
  124.7 1.5 collective-permute-start.22
  126.8 7.6 %correlate0.2.refs_9_ = f32[32,2,16,128]{3,2,1,0:T(8,128)S(1)} custom-call(bf16[32,2,16,128]{3,2,1,0:T(8,128)(2,1)S(1)} %window.3.refs_0_, bf16[32,2,16,128]{3,2,1,0:T(8,128)(2,1)S(1)} %collective-permute-done.20.refs_1_, bf16[32,2,16,128]{3,2,1,0:T(8,128)(2,1)S(1)} %collective-permute-done.21.refs_2_, ...), custom_call_target="tpu_custom_call" | custom-call | flops 536870912 | bytes 18874368 | tf_op jit(solution)/shard_map/correlate0/pallas_call | solution.py:270
  134.7 1.7 collective-permute-done.19.refs_1_
  136.4 1.5 collective-permute-done.30.refs_5_
  137.9 7.7 %correlate1.2.refs_3_ = f32[32,2,16,128]{3,2,1,0:T(8,128)S(1)} custom-call(bf16[32,2,16,128]{3,2,1,0:T(8,128)(2,1)S(1)} %collective-permute-done.18.refs_0_, bf16[32,2,16,128]{3,2,1,0:T(8,128)(2,1)S(1)} %collective-permute-done.19.refs_1_, bf16[32,2,16,128]{3,2,1,0:T(8,128)(2,1)S(1)} %collective-permute-done.22.refs_2_, ...), custom_call_target="tpu_custom_call" | custom-call | flops 536870912 | bytes 18874368 | tf_op jit(solution)/shard_map/correlate1/pallas_call | solution.py:270
  145.6 2.3 window.4.spec_ref
  148.0 11.5 %convolve.3 = (bf16[4,32,2,16,128]{4,3,2,1,0:T(8,128)(2,1)S(1)}, bf16[4,32,2,16,128]{4,3,2,1,0:T(8,128)(2,1)S(1)}, bf16[4,32,2,16,128]{4,3,2,1,0:T(8,128)(2,1)S(1)}, bf16[4,32,2,16,128]{4,3,2,1,0:T(8,128)(2,1)S(1)}) custom-call(bf16[32,2,16,128]{3,2,1,0:T(8,128)(2,1)S(1)} %window.4.spec_ref, bf16[2,32,128,2048]{3,2,1,0:T(8,128)(2,1)} %refs_8_.7), custom_call_target="tpu_custom_call" | custom-call | flops 1073741824 | bytes 37748736 | tf_op jit(solution)/shard_map/convolve/pallas_call | solution.py:212
  160.0 2.1 collective-permute-done.34
  163.0 1.5 collective-permute-start.40
  164.6 1.4 collective-permute-start.37
  166.0 5.6 %collective-permute-done.38 = bf16[32,2,16,128]{3,2,1,0:T(8,128)(2,1)S(1)} collective-permute-done((bf16[32,2,16,128]{3,2,1,0:T(8,128)(2,1)S(1)}, bf16[32,2,16,128]{3,2,1,0:T(8,128)(2,1)S(1)}, u32[]{:S(2)}, u32[]{:S(2)}) %collective-permute-start.38) | collective-permute-done | bytes 262176 | tf_op jit(solution)/shard_map/ppermute | solution.py:50
  171.6 4.8 %collective-permute-done.40 = bf16[32,2,16,128]{3,2,1,0:T(8,128)(2,1)S(1)} collective-permute-done((bf16[32,2,16,128]{3,2,1,0:T(8,128)(2,1)S(1)}, bf16[32,2,16,128]{3,2,1,0:T(8,128)(2,1)S(1)}, u32[]{:S(2)}, u32[]{:S(2)}) %collective-permute-start.40) | collective-permute-done | bytes 262176 | tf_op jit(solution)/shard_map/ppermute | solution.py:50
  176.7 2.3 collective-permute-start.41
  181.5 4.2 %collective-permute-done.41.refs_8_ = bf16[32,2,16,128]{3,2,1,0:T(8,128)(2,1)S(1)} collective-permute-done((bf16[32,2,16,128]{3,2,1,0:T(8,128)(2,1)S(1)}, bf16[32,2,16,128]{3,2,1,0:T(8,128)(2,1)S(1)}, u32[]{:S(2)}, u32[]{:S(2)}) %collective-permute-start.41) | collective-permute-done | bytes 262176 | tf_op jit(solution)/shard_map/ppermute | solution.py:50
  185.8 11.3 %collective-permute-done.39.refs_7_ = bf16[32,2,16,128]{3,2,1,0:T(8,128)(2,1)S(1)} collective-permute-done((bf16[32,2,16,128]{3,2,1,0:T(8,128)(2,1)S(1)}, bf16[32,2,16,128]{3,2,1,0:T(8,128)(2,1)S(1)}, u32[]{:S(2)}, u32[]{:S(2)}) %collective-permute-start.39) | collective-permute-done | bytes 262176 | tf_op jit(solution)/shard_map/ppermute | solution.py:50
  198.8 3.7 %collective-permute-start.44 = (bf16[16,64,128]{2,1,0:T(8,128)(2,1)S(1)}, bf16[16,64,128]{2,1,0:T(8,128)(2,1)S(1)}, u32[]{:S(2)}, u32[]{:S(2)}) collective-permute-start(bf16[16,64,128]{2,1,0:T(8,128)(2,1)S(1)} %window.5.spec_ref.refs_0_), channel_id=1, source_target_pairs={{0,12},{1,13},{2,14},{3,15},{4,0},{5,1},{6,2},{7,3},{8,4},{9,5},{1... | collective-permute-start | bytes 786440 | tf_op jit(solution)/shard_map/ppermute | solution.py:50
  202.6 2.3 window_at.8.refs_0_
  204.9 3.7 %collective-permute-done.42.spec_ref.refs_1_ = bf16[16,64,128]{2,1,0:T(8,128)(2,1)S(1)} collective-permute-done((bf16[16,64,128]{2,1,0:T(8,128)(2,1)S(1)}, bf16[16,64,128]{2,1,0:T(8,128)(2,1)S(1)}, u32[]{:S(2)}, u32[]{:S(2)}) %collective-permute-start.42) | collective-permute-done | bytes 262176 | tf_op jit(solution)/shard_map/ppermute | solution.py:50
  208.6 2.3 window_at.10.refs_1_
  212.8 2.3 window_at.11.refs_3_
  215.2 2.3 window_at.9.refs_0_
  217.5 10.9 %collective-permute-done.43.refs_2_.spec_ref = bf16[16,64,128]{2,1,0:T(8,128)(2,1)S(1)} collective-permute-done((bf16[16,64,128]{2,1,0:T(8,128)(2,1)S(1)}, bf16[16,64,128]{2,1,0:T(8,128)(2,1)S(1)}, u32[]{:S(2)}, u32[]{:S(2)}) %collective-permute-start.43) | collective-permute-done | bytes 262176 | tf_op jit(solution)/shard_map/ppermute | solution.py:50
  229.3 2.3 window_at.13.refs_2_
  232.7 3.2 %collective-permute-done.47.refs_6_.spec_ref = bf16[16,64,128]{2,1,0:T(8,128)(2,1)S(1)} collective-permute-done((bf16[16,64,128]{2,1,0:T(8,128)(2,1)S(1)}, bf16[16,64,128]{2,1,0:T(8,128)(2,1)S(1)}, u32[]{:S(2)}, u32[]{:S(2)}) %collective-permute-start.47) | collective-permute-done | bytes 262176 | tf_op jit(solution)/shard_map/ppermute | solution.py:50
  236.0 2.3 window_at.12.refs_1_
  238.3 2.3 window_at.14.refs_3_
  241.3 7.6 %correlate0.3.refs_9_ = f32[32,2,16,128]{3,2,1,0:T(8,128)S(1)} custom-call(bf16[32,2,16,128]{3,2,1,0:T(8,128)(2,1)S(1)} %window_at.8.refs_0_, bf16[32,2,16,128]{3,2,1,0:T(8,128)(2,1)S(1)} %window_at.10.refs_1_, bf16[32,2,16,128]{3,2,1,0:T(8,128)(2,1)S(1)} %window_at.13.refs_2_, bf16[32,2,16,128]{3,2,1,0:T(8,128)(2,1)S(1)} %window_at.11.refs_3_, ...), custom_call_target="tpu_custom_call" | custom-call | flops 536870912 | bytes 18874368 | tf_op jit(solution)/shard_map/correlate0/pallas_call | solution.py:270
  248.9 2.3 window_at.15.refs_2_
  253.7 7.8 %correlate1.3.refs_0_ = bf16[16,64,128]{2,1,0:T(8,128)(2,1)S(1)} custom-call(bf16[32,2,16,128]{3,2,1,0:T(8,128)(2,1)S(1)} %window_at.9.refs_0_, bf16[32,2,16,128]{3,2,1,0:T(8,128)(2,1)S(1)} %window_at.12.refs_1_, bf16[32,2,16,128]{3,2,1,0:T(8,128)(2,1)S(1)} %window_at.15.refs_2_, bf16[32,2,16,128]{3,2,1,0:T(8,128)(2,1)S(1)} %window_at.14.refs_3_, ...), custom_call_target="tpu_custom_call" | custom-call | flops 536870912 | bytes 18874368 | tf_op jit(solution)/shard_map/correlate1/pallas_call | solution.py:270
  262.5 3.7 %collective-permute-start.67 = (bf16[16,64,128]{2,1,0:T(8,128)(2,1)S(1)}, bf16[16,64,128]{2,1,0:T(8,128)(2,1)S(1)}, u32[]{:S(2)}, u32[]{:S(2)}) collective-permute-start(bf16[16,64,128]{2,1,0:T(8,128)(2,1)S(1)} %correlate1.3.refs_0_), channel_id=1, source_target_pairs={{0,12},{1,13},{2,14},{3,15},{4,0},{5,1},{6,2},{7,3},{8,4},{9,5},{1... | collective-permute-start | bytes 786440 | tf_op jit(solution)/shard_map/ppermute | solution.py:50
  270.0 3.4 %field.2 = bf16[16,32,2048]{2,1,0:T(8,128)(2,1)} custom-call(bf16[32,64]{1,0:T(8,128)(2,1)S(1)} %bitcast.100, s32[16,2048]{1,0:T(8,128)S(1)} %copy-done.2, bf16[16,64,128]{2,1,0:T(8,128)(2,1)S(1)} %window.5.spec_ref.refs_0_, bf16[16,64,128]{2,1,0:T(8,128)(2,1)S(1)} %collective-permute-done.42.spec_ref.refs_1_, ...), custom_call_target="tpu_custom_call" | custom-call | flops 134217728 | bytes 8388608 | tf_op jit(solution)/shard_map/field/pallas_call | solution.py:416
  274.6 2.9 collective-permute-done.67.refs_3_
  277.5 15.6 %collective-permute-done.66.refs_2_ = bf16[16,64,128]{2,1,0:T(8,128)(2,1)S(1)} collective-permute-done((bf16[16,64,128]{2,1,0:T(8,128)(2,1)S(1)}, bf16[16,64,128]{2,1,0:T(8,128)(2,1)S(1)}, u32[]{:S(2)}, u32[]{:S(2)}) %collective-permute-start.66) | collective-permute-done | bytes 262176 | tf_op jit(solution)/shard_map/ppermute | solution.py:50
  295.2 6.6 %collective-permute-done.70.refs_6_ = bf16[16,64,128]{2,1,0:T(8,128)(2,1)S(1)} collective-permute-done((bf16[16,64,128]{2,1,0:T(8,128)(2,1)S(1)}, bf16[16,64,128]{2,1,0:T(8,128)(2,1)S(1)}, u32[]{:S(2)}, u32[]{:S(2)}) %collective-permute-start.70) | collective-permute-done | bytes 262176 | tf_op jit(solution)/shard_map/ppermute | solution.py:50
  301.9 1.5 collective-permute-done.78.refs_14_
  303.4 2.3 field.3
  (167 shorter events, 32.3 us)
Async XLA Ops:
  7.5 10.0 %collective-permute-start.5 = (bf16[16,64,128]{2,1,0:T(8,128)(2,1)S(1)}, bf16[16,64,128]{2,1,0:T(8,128)(2,1)S(1)}, u32[]{:S(2)}, u32[]{:S(2)}) collective-permute-start(bf16[16,64,128]{2,1,0:T(8,128)(2,1)S(1)} %get-tuple-element.64), channel_id=1, source_target_pairs={{0,2},{1,3},{2,0},{3,1},{4,6},{5,7},{6,4},{7,5},{8,10},{9,11},{10,... | collective-permute-start | bytes 786440 | tf_op jit(solution)/shard_map/ppermute | solution.py:50
  10.4 12.2 %collective-permute-start.7 = (bf16[16,64,128]{2,1,0:T(8,128)(2,1)S(1)}, bf16[16,64,128]{2,1,0:T(8,128)(2,1)S(1)}, u32[]{:S(2)}, u32[]{:S(2)}) collective-permute-start(bf16[16,64,128]{2,1,0:T(8,128)(2,1)S(1)} %get-tuple-element.63), channel_id=1, source_target_pairs={{0,2},{1,3},{2,0},{3,1},{4,6},{5,7},{6,4},{7,5},{8,10},{9,11},{10,... | collective-permute-start | bytes 786440 | tf_op jit(solution)/shard_map/ppermute | solution.py:50
  10.6 12.3 %collective-permute-start.4 = (bf16[16,64,128]{2,1,0:T(8,128)(2,1)S(1)}, bf16[16,64,128]{2,1,0:T(8,128)(2,1)S(1)}, u32[]{:S(2)}, u32[]{:S(2)}) collective-permute-start(bf16[16,64,128]{2,1,0:T(8,128)(2,1)S(1)} %fusion.14), channel_id=1, source_target_pairs={{0,4},{1,5},{2,6},{3,7},{4,8},{5,9},{6,10},{7,11},{8,12},{9,13},{1... | collective-permute-start | bytes 786440 | tf_op jit(solution)/shard_map/ppermute | solution.py:50
  12.7 14.2 %collective-permute-start.2 = (bf16[16,64,128]{2,1,0:T(8,128)(2,1)S(1)}, bf16[16,64,128]{2,1,0:T(8,128)(2,1)S(1)}, u32[]{:S(2)}, u32[]{:S(2)}) collective-permute-start(bf16[16,64,128]{2,1,0:T(8,128)(2,1)S(1)} %get-tuple-element.62), channel_id=1, source_target_pairs={{0,4},{1,5},{2,6},{3,7},{4,8},{5,9},{6,10},{7,11},{8,12},{9,13},{1... | collective-permute-start | bytes 786440 | tf_op jit(solution)/shard_map/ppermute | solution.py:50
  22.9 10.6 %collective-permute-start.8 = (bf16[16,64,128]{2,1,0:T(8,128)(2,1)S(1)}, bf16[16,64,128]{2,1,0:T(8,128)(2,1)S(1)}, u32[]{:S(2)}, u32[]{:S(2)}) collective-permute-start(bf16[16,64,128]{2,1,0:T(8,128)(2,1)S(1)} %get-tuple-element.31), channel_id=1, source_target_pairs={{0,12},{1,13},{2,14},{3,15},{4,0},{5,1},{6,2},{7,3},{8,4},{9,5},{1... | collective-permute-start | bytes 786440 | tf_op jit(solution)/shard_map/ppermute | solution.py:50
  26.8 16.4 %collective-permute-start.6 = (bf16[16,64,128]{2,1,0:T(8,128)(2,1)S(1)}, bf16[16,64,128]{2,1,0:T(8,128)(2,1)S(1)}, u32[]{:S(2)}, u32[]{:S(2)}) collective-permute-start(bf16[16,64,128]{2,1,0:T(8,128)(2,1)S(1)} %get-tuple-element.65), channel_id=1, source_target_pairs={{0,8},{1,9},{2,10},{3,11},{4,12},{5,13},{6,14},{7,15},{8,0},{9,1},... | collective-permute-start | bytes 786440 | tf_op jit(solution)/shard_map/ppermute | solution.py:50
  26.9 16.3 %collective-permute-start.3 = (bf16[16,64,128]{2,1,0:T(8,128)(2,1)S(1)}, bf16[16,64,128]{2,1,0:T(8,128)(2,1)S(1)}, u32[]{:S(2)}, u32[]{:S(2)}) collective-permute-start(bf16[16,64,128]{2,1,0:T(8,128)(2,1)S(1)} %fusion.8), channel_id=1, source_target_pairs={{0,2},{1,3},{2,0},{3,1},{4,6},{5,7},{6,4},{7,5},{8,10},{9,11},{10,... | collective-permute-start | bytes 786440 | tf_op jit(solution)/shard_map/ppermute | solution.py:50
  60.7 9.3 %collective-permute-start.14 = (bf16[32,2,16,128]{3,2,1,0:T(8,128)(2,1)S(1)}, bf16[32,2,16,128]{3,2,1,0:T(8,128)(2,1)}, u32[]{:S(2)}, u32[]{:S(2)}) collective-permute-start(bf16[32,2,16,128]{3,2,1,0:T(8,128)(2,1)S(1)} %get-tuple-element.60), channel_id=1, source_target_pairs={{0,2},{1,3},{2,0},{3,1},{4,6},{5,7},{6,4},{7,5},{8,10},{9,11},{10,... | collective-permute-start | bytes 786440 | tf_op jit(solution)/shard_map/ppermute | solution.py:50
  62.2 12.5 %collective-permute-start.16 = (bf16[32,2,16,128]{3,2,1,0:T(8,128)(2,1)S(1)}, bf16[32,2,16,128]{3,2,1,0:T(8,128)(2,1)}, u32[]{:S(2)}, u32[]{:S(2)}) collective-permute-start(bf16[32,2,16,128]{3,2,1,0:T(8,128)(2,1)S(1)} %get-tuple-element.59), channel_id=1, source_target_pairs={{0,2},{1,3},{2,0},{3,1},{4,6},{5,7},{6,4},{7,5},{8,10},{9,11},{10,... | collective-permute-start | bytes 786440 | tf_op jit(solution)/shard_map/ppermute | solution.py:50
  64.2 12.0 %collective-permute-start.13 = (bf16[32,2,16,128]{3,2,1,0:T(8,128)(2,1)S(1)}, bf16[32,2,16,128]{3,2,1,0:T(8,128)(2,1)S(1)}, u32[]{:S(2)}, u32[]{:S(2)}) collective-permute-start(bf16[32,2,16,128]{3,2,1,0:T(8,128)(2,1)S(1)} %fusion.18), channel_id=1, source_target_pairs={{0,4},{1,5},{2,6},{3,7},{4,8},{5,9},{6,10},{7,11},{8,12},{9,13},{1... | collective-permute-start | bytes 786440 | tf_op jit(solution)/shard_map/ppermute | solution.py:50
  64.8 14.9 %collective-permute-start.11 = (bf16[32,2,16,128]{3,2,1,0:T(8,128)(2,1)S(1)}, bf16[32,2,16,128]{3,2,1,0:T(8,128)(2,1)S(1)}, u32[]{:S(2)}, u32[]{:S(2)}) collective-permute-start(bf16[32,2,16,128]{3,2,1,0:T(8,128)(2,1)S(1)} %get-tuple-element.61), channel_id=1, source_target_pairs={{0,4},{1,5},{2,6},{3,7},{4,8},{5,9},{6,10},{7,11},{8,12},{9,13},{1... | collective-permute-start | bytes 786440 | tf_op jit(solution)/shard_map/ppermute | solution.py:50
  76.2 10.2 %collective-permute-start.17 = (bf16[32,2,16,128]{3,2,1,0:T(8,128)(2,1)S(1)}, bf16[32,2,16,128]{3,2,1,0:T(8,128)(2,1)S(1)}, u32[]{:S(2)}, u32[]{:S(2)}) collective-permute-start(bf16[32,2,16,128]{3,2,1,0:T(8,128)(2,1)S(1)} %get-tuple-element.36), channel_id=1, source_target_pairs={{0,12},{1,13},{2,14},{3,15},{4,0},{5,1},{6,2},{7,3},{8,4},{9,5},{1... | collective-permute-start | bytes 786440 | tf_op jit(solution)/shard_map/ppermute | solution.py:50
  79.7 16.6 %collective-permute-start.15 = (bf16[32,2,16,128]{3,2,1,0:T(8,128)(2,1)S(1)}, bf16[32,2,16,128]{3,2,1,0:T(8,128)(2,1)S(1)}, u32[]{:S(2)}, u32[]{:S(2)}) collective-permute-start(bf16[32,2,16,128]{3,2,1,0:T(8,128)(2,1)S(1)} %get-tuple-element.58), channel_id=1, source_target_pairs={{0,8},{1,9},{2,10},{3,11},{4,12},{5,13},{6,14},{7,15},{8,0},{9,1},... | collective-permute-start | bytes 786440 | tf_op jit(solution)/shard_map/ppermute | solution.py:50
  80.8 15.5 %collective-permute-start.12 = (bf16[32,2,16,128]{3,2,1,0:T(8,128)(2,1)S(1)}, bf16[32,2,16,128]{3,2,1,0:T(8,128)(2,1)S(1)}, u32[]{:S(2)}, u32[]{:S(2)}) collective-permute-start(bf16[32,2,16,128]{3,2,1,0:T(8,128)(2,1)S(1)} %fusion.5), channel_id=1, source_target_pairs={{0,2},{1,3},{2,0},{3,1},{4,6},{5,7},{6,4},{7,5},{8,10},{9,11},{10,... | collective-permute-start | bytes 786440 | tf_op jit(solution)/shard_map/ppermute | solution.py:50
  98.8 11.1 %collective-permute-start.20 = (bf16[32,2,16,128]{3,2,1,0:T(8,128)(2,1)S(1)}, bf16[32,2,16,128]{3,2,1,0:T(8,128)(2,1)S(1)}, u32[]{:S(2)}, u32[]{:S(2)}) collective-permute-start(bf16[32,2,16,128]{3,2,1,0:T(8,128)(2,1)S(1)} %window.3.refs_0_), channel_id=1, source_target_pairs={{0,4},{1,5},{2,6},{3,7},{4,8},{5,9},{6,10},{7,11},{8,12},{9,13},{1... | collective-permute-start | bytes 786440 | tf_op jit(solution)/shard_map/ppermute | solution.py:50
  99.1 14.4 %collective-permute-start.23 = (bf16[32,2,16,128]{3,2,1,0:T(8,128)(2,1)S(1)}, bf16[32,2,16,128]{3,2,1,0:T(8,128)(2,1)S(1)}, u32[]{:S(2)}, u32[]{:S(2)}) collective-permute-start(bf16[32,2,16,128]{3,2,1,0:T(8,128)(2,1)S(1)} %window.3.refs_0_), channel_id=1, source_target_pairs={{0,12},{1,13},{2,14},{3,15},{4,0},{5,1},{6,2},{7,3},{8,4},{9,5},{1... | collective-permute-start | bytes 786440 | tf_op jit(solution)/shard_map/ppermute | solution.py:50
  102.6 11.4 %collective-permute-start.26 = (bf16[32,2,16,128]{3,2,1,0:T(8,128)(2,1)S(1)}, bf16[32,2,16,128]{3,2,1,0:T(8,128)(2,1)S(1)}, u32[]{:S(2)}, u32[]{:S(2)}) collective-permute-start(bf16[32,2,16,128]{3,2,1,0:T(8,128)(2,1)S(1)} %window.3.refs_0_), channel_id=1, source_target_pairs={{0,1},{1,0},{2,3},{3,2},{4,5},{5,4},{6,7},{7,6},{8,9},{9,8},{10,11... | collective-permute-start | bytes 786440 | tf_op jit(solution)/shard_map/ppermute | solution.py:50
  109.8 14.9 %collective-permute-start.21 = (bf16[32,2,16,128]{3,2,1,0:T(8,128)(2,1)S(1)}, bf16[32,2,16,128]{3,2,1,0:T(8,128)(2,1)S(1)}, u32[]{:S(2)}, u32[]{:S(2)}) collective-permute-start(bf16[32,2,16,128]{3,2,1,0:T(8,128)(2,1)S(1)} %window.3.refs_0_), channel_id=1, source_target_pairs={{0,8},{1,9},{2,10},{3,11},{4,12},{5,13},{6,14},{7,15},{8,0},{9,1},... | collective-permute-start | bytes 786440 | tf_op jit(solution)/shard_map/ppermute | solution.py:50
  112.1 12.7 %collective-permute-start.18 = (bf16[32,2,16,128]{3,2,1,0:T(8,128)(2,1)S(1)}, bf16[32,2,16,128]{3,2,1,0:T(8,128)(2,1)S(1)}, u32[]{:S(2)}, u32[]{:S(2)}) collective-permute-start(bf16[32,2,16,128]{3,2,1,0:T(8,128)(2,1)S(1)} %window.3.refs_0_), channel_id=1, source_target_pairs={{0,2},{1,3},{2,0},{3,1},{4,6},{5,7},{6,4},{7,5},{8,10},{9,11},{10,... | collective-permute-start | bytes 786440 | tf_op jit(solution)/shard_map/ppermute | solution.py:50
  113.5 12.7 %collective-permute-start.27 = (bf16[32,2,16,128]{3,2,1,0:T(8,128)(2,1)S(1)}, bf16[32,2,16,128]{3,2,1,0:T(8,128)(2,1)S(1)}, u32[]{:S(2)}, u32[]{:S(2)}) collective-permute-start(bf16[32,2,16,128]{3,2,1,0:T(8,128)(2,1)S(1)} %collective-permute-done.20.refs_1_), channel_id=1, source_target_pairs={{0,1},{1,0},{2,3},{3,2},{4,5},{5,4},{6,7},{7,6},{8,9},{9,8},{10,11... | collective-permute-start | bytes 786440 | tf_op jit(solution)/shard_map/ppermute | solution.py:50
  113.5 12.7 %collective-permute-start.29 = (bf16[32,2,16,128]{3,2,1,0:T(8,128)(2,1)S(1)}, bf16[32,2,16,128]{3,2,1,0:T(8,128)(2,1)S(1)}, u32[]{:S(2)}, u32[]{:S(2)}) collective-permute-start(bf16[32,2,16,128]{3,2,1,0:T(8,128)(2,1)S(1)} %collective-permute-done.23.refs_3_), channel_id=1, source_target_pairs={{0,1},{1,0},{2,3},{3,2},{4,5},{5,4},{6,7},{7,6},{8,9},{9,8},{10,11... | collective-permute-start | bytes 786440 | tf_op jit(solution)/shard_map/ppermute | solution.py:50
  114.0 12.5 %collective-permute-start.24 = (bf16[32,2,16,128]{3,2,1,0:T(8,128)(2,1)S(1)}, bf16[32,2,16,128]{3,2,1,0:T(8,128)(2,1)S(1)}, u32[]{:S(2)}, u32[]{:S(2)}) collective-permute-start(bf16[32,2,16,128]{3,2,1,0:T(8,128)(2,1)S(1)} %collective-permute-done.23.refs_3_), channel_id=1, source_target_pairs={{0,2},{1,3},{2,0},{3,1},{4,6},{5,7},{6,4},{7,5},{8,10},{9,11},{10,... | collective-permute-start | bytes 786440 | tf_op jit(solution)/shard_map/ppermute | solution.py:50
  124.7 9.7 %collective-permute-start.22 = (bf16[32,2,16,128]{3,2,1,0:T(8,128)(2,1)S(1)}, bf16[32,2,16,128]{3,2,1,0:T(8,128)(2,1)S(1)}, u32[]{:S(2)}, u32[]{:S(2)}) collective-permute-start(bf16[32,2,16,128]{3,2,1,0:T(8,128)(2,1)S(1)} %collective-permute-done.21.refs_2_), channel_id=1, source_target_pairs={{0,2},{1,3},{2,0},{3,1},{4,6},{5,7},{6,4},{7,5},{8,10},{9,11},{10,... | collective-permute-start | bytes 786440 | tf_op jit(solution)/shard_map/ppermute | solution.py:50
  126.2 10.2 %collective-permute-start.19 = (bf16[32,2,16,128]{3,2,1,0:T(8,128)(2,1)S(1)}, bf16[32,2,16,128]{3,2,1,0:T(8,128)(2,1)S(1)}, u32[]{:S(2)}, u32[]{:S(2)}) collective-permute-start(bf16[32,2,16,128]{3,2,1,0:T(8,128)(2,1)S(1)} %collective-permute-done.18.refs_0_), channel_id=1, source_target_pairs={{0,4},{1,5},{2,6},{3,7},{4,8},{5,9},{6,10},{7,11},{8,12},{9,13},{1... | collective-permute-start | bytes 786440 | tf_op jit(solution)/shard_map/ppermute | solution.py:50
  126.2 10.2 %collective-permute-start.25 = (bf16[32,2,16,128]{3,2,1,0:T(8,128)(2,1)S(1)}, bf16[32,2,16,128]{3,2,1,0:T(8,128)(2,1)S(1)}, u32[]{:S(2)}, u32[]{:S(2)}) collective-permute-start(bf16[32,2,16,128]{3,2,1,0:T(8,128)(2,1)S(1)} %collective-permute-done.18.refs_0_), channel_id=1, source_target_pairs={{0,1},{1,0},{2,3},{3,2},{4,5},{5,4},{6,7},{7,6},{8,9},{9,8},{10,11... | collective-permute-start | bytes 786440 | tf_op jit(solution)/shard_map/ppermute | solution.py:50
  126.5 9.9 %collective-permute-start.32 = (bf16[32,2,16,128]{3,2,1,0:T(8,128)(2,1)S(1)}, bf16[32,2,16,128]{3,2,1,0:T(8,128)(2,1)S(1)}, u32[]{:S(2)}, u32[]{:S(2)}) collective-permute-start(bf16[32,2,16,128]{3,2,1,0:T(8,128)(2,1)S(1)} %collective-permute-done.24.refs_3_), channel_id=1, source_target_pairs={{0,1},{1,0},{2,3},{3,2},{4,5},{5,4},{6,7},{7,6},{8,9},{9,8},{10,11... | collective-permute-start | bytes 786440 | tf_op jit(solution)/shard_map/ppermute | solution.py:50
  162.4 9.2 %collective-permute-start.38 = (bf16[32,2,16,128]{3,2,1,0:T(8,128)(2,1)S(1)}, bf16[32,2,16,128]{3,2,1,0:T(8,128)(2,1)S(1)}, u32[]{:S(2)}, u32[]{:S(2)}) collective-permute-start(bf16[32,2,16,128]{3,2,1,0:T(8,128)(2,1)S(1)} %get-tuple-element.55), channel_id=1, source_target_pairs={{0,2},{1,3},{2,0},{3,1},{4,6},{5,7},{6,4},{7,5},{8,10},{9,11},{10,... | collective-permute-start | bytes 786440 | tf_op jit(solution)/shard_map/ppermute | solution.py:50
  163.0 13.4 %collective-permute-start.40 = (bf16[32,2,16,128]{3,2,1,0:T(8,128)(2,1)S(1)}, bf16[32,2,16,128]{3,2,1,0:T(8,128)(2,1)S(1)}, u32[]{:S(2)}, u32[]{:S(2)}) collective-permute-start(bf16[32,2,16,128]{3,2,1,0:T(8,128)(2,1)S(1)} %get-tuple-element.54), channel_id=1, source_target_pairs={{0,2},{1,3},{2,0},{3,1},{4,6},{5,7},{6,4},{7,5},{8,10},{9,11},{10,... | collective-permute-start | bytes 786440 | tf_op jit(solution)/shard_map/ppermute | solution.py:50
  164.6 12.1 %collective-permute-start.37 = (bf16[32,2,16,128]{3,2,1,0:T(8,128)(2,1)S(1)}, bf16[32,2,16,128]{3,2,1,0:T(8,128)(2,1)S(1)}, u32[]{:S(2)}, u32[]{:S(2)}) collective-permute-start(bf16[32,2,16,128]{3,2,1,0:T(8,128)(2,1)S(1)} %fusion.22), channel_id=1, source_target_pairs={{0,4},{1,5},{2,6},{3,7},{4,8},{5,9},{6,10},{7,11},{8,12},{9,13},{1... | collective-permute-start | bytes 786440 | tf_op jit(solution)/shard_map/ppermute | solution.py:50
  166.0 14.5 %collective-permute-start.35 = (bf16[32,2,16,128]{3,2,1,0:T(8,128)(2,1)S(1)}, bf16[32,2,16,128]{3,2,1,0:T(8,128)(2,1)S(1)}, u32[]{:S(2)}, u32[]{:S(2)}) collective-permute-start(bf16[32,2,16,128]{3,2,1,0:T(8,128)(2,1)S(1)} %get-tuple-element.56), channel_id=1, source_target_pairs={{0,4},{1,5},{2,6},{3,7},{4,8},{5,9},{6,10},{7,11},{8,12},{9,13},{1... | collective-permute-start | bytes 786440 | tf_op jit(solution)/shard_map/ppermute | solution.py:50
  176.7 9.1 %collective-permute-start.41 = (bf16[32,2,16,128]{3,2,1,0:T(8,128)(2,1)S(1)}, bf16[32,2,16,128]{3,2,1,0:T(8,128)(2,1)S(1)}, u32[]{:S(2)}, u32[]{:S(2)}) collective-permute-start(bf16[32,2,16,128]{3,2,1,0:T(8,128)(2,1)S(1)} %get-tuple-element.44), channel_id=1, source_target_pairs={{0,12},{1,13},{2,14},{3,15},{4,0},{5,1},{6,2},{7,3},{8,4},{9,5},{1... | collective-permute-start | bytes 786440 | tf_op jit(solution)/shard_map/ppermute | solution.py:50
  178.9 18.1 %collective-permute-start.39 = (bf16[32,2,16,128]{3,2,1,0:T(8,128)(2,1)S(1)}, bf16[32,2,16,128]{3,2,1,0:T(8,128)(2,1)S(1)}, u32[]{:S(2)}, u32[]{:S(2)}) collective-permute-start(bf16[32,2,16,128]{3,2,1,0:T(8,128)(2,1)S(1)} %get-tuple-element.53), channel_id=1, source_target_pairs={{0,8},{1,9},{2,10},{3,11},{4,12},{5,13},{6,14},{7,15},{8,0},{9,1},... | collective-permute-start | bytes 786440 | tf_op jit(solution)/shard_map/ppermute | solution.py:50
  180.6 16.4 %collective-permute-start.36 = (bf16[32,2,16,128]{3,2,1,0:T(8,128)(2,1)S(1)}, bf16[32,2,16,128]{3,2,1,0:T(8,128)(2,1)S(1)}, u32[]{:S(2)}, u32[]{:S(2)}) collective-permute-start(bf16[32,2,16,128]{3,2,1,0:T(8,128)(2,1)S(1)} %fusion.2), channel_id=1, source_target_pairs={{0,2},{1,3},{2,0},{3,1},{4,6},{5,7},{6,4},{7,5},{8,10},{9,11},{10,... | collective-permute-start | bytes 786440 | tf_op jit(solution)/shard_map/ppermute | solution.py:50
  197.5 11.1 %collective-permute-start.42 = (bf16[16,64,128]{2,1,0:T(8,128)(2,1)S(1)}, bf16[16,64,128]{2,1,0:T(8,128)(2,1)S(1)}, u32[]{:S(2)}, u32[]{:S(2)}) collective-permute-start(bf16[16,64,128]{2,1,0:T(8,128)(2,1)S(1)} %window.5.spec_ref.refs_0_), channel_id=1, source_target_pairs={{0,4},{1,5},{2,6},{3,7},{4,8},{5,9},{6,10},{7,11},{8,12},{9,13},{1... | collective-permute-start | bytes 786440 | tf_op jit(solution)/shard_map/ppermute | solution.py:50
  197.6 13.9 %collective-permute-start.45 = (bf16[16,64,128]{2,1,0:T(8,128)(2,1)S(1)}, bf16[16,64,128]{2,1,0:T(8,128)(2,1)S(1)}, u32[]{:S(2)}, u32[]{:S(2)}) collective-permute-start(bf16[16,64,128]{2,1,0:T(8,128)(2,1)S(1)} %window.5.spec_ref.refs_0_), channel_id=1, source_target_pairs={{0,2},{1,3},{2,0},{3,1},{4,6},{5,7},{6,4},{7,5},{8,10},{9,11},{10,... | collective-permute-start | bytes 786440 | tf_op jit(solution)/shard_map/ppermute | solution.py:50
  198.8 12.8 %collective-permute-start.44 = (bf16[16,64,128]{2,1,0:T(8,128)(2,1)S(1)}, bf16[16,64,128]{2,1,0:T(8,128)(2,1)S(1)}, u32[]{:S(2)}, u32[]{:S(2)}) collective-permute-start(bf16[16,64,128]{2,1,0:T(8,128)(2,1)S(1)} %window.5.spec_ref.refs_0_), channel_id=1, source_target_pairs={{0,12},{1,13},{2,14},{3,15},{4,0},{5,1},{6,2},{7,3},{8,4},{9,5},{1... | collective-permute-start | bytes 786440 | tf_op jit(solution)/shard_map/ppermute | solution.py:50
  208.6 19.8 %collective-permute-start.43 = (bf16[16,64,128]{2,1,0:T(8,128)(2,1)S(1)}, bf16[16,64,128]{2,1,0:T(8,128)(2,1)S(1)}, u32[]{:S(2)}, u32[]{:S(2)}) collective-permute-start(bf16[16,64,128]{2,1,0:T(8,128)(2,1)S(1)} %window.5.spec_ref.refs_0_), channel_id=1, source_target_pairs={{0,8},{1,9},{2,10},{3,11},{4,12},{5,13},{6,14},{7,15},{8,0},{9,1},... | collective-permute-start | bytes 786440 | tf_op jit(solution)/shard_map/ppermute | solution.py:50
  208.6 23.0 %collective-permute-start.58 = (bf16[32,2,16,128]{3,2,1,0:T(8,128)(2,1)S(1)}, bf16[32,2,16,128]{3,2,1,0:T(8,128)(2,1)S(1)}, u32[]{:S(2)}, u32[]{:S(2)}) collective-permute-start(bf16[32,2,16,128]{3,2,1,0:T(8,128)(2,1)S(1)} %window_at.8.refs_0_), channel_id=1, source_target_pairs={{0,1},{1,0},{2,3},{3,2},{4,5},{5,4},{6,7},{7,6},{8,9},{9,8},{10,11... | collective-permute-start | bytes 786440 | tf_op jit(solution)/shard_map/ppermute | solution.py:50
  211.0 20.7 %collective-permute-start.59 = (bf16[32,2,16,128]{3,2,1,0:T(8,128)(2,1)S(1)}, bf16[32,2,16,128]{3,2,1,0:T(8,128)(2,1)S(1)}, u32[]{:S(2)}, u32[]{:S(2)}) collective-permute-start(bf16[32,2,16,128]{3,2,1,0:T(8,128)(2,1)S(1)} %window_at.10.refs_1_), channel_id=1, source_target_pairs={{0,1},{1,0},{2,3},{3,2},{4,5},{5,4},{6,7},{7,6},{8,9},{9,8},{10,11... | collective-permute-start | bytes 786440 | tf_op jit(solution)/shard_map/ppermute | solution.py:50
  211.5 20.7 %collective-permute-start.46 = (bf16[16,64,128]{2,1,0:T(8,128)(2,1)S(1)}, bf16[16,64,128]{2,1,0:T(8,128)(2,1)S(1)}, u32[]{:S(2)}, u32[]{:S(2)}) collective-permute-start(bf16[16,64,128]{2,1,0:T(8,128)(2,1)S(1)} %collective-permute-done.45.spec_ref.refs_4_), channel_id=1, source_target_pairs={{0,4},{1,5},{2,6},{3,7},{4,8},{5,9},{6,10},{7,11},{8,12},{9,13},{1... | collective-permute-start | bytes 786440 | tf_op jit(solution)/shard_map/ppermute | solution.py:50
  211.6 20.7 %collective-permute-start.48 = (bf16[16,64,128]{2,1,0:T(8,128)(2,1)S(1)}, bf16[16,64,128]{2,1,0:T(8,128)(2,1)S(1)}, u32[]{:S(2)}, u32[]{:S(2)}) collective-permute-start(bf16[16,64,128]{2,1,0:T(8,128)(2,1)S(1)} %collective-permute-done.44.spec_ref.refs_3_), channel_id=1, source_target_pairs={{0,2},{1,3},{2,0},{3,1},{4,6},{5,7},{6,4},{7,5},{8,10},{9,11},{10,... | collective-permute-start | bytes 786440 | tf_op jit(solution)/shard_map/ppermute | solution.py:50
  228.4 7.5 %collective-permute-start.47 = (bf16[16,64,128]{2,1,0:T(8,128)(2,1)S(1)}, bf16[16,64,128]{2,1,0:T(8,128)(2,1)S(1)}, u32[]{:S(2)}, u32[]{:S(2)}) collective-permute-start(bf16[16,64,128]{2,1,0:T(8,128)(2,1)S(1)} %collective-permute-done.43.refs_2_.spec_ref), channel_id=1, source_target_pairs={{0,2},{1,3},{2,0},{3,1},{4,6},{5,7},{6,4},{7,5},{8,10},{9,11},{10,... | collective-permute-start | bytes 786440 | tf_op jit(solution)/shard_map/ppermute | solution.py:50
  231.6 9.0 %collective-permute-start.61 = (bf16[32,2,16,128]{3,2,1,0:T(8,128)(2,1)S(1)}, bf16[32,2,16,128]{3,2,1,0:T(8,128)(2,1)S(1)}, u32[]{:S(2)}, u32[]{:S(2)}) collective-permute-start(bf16[32,2,16,128]{3,2,1,0:T(8,128)(2,1)S(1)} %window_at.11.refs_3_), channel_id=1, source_target_pairs={{0,1},{1,0},{2,3},{3,2},{4,5},{5,4},{6,7},{7,6},{8,9},{9,8},{10,11... | collective-permute-start | bytes 786440 | tf_op jit(solution)/shard_map/ppermute | solution.py:50
  231.7 9.5 %collective-permute-start.60 = (bf16[32,2,16,128]{3,2,1,0:T(8,128)(2,1)S(1)}, bf16[32,2,16,128]{3,2,1,0:T(8,128)(2,1)S(1)}, u32[]{:S(2)}, u32[]{:S(2)}) collective-permute-start(bf16[32,2,16,128]{3,2,1,0:T(8,128)(2,1)S(1)} %window_at.13.refs_2_), channel_id=1, source_target_pairs={{0,1},{1,0},{2,3},{3,2},{4,5},{5,4},{6,7},{7,6},{8,9},{9,8},{10,11... | collective-permute-start | bytes 786440 | tf_op jit(solution)/shard_map/ppermute | solution.py:50
  232.2 19.1 %collective-permute-start.49 = (bf16[16,64,128]{2,1,0:T(8,128)(2,1)S(1)}, bf16[16,64,128]{2,1,0:T(8,128)(2,1)S(1)}, u32[]{:S(2)}, u32[]{:S(2)}) collective-permute-start(bf16[16,64,128]{2,1,0:T(8,128)(2,1)S(1)} %window.5.spec_ref.refs_0_), channel_id=1, source_target_pairs={{0,1},{1,0},{2,3},{3,2},{4,5},{5,4},{6,7},{7,6},{8,9},{9,8},{10,11... | collective-permute-start | bytes 786440 | tf_op jit(solution)/shard_map/ppermute | solution.py:50
  232.3 19.5 %collective-permute-start.57 = (bf16[32,2,16,128]{3,2,1,0:T(8,128)(2,1)S(1)}, bf16[32,2,16,128]{3,2,1,0:T(8,128)(2,1)S(1)}, u32[]{:S(2)}, u32[]{:S(2)}) collective-permute-start(bf16[32,2,16,128]{3,2,1,0:T(8,128)(2,1)S(1)} %window_at.9.refs_0_), channel_id=1, source_target_pairs={{0,1},{1,0},{2,3},{3,2},{4,5},{5,4},{6,7},{7,6},{8,9},{9,8},{10,11... | collective-permute-start | bytes 786440 | tf_op jit(solution)/shard_map/ppermute | solution.py:50
  235.9 15.9 %collective-permute-start.50 = (bf16[16,64,128]{2,1,0:T(8,128)(2,1)S(1)}, bf16[16,64,128]{2,1,0:T(8,128)(2,1)S(1)}, u32[]{:S(2)}, u32[]{:S(2)}) collective-permute-start(bf16[16,64,128]{2,1,0:T(8,128)(2,1)S(1)} %collective-permute-done.42.spec_ref.refs_1_), channel_id=1, source_target_pairs={{0,1},{1,0},{2,3},{3,2},{4,5},{5,4},{6,7},{7,6},{8,9},{9,8},{10,11... | collective-permute-start | bytes 786440 | tf_op jit(solution)/shard_map/ppermute | solution.py:50
  240.6 11.7 %collective-permute-start.52 = (bf16[16,64,128]{2,1,0:T(8,128)(2,1)S(1)}, bf16[16,64,128]{2,1,0:T(8,128)(2,1)S(1)}, u32[]{:S(2)}, u32[]{:S(2)}) collective-permute-start(bf16[16,64,128]{2,1,0:T(8,128)(2,1)S(1)} %collective-permute-done.44.spec_ref.refs_3_), channel_id=1, source_target_pairs={{0,1},{1,0},{2,3},{3,2},{4,5},{5,4},{6,7},{7,6},{8,9},{9,8},{10,11... | collective-permute-start | bytes 786440 | tf_op jit(solution)/shard_map/ppermute | solution.py:50
  241.2 11.2 %collective-permute-start.64 = (bf16[32,2,16,128]{3,2,1,0:T(8,128)(2,1)S(1)}, bf16[32,2,16,128]{3,2,1,0:T(8,128)(2,1)S(1)}, u32[]{:S(2)}, u32[]{:S(2)}) collective-permute-start(bf16[32,2,16,128]{3,2,1,0:T(8,128)(2,1)S(1)} %window_at.14.refs_3_), channel_id=1, source_target_pairs={{0,1},{1,0},{2,3},{3,2},{4,5},{5,4},{6,7},{7,6},{8,9},{9,8},{10,11... | collective-permute-start | bytes 786440 | tf_op jit(solution)/shard_map/ppermute | solution.py:50
  251.9 9.7 %collective-permute-start.53 = (bf16[16,64,128]{2,1,0:T(8,128)(2,1)S(1)}, bf16[16,64,128]{2,1,0:T(8,128)(2,1)S(1)}, u32[]{:S(2)}, u32[]{:S(2)}) collective-permute-start(bf16[16,64,128]{2,1,0:T(8,128)(2,1)S(1)} %collective-permute-done.45.spec_ref.refs_4_), channel_id=1, source_target_pairs={{0,1},{1,0},{2,3},{3,2},{4,5},{5,4},{6,7},{7,6},{8,9},{9,8},{10,11... | collective-permute-start | bytes 786440 | tf_op jit(solution)/shard_map/ppermute | solution.py:50
  252.3 10.2 %collective-permute-start.51 = (bf16[16,64,128]{2,1,0:T(8,128)(2,1)S(1)}, bf16[16,64,128]{2,1,0:T(8,128)(2,1)}, u32[]{:S(2)}, u32[]{:S(2)}) collective-permute-start(bf16[16,64,128]{2,1,0:T(8,128)(2,1)S(1)} %collective-permute-done.43.refs_2_.spec_ref), channel_id=1, source_target_pairs={{0,1},{1,0},{2,3},{3,2},{4,5},{5,4},{6,7},{7,6},{8,9},{9,8},{10,11... | collective-permute-start | bytes 786440 | tf_op jit(solution)/shard_map/ppermute | solution.py:50
  252.4 13.8 %collective-permute-start.54 = (bf16[16,64,128]{2,1,0:T(8,128)(2,1)S(1)}, bf16[16,64,128]{2,1,0:T(8,128)(2,1)}, u32[]{:S(2)}, u32[]{:S(2)}) collective-permute-start(bf16[16,64,128]{2,1,0:T(8,128)(2,1)S(1)} %collective-permute-done.46.refs_5_.spec_ref), channel_id=1, source_target_pairs={{0,1},{1,0},{2,3},{3,2},{4,5},{5,4},{6,7},{7,6},{8,9},{9,8},{10,11... | collective-permute-start | bytes 786440 | tf_op jit(solution)/shard_map/ppermute | solution.py:50
  253.0 14.2 %collective-permute-start.56 = (bf16[16,64,128]{2,1,0:T(8,128)(2,1)S(1)}, bf16[16,64,128]{2,1,0:T(8,128)(2,1)}, u32[]{:S(2)}, u32[]{:S(2)}) collective-permute-start(bf16[16,64,128]{2,1,0:T(8,128)(2,1)S(1)} %collective-permute-done.48.refs_7_.spec_ref), channel_id=1, source_target_pairs={{0,1},{1,0},{2,3},{3,2},{4,5},{5,4},{6,7},{7,6},{8,9},{9,8},{10,11... | collective-permute-start | bytes 786440 | tf_op jit(solution)/shard_map/ppermute | solution.py:50
  253.3 13.8 %collective-permute-start.55 = (bf16[16,64,128]{2,1,0:T(8,128)(2,1)S(1)}, bf16[16,64,128]{2,1,0:T(8,128)(2,1)}, u32[]{:S(2)}, u32[]{:S(2)}) collective-permute-start(bf16[16,64,128]{2,1,0:T(8,128)(2,1)S(1)} %collective-permute-done.47.refs_6_.spec_ref), channel_id=1, source_target_pairs={{0,1},{1,0},{2,3},{3,2},{4,5},{5,4},{6,7},{7,6},{8,9},{9,8},{10,11... | collective-permute-start | bytes 786440 | tf_op jit(solution)/shard_map/ppermute | solution.py:50
  262.2 11.1 %collective-permute-start.65 = (bf16[16,64,128]{2,1,0:T(8,128)(2,1)S(1)}, bf16[16,64,128]{2,1,0:T(8,128)(2,1)S(1)}, u32[]{:S(2)}, u32[]{:S(2)}) collective-permute-start(bf16[16,64,128]{2,1,0:T(8,128)(2,1)S(1)} %correlate1.3.refs_0_), channel_id=1, source_target_pairs={{0,4},{1,5},{2,6},{3,7},{4,8},{5,9},{6,10},{7,11},{8,12},{9,13},{1... | collective-permute-start | bytes 786440 | tf_op jit(solution)/shard_map/ppermute | solution.py:50
  262.5 15.0 %collective-permute-start.67 = (bf16[16,64,128]{2,1,0:T(8,128)(2,1)S(1)}, bf16[16,64,128]{2,1,0:T(8,128)(2,1)S(1)}, u32[]{:S(2)}, u32[]{:S(2)}) collective-permute-start(bf16[16,64,128]{2,1,0:T(8,128)(2,1)S(1)} %correlate1.3.refs_0_), channel_id=1, source_target_pairs={{0,12},{1,13},{2,14},{3,15},{4,0},{5,1},{6,2},{7,3},{8,4},{9,5},{1... | collective-permute-start | bytes 786440 | tf_op jit(solution)/shard_map/ppermute | solution.py:50
  266.2 7.8 %collective-permute-start.68 = (bf16[16,64,128]{2,1,0:T(8,128)(2,1)S(1)}, bf16[16,64,128]{2,1,0:T(8,128)(2,1)S(1)}, u32[]{:S(2)}, u32[]{:S(2)}) collective-permute-start(bf16[16,64,128]{2,1,0:T(8,128)(2,1)S(1)} %correlate1.3.refs_0_), channel_id=1, source_target_pairs={{0,2},{1,3},{2,0},{3,1},{4,6},{5,7},{6,4},{7,5},{8,10},{9,11},{10,... | collective-permute-start | bytes 786440 | tf_op jit(solution)/shard_map/ppermute | solution.py:50
  273.3 19.8 %collective-permute-start.66 = (bf16[16,64,128]{2,1,0:T(8,128)(2,1)S(1)}, bf16[16,64,128]{2,1,0:T(8,128)(2,1)S(1)}, u32[]{:S(2)}, u32[]{:S(2)}) collective-permute-start(bf16[16,64,128]{2,1,0:T(8,128)(2,1)S(1)} %correlate1.3.refs_0_), channel_id=1, source_target_pairs={{0,8},{1,9},{2,10},{3,11},{4,12},{5,13},{6,14},{7,15},{8,0},{9,1},... | collective-permute-start | bytes 786440 | tf_op jit(solution)/shard_map/ppermute | solution.py:50
  273.4 19.7 %collective-permute-start.72 = (bf16[16,64,128]{2,1,0:T(8,128)(2,1)S(1)}, bf16[16,64,128]{2,1,0:T(8,128)(2,1)S(1)}, u32[]{:S(2)}, u32[]{:S(2)}) collective-permute-start(bf16[16,64,128]{2,1,0:T(8,128)(2,1)S(1)} %correlate1.3.refs_0_), channel_id=1, source_target_pairs={{0,1},{1,0},{2,3},{3,2},{4,5},{5,4},{6,7},{7,6},{8,9},{9,8},{10,11... | collective-permute-start | bytes 786440 | tf_op jit(solution)/shard_map/ppermute | solution.py:50
  273.5 21.2 %collective-permute-start.73 = (bf16[16,64,128]{2,1,0:T(8,128)(2,1)S(1)}, bf16[16,64,128]{2,1,0:T(8,128)(2,1)S(1)}, u32[]{:S(2)}, u32[]{:S(2)}) collective-permute-start(bf16[16,64,128]{2,1,0:T(8,128)(2,1)S(1)} %collective-permute-done.65.refs_1_), channel_id=1, source_target_pairs={{0,1},{1,0},{2,3},{3,2},{4,5},{5,4},{6,7},{7,6},{8,9},{9,8},{10,11... | collective-permute-start | bytes 786440 | tf_op jit(solution)/shard_map/ppermute | solution.py:50
  274.0 20.2 %collective-permute-start.69 = (bf16[16,64,128]{2,1,0:T(8,128)(2,1)S(1)}, bf16[16,64,128]{2,1,0:T(8,128)(2,1)S(1)}, u32[]{:S(2)}, u32[]{:S(2)}) collective-permute-start(bf16[16,64,128]{2,1,0:T(8,128)(2,1)S(1)} %collective-permute-done.68.refs_4_), channel_id=1, source_target_pairs={{0,4},{1,5},{2,6},{3,7},{4,8},{5,9},{6,10},{7,11},{8,12},{9,13},{1... | collective-permute-start | bytes 786440 | tf_op jit(solution)/shard_map/ppermute | solution.py:50
  277.5 16.9 %collective-permute-start.71 = (bf16[16,64,128]{2,1,0:T(8,128)(2,1)S(1)}, bf16[16,64,128]{2,1,0:T(8,128)(2,1)S(1)}, u32[]{:S(2)}, u32[]{:S(2)}) collective-permute-start(bf16[16,64,128]{2,1,0:T(8,128)(2,1)S(1)} %collective-permute-done.67.refs_3_), channel_id=1, source_target_pairs={{0,2},{1,3},{2,0},{3,1},{4,6},{5,7},{6,4},{7,5},{8,10},{9,11},{10,... | collective-permute-start | bytes 786440 | tf_op jit(solution)/shard_map/ppermute | solution.py:50
  293.1 8.7 %collective-permute-start.70 = (bf16[16,64,128]{2,1,0:T(8,128)(2,1)S(1)}, bf16[16,64,128]{2,1,0:T(8,128)(2,1)S(1)}, u32[]{:S(2)}, u32[]{:S(2)}) collective-permute-start(bf16[16,64,128]{2,1,0:T(8,128)(2,1)S(1)} %collective-permute-done.66.refs_2_), channel_id=1, source_target_pairs={{0,2},{1,3},{2,0},{3,1},{4,6},{5,7},{6,4},{7,5},{8,10},{9,11},{10,... | collective-permute-start | bytes 786440 | tf_op jit(solution)/shard_map/ppermute | solution.py:50
  294.2 7.6 %collective-permute-start.76 = (bf16[16,64,128]{2,1,0:T(8,128)(2,1)S(1)}, bf16[16,64,128]{2,1,0:T(8,128)(2,1)S(1)}, u32[]{:S(2)}, u32[]{:S(2)}) collective-permute-start(bf16[16,64,128]{2,1,0:T(8,128)(2,1)S(1)} %collective-permute-done.68.refs_4_), channel_id=1, source_target_pairs={{0,1},{1,0},{2,3},{3,2},{4,5},{5,4},{6,7},{7,6},{8,9},{9,8},{10,11... | collective-permute-start | bytes 786440 | tf_op jit(solution)/shard_map/ppermute | solution.py:50
  (26 other events, 149.8 us)

commit v6 on v5

--- a/solution.py
+++ b/solution.py
@@ -81,6 +81,7 @@
 ANY = pl.BlockSpec(memory_space=pl.ANY)
 CHUNKS = 8
 STRIPS = 4
+SLOTS = 4
 
 
 def limit(mebibytes):
@@ -171,15 +172,19 @@
     focal = spec_ref.shape[2]
     rows = NFW // CHUNKS
 
+    slots = held.shape[0]
+
     def copy(chunk):
+        slot = lax.rem(chunk, slots)
         part = pl.ds(chunk * rows, rows)
-        return pltpu.make_async_copy(panel_ref.at[:, part], held.at[:, part], sems.at[chunk])
-
-    for chunk in range(CHUNKS):
+        return pltpu.make_async_copy(panel_ref.at[:, part], held.at[slot], sems.at[slot])
+
+    for chunk in range(slots):
         copy(chunk).start()
 
     def body(chunk, carry):
         copy(chunk).wait()
+        slot = lax.rem(chunk, slots)
         for row in range(rows):
             w = chunk * rows + row
             real, imag = spec_ref[w, 0], spec_ref[w, 1]
@@ -188,11 +193,16 @@
             )
             for flip, step in relative(line):
                 columns = pl.ds(chip_columns(line, True, flip, step), 2 * LANES)
-                panel = held[:, w, :, columns].reshape(2 * LANES, 2 * LANES)
+                panel = held[slot, :, row, :, columns].reshape(2 * LANES, 2 * LANES)
                 block = jnp.dot(left, panel, preferred_element_type=F32)
                 mine, theirs = split_cores(core, block.astype(BF16))
                 keep[flip][step, w] = mine.reshape(2, focal, LANES)
                 send[flip][step, w] = theirs.reshape(2, focal, LANES)
+
+        @pl.when(chunk + slots < CHUNKS)
+        def _():
+            copy(chunk + slots).start()
+
         return carry
 
     lax.fori_loop(0, CHUNKS, body, 0)
@@ -214,8 +224,11 @@
         in_specs=[VMEM, ANY],
         out_specs=[VMEM] * 4,
         out_shape=[out] * 4,
-        scratch_shapes=[pltpu.VMEM(reflection.shape, BF16), pltpu.SemaphoreType.DMA((CHUNKS,))],
-        compiler_params=limit(36),
+        scratch_shapes=[
+            pltpu.VMEM((SLOTS, 2, NFW // CHUNKS, LANES, reflection.shape[3]), BF16),
+            pltpu.SemaphoreType.DMA((SLOTS,)),
+        ],
+        compiler_params=limit(20),
         cost_estimate=panel_cost(focal, reflection.shape[3]),
         name="convolve",
     )(spectrum, reflection)
@@ -234,13 +247,19 @@
         wait(chunk)
         for row in range(rows):
             w = chunk * rows + row
-            total = jnp.zeros((2 * focal, 2 * LANES), F32)
+            panels, specs = [], []
             for step in range(line):
-                panel = held[chunk, step, :, row].reshape(2 * LANES, 2 * LANES)
-                spec = join_cores(
-                    core, own[step][w].reshape(2 * focal, LANES), other[step][w].reshape(2 * focal, LANES)
+                panels.append(held[chunk, step, :, row].reshape(2 * LANES, 2 * LANES))
+                mine, theirs = own[step][w], other[step][w]
+                specs.append(
+                    join_cores(core, mine.reshape(2 * focal, LANES), theirs.reshape(2 * focal, LANES))
                 )
-                total += lax.dot_general(spec, panel, (((1,), (1,)), ((), ())), preferred_element_type=F32)
+            total = lax.dot_general(
+                jnp.concatenate(specs, axis=1),
+                jnp.concatenate(panels, axis=1),
+                (((1,), (1,)), ((), ())),
+                preferred_element_type=F32,
+            )
             real = total[:focal, :LANES] + total[focal:, LANES:]
             imag = total[focal:, :LANES] - total[:focal, LANES:]
             if has_base:
@@ -441,25 +460,25 @@
 
 
 def reduce_scatter(places, keep0, keep1, send0, send1):
+    size = places.line
     got1 = places.send(send1, places.core())
     got0 = places.send(send0, places.core())
     far = [add(keep, got).astype(BF16) for keep, got in zip(keep1, got1)]
-    beside = {}
-    if places.line > 1:
-        beside[1] = places.send(far[1], places.shift(1))
-    across = {step: places.send(far[step], places.pair()) for step in range(2, places.line)}
-    across[0] = places.send(add(keep1[0], got1[0], *beside.values()).astype(BF16), places.pair())
-    parts = [keep0[0], got0[0], across[0]]
-    first = []
-    for step in range(1, places.line):
-        terms = [keep0[step], got0[step]] + ([across[step]] if step in across else [])
-        ready = add(*terms).astype(BF16)
-        if step > 2:
-            ready = after(ready, *first)
-        parts.append(places.send(ready, places.shift(step)))
-        if step == 1:
-            first = [parts[-1]]
-    return parts
+    across = {step: places.send(far[step], places.pair()) for step in range(2, size)}
+    beside = [places.send(far[1], places.shift(1))] if size > 1 else []
+    parts = [keep0[0], got0[0]]
+
+    def pass_on(steps, shift):
+        carried = []
+        for step in steps:
+            terms = [keep0[step], got0[step], *([across[step]] if step in across else []), *carried]
+            carried = [places.send(add(*terms).astype(BF16), places.shift(shift))]
+        return carried
+
+    parts += pass_on(range(size // 2, 0, -1), 1)
+    parts += pass_on(range(size // 2 + 1, size), size - 1)
+    across[0] = places.send(add(keep1[0], got1[0], *beside).astype(BF16), places.pair())
+    return parts + [across[0]]
 
 
 def gather_chips(places, block, work=None):
@@ -480,8 +499,10 @@
         line[step] = places.send(block, places.shift(step))
     across = {0: places.send(block, places.pair())}
     own = run(0, [0], line)
-    for step in far:
-        line[step] = places.send(after(block, line[1], *own), places.shift(step))
+    for step in range(2, size // 2 + 1):
+        line[step] = places.send(after(line[step - 1], *own), places.shift(1))
+    for step in range(size - 2, size // 2, -1):
+        line[step] = places.send(after(line[step + 1], *own), places.shift(size - 1))
     for step in near:
         if step == 1:
             across[step] = places.send(across[0], places.shift(1))
@@ -534,7 +555,7 @@
     upgoing = field(upgoing_spec, other, own_inverse, onset_times, line)
 
     def before_far(piece, flip, step):
-        return upgoing if (flip, step) == (0, 0) else piece
+        return upgoing if (flip, step) == (1, 0) else piece
 
     own, _ = gather_chips(places, downgoing_spec, before_far)
     other = [swap_cores(places, side) for side in own]

time: 306 us -> 288 us (0.941)
  waiting for transfers between devices: 145 us -> 107 us
  starting transfers between devices: 60.1 us -> 73.2 us
  local copies, waits for them, and re-layouts: 7.74 us -> 14.8 us
    ppermute x80, waiting for transfers between devices: 145 us -> 107 us  [send(): return lax.ppermute(array, self.axis, pairs)]
    ppermute x80, starting transfers between devices: 60.1 us -> 73.2 us  [send(): return lax.ppermute(array, self.axis, pairs)]
    unnamed x20 -> x38, local copies, waits for them, and re-layouts: 6.12 us -> 13.2 us
  transfers between devices with their start and end apart: 80 -> 80, of which waited for: 28 -> 34; matrix products, arithmetic and copies ran while one was open for 2% -> 2% of each run, Pallas kernels for 15% -> 16%
where the time goes in v6:
time: 288 us
  waiting for transfers between devices  107 us (37%)
  Pallas kernels  86.3 us (30%)
  starting transfers between devices  73.2 us (25%)
  local copies, waits for them, and re-layouts  14.8 us (5%)
  other arithmetic  5.49 us (2%)
    ppermute x80, waiting for transfers between devices, send(): return lax.ppermute(array, self.axis, pairs)  107 us
    ppermute x80, starting transfers between devices, send(): return lax.ppermute(array, self.axis, pairs)  73.2 us
    pallas_call x4, Pallas kernels, correlate(): pl.pallas_call(functools.partial(correlate_kernel, line, flip, bool(more)...  30.8 us
    pallas_call x2, Pallas kernels, convolve(): pl.pallas_call(functools.partial(convolve_kernel, line), in_specs=[VMEM,...  23.4 us
    pallas_call x8, Pallas kernels, window_at(): pl.pallas_call(functools.partial(window_at_kernel, line, flip, step), in_...  18.6 us
    unnamed x38, local copies, waits for them, and re-layouts  13.2 us
    pallas_call x2, Pallas kernels, field(): pl.pallas_call(functools.partial(field_kernel, line, bool(plus)), in_spec...  6.41 us
  transfers between devices with their start and end apart: 80, of which 34 were waited for; matrix products, arithmetic and copies ran while one was open for 2% of the time, Pallas kernels for 16%

profile of v6, /device:TPU:0, one launch (start us, length us, event | category | flops | bytes accessed | tf_op | source)
XLA Modules:
  0.0 287.7 jit_solution(4427438978266950927)
XLA Ops:
  0.9 1.6 copy-done
  2.4 1.9 first_analysis.1
  4.9 2.2 collective-permute-done.1
  7.5 3.0 %collective-permute-start.2 = (bf16[16,64,128]{2,1,0:T(8,128)(2,1)S(1)}, bf16[16,64,128]{2,1,0:T(8,128)(2,1)S(1)}, u32[]{:S(2)}, u32[]{:S(2)}) collective-permute-start(bf16[16,64,128]{2,1,0:T(8,128)(2,1)S(1)} %get-tuple-element.56), channel_id=1, source_target_pairs={{0,2},{1,3},{2,0},{3,1},{4,6},{5,7},{6,4},{7,5},{8,10},{9,11},{10,... | collective-permute-start | bytes 786440 | tf_op jit(solution)/shard_map/ppermute | solution.py:50
  10.5 2.0 collective-permute-start.7
  12.5 5.0 %collective-permute-done.2 = bf16[16,64,128]{2,1,0:T(8,128)(2,1)S(1)} collective-permute-done((bf16[16,64,128]{2,1,0:T(8,128)(2,1)S(1)}, bf16[16,64,128]{2,1,0:T(8,128)(2,1)S(1)}, u32[]{:S(2)}, u32[]{:S(2)}) %collective-permute-start.2) | collective-permute-done | bytes 262176 | tf_op jit(solution)/shard_map/ppermute | solution.py:50
  17.6 2.2 collective-permute-start.3
  20.7 1.6 collective-permute-start.8
  22.9 4.0 %collective-permute-done.3 = bf16[16,64,128]{2,1,0:T(8,128)(2,1)S(1)} collective-permute-done((bf16[16,64,128]{2,1,0:T(8,128)(2,1)S(1)}, bf16[16,64,128]{2,1,0:T(8,128)(2,1)S(1)}, u32[]{:S(2)}, u32[]{:S(2)}) %collective-permute-start.3) | collective-permute-done | bytes 262176 | tf_op jit(solution)/shard_map/ppermute | solution.py:50
  27.2 3.8 %collective-permute-start.6 = (bf16[16,64,128]{2,1,0:T(8,128)(2,1)S(1)}, bf16[16,64,128]{2,1,0:T(8,128)(2,1)S(1)}, u32[]{:S(2)}, u32[]{:S(2)}) collective-permute-start(bf16[16,64,128]{2,1,0:T(8,128)(2,1)S(1)} %get-tuple-element.55), channel_id=1, source_target_pairs={{0,12},{1,13},{2,14},{3,15},{4,0},{5,1},{6,2},{7,3},{8,4},{9,5},{1... | collective-permute-start | bytes 786440 | tf_op jit(solution)/shard_map/ppermute | solution.py:50
  31.0 7.0 %collective-permute-done.4 = bf16[16,64,128]{2,1,0:T(8,128)(2,1)S(1)} collective-permute-done((bf16[16,64,128]{2,1,0:T(8,128)(2,1)S(1)}, bf16[16,64,128]{2,1,0:T(8,128)(2,1)S(1)}, u32[]{:S(2)}, u32[]{:S(2)}) %collective-permute-start.4) | collective-permute-done | bytes 262176 | tf_op jit(solution)/shard_map/ppermute | solution.py:50
  39.4 11.7 %convolve.2 = (bf16[4,32,2,16,128]{4,3,2,1,0:T(8,128)(2,1)S(1)}, bf16[4,32,2,16,128]{4,3,2,1,0:T(8,128)(2,1)S(1)}, bf16[4,32,2,16,128]{4,3,2,1,0:T(8,128)(2,1)S(1)}, bf16[4,32,2,16,128]{4,3,2,1,0:T(8,128)(2,1)S(1)}) custom-call(bf16[32,2,16,128]{3,2,1,0:T(8,128)(2,1)S(1)} %bitcast.91, bf16[2,32,128,2048]{3,2,1,0:T(8,128)(2,1)} %refs_8_.7), custom_call_target="tpu_custom_call" | custom-call | flops 1073741824 | bytes 37748736 | tf_op jit(solution)/shard_map/convolve/pallas_call | solution.py:222
  51.6 2.1 collective-permute-done.10
  57.1 6.1 %collective-permute-done.11 = bf16[32,2,16,128]{3,2,1,0:T(8,128)(2,1)S(1)} collective-permute-done((bf16[32,2,16,128]{3,2,1,0:T(8,128)(2,1)S(1)}, bf16[32,2,16,128]{3,2,1,0:T(8,128)(2,1)S(1)}, u32[]{:S(2)}, u32[]{:S(2)}) %collective-permute-start.11) | collective-permute-done | bytes 262176 | tf_op jit(solution)/shard_map/ppermute | solution.py:50
  63.2 4.8 %collective-permute-done.14 = bf16[32,2,16,128]{3,2,1,0:T(8,128)(2,1)S(1)} collective-permute-done((bf16[32,2,16,128]{3,2,1,0:T(8,128)(2,1)S(1)}, bf16[32,2,16,128]{3,2,1,0:T(8,128)(2,1)S(1)}, u32[]{:S(2)}, u32[]{:S(2)}) %collective-permute-start.14) | collective-permute-done | bytes 262176 | tf_op jit(solution)/shard_map/ppermute | solution.py:50
  71.0 1.5 collective-permute-start.17
  72.5 3.0 %collective-permute-start.15 = (bf16[32,2,16,128]{3,2,1,0:T(8,128)(2,1)S(1)}, bf16[32,2,16,128]{3,2,1,0:T(8,128)(2,1)S(1)}, u32[]{:S(2)}, u32[]{:S(2)}) collective-permute-start(bf16[32,2,16,128]{3,2,1,0:T(8,128)(2,1)S(1)} %get-tuple-element.52), channel_id=1, source_target_pairs={{0,12},{1,13},{2,14},{3,15},{4,0},{5,1},{6,2},{7,3},{8,4},{9,5},{1... | collective-permute-start | bytes 786440 | tf_op jit(solution)/shard_map/ppermute | solution.py:50
  75.5 4.8 %collective-permute-done.12 = bf16[32,2,16,128]{3,2,1,0:T(8,128)(2,1)} collective-permute-done((bf16[32,2,16,128]{3,2,1,0:T(8,128)(2,1)}, bf16[32,2,16,128]{3,2,1,0:T(8,128)(2,1)}, u32[]{:S(2)}, u32[]{:S(2)}) %collective-permute-start.12) | collective-permute-done | bytes 262176 | tf_op jit(solution)/shard_map/ppermute | solution.py:50
  81.4 2.4 collective-permute-start.13
  85.6 4.1 %collective-permute-done.13.refs_5_ = bf16[32,2,16,128]{3,2,1,0:T(8,128)(2,1)S(1)} collective-permute-done((bf16[32,2,16,128]{3,2,1,0:T(8,128)(2,1)S(1)}, bf16[32,2,16,128]{3,2,1,0:T(8,128)(2,1)S(1)}, u32[]{:S(2)}, u32[]{:S(2)}) %collective-permute-start.13) | collective-permute-done | bytes 262176 | tf_op jit(solution)/shard_map/ppermute | solution.py:50
  89.7 2.5 window.3.refs_0_
  93.4 2.6 collective-permute-start.23
  96.1 7.3 %collective-permute-done.20.refs_1_ = bf16[32,2,16,128]{3,2,1,0:T(8,128)(2,1)S(1)} collective-permute-done((bf16[32,2,16,128]{3,2,1,0:T(8,128)(2,1)S(1)}, bf16[32,2,16,128]{3,2,1,0:T(8,128)(2,1)S(1)}, u32[]{:S(2)}, u32[]{:S(2)}) %collective-permute-start.20) | collective-permute-done | bytes 262176 | tf_op jit(solution)/shard_map/ppermute | solution.py:50
  106.4 5.1 %collective-permute-done.21.refs_2_ = bf16[32,2,16,128]{3,2,1,0:T(8,128)(2,1)S(1)} collective-permute-done((bf16[32,2,16,128]{3,2,1,0:T(8,128)(2,1)S(1)}, bf16[32,2,16,128]{3,2,1,0:T(8,128)(2,1)S(1)}, u32[]{:S(2)}, u32[]{:S(2)}) %collective-permute-start.21) | collective-permute-done | bytes 262176 | tf_op jit(solution)/shard_map/ppermute | solution.py:50
  112.8 3.5 %collective-permute-start.19 = (bf16[32,2,16,128]{3,2,1,0:T(8,128)(2,1)S(1)}, bf16[32,2,16,128]{3,2,1,0:T(8,128)(2,1)S(1)}, u32[]{:S(2)}, u32[]{:S(2)}) collective-permute-start(bf16[32,2,16,128]{3,2,1,0:T(8,128)(2,1)S(1)} %collective-permute-done.18.refs_0_), channel_id=1, source_target_pairs={{0,4},{1,5},{2,6},{3,7},{4,8},{5,9},{6,10},{7,11},{8,12},{9,13},{1... | collective-permute-start | bytes 786440 | tf_op jit(solution)/shard_map/ppermute | solution.py:50
  116.7 7.6 %correlate0.2.refs_9_ = f32[32,2,16,128]{3,2,1,0:T(8,128)S(1)} custom-call(bf16[32,2,16,128]{3,2,1,0:T(8,128)(2,1)S(1)} %window.3.refs_0_, bf16[32,2,16,128]{3,2,1,0:T(8,128)(2,1)S(1)} %collective-permute-done.20.refs_1_, bf16[32,2,16,128]{3,2,1,0:T(8,128)(2,1)S(1)} %collective-permute-done.21.refs_2_, ...), custom_call_target="tpu_custom_call" | custom-call | flops 536870912 | bytes 18874368 | tf_op jit(solution)/shard_map/correlate0/pallas_call | solution.py:289
  126.4 7.7 %correlate1.2.refs_3_ = f32[32,2,16,128]{3,2,1,0:T(8,128)S(1)} custom-call(bf16[32,2,16,128]{3,2,1,0:T(8,128)(2,1)S(1)} %collective-permute-done.18.refs_0_, bf16[32,2,16,128]{3,2,1,0:T(8,128)(2,1)S(1)} %collective-permute-done.19.refs_1_, bf16[32,2,16,128]{3,2,1,0:T(8,128)(2,1)S(1)} %collective-permute-done.22.refs_2_, ...), custom_call_target="tpu_custom_call" | custom-call | flops 536870912 | bytes 18874368 | tf_op jit(solution)/shard_map/correlate1/pallas_call | solution.py:289
  134.0 2.3 window.4.spec_ref
  136.4 11.7 %convolve.3 = (bf16[4,32,2,16,128]{4,3,2,1,0:T(8,128)(2,1)S(1)}, bf16[4,32,2,16,128]{4,3,2,1,0:T(8,128)(2,1)S(1)}, bf16[4,32,2,16,128]{4,3,2,1,0:T(8,128)(2,1)S(1)}, bf16[4,32,2,16,128]{4,3,2,1,0:T(8,128)(2,1)S(1)}) custom-call(bf16[32,2,16,128]{3,2,1,0:T(8,128)(2,1)S(1)} %window.4.spec_ref, bf16[2,32,128,2048]{3,2,1,0:T(8,128)(2,1)} %refs_8_.7), custom_call_target="tpu_custom_call" | custom-call | flops 1073741824 | bytes 37748736 | tf_op jit(solution)/shard_map/convolve/pallas_call | solution.py:222
  148.7 2.1 collective-permute-done.34
  151.7 1.4 collective-permute-start.38
  153.1 3.3 %collective-permute-start.40 = (bf16[32,2,16,128]{3,2,1,0:T(8,128)(2,1)S(1)}, bf16[32,2,16,128]{3,2,1,0:T(8,128)(2,1)S(1)}, u32[]{:S(2)}, u32[]{:S(2)}) collective-permute-start(bf16[32,2,16,128]{3,2,1,0:T(8,128)(2,1)S(1)} %get-tuple-element.44), channel_id=1, source_target_pairs={{0,4},{1,5},{2,6},{3,7},{4,8},{5,9},{6,10},{7,11},{8,12},{9,13},{1... | collective-permute-start | bytes 786440 | tf_op jit(solution)/shard_map/ppermute | solution.py:50
  156.4 3.8 %collective-permute-done.35 = bf16[32,2,16,128]{3,2,1,0:T(8,128)(2,1)S(1)} collective-permute-done((bf16[32,2,16,128]{3,2,1,0:T(8,128)(2,1)S(1)}, bf16[32,2,16,128]{3,2,1,0:T(8,128)(2,1)S(1)}, u32[]{:S(2)}, u32[]{:S(2)}) %collective-permute-start.35) | collective-permute-done | bytes 262176 | tf_op jit(solution)/shard_map/ppermute | solution.py:50
  160.2 4.8 %collective-permute-done.38 = bf16[32,2,16,128]{3,2,1,0:T(8,128)(2,1)S(1)} collective-permute-done((bf16[32,2,16,128]{3,2,1,0:T(8,128)(2,1)S(1)}, bf16[32,2,16,128]{3,2,1,0:T(8,128)(2,1)S(1)}, u32[]{:S(2)}, u32[]{:S(2)}) %collective-permute-start.38) | collective-permute-done | bytes 262176 | tf_op jit(solution)/shard_map/ppermute | solution.py:50
  165.3 3.8 %collective-permute-start.36 = (bf16[32,2,16,128]{3,2,1,0:T(8,128)(2,1)S(1)}, bf16[32,2,16,128]{3,2,1,0:T(8,128)(2,1)S(1)}, u32[]{:S(2)}, u32[]{:S(2)}) collective-permute-start(bf16[32,2,16,128]{3,2,1,0:T(8,128)(2,1)S(1)} %get-tuple-element.48), channel_id=1, source_target_pairs={{0,4},{1,5},{2,6},{3,7},{4,8},{5,9},{6,10},{7,11},{8,12},{9,13},{1... | collective-permute-start | bytes 786440 | tf_op jit(solution)/shard_map/ppermute | solution.py:50
  169.2 1.8 collective-permute-start.41
  171.5 5.8 %collective-permute-done.36 = bf16[32,2,16,128]{3,2,1,0:T(8,128)(2,1)S(1)} collective-permute-done((bf16[32,2,16,128]{3,2,1,0:T(8,128)(2,1)S(1)}, bf16[32,2,16,128]{3,2,1,0:T(8,128)(2,1)S(1)}, u32[]{:S(2)}, u32[]{:S(2)}) %collective-permute-start.36) | collective-permute-done | bytes 262176 | tf_op jit(solution)/shard_map/ppermute | solution.py:50
  178.5 4.4 %collective-permute-done.39.refs_6_ = bf16[32,2,16,128]{3,2,1,0:T(8,128)(2,1)S(1)} collective-permute-done((bf16[32,2,16,128]{3,2,1,0:T(8,128)(2,1)S(1)}, bf16[32,2,16,128]{3,2,1,0:T(8,128)(2,1)S(1)}, u32[]{:S(2)}, u32[]{:S(2)}) %collective-permute-start.39) | collective-permute-done | bytes 262176 | tf_op jit(solution)/shard_map/ppermute | solution.py:50
  182.8 4.5 %collective-permute-done.37.refs_5_ = bf16[32,2,16,128]{3,2,1,0:T(8,128)(2,1)S(1)} collective-permute-done((bf16[32,2,16,128]{3,2,1,0:T(8,128)(2,1)S(1)}, bf16[32,2,16,128]{3,2,1,0:T(8,128)(2,1)S(1)}, u32[]{:S(2)}, u32[]{:S(2)}) %collective-permute-start.37) | collective-permute-done | bytes 262176 | tf_op jit(solution)/shard_map/ppermute | solution.py:50
  188.8 1.5 collective-permute-start.45
  190.3 2.6 collective-permute-start.44
  192.9 2.3 window_at.8.refs_0_
  195.2 3.8 %collective-permute-done.42.spec_ref.refs_1_ = bf16[16,64,128]{2,1,0:T(8,128)(2,1)S(1)} collective-permute-done((bf16[16,64,128]{2,1,0:T(8,128)(2,1)S(1)}, bf16[16,64,128]{2,1,0:T(8,128)(2,1)S(1)}, u32[]{:S(2)}, u32[]{:S(2)}) %collective-permute-start.42) | collective-permute-done | bytes 262176 | tf_op jit(solution)/shard_map/ppermute | solution.py:50
  199.0 1.4 collective-permute-start.43
  200.4 3.0 %collective-permute-start.46 = (bf16[16,64,128]{2,1,0:T(8,128)(2,1)S(1)}, bf16[16,64,128]{2,1,0:T(8,128)(2,1)S(1)}, u32[]{:S(2)}, u32[]{:S(2)}) collective-permute-start(bf16[16,64,128]{2,1,0:T(8,128)(2,1)S(1)} %collective-permute-done.45.spec_ref.refs_4_), channel_id=1, source_target_pairs={{0,4},{1,5},{2,6},{3,7},{4,8},{5,9},{6,10},{7,11},{8,12},{9,13},{1... | collective-permute-start | bytes 786440 | tf_op jit(solution)/shard_map/ppermute | solution.py:50
  205.1 2.3 window_at.10.refs_1_
  207.5 2.3 window_at.11.refs_3_
  209.8 2.3 window_at.9.refs_0_
  213.2 2.3 window_at.13.refs_2_
  216.7 2.3 window_at.14.refs_3_
  219.3 2.3 window_at.12.refs_1_
  221.7 7.7 %correlate0.3.refs_9_ = f32[32,2,16,128]{3,2,1,0:T(8,128)S(1)} custom-call(bf16[32,2,16,128]{3,2,1,0:T(8,128)(2,1)S(1)} %window_at.8.refs_0_, bf16[32,2,16,128]{3,2,1,0:T(8,128)(2,1)S(1)} %window_at.10.refs_1_, bf16[32,2,16,128]{3,2,1,0:T(8,128)(2,1)S(1)} %window_at.13.refs_2_, bf16[32,2,16,128]{3,2,1,0:T(8,128)(2,1)S(1)} %window_at.11.refs_3_, ...), custom_call_target="tpu_custom_call" | custom-call | flops 536870912 | bytes 18874368 | tf_op jit(solution)/shard_map/correlate0/pallas_call | solution.py:289
  229.4 2.3 window_at.15.refs_2_
  233.8 7.8 %correlate1.3.refs_0_ = bf16[16,64,128]{2,1,0:T(8,128)(2,1)S(1)} custom-call(bf16[32,2,16,128]{3,2,1,0:T(8,128)(2,1)S(1)} %window_at.9.refs_0_, bf16[32,2,16,128]{3,2,1,0:T(8,128)(2,1)S(1)} %window_at.12.refs_1_, bf16[32,2,16,128]{3,2,1,0:T(8,128)(2,1)S(1)} %window_at.15.refs_2_, bf16[32,2,16,128]{3,2,1,0:T(8,128)(2,1)S(1)} %window_at.14.refs_3_, ...), custom_call_target="tpu_custom_call" | custom-call | flops 536870912 | bytes 18874368 | tf_op jit(solution)/shard_map/correlate1/pallas_call | solution.py:289
  241.6 1.7 collective-permute-start.65
  246.5 5.6 %collective-permute-done.65.refs_1_ = bf16[16,64,128]{2,1,0:T(8,128)(2,1)S(1)} collective-permute-done((bf16[16,64,128]{2,1,0:T(8,128)(2,1)S(1)}, bf16[16,64,128]{2,1,0:T(8,128)(2,1)S(1)}, u32[]{:S(2)}, u32[]{:S(2)}) %collective-permute-start.65) | collective-permute-done | bytes 262176 | tf_op jit(solution)/shard_map/ppermute | solution.py:50
  252.8 1.3 collective-permute-start.68
  255.5 2.0 collective-permute-start.66
  265.0 3.1 %field.2 = bf16[16,32,2048]{2,1,0:T(8,128)(2,1)} custom-call(bf16[32,64]{1,0:T(8,128)(2,1)S(1)} %bitcast.104, s32[16,2048]{1,0:T(8,128)S(1)} %copy-done.2, bf16[16,64,128]{2,1,0:T(8,128)(2,1)S(1)} %window.5.spec_ref.refs_0_, bf16[16,64,128]{2,1,0:T(8,128)(2,1)S(1)} %collective-permute-done.42.spec_ref.refs_1_, ...), custom_call_target="tpu_custom_call" | custom-call | flops 134217728 | bytes 8388608 | tf_op jit(solution)/shard_map/field/pallas_call | solution.py:435
  269.6 1.3 collective-permute-start.70
  271.0 7.8 %collective-permute-done.69.refs_5_ = bf16[16,64,128]{2,1,0:T(8,128)(2,1)S(1)} collective-permute-done((bf16[16,64,128]{2,1,0:T(8,128)(2,1)S(1)}, bf16[16,64,128]{2,1,0:T(8,128)(2,1)S(1)}, u32[]{:S(2)}, u32[]{:S(2)}) %collective-permute-start.69) | collective-permute-done | bytes 262176 | tf_op jit(solution)/shard_map/ppermute | solution.py:50
  279.8 2.9 collective-permute-done.70.refs_6_
  282.7 1.5 collective-permute-done.78.refs_14_
  284.2 3.3 %field.3 = bf16[16,32,2048]{2,1,0:T(8,128)(2,1)} custom-call(bf16[32,64]{1,0:T(8,128)(2,1)S(1)} %bitcast.105, s32[16,2048]{1,0:T(8,128)S(1)} %copy-done.2, bf16[16,64,128]{2,1,0:T(8,128)(2,1)S(1)} %correlate1.3.refs_0_, bf16[16,64,128]{2,1,0:T(8,128)(2,1)S(1)} %collective-permute-done.65.refs_1_, bf16[16,64,128]{2,1,0:T(8,128)(2,1)} %collective-permute-done.66.refs_2_, ...), custom_call_target="tpu_custom_call" | custom-call | flops 134217728 | bytes 8388608 | tf_op jit(solution)/shard_map/field/pallas_call | solution.py:435
  (185 shorter events, 48.9 us)
Async XLA Ops:
  4.9 7.7 %collective-permute-start = (bf16[4,16,64,128]{3,2,1,0:T(8,128)(2,1)S(1)}, bf16[4,16,64,128]{3,2,1,0:T(8,128)(2,1)S(1)}, u32[]{:S(2)}, u32[]{:S(2)}) collective-permute-start(bf16[4,16,64,128]{3,2,1,0:T(8,128)(2,1)S(1)} %get-tuple-element.24), channel_id=1, source_target_pairs={{0,1},{1,0},{2,3},{3,2},{4,5},{5,4},{6,7},{7,6},{8,9},{9,8},{10,11... | collective-permute-start | bytes 3145736 | tf_op jit(solution)/shard_map/ppermute | solution.py:50
  7.5 10.0 %collective-permute-start.2 = (bf16[16,64,128]{2,1,0:T(8,128)(2,1)S(1)}, bf16[16,64,128]{2,1,0:T(8,128)(2,1)S(1)}, u32[]{:S(2)}, u32[]{:S(2)}) collective-permute-start(bf16[16,64,128]{2,1,0:T(8,128)(2,1)S(1)} %get-tuple-element.56), channel_id=1, source_target_pairs={{0,2},{1,3},{2,0},{3,1},{4,6},{5,7},{6,4},{7,5},{8,10},{9,11},{10,... | collective-permute-start | bytes 786440 | tf_op jit(solution)/shard_map/ppermute | solution.py:50
  10.4 12.5 %collective-permute-start.5 = (bf16[16,64,128]{2,1,0:T(8,128)(2,1)S(1)}, bf16[16,64,128]{2,1,0:T(8,128)(2,1)S(1)}, u32[]{:S(2)}, u32[]{:S(2)}) collective-permute-start(bf16[16,64,128]{2,1,0:T(8,128)(2,1)S(1)} %get-tuple-element.58), channel_id=1, source_target_pairs={{0,2},{1,3},{2,0},{3,1},{4,6},{5,7},{6,4},{7,5},{8,10},{9,11},{10,... | collective-permute-start | bytes 786440 | tf_op jit(solution)/shard_map/ppermute | solution.py:50
  10.5 10.1 %collective-permute-start.7 = (bf16[16,64,128]{2,1,0:T(8,128)(2,1)S(1)}, bf16[16,64,128]{2,1,0:T(8,128)(2,1)S(1)}, u32[]{:S(2)}, u32[]{:S(2)}) collective-permute-start(bf16[16,64,128]{2,1,0:T(8,128)(2,1)S(1)} %get-tuple-element.57), channel_id=1, source_target_pairs={{0,4},{1,5},{2,6},{3,7},{4,8},{5,9},{6,10},{7,11},{8,12},{9,13},{1... | collective-permute-start | bytes 786440 | tf_op jit(solution)/shard_map/ppermute | solution.py:50
  17.6 9.2 %collective-permute-start.3 = (bf16[16,64,128]{2,1,0:T(8,128)(2,1)S(1)}, bf16[16,64,128]{2,1,0:T(8,128)(2,1)S(1)}, u32[]{:S(2)}, u32[]{:S(2)}) collective-permute-start(bf16[16,64,128]{2,1,0:T(8,128)(2,1)S(1)} %fusion.10), channel_id=1, source_target_pairs={{0,4},{1,5},{2,6},{3,7},{4,8},{5,9},{6,10},{7,11},{8,12},{9,13},{1... | collective-permute-start | bytes 786440 | tf_op jit(solution)/shard_map/ppermute | solution.py:50
  20.7 10.3 %collective-permute-start.8 = (bf16[16,64,128]{2,1,0:T(8,128)(2,1)S(1)}, bf16[16,64,128]{2,1,0:T(8,128)(2,1)S(1)}, u32[]{:S(2)}, u32[]{:S(2)}) collective-permute-start(bf16[16,64,128]{2,1,0:T(8,128)(2,1)S(1)} %fusion.8), channel_id=1, source_target_pairs={{0,2},{1,3},{2,0},{3,1},{4,6},{5,7},{6,4},{7,5},{8,10},{9,11},{10,... | collective-permute-start | bytes 786440 | tf_op jit(solution)/shard_map/ppermute | solution.py:50
  27.1 10.8 %collective-permute-start.4 = (bf16[16,64,128]{2,1,0:T(8,128)(2,1)S(1)}, bf16[16,64,128]{2,1,0:T(8,128)(2,1)S(1)}, u32[]{:S(2)}, u32[]{:S(2)}) collective-permute-start(bf16[16,64,128]{2,1,0:T(8,128)(2,1)S(1)} %get-tuple-element.54), channel_id=1, source_target_pairs={{0,4},{1,5},{2,6},{3,7},{4,8},{5,9},{6,10},{7,11},{8,12},{9,13},{1... | collective-permute-start | bytes 786440 | tf_op jit(solution)/shard_map/ppermute | solution.py:50
  27.2 11.8 %collective-permute-start.6 = (bf16[16,64,128]{2,1,0:T(8,128)(2,1)S(1)}, bf16[16,64,128]{2,1,0:T(8,128)(2,1)S(1)}, u32[]{:S(2)}, u32[]{:S(2)}) collective-permute-start(bf16[16,64,128]{2,1,0:T(8,128)(2,1)S(1)} %get-tuple-element.55), channel_id=1, source_target_pairs={{0,12},{1,13},{2,14},{3,15},{4,0},{5,1},{6,2},{7,3},{8,4},{9,5},{1... | collective-permute-start | bytes 786440 | tf_op jit(solution)/shard_map/ppermute | solution.py:50
  54.0 9.2 %collective-permute-start.11 = (bf16[32,2,16,128]{3,2,1,0:T(8,128)(2,1)S(1)}, bf16[32,2,16,128]{3,2,1,0:T(8,128)(2,1)S(1)}, u32[]{:S(2)}, u32[]{:S(2)}) collective-permute-start(bf16[32,2,16,128]{3,2,1,0:T(8,128)(2,1)S(1)} %get-tuple-element.51), channel_id=1, source_target_pairs={{0,2},{1,3},{2,0},{3,1},{4,6},{5,7},{6,4},{7,5},{8,10},{9,11},{10,... | collective-permute-start | bytes 786440 | tf_op jit(solution)/shard_map/ppermute | solution.py:50
  55.3 12.8 %collective-permute-start.14 = (bf16[32,2,16,128]{3,2,1,0:T(8,128)(2,1)S(1)}, bf16[32,2,16,128]{3,2,1,0:T(8,128)(2,1)S(1)}, u32[]{:S(2)}, u32[]{:S(2)}) collective-permute-start(bf16[32,2,16,128]{3,2,1,0:T(8,128)(2,1)S(1)} %get-tuple-element.50), channel_id=1, source_target_pairs={{0,2},{1,3},{2,0},{3,1},{4,6},{5,7},{6,4},{7,5},{8,10},{9,11},{10,... | collective-permute-start | bytes 786440 | tf_op jit(solution)/shard_map/ppermute | solution.py:50
  56.4 13.5 %collective-permute-start.16 = (bf16[32,2,16,128]{3,2,1,0:T(8,128)(2,1)S(1)}, bf16[32,2,16,128]{3,2,1,0:T(8,128)(2,1)S(1)}, u32[]{:S(2)}, u32[]{:S(2)}) collective-permute-start(bf16[32,2,16,128]{3,2,1,0:T(8,128)(2,1)S(1)} %get-tuple-element.49), channel_id=1, source_target_pairs={{0,4},{1,5},{2,6},{3,7},{4,8},{5,9},{6,10},{7,11},{8,12},{9,13},{1... | collective-permute-start | bytes 786440 | tf_op jit(solution)/shard_map/ppermute | solution.py:50
  68.9 11.4 %collective-permute-start.12 = (bf16[32,2,16,128]{3,2,1,0:T(8,128)(2,1)}, bf16[32,2,16,128]{3,2,1,0:T(8,128)(2,1)}, u32[]{:S(2)}, u32[]{:S(2)}) collective-permute-start(bf16[32,2,16,128]{3,2,1,0:T(8,128)(2,1)} %get-tuple-element.53), channel_id=1, source_target_pairs={{0,4},{1,5},{2,6},{3,7},{4,8},{5,9},{6,10},{7,11},{8,12},{9,13},{1... | collective-permute-start | bytes 786440 | tf_op jit(solution)/shard_map/ppermute | solution.py:50
  71.0 13.8 %collective-permute-start.17 = (bf16[32,2,16,128]{3,2,1,0:T(8,128)(2,1)S(1)}, bf16[32,2,16,128]{3,2,1,0:T(8,128)(2,1)S(1)}, u32[]{:S(2)}, u32[]{:S(2)}) collective-permute-start(bf16[32,2,16,128]{3,2,1,0:T(8,128)(2,1)S(1)} %fusion.4), channel_id=1, source_target_pairs={{0,2},{1,3},{2,0},{3,1},{4,6},{5,7},{6,4},{7,5},{8,10},{9,11},{10,... | collective-permute-start | bytes 786440 | tf_op jit(solution)/shard_map/ppermute | solution.py:50
  72.5 13.1 %collective-permute-start.15 = (bf16[32,2,16,128]{3,2,1,0:T(8,128)(2,1)S(1)}, bf16[32,2,16,128]{3,2,1,0:T(8,128)(2,1)S(1)}, u32[]{:S(2)}, u32[]{:S(2)}) collective-permute-start(bf16[32,2,16,128]{3,2,1,0:T(8,128)(2,1)S(1)} %get-tuple-element.52), channel_id=1, source_target_pairs={{0,12},{1,13},{2,14},{3,15},{4,0},{5,1},{6,2},{7,3},{8,4},{9,5},{1... | collective-permute-start | bytes 786440 | tf_op jit(solution)/shard_map/ppermute | solution.py:50
  81.4 8.3 %collective-permute-start.13 = (bf16[32,2,16,128]{3,2,1,0:T(8,128)(2,1)S(1)}, bf16[32,2,16,128]{3,2,1,0:T(8,128)(2,1)S(1)}, u32[]{:S(2)}, u32[]{:S(2)}) collective-permute-start(bf16[32,2,16,128]{3,2,1,0:T(8,128)(2,1)S(1)} %fusion.7), channel_id=1, source_target_pairs={{0,4},{1,5},{2,6},{3,7},{4,8},{5,9},{6,10},{7,11},{8,12},{9,13},{1... | collective-permute-start | bytes 786440 | tf_op jit(solution)/shard_map/ppermute | solution.py:50
  92.2 11.2 %collective-permute-start.20 = (bf16[32,2,16,128]{3,2,1,0:T(8,128)(2,1)S(1)}, bf16[32,2,16,128]{3,2,1,0:T(8,128)(2,1)S(1)}, u32[]{:S(2)}, u32[]{:S(2)}) collective-permute-start(bf16[32,2,16,128]{3,2,1,0:T(8,128)(2,1)S(1)} %window.3.refs_0_), channel_id=1, source_target_pairs={{0,4},{1,5},{2,6},{3,7},{4,8},{5,9},{6,10},{7,11},{8,12},{9,13},{1... | collective-permute-start | bytes 786440 | tf_op jit(solution)/shard_map/ppermute | solution.py:50
  93.4 11.8 %collective-permute-start.23 = (bf16[32,2,16,128]{3,2,1,0:T(8,128)(2,1)S(1)}, bf16[32,2,16,128]{3,2,1,0:T(8,128)(2,1)S(1)}, u32[]{:S(2)}, u32[]{:S(2)}) collective-permute-start(bf16[32,2,16,128]{3,2,1,0:T(8,128)(2,1)S(1)} %window.3.refs_0_), channel_id=1, source_target_pairs={{0,12},{1,13},{2,14},{3,15},{4,0},{5,1},{6,2},{7,3},{8,4},{9,5},{1... | collective-permute-start | bytes 786440 | tf_op jit(solution)/shard_map/ppermute | solution.py:50
  96.0 9.2 %collective-permute-start.26 = (bf16[32,2,16,128]{3,2,1,0:T(8,128)(2,1)S(1)}, bf16[32,2,16,128]{3,2,1,0:T(8,128)(2,1)S(1)}, u32[]{:S(2)}, u32[]{:S(2)}) collective-permute-start(bf16[32,2,16,128]{3,2,1,0:T(8,128)(2,1)S(1)} %window.3.refs_0_), channel_id=1, source_target_pairs={{0,1},{1,0},{2,3},{3,2},{4,5},{5,4},{6,7},{7,6},{8,9},{9,8},{10,11... | collective-permute-start | bytes 786440 | tf_op jit(solution)/shard_map/ppermute | solution.py:50
  103.3 8.2 %collective-permute-start.21 = (bf16[32,2,16,128]{3,2,1,0:T(8,128)(2,1)S(1)}, bf16[32,2,16,128]{3,2,1,0:T(8,128)(2,1)S(1)}, u32[]{:S(2)}, u32[]{:S(2)}) collective-permute-start(bf16[32,2,16,128]{3,2,1,0:T(8,128)(2,1)S(1)} %collective-permute-done.20.refs_1_), channel_id=1, source_target_pairs={{0,4},{1,5},{2,6},{3,7},{4,8},{5,9},{6,10},{7,11},{8,12},{9,13},{1... | collective-permute-start | bytes 786440 | tf_op jit(solution)/shard_map/ppermute | solution.py:50
  103.3 8.2 %collective-permute-start.18 = (bf16[32,2,16,128]{3,2,1,0:T(8,128)(2,1)S(1)}, bf16[32,2,16,128]{3,2,1,0:T(8,128)(2,1)S(1)}, u32[]{:S(2)}, u32[]{:S(2)}) collective-permute-start(bf16[32,2,16,128]{3,2,1,0:T(8,128)(2,1)S(1)} %window.3.refs_0_), channel_id=1, source_target_pairs={{0,2},{1,3},{2,0},{3,1},{4,6},{5,7},{6,4},{7,5},{8,10},{9,11},{10,... | collective-permute-start | bytes 786440 | tf_op jit(solution)/shard_map/ppermute | solution.py:50
  104.6 8.2 %collective-permute-start.27 = (bf16[32,2,16,128]{3,2,1,0:T(8,128)(2,1)S(1)}, bf16[32,2,16,128]{3,2,1,0:T(8,128)(2,1)S(1)}, u32[]{:S(2)}, u32[]{:S(2)}) collective-permute-start(bf16[32,2,16,128]{3,2,1,0:T(8,128)(2,1)S(1)} %collective-permute-done.20.refs_1_), channel_id=1, source_target_pairs={{0,1},{1,0},{2,3},{3,2},{4,5},{5,4},{6,7},{7,6},{8,9},{9,8},{10,11... | collective-permute-start | bytes 786440 | tf_op jit(solution)/shard_map/ppermute | solution.py:50
  105.2 11.0 %collective-permute-start.29 = (bf16[32,2,16,128]{3,2,1,0:T(8,128)(2,1)S(1)}, bf16[32,2,16,128]{3,2,1,0:T(8,128)(2,1)S(1)}, u32[]{:S(2)}, u32[]{:S(2)}) collective-permute-start(bf16[32,2,16,128]{3,2,1,0:T(8,128)(2,1)S(1)} %collective-permute-done.23.refs_3_), channel_id=1, source_target_pairs={{0,1},{1,0},{2,3},{3,2},{4,5},{5,4},{6,7},{7,6},{8,9},{9,8},{10,11... | collective-permute-start | bytes 786440 | tf_op jit(solution)/shard_map/ppermute | solution.py:50
  105.2 11.0 %collective-permute-start.24 = (bf16[32,2,16,128]{3,2,1,0:T(8,128)(2,1)S(1)}, bf16[32,2,16,128]{3,2,1,0:T(8,128)(2,1)S(1)}, u32[]{:S(2)}, u32[]{:S(2)}) collective-permute-start(bf16[32,2,16,128]{3,2,1,0:T(8,128)(2,1)S(1)} %collective-permute-done.23.refs_3_), channel_id=1, source_target_pairs={{0,2},{1,3},{2,0},{3,1},{4,6},{5,7},{6,4},{7,5},{8,10},{9,11},{10,... | collective-permute-start | bytes 786440 | tf_op jit(solution)/shard_map/ppermute | solution.py:50
  111.5 12.9 %collective-permute-start.22 = (bf16[32,2,16,128]{3,2,1,0:T(8,128)(2,1)S(1)}, bf16[32,2,16,128]{3,2,1,0:T(8,128)(2,1)S(1)}, u32[]{:S(2)}, u32[]{:S(2)}) collective-permute-start(bf16[32,2,16,128]{3,2,1,0:T(8,128)(2,1)S(1)} %collective-permute-done.21.refs_2_), channel_id=1, source_target_pairs={{0,2},{1,3},{2,0},{3,1},{4,6},{5,7},{6,4},{7,5},{8,10},{9,11},{10,... | collective-permute-start | bytes 786440 | tf_op jit(solution)/shard_map/ppermute | solution.py:50
  112.8 11.8 %collective-permute-start.19 = (bf16[32,2,16,128]{3,2,1,0:T(8,128)(2,1)S(1)}, bf16[32,2,16,128]{3,2,1,0:T(8,128)(2,1)S(1)}, u32[]{:S(2)}, u32[]{:S(2)}) collective-permute-start(bf16[32,2,16,128]{3,2,1,0:T(8,128)(2,1)S(1)} %collective-permute-done.18.refs_0_), channel_id=1, source_target_pairs={{0,4},{1,5},{2,6},{3,7},{4,8},{5,9},{6,10},{7,11},{8,12},{9,13},{1... | collective-permute-start | bytes 786440 | tf_op jit(solution)/shard_map/ppermute | solution.py:50
  116.2 8.8 %collective-permute-start.25 = (bf16[32,2,16,128]{3,2,1,0:T(8,128)(2,1)S(1)}, bf16[32,2,16,128]{3,2,1,0:T(8,128)(2,1)S(1)}, u32[]{:S(2)}, u32[]{:S(2)}) collective-permute-start(bf16[32,2,16,128]{3,2,1,0:T(8,128)(2,1)S(1)} %collective-permute-done.18.refs_0_), channel_id=1, source_target_pairs={{0,1},{1,0},{2,3},{3,2},{4,5},{5,4},{6,7},{7,6},{8,9},{9,8},{10,11... | collective-permute-start | bytes 786440 | tf_op jit(solution)/shard_map/ppermute | solution.py:50
  116.2 8.8 %collective-permute-start.32 = (bf16[32,2,16,128]{3,2,1,0:T(8,128)(2,1)S(1)}, bf16[32,2,16,128]{3,2,1,0:T(8,128)(2,1)S(1)}, u32[]{:S(2)}, u32[]{:S(2)}) collective-permute-start(bf16[32,2,16,128]{3,2,1,0:T(8,128)(2,1)S(1)} %collective-permute-done.24.refs_3_), channel_id=1, source_target_pairs={{0,1},{1,0},{2,3},{3,2},{4,5},{5,4},{6,7},{7,6},{8,9},{9,8},{10,11... | collective-permute-start | bytes 786440 | tf_op jit(solution)/shard_map/ppermute | solution.py:50
  148.3 8.1 %collective-permute-start.33 = (bf16[4,32,2,16,128]{4,3,2,1,0:T(8,128)(2,1)S(1)}, bf16[4,32,2,16,128]{4,3,2,1,0:T(8,128)(2,1)S(1)}, u32[]{:S(2)}, u32[]{:S(2)}) collective-permute-start(bf16[4,32,2,16,128]{4,3,2,1,0:T(8,128)(2,1)S(1)} %get-tuple-element.34), channel_id=1, source_target_pairs={{0,1},{1,0},{2,3},{3,2},{4,5},{5,4},{6,7},{7,6},{8,9},{9,8},{10,11... | collective-permute-start | bytes 3145736 | tf_op jit(solution)/shard_map/ppermute | solution.py:50
  151.0 9.2 %collective-permute-start.35 = (bf16[32,2,16,128]{3,2,1,0:T(8,128)(2,1)S(1)}, bf16[32,2,16,128]{3,2,1,0:T(8,128)(2,1)S(1)}, u32[]{:S(2)}, u32[]{:S(2)}) collective-permute-start(bf16[32,2,16,128]{3,2,1,0:T(8,128)(2,1)S(1)} %get-tuple-element.46), channel_id=1, source_target_pairs={{0,2},{1,3},{2,0},{3,1},{4,6},{5,7},{6,4},{7,5},{8,10},{9,11},{10,... | collective-permute-start | bytes 786440 | tf_op jit(solution)/shard_map/ppermute | solution.py:50
  151.7 13.3 %collective-permute-start.38 = (bf16[32,2,16,128]{3,2,1,0:T(8,128)(2,1)S(1)}, bf16[32,2,16,128]{3,2,1,0:T(8,128)(2,1)S(1)}, u32[]{:S(2)}, u32[]{:S(2)}) collective-permute-start(bf16[32,2,16,128]{3,2,1,0:T(8,128)(2,1)S(1)} %get-tuple-element.45), channel_id=1, source_target_pairs={{0,2},{1,3},{2,0},{3,1},{4,6},{5,7},{6,4},{7,5},{8,10},{9,11},{10,... | collective-permute-start | bytes 786440 | tf_op jit(solution)/shard_map/ppermute | solution.py:50
  153.1 15.9 %collective-permute-start.40 = (bf16[32,2,16,128]{3,2,1,0:T(8,128)(2,1)S(1)}, bf16[32,2,16,128]{3,2,1,0:T(8,128)(2,1)S(1)}, u32[]{:S(2)}, u32[]{:S(2)}) collective-permute-start(bf16[32,2,16,128]{3,2,1,0:T(8,128)(2,1)S(1)} %get-tuple-element.44), channel_id=1, source_target_pairs={{0,4},{1,5},{2,6},{3,7},{4,8},{5,9},{6,10},{7,11},{8,12},{9,13},{1... | collective-permute-start | bytes 786440 | tf_op jit(solution)/shard_map/ppermute | solution.py:50
  165.3 12.0 %collective-permute-start.36 = (bf16[32,2,16,128]{3,2,1,0:T(8,128)(2,1)S(1)}, bf16[32,2,16,128]{3,2,1,0:T(8,128)(2,1)S(1)}, u32[]{:S(2)}, u32[]{:S(2)}) collective-permute-start(bf16[32,2,16,128]{3,2,1,0:T(8,128)(2,1)S(1)} %get-tuple-element.48), channel_id=1, source_target_pairs={{0,4},{1,5},{2,6},{3,7},{4,8},{5,9},{6,10},{7,11},{8,12},{9,13},{1... | collective-permute-start | bytes 786440 | tf_op jit(solution)/shard_map/ppermute | solution.py:50
  169.2 9.3 %collective-permute-start.41 = (bf16[32,2,16,128]{3,2,1,0:T(8,128)(2,1)S(1)}, bf16[32,2,16,128]{3,2,1,0:T(8,128)(2,1)S(1)}, u32[]{:S(2)}, u32[]{:S(2)}) collective-permute-start(bf16[32,2,16,128]{3,2,1,0:T(8,128)(2,1)S(1)} %fusion), channel_id=1, source_target_pairs={{0,2},{1,3},{2,0},{3,1},{4,6},{5,7},{6,4},{7,5},{8,10},{9,11},{10,... | collective-permute-start | bytes 786440 | tf_op jit(solution)/shard_map/ppermute | solution.py:50
  171.0 11.9 %collective-permute-start.39 = (bf16[32,2,16,128]{3,2,1,0:T(8,128)(2,1)S(1)}, bf16[32,2,16,128]{3,2,1,0:T(8,128)(2,1)S(1)}, u32[]{:S(2)}, u32[]{:S(2)}) collective-permute-start(bf16[32,2,16,128]{3,2,1,0:T(8,128)(2,1)S(1)} %get-tuple-element.47), channel_id=1, source_target_pairs={{0,12},{1,13},{2,14},{3,15},{4,0},{5,1},{6,2},{7,3},{8,4},{9,5},{1... | collective-permute-start | bytes 786440 | tf_op jit(solution)/shard_map/ppermute | solution.py:50
  177.4 10.0 %collective-permute-start.37 = (bf16[32,2,16,128]{3,2,1,0:T(8,128)(2,1)S(1)}, bf16[32,2,16,128]{3,2,1,0:T(8,128)(2,1)S(1)}, u32[]{:S(2)}, u32[]{:S(2)}) collective-permute-start(bf16[32,2,16,128]{3,2,1,0:T(8,128)(2,1)S(1)} %fusion.3), channel_id=1, source_target_pairs={{0,4},{1,5},{2,6},{3,7},{4,8},{5,9},{6,10},{7,11},{8,12},{9,13},{1... | collective-permute-start | bytes 786440 | tf_op jit(solution)/shard_map/ppermute | solution.py:50
  187.8 11.2 %collective-permute-start.42 = (bf16[16,64,128]{2,1,0:T(8,128)(2,1)S(1)}, bf16[16,64,128]{2,1,0:T(8,128)(2,1)S(1)}, u32[]{:S(2)}, u32[]{:S(2)}) collective-permute-start(bf16[16,64,128]{2,1,0:T(8,128)(2,1)S(1)} %window.5.spec_ref.refs_0_), channel_id=1, source_target_pairs={{0,4},{1,5},{2,6},{3,7},{4,8},{5,9},{6,10},{7,11},{8,12},{9,13},{1... | collective-permute-start | bytes 786440 | tf_op jit(solution)/shard_map/ppermute | solution.py:50
  188.8 11.6 %collective-permute-start.45 = (bf16[16,64,128]{2,1,0:T(8,128)(2,1)S(1)}, bf16[16,64,128]{2,1,0:T(8,128)(2,1)S(1)}, u32[]{:S(2)}, u32[]{:S(2)}) collective-permute-start(bf16[16,64,128]{2,1,0:T(8,128)(2,1)S(1)} %window.5.spec_ref.refs_0_), channel_id=1, source_target_pairs={{0,2},{1,3},{2,0},{3,1},{4,6},{5,7},{6,4},{7,5},{8,10},{9,11},{10,... | collective-permute-start | bytes 786440 | tf_op jit(solution)/shard_map/ppermute | solution.py:50
  190.3 13.8 %collective-permute-start.44 = (bf16[16,64,128]{2,1,0:T(8,128)(2,1)S(1)}, bf16[16,64,128]{2,1,0:T(8,128)(2,1)S(1)}, u32[]{:S(2)}, u32[]{:S(2)}) collective-permute-start(bf16[16,64,128]{2,1,0:T(8,128)(2,1)S(1)} %window.5.spec_ref.refs_0_), channel_id=1, source_target_pairs={{0,12},{1,13},{2,14},{3,15},{4,0},{5,1},{6,2},{7,3},{8,4},{9,5},{1... | collective-permute-start | bytes 786440 | tf_op jit(solution)/shard_map/ppermute | solution.py:50
  199.0 13.2 %collective-permute-start.43 = (bf16[16,64,128]{2,1,0:T(8,128)(2,1)S(1)}, bf16[16,64,128]{2,1,0:T(8,128)(2,1)S(1)}, u32[]{:S(2)}, u32[]{:S(2)}) collective-permute-start(bf16[16,64,128]{2,1,0:T(8,128)(2,1)S(1)} %collective-permute-done.42.spec_ref.refs_1_), channel_id=1, source_target_pairs={{0,4},{1,5},{2,6},{3,7},{4,8},{5,9},{6,10},{7,11},{8,12},{9,13},{1... | collective-permute-start | bytes 786440 | tf_op jit(solution)/shard_map/ppermute | solution.py:50
  200.3 15.2 %collective-permute-start.58 = (bf16[32,2,16,128]{3,2,1,0:T(8,128)(2,1)S(1)}, bf16[32,2,16,128]{3,2,1,0:T(8,128)(2,1)S(1)}, u32[]{:S(2)}, u32[]{:S(2)}) collective-permute-start(bf16[32,2,16,128]{3,2,1,0:T(8,128)(2,1)S(1)} %window_at.8.refs_0_), channel_id=1, source_target_pairs={{0,1},{1,0},{2,3},{3,2},{4,5},{5,4},{6,7},{7,6},{8,9},{9,8},{10,11... | collective-permute-start | bytes 786440 | tf_op jit(solution)/shard_map/ppermute | solution.py:50
  200.4 15.8 %collective-permute-start.46 = (bf16[16,64,128]{2,1,0:T(8,128)(2,1)S(1)}, bf16[16,64,128]{2,1,0:T(8,128)(2,1)S(1)}, u32[]{:S(2)}, u32[]{:S(2)}) collective-permute-start(bf16[16,64,128]{2,1,0:T(8,128)(2,1)S(1)} %collective-permute-done.45.spec_ref.refs_4_), channel_id=1, source_target_pairs={{0,4},{1,5},{2,6},{3,7},{4,8},{5,9},{6,10},{7,11},{8,12},{9,13},{1... | collective-permute-start | bytes 786440 | tf_op jit(solution)/shard_map/ppermute | solution.py:50
  204.1 12.1 %collective-permute-start.48 = (bf16[16,64,128]{2,1,0:T(8,128)(2,1)S(1)}, bf16[16,64,128]{2,1,0:T(8,128)(2,1)S(1)}, u32[]{:S(2)}, u32[]{:S(2)}) collective-permute-start(bf16[16,64,128]{2,1,0:T(8,128)(2,1)S(1)} %collective-permute-done.44.spec_ref.refs_3_), channel_id=1, source_target_pairs={{0,2},{1,3},{2,0},{3,1},{4,6},{5,7},{6,4},{7,5},{8,10},{9,11},{10,... | collective-permute-start | bytes 786440 | tf_op jit(solution)/shard_map/ppermute | solution.py:50
  212.1 7.2 %collective-permute-start.47 = (bf16[16,64,128]{2,1,0:T(8,128)(2,1)S(1)}, bf16[16,64,128]{2,1,0:T(8,128)(2,1)S(1)}, u32[]{:S(2)}, u32[]{:S(2)}) collective-permute-start(bf16[16,64,128]{2,1,0:T(8,128)(2,1)S(1)} %collective-permute-done.43.refs_2_.spec_ref), channel_id=1, source_target_pairs={{0,2},{1,3},{2,0},{3,1},{4,6},{5,7},{6,4},{7,5},{8,10},{9,11},{10,... | collective-permute-start | bytes 786440 | tf_op jit(solution)/shard_map/ppermute | solution.py:50
  213.2 8.4 %collective-permute-start.59 = (bf16[32,2,16,128]{3,2,1,0:T(8,128)(2,1)S(1)}, bf16[32,2,16,128]{3,2,1,0:T(8,128)(2,1)S(1)}, u32[]{:S(2)}, u32[]{:S(2)}) collective-permute-start(bf16[32,2,16,128]{3,2,1,0:T(8,128)(2,1)S(1)} %window_at.10.refs_1_), channel_id=1, source_target_pairs={{0,1},{1,0},{2,3},{3,2},{4,5},{5,4},{6,7},{7,6},{8,9},{9,8},{10,11... | collective-permute-start | bytes 786440 | tf_op jit(solution)/shard_map/ppermute | solution.py:50
  216.2 16.6 %collective-permute-start.57 = (bf16[32,2,16,128]{3,2,1,0:T(8,128)(2,1)S(1)}, bf16[32,2,16,128]{3,2,1,0:T(8,128)(2,1)S(1)}, u32[]{:S(2)}, u32[]{:S(2)}) collective-permute-start(bf16[32,2,16,128]{3,2,1,0:T(8,128)(2,1)S(1)} %window_at.9.refs_0_), channel_id=1, source_target_pairs={{0,1},{1,0},{2,3},{3,2},{4,5},{5,4},{6,7},{7,6},{8,9},{9,8},{10,11... | collective-permute-start | bytes 786440 | tf_op jit(solution)/shard_map/ppermute | solution.py:50
  219.3 13.6 %collective-permute-start.64 = (bf16[32,2,16,128]{3,2,1,0:T(8,128)(2,1)S(1)}, bf16[32,2,16,128]{3,2,1,0:T(8,128)(2,1)S(1)}, u32[]{:S(2)}, u32[]{:S(2)}) collective-permute-start(bf16[32,2,16,128]{3,2,1,0:T(8,128)(2,1)S(1)} %window_at.14.refs_3_), channel_id=1, source_target_pairs={{0,1},{1,0},{2,3},{3,2},{4,5},{5,4},{6,7},{7,6},{8,9},{9,8},{10,11... | collective-permute-start | bytes 786440 | tf_op jit(solution)/shard_map/ppermute | solution.py:50
  232.4 11.1 %collective-permute-start.49 = (bf16[16,64,128]{2,1,0:T(8,128)(2,1)S(1)}, bf16[16,64,128]{2,1,0:T(8,128)(2,1)S(1)}, u32[]{:S(2)}, u32[]{:S(2)}) collective-permute-start(bf16[16,64,128]{2,1,0:T(8,128)(2,1)S(1)} %window.5.spec_ref.refs_0_), channel_id=1, source_target_pairs={{0,1},{1,0},{2,3},{3,2},{4,5},{5,4},{6,7},{7,6},{8,9},{9,8},{10,11... | collective-permute-start | bytes 786440 | tf_op jit(solution)/shard_map/ppermute | solution.py:50
  232.8 11.8 %collective-permute-start.50 = (bf16[16,64,128]{2,1,0:T(8,128)(2,1)S(1)}, bf16[16,64,128]{2,1,0:T(8,128)(2,1)S(1)}, u32[]{:S(2)}, u32[]{:S(2)}) collective-permute-start(bf16[16,64,128]{2,1,0:T(8,128)(2,1)S(1)} %collective-permute-done.42.spec_ref.refs_1_), channel_id=1, source_target_pairs={{0,1},{1,0},{2,3},{3,2},{4,5},{5,4},{6,7},{7,6},{8,9},{9,8},{10,11... | collective-permute-start | bytes 786440 | tf_op jit(solution)/shard_map/ppermute | solution.py:50
  232.9 12.5 %collective-permute-start.52 = (bf16[16,64,128]{2,1,0:T(8,128)(2,1)S(1)}, bf16[16,64,128]{2,1,0:T(8,128)(2,1)S(1)}, u32[]{:S(2)}, u32[]{:S(2)}) collective-permute-start(bf16[16,64,128]{2,1,0:T(8,128)(2,1)S(1)} %collective-permute-done.44.spec_ref.refs_3_), channel_id=1, source_target_pairs={{0,1},{1,0},{2,3},{3,2},{4,5},{5,4},{6,7},{7,6},{8,9},{9,8},{10,11... | collective-permute-start | bytes 786440 | tf_op jit(solution)/shard_map/ppermute | solution.py:50
  241.6 10.4 %collective-permute-start.65 = (bf16[16,64,128]{2,1,0:T(8,128)(2,1)S(1)}, bf16[16,64,128]{2,1,0:T(8,128)(2,1)S(1)}, u32[]{:S(2)}, u32[]{:S(2)}) collective-permute-start(bf16[16,64,128]{2,1,0:T(8,128)(2,1)S(1)} %correlate1.3.refs_0_), channel_id=1, source_target_pairs={{0,4},{1,5},{2,6},{3,7},{4,8},{5,9},{6,10},{7,11},{8,12},{9,13},{1... | collective-permute-start | bytes 786440 | tf_op jit(solution)/shard_map/ppermute | solution.py:50
  243.4 8.7 %collective-permute-start.53 = (bf16[16,64,128]{2,1,0:T(8,128)(2,1)S(1)}, bf16[16,64,128]{2,1,0:T(8,128)(2,1)S(1)}, u32[]{:S(2)}, u32[]{:S(2)}) collective-permute-start(bf16[16,64,128]{2,1,0:T(8,128)(2,1)S(1)} %collective-permute-done.45.spec_ref.refs_4_), channel_id=1, source_target_pairs={{0,1},{1,0},{2,3},{3,2},{4,5},{5,4},{6,7},{7,6},{8,9},{9,8},{10,11... | collective-permute-start | bytes 786440 | tf_op jit(solution)/shard_map/ppermute | solution.py:50
  244.2 9.9 %collective-permute-start.51 = (bf16[16,64,128]{2,1,0:T(8,128)(2,1)S(1)}, bf16[16,64,128]{2,1,0:T(8,128)(2,1)S(1)}, u32[]{:S(2)}, u32[]{:S(2)}) collective-permute-start(bf16[16,64,128]{2,1,0:T(8,128)(2,1)S(1)} %collective-permute-done.43.refs_2_.spec_ref), channel_id=1, source_target_pairs={{0,1},{1,0},{2,3},{3,2},{4,5},{5,4},{6,7},{7,6},{8,9},{9,8},{10,11... | collective-permute-start | bytes 786440 | tf_op jit(solution)/shard_map/ppermute | solution.py:50
  245.3 9.5 %collective-permute-start.54 = (bf16[16,64,128]{2,1,0:T(8,128)(2,1)S(1)}, bf16[16,64,128]{2,1,0:T(8,128)(2,1)S(1)}, u32[]{:S(2)}, u32[]{:S(2)}) collective-permute-start(bf16[16,64,128]{2,1,0:T(8,128)(2,1)S(1)} %collective-permute-done.46.refs_5_.spec_ref), channel_id=1, source_target_pairs={{0,1},{1,0},{2,3},{3,2},{4,5},{5,4},{6,7},{7,6},{8,9},{9,8},{10,11... | collective-permute-start | bytes 786440 | tf_op jit(solution)/shard_map/ppermute | solution.py:50
  246.1 11.5 %collective-permute-start.56 = (bf16[16,64,128]{2,1,0:T(8,128)(2,1)S(1)}, bf16[16,64,128]{2,1,0:T(8,128)(2,1)S(1)}, u32[]{:S(2)}, u32[]{:S(2)}) collective-permute-start(bf16[16,64,128]{2,1,0:T(8,128)(2,1)S(1)} %collective-permute-done.48.refs_7_.spec_ref), channel_id=1, source_target_pairs={{0,1},{1,0},{2,3},{3,2},{4,5},{5,4},{6,7},{7,6},{8,9},{9,8},{10,11... | collective-permute-start | bytes 786440 | tf_op jit(solution)/shard_map/ppermute | solution.py:50
  252.1 6.3 %collective-permute-start.55 = (bf16[16,64,128]{2,1,0:T(8,128)(2,1)S(1)}, bf16[16,64,128]{2,1,0:T(8,128)(2,1)}, u32[]{:S(2)}, u32[]{:S(2)}) collective-permute-start(bf16[16,64,128]{2,1,0:T(8,128)(2,1)S(1)} %collective-permute-done.47.refs_6_.spec_ref), channel_id=1, source_target_pairs={{0,1},{1,0},{2,3},{3,2},{4,5},{5,4},{6,7},{7,6},{8,9},{9,8},{10,11... | collective-permute-start | bytes 786440 | tf_op jit(solution)/shard_map/ppermute | solution.py:50
  252.8 15.9 %collective-permute-start.68 = (bf16[16,64,128]{2,1,0:T(8,128)(2,1)S(1)}, bf16[16,64,128]{2,1,0:T(8,128)(2,1)S(1)}, u32[]{:S(2)}, u32[]{:S(2)}) collective-permute-start(bf16[16,64,128]{2,1,0:T(8,128)(2,1)S(1)} %correlate1.3.refs_0_), channel_id=1, source_target_pairs={{0,2},{1,3},{2,0},{3,1},{4,6},{5,7},{6,4},{7,5},{8,10},{9,11},{10,... | collective-permute-start | bytes 786440 | tf_op jit(solution)/shard_map/ppermute | solution.py:50
  254.8 14.1 %collective-permute-start.67 = (bf16[16,64,128]{2,1,0:T(8,128)(2,1)S(1)}, bf16[16,64,128]{2,1,0:T(8,128)(2,1)S(1)}, u32[]{:S(2)}, u32[]{:S(2)}) collective-permute-start(bf16[16,64,128]{2,1,0:T(8,128)(2,1)S(1)} %correlate1.3.refs_0_), channel_id=1, source_target_pairs={{0,12},{1,13},{2,14},{3,15},{4,0},{5,1},{6,2},{7,3},{8,4},{9,5},{1... | collective-permute-start | bytes 786440 | tf_op jit(solution)/shard_map/ppermute | solution.py:50
  255.5 14.1 %collective-permute-start.66 = (bf16[16,64,128]{2,1,0:T(8,128)(2,1)S(1)}, bf16[16,64,128]{2,1,0:T(8,128)(2,1)}, u32[]{:S(2)}, u32[]{:S(2)}) collective-permute-start(bf16[16,64,128]{2,1,0:T(8,128)(2,1)S(1)} %collective-permute-done.65.refs_1_), channel_id=1, source_target_pairs={{0,4},{1,5},{2,6},{3,7},{4,8},{5,9},{6,10},{7,11},{8,12},{9,13},{1... | collective-permute-start | bytes 786440 | tf_op jit(solution)/shard_map/ppermute | solution.py:50
  258.2 11.4 %collective-permute-start.72 = (bf16[16,64,128]{2,1,0:T(8,128)(2,1)S(1)}, bf16[16,64,128]{2,1,0:T(8,128)(2,1)}, u32[]{:S(2)}, u32[]{:S(2)}) collective-permute-start(bf16[16,64,128]{2,1,0:T(8,128)(2,1)S(1)} %correlate1.3.refs_0_), channel_id=1, source_target_pairs={{0,1},{1,0},{2,3},{3,2},{4,5},{5,4},{6,7},{7,6},{8,9},{9,8},{10,11... | collective-permute-start | bytes 786440 | tf_op jit(solution)/shard_map/ppermute | solution.py:50
  268.1 11.2 %collective-permute-start.73 = (bf16[16,64,128]{2,1,0:T(8,128)(2,1)S(1)}, bf16[16,64,128]{2,1,0:T(8,128)(2,1)S(1)}, u32[]{:S(2)}, u32[]{:S(2)}) collective-permute-start(bf16[16,64,128]{2,1,0:T(8,128)(2,1)S(1)} %collective-permute-done.65.refs_1_), channel_id=1, source_target_pairs={{0,1},{1,0},{2,3},{3,2},{4,5},{5,4},{6,7},{7,6},{8,9},{9,8},{10,11... | collective-permute-start | bytes 786440 | tf_op jit(solution)/shard_map/ppermute | solution.py:50
  268.7 10.1 %collective-permute-start.69 = (bf16[16,64,128]{2,1,0:T(8,128)(2,1)S(1)}, bf16[16,64,128]{2,1,0:T(8,128)(2,1)S(1)}, u32[]{:S(2)}, u32[]{:S(2)}) collective-permute-start(bf16[16,64,128]{2,1,0:T(8,128)(2,1)S(1)} %collective-permute-done.68.refs_4_), channel_id=1, source_target_pairs={{0,4},{1,5},{2,6},{3,7},{4,8},{5,9},{6,10},{7,11},{8,12},{9,13},{1... | collective-permute-start | bytes 786440 | tf_op jit(solution)/shard_map/ppermute | solution.py:50
  268.9 9.9 %collective-permute-start.71 = (bf16[16,64,128]{2,1,0:T(8,128)(2,1)S(1)}, bf16[16,64,128]{2,1,0:T(8,128)(2,1)S(1)}, u32[]{:S(2)}, u32[]{:S(2)}) collective-permute-start(bf16[16,64,128]{2,1,0:T(8,128)(2,1)S(1)} %collective-permute-done.67.refs_3_), channel_id=1, source_target_pairs={{0,2},{1,3},{2,0},{3,1},{4,6},{5,7},{6,4},{7,5},{8,10},{9,11},{10,... | collective-permute-start | bytes 786440 | tf_op jit(solution)/shard_map/ppermute | solution.py:50
  269.6 9.7 %collective-permute-start.75 = (bf16[16,64,128]{2,1,0:T(8,128)(2,1)S(1)}, bf16[16,64,128]{2,1,0:T(8,128)(2,1)S(1)}, u32[]{:S(2)}, u32[]{:S(2)}) collective-permute-start(bf16[16,64,128]{2,1,0:T(8,128)(2,1)S(1)} %collective-permute-done.67.refs_3_), channel_id=1, source_target_pairs={{0,1},{1,0},{2,3},{3,2},{4,5},{5,4},{6,7},{7,6},{8,9},{9,8},{10,11... | collective-permute-start | bytes 786440 | tf_op jit(solution)/shard_map/ppermute | solution.py:50
  269.6 13.1 %collective-permute-start.70 = (bf16[16,64,128]{2,1,0:T(8,128)(2,1)}, bf16[16,64,128]{2,1,0:T(8,128)(2,1)S(1)}, u32[]{:S(2)}, u32[]{:S(2)}) collective-permute-start(bf16[16,64,128]{2,1,0:T(8,128)(2,1)} %collective-permute-done.66.refs_2_), channel_id=1, source_target_pairs={{0,2},{1,3},{2,0},{3,1},{4,6},{5,7},{6,4},{7,5},{8,10},{9,11},{10,... | collective-permute-start | bytes 786440 | tf_op jit(solution)/shard_map/ppermute | solution.py:50
  (35 other events, 134.1 us)

commit v7 on v6

--- a/solution.py
+++ b/solution.py
@@ -12,6 +12,7 @@
 NFW = 32
 FREQ0 = 16
 ITERS = 2
+SURE = 128
 LANES = 128
 F32 = jnp.float32
 BF16 = jnp.bfloat16
@@ -234,11 +235,11 @@
     )(spectrum, reflection)
 
 
-def correlate_kernel(line, flip, has_base, final, *refs):
+def correlate_kernel(line, flip, has_base, *refs):
     core = own_place(line)[3]
     own, other, panel_ref = refs[:line], refs[line : 2 * line], refs[2 * line]
     base_ref = refs[2 * line + 1] if has_base else None
-    out_ref, held, sems, *spare = refs[2 * line + 1 + has_base :]
+    out_ref, held, sems = refs[2 * line + 1 + has_base :]
     focal = own[0].shape[2]
     rows = held.shape[3]
     wait = fetch_panels(line, False, flip, panel_ref, held, sems)
@@ -265,44 +266,106 @@
             if has_base:
                 real += base_ref[w, 0]
                 imag += base_ref[w, 1]
-            if final:
-                spare[0][pl.ds(2 * w * focal, focal), :] = real
-                spare[0][pl.ds((2 * w + 1) * focal, focal), :] = imag
-            else:
-                out_ref[w, 0] = real
-                out_ref[w, 1] = imag
+            out_ref[w, 0] = real
+            out_ref[w, 1] = imag
         return carry
 
     lax.fori_loop(0, CHUNKS, body, 0)
-    if final:
-        for p in range(focal):
-            out_ref[p] = spare[0][pl.ds(p, 2 * NFW, stride=focal), :].astype(BF16)
-
-
-def correlate(own, other, reflection, line, flip, base=None, final=False):
+
+
+def correlate(own, other, reflection, line, flip, base=None):
     focal = own[0].shape[2]
     more = [] if base is None else [base]
     shape = jax.ShapeDtypeStruct((NFW, 2, focal, LANES), F32)
-    if final:
-        shape = jax.ShapeDtypeStruct((focal, 2 * NFW, LANES), BF16)
-    spare = [pltpu.VMEM((2 * NFW * focal, LANES), F32)] if final else []
-    return pl.pallas_call(
-        functools.partial(correlate_kernel, line, flip, bool(more), final),
+    return pl.pallas_call(
+        functools.partial(correlate_kernel, line, flip, bool(more)),
         in_specs=[VMEM] * (2 * line) + [ANY] + [VMEM] * len(more),
         out_specs=VMEM,
         out_shape=shape,
-        scratch_shapes=panel_scratch(line) + spare,
+        scratch_shapes=panel_scratch(line),
         compiler_params=limit(24),
         cost_estimate=panel_cost(focal, reflection.shape[3] // 2),
         name=f"correlate{flip}",
     )(*own, *other, reflection, *more)
 
 
+def correlate_all_kernel(line, *refs):
+    core = own_place(line)[3]
+    places = relative(line)
+    own, other = refs[: len(places)], refs[len(places) : 2 * len(places)]
+    panel_ref, out_ref, held, sems, total_ref = refs[2 * len(places) :]
+    focal = out_ref.shape[0]
+    rows = NFW // CHUNKS
+    slots = held.shape[0]
+
+    def copy(chunk):
+        slot = lax.rem(chunk, slots)
+        part = pl.ds(chunk * rows, rows)
+        return pltpu.make_async_copy(panel_ref.at[:, part], held.at[slot], sems.at[slot])
+
+    for chunk in range(slots):
+        copy(chunk).start()
+
+    def body(chunk, carry):
+        copy(chunk).wait()
+        slot = lax.rem(chunk, slots)
+        for row in range(rows):
+            w = chunk * rows + row
+            panels, specs = [], []
+            for at, (flip, step) in enumerate(places):
+                columns = pl.ds(chip_columns(line, False, flip, step), 2 * LANES)
+                panels.append(held[slot, :, row, :, columns].reshape(2 * LANES, 2 * LANES))
+                mine, theirs = own[at][w], other[at][w]
+                specs.append(
+                    join_cores(core, mine.reshape(2 * focal, LANES), theirs.reshape(2 * focal, LANES))
+                )
+            total = lax.dot_general(
+                jnp.concatenate(specs, axis=1),
+                jnp.concatenate(panels, axis=1),
+                (((1,), (1,)), ((), ())),
+                preferred_element_type=F32,
+            )
+            real = total[:focal, :LANES] + total[focal:, LANES:]
+            imag = total[focal:, :LANES] - total[:focal, LANES:]
+            total_ref[pl.ds(2 * w * focal, focal), :] = real
+            total_ref[pl.ds((2 * w + 1) * focal, focal), :] = imag
+
+        @pl.when(chunk + slots < CHUNKS)
+        def _():
+            copy(chunk + slots).start()
+
+        return carry
+
+    lax.fori_loop(0, CHUNKS, body, 0)
+    for p in range(focal):
+        out_ref[p] = total_ref[pl.ds(p, 2 * NFW, stride=focal), :].astype(BF16)
+
+
+def correlate_all(own, other, reflection, line):
+    own, other = sum(own, []), sum(other, [])
+    focal = own[0].shape[2]
+    return pl.pallas_call(
+        functools.partial(correlate_all_kernel, line),
+        in_specs=[VMEM] * (2 * len(own)) + [ANY],
+        out_specs=VMEM,
+        out_shape=jax.ShapeDtypeStruct((focal, 2 * NFW, LANES), BF16),
+        scratch_shapes=[
+            pltpu.VMEM((SLOTS, 2, NFW // CHUNKS, LANES, reflection.shape[3]), BF16),
+            pltpu.SemaphoreType.DMA((SLOTS,)),
+            pltpu.VMEM((2 * NFW * focal, LANES), F32),
+        ],
+        compiler_params=limit(22),
+        cost_estimate=panel_cost(focal, reflection.shape[3]),
+        name="correlate_all",
+    )(*own, *other, reflection)
+
+
 def windowed_spectrum(pair, onset, forward, inverse):
-    time = lax.broadcasted_iota(jnp.int32, (NT, 2 * LANES), 0)
-    values = jnp.dot(inverse, jnp.concatenate(pair, axis=1), preferred_element_type=F32)
+    time = SURE + lax.broadcasted_iota(jnp.int32, (NT - SURE, 2 * LANES), 0)
+    spectra = jnp.concatenate(pair, axis=1)
+    values = jnp.dot(inverse, spectra, preferred_element_type=F32)
     kept = jnp.where(time < jnp.concatenate(onset, axis=1), values, 0.0).astype(BF16)
-    return jnp.dot(forward, kept, preferred_element_type=F32)
+    return jnp.dot(forward, jnp.concatenate([kept, spectra], axis=0), preferred_element_type=F32)
 
 
 def window_kernel(parts, has_base, want_spec, *refs):
@@ -388,6 +451,81 @@
     )(forward, inverse, onset_times, spec)
 
 
+def half_field_kernel(line, inverse_ref, onset_ref, *refs):
+    core = own_place(line)[3]
+    places = relative(line)
+    own, (keep, send) = refs[: len(places)], refs[len(places) :]
+    focal = keep.shape[0]
+    samples = keep.shape[1]
+    first = (lax.axis_index("blk") // 2) * (2 * samples)
+    time = first + lax.broadcasted_iota(jnp.int32, (2 * samples, 2 * LANES), 0)
+
+    for p in range(focal):
+        for at in range(0, len(places), 2):
+            onset = []
+            for flip, step in places[at : at + 2]:
+                start = chip_columns(line, False, flip, step) + core * LANES
+                onset.append(onset_ref[p : p + 1, pl.ds(pl.multiple_of(start, LANES), LANES)])
+            spec = jnp.concatenate([own[at][p], own[at + 1][p]], axis=1)
+            values = jnp.dot(inverse_ref[...], spec, preferred_element_type=F32)
+            values = jnp.where(time < jnp.concatenate(onset, axis=1), values, 0.0)
+            low, high = values[:samples].astype(BF16), values[samples:].astype(BF16)
+            columns = pl.ds(at * LANES, 2 * LANES)
+            keep[p, :, columns] = jnp.where(core == 0, low, high)
+            send[p, :, columns] = jnp.where(core == 0, high, low)
+
+
+def half_field(own, inverse, onset_times, line):
+    own = sum(own, [])
+    focal, k, _ = own[0].shape
+    shape = (focal, inverse.shape[0] // 2, len(own) * LANES)
+    return pl.pallas_call(
+        functools.partial(half_field_kernel, line),
+        in_specs=[VMEM] * (2 + len(own)),
+        out_specs=[VMEM] * 2,
+        out_shape=[jax.ShapeDtypeStruct(shape, BF16)] * 2,
+        compiler_params=limit(4),
+        cost_estimate=pl.CostEstimate(
+            flops=4 * k * math.prod(shape), bytes_accessed=4 * math.prod(shape), transcendentals=0
+        ),
+        name="half_field",
+    )(inverse, onset_times, *own)
+
+
+def merge_kernel(line, mine, theirs, out_ref, made, sems):
+    core = own_place(line)[3]
+    copy, rows = strip_copies(made, out_ref, sems, STRIPS)
+
+    def body(strip, carry):
+        for row in range(rows):
+            p = strip * rows + row
+            for at, (flip, step) in enumerate(relative(line)):
+                columns = pl.ds(chip_columns(line, False, flip, step), 2 * LANES)
+                part = pl.ds(at * LANES, LANES)
+                made[p, :, columns] = join_cores(core, mine[p, :, part], theirs[p, :, part])
+        copy(strip).start()
+        return carry
+
+    lax.fori_loop(0, STRIPS, body, 0)
+    for strip in range(STRIPS):
+        copy(strip).wait()
+
+
+def merge(mine, theirs, line):
+    focal, samples, width = mine.shape
+    shape = (focal, samples, 2 * width)
+    return pl.pallas_call(
+        functools.partial(merge_kernel, line),
+        in_specs=[VMEM] * 2,
+        out_specs=ANY,
+        out_shape=jax.ShapeDtypeStruct(shape, BF16),
+        scratch_shapes=[pltpu.VMEM(shape, BF16), pltpu.SemaphoreType.DMA((STRIPS,))],
+        compiler_params=limit(6),
+        cost_estimate=pl.CostEstimate(flops=0, bytes_accessed=8 * mine.size, transcendentals=0),
+        name="merge",
+    )(mine, theirs)
+
+
 def field_kernel(line, has_plus, inverse_ref, onset_ref, *refs):
     core = own_place(line)[3]
     places = relative(line)
@@ -468,15 +606,17 @@
     beside = [places.send(far[1], places.shift(1))] if size > 1 else []
     parts = [keep0[0], got0[0]]
 
-    def pass_on(steps, shift):
-        carried = []
+    def pass_on(steps, shift, *first):
+        carried, sent = [], []
         for step in steps:
-            terms = [keep0[step], got0[step], *([across[step]] if step in across else []), *carried]
-            carried = [places.send(add(*terms).astype(BF16), places.shift(shift))]
-        return carried
-
-    parts += pass_on(range(size // 2, 0, -1), 1)
-    parts += pass_on(range(size // 2 + 1, size), size - 1)
+            crossed = [after(across[step], *first)] if step in across else []
+            carried = [places.send(add(keep0[step], got0[step], *crossed, *carried).astype(BF16), places.shift(shift))]
+            sent += carried
+        return sent
+
+    ahead = pass_on(range(size // 2, 0, -1), 1)
+    behind = pass_on(range(size // 2 + 1, size), size - 1, *ahead[:1])
+    parts += ahead[-1:] + behind[-1:]
     across[0] = places.send(add(keep1[0], got1[0], *beside).astype(BF16), places.pair())
     return parts + [across[0]]
 
@@ -500,7 +640,7 @@
     across = {0: places.send(block, places.pair())}
     own = run(0, [0], line)
     for step in range(2, size // 2 + 1):
-        line[step] = places.send(after(line[step - 1], *own), places.shift(1))
+        line[step] = places.send(after(line[step - 1], across[0], *own), places.shift(1))
     for step in range(size - 2, size // 2, -1):
         line[step] = places.send(after(line[step + 1], *own), places.shift(size - 1))
     for step in near:
@@ -530,6 +670,11 @@
     forward, inverse = tables_of(jnp.arange(NT, dtype=jnp.int32))
     own_samples = lax.axis_index("blk") * samples + jnp.arange(samples, dtype=jnp.int32)
     own_forward, own_inverse = tables_of(own_samples)
+    chip_samples = lax.axis_index("blk") // 2 * (2 * samples) + jnp.arange(2 * samples, dtype=jnp.int32)
+    _, chip_inverse = tables_of(chip_samples)
+    sure = contract("kt,tj->kj", forward[:, :SURE], inverse[:SURE]).astype(BF16)
+    forward = jnp.concatenate([forward[:, SURE:], sure], axis=1)
+    inverse = inverse[SURE:]
 
     def window_piece(piece, flip, step):
         return window_at(piece, forward, inverse, onset_times, line, flip, step)
@@ -544,21 +689,25 @@
         windowed = window(parts, forward, inverse, onset_times, want_spec=last)
         if last:
             upgoing_spec, own = gather_chips(places, windowed, window_piece)
-        else:
-            own, _ = gather_chips(places, windowed)
+            other = [swap_cores(places, side) for side in own]
+            downgoing_spec = correlate_all(own, other, reflection, line)
+            break
+        own, _ = gather_chips(places, windowed)
         half = correlate(own[0], swap_cores(places, own[0]), reflection, line, 0)
         across = [own[1][step] if step in (0, line - 1) else after(own[1][step], half) for step in range(line)]
-        downgoing_spec = correlate(own[1], swap_cores(places, across), reflection, line, 1, half, last)
-        if not last:
-            spectrum_plus = window([downgoing_spec], forward, inverse, onset_times, base=start)
-    other = [swap_cores(places, side) for side in upgoing_spec]
-    upgoing = field(upgoing_spec, other, own_inverse, onset_times, line)
+        downgoing_spec = correlate(own[1], swap_cores(places, across), reflection, line, 1, half)
+        spectrum_plus = window([downgoing_spec], forward, inverse, onset_times, base=start)
+    mine, theirs = half_field(upgoing_spec, chip_inverse, onset_times, line)
+    theirs = places.send(theirs, places.core())
 
     def before_far(piece, flip, step):
-        return upgoing if (flip, step) == (1, 0) else piece
+        return mine if (flip, step) == (1, 0) else piece
 
     own, _ = gather_chips(places, downgoing_spec, before_far)
-    other = [swap_cores(places, side) for side in own]
+    upgoing = merge(mine, theirs, line)
+    other = [swap_cores(places, own[0])]
+    across = [own[1][step] if step in (0, 1, line - 1) else after(own[1][step], upgoing) for step in range(line)]
+    other.append(swap_cores(places, across))
     downgoing = field(own, other, own_inverse, onset_times, line, plus_start)
     return upgoing, downgoing
 

time: 288 us -> 291 us (1.010)
  starting transfers between devices: 73.2 us -> 55.4 us
  waiting for transfers between devices: 107 us -> 121 us
  local copies, waits for them, and re-layouts: 14.8 us -> 19.6 us
    ppermute x80 -> x73, starting transfers between devices: 73.2 us -> 55.4 us  [send(): return lax.ppermute(array, self.axis, pairs)]
    pallas_call x0 -> x3, Pallas kernels: none -> 17.5 us  [the longest x1 14.4 us: correlate_all(): pl.pallas_call(functools.partial(correlate_all_kernel, line), in_specs=[V...]
    pallas_call x4 -> x2, Pallas kernels: 30.8 us -> 15.3 us  [correlate(): pl.pallas_call(functools.partial(correlate_kernel, line, flip, bool(more)...]
    ppermute x80 -> x73, waiting for transfers between devices: 107 us -> 121 us  [send(): return lax.ppermute(array, self.axis, pairs)]
    unnamed x38 -> x54, local copies, waits for them, and re-layouts: 13.2 us -> 16.5 us
    pallas_call x2 -> x1, Pallas kernels: 6.41 us -> 3.76 us  [field(): pl.pallas_call(functools.partial(field_kernel, line, bool(plus)), in_spec...]
  transfers between devices with their start and end apart: 80 -> 73, of which waited for: 34 -> 35; matrix products, arithmetic and copies ran while one was open for 2% -> 3% of each run, Pallas kernels for 16% -> 15%
where the time goes in v7:
time: 291 us; the launch traced here: 290 us
  waiting for transfers between devices  121 us (42%)
  Pallas kernels  86 us (30%)
  starting transfers between devices  55.4 us (19%)
  local copies, waits for them, and re-layouts  19.6 us (7%)
  other arithmetic  7.11 us (2%)
    ppermute x73, waiting for transfers between devices, send(): return lax.ppermute(array, self.axis, pairs)  121 us
    ppermute x73, starting transfers between devices, send(): return lax.ppermute(array, self.axis, pairs)  55.4 us
    pallas_call x2, Pallas kernels, convolve(): pl.pallas_call(functools.partial(convolve_kernel, line), in_specs=[VMEM,...  24.3 us
    pallas_call x8, Pallas kernels, window_at(): pl.pallas_call(functools.partial(window_at_kernel, line, flip, step), in_...  18.5 us
    unnamed x54, local copies, waits for them, and re-layouts  16.5 us
    pallas_call x2, Pallas kernels, correlate(): pl.pallas_call(functools.partial(correlate_kernel, line, flip, bool(more)...  15.3 us
    pallas_call x1, Pallas kernels, correlate_all(): pl.pallas_call(functools.partial(correlate_all_kernel, line), in_specs=[V...  14.4 us
  transfers between devices with their start and end apart: 73, of which 35 were waited for; matrix products, arithmetic and copies ran while one was open for 3% of the time, Pallas kernels for 15%

profile of v7, /device:TPU:0, one launch (start us, length us, event | category | flops | bytes accessed | tf_op | source)
XLA Modules:
  0.0 290.2 jit_solution(5490505674196755470)
XLA Ops:
  0.9 1.6 copy-done
  2.4 1.9 first_analysis.1
  5.0 2.2 collective-permute-done.1
  7.5 3.0 %collective-permute-start.2 = (bf16[16,64,128]{2,1,0:T(8,128)(2,1)S(1)}, bf16[16,64,128]{2,1,0:T(8,128)(2,1)S(1)}, u32[]{:S(2)}, u32[]{:S(2)}) collective-permute-start(bf16[16,64,128]{2,1,0:T(8,128)(2,1)S(1)} %get-tuple-element.66), channel_id=1, source_target_pairs={{0,2},{1,3},{2,0},{3,1},{4,6},{5,7},{6,4},{7,5},{8,10},{9,11},{10,... | collective-permute-start | bytes 786440 | tf_op jit(solution)/shard_map/ppermute | solution.py:51
  10.4 1.6 collective-permute-start.7
  12.5 5.0 %collective-permute-done.2 = bf16[16,64,128]{2,1,0:T(8,128)(2,1)S(1)} collective-permute-done((bf16[16,64,128]{2,1,0:T(8,128)(2,1)S(1)}, bf16[16,64,128]{2,1,0:T(8,128)(2,1)S(1)}, u32[]{:S(2)}, u32[]{:S(2)}) %collective-permute-start.2) | collective-permute-done | bytes 262176 | tf_op jit(solution)/shard_map/ppermute | solution.py:51
  17.6 2.2 collective-permute-start.3
  21.5 1.5 collective-permute-done.5
  23.1 3.8 %collective-permute-done.3 = bf16[16,64,128]{2,1,0:T(8,128)(2,1)S(1)} collective-permute-done((bf16[16,64,128]{2,1,0:T(8,128)(2,1)S(1)}, bf16[16,64,128]{2,1,0:T(8,128)(2,1)S(1)}, u32[]{:S(2)}, u32[]{:S(2)}) %collective-permute-start.3) | collective-permute-done | bytes 262176 | tf_op jit(solution)/shard_map/ppermute | solution.py:51
  27.2 3.8 %collective-permute-start.6 = (bf16[16,64,128]{2,1,0:T(8,128)(2,1)S(1)}, bf16[16,64,128]{2,1,0:T(8,128)(2,1)S(1)}, u32[]{:S(2)}, u32[]{:S(2)}) collective-permute-start(bf16[16,64,128]{2,1,0:T(8,128)(2,1)S(1)} %get-tuple-element.65), channel_id=1, source_target_pairs={{0,12},{1,13},{2,14},{3,15},{4,0},{5,1},{6,2},{7,3},{8,4},{9,5},{1... | collective-permute-start | bytes 786440 | tf_op jit(solution)/shard_map/ppermute | solution.py:51
  31.0 7.0 %collective-permute-done.4 = bf16[16,64,128]{2,1,0:T(8,128)(2,1)S(1)} collective-permute-done((bf16[16,64,128]{2,1,0:T(8,128)(2,1)S(1)}, bf16[16,64,128]{2,1,0:T(8,128)(2,1)S(1)}, u32[]{:S(2)}, u32[]{:S(2)}) %collective-permute-start.4) | collective-permute-done | bytes 262176 | tf_op jit(solution)/shard_map/ppermute | solution.py:51
  39.4 12.6 %convolve.2 = (bf16[4,32,2,16,128]{4,3,2,1,0:T(8,128)(2,1)S(1)}, bf16[4,32,2,16,128]{4,3,2,1,0:T(8,128)(2,1)S(1)}, bf16[4,32,2,16,128]{4,3,2,1,0:T(8,128)(2,1)}, bf16[4,32,2,16,128]{4,3,2,1,0:T(8,128)(2,1)S(1)}) custom-call(bf16[32,2,16,128]{3,2,1,0:T(8,128)(2,1)S(1)} %bitcast.93, bf16[2,32,128,2048]{3,2,1,0:T(8,128)(2,1)} %refs_16_.2), custom_call_target="tpu_custom_call" | custom-call | flops 1073741824 | bytes 37748736 | tf_op jit(solution)/shard_map/convolve/pallas_call | solution.py:223
  52.9 2.6 collective-permute-done.10
  55.5 1.3 fusion.20
  56.8 1.3 collective-permute-start.11
  60.1 6.1 %collective-permute-done.11 = bf16[32,2,16,128]{3,2,1,0:T(8,128)(2,1)} collective-permute-done((bf16[32,2,16,128]{3,2,1,0:T(8,128)(2,1)S(1)}, bf16[32,2,16,128]{3,2,1,0:T(8,128)(2,1)}, u32[]{:S(2)}, u32[]{:S(2)}) %collective-permute-start.11) | collective-permute-done | bytes 262176 | tf_op jit(solution)/shard_map/ppermute | solution.py:51
  70.9 5.0 %collective-permute-done.12 = bf16[32,2,16,128]{3,2,1,0:T(8,128)(2,1)S(1)} collective-permute-done((bf16[32,2,16,128]{3,2,1,0:T(8,128)(2,1)S(1)}, bf16[32,2,16,128]{3,2,1,0:T(8,128)(2,1)S(1)}, u32[]{:S(2)}, u32[]{:S(2)}) %collective-permute-start.12) | collective-permute-done | bytes 262176 | tf_op jit(solution)/shard_map/ppermute | solution.py:51
  75.9 1.2 fusion.5
  77.4 1.8 collective-permute-start.13
  80.2 5.7 %collective-permute-done.15.refs_6_ = bf16[32,2,16,128]{3,2,1,0:T(8,128)(2,1)S(1)} collective-permute-done((bf16[32,2,16,128]{3,2,1,0:T(8,128)(2,1)S(1)}, bf16[32,2,16,128]{3,2,1,0:T(8,128)(2,1)S(1)}, u32[]{:S(2)}, u32[]{:S(2)}) %collective-permute-start.15) | collective-permute-done | bytes 262176 | tf_op jit(solution)/shard_map/ppermute | solution.py:51
  85.9 2.8 collective-permute-done.13.refs_5_
  88.7 2.2 window.3.refs_0_
  91.2 1.4 collective-permute-start.18
  92.6 3.4 %collective-permute-start.23 = (bf16[32,2,16,128]{3,2,1,0:T(8,128)(2,1)S(1)}, bf16[32,2,16,128]{3,2,1,0:T(8,128)(2,1)S(1)}, u32[]{:S(2)}, u32[]{:S(2)}) collective-permute-start(bf16[32,2,16,128]{3,2,1,0:T(8,128)(2,1)S(1)} %window.3.refs_0_), channel_id=1, source_target_pairs={{0,12},{1,13},{2,14},{3,15},{4,0},{5,1},{6,2},{7,3},{8,4},{9,5},{1... | collective-permute-start | bytes 786440 | tf_op jit(solution)/shard_map/ppermute | solution.py:51
  96.0 6.1 %collective-permute-done.20.refs_1_ = bf16[32,2,16,128]{3,2,1,0:T(8,128)(2,1)S(1)} collective-permute-done((bf16[32,2,16,128]{3,2,1,0:T(8,128)(2,1)S(1)}, bf16[32,2,16,128]{3,2,1,0:T(8,128)(2,1)S(1)}, u32[]{:S(2)}, u32[]{:S(2)}) %collective-permute-start.20) | collective-permute-done | bytes 262176 | tf_op jit(solution)/shard_map/ppermute | solution.py:51
  102.8 3.8 %collective-permute-done.23.refs_3_ = bf16[32,2,16,128]{3,2,1,0:T(8,128)(2,1)S(1)} collective-permute-done((bf16[32,2,16,128]{3,2,1,0:T(8,128)(2,1)S(1)}, bf16[32,2,16,128]{3,2,1,0:T(8,128)(2,1)S(1)}, u32[]{:S(2)}, u32[]{:S(2)}) %collective-permute-start.23) | collective-permute-done | bytes 262176 | tf_op jit(solution)/shard_map/ppermute | solution.py:51
  106.7 1.2 collective-permute-start.24
  108.1 2.1 collective-permute-done.21.refs_2_
  111.4 4.4 %collective-permute-done.24.refs_3_ = bf16[32,2,16,128]{3,2,1,0:T(8,128)(2,1)S(1)} collective-permute-done((bf16[32,2,16,128]{3,2,1,0:T(8,128)(2,1)S(1)}, bf16[32,2,16,128]{3,2,1,0:T(8,128)(2,1)S(1)}, u32[]{:S(2)}, u32[]{:S(2)}) %collective-permute-start.24) | collective-permute-done | bytes 262176 | tf_op jit(solution)/shard_map/ppermute | solution.py:51
  116.3 7.6 %correlate0.1.refs_9_ = f32[32,2,16,128]{3,2,1,0:T(8,128)S(1)} custom-call(bf16[32,2,16,128]{3,2,1,0:T(8,128)(2,1)S(1)} %window.3.refs_0_, bf16[32,2,16,128]{3,2,1,0:T(8,128)(2,1)S(1)} %collective-permute-done.20.refs_1_, bf16[32,2,16,128]{3,2,1,0:T(8,128)(2,1)S(1)} %collective-permute-done.21.refs_2_, ...), custom_call_target="tpu_custom_call" | custom-call | flops 536870912 | bytes 18874368 | tf_op jit(solution)/shard_map/correlate0/pallas_call | solution.py:280
  126.0 7.7 %correlate1.1.refs_3_ = f32[32,2,16,128]{3,2,1,0:T(8,128)S(1)} custom-call(bf16[32,2,16,128]{3,2,1,0:T(8,128)(2,1)S(1)} %collective-permute-done.18.refs_0_, bf16[32,2,16,128]{3,2,1,0:T(8,128)(2,1)S(1)} %collective-permute-done.19.refs_1_, bf16[32,2,16,128]{3,2,1,0:T(8,128)(2,1)S(1)} %collective-permute-done.22.refs_2_, ...), custom_call_target="tpu_custom_call" | custom-call | flops 536870912 | bytes 18874368 | tf_op jit(solution)/shard_map/correlate1/pallas_call | solution.py:280
  133.6 2.2 window.4.spec_ref
  135.8 11.7 %convolve.3 = (bf16[4,32,2,16,128]{4,3,2,1,0:T(8,128)(2,1)S(1)}, bf16[4,32,2,16,128]{4,3,2,1,0:T(8,128)(2,1)S(1)}, bf16[4,32,2,16,128]{4,3,2,1,0:T(8,128)(2,1)S(1)}, bf16[4,32,2,16,128]{4,3,2,1,0:T(8,128)(2,1)S(1)}) custom-call(bf16[32,2,16,128]{3,2,1,0:T(8,128)(2,1)S(1)} %window.4.spec_ref, bf16[2,32,128,2048]{3,2,1,0:T(8,128)(2,1)} %refs_16_.2), custom_call_target="tpu_custom_call" | custom-call | flops 1073741824 | bytes 37748736 | tf_op jit(solution)/shard_map/convolve/pallas_call | solution.py:223
  148.1 2.1 collective-permute-done.34
  150.4 1.3 collective-permute-start.35
  153.1 6.6 %collective-permute-done.35 = bf16[32,2,16,128]{3,2,1,0:T(8,128)(2,1)S(1)} collective-permute-done((bf16[32,2,16,128]{3,2,1,0:T(8,128)(2,1)S(1)}, bf16[32,2,16,128]{3,2,1,0:T(8,128)(2,1)S(1)}, u32[]{:S(2)}, u32[]{:S(2)}) %collective-permute-start.35) | collective-permute-done | bytes 262176 | tf_op jit(solution)/shard_map/ppermute | solution.py:51
  162.6 2.7 collective-permute-done.38
  165.2 4.3 %collective-permute-done.36 = bf16[32,2,16,128]{3,2,1,0:T(8,128)(2,1)S(1)} collective-permute-done((bf16[32,2,16,128]{3,2,1,0:T(8,128)(2,1)S(1)}, bf16[32,2,16,128]{3,2,1,0:T(8,128)(2,1)S(1)}, u32[]{:S(2)}, u32[]{:S(2)}) %collective-permute-start.36) | collective-permute-done | bytes 262176 | tf_op jit(solution)/shard_map/ppermute | solution.py:51
  169.8 2.0 collective-permute-start.37
  171.9 8.8 %collective-permute-done.39.refs_6_ = bf16[32,2,16,128]{3,2,1,0:T(8,128)(2,1)S(1)} collective-permute-done((bf16[32,2,16,128]{3,2,1,0:T(8,128)(2,1)S(1)}, bf16[32,2,16,128]{3,2,1,0:T(8,128)(2,1)S(1)}, u32[]{:S(2)}, u32[]{:S(2)}) %collective-permute-start.39) | collective-permute-done | bytes 262176 | tf_op jit(solution)/shard_map/ppermute | solution.py:51
  181.2 1.3 collective-permute-start.43
  182.4 3.8 %collective-permute-start.45 = (bf16[16,64,128]{2,1,0:T(8,128)(2,1)S(1)}, bf16[16,64,128]{2,1,0:T(8,128)(2,1)S(1)}, u32[]{:S(2)}, u32[]{:S(2)}) collective-permute-start(bf16[16,64,128]{2,1,0:T(8,128)(2,1)S(1)} %window.5.spec_ref.refs_0_), channel_id=1, source_target_pairs={{0,12},{1,13},{2,14},{3,15},{4,0},{5,1},{6,2},{7,3},{8,4},{9,5},{1... | collective-permute-start | bytes 786440 | tf_op jit(solution)/shard_map/ppermute | solution.py:51
  186.2 2.1 window_at.8.refs_0_
  188.4 4.2 %collective-permute-done.42.spec_ref.refs_1_ = bf16[16,64,128]{2,1,0:T(8,128)(2,1)S(1)} collective-permute-done((bf16[16,64,128]{2,1,0:T(8,128)(2,1)S(1)}, bf16[16,64,128]{2,1,0:T(8,128)(2,1)S(1)}, u32[]{:S(2)}, u32[]{:S(2)}) %collective-permute-start.42) | collective-permute-done | bytes 262176 | tf_op jit(solution)/shard_map/ppermute | solution.py:51
  192.6 3.3 %collective-permute-done.45.spec_ref.refs_3_ = bf16[16,64,128]{2,1,0:T(8,128)(2,1)S(1)} collective-permute-done((bf16[16,64,128]{2,1,0:T(8,128)(2,1)S(1)}, bf16[16,64,128]{2,1,0:T(8,128)(2,1)S(1)}, u32[]{:S(2)}, u32[]{:S(2)}) %collective-permute-start.45) | collective-permute-done | bytes 262176 | tf_op jit(solution)/shard_map/ppermute | solution.py:51
  196.8 1.4 collective-permute-start.46
  198.2 2.1 window_at.11.refs_3_
  200.9 2.1 window_at.9.refs_4_
  203.0 2.1 window_at.10.refs_1_
  207.2 1.2 collective-permute-start.47
  208.5 3.1 %window_at.12.refs_2_ = bf16[32,2,16,128]{3,2,1,0:T(8,128)(2,1)S(1)} custom-call(bf16[64,448]{1,0:T(8,128)(2,1)S(1)} %pad_maximum_fusion.1.refs_0_.forward_ref, bf16[384,64]{1,0:T(8,128)(2,1)S(1)} %slice.139.refs_1_.inverse_ref, s32[16,2048]{1,0:T(8,128)S(1)} %copy-done.2, bf16[16,64,128]{2,1,0:T(8,128)(2,1)} %collective-permute-done.44.refs_2_.spec_ref), custom_call_target="tpu_custom_call" | custom-call | flops 268435456 | bytes 1572864 | tf_op jit(solution)/shard_map/window_at/pallas_call | solution.py:440
  212.5 2.1 window_at.14.refs_7_
  215.6 2.1 window_at.13.refs_5_
  217.8 2.8 window_at.15.refs_6_
  227.5 1.7 half_field.1
  230.3 14.4 %correlate_all.1.refs_0_ = bf16[16,64,128]{2,1,0:T(8,128)(2,1)S(1)} custom-call(bf16[32,2,16,128]{3,2,1,0:T(8,128)(2,1)S(1)} %window_at.8.refs_0_, bf16[32,2,16,128]{3,2,1,0:T(8,128)(2,1)S(1)} %window_at.10.refs_1_, bf16[32,2,16,128]{3,2,1,0:T(8,128)(2,1)S(1)} %window_at.12.refs_2_, bf16[32,2,16,128]{3,2,1,0:T(8,128)(2,1)S(1)} %window_at.11.refs_3_, ...), custom_call_target="tpu_custom_call" | custom-call | flops 1073741824 | bytes 37748736 | tf_op jit(solution)/shard_map/correlate_all/pallas_call | solution.py:347
  246.3 3.2 %collective-permute-start.61 = (bf16[16,64,128]{2,1,0:T(8,128)(2,1)S(1)}, bf16[16,64,128]{2,1,0:T(8,128)(2,1)S(1)}, u32[]{:S(2)}, u32[]{:S(2)}) collective-permute-start(bf16[16,64,128]{2,1,0:T(8,128)(2,1)S(1)} %correlate_all.1.refs_0_), channel_id=1, source_target_pairs={{0,12},{1,13},{2,14},{3,15},{4,0},{5,1},{6,2},{7,3},{8,4},{9,5},{1... | collective-permute-start | bytes 786440 | tf_op jit(solution)/shard_map/ppermute | solution.py:51
  249.4 4.0 %collective-permute-done.59.refs_4_ = bf16[16,64,128]{2,1,0:T(8,128)(2,1)S(1)} collective-permute-done((bf16[16,64,128]{2,1,0:T(8,128)(2,1)S(1)}, bf16[16,64,128]{2,1,0:T(8,128)(2,1)S(1)}, u32[]{:S(2)}, u32[]{:S(2)}) %collective-permute-start.59) | collective-permute-done | bytes 262176 | tf_op jit(solution)/shard_map/ppermute | solution.py:51
  253.4 3.2 %collective-permute-done.58.refs_1_ = bf16[16,64,128]{2,1,0:T(8,128)(2,1)S(1)} collective-permute-done((bf16[16,64,128]{2,1,0:T(8,128)(2,1)S(1)}, bf16[16,64,128]{2,1,0:T(8,128)(2,1)S(1)}, u32[]{:S(2)}, u32[]{:S(2)}) %collective-permute-start.58) | collective-permute-done | bytes 262176 | tf_op jit(solution)/shard_map/ppermute | solution.py:51
  256.6 3.4 %collective-permute-done.61.refs_3_ = bf16[16,64,128]{2,1,0:T(8,128)(2,1)S(1)} collective-permute-done((bf16[16,64,128]{2,1,0:T(8,128)(2,1)S(1)}, bf16[16,64,128]{2,1,0:T(8,128)(2,1)S(1)}, u32[]{:S(2)}, u32[]{:S(2)}) %collective-permute-start.61) | collective-permute-done | bytes 262176 | tf_op jit(solution)/shard_map/ppermute | solution.py:51
  260.0 7.1 %collective-permute-done.60.refs_2_ = bf16[16,64,128]{2,1,0:T(8,128)(2,1)S(1)} collective-permute-done((bf16[16,64,128]{2,1,0:T(8,128)(2,1)S(1)}, bf16[16,64,128]{2,1,0:T(8,128)(2,1)S(1)}, u32[]{:S(2)}, u32[]{:S(2)}) %collective-permute-start.60) | collective-permute-done | bytes 262176 | tf_op jit(solution)/shard_map/ppermute | solution.py:51
  269.6 6.8 %collective-permute-done.63.refs_6_ = bf16[16,64,128]{2,1,0:T(8,128)(2,1)} collective-permute-done((bf16[16,64,128]{2,1,0:T(8,128)(2,1)S(1)}, bf16[16,64,128]{2,1,0:T(8,128)(2,1)}, u32[]{:S(2)}, u32[]{:S(2)}) %collective-permute-start.63) | collective-permute-done | bytes 262176 | tf_op jit(solution)/shard_map/ppermute | solution.py:51
  276.4 1.4 merge.1
  286.3 3.8 %field.1 = bf16[16,32,2048]{2,1,0:T(8,128)(2,1)} custom-call(bf16[32,64]{1,0:T(8,128)(2,1)S(1)} %bitcast.97, s32[16,2048]{1,0:T(8,128)S(1)} %copy-done.2, bf16[16,64,128]{2,1,0:T(8,128)(2,1)S(1)} %correlate_all.1.refs_0_, bf16[16,64,128]{2,1,0:T(8,128)(2,1)S(1)} %collective-permute-done.58.refs_1_, bf16[16,64,128]{2,1,0:T(8,128)(2,1)S(1)} %collective-permute-done.60.refs_2_, ...), custom_call_target="tpu_custom_call" | custom-call | flops 134217728 | bytes 8388608 | tf_op jit(solution)/shard_map/field/pallas_call | solution.py:573
  (196 shorter events, 50.8 us)
Async XLA Ops:
  4.9 7.7 %collective-permute-start = (bf16[4,16,64,128]{3,2,1,0:T(8,128)(2,1)S(1)}, bf16[4,16,64,128]{3,2,1,0:T(8,128)(2,1)S(1)}, u32[]{:S(2)}, u32[]{:S(2)}) collective-permute-start(bf16[4,16,64,128]{3,2,1,0:T(8,128)(2,1)S(1)} %get-tuple-element.29), channel_id=1, source_target_pairs={{0,1},{1,0},{2,3},{3,2},{4,5},{5,4},{6,7},{7,6},{8,9},{9,8},{10,11... | collective-permute-start | bytes 3145736 | tf_op jit(solution)/shard_map/ppermute | solution.py:51
  7.5 10.0 %collective-permute-start.2 = (bf16[16,64,128]{2,1,0:T(8,128)(2,1)S(1)}, bf16[16,64,128]{2,1,0:T(8,128)(2,1)S(1)}, u32[]{:S(2)}, u32[]{:S(2)}) collective-permute-start(bf16[16,64,128]{2,1,0:T(8,128)(2,1)S(1)} %get-tuple-element.66), channel_id=1, source_target_pairs={{0,2},{1,3},{2,0},{3,1},{4,6},{5,7},{6,4},{7,5},{8,10},{9,11},{10,... | collective-permute-start | bytes 786440 | tf_op jit(solution)/shard_map/ppermute | solution.py:51
  10.4 9.9 %collective-permute-start.7 = (bf16[16,64,128]{2,1,0:T(8,128)(2,1)S(1)}, bf16[16,64,128]{2,1,0:T(8,128)(2,1)S(1)}, u32[]{:S(2)}, u32[]{:S(2)}) collective-permute-start(bf16[16,64,128]{2,1,0:T(8,128)(2,1)S(1)} %get-tuple-element.67), channel_id=1, source_target_pairs={{0,4},{1,5},{2,6},{3,7},{4,8},{5,9},{6,10},{7,11},{8,12},{9,13},{1... | collective-permute-start | bytes 786440 | tf_op jit(solution)/shard_map/ppermute | solution.py:51
  12.0 11.0 %collective-permute-start.5 = (bf16[16,64,128]{2,1,0:T(8,128)(2,1)S(1)}, bf16[16,64,128]{2,1,0:T(8,128)(2,1)S(1)}, u32[]{:S(2)}, u32[]{:S(2)}) collective-permute-start(bf16[16,64,128]{2,1,0:T(8,128)(2,1)S(1)} %get-tuple-element.68), channel_id=1, source_target_pairs={{0,2},{1,3},{2,0},{3,1},{4,6},{5,7},{6,4},{7,5},{8,10},{9,11},{10,... | collective-permute-start | bytes 786440 | tf_op jit(solution)/shard_map/ppermute | solution.py:51
  17.6 9.2 %collective-permute-start.3 = (bf16[16,64,128]{2,1,0:T(8,128)(2,1)S(1)}, bf16[16,64,128]{2,1,0:T(8,128)(2,1)S(1)}, u32[]{:S(2)}, u32[]{:S(2)}) collective-permute-start(bf16[16,64,128]{2,1,0:T(8,128)(2,1)S(1)} %fusion.10), channel_id=1, source_target_pairs={{0,4},{1,5},{2,6},{3,7},{4,8},{5,9},{6,10},{7,11},{8,12},{9,13},{1... | collective-permute-start | bytes 786440 | tf_op jit(solution)/shard_map/ppermute | solution.py:51
  20.5 10.5 %collective-permute-start.8 = (bf16[16,64,128]{2,1,0:T(8,128)(2,1)S(1)}, bf16[16,64,128]{2,1,0:T(8,128)(2,1)S(1)}, u32[]{:S(2)}, u32[]{:S(2)}) collective-permute-start(bf16[16,64,128]{2,1,0:T(8,128)(2,1)S(1)} %fusion.8), channel_id=1, source_target_pairs={{0,2},{1,3},{2,0},{3,1},{4,6},{5,7},{6,4},{7,5},{8,10},{9,11},{10,... | collective-permute-start | bytes 786440 | tf_op jit(solution)/shard_map/ppermute | solution.py:51
  27.1 10.8 %collective-permute-start.4 = (bf16[16,64,128]{2,1,0:T(8,128)(2,1)S(1)}, bf16[16,64,128]{2,1,0:T(8,128)(2,1)S(1)}, u32[]{:S(2)}, u32[]{:S(2)}) collective-permute-start(bf16[16,64,128]{2,1,0:T(8,128)(2,1)S(1)} %get-tuple-element.64), channel_id=1, source_target_pairs={{0,4},{1,5},{2,6},{3,7},{4,8},{5,9},{6,10},{7,11},{8,12},{9,13},{1... | collective-permute-start | bytes 786440 | tf_op jit(solution)/shard_map/ppermute | solution.py:51
  27.2 11.8 %collective-permute-start.6 = (bf16[16,64,128]{2,1,0:T(8,128)(2,1)S(1)}, bf16[16,64,128]{2,1,0:T(8,128)(2,1)S(1)}, u32[]{:S(2)}, u32[]{:S(2)}) collective-permute-start(bf16[16,64,128]{2,1,0:T(8,128)(2,1)S(1)} %get-tuple-element.65), channel_id=1, source_target_pairs={{0,12},{1,13},{2,14},{3,15},{4,0},{5,1},{6,2},{7,3},{8,4},{9,5},{1... | collective-permute-start | bytes 786440 | tf_op jit(solution)/shard_map/ppermute | solution.py:51
  52.0 8.0 %collective-permute-start.9 = (bf16[4,32,2,16,128]{4,3,2,1,0:T(8,128)(2,1)}, bf16[4,32,2,16,128]{4,3,2,1,0:T(8,128)(2,1)}, u32[]{:S(2)}, u32[]{:S(2)}) collective-permute-start(bf16[4,32,2,16,128]{4,3,2,1,0:T(8,128)(2,1)} %get-tuple-element.34), channel_id=1, source_target_pairs={{0,1},{1,0},{2,3},{3,2},{4,5},{5,4},{6,7},{7,6},{8,9},{9,8},{10,11... | collective-permute-start | bytes 3145736 | tf_op jit(solution)/shard_map/ppermute | solution.py:51
  56.8 9.3 %collective-permute-start.11 = (bf16[32,2,16,128]{3,2,1,0:T(8,128)(2,1)S(1)}, bf16[32,2,16,128]{3,2,1,0:T(8,128)(2,1)}, u32[]{:S(2)}, u32[]{:S(2)}) collective-permute-start(bf16[32,2,16,128]{3,2,1,0:T(8,128)(2,1)S(1)} %get-tuple-element.61), channel_id=1, source_target_pairs={{0,2},{1,3},{2,0},{3,1},{4,6},{5,7},{6,4},{7,5},{8,10},{9,11},{10,... | collective-permute-start | bytes 786440 | tf_op jit(solution)/shard_map/ppermute | solution.py:51
  58.6 9.9 %collective-permute-start.16 = (bf16[32,2,16,128]{3,2,1,0:T(8,128)(2,1)S(1)}, bf16[32,2,16,128]{3,2,1,0:T(8,128)(2,1)S(1)}, u32[]{:S(2)}, u32[]{:S(2)}) collective-permute-start(bf16[32,2,16,128]{3,2,1,0:T(8,128)(2,1)S(1)} %get-tuple-element.59), channel_id=1, source_target_pairs={{0,4},{1,5},{2,6},{3,7},{4,8},{5,9},{6,10},{7,11},{8,12},{9,13},{1... | collective-permute-start | bytes 786440 | tf_op jit(solution)/shard_map/ppermute | solution.py:51
  59.6 11.3 %collective-permute-start.14 = (bf16[32,2,16,128]{3,2,1,0:T(8,128)(2,1)S(1)}, bf16[32,2,16,128]{3,2,1,0:T(8,128)(2,1)S(1)}, u32[]{:S(2)}, u32[]{:S(2)}) collective-permute-start(bf16[32,2,16,128]{3,2,1,0:T(8,128)(2,1)S(1)} %get-tuple-element.60), channel_id=1, source_target_pairs={{0,2},{1,3},{2,0},{3,1},{4,6},{5,7},{6,4},{7,5},{8,10},{9,11},{10,... | collective-permute-start | bytes 786440 | tf_op jit(solution)/shard_map/ppermute | solution.py:51
  67.3 8.6 %collective-permute-start.12 = (bf16[32,2,16,128]{3,2,1,0:T(8,128)(2,1)S(1)}, bf16[32,2,16,128]{3,2,1,0:T(8,128)(2,1)S(1)}, u32[]{:S(2)}, u32[]{:S(2)}) collective-permute-start(bf16[32,2,16,128]{3,2,1,0:T(8,128)(2,1)S(1)} %fusion.6), channel_id=1, source_target_pairs={{0,4},{1,5},{2,6},{3,7},{4,8},{5,9},{6,10},{7,11},{8,12},{9,13},{1... | collective-permute-start | bytes 786440 | tf_op jit(solution)/shard_map/ppermute | solution.py:51
  69.6 10.6 %collective-permute-start.17 = (bf16[32,2,16,128]{3,2,1,0:T(8,128)(2,1)S(1)}, bf16[32,2,16,128]{3,2,1,0:T(8,128)(2,1)S(1)}, u32[]{:S(2)}, u32[]{:S(2)}) collective-permute-start(bf16[32,2,16,128]{3,2,1,0:T(8,128)(2,1)S(1)} %fusion.4), channel_id=1, source_target_pairs={{0,2},{1,3},{2,0},{3,1},{4,6},{5,7},{6,4},{7,5},{8,10},{9,11},{10,... | collective-permute-start | bytes 786440 | tf_op jit(solution)/shard_map/ppermute | solution.py:51
  77.1 8.8 %collective-permute-start.15 = (bf16[32,2,16,128]{3,2,1,0:T(8,128)(2,1)S(1)}, bf16[32,2,16,128]{3,2,1,0:T(8,128)(2,1)S(1)}, u32[]{:S(2)}, u32[]{:S(2)}) collective-permute-start(bf16[32,2,16,128]{3,2,1,0:T(8,128)(2,1)S(1)} %get-tuple-element.62), channel_id=1, source_target_pairs={{0,12},{1,13},{2,14},{3,15},{4,0},{5,1},{6,2},{7,3},{8,4},{9,5},{1... | collective-permute-start | bytes 786440 | tf_op jit(solution)/shard_map/ppermute | solution.py:51
  77.4 11.2 %collective-permute-start.13 = (bf16[32,2,16,128]{3,2,1,0:T(8,128)(2,1)S(1)}, bf16[32,2,16,128]{3,2,1,0:T(8,128)(2,1)S(1)}, u32[]{:S(2)}, u32[]{:S(2)}) collective-permute-start(bf16[32,2,16,128]{3,2,1,0:T(8,128)(2,1)S(1)} %get-tuple-element.63), channel_id=1, source_target_pairs={{0,4},{1,5},{2,6},{3,7},{4,8},{5,9},{6,10},{7,11},{8,12},{9,13},{1... | collective-permute-start | bytes 786440 | tf_op jit(solution)/shard_map/ppermute | solution.py:51
  90.9 11.1 %collective-permute-start.20 = (bf16[32,2,16,128]{3,2,1,0:T(8,128)(2,1)S(1)}, bf16[32,2,16,128]{3,2,1,0:T(8,128)(2,1)S(1)}, u32[]{:S(2)}, u32[]{:S(2)}) collective-permute-start(bf16[32,2,16,128]{3,2,1,0:T(8,128)(2,1)S(1)} %window.3.refs_0_), channel_id=1, source_target_pairs={{0,4},{1,5},{2,6},{3,7},{4,8},{5,9},{6,10},{7,11},{8,12},{9,13},{1... | collective-permute-start | bytes 786440 | tf_op jit(solution)/shard_map/ppermute | solution.py:51
  91.2 10.8 %collective-permute-start.18 = (bf16[32,2,16,128]{3,2,1,0:T(8,128)(2,1)S(1)}, bf16[32,2,16,128]{3,2,1,0:T(8,128)(2,1)S(1)}, u32[]{:S(2)}, u32[]{:S(2)}) collective-permute-start(bf16[32,2,16,128]{3,2,1,0:T(8,128)(2,1)S(1)} %window.3.refs_0_), channel_id=1, source_target_pairs={{0,2},{1,3},{2,0},{3,1},{4,6},{5,7},{6,4},{7,5},{8,10},{9,11},{10,... | collective-permute-start | bytes 786440 | tf_op jit(solution)/shard_map/ppermute | solution.py:51
  92.6 14.1 %collective-permute-start.23 = (bf16[32,2,16,128]{3,2,1,0:T(8,128)(2,1)S(1)}, bf16[32,2,16,128]{3,2,1,0:T(8,128)(2,1)S(1)}, u32[]{:S(2)}, u32[]{:S(2)}) collective-permute-start(bf16[32,2,16,128]{3,2,1,0:T(8,128)(2,1)S(1)} %window.3.refs_0_), channel_id=1, source_target_pairs={{0,12},{1,13},{2,14},{3,15},{4,0},{5,1},{6,2},{7,3},{8,4},{9,5},{1... | collective-permute-start | bytes 786440 | tf_op jit(solution)/shard_map/ppermute | solution.py:51
  102.0 8.2 %collective-permute-start.21 = (bf16[32,2,16,128]{3,2,1,0:T(8,128)(2,1)S(1)}, bf16[32,2,16,128]{3,2,1,0:T(8,128)(2,1)S(1)}, u32[]{:S(2)}, u32[]{:S(2)}) collective-permute-start(bf16[32,2,16,128]{3,2,1,0:T(8,128)(2,1)S(1)} %collective-permute-done.20.refs_1_), channel_id=1, source_target_pairs={{0,4},{1,5},{2,6},{3,7},{4,8},{5,9},{6,10},{7,11},{8,12},{9,13},{1... | collective-permute-start | bytes 786440 | tf_op jit(solution)/shard_map/ppermute | solution.py:51
  102.8 7.4 %collective-permute-start.26 = (bf16[32,2,16,128]{3,2,1,0:T(8,128)(2,1)S(1)}, bf16[32,2,16,128]{3,2,1,0:T(8,128)(2,1)S(1)}, u32[]{:S(2)}, u32[]{:S(2)}) collective-permute-start(bf16[32,2,16,128]{3,2,1,0:T(8,128)(2,1)S(1)} %window.3.refs_0_), channel_id=1, source_target_pairs={{0,1},{1,0},{2,3},{3,2},{4,5},{5,4},{6,7},{7,6},{8,9},{9,8},{10,11... | collective-permute-start | bytes 786440 | tf_op jit(solution)/shard_map/ppermute | solution.py:51
  106.7 4.7 %collective-permute-start.29 = (bf16[32,2,16,128]{3,2,1,0:T(8,128)(2,1)S(1)}, bf16[32,2,16,128]{3,2,1,0:T(8,128)(2,1)S(1)}, u32[]{:S(2)}, u32[]{:S(2)}) collective-permute-start(bf16[32,2,16,128]{3,2,1,0:T(8,128)(2,1)S(1)} %collective-permute-done.23.refs_3_), channel_id=1, source_target_pairs={{0,1},{1,0},{2,3},{3,2},{4,5},{5,4},{6,7},{7,6},{8,9},{9,8},{10,11... | collective-permute-start | bytes 786440 | tf_op jit(solution)/shard_map/ppermute | solution.py:51
  106.7 9.1 %collective-permute-start.24 = (bf16[32,2,16,128]{3,2,1,0:T(8,128)(2,1)S(1)}, bf16[32,2,16,128]{3,2,1,0:T(8,128)(2,1)S(1)}, u32[]{:S(2)}, u32[]{:S(2)}) collective-permute-start(bf16[32,2,16,128]{3,2,1,0:T(8,128)(2,1)S(1)} %collective-permute-done.23.refs_3_), channel_id=1, source_target_pairs={{0,2},{1,3},{2,0},{3,1},{4,6},{5,7},{6,4},{7,5},{8,10},{9,11},{10,... | collective-permute-start | bytes 786440 | tf_op jit(solution)/shard_map/ppermute | solution.py:51
  107.9 7.9 %collective-permute-start.27 = (bf16[32,2,16,128]{3,2,1,0:T(8,128)(2,1)S(1)}, bf16[32,2,16,128]{3,2,1,0:T(8,128)(2,1)S(1)}, u32[]{:S(2)}, u32[]{:S(2)}) collective-permute-start(bf16[32,2,16,128]{3,2,1,0:T(8,128)(2,1)S(1)} %collective-permute-done.20.refs_1_), channel_id=1, source_target_pairs={{0,1},{1,0},{2,3},{3,2},{4,5},{5,4},{6,7},{7,6},{8,9},{9,8},{10,11... | collective-permute-start | bytes 786440 | tf_op jit(solution)/shard_map/ppermute | solution.py:51
  110.2 6.1 %collective-permute-start.28 = (bf16[32,2,16,128]{3,2,1,0:T(8,128)(2,1)S(1)}, bf16[32,2,16,128]{3,2,1,0:T(8,128)(2,1)S(1)}, u32[]{:S(2)}, u32[]{:S(2)}) collective-permute-start(bf16[32,2,16,128]{3,2,1,0:T(8,128)(2,1)S(1)} %collective-permute-done.21.refs_2_), channel_id=1, source_target_pairs={{0,1},{1,0},{2,3},{3,2},{4,5},{5,4},{6,7},{7,6},{8,9},{9,8},{10,11... | collective-permute-start | bytes 786440 | tf_op jit(solution)/shard_map/ppermute | solution.py:51
  110.2 13.8 %collective-permute-start.22 = (bf16[32,2,16,128]{3,2,1,0:T(8,128)(2,1)S(1)}, bf16[32,2,16,128]{3,2,1,0:T(8,128)(2,1)S(1)}, u32[]{:S(2)}, u32[]{:S(2)}) collective-permute-start(bf16[32,2,16,128]{3,2,1,0:T(8,128)(2,1)S(1)} %collective-permute-done.21.refs_2_), channel_id=1, source_target_pairs={{0,2},{1,3},{2,0},{3,1},{4,6},{5,7},{6,4},{7,5},{8,10},{9,11},{10,... | collective-permute-start | bytes 786440 | tf_op jit(solution)/shard_map/ppermute | solution.py:51
  111.4 12.7 %collective-permute-start.19 = (bf16[32,2,16,128]{3,2,1,0:T(8,128)(2,1)S(1)}, bf16[32,2,16,128]{3,2,1,0:T(8,128)(2,1)S(1)}, u32[]{:S(2)}, u32[]{:S(2)}) collective-permute-start(bf16[32,2,16,128]{3,2,1,0:T(8,128)(2,1)S(1)} %collective-permute-done.18.refs_0_), channel_id=1, source_target_pairs={{0,4},{1,5},{2,6},{3,7},{4,8},{5,9},{6,10},{7,11},{8,12},{9,13},{1... | collective-permute-start | bytes 786440 | tf_op jit(solution)/shard_map/ppermute | solution.py:51
  115.8 8.8 %collective-permute-start.25 = (bf16[32,2,16,128]{3,2,1,0:T(8,128)(2,1)S(1)}, bf16[32,2,16,128]{3,2,1,0:T(8,128)(2,1)S(1)}, u32[]{:S(2)}, u32[]{:S(2)}) collective-permute-start(bf16[32,2,16,128]{3,2,1,0:T(8,128)(2,1)S(1)} %collective-permute-done.18.refs_0_), channel_id=1, source_target_pairs={{0,1},{1,0},{2,3},{3,2},{4,5},{5,4},{6,7},{7,6},{8,9},{9,8},{10,11... | collective-permute-start | bytes 786440 | tf_op jit(solution)/shard_map/ppermute | solution.py:51
  115.8 8.8 %collective-permute-start.32 = (bf16[32,2,16,128]{3,2,1,0:T(8,128)(2,1)S(1)}, bf16[32,2,16,128]{3,2,1,0:T(8,128)(2,1)S(1)}, u32[]{:S(2)}, u32[]{:S(2)}) collective-permute-start(bf16[32,2,16,128]{3,2,1,0:T(8,128)(2,1)S(1)} %collective-permute-done.24.refs_3_), channel_id=1, source_target_pairs={{0,1},{1,0},{2,3},{3,2},{4,5},{5,4},{6,7},{7,6},{8,9},{9,8},{10,11... | collective-permute-start | bytes 786440 | tf_op jit(solution)/shard_map/ppermute | solution.py:51
  147.7 5.4 %collective-permute-start.33 = (bf16[4,32,2,16,128]{4,3,2,1,0:T(8,128)(2,1)S(1)}, bf16[4,32,2,16,128]{4,3,2,1,0:T(8,128)(2,1)S(1)}, u32[]{:S(2)}, u32[]{:S(2)}) collective-permute-start(bf16[4,32,2,16,128]{4,3,2,1,0:T(8,128)(2,1)S(1)} %get-tuple-element.42), channel_id=1, source_target_pairs={{0,1},{1,0},{2,3},{3,2},{4,5},{5,4},{6,7},{7,6},{8,9},{9,8},{10,11... | collective-permute-start | bytes 3145736 | tf_op jit(solution)/shard_map/ppermute | solution.py:51
  150.4 9.2 %collective-permute-start.35 = (bf16[32,2,16,128]{3,2,1,0:T(8,128)(2,1)S(1)}, bf16[32,2,16,128]{3,2,1,0:T(8,128)(2,1)S(1)}, u32[]{:S(2)}, u32[]{:S(2)}) collective-permute-start(bf16[32,2,16,128]{3,2,1,0:T(8,128)(2,1)S(1)} %get-tuple-element.56), channel_id=1, source_target_pairs={{0,2},{1,3},{2,0},{3,1},{4,6},{5,7},{6,4},{7,5},{8,10},{9,11},{10,... | collective-permute-start | bytes 786440 | tf_op jit(solution)/shard_map/ppermute | solution.py:51
  151.7 9.9 %collective-permute-start.40 = (bf16[32,2,16,128]{3,2,1,0:T(8,128)(2,1)S(1)}, bf16[32,2,16,128]{3,2,1,0:T(8,128)(2,1)S(1)}, u32[]{:S(2)}, u32[]{:S(2)}) collective-permute-start(bf16[32,2,16,128]{3,2,1,0:T(8,128)(2,1)S(1)} %get-tuple-element.54), channel_id=1, source_target_pairs={{0,4},{1,5},{2,6},{3,7},{4,8},{5,9},{6,10},{7,11},{8,12},{9,13},{1... | collective-permute-start | bytes 786440 | tf_op jit(solution)/shard_map/ppermute | solution.py:51
  152.2 13.0 %collective-permute-start.38 = (bf16[32,2,16,128]{3,2,1,0:T(8,128)(2,1)S(1)}, bf16[32,2,16,128]{3,2,1,0:T(8,128)(2,1)S(1)}, u32[]{:S(2)}, u32[]{:S(2)}) collective-permute-start(bf16[32,2,16,128]{3,2,1,0:T(8,128)(2,1)S(1)} %get-tuple-element.55), channel_id=1, source_target_pairs={{0,2},{1,3},{2,0},{3,1},{4,6},{5,7},{6,4},{7,5},{8,10},{9,11},{10,... | collective-permute-start | bytes 786440 | tf_op jit(solution)/shard_map/ppermute | solution.py:51
  159.7 9.8 %collective-permute-start.36 = (bf16[32,2,16,128]{3,2,1,0:T(8,128)(2,1)S(1)}, bf16[32,2,16,128]{3,2,1,0:T(8,128)(2,1)S(1)}, u32[]{:S(2)}, u32[]{:S(2)}) collective-permute-start(bf16[32,2,16,128]{3,2,1,0:T(8,128)(2,1)S(1)} %fusion.2), channel_id=1, source_target_pairs={{0,4},{1,5},{2,6},{3,7},{4,8},{5,9},{6,10},{7,11},{8,12},{9,13},{1... | collective-permute-start | bytes 786440 | tf_op jit(solution)/shard_map/ppermute | solution.py:51
  161.6 10.2 %collective-permute-start.41 = (bf16[32,2,16,128]{3,2,1,0:T(8,128)(2,1)S(1)}, bf16[32,2,16,128]{3,2,1,0:T(8,128)(2,1)S(1)}, u32[]{:S(2)}, u32[]{:S(2)}) collective-permute-start(bf16[32,2,16,128]{3,2,1,0:T(8,128)(2,1)S(1)} %fusion), channel_id=1, source_target_pairs={{0,2},{1,3},{2,0},{3,1},{4,6},{5,7},{6,4},{7,5},{8,10},{9,11},{10,... | collective-permute-start | bytes 786440 | tf_op jit(solution)/shard_map/ppermute | solution.py:51
  169.8 11.0 %collective-permute-start.39 = (bf16[32,2,16,128]{3,2,1,0:T(8,128)(2,1)S(1)}, bf16[32,2,16,128]{3,2,1,0:T(8,128)(2,1)S(1)}, u32[]{:S(2)}, u32[]{:S(2)}) collective-permute-start(bf16[32,2,16,128]{3,2,1,0:T(8,128)(2,1)S(1)} %get-tuple-element.57), channel_id=1, source_target_pairs={{0,12},{1,13},{2,14},{3,15},{4,0},{5,1},{6,2},{7,3},{8,4},{9,5},{1... | collective-permute-start | bytes 786440 | tf_op jit(solution)/shard_map/ppermute | solution.py:51
  169.8 10.9 %collective-permute-start.37 = (bf16[32,2,16,128]{3,2,1,0:T(8,128)(2,1)S(1)}, bf16[32,2,16,128]{3,2,1,0:T(8,128)(2,1)S(1)}, u32[]{:S(2)}, u32[]{:S(2)}) collective-permute-start(bf16[32,2,16,128]{3,2,1,0:T(8,128)(2,1)S(1)} %get-tuple-element.58), channel_id=1, source_target_pairs={{0,4},{1,5},{2,6},{3,7},{4,8},{5,9},{6,10},{7,11},{8,12},{9,13},{1... | collective-permute-start | bytes 786440 | tf_op jit(solution)/shard_map/ppermute | solution.py:51
  181.2 7.2 %collective-permute-start.43 = (bf16[16,64,128]{2,1,0:T(8,128)(2,1)S(1)}, bf16[16,64,128]{2,1,0:T(8,128)(2,1)S(1)}, u32[]{:S(2)}, u32[]{:S(2)}) collective-permute-start(bf16[16,64,128]{2,1,0:T(8,128)(2,1)S(1)} %window.5.spec_ref.refs_0_), channel_id=1, source_target_pairs={{0,2},{1,3},{2,0},{3,1},{4,6},{5,7},{6,4},{7,5},{8,10},{9,11},{10,... | collective-permute-start | bytes 786440 | tf_op jit(solution)/shard_map/ppermute | solution.py:51
  182.4 10.2 %collective-permute-start.42 = (bf16[16,64,128]{2,1,0:T(8,128)(2,1)S(1)}, bf16[16,64,128]{2,1,0:T(8,128)(2,1)S(1)}, u32[]{:S(2)}, u32[]{:S(2)}) collective-permute-start(bf16[16,64,128]{2,1,0:T(8,128)(2,1)S(1)} %window.5.spec_ref.refs_0_), channel_id=1, source_target_pairs={{0,4},{1,5},{2,6},{3,7},{4,8},{5,9},{6,10},{7,11},{8,12},{9,13},{1... | collective-permute-start | bytes 786440 | tf_op jit(solution)/shard_map/ppermute | solution.py:51
  182.4 13.5 %collective-permute-start.45 = (bf16[16,64,128]{2,1,0:T(8,128)(2,1)S(1)}, bf16[16,64,128]{2,1,0:T(8,128)(2,1)S(1)}, u32[]{:S(2)}, u32[]{:S(2)}) collective-permute-start(bf16[16,64,128]{2,1,0:T(8,128)(2,1)S(1)} %window.5.spec_ref.refs_0_), channel_id=1, source_target_pairs={{0,12},{1,13},{2,14},{3,15},{4,0},{5,1},{6,2},{7,3},{8,4},{9,5},{1... | collective-permute-start | bytes 786440 | tf_op jit(solution)/shard_map/ppermute | solution.py:51
  192.6 12.5 %collective-permute-start.44 = (bf16[16,64,128]{2,1,0:T(8,128)(2,1)S(1)}, bf16[16,64,128]{2,1,0:T(8,128)(2,1)}, u32[]{:S(2)}, u32[]{:S(2)}) collective-permute-start(bf16[16,64,128]{2,1,0:T(8,128)(2,1)S(1)} %collective-permute-done.42.spec_ref.refs_1_), channel_id=1, source_target_pairs={{0,4},{1,5},{2,6},{3,7},{4,8},{5,9},{6,10},{7,11},{8,12},{9,13},{1... | collective-permute-start | bytes 786440 | tf_op jit(solution)/shard_map/ppermute | solution.py:51
  195.9 9.3 %collective-permute-start.48 = (bf16[16,64,128]{2,1,0:T(8,128)(2,1)S(1)}, bf16[16,64,128]{2,1,0:T(8,128)(2,1)S(1)}, u32[]{:S(2)}, u32[]{:S(2)}) collective-permute-start(bf16[16,64,128]{2,1,0:T(8,128)(2,1)S(1)} %collective-permute-done.45.spec_ref.refs_3_), channel_id=1, source_target_pairs={{0,2},{1,3},{2,0},{3,1},{4,6},{5,7},{6,4},{7,5},{8,10},{9,11},{10,... | collective-permute-start | bytes 786440 | tf_op jit(solution)/shard_map/ppermute | solution.py:51
  196.8 9.7 %collective-permute-start.46 = (bf16[16,64,128]{2,1,0:T(8,128)(2,1)S(1)}, bf16[16,64,128]{2,1,0:T(8,128)(2,1)S(1)}, u32[]{:S(2)}, u32[]{:S(2)}) collective-permute-start(bf16[16,64,128]{2,1,0:T(8,128)(2,1)S(1)} %collective-permute-done.43.spec_ref.refs_4_), channel_id=1, source_target_pairs={{0,4},{1,5},{2,6},{3,7},{4,8},{5,9},{6,10},{7,11},{8,12},{9,13},{1... | collective-permute-start | bytes 786440 | tf_op jit(solution)/shard_map/ppermute | solution.py:51
  198.2 22.4 %collective-permute-start.50 = (bf16[32,2,16,128]{3,2,1,0:T(8,128)(2,1)S(1)}, bf16[32,2,16,128]{3,2,1,0:T(8,128)(2,1)S(1)}, u32[]{:S(2)}, u32[]{:S(2)}) collective-permute-start(bf16[32,2,16,128]{3,2,1,0:T(8,128)(2,1)S(1)} %window_at.8.refs_0_), channel_id=1, source_target_pairs={{0,1},{1,0},{2,3},{3,2},{4,5},{5,4},{6,7},{7,6},{8,9},{9,8},{10,11... | collective-permute-start | bytes 786440 | tf_op jit(solution)/shard_map/ppermute | solution.py:51
  200.3 20.8 %collective-permute-start.53 = (bf16[32,2,16,128]{3,2,1,0:T(8,128)(2,1)S(1)}, bf16[32,2,16,128]{3,2,1,0:T(8,128)(2,1)S(1)}, u32[]{:S(2)}, u32[]{:S(2)}) collective-permute-start(bf16[32,2,16,128]{3,2,1,0:T(8,128)(2,1)S(1)} %window_at.11.refs_3_), channel_id=1, source_target_pairs={{0,1},{1,0},{2,3},{3,2},{4,5},{5,4},{6,7},{7,6},{8,9},{9,8},{10,11... | collective-permute-start | bytes 786440 | tf_op jit(solution)/shard_map/ppermute | solution.py:51
  205.2 16.0 %collective-permute-start.54 = (bf16[32,2,16,128]{3,2,1,0:T(8,128)(2,1)S(1)}, bf16[32,2,16,128]{3,2,1,0:T(8,128)(2,1)S(1)}, u32[]{:S(2)}, u32[]{:S(2)}) collective-permute-start(bf16[32,2,16,128]{3,2,1,0:T(8,128)(2,1)S(1)} %window_at.9.refs_4_), channel_id=1, source_target_pairs={{0,1},{1,0},{2,3},{3,2},{4,5},{5,4},{6,7},{7,6},{8,9},{9,8},{10,11... | collective-permute-start | bytes 786440 | tf_op jit(solution)/shard_map/ppermute | solution.py:51
  206.0 23.2 %collective-permute-start.51 = (bf16[32,2,16,128]{3,2,1,0:T(8,128)(2,1)S(1)}, bf16[32,2,16,128]{3,2,1,0:T(8,128)(2,1)S(1)}, u32[]{:S(2)}, u32[]{:S(2)}) collective-permute-start(bf16[32,2,16,128]{3,2,1,0:T(8,128)(2,1)S(1)} %window_at.10.refs_1_), channel_id=1, source_target_pairs={{0,1},{1,0},{2,3},{3,2},{4,5},{5,4},{6,7},{7,6},{8,9},{9,8},{10,11... | collective-permute-start | bytes 786440 | tf_op jit(solution)/shard_map/ppermute | solution.py:51
  207.2 10.6 %collective-permute-start.47 = (bf16[16,64,128]{2,1,0:T(8,128)(2,1)}, bf16[16,64,128]{2,1,0:T(8,128)(2,1)S(1)}, u32[]{:S(2)}, u32[]{:S(2)}) collective-permute-start(bf16[16,64,128]{2,1,0:T(8,128)(2,1)} %collective-permute-done.44.refs_2_.spec_ref), channel_id=1, source_target_pairs={{0,2},{1,3},{2,0},{3,1},{4,6},{5,7},{6,4},{7,5},{8,10},{9,11},{10,... | collective-permute-start | bytes 786440 | tf_op jit(solution)/shard_map/ppermute | solution.py:51
  217.7 11.5 %collective-permute-start.57 = (bf16[32,2,16,128]{3,2,1,0:T(8,128)(2,1)S(1)}, bf16[32,2,16,128]{3,2,1,0:T(8,128)(2,1)}, u32[]{:S(2)}, u32[]{:S(2)}) collective-permute-start(bf16[32,2,16,128]{3,2,1,0:T(8,128)(2,1)S(1)} %window_at.14.refs_7_), channel_id=1, source_target_pairs={{0,1},{1,0},{2,3},{3,2},{4,5},{5,4},{6,7},{7,6},{8,9},{9,8},{10,11... | collective-permute-start | bytes 786440 | tf_op jit(solution)/shard_map/ppermute | solution.py:51
  220.6 8.7 %collective-permute-start.55 = (bf16[32,2,16,128]{3,2,1,0:T(8,128)(2,1)S(1)}, bf16[32,2,16,128]{3,2,1,0:T(8,128)(2,1)}, u32[]{:S(2)}, u32[]{:S(2)}) collective-permute-start(bf16[32,2,16,128]{3,2,1,0:T(8,128)(2,1)S(1)} %window_at.13.refs_5_), channel_id=1, source_target_pairs={{0,1},{1,0},{2,3},{3,2},{4,5},{5,4},{6,7},{7,6},{8,9},{9,8},{10,11... | collective-permute-start | bytes 786440 | tf_op jit(solution)/shard_map/ppermute | solution.py:51
  221.1 8.2 %collective-permute-start.52 = (bf16[32,2,16,128]{3,2,1,0:T(8,128)(2,1)S(1)}, bf16[32,2,16,128]{3,2,1,0:T(8,128)(2,1)}, u32[]{:S(2)}, u32[]{:S(2)}) collective-permute-start(bf16[32,2,16,128]{3,2,1,0:T(8,128)(2,1)S(1)} %window_at.12.refs_2_), channel_id=1, source_target_pairs={{0,1},{1,0},{2,3},{3,2},{4,5},{5,4},{6,7},{7,6},{8,9},{9,8},{10,11... | collective-permute-start | bytes 786440 | tf_op jit(solution)/shard_map/ppermute | solution.py:51
  221.2 8.1 %collective-permute-start.56 = (bf16[32,2,16,128]{3,2,1,0:T(8,128)(2,1)}, bf16[32,2,16,128]{3,2,1,0:T(8,128)(2,1)}, u32[]{:S(2)}, u32[]{:S(2)}) collective-permute-start(bf16[32,2,16,128]{3,2,1,0:T(8,128)(2,1)} %window_at.15.refs_6_), channel_id=1, source_target_pairs={{0,1},{1,0},{2,3},{3,2},{4,5},{5,4},{6,7},{7,6},{8,9},{9,8},{10,11... | collective-permute-start | bytes 786440 | tf_op jit(solution)/shard_map/ppermute | solution.py:51
  229.2 40.5 %collective-permute-start.49 = (bf16[16,32,1024]{2,1,0:T(8,128)(2,1)S(1)}, bf16[16,32,1024]{2,1,0:T(8,128)(2,1)S(1)}, u32[]{:S(2)}, u32[]{:S(2)}) collective-permute-start(bf16[16,32,1024]{2,1,0:T(8,128)(2,1)S(1)} %get-tuple-element.49), channel_id=1, source_target_pairs={{0,1},{1,0},{2,3},{3,2},{4,5},{5,4},{6,7},{7,6},{8,9},{9,8},{10,11... | collective-permute-start | bytes 3145736 | tf_op jit(solution)/shard_map/ppermute | solution.py:51
  244.7 8.7 %collective-permute-start.59 = (bf16[16,64,128]{2,1,0:T(8,128)(2,1)S(1)}, bf16[16,64,128]{2,1,0:T(8,128)(2,1)S(1)}, u32[]{:S(2)}, u32[]{:S(2)}) collective-permute-start(bf16[16,64,128]{2,1,0:T(8,128)(2,1)S(1)} %correlate_all.1.refs_0_), channel_id=1, source_target_pairs={{0,2},{1,3},{2,0},{3,1},{4,6},{5,7},{6,4},{7,5},{8,10},{9,11},{10,... | collective-permute-start | bytes 786440 | tf_op jit(solution)/shard_map/ppermute | solution.py:51
  245.6 11.0 %collective-permute-start.58 = (bf16[16,64,128]{2,1,0:T(8,128)(2,1)S(1)}, bf16[16,64,128]{2,1,0:T(8,128)(2,1)S(1)}, u32[]{:S(2)}, u32[]{:S(2)}) collective-permute-start(bf16[16,64,128]{2,1,0:T(8,128)(2,1)S(1)} %correlate_all.1.refs_0_), channel_id=1, source_target_pairs={{0,4},{1,5},{2,6},{3,7},{4,8},{5,9},{6,10},{7,11},{8,12},{9,13},{1... | collective-permute-start | bytes 786440 | tf_op jit(solution)/shard_map/ppermute | solution.py:51
  246.3 13.7 %collective-permute-start.61 = (bf16[16,64,128]{2,1,0:T(8,128)(2,1)S(1)}, bf16[16,64,128]{2,1,0:T(8,128)(2,1)S(1)}, u32[]{:S(2)}, u32[]{:S(2)}) collective-permute-start(bf16[16,64,128]{2,1,0:T(8,128)(2,1)S(1)} %correlate_all.1.refs_0_), channel_id=1, source_target_pairs={{0,12},{1,13},{2,14},{3,15},{4,0},{5,1},{6,2},{7,3},{8,4},{9,5},{1... | collective-permute-start | bytes 786440 | tf_op jit(solution)/shard_map/ppermute | solution.py:51
  256.6 10.5 %collective-permute-start.60 = (bf16[16,64,128]{2,1,0:T(8,128)(2,1)S(1)}, bf16[16,64,128]{2,1,0:T(8,128)(2,1)S(1)}, u32[]{:S(2)}, u32[]{:S(2)}) collective-permute-start(bf16[16,64,128]{2,1,0:T(8,128)(2,1)S(1)} %collective-permute-done.58.refs_1_), channel_id=1, source_target_pairs={{0,4},{1,5},{2,6},{3,7},{4,8},{5,9},{6,10},{7,11},{8,12},{9,13},{1... | collective-permute-start | bytes 786440 | tf_op jit(solution)/shard_map/ppermute | solution.py:51
  267.1 9.3 %collective-permute-start.63 = (bf16[16,64,128]{2,1,0:T(8,128)(2,1)S(1)}, bf16[16,64,128]{2,1,0:T(8,128)(2,1)}, u32[]{:S(2)}, u32[]{:S(2)}) collective-permute-start(bf16[16,64,128]{2,1,0:T(8,128)(2,1)S(1)} %collective-permute-done.60.refs_2_), channel_id=1, source_target_pairs={{0,2},{1,3},{2,0},{3,1},{4,6},{5,7},{6,4},{7,5},{8,10},{9,11},{10,... | collective-permute-start | bytes 786440 | tf_op jit(solution)/shard_map/ppermute | solution.py:51
  268.2 9.6 %collective-permute-start.65 = (bf16[16,64,128]{2,1,0:T(8,128)(2,1)S(1)}, bf16[16,64,128]{2,1,0:T(8,128)(2,1)S(1)}, u32[]{:S(2)}, u32[]{:S(2)}) collective-permute-start(bf16[16,64,128]{2,1,0:T(8,128)(2,1)S(1)} %correlate_all.1.refs_0_), channel_id=1, source_target_pairs={{0,1},{1,0},{2,3},{3,2},{4,5},{5,4},{6,7},{7,6},{8,9},{9,8},{10,11... | collective-permute-start | bytes 786440 | tf_op jit(solution)/shard_map/ppermute | solution.py:51
  268.2 10.8 %collective-permute-start.68 = (bf16[16,64,128]{2,1,0:T(8,128)(2,1)S(1)}, bf16[16,64,128]{2,1,0:T(8,128)(2,1)S(1)}, u32[]{:S(2)}, u32[]{:S(2)}) collective-permute-start(bf16[16,64,128]{2,1,0:T(8,128)(2,1)S(1)} %collective-permute-done.61.refs_3_), channel_id=1, source_target_pairs={{0,1},{1,0},{2,3},{3,2},{4,5},{5,4},{6,7},{7,6},{8,9},{9,8},{10,11... | collective-permute-start | bytes 786440 | tf_op jit(solution)/shard_map/ppermute | solution.py:51
  268.8 11.6 %collective-permute-start.64 = (bf16[16,64,128]{2,1,0:T(8,128)(2,1)S(1)}, bf16[16,64,128]{2,1,0:T(8,128)(2,1)}, u32[]{:S(2)}, u32[]{:S(2)}) collective-permute-start(bf16[16,64,128]{2,1,0:T(8,128)(2,1)S(1)} %collective-permute-done.61.refs_3_), channel_id=1, source_target_pairs={{0,2},{1,3},{2,0},{3,1},{4,6},{5,7},{6,4},{7,5},{8,10},{9,11},{10,... | collective-permute-start | bytes 786440 | tf_op jit(solution)/shard_map/ppermute | solution.py:51
  269.6 10.7 %collective-permute-start.62 = (bf16[16,64,128]{2,1,0:T(8,128)(2,1)S(1)}, bf16[16,64,128]{2,1,0:T(8,128)(2,1)}, u32[]{:S(2)}, u32[]{:S(2)}) collective-permute-start(bf16[16,64,128]{2,1,0:T(8,128)(2,1)S(1)} %collective-permute-done.59.refs_4_), channel_id=1, source_target_pairs={{0,4},{1,5},{2,6},{3,7},{4,8},{5,9},{6,10},{7,11},{8,12},{9,13},{1... | collective-permute-start | bytes 786440 | tf_op jit(solution)/shard_map/ppermute | solution.py:51
  276.4 4.5 %collective-permute-start.69 = (bf16[16,64,128]{2,1,0:T(8,128)(2,1)S(1)}, bf16[16,64,128]{2,1,0:T(8,128)(2,1)S(1)}, u32[]{:S(2)}, u32[]{:S(2)}) collective-permute-start(bf16[16,64,128]{2,1,0:T(8,128)(2,1)S(1)} %collective-permute-done.59.refs_4_), channel_id=1, source_target_pairs={{0,1},{1,0},{2,3},{3,2},{4,5},{5,4},{6,7},{7,6},{8,9},{9,8},{10,11... | collective-permute-start | bytes 786440 | tf_op jit(solution)/shard_map/ppermute | solution.py:51
  278.6 4.4 %collective-permute-start.66 = (bf16[16,64,128]{2,1,0:T(8,128)(2,1)S(1)}, bf16[16,64,128]{2,1,0:T(8,128)(2,1)}, u32[]{:S(2)}, u32[]{:S(2)}) collective-permute-start(bf16[16,64,128]{2,1,0:T(8,128)(2,1)S(1)} %collective-permute-done.58.refs_1_), channel_id=1, source_target_pairs={{0,1},{1,0},{2,3},{3,2},{4,5},{5,4},{6,7},{7,6},{8,9},{9,8},{10,11... | collective-permute-start | bytes 786440 | tf_op jit(solution)/shard_map/ppermute | solution.py:51
  (36 other events, 215.7 us)

commit v8 on v6

--- a/solution.py
+++ b/solution.py
@@ -12,6 +12,7 @@
 NFW = 32
 FREQ0 = 16
 ITERS = 2
+SURE = 128
 LANES = 128
 F32 = jnp.float32
 BF16 = jnp.bfloat16
@@ -299,10 +300,11 @@
 
 
 def windowed_spectrum(pair, onset, forward, inverse):
-    time = lax.broadcasted_iota(jnp.int32, (NT, 2 * LANES), 0)
-    values = jnp.dot(inverse, jnp.concatenate(pair, axis=1), preferred_element_type=F32)
+    time = SURE + lax.broadcasted_iota(jnp.int32, (NT - SURE, 2 * LANES), 0)
+    spectra = jnp.concatenate(pair, axis=1)
+    values = jnp.dot(inverse, spectra, preferred_element_type=F32)
     kept = jnp.where(time < jnp.concatenate(onset, axis=1), values, 0.0).astype(BF16)
-    return jnp.dot(forward, kept, preferred_element_type=F32)
+    return jnp.dot(forward, jnp.concatenate([kept, spectra], axis=0), preferred_element_type=F32)
 
 
 def window_kernel(parts, has_base, want_spec, *refs):
@@ -358,34 +360,106 @@
     )(*operands)
 
 
-def window_at_kernel(line, flip, step, forward_ref, inverse_ref, onset_ref, spec_ref, out_ref, result):
+def window_at_kernel(line, flip, step, begun, *refs):
+    forward_ref, inverse_ref, onset_ref, chip_inverse_ref, spec_ref = refs[:5]
+    out_ref, keep_ref, send_ref, result, made, sems = refs[5 + 2 * begun :]
     core = own_place(line)[3]
     focal, k, _ = spec_ref.shape
     start = chip_columns(line, False, flip, step) + core * LANES
     columns = pl.ds(pl.multiple_of(start, LANES), LANES)
+    samples = made.shape[2]
+    first = (lax.axis_index("blk") // 2) * (2 * samples)
+    time = first + lax.broadcasted_iota(jnp.int32, (2 * samples, 2 * LANES), 0)
+
+    def pair_of(p):
+        onset = [onset_ref[p + q : p + q + 1, columns] for q in range(2)]
+        return [spec_ref[p + q] for q in range(2)], onset
+
     for p in range(0, focal, 2):
-        onset = [onset_ref[p + q : p + q + 1, columns] for q in range(2)]
-        pair = [spec_ref[p + q] for q in range(2)]
+        pair, onset = pair_of(p)
+        values = jnp.dot(
+            chip_inverse_ref[...], jnp.concatenate(pair, axis=1), preferred_element_type=F32
+        )
+        values = jnp.where(time < jnp.concatenate(onset, axis=1), values, 0.0).astype(BF16)
+        low, high = values[:samples], values[samples:]
+        mine, theirs = jnp.where(core == 0, low, high), jnp.where(core == 0, high, low)
+        for q in range(2):
+            part = slice(q * LANES, (q + 1) * LANES)
+            made[0, p + q] = mine[:, part]
+            made[1, p + q] = theirs[:, part]
+    place = pl.ds((flip * line + step) * LANES, LANES)
+    copies = [
+        pltpu.make_async_copy(made.at[side], target.at[:, :, place], sems.at[side])
+        for side, target in enumerate((keep_ref, send_ref))
+    ]
+    for copy in copies:
+        copy.start()
+    for p in range(0, focal, 2):
+        pair, onset = pair_of(p)
         spectrum = windowed_spectrum(pair, onset, forward_ref[...], inverse_ref[...])
         for q in range(2):
             result[pl.ds(p + q, k, stride=focal), :] = spectrum[:, q * LANES : (q + 1) * LANES]
     out_ref[...] = result[...].reshape(NFW, 2, focal, LANES).astype(BF16)
-
-
-def window_at(spec, forward, inverse, onset_times, line, flip, step):
+    for copy in copies:
+        copy.wait()
+
+
+def window_at(spec, forward, inverse, onset_times, chip_inverse, line, flip, step, fields):
     focal, k, _ = spec.shape
+    samples = chip_inverse.shape[0] // 2
+    field_shape = jax.ShapeDtypeStruct((focal, samples, 2 * line * LANES), BF16)
+    begun = bool(fields)
     return pl.pallas_call(
-        functools.partial(window_at_kernel, line, flip, step),
-        in_specs=[VMEM] * 4,
-        out_specs=VMEM,
-        out_shape=jax.ShapeDtypeStruct((NFW, 2, focal, LANES), BF16),
-        scratch_shapes=[pltpu.VMEM((k * focal, LANES), F32)],
+        functools.partial(window_at_kernel, line, flip, step, begun),
+        in_specs=[VMEM] * 5 + [ANY] * len(fields),
+        out_specs=[VMEM, ANY, ANY],
+        out_shape=[jax.ShapeDtypeStruct((NFW, 2, focal, LANES), BF16), field_shape, field_shape],
+        input_output_aliases={5: 1, 6: 2} if begun else {},
+        scratch_shapes=[
+            pltpu.VMEM((k * focal, LANES), F32),
+            pltpu.VMEM((2, focal, samples, LANES), BF16),
+            pltpu.SemaphoreType.DMA((2,)),
+        ],
         compiler_params=limit(8),
         cost_estimate=pl.CostEstimate(
             flops=4 * k * NT * focal * LANES, bytes_accessed=2 * k * focal * LANES * 6, transcendentals=0
         ),
         name="window_at",
-    )(forward, inverse, onset_times, spec)
+    )(forward, inverse, onset_times, chip_inverse, spec, *fields)
+
+
+def merge_kernel(line, mine, theirs, out_ref, made, sems):
+    core = own_place(line)[3]
+    copy, rows = strip_copies(made, out_ref, sems, STRIPS)
+
+    def body(strip, carry):
+        for row in range(rows):
+            p = strip * rows + row
+            for at, (flip, step) in enumerate(relative(line)):
+                columns = pl.ds(chip_columns(line, False, flip, step), 2 * LANES)
+                part = pl.ds(at * LANES, LANES)
+                made[p, :, columns] = join_cores(core, mine[p, :, part], theirs[p, :, part])
+        copy(strip).start()
+        return carry
+
+    lax.fori_loop(0, STRIPS, body, 0)
+    for strip in range(STRIPS):
+        copy(strip).wait()
+
+
+def merge(mine, theirs, line):
+    focal, samples, width = mine.shape
+    shape = (focal, samples, 2 * width)
+    return pl.pallas_call(
+        functools.partial(merge_kernel, line),
+        in_specs=[VMEM] * 2,
+        out_specs=ANY,
+        out_shape=jax.ShapeDtypeStruct(shape, BF16),
+        scratch_shapes=[pltpu.VMEM(shape, BF16), pltpu.SemaphoreType.DMA((STRIPS,))],
+        compiler_params=limit(6),
+        cost_estimate=pl.CostEstimate(flops=0, bytes_accessed=8 * mine.size, transcendentals=0),
+        name="merge",
+    )(mine, theirs)
 
 
 def field_kernel(line, has_plus, inverse_ref, onset_ref, *refs):
@@ -468,15 +542,17 @@
     beside = [places.send(far[1], places.shift(1))] if size > 1 else []
     parts = [keep0[0], got0[0]]
 
-    def pass_on(steps, shift):
-        carried = []
+    def pass_on(steps, shift, *first):
+        carried, sent = [], []
         for step in steps:
-            terms = [keep0[step], got0[step], *([across[step]] if step in across else []), *carried]
-            carried = [places.send(add(*terms).astype(BF16), places.shift(shift))]
-        return carried
-
-    parts += pass_on(range(size // 2, 0, -1), 1)
-    parts += pass_on(range(size // 2 + 1, size), size - 1)
+            crossed = [after(across[step], *first)] if step in across else []
+            carried = [places.send(add(keep0[step], got0[step], *crossed, *carried).astype(BF16), places.shift(shift))]
+            sent += carried
+        return sent
+
+    ahead = pass_on(range(size // 2, 0, -1), 1)
+    behind = pass_on(range(size // 2 + 1, size), size - 1, *ahead[:1])
+    parts += ahead[-1:] + behind[-1:]
     across[0] = places.send(add(keep1[0], got1[0], *beside).astype(BF16), places.pair())
     return parts + [across[0]]
 
@@ -500,7 +576,7 @@
     across = {0: places.send(block, places.pair())}
     own = run(0, [0], line)
     for step in range(2, size // 2 + 1):
-        line[step] = places.send(after(line[step - 1], *own), places.shift(1))
+        line[step] = places.send(after(line[step - 1], across[0], *own), places.shift(1))
     for step in range(size - 2, size // 2, -1):
         line[step] = places.send(after(line[step + 1], *own), places.shift(size - 1))
     for step in near:
@@ -530,9 +606,19 @@
     forward, inverse = tables_of(jnp.arange(NT, dtype=jnp.int32))
     own_samples = lax.axis_index("blk") * samples + jnp.arange(samples, dtype=jnp.int32)
     own_forward, own_inverse = tables_of(own_samples)
+    chip_samples = lax.axis_index("blk") // 2 * (2 * samples) + jnp.arange(2 * samples, dtype=jnp.int32)
+    _, chip_inverse = tables_of(chip_samples)
+    sure = contract("kt,tj->kj", forward[:, :SURE], inverse[:SURE]).astype(BF16)
+    forward = jnp.concatenate([forward[:, SURE:], sure], axis=1)
+    inverse = inverse[SURE:]
+
+    fields = []
 
     def window_piece(piece, flip, step):
-        return window_at(piece, forward, inverse, onset_times, line, flip, step)
+        spectrum, *fields[:] = window_at(
+            piece, forward, inverse, onset_times, chip_inverse, line, flip, step, tuple(fields)
+        )
+        return spectrum
 
     parts = reduce_scatter(places, *first_analysis(plus_start, own_forward, line))
     start = add(*parts).astype(BF16)
@@ -543,7 +629,7 @@
         parts = reduce_scatter(places, *convolve(spectrum_plus, reflection, line))
         windowed = window(parts, forward, inverse, onset_times, want_spec=last)
         if last:
-            upgoing_spec, own = gather_chips(places, windowed, window_piece)
+            _, own = gather_chips(places, windowed, window_piece)
         else:
             own, _ = gather_chips(places, windowed)
         half = correlate(own[0], swap_cores(places, own[0]), reflection, line, 0)
@@ -551,14 +637,13 @@
         downgoing_spec = correlate(own[1], swap_cores(places, across), reflection, line, 1, half, last)
         if not last:
             spectrum_plus = window([downgoing_spec], forward, inverse, onset_times, base=start)
-    other = [swap_cores(places, side) for side in upgoing_spec]
-    upgoing = field(upgoing_spec, other, own_inverse, onset_times, line)
-
-    def before_far(piece, flip, step):
-        return upgoing if (flip, step) == (1, 0) else piece
-
-    own, _ = gather_chips(places, downgoing_spec, before_far)
-    other = [swap_cores(places, side) for side in own]
+    mine, theirs = fields
+    theirs = places.send(after(theirs, downgoing_spec), places.core())
+    own, _ = gather_chips(places, after(downgoing_spec, own_inverse))
+    upgoing = merge(mine, theirs, line)
+    other = [swap_cores(places, own[0])]
+    across = [own[1][step] if step in (0, 1, line - 1) else after(own[1][step], upgoing) for step in range(line)]
+    other.append(swap_cores(places, across))
     downgoing = field(own, other, own_inverse, onset_times, line, plus_start)
     return upgoing, downgoing
 

time: 288 us -> 290 us (level)
  starting transfers between devices: 73.2 us -> 52.1 us
  waiting for transfers between devices: 107 us -> 125 us
  other arithmetic: 5.49 us -> 14 us
  local copies, waits for them, and re-layouts: 14.8 us -> 11.5 us
    ppermute x80 -> x73, starting transfers between devices: 73.2 us -> 52.1 us  [send(): return lax.ppermute(array, self.axis, pairs)]
    ppermute x80 -> x73, waiting for transfers between devices: 107 us -> 125 us  [send(): return lax.ppermute(array, self.axis, pairs)]
    unnamed x38 -> x14, local copies, waits for them, and re-layouts: 13.2 us -> 2.21 us
    convert_element_type x5 -> x7, local copies, waits for them, and re-layouts: 0.31 us -> 4.66 us  [tables_of(): inverse = (basis * math.sqrt(2.0 / NFW)).astype(BF16)]
    pallas_call x2 -> x1, Pallas kernels: 6.41 us -> 2.28 us  [field(): pl.pallas_call(functools.partial(field_kernel, line, bool(plus)), in_spec...]
    convert_element_type x3, other arithmetic: 0.73 us -> 4.53 us  [reduce_scatter(): far = [add(keep, got).astype(BF16) for keep, got in zip(keep1, got1)]]
    pallas_call x8 -> x9, Pallas kernels: 18.6 us -> 20.7 us  [the longest x8 19.3 us: window_at(): pl.pallas_call(functools.partial(window_at_kernel, line, flip, step, begu...]
  transfers between devices with their start and end apart: 80 -> 73, of which waited for: 34 -> 37; matrix products, arithmetic and copies ran while one was open for 2% -> 8% of each run, Pallas kernels for 16% -> 12%
where the time goes in v8:
time: 290 us; the launch traced here: 289 us
  waiting for transfers between devices  125 us (43%)
  Pallas kernels  83.8 us (29%)
  starting transfers between devices  52.1 us (18%)
  other arithmetic  14 us (5%)
  local copies, waits for them, and re-layouts  11.5 us (4%)
    ppermute x73, waiting for transfers between devices, send(): return lax.ppermute(array, self.axis, pairs)  125 us
    ppermute x73, starting transfers between devices, send(): return lax.ppermute(array, self.axis, pairs)  52.1 us
    pallas_call x4, Pallas kernels, correlate(): pl.pallas_call(functools.partial(correlate_kernel, line, flip, bool(more)...  30.8 us
    pallas_call x2, Pallas kernels, convolve(): pl.pallas_call(functools.partial(convolve_kernel, line), in_specs=[VMEM,...  23.4 us
    pallas_call x8, Pallas kernels, window_at(): pl.pallas_call(functools.partial(window_at_kernel, line, flip, step, begu...  19.3 us
  transfers between devices with their start and end apart: 73, of which 37 were waited for; matrix products, arithmetic and copies ran while one was open for 8% of the time, Pallas kernels for 12%

profile of v8, /device:TPU:0, one launch (start us, length us, event | category | flops | bytes accessed | tf_op | source)
XLA Modules:
  0.0 288.8 jit_solution(2353093697952102031)
XLA Ops:
  1.5 1.6 copy-done.1
  3.0 1.9 first_analysis.1
  5.5 2.2 collective-permute-done.1
  8.1 3.0 %collective-permute-start.2 = (bf16[16,64,128]{2,1,0:T(8,128)(2,1)S(1)}, bf16[16,64,128]{2,1,0:T(8,128)(2,1)S(1)}, u32[]{:S(2)}, u32[]{:S(2)}) collective-permute-start(bf16[16,64,128]{2,1,0:T(8,128)(2,1)S(1)} %get-tuple-element.116), channel_id=1, source_target_pairs={{0,2},{1,3},{2,0},{3,1},{4,6},{5,7},{6,4},{7,5},{8,10},{9,11},{10,... | collective-permute-start | bytes 786440 | tf_op jit(solution)/shard_map/ppermute | solution.py:51
  11.0 1.6 collective-permute-start.7
  13.1 5.0 %collective-permute-done.2 = bf16[16,64,128]{2,1,0:T(8,128)(2,1)S(1)} collective-permute-done((bf16[16,64,128]{2,1,0:T(8,128)(2,1)S(1)}, bf16[16,64,128]{2,1,0:T(8,128)(2,1)S(1)}, u32[]{:S(2)}, u32[]{:S(2)}) %collective-permute-start.2) | collective-permute-done | bytes 262176 | tf_op jit(solution)/shard_map/ppermute | solution.py:51
  18.2 2.2 collective-permute-start.3
  22.1 1.5 collective-permute-done.5
  23.7 3.8 %collective-permute-done.3 = bf16[16,64,128]{2,1,0:T(8,128)(2,1)S(1)} collective-permute-done((bf16[16,64,128]{2,1,0:T(8,128)(2,1)S(1)}, bf16[16,64,128]{2,1,0:T(8,128)(2,1)S(1)}, u32[]{:S(2)}, u32[]{:S(2)}) %collective-permute-start.3) | collective-permute-done | bytes 262176 | tf_op jit(solution)/shard_map/ppermute | solution.py:51
  27.8 3.8 %collective-permute-start.6 = (bf16[16,64,128]{2,1,0:T(8,128)(2,1)S(1)}, bf16[16,64,128]{2,1,0:T(8,128)(2,1)S(1)}, u32[]{:S(2)}, u32[]{:S(2)}) collective-permute-start(bf16[16,64,128]{2,1,0:T(8,128)(2,1)S(1)} %get-tuple-element.115), channel_id=1, source_target_pairs={{0,12},{1,13},{2,14},{3,15},{4,0},{5,1},{6,2},{7,3},{8,4},{9,5},{1... | collective-permute-start | bytes 786440 | tf_op jit(solution)/shard_map/ppermute | solution.py:51
  31.6 7.0 %collective-permute-done.4 = bf16[16,64,128]{2,1,0:T(8,128)(2,1)S(1)} collective-permute-done((bf16[16,64,128]{2,1,0:T(8,128)(2,1)S(1)}, bf16[16,64,128]{2,1,0:T(8,128)(2,1)S(1)}, u32[]{:S(2)}, u32[]{:S(2)}) %collective-permute-start.4) | collective-permute-done | bytes 262176 | tf_op jit(solution)/shard_map/ppermute | solution.py:51
  40.0 11.7 %convolve.2 = (bf16[4,32,2,16,128]{4,3,2,1,0:T(8,128)(2,1)S(1)}, bf16[4,32,2,16,128]{4,3,2,1,0:T(8,128)(2,1)S(1)}, bf16[4,32,2,16,128]{4,3,2,1,0:T(8,128)(2,1)S(1)}, bf16[4,32,2,16,128]{4,3,2,1,0:T(8,128)(2,1)S(1)}) custom-call(bf16[32,2,16,128]{3,2,1,0:T(8,128)(2,1)S(1)} %bitcast.93, bf16[2,32,128,2048]{3,2,1,0:T(8,128)(2,1)} %refs_8_.7), custom_call_target="tpu_custom_call" | custom-call | flops 1073741824 | bytes 37748736 | tf_op jit(solution)/shard_map/convolve/pallas_call | solution.py:223
  52.6 1.9 collective-permute-done.10
  54.5 2.1 fusion.20
  60.6 1.5 copy.27
  67.3 2.4 collective-permute-start.12
  70.6 5.3 %collective-permute-done.16 = bf16[32,2,16,128]{3,2,1,0:T(8,128)(2,1)S(1)} collective-permute-done((bf16[32,2,16,128]{3,2,1,0:T(8,128)(2,1)}, bf16[32,2,16,128]{3,2,1,0:T(8,128)(2,1)S(1)}, u32[]{:S(2)}, u32[]{:S(2)}) %collective-permute-start.16) | collective-permute-done | bytes 262176 | tf_op jit(solution)/shard_map/ppermute | solution.py:51
  77.9 2.5 collective-permute-done.12
  80.4 1.2 fusion.5
  82.2 1.6 collective-permute-start.13
  84.7 6.4 %collective-permute-done.15.refs_6_ = bf16[32,2,16,128]{3,2,1,0:T(8,128)(2,1)S(1)} collective-permute-done((bf16[32,2,16,128]{3,2,1,0:T(8,128)(2,1)S(1)}, bf16[32,2,16,128]{3,2,1,0:T(8,128)(2,1)S(1)}, u32[]{:S(2)}, u32[]{:S(2)}) %collective-permute-start.15) | collective-permute-done | bytes 262176 | tf_op jit(solution)/shard_map/ppermute | solution.py:51
  91.1 3.4 %collective-permute-done.13.refs_5_ = bf16[32,2,16,128]{3,2,1,0:T(8,128)(2,1)S(1)} collective-permute-done((bf16[32,2,16,128]{3,2,1,0:T(8,128)(2,1)S(1)}, bf16[32,2,16,128]{3,2,1,0:T(8,128)(2,1)S(1)}, u32[]{:S(2)}, u32[]{:S(2)}) %collective-permute-start.13) | collective-permute-done | bytes 262176 | tf_op jit(solution)/shard_map/ppermute | solution.py:51
  94.5 2.2 window.3.refs_0_
  98.0 3.5 %collective-permute-start.23 = (bf16[32,2,16,128]{3,2,1,0:T(8,128)(2,1)S(1)}, bf16[32,2,16,128]{3,2,1,0:T(8,128)(2,1)S(1)}, u32[]{:S(2)}, u32[]{:S(2)}) collective-permute-start(bf16[32,2,16,128]{3,2,1,0:T(8,128)(2,1)S(1)} %window.3.refs_0_), channel_id=1, source_target_pairs={{0,12},{1,13},{2,14},{3,15},{4,0},{5,1},{6,2},{7,3},{8,4},{9,5},{1... | collective-permute-start | bytes 786440 | tf_op jit(solution)/shard_map/ppermute | solution.py:51
  101.5 6.4 %collective-permute-done.20.refs_1_ = bf16[32,2,16,128]{3,2,1,0:T(8,128)(2,1)S(1)} collective-permute-done((bf16[32,2,16,128]{3,2,1,0:T(8,128)(2,1)S(1)}, bf16[32,2,16,128]{3,2,1,0:T(8,128)(2,1)S(1)}, u32[]{:S(2)}, u32[]{:S(2)}) %collective-permute-start.20) | collective-permute-done | bytes 262176 | tf_op jit(solution)/shard_map/ppermute | solution.py:51
  107.9 1.4 collective-permute-start.21
  109.3 4.0 %collective-permute-done.23.refs_3_ = bf16[32,2,16,128]{3,2,1,0:T(8,128)(2,1)S(1)} collective-permute-done((bf16[32,2,16,128]{3,2,1,0:T(8,128)(2,1)S(1)}, bf16[32,2,16,128]{3,2,1,0:T(8,128)(2,1)S(1)}, u32[]{:S(2)}, u32[]{:S(2)}) %collective-permute-start.23) | collective-permute-done | bytes 262176 | tf_op jit(solution)/shard_map/ppermute | solution.py:51
  114.4 1.7 collective-permute-done.21.refs_2_
  117.0 5.4 %collective-permute-done.24.refs_3_ = bf16[32,2,16,128]{3,2,1,0:T(8,128)(2,1)S(1)} collective-permute-done((bf16[32,2,16,128]{3,2,1,0:T(8,128)(2,1)S(1)}, bf16[32,2,16,128]{3,2,1,0:T(8,128)(2,1)S(1)}, u32[]{:S(2)}, u32[]{:S(2)}) %collective-permute-start.24) | collective-permute-done | bytes 262176 | tf_op jit(solution)/shard_map/ppermute | solution.py:51
  122.9 7.6 %correlate0.2.refs_9_ = f32[32,2,16,128]{3,2,1,0:T(8,128)S(1)} custom-call(bf16[32,2,16,128]{3,2,1,0:T(8,128)(2,1)S(1)} %window.3.refs_0_, bf16[32,2,16,128]{3,2,1,0:T(8,128)(2,1)S(1)} %collective-permute-done.20.refs_1_, bf16[32,2,16,128]{3,2,1,0:T(8,128)(2,1)S(1)} %collective-permute-done.21.refs_2_, ...), custom_call_target="tpu_custom_call" | custom-call | flops 536870912 | bytes 18874368 | tf_op jit(solution)/shard_map/correlate0/pallas_call | solution.py:290
  132.6 7.7 %correlate1.2.refs_3_ = f32[32,2,16,128]{3,2,1,0:T(8,128)S(1)} custom-call(bf16[32,2,16,128]{3,2,1,0:T(8,128)(2,1)S(1)} %collective-permute-done.18.refs_0_, bf16[32,2,16,128]{3,2,1,0:T(8,128)(2,1)S(1)} %collective-permute-done.19.refs_1_, bf16[32,2,16,128]{3,2,1,0:T(8,128)(2,1)S(1)} %collective-permute-done.22.refs_2_, ...), custom_call_target="tpu_custom_call" | custom-call | flops 536870912 | bytes 18874368 | tf_op jit(solution)/shard_map/correlate1/pallas_call | solution.py:290
  140.2 2.2 window.4.spec_ref
  142.4 11.7 %convolve.3 = (bf16[4,32,2,16,128]{4,3,2,1,0:T(8,128)(2,1)S(1)}, bf16[4,32,2,16,128]{4,3,2,1,0:T(8,128)(2,1)S(1)}, bf16[4,32,2,16,128]{4,3,2,1,0:T(8,128)(2,1)S(1)}, bf16[4,32,2,16,128]{4,3,2,1,0:T(8,128)(2,1)S(1)}) custom-call(bf16[32,2,16,128]{3,2,1,0:T(8,128)(2,1)S(1)} %window.4.spec_ref, bf16[2,32,128,2048]{3,2,1,0:T(8,128)(2,1)} %refs_8_.7), custom_call_target="tpu_custom_call" | custom-call | flops 1073741824 | bytes 37748736 | tf_op jit(solution)/shard_map/convolve/pallas_call | solution.py:223
  154.7 2.3 collective-permute-done.34
  156.9 2.1 fusion.23
  161.6 6.9 %collective-permute-done.35 = bf16[32,2,16,128]{3,2,1,0:T(8,128)(2,1)} collective-permute-done((bf16[32,2,16,128]{3,2,1,0:T(8,128)(2,1)}, bf16[32,2,16,128]{3,2,1,0:T(8,128)(2,1)}, u32[]{:S(2)}, u32[]{:S(2)}) %collective-permute-start.35) | collective-permute-done | bytes 262176 | tf_op jit(solution)/shard_map/ppermute | solution.py:51
  172.3 1.4 collective-permute-done.38
  173.7 4.8 %collective-permute-done.36 = bf16[32,2,16,128]{3,2,1,0:T(8,128)(2,1)S(1)} collective-permute-done((bf16[32,2,16,128]{3,2,1,0:T(8,128)(2,1)S(1)}, bf16[32,2,16,128]{3,2,1,0:T(8,128)(2,1)S(1)}, u32[]{:S(2)}, u32[]{:S(2)}) %collective-permute-start.36) | collective-permute-done | bytes 262176 | tf_op jit(solution)/shard_map/ppermute | solution.py:51
  178.5 1.2 fusion.1
  179.8 2.0 collective-permute-start.37
  182.8 8.3 %collective-permute-done.39.refs_6_ = bf16[32,2,16,128]{3,2,1,0:T(8,128)(2,1)S(1)} collective-permute-done((bf16[32,2,16,128]{3,2,1,0:T(8,128)(2,1)S(1)}, bf16[32,2,16,128]{3,2,1,0:T(8,128)(2,1)S(1)}, u32[]{:S(2)}, u32[]{:S(2)}) %collective-permute-start.39) | collective-permute-done | bytes 262176 | tf_op jit(solution)/shard_map/ppermute | solution.py:51
  192.5 1.9 collective-permute-start.42
  194.7 2.4 window_at.8
  198.0 7.0 %collective-permute-done.42.refs_4_ = bf16[16,64,128]{2,1,0:T(8,128)(2,1)S(1)} collective-permute-done((bf16[16,64,128]{2,1,0:T(8,128)(2,1)S(1)}, bf16[16,64,128]{2,1,0:T(8,128)(2,1)S(1)}, u32[]{:S(2)}, u32[]{:S(2)}) %collective-permute-start.42) | collective-permute-done | bytes 262176 | tf_op jit(solution)/shard_map/ppermute | solution.py:51
  205.9 2.4 window_at.9
  208.3 2.4 window_at.10
  210.7 2.4 window_at.11
  213.7 1.9 collective-permute-done.44.refs_4_
  216.4 2.4 window_at.12
  219.4 2.4 window_at.13
  221.8 2.4 window_at.14
  224.9 7.7 %correlate0.3.refs_9_ = f32[32,2,16,128]{3,2,1,0:T(8,128)S(1)} custom-call(bf16[32,2,16,128]{3,2,1,0:T(8,128)(2,1)S(1)} %get-tuple-element.71.refs_0_, bf16[32,2,16,128]{3,2,1,0:T(8,128)(2,1)S(1)} %get-tuple-element.78.refs_1_, bf16[32,2,16,128]{3,2,1,0:T(8,128)(2,1)S(1)} %get-tuple-element.85.refs_2_, ...), custom_call_target="tpu_custom_call" | custom-call | flops 536870912 | bytes 18874368 | tf_op jit(solution)/shard_map/correlate0/pallas_call | solution.py:290
  232.5 2.4 window_at.15
  236.9 7.8 %correlate1.3.refs_0_ = bf16[16,64,128]{2,1,0:T(8,128)(2,1)S(1)} custom-call(bf16[32,2,16,128]{3,2,1,0:T(8,128)(2,1)S(1)} %get-tuple-element.75.refs_0_, bf16[32,2,16,128]{3,2,1,0:T(8,128)(2,1)S(1)} %get-tuple-element.98.refs_1_, bf16[32,2,16,128]{3,2,1,0:T(8,128)(2,1)S(1)} %get-tuple-element.99.refs_2_, ...), custom_call_target="tpu_custom_call" | custom-call | flops 536870912 | bytes 18874368 | tf_op jit(solution)/shard_map/correlate1/pallas_call | solution.py:290
  246.4 1.2 collective-permute-start.59
  247.6 7.4 %collective-permute-done.59.refs_4_ = bf16[16,64,128]{2,1,0:T(8,128)(2,1)S(1)} collective-permute-done((bf16[16,64,128]{2,1,0:T(8,128)(2,1)S(1)}, bf16[16,64,128]{2,1,0:T(8,128)(2,1)S(1)}, u32[]{:S(2)}, u32[]{:S(2)}) %collective-permute-start.59) | collective-permute-done | bytes 262176 | tf_op jit(solution)/shard_map/ppermute | solution.py:51
  255.0 2.7 collective-permute-done.58.refs_1_
  257.7 3.8 %collective-permute-start.61 = (bf16[16,64,128]{2,1,0:T(8,128)(2,1)S(1)}, bf16[16,64,128]{2,1,0:T(8,128)(2,1)S(1)}, u32[]{:S(2)}, u32[]{:S(2)}) collective-permute-start(bf16[16,64,128]{2,1,0:T(8,128)(2,1)S(1)} %correlate1.3.refs_0_), channel_id=1, source_target_pairs={{0,12},{1,13},{2,14},{3,15},{4,0},{5,1},{6,2},{7,3},{8,4},{9,5},{1... | collective-permute-start | bytes 786440 | tf_op jit(solution)/shard_map/ppermute | solution.py:51
  261.5 7.2 %collective-permute-done.60.refs_2_ = bf16[16,64,128]{2,1,0:T(8,128)(2,1)S(1)} collective-permute-done((bf16[16,64,128]{2,1,0:T(8,128)(2,1)S(1)}, bf16[16,64,128]{2,1,0:T(8,128)(2,1)S(1)}, u32[]{:S(2)}, u32[]{:S(2)}) %collective-permute-start.60) | collective-permute-done | bytes 262176 | tf_op jit(solution)/shard_map/ppermute | solution.py:51
  271.6 4.7 %collective-permute-done.63.refs_6_ = bf16[16,64,128]{2,1,0:T(8,128)(2,1)S(1)} collective-permute-done((bf16[16,64,128]{2,1,0:T(8,128)(2,1)S(1)}, bf16[16,64,128]{2,1,0:T(8,128)(2,1)S(1)}, u32[]{:S(2)}, u32[]{:S(2)}) %collective-permute-start.63) | collective-permute-done | bytes 262176 | tf_op jit(solution)/shard_map/ppermute | solution.py:51
  276.3 1.4 merge.1
  278.4 2.3 collective-permute-done.64.refs_7_
  280.7 3.7 %collective-permute-done.62.refs_5_ = bf16[16,64,128]{2,1,0:T(8,128)(2,1)S(1)} collective-permute-done((bf16[16,64,128]{2,1,0:T(8,128)(2,1)S(1)}, bf16[16,64,128]{2,1,0:T(8,128)(2,1)S(1)}, u32[]{:S(2)}, u32[]{:S(2)}) %collective-permute-start.62) | collective-permute-done | bytes 262176 | tf_op jit(solution)/shard_map/ppermute | solution.py:51
  286.4 2.3 field.1
  (156 shorter events, 48.7 us)
Async XLA Ops:
  5.5 7.7 %collective-permute-start = (bf16[4,16,64,128]{3,2,1,0:T(8,128)(2,1)S(1)}, bf16[4,16,64,128]{3,2,1,0:T(8,128)(2,1)S(1)}, u32[]{:S(2)}, u32[]{:S(2)}) collective-permute-start(bf16[4,16,64,128]{3,2,1,0:T(8,128)(2,1)S(1)} %get-tuple-element.54), channel_id=1, source_target_pairs={{0,1},{1,0},{2,3},{3,2},{4,5},{5,4},{6,7},{7,6},{8,9},{9,8},{10,11... | collective-permute-start | bytes 3145736 | tf_op jit(solution)/shard_map/ppermute | solution.py:51
  8.1 10.0 %collective-permute-start.2 = (bf16[16,64,128]{2,1,0:T(8,128)(2,1)S(1)}, bf16[16,64,128]{2,1,0:T(8,128)(2,1)S(1)}, u32[]{:S(2)}, u32[]{:S(2)}) collective-permute-start(bf16[16,64,128]{2,1,0:T(8,128)(2,1)S(1)} %get-tuple-element.116), channel_id=1, source_target_pairs={{0,2},{1,3},{2,0},{3,1},{4,6},{5,7},{6,4},{7,5},{8,10},{9,11},{10,... | collective-permute-start | bytes 786440 | tf_op jit(solution)/shard_map/ppermute | solution.py:51
  11.0 9.9 %collective-permute-start.7 = (bf16[16,64,128]{2,1,0:T(8,128)(2,1)S(1)}, bf16[16,64,128]{2,1,0:T(8,128)(2,1)S(1)}, u32[]{:S(2)}, u32[]{:S(2)}) collective-permute-start(bf16[16,64,128]{2,1,0:T(8,128)(2,1)S(1)} %get-tuple-element.117), channel_id=1, source_target_pairs={{0,4},{1,5},{2,6},{3,7},{4,8},{5,9},{6,10},{7,11},{8,12},{9,13},{1... | collective-permute-start | bytes 786440 | tf_op jit(solution)/shard_map/ppermute | solution.py:51
  12.6 11.0 %collective-permute-start.5 = (bf16[16,64,128]{2,1,0:T(8,128)(2,1)S(1)}, bf16[16,64,128]{2,1,0:T(8,128)(2,1)S(1)}, u32[]{:S(2)}, u32[]{:S(2)}) collective-permute-start(bf16[16,64,128]{2,1,0:T(8,128)(2,1)S(1)} %get-tuple-element.118), channel_id=1, source_target_pairs={{0,2},{1,3},{2,0},{3,1},{4,6},{5,7},{6,4},{7,5},{8,10},{9,11},{10,... | collective-permute-start | bytes 786440 | tf_op jit(solution)/shard_map/ppermute | solution.py:51
  18.2 9.2 %collective-permute-start.3 = (bf16[16,64,128]{2,1,0:T(8,128)(2,1)S(1)}, bf16[16,64,128]{2,1,0:T(8,128)(2,1)S(1)}, u32[]{:S(2)}, u32[]{:S(2)}) collective-permute-start(bf16[16,64,128]{2,1,0:T(8,128)(2,1)S(1)} %fusion.10), channel_id=1, source_target_pairs={{0,4},{1,5},{2,6},{3,7},{4,8},{5,9},{6,10},{7,11},{8,12},{9,13},{1... | collective-permute-start | bytes 786440 | tf_op jit(solution)/shard_map/ppermute | solution.py:51
  21.1 10.5 %collective-permute-start.8 = (bf16[16,64,128]{2,1,0:T(8,128)(2,1)S(1)}, bf16[16,64,128]{2,1,0:T(8,128)(2,1)S(1)}, u32[]{:S(2)}, u32[]{:S(2)}) collective-permute-start(bf16[16,64,128]{2,1,0:T(8,128)(2,1)S(1)} %fusion.8), channel_id=1, source_target_pairs={{0,2},{1,3},{2,0},{3,1},{4,6},{5,7},{6,4},{7,5},{8,10},{9,11},{10,... | collective-permute-start | bytes 786440 | tf_op jit(solution)/shard_map/ppermute | solution.py:51
  27.7 10.8 %collective-permute-start.4 = (bf16[16,64,128]{2,1,0:T(8,128)(2,1)S(1)}, bf16[16,64,128]{2,1,0:T(8,128)(2,1)S(1)}, u32[]{:S(2)}, u32[]{:S(2)}) collective-permute-start(bf16[16,64,128]{2,1,0:T(8,128)(2,1)S(1)} %get-tuple-element.114), channel_id=1, source_target_pairs={{0,4},{1,5},{2,6},{3,7},{4,8},{5,9},{6,10},{7,11},{8,12},{9,13},{1... | collective-permute-start | bytes 786440 | tf_op jit(solution)/shard_map/ppermute | solution.py:51
  27.8 11.8 %collective-permute-start.6 = (bf16[16,64,128]{2,1,0:T(8,128)(2,1)S(1)}, bf16[16,64,128]{2,1,0:T(8,128)(2,1)S(1)}, u32[]{:S(2)}, u32[]{:S(2)}) collective-permute-start(bf16[16,64,128]{2,1,0:T(8,128)(2,1)S(1)} %get-tuple-element.115), channel_id=1, source_target_pairs={{0,12},{1,13},{2,14},{3,15},{4,0},{5,1},{6,2},{7,3},{8,4},{9,5},{1... | collective-permute-start | bytes 786440 | tf_op jit(solution)/shard_map/ppermute | solution.py:51
  51.8 14.4 %collective-permute-start.9 = (bf16[4,32,2,16,128]{4,3,2,1,0:T(8,128)(2,1)S(1)}, bf16[4,32,2,16,128]{4,3,2,1,0:T(8,128)(2,1)}, u32[]{:S(2)}, u32[]{:S(2)}) collective-permute-start(bf16[4,32,2,16,128]{4,3,2,1,0:T(8,128)(2,1)S(1)} %get-tuple-element.59), channel_id=1, source_target_pairs={{0,1},{1,0},{2,3},{3,2},{4,5},{5,4},{6,7},{7,6},{8,9},{9,8},{10,11... | collective-permute-start | bytes 3145736 | tf_op jit(solution)/shard_map/ppermute | solution.py:51
  56.6 9.5 %collective-permute-start.11 = (bf16[32,2,16,128]{3,2,1,0:T(8,128)(2,1)}, bf16[32,2,16,128]{3,2,1,0:T(8,128)(2,1)}, u32[]{:S(2)}, u32[]{:S(2)}) collective-permute-start(bf16[32,2,16,128]{3,2,1,0:T(8,128)(2,1)} %get-tuple-element.111), channel_id=1, source_target_pairs={{0,2},{1,3},{2,0},{3,1},{4,6},{5,7},{6,4},{7,5},{8,10},{9,11},{10,... | collective-permute-start | bytes 786440 | tf_op jit(solution)/shard_map/ppermute | solution.py:51
  64.7 11.2 %collective-permute-start.16 = (bf16[32,2,16,128]{3,2,1,0:T(8,128)(2,1)}, bf16[32,2,16,128]{3,2,1,0:T(8,128)(2,1)S(1)}, u32[]{:S(2)}, u32[]{:S(2)}) collective-permute-start(bf16[32,2,16,128]{3,2,1,0:T(8,128)(2,1)} %get-tuple-element.109), channel_id=1, source_target_pairs={{0,4},{1,5},{2,6},{3,7},{4,8},{5,9},{6,10},{7,11},{8,12},{9,13},{1... | collective-permute-start | bytes 786440 | tf_op jit(solution)/shard_map/ppermute | solution.py:51
  65.6 12.2 %collective-permute-start.14 = (bf16[32,2,16,128]{3,2,1,0:T(8,128)(2,1)}, bf16[32,2,16,128]{3,2,1,0:T(8,128)(2,1)S(1)}, u32[]{:S(2)}, u32[]{:S(2)}) collective-permute-start(bf16[32,2,16,128]{3,2,1,0:T(8,128)(2,1)} %get-tuple-element.110), channel_id=1, source_target_pairs={{0,2},{1,3},{2,0},{3,1},{4,6},{5,7},{6,4},{7,5},{8,10},{9,11},{10,... | collective-permute-start | bytes 786440 | tf_op jit(solution)/shard_map/ppermute | solution.py:51
  67.3 13.1 %collective-permute-start.12 = (bf16[32,2,16,128]{3,2,1,0:T(8,128)(2,1)S(1)}, bf16[32,2,16,128]{3,2,1,0:T(8,128)(2,1)S(1)}, u32[]{:S(2)}, u32[]{:S(2)}) collective-permute-start(bf16[32,2,16,128]{3,2,1,0:T(8,128)(2,1)S(1)} %fusion.6), channel_id=1, source_target_pairs={{0,4},{1,5},{2,6},{3,7},{4,8},{5,9},{6,10},{7,11},{8,12},{9,13},{1... | collective-permute-start | bytes 786440 | tf_op jit(solution)/shard_map/ppermute | solution.py:51
  77.0 7.7 %collective-permute-start.17 = (bf16[32,2,16,128]{3,2,1,0:T(8,128)(2,1)S(1)}, bf16[32,2,16,128]{3,2,1,0:T(8,128)(2,1)S(1)}, u32[]{:S(2)}, u32[]{:S(2)}) collective-permute-start(bf16[32,2,16,128]{3,2,1,0:T(8,128)(2,1)S(1)} %fusion.4), channel_id=1, source_target_pairs={{0,2},{1,3},{2,0},{3,1},{4,6},{5,7},{6,4},{7,5},{8,10},{9,11},{10,... | collective-permute-start | bytes 786440 | tf_op jit(solution)/shard_map/ppermute | solution.py:51
  81.6 9.4 %collective-permute-start.15 = (bf16[32,2,16,128]{3,2,1,0:T(8,128)(2,1)S(1)}, bf16[32,2,16,128]{3,2,1,0:T(8,128)(2,1)S(1)}, u32[]{:S(2)}, u32[]{:S(2)}) collective-permute-start(bf16[32,2,16,128]{3,2,1,0:T(8,128)(2,1)S(1)} %get-tuple-element.112), channel_id=1, source_target_pairs={{0,12},{1,13},{2,14},{3,15},{4,0},{5,1},{6,2},{7,3},{8,4},{9,5},{1... | collective-permute-start | bytes 786440 | tf_op jit(solution)/shard_map/ppermute | solution.py:51
  82.2 12.3 %collective-permute-start.13 = (bf16[32,2,16,128]{3,2,1,0:T(8,128)(2,1)S(1)}, bf16[32,2,16,128]{3,2,1,0:T(8,128)(2,1)S(1)}, u32[]{:S(2)}, u32[]{:S(2)}) collective-permute-start(bf16[32,2,16,128]{3,2,1,0:T(8,128)(2,1)S(1)} %get-tuple-element.113), channel_id=1, source_target_pairs={{0,4},{1,5},{2,6},{3,7},{4,8},{5,9},{6,10},{7,11},{8,12},{9,13},{1... | collective-permute-start | bytes 786440 | tf_op jit(solution)/shard_map/ppermute | solution.py:51
  96.7 11.1 %collective-permute-start.20 = (bf16[32,2,16,128]{3,2,1,0:T(8,128)(2,1)S(1)}, bf16[32,2,16,128]{3,2,1,0:T(8,128)(2,1)S(1)}, u32[]{:S(2)}, u32[]{:S(2)}) collective-permute-start(bf16[32,2,16,128]{3,2,1,0:T(8,128)(2,1)S(1)} %window.3.refs_0_), channel_id=1, source_target_pairs={{0,4},{1,5},{2,6},{3,7},{4,8},{5,9},{6,10},{7,11},{8,12},{9,13},{1... | collective-permute-start | bytes 786440 | tf_op jit(solution)/shard_map/ppermute | solution.py:51
  97.3 10.6 %collective-permute-start.18 = (bf16[32,2,16,128]{3,2,1,0:T(8,128)(2,1)S(1)}, bf16[32,2,16,128]{3,2,1,0:T(8,128)(2,1)S(1)}, u32[]{:S(2)}, u32[]{:S(2)}) collective-permute-start(bf16[32,2,16,128]{3,2,1,0:T(8,128)(2,1)S(1)} %window.3.refs_0_), channel_id=1, source_target_pairs={{0,2},{1,3},{2,0},{3,1},{4,6},{5,7},{6,4},{7,5},{8,10},{9,11},{10,... | collective-permute-start | bytes 786440 | tf_op jit(solution)/shard_map/ppermute | solution.py:51
  98.0 15.3 %collective-permute-start.23 = (bf16[32,2,16,128]{3,2,1,0:T(8,128)(2,1)S(1)}, bf16[32,2,16,128]{3,2,1,0:T(8,128)(2,1)S(1)}, u32[]{:S(2)}, u32[]{:S(2)}) collective-permute-start(bf16[32,2,16,128]{3,2,1,0:T(8,128)(2,1)S(1)} %window.3.refs_0_), channel_id=1, source_target_pairs={{0,12},{1,13},{2,14},{3,15},{4,0},{5,1},{6,2},{7,3},{8,4},{9,5},{1... | collective-permute-start | bytes 786440 | tf_op jit(solution)/shard_map/ppermute | solution.py:51
  107.9 8.2 %collective-permute-start.21 = (bf16[32,2,16,128]{3,2,1,0:T(8,128)(2,1)S(1)}, bf16[32,2,16,128]{3,2,1,0:T(8,128)(2,1)S(1)}, u32[]{:S(2)}, u32[]{:S(2)}) collective-permute-start(bf16[32,2,16,128]{3,2,1,0:T(8,128)(2,1)S(1)} %collective-permute-done.20.refs_1_), channel_id=1, source_target_pairs={{0,4},{1,5},{2,6},{3,7},{4,8},{5,9},{6,10},{7,11},{8,12},{9,13},{1... | collective-permute-start | bytes 786440 | tf_op jit(solution)/shard_map/ppermute | solution.py:51
  109.3 6.8 %collective-permute-start.26 = (bf16[32,2,16,128]{3,2,1,0:T(8,128)(2,1)S(1)}, bf16[32,2,16,128]{3,2,1,0:T(8,128)(2,1)S(1)}, u32[]{:S(2)}, u32[]{:S(2)}) collective-permute-start(bf16[32,2,16,128]{3,2,1,0:T(8,128)(2,1)S(1)} %window.3.refs_0_), channel_id=1, source_target_pairs={{0,1},{1,0},{2,3},{3,2},{4,5},{5,4},{6,7},{7,6},{8,9},{9,8},{10,11... | collective-permute-start | bytes 786440 | tf_op jit(solution)/shard_map/ppermute | solution.py:51
  113.3 3.7 %collective-permute-start.29 = (bf16[32,2,16,128]{3,2,1,0:T(8,128)(2,1)S(1)}, bf16[32,2,16,128]{3,2,1,0:T(8,128)(2,1)S(1)}, u32[]{:S(2)}, u32[]{:S(2)}) collective-permute-start(bf16[32,2,16,128]{3,2,1,0:T(8,128)(2,1)S(1)} %collective-permute-done.23.refs_3_), channel_id=1, source_target_pairs={{0,1},{1,0},{2,3},{3,2},{4,5},{5,4},{6,7},{7,6},{8,9},{9,8},{10,11... | collective-permute-start | bytes 786440 | tf_op jit(solution)/shard_map/ppermute | solution.py:51
  113.3 9.1 %collective-permute-start.24 = (bf16[32,2,16,128]{3,2,1,0:T(8,128)(2,1)S(1)}, bf16[32,2,16,128]{3,2,1,0:T(8,128)(2,1)S(1)}, u32[]{:S(2)}, u32[]{:S(2)}) collective-permute-start(bf16[32,2,16,128]{3,2,1,0:T(8,128)(2,1)S(1)} %collective-permute-done.23.refs_3_), channel_id=1, source_target_pairs={{0,2},{1,3},{2,0},{3,1},{4,6},{5,7},{6,4},{7,5},{8,10},{9,11},{10,... | collective-permute-start | bytes 786440 | tf_op jit(solution)/shard_map/ppermute | solution.py:51
  114.1 8.3 %collective-permute-start.27 = (bf16[32,2,16,128]{3,2,1,0:T(8,128)(2,1)S(1)}, bf16[32,2,16,128]{3,2,1,0:T(8,128)(2,1)S(1)}, u32[]{:S(2)}, u32[]{:S(2)}) collective-permute-start(bf16[32,2,16,128]{3,2,1,0:T(8,128)(2,1)S(1)} %collective-permute-done.20.refs_1_), channel_id=1, source_target_pairs={{0,1},{1,0},{2,3},{3,2},{4,5},{5,4},{6,7},{7,6},{8,9},{9,8},{10,11... | collective-permute-start | bytes 786440 | tf_op jit(solution)/shard_map/ppermute | solution.py:51
  116.1 6.8 %collective-permute-start.28 = (bf16[32,2,16,128]{3,2,1,0:T(8,128)(2,1)S(1)}, bf16[32,2,16,128]{3,2,1,0:T(8,128)(2,1)S(1)}, u32[]{:S(2)}, u32[]{:S(2)}) collective-permute-start(bf16[32,2,16,128]{3,2,1,0:T(8,128)(2,1)S(1)} %collective-permute-done.21.refs_2_), channel_id=1, source_target_pairs={{0,1},{1,0},{2,3},{3,2},{4,5},{5,4},{6,7},{7,6},{8,9},{9,8},{10,11... | collective-permute-start | bytes 786440 | tf_op jit(solution)/shard_map/ppermute | solution.py:51
  116.1 14.5 %collective-permute-start.22 = (bf16[32,2,16,128]{3,2,1,0:T(8,128)(2,1)S(1)}, bf16[32,2,16,128]{3,2,1,0:T(8,128)(2,1)S(1)}, u32[]{:S(2)}, u32[]{:S(2)}) collective-permute-start(bf16[32,2,16,128]{3,2,1,0:T(8,128)(2,1)S(1)} %collective-permute-done.21.refs_2_), channel_id=1, source_target_pairs={{0,2},{1,3},{2,0},{3,1},{4,6},{5,7},{6,4},{7,5},{8,10},{9,11},{10,... | collective-permute-start | bytes 786440 | tf_op jit(solution)/shard_map/ppermute | solution.py:51
  116.9 13.7 %collective-permute-start.19 = (bf16[32,2,16,128]{3,2,1,0:T(8,128)(2,1)S(1)}, bf16[32,2,16,128]{3,2,1,0:T(8,128)(2,1)S(1)}, u32[]{:S(2)}, u32[]{:S(2)}) collective-permute-start(bf16[32,2,16,128]{3,2,1,0:T(8,128)(2,1)S(1)} %collective-permute-done.18.refs_0_), channel_id=1, source_target_pairs={{0,4},{1,5},{2,6},{3,7},{4,8},{5,9},{6,10},{7,11},{8,12},{9,13},{1... | collective-permute-start | bytes 786440 | tf_op jit(solution)/shard_map/ppermute | solution.py:51
  122.4 8.8 %collective-permute-start.25 = (bf16[32,2,16,128]{3,2,1,0:T(8,128)(2,1)S(1)}, bf16[32,2,16,128]{3,2,1,0:T(8,128)(2,1)S(1)}, u32[]{:S(2)}, u32[]{:S(2)}) collective-permute-start(bf16[32,2,16,128]{3,2,1,0:T(8,128)(2,1)S(1)} %collective-permute-done.18.refs_0_), channel_id=1, source_target_pairs={{0,1},{1,0},{2,3},{3,2},{4,5},{5,4},{6,7},{7,6},{8,9},{9,8},{10,11... | collective-permute-start | bytes 786440 | tf_op jit(solution)/shard_map/ppermute | solution.py:51
  122.4 8.8 %collective-permute-start.32 = (bf16[32,2,16,128]{3,2,1,0:T(8,128)(2,1)S(1)}, bf16[32,2,16,128]{3,2,1,0:T(8,128)(2,1)S(1)}, u32[]{:S(2)}, u32[]{:S(2)}) collective-permute-start(bf16[32,2,16,128]{3,2,1,0:T(8,128)(2,1)S(1)} %collective-permute-done.24.refs_3_), channel_id=1, source_target_pairs={{0,1},{1,0},{2,3},{3,2},{4,5},{5,4},{6,7},{7,6},{8,9},{9,8},{10,11... | collective-permute-start | bytes 786440 | tf_op jit(solution)/shard_map/ppermute | solution.py:51
  154.3 7.4 %collective-permute-start.33 = (bf16[4,32,2,16,128]{4,3,2,1,0:T(8,128)(2,1)S(1)}, bf16[4,32,2,16,128]{4,3,2,1,0:T(8,128)(2,1)}, u32[]{:S(2)}, u32[]{:S(2)}) collective-permute-start(bf16[4,32,2,16,128]{4,3,2,1,0:T(8,128)(2,1)S(1)} %get-tuple-element.67), channel_id=1, source_target_pairs={{0,1},{1,0},{2,3},{3,2},{4,5},{5,4},{6,7},{7,6},{8,9},{9,8},{10,11... | collective-permute-start | bytes 3145736 | tf_op jit(solution)/shard_map/ppermute | solution.py:51
  159.0 9.5 %collective-permute-start.35 = (bf16[32,2,16,128]{3,2,1,0:T(8,128)(2,1)}, bf16[32,2,16,128]{3,2,1,0:T(8,128)(2,1)}, u32[]{:S(2)}, u32[]{:S(2)}) collective-permute-start(bf16[32,2,16,128]{3,2,1,0:T(8,128)(2,1)} %get-tuple-element.106), channel_id=1, source_target_pairs={{0,2},{1,3},{2,0},{3,1},{4,6},{5,7},{6,4},{7,5},{8,10},{9,11},{10,... | collective-permute-start | bytes 786440 | tf_op jit(solution)/shard_map/ppermute | solution.py:51
  159.9 10.4 %collective-permute-start.40 = (bf16[32,2,16,128]{3,2,1,0:T(8,128)(2,1)}, bf16[32,2,16,128]{3,2,1,0:T(8,128)(2,1)S(1)}, u32[]{:S(2)}, u32[]{:S(2)}) collective-permute-start(bf16[32,2,16,128]{3,2,1,0:T(8,128)(2,1)} %get-tuple-element.104), channel_id=1, source_target_pairs={{0,4},{1,5},{2,6},{3,7},{4,8},{5,9},{6,10},{7,11},{8,12},{9,13},{1... | collective-permute-start | bytes 786440 | tf_op jit(solution)/shard_map/ppermute | solution.py:51
  160.4 13.2 %collective-permute-start.38 = (bf16[32,2,16,128]{3,2,1,0:T(8,128)(2,1)}, bf16[32,2,16,128]{3,2,1,0:T(8,128)(2,1)S(1)}, u32[]{:S(2)}, u32[]{:S(2)}) collective-permute-start(bf16[32,2,16,128]{3,2,1,0:T(8,128)(2,1)} %get-tuple-element.105), channel_id=1, source_target_pairs={{0,2},{1,3},{2,0},{3,1},{4,6},{5,7},{6,4},{7,5},{8,10},{9,11},{10,... | collective-permute-start | bytes 786440 | tf_op jit(solution)/shard_map/ppermute | solution.py:51
  169.6 8.8 %collective-permute-start.36 = (bf16[32,2,16,128]{3,2,1,0:T(8,128)(2,1)S(1)}, bf16[32,2,16,128]{3,2,1,0:T(8,128)(2,1)S(1)}, u32[]{:S(2)}, u32[]{:S(2)}) collective-permute-start(bf16[32,2,16,128]{3,2,1,0:T(8,128)(2,1)S(1)} %fusion.2), channel_id=1, source_target_pairs={{0,4},{1,5},{2,6},{3,7},{4,8},{5,9},{6,10},{7,11},{8,12},{9,13},{1... | collective-permute-start | bytes 786440 | tf_op jit(solution)/shard_map/ppermute | solution.py:51
  171.3 11.4 %collective-permute-start.41 = (bf16[32,2,16,128]{3,2,1,0:T(8,128)(2,1)S(1)}, bf16[32,2,16,128]{3,2,1,0:T(8,128)(2,1)S(1)}, u32[]{:S(2)}, u32[]{:S(2)}) collective-permute-start(bf16[32,2,16,128]{3,2,1,0:T(8,128)(2,1)S(1)} %fusion), channel_id=1, source_target_pairs={{0,2},{1,3},{2,0},{3,1},{4,6},{5,7},{6,4},{7,5},{8,10},{9,11},{10,... | collective-permute-start | bytes 786440 | tf_op jit(solution)/shard_map/ppermute | solution.py:51
  179.7 11.4 %collective-permute-start.39 = (bf16[32,2,16,128]{3,2,1,0:T(8,128)(2,1)S(1)}, bf16[32,2,16,128]{3,2,1,0:T(8,128)(2,1)S(1)}, u32[]{:S(2)}, u32[]{:S(2)}) collective-permute-start(bf16[32,2,16,128]{3,2,1,0:T(8,128)(2,1)S(1)} %get-tuple-element.107), channel_id=1, source_target_pairs={{0,12},{1,13},{2,14},{3,15},{4,0},{5,1},{6,2},{7,3},{8,4},{9,5},{1... | collective-permute-start | bytes 786440 | tf_op jit(solution)/shard_map/ppermute | solution.py:51
  179.8 11.3 %collective-permute-start.37 = (bf16[32,2,16,128]{3,2,1,0:T(8,128)(2,1)S(1)}, bf16[32,2,16,128]{3,2,1,0:T(8,128)(2,1)S(1)}, u32[]{:S(2)}, u32[]{:S(2)}) collective-permute-start(bf16[32,2,16,128]{3,2,1,0:T(8,128)(2,1)S(1)} %get-tuple-element.108), channel_id=1, source_target_pairs={{0,4},{1,5},{2,6},{3,7},{4,8},{5,9},{6,10},{7,11},{8,12},{9,13},{1... | collective-permute-start | bytes 786440 | tf_op jit(solution)/shard_map/ppermute | solution.py:51
  191.5 13.5 %collective-permute-start.45 = (bf16[16,64,128]{2,1,0:T(8,128)(2,1)S(1)}, bf16[16,64,128]{2,1,0:T(8,128)(2,1)S(1)}, u32[]{:S(2)}, u32[]{:S(2)}) collective-permute-start(bf16[16,64,128]{2,1,0:T(8,128)(2,1)S(1)} %window.5.refs_4_), channel_id=1, source_target_pairs={{0,12},{1,13},{2,14},{3,15},{4,0},{5,1},{6,2},{7,3},{8,4},{9,5},{1... | collective-permute-start | bytes 786440 | tf_op jit(solution)/shard_map/ppermute | solution.py:51
  191.6 6.4 %collective-permute-start.43 = (bf16[16,64,128]{2,1,0:T(8,128)(2,1)S(1)}, bf16[16,64,128]{2,1,0:T(8,128)(2,1)S(1)}, u32[]{:S(2)}, u32[]{:S(2)}) collective-permute-start(bf16[16,64,128]{2,1,0:T(8,128)(2,1)S(1)} %window.5.refs_4_), channel_id=1, source_target_pairs={{0,2},{1,3},{2,0},{3,1},{4,6},{5,7},{6,4},{7,5},{8,10},{9,11},{10,... | collective-permute-start | bytes 786440 | tf_op jit(solution)/shard_map/ppermute | solution.py:51
  192.5 12.5 %collective-permute-start.42 = (bf16[16,64,128]{2,1,0:T(8,128)(2,1)S(1)}, bf16[16,64,128]{2,1,0:T(8,128)(2,1)S(1)}, u32[]{:S(2)}, u32[]{:S(2)}) collective-permute-start(bf16[16,64,128]{2,1,0:T(8,128)(2,1)S(1)} %window.5.refs_4_), channel_id=1, source_target_pairs={{0,4},{1,5},{2,6},{3,7},{4,8},{5,9},{6,10},{7,11},{8,12},{9,13},{1... | collective-permute-start | bytes 786440 | tf_op jit(solution)/shard_map/ppermute | solution.py:51
  205.0 10.6 %collective-permute-start.44 = (bf16[16,64,128]{2,1,0:T(8,128)(2,1)S(1)}, bf16[16,64,128]{2,1,0:T(8,128)(2,1)S(1)}, u32[]{:S(2)}, u32[]{:S(2)}) collective-permute-start(bf16[16,64,128]{2,1,0:T(8,128)(2,1)S(1)} %collective-permute-done.42.refs_4_), channel_id=1, source_target_pairs={{0,4},{1,5},{2,6},{3,7},{4,8},{5,9},{6,10},{7,11},{8,12},{9,13},{1... | collective-permute-start | bytes 786440 | tf_op jit(solution)/shard_map/ppermute | solution.py:51
  205.0 13.8 %collective-permute-start.48 = (bf16[16,64,128]{2,1,0:T(8,128)(2,1)S(1)}, bf16[16,64,128]{2,1,0:T(8,128)(2,1)S(1)}, u32[]{:S(2)}, u32[]{:S(2)}) collective-permute-start(bf16[16,64,128]{2,1,0:T(8,128)(2,1)S(1)} %collective-permute-done.45.refs_4_), channel_id=1, source_target_pairs={{0,2},{1,3},{2,0},{3,1},{4,6},{5,7},{6,4},{7,5},{8,10},{9,11},{10,... | collective-permute-start | bytes 786440 | tf_op jit(solution)/shard_map/ppermute | solution.py:51
  205.9 13.1 %collective-permute-start.47 = (bf16[16,64,128]{2,1,0:T(8,128)(2,1)S(1)}, bf16[16,64,128]{2,1,0:T(8,128)(2,1)S(1)}, u32[]{:S(2)}, u32[]{:S(2)}) collective-permute-start(bf16[16,64,128]{2,1,0:T(8,128)(2,1)S(1)} %collective-permute-done.43.refs_4_), channel_id=1, source_target_pairs={{0,4},{1,5},{2,6},{3,7},{4,8},{5,9},{6,10},{7,11},{8,12},{9,13},{1... | collective-permute-start | bytes 786440 | tf_op jit(solution)/shard_map/ppermute | solution.py:51
  205.9 18.6 %collective-permute-start.50 = (bf16[32,2,16,128]{3,2,1,0:T(8,128)(2,1)S(1)}, bf16[32,2,16,128]{3,2,1,0:T(8,128)(2,1)S(1)}, u32[]{:S(2)}, u32[]{:S(2)}) collective-permute-start(bf16[32,2,16,128]{3,2,1,0:T(8,128)(2,1)S(1)} %get-tuple-element.71.refs_0_), channel_id=1, source_target_pairs={{0,1},{1,0},{2,3},{3,2},{4,5},{5,4},{6,7},{7,6},{8,9},{9,8},{10,11... | collective-permute-start | bytes 786440 | tf_op jit(solution)/shard_map/ppermute | solution.py:51
  213.1 11.7 %collective-permute-start.53 = (bf16[32,2,16,128]{3,2,1,0:T(8,128)(2,1)S(1)}, bf16[32,2,16,128]{3,2,1,0:T(8,128)(2,1)S(1)}, u32[]{:S(2)}, u32[]{:S(2)}) collective-permute-start(bf16[32,2,16,128]{3,2,1,0:T(8,128)(2,1)S(1)} %get-tuple-element.81.refs_3_), channel_id=1, source_target_pairs={{0,1},{1,0},{2,3},{3,2},{4,5},{5,4},{6,7},{7,6},{8,9},{9,8},{10,11... | collective-permute-start | bytes 786440 | tf_op jit(solution)/shard_map/ppermute | solution.py:51
  215.6 8.7 %collective-permute-start.46 = (bf16[16,64,128]{2,1,0:T(8,128)(2,1)S(1)}, bf16[16,64,128]{2,1,0:T(8,128)(2,1)S(1)}, u32[]{:S(2)}, u32[]{:S(2)}) collective-permute-start(bf16[16,64,128]{2,1,0:T(8,128)(2,1)S(1)} %collective-permute-done.44.refs_4_), channel_id=1, source_target_pairs={{0,2},{1,3},{2,0},{3,1},{4,6},{5,7},{6,4},{7,5},{8,10},{9,11},{10,... | collective-permute-start | bytes 786440 | tf_op jit(solution)/shard_map/ppermute | solution.py:51
  218.9 6.0 %collective-permute-start.51 = (bf16[32,2,16,128]{3,2,1,0:T(8,128)(2,1)S(1)}, bf16[32,2,16,128]{3,2,1,0:T(8,128)(2,1)S(1)}, u32[]{:S(2)}, u32[]{:S(2)}) collective-permute-start(bf16[32,2,16,128]{3,2,1,0:T(8,128)(2,1)S(1)} %get-tuple-element.78.refs_1_), channel_id=1, source_target_pairs={{0,1},{1,0},{2,3},{3,2},{4,5},{5,4},{6,7},{7,6},{8,9},{9,8},{10,11... | collective-permute-start | bytes 786440 | tf_op jit(solution)/shard_map/ppermute | solution.py:51
  218.9 5.9 %collective-permute-start.52 = (bf16[32,2,16,128]{3,2,1,0:T(8,128)(2,1)S(1)}, bf16[32,2,16,128]{3,2,1,0:T(8,128)(2,1)S(1)}, u32[]{:S(2)}, u32[]{:S(2)}) collective-permute-start(bf16[32,2,16,128]{3,2,1,0:T(8,128)(2,1)S(1)} %get-tuple-element.85.refs_2_), channel_id=1, source_target_pairs={{0,1},{1,0},{2,3},{3,2},{4,5},{5,4},{6,7},{7,6},{8,9},{9,8},{10,11... | collective-permute-start | bytes 786440 | tf_op jit(solution)/shard_map/ppermute | solution.py:51
  224.3 11.3 %collective-permute-start.49 = (bf16[32,2,16,128]{3,2,1,0:T(8,128)(2,1)S(1)}, bf16[32,2,16,128]{3,2,1,0:T(8,128)(2,1)S(1)}, u32[]{:S(2)}, u32[]{:S(2)}) collective-permute-start(bf16[32,2,16,128]{3,2,1,0:T(8,128)(2,1)S(1)} %get-tuple-element.75.refs_0_), channel_id=1, source_target_pairs={{0,1},{1,0},{2,3},{3,2},{4,5},{5,4},{6,7},{7,6},{8,9},{9,8},{10,11... | collective-permute-start | bytes 786440 | tf_op jit(solution)/shard_map/ppermute | solution.py:51
  224.4 11.1 %collective-permute-start.56 = (bf16[32,2,16,128]{3,2,1,0:T(8,128)(2,1)S(1)}, bf16[32,2,16,128]{3,2,1,0:T(8,128)(2,1)S(1)}, u32[]{:S(2)}, u32[]{:S(2)}) collective-permute-start(bf16[32,2,16,128]{3,2,1,0:T(8,128)(2,1)S(1)} %get-tuple-element.91.refs_3_), channel_id=1, source_target_pairs={{0,1},{1,0},{2,3},{3,2},{4,5},{5,4},{6,7},{7,6},{8,9},{9,8},{10,11... | collective-permute-start | bytes 786440 | tf_op jit(solution)/shard_map/ppermute | solution.py:51
  244.8 31.5 %collective-permute-start.57 = (bf16[16,32,1024]{2,1,0:T(8,128)(2,1)S(1)}, bf16[16,32,1024]{2,1,0:T(8,128)(2,1)S(1)}, u32[]{:S(2)}, u32[]{:S(2)}) collective-permute-start(bf16[16,32,1024]{2,1,0:T(8,128)(2,1)S(1)} %get-tuple-element.100), channel_id=1, source_target_pairs={{0,1},{1,0},{2,3},{3,2},{4,5},{5,4},{6,7},{7,6},{8,9},{9,8},{10,11... | collective-permute-start | bytes 3145736 | tf_op jit(solution)/shard_map/ppermute | solution.py:51
  246.4 8.6 %collective-permute-start.59 = (bf16[16,64,128]{2,1,0:T(8,128)(2,1)S(1)}, bf16[16,64,128]{2,1,0:T(8,128)(2,1)S(1)}, u32[]{:S(2)}, u32[]{:S(2)}) collective-permute-start(bf16[16,64,128]{2,1,0:T(8,128)(2,1)S(1)} %correlate1.3.refs_0_), channel_id=1, source_target_pairs={{0,2},{1,3},{2,0},{3,1},{4,6},{5,7},{6,4},{7,5},{8,10},{9,11},{10,... | collective-permute-start | bytes 786440 | tf_op jit(solution)/shard_map/ppermute | solution.py:51
  247.6 10.1 %collective-permute-start.58 = (bf16[16,64,128]{2,1,0:T(8,128)(2,1)S(1)}, bf16[16,64,128]{2,1,0:T(8,128)(2,1)S(1)}, u32[]{:S(2)}, u32[]{:S(2)}) collective-permute-start(bf16[16,64,128]{2,1,0:T(8,128)(2,1)S(1)} %correlate1.3.refs_0_), channel_id=1, source_target_pairs={{0,4},{1,5},{2,6},{3,7},{4,8},{5,9},{6,10},{7,11},{8,12},{9,13},{1... | collective-permute-start | bytes 786440 | tf_op jit(solution)/shard_map/ppermute | solution.py:51
  257.7 11.1 %collective-permute-start.60 = (bf16[16,64,128]{2,1,0:T(8,128)(2,1)S(1)}, bf16[16,64,128]{2,1,0:T(8,128)(2,1)S(1)}, u32[]{:S(2)}, u32[]{:S(2)}) collective-permute-start(bf16[16,64,128]{2,1,0:T(8,128)(2,1)S(1)} %collective-permute-done.58.refs_1_), channel_id=1, source_target_pairs={{0,4},{1,5},{2,6},{3,7},{4,8},{5,9},{6,10},{7,11},{8,12},{9,13},{1... | collective-permute-start | bytes 786440 | tf_op jit(solution)/shard_map/ppermute | solution.py:51
  257.7 13.1 %collective-permute-start.61 = (bf16[16,64,128]{2,1,0:T(8,128)(2,1)S(1)}, bf16[16,64,128]{2,1,0:T(8,128)(2,1)S(1)}, u32[]{:S(2)}, u32[]{:S(2)}) collective-permute-start(bf16[16,64,128]{2,1,0:T(8,128)(2,1)S(1)} %correlate1.3.refs_0_), channel_id=1, source_target_pairs={{0,12},{1,13},{2,14},{3,15},{4,0},{5,1},{6,2},{7,3},{8,4},{9,5},{1... | collective-permute-start | bytes 786440 | tf_op jit(solution)/shard_map/ppermute | solution.py:51
  268.7 7.6 %collective-permute-start.63 = (bf16[16,64,128]{2,1,0:T(8,128)(2,1)S(1)}, bf16[16,64,128]{2,1,0:T(8,128)(2,1)S(1)}, u32[]{:S(2)}, u32[]{:S(2)}) collective-permute-start(bf16[16,64,128]{2,1,0:T(8,128)(2,1)S(1)} %collective-permute-done.60.refs_2_), channel_id=1, source_target_pairs={{0,2},{1,3},{2,0},{3,1},{4,6},{5,7},{6,4},{7,5},{8,10},{9,11},{10,... | collective-permute-start | bytes 786440 | tf_op jit(solution)/shard_map/ppermute | solution.py:51
  269.6 8.2 %collective-permute-start.65 = (bf16[16,64,128]{2,1,0:T(8,128)(2,1)S(1)}, bf16[16,64,128]{2,1,0:T(8,128)(2,1)S(1)}, u32[]{:S(2)}, u32[]{:S(2)}) collective-permute-start(bf16[16,64,128]{2,1,0:T(8,128)(2,1)S(1)} %correlate1.3.refs_0_), channel_id=1, source_target_pairs={{0,1},{1,0},{2,3},{3,2},{4,5},{5,4},{6,7},{7,6},{8,9},{9,8},{10,11... | collective-permute-start | bytes 786440 | tf_op jit(solution)/shard_map/ppermute | solution.py:51
  270.7 7.6 %collective-permute-start.68 = (bf16[16,64,128]{2,1,0:T(8,128)(2,1)S(1)}, bf16[16,64,128]{2,1,0:T(8,128)(2,1)S(1)}, u32[]{:S(2)}, u32[]{:S(2)}) collective-permute-start(bf16[16,64,128]{2,1,0:T(8,128)(2,1)S(1)} %collective-permute-done.61.refs_3_), channel_id=1, source_target_pairs={{0,1},{1,0},{2,3},{3,2},{4,5},{5,4},{6,7},{7,6},{8,9},{9,8},{10,11... | collective-permute-start | bytes 786440 | tf_op jit(solution)/shard_map/ppermute | solution.py:51
  270.7 10.0 %collective-permute-start.64 = (bf16[16,64,128]{2,1,0:T(8,128)(2,1)S(1)}, bf16[16,64,128]{2,1,0:T(8,128)(2,1)S(1)}, u32[]{:S(2)}, u32[]{:S(2)}) collective-permute-start(bf16[16,64,128]{2,1,0:T(8,128)(2,1)S(1)} %collective-permute-done.61.refs_3_), channel_id=1, source_target_pairs={{0,2},{1,3},{2,0},{3,1},{4,6},{5,7},{6,4},{7,5},{8,10},{9,11},{10,... | collective-permute-start | bytes 786440 | tf_op jit(solution)/shard_map/ppermute | solution.py:51
  276.3 8.2 %collective-permute-start.62 = (bf16[16,64,128]{2,1,0:T(8,128)(2,1)S(1)}, bf16[16,64,128]{2,1,0:T(8,128)(2,1)S(1)}, u32[]{:S(2)}, u32[]{:S(2)}) collective-permute-start(bf16[16,64,128]{2,1,0:T(8,128)(2,1)S(1)} %collective-permute-done.59.refs_4_), channel_id=1, source_target_pairs={{0,4},{1,5},{2,6},{3,7},{4,8},{5,9},{6,10},{7,11},{8,12},{9,13},{1... | collective-permute-start | bytes 786440 | tf_op jit(solution)/shard_map/ppermute | solution.py:51
  276.3 8.2 %collective-permute-start.69 = (bf16[16,64,128]{2,1,0:T(8,128)(2,1)S(1)}, bf16[16,64,128]{2,1,0:T(8,128)(2,1)S(1)}, u32[]{:S(2)}, u32[]{:S(2)}) collective-permute-start(bf16[16,64,128]{2,1,0:T(8,128)(2,1)S(1)} %collective-permute-done.59.refs_4_), channel_id=1, source_target_pairs={{0,1},{1,0},{2,3},{3,2},{4,5},{5,4},{6,7},{7,6},{8,9},{9,8},{10,11... | collective-permute-start | bytes 786440 | tf_op jit(solution)/shard_map/ppermute | solution.py:51
  277.8 7.2 %collective-permute-start.66 = (bf16[16,64,128]{2,1,0:T(8,128)(2,1)S(1)}, bf16[16,64,128]{2,1,0:T(8,128)(2,1)S(1)}, u32[]{:S(2)}, u32[]{:S(2)}) collective-permute-start(bf16[16,64,128]{2,1,0:T(8,128)(2,1)S(1)} %collective-permute-done.58.refs_1_), channel_id=1, source_target_pairs={{0,1},{1,0},{2,3},{3,2},{4,5},{5,4},{6,7},{7,6},{8,9},{9,8},{10,11... | collective-permute-start | bytes 786440 | tf_op jit(solution)/shard_map/ppermute | solution.py:51
  278.3 7.7 %collective-permute-start.67 = (bf16[16,64,128]{2,1,0:T(8,128)(2,1)S(1)}, bf16[16,64,128]{2,1,0:T(8,128)(2,1)S(1)}, u32[]{:S(2)}, u32[]{:S(2)}) collective-permute-start(bf16[16,64,128]{2,1,0:T(8,128)(2,1)S(1)} %collective-permute-done.60.refs_2_), channel_id=1, source_target_pairs={{0,1},{1,0},{2,3},{3,2},{4,5},{5,4},{6,7},{7,6},{8,9},{9,8},{10,11... | collective-permute-start | bytes 786440 | tf_op jit(solution)/shard_map/ppermute | solution.py:51
  280.7 4.3 %collective-permute-start.72 = (bf16[16,64,128]{2,1,0:T(8,128)(2,1)S(1)}, bf16[16,64,128]{2,1,0:T(8,128)(2,1)S(1)}, u32[]{:S(2)}, u32[]{:S(2)}) collective-permute-start(bf16[16,64,128]{2,1,0:T(8,128)(2,1)S(1)} %collective-permute-done.64.refs_7_), channel_id=1, source_target_pairs={{0,1},{1,0},{2,3},{3,2},{4,5},{5,4},{6,7},{7,6},{8,9},{9,8},{10,11... | collective-permute-start | bytes 786440 | tf_op jit(solution)/shard_map/ppermute | solution.py:51
  (16 other events, 139.8 us)

commit v9 on v8

--- a/solution.py
+++ b/solution.py
@@ -3,6 +3,7 @@
 
 import jax
 import jax.numpy as jnp
+import numpy as np
 from jax import lax
 from jax.experimental import pallas as pl
 from jax.experimental.pallas import tpu as pltpu
@@ -32,6 +33,16 @@
     return forward, inverse.T
 
 
+def constant_tables():
+    freqs = FREQ0 + np.arange(NFW, dtype=np.int32)
+    turns = freqs[:, None] * np.arange(NT, dtype=np.int32)[None, :] % NT
+    phase = turns.astype(np.float32) * np.float32(2.0 * math.pi / NT)
+    basis = np.stack([np.cos(phase), -np.sin(phase)], axis=1).reshape(2 * NFW, NT)
+    forward = (basis * np.float32(1.0 / math.sqrt(NT))).astype(BF16)
+    inverse = (basis * np.float32(math.sqrt(2.0 / NFW))).astype(BF16)
+    return forward, np.ascontiguousarray(inverse.T)
+
+
 class Places:
     def __init__(self, axis, size):
         self.axis = axis
@@ -80,9 +91,9 @@
 
 VMEM = pl.BlockSpec(memory_space=pltpu.VMEM)
 ANY = pl.BlockSpec(memory_space=pl.ANY)
-CHUNKS = 8
+CHUNKS = 16
 STRIPS = 4
-SLOTS = 4
+SLOTS = 5
 
 
 def limit(mebibytes):
@@ -102,6 +113,7 @@
 def analysis_kernel(line, forward_ref, plus_ref, keep0, keep1, send0, send1, held, sems):
     core = own_place(line)[3]
     keep, send = (keep0, keep1), (send0, send1)
+    forward = forward_ref[own_place(line)[0]]
     copy, rows = strip_copies(plus_ref, held, sems, STRIPS)
     for strip in range(STRIPS):
         copy(strip).start()
@@ -112,7 +124,7 @@
             p = strip * rows + row
             for flip, step in relative(line):
                 columns = pl.ds(chip_columns(line, True, flip, step), 2 * LANES)
-                block = jnp.dot(forward_ref[...], held[p, :, columns], preferred_element_type=F32)
+                block = jnp.dot(forward, held[p, :, columns], preferred_element_type=F32)
                 mine, theirs = split_cores(core, block.astype(BF16))
                 keep[flip][step, p] = mine
                 send[flip][step, p] = theirs
@@ -141,14 +153,15 @@
 
 
 def fetch_panels(line, ahead, flip, panel_ref, held, sems):
-    chunks, _, _, rows = held.shape[:4]
+    slots, _, _, rows = held.shape[:4]
 
     def copy(chunk, step):
+        slot = lax.rem(chunk, slots)
         columns = pl.ds(chip_columns(line, ahead, flip, step), 2 * LANES)
         source = panel_ref.at[:, pl.ds(chunk * rows, rows), :, columns]
-        return pltpu.make_async_copy(source, held.at[chunk, step], sems.at[chunk, step])
-
-    for chunk in range(chunks):
+        return pltpu.make_async_copy(source, held.at[slot, step], sems.at[slot, step])
+
+    def start(chunk):
         for step in range(line):
             copy(chunk, step).start()
 
@@ -156,14 +169,16 @@
         for step in range(line):
             copy(chunk, step).wait()
 
-    return wait
+    for chunk in range(slots):
+        start(chunk)
+    return wait, start
 
 
 def panel_scratch(line):
     rows = NFW // CHUNKS
     return [
-        pltpu.VMEM((CHUNKS, line, 2, rows, LANES, 2 * LANES), BF16),
-        pltpu.SemaphoreType.DMA((CHUNKS, line)),
+        pltpu.VMEM((SLOTS, line, 2, rows, LANES, 2 * LANES), BF16),
+        pltpu.SemaphoreType.DMA((SLOTS, line)),
     ]
 
 
@@ -229,7 +244,7 @@
             pltpu.VMEM((SLOTS, 2, NFW // CHUNKS, LANES, reflection.shape[3]), BF16),
             pltpu.SemaphoreType.DMA((SLOTS,)),
         ],
-        compiler_params=limit(20),
+        compiler_params=limit(14),
         cost_estimate=panel_cost(focal, reflection.shape[3]),
         name="convolve",
     )(spectrum, reflection)
@@ -242,15 +257,17 @@
     out_ref, held, sems, *spare = refs[2 * line + 1 + has_base :]
     focal = own[0].shape[2]
     rows = held.shape[3]
-    wait = fetch_panels(line, False, flip, panel_ref, held, sems)
+    slots = held.shape[0]
+    wait, start = fetch_panels(line, False, flip, panel_ref, held, sems)
 
     def body(chunk, carry):
         wait(chunk)
+        slot = lax.rem(chunk, slots)
         for row in range(rows):
             w = chunk * rows + row
             panels, specs = [], []
             for step in range(line):
-                panels.append(held[chunk, step, :, row].reshape(2 * LANES, 2 * LANES))
+                panels.append(held[slot, step, :, row].reshape(2 * LANES, 2 * LANES))
                 mine, theirs = own[step][w], other[step][w]
                 specs.append(
                     join_cores(core, mine.reshape(2 * focal, LANES), theirs.reshape(2 * focal, LANES))
@@ -272,6 +289,11 @@
             else:
                 out_ref[w, 0] = real
                 out_ref[w, 1] = imag
+
+        @pl.when(chunk + slots < CHUNKS)
+        def _():
+            start(chunk + slots)
+
         return carry
 
     lax.fori_loop(0, CHUNKS, body, 0)
@@ -293,7 +315,7 @@
         out_specs=VMEM,
         out_shape=shape,
         scratch_shapes=panel_scratch(line) + spare,
-        compiler_params=limit(24),
+        compiler_params=limit(9),
         cost_estimate=panel_cost(focal, reflection.shape[3] // 2),
         name=f"correlate{flip}",
     )(*own, *other, reflection, *more)
@@ -368,7 +390,9 @@
     start = chip_columns(line, False, flip, step) + core * LANES
     columns = pl.ds(pl.multiple_of(start, LANES), LANES)
     samples = made.shape[2]
-    first = (lax.axis_index("blk") // 2) * (2 * samples)
+    chip = lax.axis_index("blk") // 2
+    chip_inverse = chip_inverse_ref[chip]
+    first = chip * (2 * samples)
     time = first + lax.broadcasted_iota(jnp.int32, (2 * samples, 2 * LANES), 0)
 
     def pair_of(p):
@@ -377,9 +401,7 @@
 
     for p in range(0, focal, 2):
         pair, onset = pair_of(p)
-        values = jnp.dot(
-            chip_inverse_ref[...], jnp.concatenate(pair, axis=1), preferred_element_type=F32
-        )
+        values = jnp.dot(chip_inverse, jnp.concatenate(pair, axis=1), preferred_element_type=F32)
         values = jnp.where(time < jnp.concatenate(onset, axis=1), values, 0.0).astype(BF16)
         low, high = values[:samples], values[samples:]
         mine, theirs = jnp.where(core == 0, low, high), jnp.where(core == 0, high, low)
@@ -406,7 +428,7 @@
 
 def window_at(spec, forward, inverse, onset_times, chip_inverse, line, flip, step, fields):
     focal, k, _ = spec.shape
-    samples = chip_inverse.shape[0] // 2
+    samples = chip_inverse.shape[1] // 2
     field_shape = jax.ShapeDtypeStruct((focal, samples, 2 * line * LANES), BF16)
     begun = bool(fields)
     return pl.pallas_call(
@@ -470,6 +492,7 @@
     plus_ref = rest.pop(0) if has_plus else None
     out_ref, made, out_sems, *spare = rest
     samples = out_ref.shape[1]
+    inverse = inverse_ref[own_place(line)[0]]
     out_copy, rows = strip_copies(made, out_ref, out_sems, STRIPS)
     if has_plus:
         plus, plus_sems = spare
@@ -486,7 +509,7 @@
             for at, (flip, step) in enumerate(places):
                 columns = pl.ds(chip_columns(line, False, flip, step), 2 * LANES)
                 spec = join_cores(core, own[at][p], other[at][p])
-                values = jnp.dot(inverse_ref[...], spec, preferred_element_type=F32)
+                values = jnp.dot(inverse, spec, preferred_element_type=F32)
                 values = jnp.where(time < onset_ref[pl.ds(p, 1), columns], values, 0.0)
                 if has_plus:
                     values += plus[p, :, columns].astype(F32)
@@ -502,7 +525,7 @@
 def field(own, other, inverse, onset_times, line, plus_start=None):
     own, other = sum(own, []), sum(other, [])
     focal, k, _ = own[0].shape
-    samples = inverse.shape[0]
+    samples = inverse.shape[1]
     shape = (focal, samples, onset_times.shape[1])
     plus = [] if plus_start is None else [plus_start]
     moved = [pltpu.VMEM(shape, BF16), pltpu.SemaphoreType.DMA((STRIPS,))]
@@ -581,7 +604,7 @@
         line[step] = places.send(after(line[step + 1], *own), places.shift(size - 1))
     for step in near:
         if step == 1:
-            across[step] = places.send(across[0], places.shift(1))
+            across[step] = places.send(after(across[0], line[size - 1]), places.shift(1))
         else:
             across[step] = places.send(line[step], places.pair())
     middle = run(1, [0], across) + run(0, near, line)
@@ -603,14 +626,14 @@
     places = Places("blk", size)
     line = places.line
     focal, samples, _ = plus_start.shape
-    forward, inverse = tables_of(jnp.arange(NT, dtype=jnp.int32))
-    own_samples = lax.axis_index("blk") * samples + jnp.arange(samples, dtype=jnp.int32)
-    own_forward, own_inverse = tables_of(own_samples)
-    chip_samples = lax.axis_index("blk") // 2 * (2 * samples) + jnp.arange(2 * samples, dtype=jnp.int32)
-    _, chip_inverse = tables_of(chip_samples)
-    sure = contract("kt,tj->kj", forward[:, :SURE], inverse[:SURE]).astype(BF16)
-    forward = jnp.concatenate([forward[:, SURE:], sure], axis=1)
-    inverse = inverse[SURE:]
+    forward, inverse = constant_tables()
+    own_forward = np.ascontiguousarray(forward.reshape(2 * NFW, size, samples).transpose(1, 0, 2))
+    own_inverse = inverse.reshape(size, samples, 2 * NFW)
+    chip_inverse = inverse.reshape(size // 2, 2 * samples, 2 * NFW)
+    sure = forward[:, :SURE].astype(np.float32) @ inverse[:SURE].astype(np.float32)
+    forward = jnp.asarray(np.concatenate([forward[:, SURE:], sure.astype(BF16)], axis=1))
+    inverse = jnp.asarray(inverse[SURE:])
+    own_forward, own_inverse, chip_inverse = map(jnp.asarray, (own_forward, own_inverse, chip_inverse))
 
     fields = []
 
@@ -639,7 +662,7 @@
             spectrum_plus = window([downgoing_spec], forward, inverse, onset_times, base=start)
     mine, theirs = fields
     theirs = places.send(after(theirs, downgoing_spec), places.core())
-    own, _ = gather_chips(places, after(downgoing_spec, own_inverse))
+    own, _ = gather_chips(places, downgoing_spec)
     upgoing = merge(mine, theirs, line)
     other = [swap_cores(places, own[0])]
     across = [own[1][step] if step in (0, 1, line - 1) else after(own[1][step], upgoing) for step in range(line)]

time: 290 us -> 331 us (1.14)
  local copies, waits for them, and re-layouts: 11.5 us -> 55.5 us
  other arithmetic: 14 us -> 2.28 us
  Pallas kernels: 83.8 us -> 87.8 us
  waiting for transfers between devices: 125 us -> 129 us
    unnamed x14 -> x26, local copies, waits for them, and re-layouts: 2.21 us -> 55.3 us
    pallas_call x4, Pallas kernels: 30.8 us -> 38.1 us  [correlate(): pl.pallas_call(functools.partial(correlate_kernel, line, flip, bool(more)...]
    convert_element_type x10 -> x0, local copies, waits for them, and re-layouts: 6.23 us -> none  [the longest x7 4.66 us: tables_of(): inverse = (basis * math.sqrt(2.0 / NFW)).astype(BF16)]
    convert_element_type x6, other arithmetic: 5.12 us -> 1 us  [pass_on(): add(keep0[step], got0[step], *crossed, *carried).astype(BF16)]
    ppermute x73, waiting for transfers between devices: 125 us -> 129 us  [send(): return lax.ppermute(array, self.axis, pairs)]
    convert_element_type x3, other arithmetic: 4.53 us -> 0.73 us  [reduce_scatter(): far = [add(keep, got).astype(BF16) for keep, got in zip(keep1, got1)]]
    pallas_call x2, Pallas kernels: 23.4 us -> 20 us  [convolve(): pl.pallas_call(functools.partial(convolve_kernel, line), in_specs=[VMEM,...]
  transfers between devices with their start and end apart: 73 -> 73, of which waited for: 37 -> 39; matrix products, arithmetic and copies ran while one was open for 8% -> 1% of each run, Pallas kernels for 12% -> 12%
where the time goes in v9:
time: 331 us
  waiting for transfers between devices  129 us (39%)
  Pallas kernels  87.8 us (27%)
  local copies, waits for them, and re-layouts  55.5 us (17%)
  starting transfers between devices  54.9 us (17%)
    ppermute x73, waiting for transfers between devices, send(): return lax.ppermute(array, self.axis, pairs)  129 us
    unnamed x26, local copies, waits for them, and re-layouts  55.3 us
    ppermute x73, starting transfers between devices, send(): return lax.ppermute(array, self.axis, pairs)  54.9 us
    pallas_call x4, Pallas kernels, correlate(): pl.pallas_call(functools.partial(correlate_kernel, line, flip, bool(more)...  38.1 us
    pallas_call x2, Pallas kernels, convolve(): pl.pallas_call(functools.partial(convolve_kernel, line), in_specs=[VMEM,...  20 us
    pallas_call x8, Pallas kernels, window_at(): pl.pallas_call(functools.partial(window_at_kernel, line, flip, step, begu...  19.3 us
  transfers between devices with their start and end apart: 73, of which 39 were waited for; matrix products, arithmetic and copies ran while one was open for 1% of the time, Pallas kernels for 12%

profile of v9, /device:TPU:0, one launch (start us, length us, event | category | flops | bytes accessed | tf_op | source)
XLA Modules:
  0.0 330.9 jit_solution(5864352356399850783)
XLA Ops:
  0.6 1.6 copy-done.7
  3.2 1.9 first_analysis.1
  5.7 2.2 collective-permute-done.1
  8.2 3.0 collective-permute-start.2
  11.2 1.6 collective-permute-start.7
  13.3 5.0 %collective-permute-done.2 = bf16[16,64,128]{2,1,0:T(8,128)(2,1)S(1)} collective-permute-done((bf16[16,64,128]{2,1,0:T(8,128)(2,1)S(1)}, bf16[16,64,128]{2,1,0:T(8,128)(2,1)S(1)}, u32[]{:S(2)}, u32[]{:S(2)}) %collective-permute-start.2) | collective-permute-done | bytes 262176 | tf_op jit(solution)/shard_map/ppermute | solution.py:62
  18.4 2.2 collective-permute-start.3
  22.3 1.5 collective-permute-done.5
  23.8 3.8 %collective-permute-done.3 = bf16[16,64,128]{2,1,0:T(8,128)(2,1)S(1)} collective-permute-done((bf16[16,64,128]{2,1,0:T(8,128)(2,1)S(1)}, bf16[16,64,128]{2,1,0:T(8,128)(2,1)S(1)}, u32[]{:S(2)}, u32[]{:S(2)}) %collective-permute-start.3) | collective-permute-done | bytes 262176 | tf_op jit(solution)/shard_map/ppermute | solution.py:62
  27.9 3.8 %collective-permute-start.6 = (bf16[16,64,128]{2,1,0:T(8,128)(2,1)S(1)}, bf16[16,64,128]{2,1,0:T(8,128)(2,1)S(1)}, u32[]{:S(2)}, u32[]{:S(2)}) collective-permute-start(bf16[16,64,128]{2,1,0:T(8,128)(2,1)S(1)} %get-tuple-element.119), channel_id=1, source_target_pairs={{0,12},{1,13},{2,14},{3,15},{4,0},{5,1},{6,2},{7,3},{8,4},{9,5},{1... | collective-permute-start | bytes 786440 | tf_op jit(solution)/shard_map/ppermute | solution.py:62
  31.7 7.0 %collective-permute-done.4 = bf16[16,64,128]{2,1,0:T(8,128)(2,1)S(1)} collective-permute-done((bf16[16,64,128]{2,1,0:T(8,128)(2,1)S(1)}, bf16[16,64,128]{2,1,0:T(8,128)(2,1)S(1)}, u32[]{:S(2)}, u32[]{:S(2)}) %collective-permute-start.4) | collective-permute-done | bytes 262176 | tf_op jit(solution)/shard_map/ppermute | solution.py:62
  40.1 10.5 %copy-done = bf16[2,32,128,2048]{3,2,1,0:T(8,128)(2,1)S(1)} copy-done((bf16[2,32,128,2048]{3,2,1,0:T(8,128)(2,1)S(1)}, bf16[2,32,128,2048]{3,2,1,0:T(8,128)(2,1)}, u32[]{:S(2)}) %copy-start) | copy-done | bytes 33554456
  50.7 10.0 %convolve.2 = (bf16[4,32,2,16,128]{4,3,2,1,0:T(8,128)(2,1)S(1)}, bf16[4,32,2,16,128]{4,3,2,1,0:T(8,128)(2,1)S(1)}, bf16[4,32,2,16,128]{4,3,2,1,0:T(8,128)(2,1)S(1)}, bf16[4,32,2,16,128]{4,3,2,1,0:T(8,128)(2,1)S(1)}) custom-call(bf16[32,2,16,128]{3,2,1,0:T(8,128)(2,1)S(1)} %bitcast.87, bf16[2,32,128,2048]{3,2,1,0:T(8,128)(2,1)S(1)} %copy-done), custom_call_target="tpu_custom_call" | custom-call | flops 1073741824 | bytes 37748736 | tf_op jit(solution)/shard_map/convolve/pallas_call | solution.py:238
  61.2 2.1 collective-permute-done.10
  66.3 6.5 %collective-permute-done.11 = bf16[32,2,16,128]{3,2,1,0:T(8,128)(2,1)S(1)} collective-permute-done((bf16[32,2,16,128]{3,2,1,0:T(8,128)(2,1)S(1)}, bf16[32,2,16,128]{3,2,1,0:T(8,128)(2,1)S(1)}, u32[]{:S(2)}, u32[]{:S(2)}) %collective-permute-start.11) | collective-permute-done | bytes 262176 | tf_op jit(solution)/shard_map/ppermute | solution.py:62
  75.7 2.7 collective-permute-done.14
  78.4 3.2 collective-permute-done.12
  82.0 1.8 collective-permute-start.13
  83.9 6.5 %collective-permute-done.15.refs_6_ = bf16[32,2,16,128]{3,2,1,0:T(8,128)(2,1)S(1)} collective-permute-done((bf16[32,2,16,128]{3,2,1,0:T(8,128)(2,1)S(1)}, bf16[32,2,16,128]{3,2,1,0:T(8,128)(2,1)S(1)}, u32[]{:S(2)}, u32[]{:S(2)}) %collective-permute-start.15) | collective-permute-done | bytes 262176 | tf_op jit(solution)/shard_map/ppermute | solution.py:62
  90.5 2.8 collective-permute-done.13.refs_5_
  93.3 2.2 window.3.refs_0_
  95.9 1.3 collective-permute-start.18
  97.2 3.4 %collective-permute-start.19 = (bf16[32,2,16,128]{3,2,1,0:T(8,128)(2,1)S(1)}, bf16[32,2,16,128]{3,2,1,0:T(8,128)(2,1)S(1)}, u32[]{:S(2)}, u32[]{:S(2)}) collective-permute-start(bf16[32,2,16,128]{3,2,1,0:T(8,128)(2,1)S(1)} %window.3.refs_0_), channel_id=1, source_target_pairs={{0,12},{1,13},{2,14},{3,15},{4,0},{5,1},{6,2},{7,3},{8,4},{9,5},{1... | collective-permute-start | bytes 786440 | tf_op jit(solution)/shard_map/ppermute | solution.py:62
  100.6 6.1 %collective-permute-done.21.refs_1_ = bf16[32,2,16,128]{3,2,1,0:T(8,128)(2,1)S(1)} collective-permute-done((bf16[32,2,16,128]{3,2,1,0:T(8,128)(2,1)S(1)}, bf16[32,2,16,128]{3,2,1,0:T(8,128)(2,1)S(1)}, u32[]{:S(2)}, u32[]{:S(2)}) %collective-permute-start.21) | collective-permute-done | bytes 262176 | tf_op jit(solution)/shard_map/ppermute | solution.py:62
  108.0 3.3 collective-permute-done.19.refs_3_
  112.5 2.3 collective-permute-done.22.refs_2_
  116.2 4.3 %collective-permute-done.24.refs_3_ = bf16[32,2,16,128]{3,2,1,0:T(8,128)(2,1)S(1)} collective-permute-done((bf16[32,2,16,128]{3,2,1,0:T(8,128)(2,1)S(1)}, bf16[32,2,16,128]{3,2,1,0:T(8,128)(2,1)S(1)}, u32[]{:S(2)}, u32[]{:S(2)}) %collective-permute-start.24) | collective-permute-done | bytes 262176 | tf_op jit(solution)/shard_map/ppermute | solution.py:62
  120.4 10.5 %copy-done.1 = bf16[2,32,128,2048]{3,2,1,0:T(8,128)(2,1)S(1)} copy-done((bf16[2,32,128,2048]{3,2,1,0:T(8,128)(2,1)S(1)}, bf16[2,32,128,2048]{3,2,1,0:T(8,128)(2,1)}, u32[]{:S(2)}) %copy-start.1) | copy-done | bytes 33554456
  131.0 9.5 %correlate0.2.refs_9_ = f32[32,2,16,128]{3,2,1,0:T(8,128)S(1)} custom-call(bf16[32,2,16,128]{3,2,1,0:T(8,128)(2,1)S(1)} %window.3.refs_0_, bf16[32,2,16,128]{3,2,1,0:T(8,128)(2,1)S(1)} %collective-permute-done.21.refs_1_, bf16[32,2,16,128]{3,2,1,0:T(8,128)(2,1)S(1)} %collective-permute-done.22.refs_2_, ...), custom_call_target="tpu_custom_call" | custom-call | flops 536870912 | bytes 18874368 | tf_op jit(solution)/shard_map/correlate0/pallas_call | solution.py:312
  142.6 9.5 %correlate1.2.refs_3_ = f32[32,2,16,128]{3,2,1,0:T(8,128)S(1)} custom-call(bf16[32,2,16,128]{3,2,1,0:T(8,128)(2,1)S(1)} %collective-permute-done.18.refs_0_, bf16[32,2,16,128]{3,2,1,0:T(8,128)(2,1)S(1)} %collective-permute-done.20.refs_1_, bf16[32,2,16,128]{3,2,1,0:T(8,128)(2,1)S(1)} %collective-permute-done.23.refs_2_, ...), custom_call_target="tpu_custom_call" | custom-call | flops 536870912 | bytes 18874368 | tf_op jit(solution)/shard_map/correlate1/pallas_call | solution.py:312
  152.1 2.2 window.4.spec_ref
  154.3 10.5 %copy-done.2 = bf16[2,32,128,2048]{3,2,1,0:T(8,128)(2,1)S(1)} copy-done((bf16[2,32,128,2048]{3,2,1,0:T(8,128)(2,1)S(1)}, bf16[2,32,128,2048]{3,2,1,0:T(8,128)(2,1)}, u32[]{:S(2)}) %copy-start.2) | copy-done | bytes 33554456
  164.8 10.0 %convolve.3 = (bf16[4,32,2,16,128]{4,3,2,1,0:T(8,128)(2,1)S(1)}, bf16[4,32,2,16,128]{4,3,2,1,0:T(8,128)(2,1)S(1)}, bf16[4,32,2,16,128]{4,3,2,1,0:T(8,128)(2,1)S(1)}, bf16[4,32,2,16,128]{4,3,2,1,0:T(8,128)(2,1)S(1)}) custom-call(bf16[32,2,16,128]{3,2,1,0:T(8,128)(2,1)S(1)} %window.4.spec_ref, bf16[2,32,128,2048]{3,2,1,0:T(8,128)(2,1)S(1)} %copy-done.2), custom_call_target="tpu_custom_call" | custom-call | flops 1073741824 | bytes 37748736 | tf_op jit(solution)/shard_map/convolve/pallas_call | solution.py:238
  175.4 2.1 collective-permute-done.34
  180.4 6.5 %collective-permute-done.35 = bf16[32,2,16,128]{3,2,1,0:T(8,128)(2,1)S(1)} collective-permute-done((bf16[32,2,16,128]{3,2,1,0:T(8,128)(2,1)S(1)}, bf16[32,2,16,128]{3,2,1,0:T(8,128)(2,1)S(1)}, u32[]{:S(2)}, u32[]{:S(2)}) %collective-permute-start.35) | collective-permute-done | bytes 262176 | tf_op jit(solution)/shard_map/ppermute | solution.py:62
  187.7 1.4 collective-permute-done.40
  190.1 2.4 collective-permute-done.38
  192.6 4.3 %collective-permute-done.36 = bf16[32,2,16,128]{3,2,1,0:T(8,128)(2,1)S(1)} collective-permute-done((bf16[32,2,16,128]{3,2,1,0:T(8,128)(2,1)S(1)}, bf16[32,2,16,128]{3,2,1,0:T(8,128)(2,1)S(1)}, u32[]{:S(2)}, u32[]{:S(2)}) %collective-permute-start.36) | collective-permute-done | bytes 262176 | tf_op jit(solution)/shard_map/ppermute | solution.py:62
  197.1 2.0 collective-permute-start.37
  199.2 9.3 %collective-permute-done.39.refs_6_ = bf16[32,2,16,128]{3,2,1,0:T(8,128)(2,1)S(1)} collective-permute-done((bf16[32,2,16,128]{3,2,1,0:T(8,128)(2,1)S(1)}, bf16[32,2,16,128]{3,2,1,0:T(8,128)(2,1)S(1)}, u32[]{:S(2)}, u32[]{:S(2)}) %collective-permute-start.39) | collective-permute-done | bytes 262176 | tf_op jit(solution)/shard_map/ppermute | solution.py:62
  210.2 3.8 %collective-permute-start.45 = (bf16[16,64,128]{2,1,0:T(8,128)(2,1)S(1)}, bf16[16,64,128]{2,1,0:T(8,128)(2,1)S(1)}, u32[]{:S(2)}, u32[]{:S(2)}) collective-permute-start(bf16[16,64,128]{2,1,0:T(8,128)(2,1)S(1)} %window.5.refs_4_), channel_id=1, source_target_pairs={{0,12},{1,13},{2,14},{3,15},{4,0},{5,1},{6,2},{7,3},{8,4},{9,5},{1... | collective-permute-start | bytes 786440 | tf_op jit(solution)/shard_map/ppermute | solution.py:62
  214.0 2.4 window_at.8
  216.4 4.3 %collective-permute-done.42.refs_4_ = bf16[16,64,128]{2,1,0:T(8,128)(2,1)S(1)} collective-permute-done((bf16[16,64,128]{2,1,0:T(8,128)(2,1)S(1)}, bf16[16,64,128]{2,1,0:T(8,128)(2,1)S(1)}, u32[]{:S(2)}, u32[]{:S(2)}) %collective-permute-start.42) | collective-permute-done | bytes 262176 | tf_op jit(solution)/shard_map/ppermute | solution.py:62
  220.8 4.3 %collective-permute-done.45.refs_4_ = bf16[16,64,128]{2,1,0:T(8,128)(2,1)S(1)} collective-permute-done((bf16[16,64,128]{2,1,0:T(8,128)(2,1)S(1)}, bf16[16,64,128]{2,1,0:T(8,128)(2,1)S(1)}, u32[]{:S(2)}, u32[]{:S(2)}) %collective-permute-start.45) | collective-permute-done | bytes 262176 | tf_op jit(solution)/shard_map/ppermute | solution.py:62
  226.5 2.4 window_at.9
  228.9 2.4 window_at.10
  231.3 2.4 window_at.11
  235.5 2.4 window_at.12
  238.5 2.4 window_at.13
  240.9 2.4 window_at.14
  244.0 10.5 %copy-done.3 = bf16[2,32,128,2048]{3,2,1,0:T(8,128)(2,1)S(1)} copy-done((bf16[2,32,128,2048]{3,2,1,0:T(8,128)(2,1)S(1)}, bf16[2,32,128,2048]{3,2,1,0:T(8,128)(2,1)}, u32[]{:S(2)}) %copy-start.3) | copy-done | bytes 33554456
  254.5 9.5 %correlate0.3.refs_9_ = f32[32,2,16,128]{3,2,1,0:T(8,128)S(1)} custom-call(bf16[32,2,16,128]{3,2,1,0:T(8,128)(2,1)S(1)} %get-tuple-element.74.refs_0_, bf16[32,2,16,128]{3,2,1,0:T(8,128)(2,1)S(1)} %get-tuple-element.81.refs_1_, bf16[32,2,16,128]{3,2,1,0:T(8,128)(2,1)S(1)} %get-tuple-element.88.refs_2_, ...), custom_call_target="tpu_custom_call" | custom-call | flops 536870912 | bytes 18874368 | tf_op jit(solution)/shard_map/correlate0/pallas_call | solution.py:312
  264.0 2.4 window_at.15
  268.4 10.5 %copy-done.4 = bf16[2,32,128,2048]{3,2,1,0:T(8,128)(2,1)S(1)} copy-done((bf16[2,32,128,2048]{3,2,1,0:T(8,128)(2,1)S(1)}, bf16[2,32,128,2048]{3,2,1,0:T(8,128)(2,1)}, u32[]{:S(2)}) %copy-start.4) | copy-done | bytes 33554456
  278.9 9.7 %correlate1.3.refs_0_ = bf16[16,64,128]{2,1,0:T(8,128)(2,1)S(1)} custom-call(bf16[32,2,16,128]{3,2,1,0:T(8,128)(2,1)S(1)} %get-tuple-element.78.refs_0_, bf16[32,2,16,128]{3,2,1,0:T(8,128)(2,1)S(1)} %get-tuple-element.102.refs_1_, bf16[32,2,16,128]{3,2,1,0:T(8,128)(2,1)S(1)} %get-tuple-element.103.refs_2_, ...), custom_call_target="tpu_custom_call" | custom-call | flops 536870912 | bytes 18874368 | tf_op jit(solution)/shard_map/correlate1/pallas_call | solution.py:312
  290.3 7.1 %collective-permute-done.59.refs_4_ = bf16[16,64,128]{2,1,0:T(8,128)(2,1)S(1)} collective-permute-done((bf16[16,64,128]{2,1,0:T(8,128)(2,1)S(1)}, bf16[16,64,128]{2,1,0:T(8,128)(2,1)S(1)}, u32[]{:S(2)}, u32[]{:S(2)}) %collective-permute-start.59) | collective-permute-done | bytes 262176 | tf_op jit(solution)/shard_map/ppermute | solution.py:62
  297.4 2.4 collective-permute-done.58.refs_1_
  299.8 3.8 %collective-permute-start.61 = (bf16[16,64,128]{2,1,0:T(8,128)(2,1)S(1)}, bf16[16,64,128]{2,1,0:T(8,128)(2,1)S(1)}, u32[]{:S(2)}, u32[]{:S(2)}) collective-permute-start(bf16[16,64,128]{2,1,0:T(8,128)(2,1)S(1)} %correlate1.3.refs_0_), channel_id=1, source_target_pairs={{0,12},{1,13},{2,14},{3,15},{4,0},{5,1},{6,2},{7,3},{8,4},{9,5},{1... | collective-permute-start | bytes 786440 | tf_op jit(solution)/shard_map/ppermute | solution.py:62
  303.6 7.2 %collective-permute-done.60.refs_2_ = bf16[16,64,128]{2,1,0:T(8,128)(2,1)S(1)} collective-permute-done((bf16[16,64,128]{2,1,0:T(8,128)(2,1)S(1)}, bf16[16,64,128]{2,1,0:T(8,128)(2,1)S(1)}, u32[]{:S(2)}, u32[]{:S(2)}) %collective-permute-start.60) | collective-permute-done | bytes 262176 | tf_op jit(solution)/shard_map/ppermute | solution.py:62
  314.0 4.4 %collective-permute-done.63.refs_6_ = bf16[16,64,128]{2,1,0:T(8,128)(2,1)S(1)} collective-permute-done((bf16[16,64,128]{2,1,0:T(8,128)(2,1)S(1)}, bf16[16,64,128]{2,1,0:T(8,128)(2,1)S(1)}, u32[]{:S(2)}, u32[]{:S(2)}) %collective-permute-start.63) | collective-permute-done | bytes 262176 | tf_op jit(solution)/shard_map/ppermute | solution.py:62
  318.4 1.4 merge.1
  320.5 2.3 collective-permute-done.64.refs_7_
  322.8 3.7 %collective-permute-done.62.refs_5_ = bf16[16,64,128]{2,1,0:T(8,128)(2,1)S(1)} collective-permute-done((bf16[16,64,128]{2,1,0:T(8,128)(2,1)S(1)}, bf16[16,64,128]{2,1,0:T(8,128)(2,1)S(1)}, u32[]{:S(2)}, u32[]{:S(2)}) %collective-permute-start.62) | collective-permute-done | bytes 262176 | tf_op jit(solution)/shard_map/ppermute | solution.py:62
  328.4 2.3 field.1
  (146 shorter events, 40.0 us)
Async XLA Ops:
  5.6 7.7 %collective-permute-start = (bf16[4,16,64,128]{3,2,1,0:T(8,128)(2,1)S(1)}, bf16[4,16,64,128]{3,2,1,0:T(8,128)(2,1)S(1)}, u32[]{:S(2)}, u32[]{:S(2)}) collective-permute-start(bf16[4,16,64,128]{3,2,1,0:T(8,128)(2,1)S(1)} %get-tuple-element.56), channel_id=1, source_target_pairs={{0,1},{1,0},{2,3},{3,2},{4,5},{5,4},{6,7},{7,6},{8,9},{9,8},{10,11... | collective-permute-start | bytes 3145736 | tf_op jit(solution)/shard_map/ppermute | solution.py:62
  8.2 10.0 %collective-permute-start.2 = (bf16[16,64,128]{2,1,0:T(8,128)(2,1)S(1)}, bf16[16,64,128]{2,1,0:T(8,128)(2,1)S(1)}, u32[]{:S(2)}, u32[]{:S(2)}) collective-permute-start(bf16[16,64,128]{2,1,0:T(8,128)(2,1)S(1)} %get-tuple-element.120), channel_id=1, source_target_pairs={{0,2},{1,3},{2,0},{3,1},{4,6},{5,7},{6,4},{7,5},{8,10},{9,11},{10,... | collective-permute-start | bytes 786440 | tf_op jit(solution)/shard_map/ppermute | solution.py:62
  11.2 9.9 %collective-permute-start.7 = (bf16[16,64,128]{2,1,0:T(8,128)(2,1)S(1)}, bf16[16,64,128]{2,1,0:T(8,128)(2,1)S(1)}, u32[]{:S(2)}, u32[]{:S(2)}) collective-permute-start(bf16[16,64,128]{2,1,0:T(8,128)(2,1)S(1)} %get-tuple-element.121), channel_id=1, source_target_pairs={{0,4},{1,5},{2,6},{3,7},{4,8},{5,9},{6,10},{7,11},{8,12},{9,13},{1... | collective-permute-start | bytes 786440 | tf_op jit(solution)/shard_map/ppermute | solution.py:62
  12.7 11.0 %collective-permute-start.5 = (bf16[16,64,128]{2,1,0:T(8,128)(2,1)S(1)}, bf16[16,64,128]{2,1,0:T(8,128)(2,1)S(1)}, u32[]{:S(2)}, u32[]{:S(2)}) collective-permute-start(bf16[16,64,128]{2,1,0:T(8,128)(2,1)S(1)} %get-tuple-element.122), channel_id=1, source_target_pairs={{0,2},{1,3},{2,0},{3,1},{4,6},{5,7},{6,4},{7,5},{8,10},{9,11},{10,... | collective-permute-start | bytes 786440 | tf_op jit(solution)/shard_map/ppermute | solution.py:62
  18.4 9.2 %collective-permute-start.3 = (bf16[16,64,128]{2,1,0:T(8,128)(2,1)S(1)}, bf16[16,64,128]{2,1,0:T(8,128)(2,1)S(1)}, u32[]{:S(2)}, u32[]{:S(2)}) collective-permute-start(bf16[16,64,128]{2,1,0:T(8,128)(2,1)S(1)} %fusion.10), channel_id=1, source_target_pairs={{0,4},{1,5},{2,6},{3,7},{4,8},{5,9},{6,10},{7,11},{8,12},{9,13},{1... | collective-permute-start | bytes 786440 | tf_op jit(solution)/shard_map/ppermute | solution.py:62
  21.2 10.5 %collective-permute-start.8 = (bf16[16,64,128]{2,1,0:T(8,128)(2,1)S(1)}, bf16[16,64,128]{2,1,0:T(8,128)(2,1)S(1)}, u32[]{:S(2)}, u32[]{:S(2)}) collective-permute-start(bf16[16,64,128]{2,1,0:T(8,128)(2,1)S(1)} %fusion.8), channel_id=1, source_target_pairs={{0,2},{1,3},{2,0},{3,1},{4,6},{5,7},{6,4},{7,5},{8,10},{9,11},{10,... | collective-permute-start | bytes 786440 | tf_op jit(solution)/shard_map/ppermute | solution.py:62
  27.9 10.8 %collective-permute-start.4 = (bf16[16,64,128]{2,1,0:T(8,128)(2,1)S(1)}, bf16[16,64,128]{2,1,0:T(8,128)(2,1)S(1)}, u32[]{:S(2)}, u32[]{:S(2)}) collective-permute-start(bf16[16,64,128]{2,1,0:T(8,128)(2,1)S(1)} %get-tuple-element.118), channel_id=1, source_target_pairs={{0,4},{1,5},{2,6},{3,7},{4,8},{5,9},{6,10},{7,11},{8,12},{9,13},{1... | collective-permute-start | bytes 786440 | tf_op jit(solution)/shard_map/ppermute | solution.py:62
  27.9 11.8 %collective-permute-start.6 = (bf16[16,64,128]{2,1,0:T(8,128)(2,1)S(1)}, bf16[16,64,128]{2,1,0:T(8,128)(2,1)S(1)}, u32[]{:S(2)}, u32[]{:S(2)}) collective-permute-start(bf16[16,64,128]{2,1,0:T(8,128)(2,1)S(1)} %get-tuple-element.119), channel_id=1, source_target_pairs={{0,12},{1,13},{2,14},{3,15},{4,0},{5,1},{6,2},{7,3},{8,4},{9,5},{1... | collective-permute-start | bytes 786440 | tf_op jit(solution)/shard_map/ppermute | solution.py:62
  60.7 5.5 %collective-permute-start.9 = (bf16[4,32,2,16,128]{4,3,2,1,0:T(8,128)(2,1)S(1)}, bf16[4,32,2,16,128]{4,3,2,1,0:T(8,128)(2,1)S(1)}, u32[]{:S(2)}, u32[]{:S(2)}) collective-permute-start(bf16[4,32,2,16,128]{4,3,2,1,0:T(8,128)(2,1)S(1)} %get-tuple-element.61), channel_id=1, source_target_pairs={{0,1},{1,0},{2,3},{3,2},{4,5},{5,4},{6,7},{7,6},{8,9},{9,8},{10,11... | collective-permute-start | bytes 3145736 | tf_op jit(solution)/shard_map/ppermute | solution.py:62
  63.6 9.2 %collective-permute-start.11 = (bf16[32,2,16,128]{3,2,1,0:T(8,128)(2,1)S(1)}, bf16[32,2,16,128]{3,2,1,0:T(8,128)(2,1)S(1)}, u32[]{:S(2)}, u32[]{:S(2)}) collective-permute-start(bf16[32,2,16,128]{3,2,1,0:T(8,128)(2,1)S(1)} %get-tuple-element.115), channel_id=1, source_target_pairs={{0,2},{1,3},{2,0},{3,1},{4,6},{5,7},{6,4},{7,5},{8,10},{9,11},{10,... | collective-permute-start | bytes 786440 | tf_op jit(solution)/shard_map/ppermute | solution.py:62
  64.8 9.9 %collective-permute-start.16 = (bf16[32,2,16,128]{3,2,1,0:T(8,128)(2,1)S(1)}, bf16[32,2,16,128]{3,2,1,0:T(8,128)(2,1)S(1)}, u32[]{:S(2)}, u32[]{:S(2)}) collective-permute-start(bf16[32,2,16,128]{3,2,1,0:T(8,128)(2,1)S(1)} %get-tuple-element.113), channel_id=1, source_target_pairs={{0,4},{1,5},{2,6},{3,7},{4,8},{5,9},{6,10},{7,11},{8,12},{9,13},{1... | collective-permute-start | bytes 786440 | tf_op jit(solution)/shard_map/ppermute | solution.py:62
  65.7 12.7 %collective-permute-start.14 = (bf16[32,2,16,128]{3,2,1,0:T(8,128)(2,1)S(1)}, bf16[32,2,16,128]{3,2,1,0:T(8,128)(2,1)S(1)}, u32[]{:S(2)}, u32[]{:S(2)}) collective-permute-start(bf16[32,2,16,128]{3,2,1,0:T(8,128)(2,1)S(1)} %get-tuple-element.114), channel_id=1, source_target_pairs={{0,2},{1,3},{2,0},{3,1},{4,6},{5,7},{6,4},{7,5},{8,10},{9,11},{10,... | collective-permute-start | bytes 786440 | tf_op jit(solution)/shard_map/ppermute | solution.py:62
  72.9 8.7 %collective-permute-start.12 = (bf16[32,2,16,128]{3,2,1,0:T(8,128)(2,1)S(1)}, bf16[32,2,16,128]{3,2,1,0:T(8,128)(2,1)S(1)}, u32[]{:S(2)}, u32[]{:S(2)}) collective-permute-start(bf16[32,2,16,128]{3,2,1,0:T(8,128)(2,1)S(1)} %fusion.6), channel_id=1, source_target_pairs={{0,4},{1,5},{2,6},{3,7},{4,8},{5,9},{6,10},{7,11},{8,12},{9,13},{1... | collective-permute-start | bytes 786440 | tf_op jit(solution)/shard_map/ppermute | solution.py:62
  74.8 9.1 %collective-permute-start.17 = (bf16[32,2,16,128]{3,2,1,0:T(8,128)(2,1)S(1)}, bf16[32,2,16,128]{3,2,1,0:T(8,128)(2,1)S(1)}, u32[]{:S(2)}, u32[]{:S(2)}) collective-permute-start(bf16[32,2,16,128]{3,2,1,0:T(8,128)(2,1)S(1)} %fusion.4), channel_id=1, source_target_pairs={{0,2},{1,3},{2,0},{3,1},{4,6},{5,7},{6,4},{7,5},{8,10},{9,11},{10,... | collective-permute-start | bytes 786440 | tf_op jit(solution)/shard_map/ppermute | solution.py:62
  81.8 8.7 %collective-permute-start.15 = (bf16[32,2,16,128]{3,2,1,0:T(8,128)(2,1)S(1)}, bf16[32,2,16,128]{3,2,1,0:T(8,128)(2,1)S(1)}, u32[]{:S(2)}, u32[]{:S(2)}) collective-permute-start(bf16[32,2,16,128]{3,2,1,0:T(8,128)(2,1)S(1)} %get-tuple-element.116), channel_id=1, source_target_pairs={{0,12},{1,13},{2,14},{3,15},{4,0},{5,1},{6,2},{7,3},{8,4},{9,5},{1... | collective-permute-start | bytes 786440 | tf_op jit(solution)/shard_map/ppermute | solution.py:62
  82.0 11.2 %collective-permute-start.13 = (bf16[32,2,16,128]{3,2,1,0:T(8,128)(2,1)S(1)}, bf16[32,2,16,128]{3,2,1,0:T(8,128)(2,1)S(1)}, u32[]{:S(2)}, u32[]{:S(2)}) collective-permute-start(bf16[32,2,16,128]{3,2,1,0:T(8,128)(2,1)S(1)} %get-tuple-element.117), channel_id=1, source_target_pairs={{0,4},{1,5},{2,6},{3,7},{4,8},{5,9},{6,10},{7,11},{8,12},{9,13},{1... | collective-permute-start | bytes 786440 | tf_op jit(solution)/shard_map/ppermute | solution.py:62
  95.5 11.1 %collective-permute-start.21 = (bf16[32,2,16,128]{3,2,1,0:T(8,128)(2,1)S(1)}, bf16[32,2,16,128]{3,2,1,0:T(8,128)(2,1)S(1)}, u32[]{:S(2)}, u32[]{:S(2)}) collective-permute-start(bf16[32,2,16,128]{3,2,1,0:T(8,128)(2,1)S(1)} %window.3.refs_0_), channel_id=1, source_target_pairs={{0,4},{1,5},{2,6},{3,7},{4,8},{5,9},{6,10},{7,11},{8,12},{9,13},{1... | collective-permute-start | bytes 786440 | tf_op jit(solution)/shard_map/ppermute | solution.py:62
  95.9 10.8 %collective-permute-start.18 = (bf16[32,2,16,128]{3,2,1,0:T(8,128)(2,1)S(1)}, bf16[32,2,16,128]{3,2,1,0:T(8,128)(2,1)S(1)}, u32[]{:S(2)}, u32[]{:S(2)}) collective-permute-start(bf16[32,2,16,128]{3,2,1,0:T(8,128)(2,1)S(1)} %window.3.refs_0_), channel_id=1, source_target_pairs={{0,2},{1,3},{2,0},{3,1},{4,6},{5,7},{6,4},{7,5},{8,10},{9,11},{10,... | collective-permute-start | bytes 786440 | tf_op jit(solution)/shard_map/ppermute | solution.py:62
  97.2 14.1 %collective-permute-start.19 = (bf16[32,2,16,128]{3,2,1,0:T(8,128)(2,1)S(1)}, bf16[32,2,16,128]{3,2,1,0:T(8,128)(2,1)S(1)}, u32[]{:S(2)}, u32[]{:S(2)}) collective-permute-start(bf16[32,2,16,128]{3,2,1,0:T(8,128)(2,1)S(1)} %window.3.refs_0_), channel_id=1, source_target_pairs={{0,12},{1,13},{2,14},{3,15},{4,0},{5,1},{6,2},{7,3},{8,4},{9,5},{1... | collective-permute-start | bytes 786440 | tf_op jit(solution)/shard_map/ppermute | solution.py:62
  106.7 8.2 %collective-permute-start.22 = (bf16[32,2,16,128]{3,2,1,0:T(8,128)(2,1)S(1)}, bf16[32,2,16,128]{3,2,1,0:T(8,128)(2,1)S(1)}, u32[]{:S(2)}, u32[]{:S(2)}) collective-permute-start(bf16[32,2,16,128]{3,2,1,0:T(8,128)(2,1)S(1)} %collective-permute-done.21.refs_1_), channel_id=1, source_target_pairs={{0,4},{1,5},{2,6},{3,7},{4,8},{5,9},{6,10},{7,11},{8,12},{9,13},{1... | collective-permute-start | bytes 786440 | tf_op jit(solution)/shard_map/ppermute | solution.py:62
  107.5 7.3 %collective-permute-start.26 = (bf16[32,2,16,128]{3,2,1,0:T(8,128)(2,1)S(1)}, bf16[32,2,16,128]{3,2,1,0:T(8,128)(2,1)S(1)}, u32[]{:S(2)}, u32[]{:S(2)}) collective-permute-start(bf16[32,2,16,128]{3,2,1,0:T(8,128)(2,1)S(1)} %window.3.refs_0_), channel_id=1, source_target_pairs={{0,1},{1,0},{2,3},{3,2},{4,5},{5,4},{6,7},{7,6},{8,9},{9,8},{10,11... | collective-permute-start | bytes 786440 | tf_op jit(solution)/shard_map/ppermute | solution.py:62
  107.5 7.3 %collective-permute-start.27 = (bf16[32,2,16,128]{3,2,1,0:T(8,128)(2,1)S(1)}, bf16[32,2,16,128]{3,2,1,0:T(8,128)(2,1)S(1)}, u32[]{:S(2)}, u32[]{:S(2)}) collective-permute-start(bf16[32,2,16,128]{3,2,1,0:T(8,128)(2,1)S(1)} %collective-permute-done.21.refs_1_), channel_id=1, source_target_pairs={{0,1},{1,0},{2,3},{3,2},{4,5},{5,4},{6,7},{7,6},{8,9},{9,8},{10,11... | collective-permute-start | bytes 786440 | tf_op jit(solution)/shard_map/ppermute | solution.py:62
  111.3 4.6 %collective-permute-start.29 = (bf16[32,2,16,128]{3,2,1,0:T(8,128)(2,1)S(1)}, bf16[32,2,16,128]{3,2,1,0:T(8,128)(2,1)S(1)}, u32[]{:S(2)}, u32[]{:S(2)}) collective-permute-start(bf16[32,2,16,128]{3,2,1,0:T(8,128)(2,1)S(1)} %collective-permute-done.19.refs_3_), channel_id=1, source_target_pairs={{0,1},{1,0},{2,3},{3,2},{4,5},{5,4},{6,7},{7,6},{8,9},{9,8},{10,11... | collective-permute-start | bytes 786440 | tf_op jit(solution)/shard_map/ppermute | solution.py:62
  111.3 9.1 %collective-permute-start.24 = (bf16[32,2,16,128]{3,2,1,0:T(8,128)(2,1)S(1)}, bf16[32,2,16,128]{3,2,1,0:T(8,128)(2,1)S(1)}, u32[]{:S(2)}, u32[]{:S(2)}) collective-permute-start(bf16[32,2,16,128]{3,2,1,0:T(8,128)(2,1)S(1)} %collective-permute-done.19.refs_3_), channel_id=1, source_target_pairs={{0,2},{1,3},{2,0},{3,1},{4,6},{5,7},{6,4},{7,5},{8,10},{9,11},{10,... | collective-permute-start | bytes 786440 | tf_op jit(solution)/shard_map/ppermute | solution.py:62
  114.8 5.6 %collective-permute-start.28 = (bf16[32,2,16,128]{3,2,1,0:T(8,128)(2,1)S(1)}, bf16[32,2,16,128]{3,2,1,0:T(8,128)(2,1)S(1)}, u32[]{:S(2)}, u32[]{:S(2)}) collective-permute-start(bf16[32,2,16,128]{3,2,1,0:T(8,128)(2,1)S(1)} %collective-permute-done.22.refs_2_), channel_id=1, source_target_pairs={{0,1},{1,0},{2,3},{3,2},{4,5},{5,4},{6,7},{7,6},{8,9},{9,8},{10,11... | collective-permute-start | bytes 786440 | tf_op jit(solution)/shard_map/ppermute | solution.py:62
  114.8 25.6 %collective-permute-start.20 = (bf16[32,2,16,128]{3,2,1,0:T(8,128)(2,1)S(1)}, bf16[32,2,16,128]{3,2,1,0:T(8,128)(2,1)S(1)}, u32[]{:S(2)}, u32[]{:S(2)}) collective-permute-start(bf16[32,2,16,128]{3,2,1,0:T(8,128)(2,1)S(1)} %collective-permute-done.18.refs_0_), channel_id=1, source_target_pairs={{0,4},{1,5},{2,6},{3,7},{4,8},{5,9},{6,10},{7,11},{8,12},{9,13},{1... | collective-permute-start | bytes 786440 | tf_op jit(solution)/shard_map/ppermute | solution.py:62
  114.9 26.2 %collective-permute-start.23 = (bf16[32,2,16,128]{3,2,1,0:T(8,128)(2,1)S(1)}, bf16[32,2,16,128]{3,2,1,0:T(8,128)(2,1)S(1)}, u32[]{:S(2)}, u32[]{:S(2)}) collective-permute-start(bf16[32,2,16,128]{3,2,1,0:T(8,128)(2,1)S(1)} %collective-permute-done.22.refs_2_), channel_id=1, source_target_pairs={{0,2},{1,3},{2,0},{3,1},{4,6},{5,7},{6,4},{7,5},{8,10},{9,11},{10,... | collective-permute-start | bytes 786440 | tf_op jit(solution)/shard_map/ppermute | solution.py:62
  115.9 25.2 %collective-permute-start.25 = (bf16[32,2,16,128]{3,2,1,0:T(8,128)(2,1)S(1)}, bf16[32,2,16,128]{3,2,1,0:T(8,128)(2,1)S(1)}, u32[]{:S(2)}, u32[]{:S(2)}) collective-permute-start(bf16[32,2,16,128]{3,2,1,0:T(8,128)(2,1)S(1)} %collective-permute-done.18.refs_0_), channel_id=1, source_target_pairs={{0,1},{1,0},{2,3},{3,2},{4,5},{5,4},{6,7},{7,6},{8,9},{9,8},{10,11... | collective-permute-start | bytes 786440 | tf_op jit(solution)/shard_map/ppermute | solution.py:62
  120.4 20.7 %collective-permute-start.32 = (bf16[32,2,16,128]{3,2,1,0:T(8,128)(2,1)S(1)}, bf16[32,2,16,128]{3,2,1,0:T(8,128)(2,1)S(1)}, u32[]{:S(2)}, u32[]{:S(2)}) collective-permute-start(bf16[32,2,16,128]{3,2,1,0:T(8,128)(2,1)S(1)} %collective-permute-done.24.refs_3_), channel_id=1, source_target_pairs={{0,1},{1,0},{2,3},{3,2},{4,5},{5,4},{6,7},{7,6},{8,9},{9,8},{10,11... | collective-permute-start | bytes 786440 | tf_op jit(solution)/shard_map/ppermute | solution.py:62
  175.2 5.2 %collective-permute-start.33 = (bf16[4,32,2,16,128]{4,3,2,1,0:T(8,128)(2,1)S(1)}, bf16[4,32,2,16,128]{4,3,2,1,0:T(8,128)(2,1)S(1)}, u32[]{:S(2)}, u32[]{:S(2)}) collective-permute-start(bf16[4,32,2,16,128]{4,3,2,1,0:T(8,128)(2,1)S(1)} %get-tuple-element.70), channel_id=1, source_target_pairs={{0,1},{1,0},{2,3},{3,2},{4,5},{5,4},{6,7},{7,6},{8,9},{9,8},{10,11... | collective-permute-start | bytes 3145736 | tf_op jit(solution)/shard_map/ppermute | solution.py:62
  177.7 9.2 %collective-permute-start.35 = (bf16[32,2,16,128]{3,2,1,0:T(8,128)(2,1)S(1)}, bf16[32,2,16,128]{3,2,1,0:T(8,128)(2,1)S(1)}, u32[]{:S(2)}, u32[]{:S(2)}) collective-permute-start(bf16[32,2,16,128]{3,2,1,0:T(8,128)(2,1)S(1)} %get-tuple-element.110), channel_id=1, source_target_pairs={{0,2},{1,3},{2,0},{3,1},{4,6},{5,7},{6,4},{7,5},{8,10},{9,11},{10,... | collective-permute-start | bytes 786440 | tf_op jit(solution)/shard_map/ppermute | solution.py:62
  179.0 10.1 %collective-permute-start.40 = (bf16[32,2,16,128]{3,2,1,0:T(8,128)(2,1)S(1)}, bf16[32,2,16,128]{3,2,1,0:T(8,128)(2,1)S(1)}, u32[]{:S(2)}, u32[]{:S(2)}) collective-permute-start(bf16[32,2,16,128]{3,2,1,0:T(8,128)(2,1)S(1)} %get-tuple-element.108), channel_id=1, source_target_pairs={{0,4},{1,5},{2,6},{3,7},{4,8},{5,9},{6,10},{7,11},{8,12},{9,13},{1... | collective-permute-start | bytes 786440 | tf_op jit(solution)/shard_map/ppermute | solution.py:62
  179.5 13.0 %collective-permute-start.38 = (bf16[32,2,16,128]{3,2,1,0:T(8,128)(2,1)S(1)}, bf16[32,2,16,128]{3,2,1,0:T(8,128)(2,1)S(1)}, u32[]{:S(2)}, u32[]{:S(2)}) collective-permute-start(bf16[32,2,16,128]{3,2,1,0:T(8,128)(2,1)S(1)} %get-tuple-element.109), channel_id=1, source_target_pairs={{0,2},{1,3},{2,0},{3,1},{4,6},{5,7},{6,4},{7,5},{8,10},{9,11},{10,... | collective-permute-start | bytes 786440 | tf_op jit(solution)/shard_map/ppermute | solution.py:62
  187.0 9.8 %collective-permute-start.36 = (bf16[32,2,16,128]{3,2,1,0:T(8,128)(2,1)S(1)}, bf16[32,2,16,128]{3,2,1,0:T(8,128)(2,1)S(1)}, u32[]{:S(2)}, u32[]{:S(2)}) collective-permute-start(bf16[32,2,16,128]{3,2,1,0:T(8,128)(2,1)S(1)} %fusion.2), channel_id=1, source_target_pairs={{0,4},{1,5},{2,6},{3,7},{4,8},{5,9},{6,10},{7,11},{8,12},{9,13},{1... | collective-permute-start | bytes 786440 | tf_op jit(solution)/shard_map/ppermute | solution.py:62
  189.2 10.0 %collective-permute-start.41 = (bf16[32,2,16,128]{3,2,1,0:T(8,128)(2,1)S(1)}, bf16[32,2,16,128]{3,2,1,0:T(8,128)(2,1)S(1)}, u32[]{:S(2)}, u32[]{:S(2)}) collective-permute-start(bf16[32,2,16,128]{3,2,1,0:T(8,128)(2,1)S(1)} %fusion), channel_id=1, source_target_pairs={{0,2},{1,3},{2,0},{3,1},{4,6},{5,7},{6,4},{7,5},{8,10},{9,11},{10,... | collective-permute-start | bytes 786440 | tf_op jit(solution)/shard_map/ppermute | solution.py:62
  197.1 11.5 %collective-permute-start.39 = (bf16[32,2,16,128]{3,2,1,0:T(8,128)(2,1)S(1)}, bf16[32,2,16,128]{3,2,1,0:T(8,128)(2,1)S(1)}, u32[]{:S(2)}, u32[]{:S(2)}) collective-permute-start(bf16[32,2,16,128]{3,2,1,0:T(8,128)(2,1)S(1)} %get-tuple-element.111), channel_id=1, source_target_pairs={{0,12},{1,13},{2,14},{3,15},{4,0},{5,1},{6,2},{7,3},{8,4},{9,5},{1... | collective-permute-start | bytes 786440 | tf_op jit(solution)/shard_map/ppermute | solution.py:62
  197.1 11.4 %collective-permute-start.37 = (bf16[32,2,16,128]{3,2,1,0:T(8,128)(2,1)S(1)}, bf16[32,2,16,128]{3,2,1,0:T(8,128)(2,1)S(1)}, u32[]{:S(2)}, u32[]{:S(2)}) collective-permute-start(bf16[32,2,16,128]{3,2,1,0:T(8,128)(2,1)S(1)} %get-tuple-element.112), channel_id=1, source_target_pairs={{0,4},{1,5},{2,6},{3,7},{4,8},{5,9},{6,10},{7,11},{8,12},{9,13},{1... | collective-permute-start | bytes 786440 | tf_op jit(solution)/shard_map/ppermute | solution.py:62
  208.9 7.5 %collective-permute-start.43 = (bf16[16,64,128]{2,1,0:T(8,128)(2,1)S(1)}, bf16[16,64,128]{2,1,0:T(8,128)(2,1)S(1)}, u32[]{:S(2)}, u32[]{:S(2)}) collective-permute-start(bf16[16,64,128]{2,1,0:T(8,128)(2,1)S(1)} %window.5.refs_4_), channel_id=1, source_target_pairs={{0,2},{1,3},{2,0},{3,1},{4,6},{5,7},{6,4},{7,5},{8,10},{9,11},{10,... | collective-permute-start | bytes 786440 | tf_op jit(solution)/shard_map/ppermute | solution.py:62
  210.2 10.6 %collective-permute-start.42 = (bf16[16,64,128]{2,1,0:T(8,128)(2,1)S(1)}, bf16[16,64,128]{2,1,0:T(8,128)(2,1)S(1)}, u32[]{:S(2)}, u32[]{:S(2)}) collective-permute-start(bf16[16,64,128]{2,1,0:T(8,128)(2,1)S(1)} %window.5.refs_4_), channel_id=1, source_target_pairs={{0,4},{1,5},{2,6},{3,7},{4,8},{5,9},{6,10},{7,11},{8,12},{9,13},{1... | collective-permute-start | bytes 786440 | tf_op jit(solution)/shard_map/ppermute | solution.py:62
  210.2 14.8 %collective-permute-start.45 = (bf16[16,64,128]{2,1,0:T(8,128)(2,1)S(1)}, bf16[16,64,128]{2,1,0:T(8,128)(2,1)S(1)}, u32[]{:S(2)}, u32[]{:S(2)}) collective-permute-start(bf16[16,64,128]{2,1,0:T(8,128)(2,1)S(1)} %window.5.refs_4_), channel_id=1, source_target_pairs={{0,12},{1,13},{2,14},{3,15},{4,0},{5,1},{6,2},{7,3},{8,4},{9,5},{1... | collective-permute-start | bytes 786440 | tf_op jit(solution)/shard_map/ppermute | solution.py:62
  220.8 13.5 %collective-permute-start.44 = (bf16[16,64,128]{2,1,0:T(8,128)(2,1)S(1)}, bf16[16,64,128]{2,1,0:T(8,128)(2,1)S(1)}, u32[]{:S(2)}, u32[]{:S(2)}) collective-permute-start(bf16[16,64,128]{2,1,0:T(8,128)(2,1)S(1)} %collective-permute-done.42.refs_4_), channel_id=1, source_target_pairs={{0,4},{1,5},{2,6},{3,7},{4,8},{5,9},{6,10},{7,11},{8,12},{9,13},{1... | collective-permute-start | bytes 786440 | tf_op jit(solution)/shard_map/ppermute | solution.py:62
  225.1 12.8 %collective-permute-start.48 = (bf16[16,64,128]{2,1,0:T(8,128)(2,1)S(1)}, bf16[16,64,128]{2,1,0:T(8,128)(2,1)S(1)}, u32[]{:S(2)}, u32[]{:S(2)}) collective-permute-start(bf16[16,64,128]{2,1,0:T(8,128)(2,1)S(1)} %collective-permute-done.45.refs_4_), channel_id=1, source_target_pairs={{0,2},{1,3},{2,0},{3,1},{4,6},{5,7},{6,4},{7,5},{8,10},{9,11},{10,... | collective-permute-start | bytes 786440 | tf_op jit(solution)/shard_map/ppermute | solution.py:62
  225.9 12.1 %collective-permute-start.47 = (bf16[16,64,128]{2,1,0:T(8,128)(2,1)S(1)}, bf16[16,64,128]{2,1,0:T(8,128)(2,1)S(1)}, u32[]{:S(2)}, u32[]{:S(2)}) collective-permute-start(bf16[16,64,128]{2,1,0:T(8,128)(2,1)S(1)} %collective-permute-done.43.refs_4_), channel_id=1, source_target_pairs={{0,4},{1,5},{2,6},{3,7},{4,8},{5,9},{6,10},{7,11},{8,12},{9,13},{1... | collective-permute-start | bytes 786440 | tf_op jit(solution)/shard_map/ppermute | solution.py:62
  226.5 17.0 %collective-permute-start.50 = (bf16[32,2,16,128]{3,2,1,0:T(8,128)(2,1)S(1)}, bf16[32,2,16,128]{3,2,1,0:T(8,128)(2,1)S(1)}, u32[]{:S(2)}, u32[]{:S(2)}) collective-permute-start(bf16[32,2,16,128]{3,2,1,0:T(8,128)(2,1)S(1)} %get-tuple-element.74.refs_0_), channel_id=1, source_target_pairs={{0,1},{1,0},{2,3},{3,2},{4,5},{5,4},{6,7},{7,6},{8,9},{9,8},{10,11... | collective-permute-start | bytes 786440 | tf_op jit(solution)/shard_map/ppermute | solution.py:62
  233.7 10.2 %collective-permute-start.53 = (bf16[32,2,16,128]{3,2,1,0:T(8,128)(2,1)S(1)}, bf16[32,2,16,128]{3,2,1,0:T(8,128)(2,1)S(1)}, u32[]{:S(2)}, u32[]{:S(2)}) collective-permute-start(bf16[32,2,16,128]{3,2,1,0:T(8,128)(2,1)S(1)} %get-tuple-element.84.refs_3_), channel_id=1, source_target_pairs={{0,1},{1,0},{2,3},{3,2},{4,5},{5,4},{6,7},{7,6},{8,9},{9,8},{10,11... | collective-permute-start | bytes 786440 | tf_op jit(solution)/shard_map/ppermute | solution.py:62
  234.3 9.0 %collective-permute-start.46 = (bf16[16,64,128]{2,1,0:T(8,128)(2,1)S(1)}, bf16[16,64,128]{2,1,0:T(8,128)(2,1)S(1)}, u32[]{:S(2)}, u32[]{:S(2)}) collective-permute-start(bf16[16,64,128]{2,1,0:T(8,128)(2,1)S(1)} %collective-permute-done.44.refs_4_), channel_id=1, source_target_pairs={{0,2},{1,3},{2,0},{3,1},{4,6},{5,7},{6,4},{7,5},{8,10},{9,11},{10,... | collective-permute-start | bytes 786440 | tf_op jit(solution)/shard_map/ppermute | solution.py:62
  237.9 6.0 %collective-permute-start.51 = (bf16[32,2,16,128]{3,2,1,0:T(8,128)(2,1)S(1)}, bf16[32,2,16,128]{3,2,1,0:T(8,128)(2,1)S(1)}, u32[]{:S(2)}, u32[]{:S(2)}) collective-permute-start(bf16[32,2,16,128]{3,2,1,0:T(8,128)(2,1)S(1)} %get-tuple-element.81.refs_1_), channel_id=1, source_target_pairs={{0,1},{1,0},{2,3},{3,2},{4,5},{5,4},{6,7},{7,6},{8,9},{9,8},{10,11... | collective-permute-start | bytes 786440 | tf_op jit(solution)/shard_map/ppermute | solution.py:62
  238.0 5.9 %collective-permute-start.52 = (bf16[32,2,16,128]{3,2,1,0:T(8,128)(2,1)S(1)}, bf16[32,2,16,128]{3,2,1,0:T(8,128)(2,1)S(1)}, u32[]{:S(2)}, u32[]{:S(2)}) collective-permute-start(bf16[32,2,16,128]{3,2,1,0:T(8,128)(2,1)S(1)} %get-tuple-element.88.refs_2_), channel_id=1, source_target_pairs={{0,1},{1,0},{2,3},{3,2},{4,5},{5,4},{6,7},{7,6},{8,9},{9,8},{10,11... | collective-permute-start | bytes 786440 | tf_op jit(solution)/shard_map/ppermute | solution.py:62
  243.3 23.6 %collective-permute-start.49 = (bf16[32,2,16,128]{3,2,1,0:T(8,128)(2,1)S(1)}, bf16[32,2,16,128]{3,2,1,0:T(8,128)(2,1)S(1)}, u32[]{:S(2)}, u32[]{:S(2)}) collective-permute-start(bf16[32,2,16,128]{3,2,1,0:T(8,128)(2,1)S(1)} %get-tuple-element.78.refs_0_), channel_id=1, source_target_pairs={{0,1},{1,0},{2,3},{3,2},{4,5},{5,4},{6,7},{7,6},{8,9},{9,8},{10,11... | collective-permute-start | bytes 786440 | tf_op jit(solution)/shard_map/ppermute | solution.py:62
  243.5 23.5 %collective-permute-start.56 = (bf16[32,2,16,128]{3,2,1,0:T(8,128)(2,1)S(1)}, bf16[32,2,16,128]{3,2,1,0:T(8,128)(2,1)S(1)}, u32[]{:S(2)}, u32[]{:S(2)}) collective-permute-start(bf16[32,2,16,128]{3,2,1,0:T(8,128)(2,1)S(1)} %get-tuple-element.95.refs_3_), channel_id=1, source_target_pairs={{0,1},{1,0},{2,3},{3,2},{4,5},{5,4},{6,7},{7,6},{8,9},{9,8},{10,11... | collective-permute-start | bytes 786440 | tf_op jit(solution)/shard_map/ppermute | solution.py:62
  288.6 29.8 %collective-permute-start.57 = (bf16[16,32,1024]{2,1,0:T(8,128)(2,1)S(1)}, bf16[16,32,1024]{2,1,0:T(8,128)(2,1)S(1)}, u32[]{:S(2)}, u32[]{:S(2)}) collective-permute-start(bf16[16,32,1024]{2,1,0:T(8,128)(2,1)S(1)} %get-tuple-element.104), channel_id=1, source_target_pairs={{0,1},{1,0},{2,3},{3,2},{4,5},{5,4},{6,7},{7,6},{8,9},{9,8},{10,11... | collective-permute-start | bytes 3145736 | tf_op jit(solution)/shard_map/ppermute | solution.py:62
  288.8 8.6 %collective-permute-start.59 = (bf16[16,64,128]{2,1,0:T(8,128)(2,1)S(1)}, bf16[16,64,128]{2,1,0:T(8,128)(2,1)S(1)}, u32[]{:S(2)}, u32[]{:S(2)}) collective-permute-start(bf16[16,64,128]{2,1,0:T(8,128)(2,1)S(1)} %correlate1.3.refs_0_), channel_id=1, source_target_pairs={{0,2},{1,3},{2,0},{3,1},{4,6},{5,7},{6,4},{7,5},{8,10},{9,11},{10,... | collective-permute-start | bytes 786440 | tf_op jit(solution)/shard_map/ppermute | solution.py:62
  289.7 10.1 %collective-permute-start.58 = (bf16[16,64,128]{2,1,0:T(8,128)(2,1)S(1)}, bf16[16,64,128]{2,1,0:T(8,128)(2,1)S(1)}, u32[]{:S(2)}, u32[]{:S(2)}) collective-permute-start(bf16[16,64,128]{2,1,0:T(8,128)(2,1)S(1)} %correlate1.3.refs_0_), channel_id=1, source_target_pairs={{0,4},{1,5},{2,6},{3,7},{4,8},{5,9},{6,10},{7,11},{8,12},{9,13},{1... | collective-permute-start | bytes 786440 | tf_op jit(solution)/shard_map/ppermute | solution.py:62
  299.8 11.0 %collective-permute-start.60 = (bf16[16,64,128]{2,1,0:T(8,128)(2,1)S(1)}, bf16[16,64,128]{2,1,0:T(8,128)(2,1)S(1)}, u32[]{:S(2)}, u32[]{:S(2)}) collective-permute-start(bf16[16,64,128]{2,1,0:T(8,128)(2,1)S(1)} %collective-permute-done.58.refs_1_), channel_id=1, source_target_pairs={{0,4},{1,5},{2,6},{3,7},{4,8},{5,9},{6,10},{7,11},{8,12},{9,13},{1... | collective-permute-start | bytes 786440 | tf_op jit(solution)/shard_map/ppermute | solution.py:62
  299.8 13.1 %collective-permute-start.61 = (bf16[16,64,128]{2,1,0:T(8,128)(2,1)S(1)}, bf16[16,64,128]{2,1,0:T(8,128)(2,1)S(1)}, u32[]{:S(2)}, u32[]{:S(2)}) collective-permute-start(bf16[16,64,128]{2,1,0:T(8,128)(2,1)S(1)} %correlate1.3.refs_0_), channel_id=1, source_target_pairs={{0,12},{1,13},{2,14},{3,15},{4,0},{5,1},{6,2},{7,3},{8,4},{9,5},{1... | collective-permute-start | bytes 786440 | tf_op jit(solution)/shard_map/ppermute | solution.py:62
  310.8 7.5 %collective-permute-start.63 = (bf16[16,64,128]{2,1,0:T(8,128)(2,1)S(1)}, bf16[16,64,128]{2,1,0:T(8,128)(2,1)S(1)}, u32[]{:S(2)}, u32[]{:S(2)}) collective-permute-start(bf16[16,64,128]{2,1,0:T(8,128)(2,1)S(1)} %collective-permute-done.60.refs_2_), channel_id=1, source_target_pairs={{0,2},{1,3},{2,0},{3,1},{4,6},{5,7},{6,4},{7,5},{8,10},{9,11},{10,... | collective-permute-start | bytes 786440 | tf_op jit(solution)/shard_map/ppermute | solution.py:62
  312.0 7.9 %collective-permute-start.65 = (bf16[16,64,128]{2,1,0:T(8,128)(2,1)S(1)}, bf16[16,64,128]{2,1,0:T(8,128)(2,1)S(1)}, u32[]{:S(2)}, u32[]{:S(2)}) collective-permute-start(bf16[16,64,128]{2,1,0:T(8,128)(2,1)S(1)} %correlate1.3.refs_0_), channel_id=1, source_target_pairs={{0,1},{1,0},{2,3},{3,2},{4,5},{5,4},{6,7},{7,6},{8,9},{9,8},{10,11... | collective-permute-start | bytes 786440 | tf_op jit(solution)/shard_map/ppermute | solution.py:62
  312.8 7.5 %collective-permute-start.68 = (bf16[16,64,128]{2,1,0:T(8,128)(2,1)S(1)}, bf16[16,64,128]{2,1,0:T(8,128)(2,1)S(1)}, u32[]{:S(2)}, u32[]{:S(2)}) collective-permute-start(bf16[16,64,128]{2,1,0:T(8,128)(2,1)S(1)} %collective-permute-done.61.refs_3_), channel_id=1, source_target_pairs={{0,1},{1,0},{2,3},{3,2},{4,5},{5,4},{6,7},{7,6},{8,9},{9,8},{10,11... | collective-permute-start | bytes 786440 | tf_op jit(solution)/shard_map/ppermute | solution.py:62
  312.8 10.0 %collective-permute-start.64 = (bf16[16,64,128]{2,1,0:T(8,128)(2,1)S(1)}, bf16[16,64,128]{2,1,0:T(8,128)(2,1)S(1)}, u32[]{:S(2)}, u32[]{:S(2)}) collective-permute-start(bf16[16,64,128]{2,1,0:T(8,128)(2,1)S(1)} %collective-permute-done.61.refs_3_), channel_id=1, source_target_pairs={{0,2},{1,3},{2,0},{3,1},{4,6},{5,7},{6,4},{7,5},{8,10},{9,11},{10,... | collective-permute-start | bytes 786440 | tf_op jit(solution)/shard_map/ppermute | solution.py:62
  318.3 8.2 %collective-permute-start.62 = (bf16[16,64,128]{2,1,0:T(8,128)(2,1)S(1)}, bf16[16,64,128]{2,1,0:T(8,128)(2,1)S(1)}, u32[]{:S(2)}, u32[]{:S(2)}) collective-permute-start(bf16[16,64,128]{2,1,0:T(8,128)(2,1)S(1)} %collective-permute-done.59.refs_4_), channel_id=1, source_target_pairs={{0,4},{1,5},{2,6},{3,7},{4,8},{5,9},{6,10},{7,11},{8,12},{9,13},{1... | collective-permute-start | bytes 786440 | tf_op jit(solution)/shard_map/ppermute | solution.py:62
  318.4 8.2 %collective-permute-start.69 = (bf16[16,64,128]{2,1,0:T(8,128)(2,1)S(1)}, bf16[16,64,128]{2,1,0:T(8,128)(2,1)S(1)}, u32[]{:S(2)}, u32[]{:S(2)}) collective-permute-start(bf16[16,64,128]{2,1,0:T(8,128)(2,1)S(1)} %collective-permute-done.59.refs_4_), channel_id=1, source_target_pairs={{0,1},{1,0},{2,3},{3,2},{4,5},{5,4},{6,7},{7,6},{8,9},{9,8},{10,11... | collective-permute-start | bytes 786440 | tf_op jit(solution)/shard_map/ppermute | solution.py:62
  319.8 7.2 %collective-permute-start.66 = (bf16[16,64,128]{2,1,0:T(8,128)(2,1)S(1)}, bf16[16,64,128]{2,1,0:T(8,128)(2,1)S(1)}, u32[]{:S(2)}, u32[]{:S(2)}) collective-permute-start(bf16[16,64,128]{2,1,0:T(8,128)(2,1)S(1)} %collective-permute-done.58.refs_1_), channel_id=1, source_target_pairs={{0,1},{1,0},{2,3},{3,2},{4,5},{5,4},{6,7},{7,6},{8,9},{9,8},{10,11... | collective-permute-start | bytes 786440 | tf_op jit(solution)/shard_map/ppermute | solution.py:62
  320.4 7.7 %collective-permute-start.67 = (bf16[16,64,128]{2,1,0:T(8,128)(2,1)S(1)}, bf16[16,64,128]{2,1,0:T(8,128)(2,1)S(1)}, u32[]{:S(2)}, u32[]{:S(2)}) collective-permute-start(bf16[16,64,128]{2,1,0:T(8,128)(2,1)S(1)} %collective-permute-done.60.refs_2_), channel_id=1, source_target_pairs={{0,1},{1,0},{2,3},{3,2},{4,5},{5,4},{6,7},{7,6},{8,9},{9,8},{10,11... | collective-permute-start | bytes 786440 | tf_op jit(solution)/shard_map/ppermute | solution.py:62
  322.8 4.2 %collective-permute-start.72 = (bf16[16,64,128]{2,1,0:T(8,128)(2,1)S(1)}, bf16[16,64,128]{2,1,0:T(8,128)(2,1)S(1)}, u32[]{:S(2)}, u32[]{:S(2)}) collective-permute-start(bf16[16,64,128]{2,1,0:T(8,128)(2,1)S(1)} %collective-permute-done.64.refs_7_), channel_id=1, source_target_pairs={{0,1},{1,0},{2,3},{3,2},{4,5},{5,4},{6,7},{7,6},{8,9},{9,8},{10,11... | collective-permute-start | bytes 786440 | tf_op jit(solution)/shard_map/ppermute | solution.py:62
  (22 other events, 179.7 us)

commit v10 on v9

--- a/solution.py
+++ b/solution.py
@@ -90,10 +90,10 @@
 
 
 VMEM = pl.BlockSpec(memory_space=pltpu.VMEM)
-ANY = pl.BlockSpec(memory_space=pl.ANY)
-CHUNKS = 16
+FAR = pl.BlockSpec(memory_space=pltpu.HBM)
+CHUNKS = 8
 STRIPS = 4
-SLOTS = 5
+SLOTS = 4
 
 
 def limit(mebibytes):
@@ -138,7 +138,7 @@
     out = jax.ShapeDtypeStruct((line, focal, 2 * NFW, LANES), BF16)
     return pl.pallas_call(
         functools.partial(analysis_kernel, line),
-        in_specs=[VMEM, ANY],
+        in_specs=[VMEM, FAR],
         out_specs=[VMEM] * 4,
         out_shape=[out] * 4,
         scratch_shapes=[pltpu.VMEM(plus_start.shape, BF16), pltpu.SemaphoreType.DMA((STRIPS,))],
@@ -237,14 +237,14 @@
     out = jax.ShapeDtypeStruct((line, NFW, 2, focal, LANES), BF16)
     return pl.pallas_call(
         functools.partial(convolve_kernel, line),
-        in_specs=[VMEM, ANY],
+        in_specs=[VMEM, FAR],
         out_specs=[VMEM] * 4,
         out_shape=[out] * 4,
         scratch_shapes=[
             pltpu.VMEM((SLOTS, 2, NFW // CHUNKS, LANES, reflection.shape[3]), BF16),
             pltpu.SemaphoreType.DMA((SLOTS,)),
         ],
-        compiler_params=limit(14),
+        compiler_params=limit(20),
         cost_estimate=panel_cost(focal, reflection.shape[3]),
         name="convolve",
     )(spectrum, reflection)
@@ -311,11 +311,11 @@
     spare = [pltpu.VMEM((2 * NFW * focal, LANES), F32)] if final else []
     return pl.pallas_call(
         functools.partial(correlate_kernel, line, flip, bool(more), final),
-        in_specs=[VMEM] * (2 * line) + [ANY] + [VMEM] * len(more),
+        in_specs=[VMEM] * (2 * line) + [FAR] + [VMEM] * len(more),
         out_specs=VMEM,
         out_shape=shape,
         scratch_shapes=panel_scratch(line) + spare,
-        compiler_params=limit(9),
+        compiler_params=limit(24),
         cost_estimate=panel_cost(focal, reflection.shape[3] // 2),
         name=f"correlate{flip}",
     )(*own, *other, reflection, *more)
@@ -433,8 +433,8 @@
     begun = bool(fields)
     return pl.pallas_call(
         functools.partial(window_at_kernel, line, flip, step, begun),
-        in_specs=[VMEM] * 5 + [ANY] * len(fields),
-        out_specs=[VMEM, ANY, ANY],
+        in_specs=[VMEM] * 5 + [FAR] * len(fields),
+        out_specs=[VMEM, FAR, FAR],
         out_shape=[jax.ShapeDtypeStruct((NFW, 2, focal, LANES), BF16), field_shape, field_shape],
         input_output_aliases={5: 1, 6: 2} if begun else {},
         scratch_shapes=[
@@ -475,7 +475,7 @@
     return pl.pallas_call(
         functools.partial(merge_kernel, line),
         in_specs=[VMEM] * 2,
-        out_specs=ANY,
+        out_specs=FAR,
         out_shape=jax.ShapeDtypeStruct(shape, BF16),
         scratch_shapes=[pltpu.VMEM(shape, BF16), pltpu.SemaphoreType.DMA((STRIPS,))],
         compiler_params=limit(6),
@@ -531,8 +531,8 @@
     moved = [pltpu.VMEM(shape, BF16), pltpu.SemaphoreType.DMA((STRIPS,))]
     return pl.pallas_call(
         functools.partial(field_kernel, line, bool(plus)),
-        in_specs=[VMEM] * (2 + len(own) + len(other)) + [ANY] * len(plus),
-        out_specs=ANY,
+        in_specs=[VMEM] * (2 + len(own) + len(other)) + [FAR] * len(plus),
+        out_specs=FAR,
         out_shape=jax.ShapeDtypeStruct(shape, BF16),
         scratch_shapes=moved * (1 + len(plus)),
         compiler_params=limit(12),
@@ -580,7 +580,7 @@
     return parts + [across[0]]
 
 
-def gather_chips(places, block, work=None):
+def gather_chips(places, block, work=None, together=False):
     size = places.line
     near = [1, size - 1] if size > 2 else [1] if size > 1 else []
     far = list(range(2, size - 1))
@@ -598,6 +598,8 @@
         line[step] = places.send(block, places.shift(step))
     across = {0: places.send(block, places.pair())}
     own = run(0, [0], line)
+    if together:
+        own = [line[size - 1]]
     for step in range(2, size // 2 + 1):
         line[step] = places.send(after(line[step - 1], across[0], *own), places.shift(1))
     for step in range(size - 2, size // 2, -1):
@@ -662,7 +664,7 @@
             spectrum_plus = window([downgoing_spec], forward, inverse, onset_times, base=start)
     mine, theirs = fields
     theirs = places.send(after(theirs, downgoing_spec), places.core())
-    own, _ = gather_chips(places, downgoing_spec)
+    own, _ = gather_chips(places, downgoing_spec, together=True)
     upgoing = merge(mine, theirs, line)
     other = [swap_cores(places, own[0])]
     across = [own[1][step] if step in (0, 1, line - 1) else after(own[1][step], upgoing) for step in range(line)]

time: 331 us -> 279 us (0.84)
  local copies, waits for them, and re-layouts: 55.5 us -> 2.82 us
  Pallas kernels: 87.8 us -> 83.3 us
    unnamed x26 -> x16, local copies, waits for them, and re-layouts: 55.3 us -> 2.58 us
    pallas_call x4, Pallas kernels: 38.1 us -> 30.2 us  [correlate(): pl.pallas_call(functools.partial(correlate_kernel, line, flip, bool(more)...]
    pallas_call x2, Pallas kernels: 20 us -> 23.4 us  [convolve(): pl.pallas_call(functools.partial(convolve_kernel, line), in_specs=[VMEM,...]
    ppermute x73, waiting for transfers between devices: 129 us -> 132 us  [send(): return lax.ppermute(array, self.axis, pairs)]
  transfers between devices with their start and end apart: 73 -> 73, of which waited for: 39 -> 39; matrix products, arithmetic and copies ran while one was open for 1% -> 1% of each run, Pallas kernels for 12% -> 13%
where the time goes in v10:
time: 279 us
  waiting for transfers between devices  132 us (47%)
  Pallas kernels  83.3 us (30%)
  starting transfers between devices  56.4 us (20%)
  local copies, waits for them, and re-layouts  2.82 us (1%)
    ppermute x73, waiting for transfers between devices, send(): return lax.ppermute(array, self.axis, pairs)  132 us
    ppermute x73, starting transfers between devices, send(): return lax.ppermute(array, self.axis, pairs)  56.4 us
    pallas_call x4, Pallas kernels, correlate(): pl.pallas_call(functools.partial(correlate_kernel, line, flip, bool(more)...  30.2 us
    pallas_call x2, Pallas kernels, convolve(): pl.pallas_call(functools.partial(convolve_kernel, line), in_specs=[VMEM,...  23.4 us
    pallas_call x8, Pallas kernels, window_at(): pl.pallas_call(functools.partial(window_at_kernel, line, flip, step, begu...  19.3 us
  transfers between devices with their start and end apart: 73, of which 39 were waited for; matrix products, arithmetic and copies ran while one was open for 1% of the time, Pallas kernels for 13%

profile of v10, /device:TPU:0, one launch (start us, length us, event | category | flops | bytes accessed | tf_op | source)
XLA Modules:
  0.0 278.5 jit_solution(3512402840491759560)
XLA Ops:
  0.6 1.6 copy-done.2
  3.2 1.9 first_analysis.1
  5.7 2.2 collective-permute-done.1
  8.2 3.0 %collective-permute-start.2 = (bf16[16,64,128]{2,1,0:T(8,128)(2,1)S(1)}, bf16[16,64,128]{2,1,0:T(8,128)(2,1)S(1)}, u32[]{:S(2)}, u32[]{:S(2)}) collective-permute-start(bf16[16,64,128]{2,1,0:T(8,128)(2,1)S(1)} %get-tuple-element.120), channel_id=1, source_target_pairs={{0,2},{1,3},{2,0},{3,1},{4,6},{5,7},{6,4},{7,5},{8,10},{9,11},{10,... | collective-permute-start | bytes 786440 | tf_op jit(solution)/shard_map/ppermute | solution.py:62
  11.2 1.6 collective-permute-start.7
  13.3 5.0 %collective-permute-done.2 = bf16[16,64,128]{2,1,0:T(8,128)(2,1)S(1)} collective-permute-done((bf16[16,64,128]{2,1,0:T(8,128)(2,1)S(1)}, bf16[16,64,128]{2,1,0:T(8,128)(2,1)S(1)}, u32[]{:S(2)}, u32[]{:S(2)}) %collective-permute-start.2) | collective-permute-done | bytes 262176 | tf_op jit(solution)/shard_map/ppermute | solution.py:62
  18.4 2.2 collective-permute-start.3
  22.3 1.5 collective-permute-done.5
  23.8 3.8 %collective-permute-done.3 = bf16[16,64,128]{2,1,0:T(8,128)(2,1)S(1)} collective-permute-done((bf16[16,64,128]{2,1,0:T(8,128)(2,1)S(1)}, bf16[16,64,128]{2,1,0:T(8,128)(2,1)S(1)}, u32[]{:S(2)}, u32[]{:S(2)}) %collective-permute-start.3) | collective-permute-done | bytes 262176 | tf_op jit(solution)/shard_map/ppermute | solution.py:62
  27.9 3.8 %collective-permute-start.6 = (bf16[16,64,128]{2,1,0:T(8,128)(2,1)S(1)}, bf16[16,64,128]{2,1,0:T(8,128)(2,1)S(1)}, u32[]{:S(2)}, u32[]{:S(2)}) collective-permute-start(bf16[16,64,128]{2,1,0:T(8,128)(2,1)S(1)} %get-tuple-element.119), channel_id=1, source_target_pairs={{0,12},{1,13},{2,14},{3,15},{4,0},{5,1},{6,2},{7,3},{8,4},{9,5},{1... | collective-permute-start | bytes 786440 | tf_op jit(solution)/shard_map/ppermute | solution.py:62
  31.7 7.0 %collective-permute-done.4 = bf16[16,64,128]{2,1,0:T(8,128)(2,1)S(1)} collective-permute-done((bf16[16,64,128]{2,1,0:T(8,128)(2,1)S(1)}, bf16[16,64,128]{2,1,0:T(8,128)(2,1)S(1)}, u32[]{:S(2)}, u32[]{:S(2)}) %collective-permute-start.4) | collective-permute-done | bytes 262176 | tf_op jit(solution)/shard_map/ppermute | solution.py:62
  40.1 11.7 %convolve.2 = (bf16[4,32,2,16,128]{4,3,2,1,0:T(8,128)(2,1)S(1)}, bf16[4,32,2,16,128]{4,3,2,1,0:T(8,128)(2,1)S(1)}, bf16[4,32,2,16,128]{4,3,2,1,0:T(8,128)(2,1)S(1)}, bf16[4,32,2,16,128]{4,3,2,1,0:T(8,128)(2,1)S(1)}) custom-call(bf16[32,2,16,128]{3,2,1,0:T(8,128)(2,1)S(1)} %bitcast.87, bf16[2,32,128,2048]{3,2,1,0:T(8,128)(2,1)} %refs_8_.7), custom_call_target="tpu_custom_call" | custom-call | flops 1073741824 | bytes 37748736 | tf_op jit(solution)/shard_map/convolve/pallas_call | solution.py:238
  52.4 2.1 collective-permute-done.10
  54.7 1.3 collective-permute-start.11
  57.4 6.5 %collective-permute-done.11 = bf16[32,2,16,128]{3,2,1,0:T(8,128)(2,1)S(1)} collective-permute-done((bf16[32,2,16,128]{3,2,1,0:T(8,128)(2,1)S(1)}, bf16[32,2,16,128]{3,2,1,0:T(8,128)(2,1)S(1)}, u32[]{:S(2)}, u32[]{:S(2)}) %collective-permute-start.11) | collective-permute-done | bytes 262176 | tf_op jit(solution)/shard_map/ppermute | solution.py:62
  66.9 2.7 collective-permute-done.14
  69.6 3.2 %collective-permute-done.12 = bf16[32,2,16,128]{3,2,1,0:T(8,128)(2,1)S(1)} collective-permute-done((bf16[32,2,16,128]{3,2,1,0:T(8,128)(2,1)S(1)}, bf16[32,2,16,128]{3,2,1,0:T(8,128)(2,1)S(1)}, u32[]{:S(2)}, u32[]{:S(2)}) %collective-permute-start.12) | collective-permute-done | bytes 262176 | tf_op jit(solution)/shard_map/ppermute | solution.py:62
  73.2 1.8 collective-permute-start.13
  75.1 6.5 %collective-permute-done.15.refs_6_ = bf16[32,2,16,128]{3,2,1,0:T(8,128)(2,1)S(1)} collective-permute-done((bf16[32,2,16,128]{3,2,1,0:T(8,128)(2,1)S(1)}, bf16[32,2,16,128]{3,2,1,0:T(8,128)(2,1)S(1)}, u32[]{:S(2)}, u32[]{:S(2)}) %collective-permute-start.15) | collective-permute-done | bytes 262176 | tf_op jit(solution)/shard_map/ppermute | solution.py:62
  81.6 2.8 %collective-permute-done.13.refs_5_ = bf16[32,2,16,128]{3,2,1,0:T(8,128)(2,1)S(1)} collective-permute-done((bf16[32,2,16,128]{3,2,1,0:T(8,128)(2,1)S(1)}, bf16[32,2,16,128]{3,2,1,0:T(8,128)(2,1)S(1)}, u32[]{:S(2)}, u32[]{:S(2)}) %collective-permute-start.13) | collective-permute-done | bytes 262176 | tf_op jit(solution)/shard_map/ppermute | solution.py:62
  84.5 2.2 window.3.refs_0_
  87.0 1.4 collective-permute-start.18
  88.4 3.4 %collective-permute-start.19 = (bf16[32,2,16,128]{3,2,1,0:T(8,128)(2,1)S(1)}, bf16[32,2,16,128]{3,2,1,0:T(8,128)(2,1)S(1)}, u32[]{:S(2)}, u32[]{:S(2)}) collective-permute-start(bf16[32,2,16,128]{3,2,1,0:T(8,128)(2,1)S(1)} %window.3.refs_0_), channel_id=1, source_target_pairs={{0,12},{1,13},{2,14},{3,15},{4,0},{5,1},{6,2},{7,3},{8,4},{9,5},{1... | collective-permute-start | bytes 786440 | tf_op jit(solution)/shard_map/ppermute | solution.py:62
  91.8 6.1 %collective-permute-done.21.refs_1_ = bf16[32,2,16,128]{3,2,1,0:T(8,128)(2,1)S(1)} collective-permute-done((bf16[32,2,16,128]{3,2,1,0:T(8,128)(2,1)S(1)}, bf16[32,2,16,128]{3,2,1,0:T(8,128)(2,1)S(1)}, u32[]{:S(2)}, u32[]{:S(2)}) %collective-permute-start.21) | collective-permute-done | bytes 262176 | tf_op jit(solution)/shard_map/ppermute | solution.py:62
  99.3 3.2 %collective-permute-done.19.refs_3_ = bf16[32,2,16,128]{3,2,1,0:T(8,128)(2,1)S(1)} collective-permute-done((bf16[32,2,16,128]{3,2,1,0:T(8,128)(2,1)S(1)}, bf16[32,2,16,128]{3,2,1,0:T(8,128)(2,1)S(1)}, u32[]{:S(2)}, u32[]{:S(2)}) %collective-permute-start.19) | collective-permute-done | bytes 262176 | tf_op jit(solution)/shard_map/ppermute | solution.py:62
  103.7 2.3 collective-permute-done.22.refs_2_
  107.4 4.2 %collective-permute-done.24.refs_3_ = bf16[32,2,16,128]{3,2,1,0:T(8,128)(2,1)S(1)} collective-permute-done((bf16[32,2,16,128]{3,2,1,0:T(8,128)(2,1)S(1)}, bf16[32,2,16,128]{3,2,1,0:T(8,128)(2,1)S(1)}, u32[]{:S(2)}, u32[]{:S(2)}) %collective-permute-start.24) | collective-permute-done | bytes 262176 | tf_op jit(solution)/shard_map/ppermute | solution.py:62
  111.6 7.5 %correlate0.2.refs_9_ = f32[32,2,16,128]{3,2,1,0:T(8,128)S(1)} custom-call(bf16[32,2,16,128]{3,2,1,0:T(8,128)(2,1)S(1)} %window.3.refs_0_, bf16[32,2,16,128]{3,2,1,0:T(8,128)(2,1)S(1)} %collective-permute-done.21.refs_1_, bf16[32,2,16,128]{3,2,1,0:T(8,128)(2,1)S(1)} %collective-permute-done.22.refs_2_, ...), custom_call_target="tpu_custom_call" | custom-call | flops 536870912 | bytes 18874368 | tf_op jit(solution)/shard_map/correlate0/pallas_call | solution.py:312
  121.2 7.5 %correlate1.2.refs_3_ = f32[32,2,16,128]{3,2,1,0:T(8,128)S(1)} custom-call(bf16[32,2,16,128]{3,2,1,0:T(8,128)(2,1)S(1)} %collective-permute-done.18.refs_0_, bf16[32,2,16,128]{3,2,1,0:T(8,128)(2,1)S(1)} %collective-permute-done.20.refs_1_, bf16[32,2,16,128]{3,2,1,0:T(8,128)(2,1)S(1)} %collective-permute-done.23.refs_2_, ...), custom_call_target="tpu_custom_call" | custom-call | flops 536870912 | bytes 18874368 | tf_op jit(solution)/shard_map/correlate1/pallas_call | solution.py:312
  128.8 2.1 window.4.spec_ref
  130.9 11.7 %convolve.3 = (bf16[4,32,2,16,128]{4,3,2,1,0:T(8,128)(2,1)S(1)}, bf16[4,32,2,16,128]{4,3,2,1,0:T(8,128)(2,1)S(1)}, bf16[4,32,2,16,128]{4,3,2,1,0:T(8,128)(2,1)S(1)}, bf16[4,32,2,16,128]{4,3,2,1,0:T(8,128)(2,1)S(1)}) custom-call(bf16[32,2,16,128]{3,2,1,0:T(8,128)(2,1)S(1)} %window.4.spec_ref, bf16[2,32,128,2048]{3,2,1,0:T(8,128)(2,1)} %refs_8_.7), custom_call_target="tpu_custom_call" | custom-call | flops 1073741824 | bytes 37748736 | tf_op jit(solution)/shard_map/convolve/pallas_call | solution.py:238
  143.2 2.2 collective-permute-done.34
  145.6 1.3 collective-permute-start.35
  148.2 6.5 %collective-permute-done.35 = bf16[32,2,16,128]{3,2,1,0:T(8,128)(2,1)S(1)} collective-permute-done((bf16[32,2,16,128]{3,2,1,0:T(8,128)(2,1)S(1)}, bf16[32,2,16,128]{3,2,1,0:T(8,128)(2,1)S(1)}, u32[]{:S(2)}, u32[]{:S(2)}) %collective-permute-start.35) | collective-permute-done | bytes 262176 | tf_op jit(solution)/shard_map/ppermute | solution.py:62
  155.5 1.4 collective-permute-done.40
  157.9 2.4 collective-permute-done.38
  160.4 4.1 %collective-permute-done.36 = bf16[32,2,16,128]{3,2,1,0:T(8,128)(2,1)S(1)} collective-permute-done((bf16[32,2,16,128]{3,2,1,0:T(8,128)(2,1)S(1)}, bf16[32,2,16,128]{3,2,1,0:T(8,128)(2,1)S(1)}, u32[]{:S(2)}, u32[]{:S(2)}) %collective-permute-start.36) | collective-permute-done | bytes 262176 | tf_op jit(solution)/shard_map/ppermute | solution.py:62
  165.0 2.0 collective-permute-start.37
  167.0 9.3 %collective-permute-done.39.refs_6_ = bf16[32,2,16,128]{3,2,1,0:T(8,128)(2,1)S(1)} collective-permute-done((bf16[32,2,16,128]{3,2,1,0:T(8,128)(2,1)S(1)}, bf16[32,2,16,128]{3,2,1,0:T(8,128)(2,1)S(1)}, u32[]{:S(2)}, u32[]{:S(2)}) %collective-permute-start.39) | collective-permute-done | bytes 262176 | tf_op jit(solution)/shard_map/ppermute | solution.py:62
  176.7 1.2 collective-permute-start.43
  178.3 3.5 %collective-permute-start.45 = (bf16[16,64,128]{2,1,0:T(8,128)(2,1)S(1)}, bf16[16,64,128]{2,1,0:T(8,128)(2,1)S(1)}, u32[]{:S(2)}, u32[]{:S(2)}) collective-permute-start(bf16[16,64,128]{2,1,0:T(8,128)(2,1)S(1)} %window.5.refs_4_), channel_id=1, source_target_pairs={{0,12},{1,13},{2,14},{3,15},{4,0},{5,1},{6,2},{7,3},{8,4},{9,5},{1... | collective-permute-start | bytes 786440 | tf_op jit(solution)/shard_map/ppermute | solution.py:62
  181.8 2.4 window_at.8
  184.2 3.7 %collective-permute-done.42.refs_4_ = bf16[16,64,128]{2,1,0:T(8,128)(2,1)S(1)} collective-permute-done((bf16[16,64,128]{2,1,0:T(8,128)(2,1)S(1)}, bf16[16,64,128]{2,1,0:T(8,128)(2,1)S(1)}, u32[]{:S(2)}, u32[]{:S(2)}) %collective-permute-start.42) | collective-permute-done | bytes 262176 | tf_op jit(solution)/shard_map/ppermute | solution.py:62
  188.2 4.5 %collective-permute-done.45.refs_4_ = bf16[16,64,128]{2,1,0:T(8,128)(2,1)S(1)} collective-permute-done((bf16[16,64,128]{2,1,0:T(8,128)(2,1)S(1)}, bf16[16,64,128]{2,1,0:T(8,128)(2,1)S(1)}, u32[]{:S(2)}, u32[]{:S(2)}) %collective-permute-start.45) | collective-permute-done | bytes 262176 | tf_op jit(solution)/shard_map/ppermute | solution.py:62
  194.2 2.4 window_at.9
  196.6 2.4 window_at.10
  199.0 2.4 window_at.11
  202.0 1.2 collective-permute-start.46
  203.2 2.4 window_at.12
  206.2 2.4 window_at.13
  208.6 2.4 window_at.14
  211.7 7.5 %correlate0.3.refs_9_ = f32[32,2,16,128]{3,2,1,0:T(8,128)S(1)} custom-call(bf16[32,2,16,128]{3,2,1,0:T(8,128)(2,1)S(1)} %get-tuple-element.74.refs_0_, bf16[32,2,16,128]{3,2,1,0:T(8,128)(2,1)S(1)} %get-tuple-element.81.refs_1_, bf16[32,2,16,128]{3,2,1,0:T(8,128)(2,1)S(1)} %get-tuple-element.88.refs_2_, ...), custom_call_target="tpu_custom_call" | custom-call | flops 536870912 | bytes 18874368 | tf_op jit(solution)/shard_map/correlate0/pallas_call | solution.py:312
  219.2 2.4 window_at.15
  223.6 7.7 %correlate1.3.refs_0_ = bf16[16,64,128]{2,1,0:T(8,128)(2,1)S(1)} custom-call(bf16[32,2,16,128]{3,2,1,0:T(8,128)(2,1)S(1)} %get-tuple-element.78.refs_0_, bf16[32,2,16,128]{3,2,1,0:T(8,128)(2,1)S(1)} %get-tuple-element.102.refs_1_, bf16[32,2,16,128]{3,2,1,0:T(8,128)(2,1)S(1)} %get-tuple-element.103.refs_2_, ...), custom_call_target="tpu_custom_call" | custom-call | flops 536870912 | bytes 18874368 | tf_op jit(solution)/shard_map/correlate1/pallas_call | solution.py:312
  231.5 3.3 %collective-permute-start.60 = (bf16[16,64,128]{2,1,0:T(8,128)(2,1)S(1)}, bf16[16,64,128]{2,1,0:T(8,128)(2,1)S(1)}, u32[]{:S(2)}, u32[]{:S(2)}) collective-permute-start(bf16[16,64,128]{2,1,0:T(8,128)(2,1)S(1)} %correlate1.3.refs_0_), channel_id=1, source_target_pairs={{0,12},{1,13},{2,14},{3,15},{4,0},{5,1},{6,2},{7,3},{8,4},{9,5},{1... | collective-permute-start | bytes 786440 | tf_op jit(solution)/shard_map/ppermute | solution.py:62
  235.6 5.8 %collective-permute-done.60.refs_3_ = bf16[16,64,128]{2,1,0:T(8,128)(2,1)S(1)} collective-permute-done((bf16[16,64,128]{2,1,0:T(8,128)(2,1)S(1)}, bf16[16,64,128]{2,1,0:T(8,128)(2,1)S(1)}, u32[]{:S(2)}, u32[]{:S(2)}) %collective-permute-start.60) | collective-permute-done | bytes 262176 | tf_op jit(solution)/shard_map/ppermute | solution.py:62
  241.4 1.6 collective-permute-done.59.refs_4_
  243.0 4.2 %collective-permute-done.58.refs_1_ = bf16[16,64,128]{2,1,0:T(8,128)(2,1)S(1)} collective-permute-done((bf16[16,64,128]{2,1,0:T(8,128)(2,1)S(1)}, bf16[16,64,128]{2,1,0:T(8,128)(2,1)S(1)}, u32[]{:S(2)}, u32[]{:S(2)}) %collective-permute-start.58) | collective-permute-done | bytes 262176 | tf_op jit(solution)/shard_map/ppermute | solution.py:62
  247.2 1.8 collective-permute-start.61
  249.0 7.8 %collective-permute-done.61.refs_2_ = bf16[16,64,128]{2,1,0:T(8,128)(2,1)S(1)} collective-permute-done((bf16[16,64,128]{2,1,0:T(8,128)(2,1)S(1)}, bf16[16,64,128]{2,1,0:T(8,128)(2,1)S(1)}, u32[]{:S(2)}, u32[]{:S(2)}) %collective-permute-start.61) | collective-permute-done | bytes 262176 | tf_op jit(solution)/shard_map/ppermute | solution.py:62
  259.3 6.7 %collective-permute-done.63.refs_6_ = bf16[16,64,128]{2,1,0:T(8,128)(2,1)S(1)} collective-permute-done((bf16[16,64,128]{2,1,0:T(8,128)(2,1)S(1)}, bf16[16,64,128]{2,1,0:T(8,128)(2,1)S(1)}, u32[]{:S(2)}, u32[]{:S(2)}) %collective-permute-start.63) | collective-permute-done | bytes 262176 | tf_op jit(solution)/shard_map/ppermute | solution.py:62
  266.1 1.4 merge.1
  269.3 4.9 %collective-permute-done.62.refs_5_ = bf16[16,64,128]{2,1,0:T(8,128)(2,1)S(1)} collective-permute-done((bf16[16,64,128]{2,1,0:T(8,128)(2,1)S(1)}, bf16[16,64,128]{2,1,0:T(8,128)(2,1)S(1)}, u32[]{:S(2)}, u32[]{:S(2)}) %collective-permute-start.62) | collective-permute-done | bytes 262176 | tf_op jit(solution)/shard_map/ppermute | solution.py:62
  276.1 2.3 field.1
  (136 shorter events, 35.8 us)
Async XLA Ops:
  5.6 7.7 %collective-permute-start = (bf16[4,16,64,128]{3,2,1,0:T(8,128)(2,1)S(1)}, bf16[4,16,64,128]{3,2,1,0:T(8,128)(2,1)S(1)}, u32[]{:S(2)}, u32[]{:S(2)}) collective-permute-start(bf16[4,16,64,128]{3,2,1,0:T(8,128)(2,1)S(1)} %get-tuple-element.56), channel_id=1, source_target_pairs={{0,1},{1,0},{2,3},{3,2},{4,5},{5,4},{6,7},{7,6},{8,9},{9,8},{10,11... | collective-permute-start | bytes 3145736 | tf_op jit(solution)/shard_map/ppermute | solution.py:62
  8.2 10.0 %collective-permute-start.2 = (bf16[16,64,128]{2,1,0:T(8,128)(2,1)S(1)}, bf16[16,64,128]{2,1,0:T(8,128)(2,1)S(1)}, u32[]{:S(2)}, u32[]{:S(2)}) collective-permute-start(bf16[16,64,128]{2,1,0:T(8,128)(2,1)S(1)} %get-tuple-element.120), channel_id=1, source_target_pairs={{0,2},{1,3},{2,0},{3,1},{4,6},{5,7},{6,4},{7,5},{8,10},{9,11},{10,... | collective-permute-start | bytes 786440 | tf_op jit(solution)/shard_map/ppermute | solution.py:62
  11.2 9.9 %collective-permute-start.7 = (bf16[16,64,128]{2,1,0:T(8,128)(2,1)S(1)}, bf16[16,64,128]{2,1,0:T(8,128)(2,1)S(1)}, u32[]{:S(2)}, u32[]{:S(2)}) collective-permute-start(bf16[16,64,128]{2,1,0:T(8,128)(2,1)S(1)} %get-tuple-element.121), channel_id=1, source_target_pairs={{0,4},{1,5},{2,6},{3,7},{4,8},{5,9},{6,10},{7,11},{8,12},{9,13},{1... | collective-permute-start | bytes 786440 | tf_op jit(solution)/shard_map/ppermute | solution.py:62
  12.7 11.0 %collective-permute-start.5 = (bf16[16,64,128]{2,1,0:T(8,128)(2,1)S(1)}, bf16[16,64,128]{2,1,0:T(8,128)(2,1)S(1)}, u32[]{:S(2)}, u32[]{:S(2)}) collective-permute-start(bf16[16,64,128]{2,1,0:T(8,128)(2,1)S(1)} %get-tuple-element.122), channel_id=1, source_target_pairs={{0,2},{1,3},{2,0},{3,1},{4,6},{5,7},{6,4},{7,5},{8,10},{9,11},{10,... | collective-permute-start | bytes 786440 | tf_op jit(solution)/shard_map/ppermute | solution.py:62
  18.4 9.2 %collective-permute-start.3 = (bf16[16,64,128]{2,1,0:T(8,128)(2,1)S(1)}, bf16[16,64,128]{2,1,0:T(8,128)(2,1)S(1)}, u32[]{:S(2)}, u32[]{:S(2)}) collective-permute-start(bf16[16,64,128]{2,1,0:T(8,128)(2,1)S(1)} %fusion.10), channel_id=1, source_target_pairs={{0,4},{1,5},{2,6},{3,7},{4,8},{5,9},{6,10},{7,11},{8,12},{9,13},{1... | collective-permute-start | bytes 786440 | tf_op jit(solution)/shard_map/ppermute | solution.py:62
  21.2 10.5 %collective-permute-start.8 = (bf16[16,64,128]{2,1,0:T(8,128)(2,1)S(1)}, bf16[16,64,128]{2,1,0:T(8,128)(2,1)S(1)}, u32[]{:S(2)}, u32[]{:S(2)}) collective-permute-start(bf16[16,64,128]{2,1,0:T(8,128)(2,1)S(1)} %fusion.8), channel_id=1, source_target_pairs={{0,2},{1,3},{2,0},{3,1},{4,6},{5,7},{6,4},{7,5},{8,10},{9,11},{10,... | collective-permute-start | bytes 786440 | tf_op jit(solution)/shard_map/ppermute | solution.py:62
  27.9 10.8 %collective-permute-start.4 = (bf16[16,64,128]{2,1,0:T(8,128)(2,1)S(1)}, bf16[16,64,128]{2,1,0:T(8,128)(2,1)S(1)}, u32[]{:S(2)}, u32[]{:S(2)}) collective-permute-start(bf16[16,64,128]{2,1,0:T(8,128)(2,1)S(1)} %get-tuple-element.118), channel_id=1, source_target_pairs={{0,4},{1,5},{2,6},{3,7},{4,8},{5,9},{6,10},{7,11},{8,12},{9,13},{1... | collective-permute-start | bytes 786440 | tf_op jit(solution)/shard_map/ppermute | solution.py:62
  27.9 11.8 %collective-permute-start.6 = (bf16[16,64,128]{2,1,0:T(8,128)(2,1)S(1)}, bf16[16,64,128]{2,1,0:T(8,128)(2,1)S(1)}, u32[]{:S(2)}, u32[]{:S(2)}) collective-permute-start(bf16[16,64,128]{2,1,0:T(8,128)(2,1)S(1)} %get-tuple-element.119), channel_id=1, source_target_pairs={{0,12},{1,13},{2,14},{3,15},{4,0},{5,1},{6,2},{7,3},{8,4},{9,5},{1... | collective-permute-start | bytes 786440 | tf_op jit(solution)/shard_map/ppermute | solution.py:62
  51.9 5.6 %collective-permute-start.9 = (bf16[4,32,2,16,128]{4,3,2,1,0:T(8,128)(2,1)S(1)}, bf16[4,32,2,16,128]{4,3,2,1,0:T(8,128)(2,1)S(1)}, u32[]{:S(2)}, u32[]{:S(2)}) collective-permute-start(bf16[4,32,2,16,128]{4,3,2,1,0:T(8,128)(2,1)S(1)} %get-tuple-element.61), channel_id=1, source_target_pairs={{0,1},{1,0},{2,3},{3,2},{4,5},{5,4},{6,7},{7,6},{8,9},{9,8},{10,11... | collective-permute-start | bytes 3145736 | tf_op jit(solution)/shard_map/ppermute | solution.py:62
  54.7 9.2 %collective-permute-start.11 = (bf16[32,2,16,128]{3,2,1,0:T(8,128)(2,1)S(1)}, bf16[32,2,16,128]{3,2,1,0:T(8,128)(2,1)S(1)}, u32[]{:S(2)}, u32[]{:S(2)}) collective-permute-start(bf16[32,2,16,128]{3,2,1,0:T(8,128)(2,1)S(1)} %get-tuple-element.115), channel_id=1, source_target_pairs={{0,2},{1,3},{2,0},{3,1},{4,6},{5,7},{6,4},{7,5},{8,10},{9,11},{10,... | collective-permute-start | bytes 786440 | tf_op jit(solution)/shard_map/ppermute | solution.py:62
  56.0 9.9 %collective-permute-start.16 = (bf16[32,2,16,128]{3,2,1,0:T(8,128)(2,1)S(1)}, bf16[32,2,16,128]{3,2,1,0:T(8,128)(2,1)S(1)}, u32[]{:S(2)}, u32[]{:S(2)}) collective-permute-start(bf16[32,2,16,128]{3,2,1,0:T(8,128)(2,1)S(1)} %get-tuple-element.113), channel_id=1, source_target_pairs={{0,4},{1,5},{2,6},{3,7},{4,8},{5,9},{6,10},{7,11},{8,12},{9,13},{1... | collective-permute-start | bytes 786440 | tf_op jit(solution)/shard_map/ppermute | solution.py:62
  56.9 12.6 %collective-permute-start.14 = (bf16[32,2,16,128]{3,2,1,0:T(8,128)(2,1)S(1)}, bf16[32,2,16,128]{3,2,1,0:T(8,128)(2,1)S(1)}, u32[]{:S(2)}, u32[]{:S(2)}) collective-permute-start(bf16[32,2,16,128]{3,2,1,0:T(8,128)(2,1)S(1)} %get-tuple-element.114), channel_id=1, source_target_pairs={{0,2},{1,3},{2,0},{3,1},{4,6},{5,7},{6,4},{7,5},{8,10},{9,11},{10,... | collective-permute-start | bytes 786440 | tf_op jit(solution)/shard_map/ppermute | solution.py:62
  64.1 8.7 %collective-permute-start.12 = (bf16[32,2,16,128]{3,2,1,0:T(8,128)(2,1)S(1)}, bf16[32,2,16,128]{3,2,1,0:T(8,128)(2,1)S(1)}, u32[]{:S(2)}, u32[]{:S(2)}) collective-permute-start(bf16[32,2,16,128]{3,2,1,0:T(8,128)(2,1)S(1)} %fusion.6), channel_id=1, source_target_pairs={{0,4},{1,5},{2,6},{3,7},{4,8},{5,9},{6,10},{7,11},{8,12},{9,13},{1... | collective-permute-start | bytes 786440 | tf_op jit(solution)/shard_map/ppermute | solution.py:62
  66.0 9.1 %collective-permute-start.17 = (bf16[32,2,16,128]{3,2,1,0:T(8,128)(2,1)S(1)}, bf16[32,2,16,128]{3,2,1,0:T(8,128)(2,1)S(1)}, u32[]{:S(2)}, u32[]{:S(2)}) collective-permute-start(bf16[32,2,16,128]{3,2,1,0:T(8,128)(2,1)S(1)} %fusion.4), channel_id=1, source_target_pairs={{0,2},{1,3},{2,0},{3,1},{4,6},{5,7},{6,4},{7,5},{8,10},{9,11},{10,... | collective-permute-start | bytes 786440 | tf_op jit(solution)/shard_map/ppermute | solution.py:62
  73.0 8.7 %collective-permute-start.15 = (bf16[32,2,16,128]{3,2,1,0:T(8,128)(2,1)S(1)}, bf16[32,2,16,128]{3,2,1,0:T(8,128)(2,1)S(1)}, u32[]{:S(2)}, u32[]{:S(2)}) collective-permute-start(bf16[32,2,16,128]{3,2,1,0:T(8,128)(2,1)S(1)} %get-tuple-element.116), channel_id=1, source_target_pairs={{0,12},{1,13},{2,14},{3,15},{4,0},{5,1},{6,2},{7,3},{8,4},{9,5},{1... | collective-permute-start | bytes 786440 | tf_op jit(solution)/shard_map/ppermute | solution.py:62
  73.2 11.2 %collective-permute-start.13 = (bf16[32,2,16,128]{3,2,1,0:T(8,128)(2,1)S(1)}, bf16[32,2,16,128]{3,2,1,0:T(8,128)(2,1)S(1)}, u32[]{:S(2)}, u32[]{:S(2)}) collective-permute-start(bf16[32,2,16,128]{3,2,1,0:T(8,128)(2,1)S(1)} %get-tuple-element.117), channel_id=1, source_target_pairs={{0,4},{1,5},{2,6},{3,7},{4,8},{5,9},{6,10},{7,11},{8,12},{9,13},{1... | collective-permute-start | bytes 786440 | tf_op jit(solution)/shard_map/ppermute | solution.py:62
  86.7 11.1 %collective-permute-start.21 = (bf16[32,2,16,128]{3,2,1,0:T(8,128)(2,1)S(1)}, bf16[32,2,16,128]{3,2,1,0:T(8,128)(2,1)S(1)}, u32[]{:S(2)}, u32[]{:S(2)}) collective-permute-start(bf16[32,2,16,128]{3,2,1,0:T(8,128)(2,1)S(1)} %window.3.refs_0_), channel_id=1, source_target_pairs={{0,4},{1,5},{2,6},{3,7},{4,8},{5,9},{6,10},{7,11},{8,12},{9,13},{1... | collective-permute-start | bytes 786440 | tf_op jit(solution)/shard_map/ppermute | solution.py:62
  87.0 10.8 %collective-permute-start.18 = (bf16[32,2,16,128]{3,2,1,0:T(8,128)(2,1)S(1)}, bf16[32,2,16,128]{3,2,1,0:T(8,128)(2,1)S(1)}, u32[]{:S(2)}, u32[]{:S(2)}) collective-permute-start(bf16[32,2,16,128]{3,2,1,0:T(8,128)(2,1)S(1)} %window.3.refs_0_), channel_id=1, source_target_pairs={{0,2},{1,3},{2,0},{3,1},{4,6},{5,7},{6,4},{7,5},{8,10},{9,11},{10,... | collective-permute-start | bytes 786440 | tf_op jit(solution)/shard_map/ppermute | solution.py:62
  88.4 14.1 %collective-permute-start.19 = (bf16[32,2,16,128]{3,2,1,0:T(8,128)(2,1)S(1)}, bf16[32,2,16,128]{3,2,1,0:T(8,128)(2,1)S(1)}, u32[]{:S(2)}, u32[]{:S(2)}) collective-permute-start(bf16[32,2,16,128]{3,2,1,0:T(8,128)(2,1)S(1)} %window.3.refs_0_), channel_id=1, source_target_pairs={{0,12},{1,13},{2,14},{3,15},{4,0},{5,1},{6,2},{7,3},{8,4},{9,5},{1... | collective-permute-start | bytes 786440 | tf_op jit(solution)/shard_map/ppermute | solution.py:62
  97.8 8.2 %collective-permute-start.22 = (bf16[32,2,16,128]{3,2,1,0:T(8,128)(2,1)S(1)}, bf16[32,2,16,128]{3,2,1,0:T(8,128)(2,1)S(1)}, u32[]{:S(2)}, u32[]{:S(2)}) collective-permute-start(bf16[32,2,16,128]{3,2,1,0:T(8,128)(2,1)S(1)} %collective-permute-done.21.refs_1_), channel_id=1, source_target_pairs={{0,4},{1,5},{2,6},{3,7},{4,8},{5,9},{6,10},{7,11},{8,12},{9,13},{1... | collective-permute-start | bytes 786440 | tf_op jit(solution)/shard_map/ppermute | solution.py:62
  98.8 7.2 %collective-permute-start.26 = (bf16[32,2,16,128]{3,2,1,0:T(8,128)(2,1)S(1)}, bf16[32,2,16,128]{3,2,1,0:T(8,128)(2,1)S(1)}, u32[]{:S(2)}, u32[]{:S(2)}) collective-permute-start(bf16[32,2,16,128]{3,2,1,0:T(8,128)(2,1)S(1)} %window.3.refs_0_), channel_id=1, source_target_pairs={{0,1},{1,0},{2,3},{3,2},{4,5},{5,4},{6,7},{7,6},{8,9},{9,8},{10,11... | collective-permute-start | bytes 786440 | tf_op jit(solution)/shard_map/ppermute | solution.py:62
  98.8 7.2 %collective-permute-start.27 = (bf16[32,2,16,128]{3,2,1,0:T(8,128)(2,1)S(1)}, bf16[32,2,16,128]{3,2,1,0:T(8,128)(2,1)S(1)}, u32[]{:S(2)}, u32[]{:S(2)}) collective-permute-start(bf16[32,2,16,128]{3,2,1,0:T(8,128)(2,1)S(1)} %collective-permute-done.21.refs_1_), channel_id=1, source_target_pairs={{0,1},{1,0},{2,3},{3,2},{4,5},{5,4},{6,7},{7,6},{8,9},{9,8},{10,11... | collective-permute-start | bytes 786440 | tf_op jit(solution)/shard_map/ppermute | solution.py:62
  102.5 4.7 %collective-permute-start.29 = (bf16[32,2,16,128]{3,2,1,0:T(8,128)(2,1)S(1)}, bf16[32,2,16,128]{3,2,1,0:T(8,128)(2,1)S(1)}, u32[]{:S(2)}, u32[]{:S(2)}) collective-permute-start(bf16[32,2,16,128]{3,2,1,0:T(8,128)(2,1)S(1)} %collective-permute-done.19.refs_3_), channel_id=1, source_target_pairs={{0,1},{1,0},{2,3},{3,2},{4,5},{5,4},{6,7},{7,6},{8,9},{9,8},{10,11... | collective-permute-start | bytes 786440 | tf_op jit(solution)/shard_map/ppermute | solution.py:62
  102.5 9.1 %collective-permute-start.24 = (bf16[32,2,16,128]{3,2,1,0:T(8,128)(2,1)S(1)}, bf16[32,2,16,128]{3,2,1,0:T(8,128)(2,1)S(1)}, u32[]{:S(2)}, u32[]{:S(2)}) collective-permute-start(bf16[32,2,16,128]{3,2,1,0:T(8,128)(2,1)S(1)} %collective-permute-done.19.refs_3_), channel_id=1, source_target_pairs={{0,2},{1,3},{2,0},{3,1},{4,6},{5,7},{6,4},{7,5},{8,10},{9,11},{10,... | collective-permute-start | bytes 786440 | tf_op jit(solution)/shard_map/ppermute | solution.py:62
  106.0 5.6 %collective-permute-start.28 = (bf16[32,2,16,128]{3,2,1,0:T(8,128)(2,1)S(1)}, bf16[32,2,16,128]{3,2,1,0:T(8,128)(2,1)S(1)}, u32[]{:S(2)}, u32[]{:S(2)}) collective-permute-start(bf16[32,2,16,128]{3,2,1,0:T(8,128)(2,1)S(1)} %collective-permute-done.22.refs_2_), channel_id=1, source_target_pairs={{0,1},{1,0},{2,3},{3,2},{4,5},{5,4},{6,7},{7,6},{8,9},{9,8},{10,11... | collective-permute-start | bytes 786440 | tf_op jit(solution)/shard_map/ppermute | solution.py:62
  106.0 13.1 %collective-permute-start.20 = (bf16[32,2,16,128]{3,2,1,0:T(8,128)(2,1)S(1)}, bf16[32,2,16,128]{3,2,1,0:T(8,128)(2,1)S(1)}, u32[]{:S(2)}, u32[]{:S(2)}) collective-permute-start(bf16[32,2,16,128]{3,2,1,0:T(8,128)(2,1)S(1)} %collective-permute-done.18.refs_0_), channel_id=1, source_target_pairs={{0,4},{1,5},{2,6},{3,7},{4,8},{5,9},{6,10},{7,11},{8,12},{9,13},{1... | collective-permute-start | bytes 786440 | tf_op jit(solution)/shard_map/ppermute | solution.py:62
  106.0 13.7 %collective-permute-start.23 = (bf16[32,2,16,128]{3,2,1,0:T(8,128)(2,1)S(1)}, bf16[32,2,16,128]{3,2,1,0:T(8,128)(2,1)S(1)}, u32[]{:S(2)}, u32[]{:S(2)}) collective-permute-start(bf16[32,2,16,128]{3,2,1,0:T(8,128)(2,1)S(1)} %collective-permute-done.22.refs_2_), channel_id=1, source_target_pairs={{0,2},{1,3},{2,0},{3,1},{4,6},{5,7},{6,4},{7,5},{8,10},{9,11},{10,... | collective-permute-start | bytes 786440 | tf_op jit(solution)/shard_map/ppermute | solution.py:62
  107.1 12.6 %collective-permute-start.25 = (bf16[32,2,16,128]{3,2,1,0:T(8,128)(2,1)S(1)}, bf16[32,2,16,128]{3,2,1,0:T(8,128)(2,1)S(1)}, u32[]{:S(2)}, u32[]{:S(2)}) collective-permute-start(bf16[32,2,16,128]{3,2,1,0:T(8,128)(2,1)S(1)} %collective-permute-done.18.refs_0_), channel_id=1, source_target_pairs={{0,1},{1,0},{2,3},{3,2},{4,5},{5,4},{6,7},{7,6},{8,9},{9,8},{10,11... | collective-permute-start | bytes 786440 | tf_op jit(solution)/shard_map/ppermute | solution.py:62
  111.6 8.2 %collective-permute-start.32 = (bf16[32,2,16,128]{3,2,1,0:T(8,128)(2,1)S(1)}, bf16[32,2,16,128]{3,2,1,0:T(8,128)(2,1)S(1)}, u32[]{:S(2)}, u32[]{:S(2)}) collective-permute-start(bf16[32,2,16,128]{3,2,1,0:T(8,128)(2,1)S(1)} %collective-permute-done.24.refs_3_), channel_id=1, source_target_pairs={{0,1},{1,0},{2,3},{3,2},{4,5},{5,4},{6,7},{7,6},{8,9},{9,8},{10,11... | collective-permute-start | bytes 786440 | tf_op jit(solution)/shard_map/ppermute | solution.py:62
  143.1 5.2 %collective-permute-start.33 = (bf16[4,32,2,16,128]{4,3,2,1,0:T(8,128)(2,1)S(1)}, bf16[4,32,2,16,128]{4,3,2,1,0:T(8,128)(2,1)S(1)}, u32[]{:S(2)}, u32[]{:S(2)}) collective-permute-start(bf16[4,32,2,16,128]{4,3,2,1,0:T(8,128)(2,1)S(1)} %get-tuple-element.70), channel_id=1, source_target_pairs={{0,1},{1,0},{2,3},{3,2},{4,5},{5,4},{6,7},{7,6},{8,9},{9,8},{10,11... | collective-permute-start | bytes 3145736 | tf_op jit(solution)/shard_map/ppermute | solution.py:62
  145.6 9.2 %collective-permute-start.35 = (bf16[32,2,16,128]{3,2,1,0:T(8,128)(2,1)S(1)}, bf16[32,2,16,128]{3,2,1,0:T(8,128)(2,1)S(1)}, u32[]{:S(2)}, u32[]{:S(2)}) collective-permute-start(bf16[32,2,16,128]{3,2,1,0:T(8,128)(2,1)S(1)} %get-tuple-element.110), channel_id=1, source_target_pairs={{0,2},{1,3},{2,0},{3,1},{4,6},{5,7},{6,4},{7,5},{8,10},{9,11},{10,... | collective-permute-start | bytes 786440 | tf_op jit(solution)/shard_map/ppermute | solution.py:62
  146.8 10.1 %collective-permute-start.40 = (bf16[32,2,16,128]{3,2,1,0:T(8,128)(2,1)S(1)}, bf16[32,2,16,128]{3,2,1,0:T(8,128)(2,1)S(1)}, u32[]{:S(2)}, u32[]{:S(2)}) collective-permute-start(bf16[32,2,16,128]{3,2,1,0:T(8,128)(2,1)S(1)} %get-tuple-element.108), channel_id=1, source_target_pairs={{0,4},{1,5},{2,6},{3,7},{4,8},{5,9},{6,10},{7,11},{8,12},{9,13},{1... | collective-permute-start | bytes 786440 | tf_op jit(solution)/shard_map/ppermute | solution.py:62
  147.4 13.0 %collective-permute-start.38 = (bf16[32,2,16,128]{3,2,1,0:T(8,128)(2,1)S(1)}, bf16[32,2,16,128]{3,2,1,0:T(8,128)(2,1)S(1)}, u32[]{:S(2)}, u32[]{:S(2)}) collective-permute-start(bf16[32,2,16,128]{3,2,1,0:T(8,128)(2,1)S(1)} %get-tuple-element.109), channel_id=1, source_target_pairs={{0,2},{1,3},{2,0},{3,1},{4,6},{5,7},{6,4},{7,5},{8,10},{9,11},{10,... | collective-permute-start | bytes 786440 | tf_op jit(solution)/shard_map/ppermute | solution.py:62
  154.9 9.7 %collective-permute-start.36 = (bf16[32,2,16,128]{3,2,1,0:T(8,128)(2,1)S(1)}, bf16[32,2,16,128]{3,2,1,0:T(8,128)(2,1)S(1)}, u32[]{:S(2)}, u32[]{:S(2)}) collective-permute-start(bf16[32,2,16,128]{3,2,1,0:T(8,128)(2,1)S(1)} %fusion.2), channel_id=1, source_target_pairs={{0,4},{1,5},{2,6},{3,7},{4,8},{5,9},{6,10},{7,11},{8,12},{9,13},{1... | collective-permute-start | bytes 786440 | tf_op jit(solution)/shard_map/ppermute | solution.py:62
  157.0 10.0 %collective-permute-start.41 = (bf16[32,2,16,128]{3,2,1,0:T(8,128)(2,1)S(1)}, bf16[32,2,16,128]{3,2,1,0:T(8,128)(2,1)S(1)}, u32[]{:S(2)}, u32[]{:S(2)}) collective-permute-start(bf16[32,2,16,128]{3,2,1,0:T(8,128)(2,1)S(1)} %fusion), channel_id=1, source_target_pairs={{0,2},{1,3},{2,0},{3,1},{4,6},{5,7},{6,4},{7,5},{8,10},{9,11},{10,... | collective-permute-start | bytes 786440 | tf_op jit(solution)/shard_map/ppermute | solution.py:62
  164.7 11.6 %collective-permute-start.39 = (bf16[32,2,16,128]{3,2,1,0:T(8,128)(2,1)S(1)}, bf16[32,2,16,128]{3,2,1,0:T(8,128)(2,1)S(1)}, u32[]{:S(2)}, u32[]{:S(2)}) collective-permute-start(bf16[32,2,16,128]{3,2,1,0:T(8,128)(2,1)S(1)} %get-tuple-element.111), channel_id=1, source_target_pairs={{0,12},{1,13},{2,14},{3,15},{4,0},{5,1},{6,2},{7,3},{8,4},{9,5},{1... | collective-permute-start | bytes 786440 | tf_op jit(solution)/shard_map/ppermute | solution.py:62
  165.0 11.3 %collective-permute-start.37 = (bf16[32,2,16,128]{3,2,1,0:T(8,128)(2,1)S(1)}, bf16[32,2,16,128]{3,2,1,0:T(8,128)(2,1)S(1)}, u32[]{:S(2)}, u32[]{:S(2)}) collective-permute-start(bf16[32,2,16,128]{3,2,1,0:T(8,128)(2,1)S(1)} %get-tuple-element.112), channel_id=1, source_target_pairs={{0,4},{1,5},{2,6},{3,7},{4,8},{5,9},{6,10},{7,11},{8,12},{9,13},{1... | collective-permute-start | bytes 786440 | tf_op jit(solution)/shard_map/ppermute | solution.py:62
  176.7 7.5 %collective-permute-start.43 = (bf16[16,64,128]{2,1,0:T(8,128)(2,1)S(1)}, bf16[16,64,128]{2,1,0:T(8,128)(2,1)S(1)}, u32[]{:S(2)}, u32[]{:S(2)}) collective-permute-start(bf16[16,64,128]{2,1,0:T(8,128)(2,1)S(1)} %window.5.refs_4_), channel_id=1, source_target_pairs={{0,2},{1,3},{2,0},{3,1},{4,6},{5,7},{6,4},{7,5},{8,10},{9,11},{10,... | collective-permute-start | bytes 786440 | tf_op jit(solution)/shard_map/ppermute | solution.py:62
  178.0 9.9 %collective-permute-start.42 = (bf16[16,64,128]{2,1,0:T(8,128)(2,1)S(1)}, bf16[16,64,128]{2,1,0:T(8,128)(2,1)S(1)}, u32[]{:S(2)}, u32[]{:S(2)}) collective-permute-start(bf16[16,64,128]{2,1,0:T(8,128)(2,1)S(1)} %window.5.refs_4_), channel_id=1, source_target_pairs={{0,4},{1,5},{2,6},{3,7},{4,8},{5,9},{6,10},{7,11},{8,12},{9,13},{1... | collective-permute-start | bytes 786440 | tf_op jit(solution)/shard_map/ppermute | solution.py:62
  178.3 14.5 %collective-permute-start.45 = (bf16[16,64,128]{2,1,0:T(8,128)(2,1)S(1)}, bf16[16,64,128]{2,1,0:T(8,128)(2,1)S(1)}, u32[]{:S(2)}, u32[]{:S(2)}) collective-permute-start(bf16[16,64,128]{2,1,0:T(8,128)(2,1)S(1)} %window.5.refs_4_), channel_id=1, source_target_pairs={{0,12},{1,13},{2,14},{3,15},{4,0},{5,1},{6,2},{7,3},{8,4},{9,5},{1... | collective-permute-start | bytes 786440 | tf_op jit(solution)/shard_map/ppermute | solution.py:62
  187.9 14.1 %collective-permute-start.44 = (bf16[16,64,128]{2,1,0:T(8,128)(2,1)S(1)}, bf16[16,64,128]{2,1,0:T(8,128)(2,1)S(1)}, u32[]{:S(2)}, u32[]{:S(2)}) collective-permute-start(bf16[16,64,128]{2,1,0:T(8,128)(2,1)S(1)} %collective-permute-done.42.refs_4_), channel_id=1, source_target_pairs={{0,4},{1,5},{2,6},{3,7},{4,8},{5,9},{6,10},{7,11},{8,12},{9,13},{1... | collective-permute-start | bytes 786440 | tf_op jit(solution)/shard_map/ppermute | solution.py:62
  192.8 12.9 %collective-permute-start.48 = (bf16[16,64,128]{2,1,0:T(8,128)(2,1)S(1)}, bf16[16,64,128]{2,1,0:T(8,128)(2,1)S(1)}, u32[]{:S(2)}, u32[]{:S(2)}) collective-permute-start(bf16[16,64,128]{2,1,0:T(8,128)(2,1)S(1)} %collective-permute-done.45.refs_4_), channel_id=1, source_target_pairs={{0,2},{1,3},{2,0},{3,1},{4,6},{5,7},{6,4},{7,5},{8,10},{9,11},{10,... | collective-permute-start | bytes 786440 | tf_op jit(solution)/shard_map/ppermute | solution.py:62
  193.6 12.1 %collective-permute-start.47 = (bf16[16,64,128]{2,1,0:T(8,128)(2,1)S(1)}, bf16[16,64,128]{2,1,0:T(8,128)(2,1)S(1)}, u32[]{:S(2)}, u32[]{:S(2)}) collective-permute-start(bf16[16,64,128]{2,1,0:T(8,128)(2,1)S(1)} %collective-permute-done.43.refs_4_), channel_id=1, source_target_pairs={{0,4},{1,5},{2,6},{3,7},{4,8},{5,9},{6,10},{7,11},{8,12},{9,13},{1... | collective-permute-start | bytes 786440 | tf_op jit(solution)/shard_map/ppermute | solution.py:62
  194.2 17.0 %collective-permute-start.50 = (bf16[32,2,16,128]{3,2,1,0:T(8,128)(2,1)S(1)}, bf16[32,2,16,128]{3,2,1,0:T(8,128)(2,1)S(1)}, u32[]{:S(2)}, u32[]{:S(2)}) collective-permute-start(bf16[32,2,16,128]{3,2,1,0:T(8,128)(2,1)S(1)} %get-tuple-element.74.refs_0_), channel_id=1, source_target_pairs={{0,1},{1,0},{2,3},{3,2},{4,5},{5,4},{6,7},{7,6},{8,9},{9,8},{10,11... | collective-permute-start | bytes 786440 | tf_op jit(solution)/shard_map/ppermute | solution.py:62
  201.5 10.2 %collective-permute-start.53 = (bf16[32,2,16,128]{3,2,1,0:T(8,128)(2,1)S(1)}, bf16[32,2,16,128]{3,2,1,0:T(8,128)(2,1)S(1)}, u32[]{:S(2)}, u32[]{:S(2)}) collective-permute-start(bf16[32,2,16,128]{3,2,1,0:T(8,128)(2,1)S(1)} %get-tuple-element.84.refs_3_), channel_id=1, source_target_pairs={{0,1},{1,0},{2,3},{3,2},{4,5},{5,4},{6,7},{7,6},{8,9},{9,8},{10,11... | collective-permute-start | bytes 786440 | tf_op jit(solution)/shard_map/ppermute | solution.py:62
  202.0 9.0 %collective-permute-start.46 = (bf16[16,64,128]{2,1,0:T(8,128)(2,1)S(1)}, bf16[16,64,128]{2,1,0:T(8,128)(2,1)S(1)}, u32[]{:S(2)}, u32[]{:S(2)}) collective-permute-start(bf16[16,64,128]{2,1,0:T(8,128)(2,1)S(1)} %collective-permute-done.44.refs_4_), channel_id=1, source_target_pairs={{0,2},{1,3},{2,0},{3,1},{4,6},{5,7},{6,4},{7,5},{8,10},{9,11},{10,... | collective-permute-start | bytes 786440 | tf_op jit(solution)/shard_map/ppermute | solution.py:62
  205.6 6.0 %collective-permute-start.51 = (bf16[32,2,16,128]{3,2,1,0:T(8,128)(2,1)S(1)}, bf16[32,2,16,128]{3,2,1,0:T(8,128)(2,1)S(1)}, u32[]{:S(2)}, u32[]{:S(2)}) collective-permute-start(bf16[32,2,16,128]{3,2,1,0:T(8,128)(2,1)S(1)} %get-tuple-element.81.refs_1_), channel_id=1, source_target_pairs={{0,1},{1,0},{2,3},{3,2},{4,5},{5,4},{6,7},{7,6},{8,9},{9,8},{10,11... | collective-permute-start | bytes 786440 | tf_op jit(solution)/shard_map/ppermute | solution.py:62
  205.7 5.9 %collective-permute-start.52 = (bf16[32,2,16,128]{3,2,1,0:T(8,128)(2,1)S(1)}, bf16[32,2,16,128]{3,2,1,0:T(8,128)(2,1)S(1)}, u32[]{:S(2)}, u32[]{:S(2)}) collective-permute-start(bf16[32,2,16,128]{3,2,1,0:T(8,128)(2,1)S(1)} %get-tuple-element.88.refs_2_), channel_id=1, source_target_pairs={{0,1},{1,0},{2,3},{3,2},{4,5},{5,4},{6,7},{7,6},{8,9},{9,8},{10,11... | collective-permute-start | bytes 786440 | tf_op jit(solution)/shard_map/ppermute | solution.py:62
  211.1 11.1 %collective-permute-start.49 = (bf16[32,2,16,128]{3,2,1,0:T(8,128)(2,1)S(1)}, bf16[32,2,16,128]{3,2,1,0:T(8,128)(2,1)S(1)}, u32[]{:S(2)}, u32[]{:S(2)}) collective-permute-start(bf16[32,2,16,128]{3,2,1,0:T(8,128)(2,1)S(1)} %get-tuple-element.78.refs_0_), channel_id=1, source_target_pairs={{0,1},{1,0},{2,3},{3,2},{4,5},{5,4},{6,7},{7,6},{8,9},{9,8},{10,11... | collective-permute-start | bytes 786440 | tf_op jit(solution)/shard_map/ppermute | solution.py:62
  211.2 11.0 %collective-permute-start.56 = (bf16[32,2,16,128]{3,2,1,0:T(8,128)(2,1)S(1)}, bf16[32,2,16,128]{3,2,1,0:T(8,128)(2,1)S(1)}, u32[]{:S(2)}, u32[]{:S(2)}) collective-permute-start(bf16[32,2,16,128]{3,2,1,0:T(8,128)(2,1)S(1)} %get-tuple-element.95.refs_3_), channel_id=1, source_target_pairs={{0,1},{1,0},{2,3},{3,2},{4,5},{5,4},{6,7},{7,6},{8,9},{9,8},{10,11... | collective-permute-start | bytes 786440 | tf_op jit(solution)/shard_map/ppermute | solution.py:62
  231.3 34.7 %collective-permute-start.57 = (bf16[16,32,1024]{2,1,0:T(8,128)(2,1)S(1)}, bf16[16,32,1024]{2,1,0:T(8,128)(2,1)S(1)}, u32[]{:S(2)}, u32[]{:S(2)}) collective-permute-start(bf16[16,32,1024]{2,1,0:T(8,128)(2,1)S(1)} %get-tuple-element.104), channel_id=1, source_target_pairs={{0,1},{1,0},{2,3},{3,2},{4,5},{5,4},{6,7},{7,6},{8,9},{9,8},{10,11... | collective-permute-start | bytes 3145736 | tf_op jit(solution)/shard_map/ppermute | solution.py:62
  231.5 10.0 %collective-permute-start.60 = (bf16[16,64,128]{2,1,0:T(8,128)(2,1)S(1)}, bf16[16,64,128]{2,1,0:T(8,128)(2,1)S(1)}, u32[]{:S(2)}, u32[]{:S(2)}) collective-permute-start(bf16[16,64,128]{2,1,0:T(8,128)(2,1)S(1)} %correlate1.3.refs_0_), channel_id=1, source_target_pairs={{0,12},{1,13},{2,14},{3,15},{4,0},{5,1},{6,2},{7,3},{8,4},{9,5},{1... | collective-permute-start | bytes 786440 | tf_op jit(solution)/shard_map/ppermute | solution.py:62
  234.8 8.3 %collective-permute-start.59 = (bf16[16,64,128]{2,1,0:T(8,128)(2,1)S(1)}, bf16[16,64,128]{2,1,0:T(8,128)(2,1)S(1)}, u32[]{:S(2)}, u32[]{:S(2)}) collective-permute-start(bf16[16,64,128]{2,1,0:T(8,128)(2,1)S(1)} %correlate1.3.refs_0_), channel_id=1, source_target_pairs={{0,2},{1,3},{2,0},{3,1},{4,6},{5,7},{6,4},{7,5},{8,10},{9,11},{10,... | collective-permute-start | bytes 786440 | tf_op jit(solution)/shard_map/ppermute | solution.py:62
  235.6 11.6 %collective-permute-start.58 = (bf16[16,64,128]{2,1,0:T(8,128)(2,1)S(1)}, bf16[16,64,128]{2,1,0:T(8,128)(2,1)S(1)}, u32[]{:S(2)}, u32[]{:S(2)}) collective-permute-start(bf16[16,64,128]{2,1,0:T(8,128)(2,1)S(1)} %correlate1.3.refs_0_), channel_id=1, source_target_pairs={{0,4},{1,5},{2,6},{3,7},{4,8},{5,9},{6,10},{7,11},{8,12},{9,13},{1... | collective-permute-start | bytes 786440 | tf_op jit(solution)/shard_map/ppermute | solution.py:62
  247.2 9.6 %collective-permute-start.61 = (bf16[16,64,128]{2,1,0:T(8,128)(2,1)S(1)}, bf16[16,64,128]{2,1,0:T(8,128)(2,1)S(1)}, u32[]{:S(2)}, u32[]{:S(2)}) collective-permute-start(bf16[16,64,128]{2,1,0:T(8,128)(2,1)S(1)} %collective-permute-done.58.refs_1_), channel_id=1, source_target_pairs={{0,4},{1,5},{2,6},{3,7},{4,8},{5,9},{6,10},{7,11},{8,12},{9,13},{1... | collective-permute-start | bytes 786440 | tf_op jit(solution)/shard_map/ppermute | solution.py:62
  256.8 9.2 %collective-permute-start.63 = (bf16[16,64,128]{2,1,0:T(8,128)(2,1)S(1)}, bf16[16,64,128]{2,1,0:T(8,128)(2,1)S(1)}, u32[]{:S(2)}, u32[]{:S(2)}) collective-permute-start(bf16[16,64,128]{2,1,0:T(8,128)(2,1)S(1)} %collective-permute-done.61.refs_2_), channel_id=1, source_target_pairs={{0,2},{1,3},{2,0},{3,1},{4,6},{5,7},{6,4},{7,5},{8,10},{9,11},{10,... | collective-permute-start | bytes 786440 | tf_op jit(solution)/shard_map/ppermute | solution.py:62
  257.6 9.9 %collective-permute-start.65 = (bf16[16,64,128]{2,1,0:T(8,128)(2,1)S(1)}, bf16[16,64,128]{2,1,0:T(8,128)(2,1)S(1)}, u32[]{:S(2)}, u32[]{:S(2)}) collective-permute-start(bf16[16,64,128]{2,1,0:T(8,128)(2,1)S(1)} %correlate1.3.refs_0_), channel_id=1, source_target_pairs={{0,1},{1,0},{2,3},{3,2},{4,5},{5,4},{6,7},{7,6},{8,9},{9,8},{10,11... | collective-permute-start | bytes 786440 | tf_op jit(solution)/shard_map/ppermute | solution.py:62
  257.6 10.4 %collective-permute-start.68 = (bf16[16,64,128]{2,1,0:T(8,128)(2,1)S(1)}, bf16[16,64,128]{2,1,0:T(8,128)(2,1)S(1)}, u32[]{:S(2)}, u32[]{:S(2)}) collective-permute-start(bf16[16,64,128]{2,1,0:T(8,128)(2,1)S(1)} %collective-permute-done.60.refs_3_), channel_id=1, source_target_pairs={{0,1},{1,0},{2,3},{3,2},{4,5},{5,4},{6,7},{7,6},{8,9},{9,8},{10,11... | collective-permute-start | bytes 786440 | tf_op jit(solution)/shard_map/ppermute | solution.py:62
  258.2 11.1 %collective-permute-start.64 = (bf16[16,64,128]{2,1,0:T(8,128)(2,1)S(1)}, bf16[16,64,128]{2,1,0:T(8,128)(2,1)S(1)}, u32[]{:S(2)}, u32[]{:S(2)}) collective-permute-start(bf16[16,64,128]{2,1,0:T(8,128)(2,1)S(1)} %collective-permute-done.60.refs_3_), channel_id=1, source_target_pairs={{0,2},{1,3},{2,0},{3,1},{4,6},{5,7},{6,4},{7,5},{8,10},{9,11},{10,... | collective-permute-start | bytes 786440 | tf_op jit(solution)/shard_map/ppermute | solution.py:62
  266.0 8.2 %collective-permute-start.62 = (bf16[16,64,128]{2,1,0:T(8,128)(2,1)S(1)}, bf16[16,64,128]{2,1,0:T(8,128)(2,1)S(1)}, u32[]{:S(2)}, u32[]{:S(2)}) collective-permute-start(bf16[16,64,128]{2,1,0:T(8,128)(2,1)S(1)} %collective-permute-done.59.refs_4_), channel_id=1, source_target_pairs={{0,4},{1,5},{2,6},{3,7},{4,8},{5,9},{6,10},{7,11},{8,12},{9,13},{1... | collective-permute-start | bytes 786440 | tf_op jit(solution)/shard_map/ppermute | solution.py:62
  266.0 8.2 %collective-permute-start.69 = (bf16[16,64,128]{2,1,0:T(8,128)(2,1)S(1)}, bf16[16,64,128]{2,1,0:T(8,128)(2,1)S(1)}, u32[]{:S(2)}, u32[]{:S(2)}) collective-permute-start(bf16[16,64,128]{2,1,0:T(8,128)(2,1)S(1)} %collective-permute-done.59.refs_4_), channel_id=1, source_target_pairs={{0,1},{1,0},{2,3},{3,2},{4,5},{5,4},{6,7},{7,6},{8,9},{9,8},{10,11... | collective-permute-start | bytes 786440 | tf_op jit(solution)/shard_map/ppermute | solution.py:62
  267.5 7.2 %collective-permute-start.66 = (bf16[16,64,128]{2,1,0:T(8,128)(2,1)S(1)}, bf16[16,64,128]{2,1,0:T(8,128)(2,1)S(1)}, u32[]{:S(2)}, u32[]{:S(2)}) collective-permute-start(bf16[16,64,128]{2,1,0:T(8,128)(2,1)S(1)} %collective-permute-done.58.refs_1_), channel_id=1, source_target_pairs={{0,1},{1,0},{2,3},{3,2},{4,5},{5,4},{6,7},{7,6},{8,9},{9,8},{10,11... | collective-permute-start | bytes 786440 | tf_op jit(solution)/shard_map/ppermute | solution.py:62
  268.1 7.7 %collective-permute-start.67 = (bf16[16,64,128]{2,1,0:T(8,128)(2,1)S(1)}, bf16[16,64,128]{2,1,0:T(8,128)(2,1)S(1)}, u32[]{:S(2)}, u32[]{:S(2)}) collective-permute-start(bf16[16,64,128]{2,1,0:T(8,128)(2,1)S(1)} %collective-permute-done.61.refs_2_), channel_id=1, source_target_pairs={{0,1},{1,0},{2,3},{3,2},{4,5},{5,4},{6,7},{7,6},{8,9},{9,8},{10,11... | collective-permute-start | bytes 786440 | tf_op jit(solution)/shard_map/ppermute | solution.py:62
  269.3 5.4 %collective-permute-start.72 = (bf16[16,64,128]{2,1,0:T(8,128)(2,1)S(1)}, bf16[16,64,128]{2,1,0:T(8,128)(2,1)S(1)}, u32[]{:S(2)}, u32[]{:S(2)}) collective-permute-start(bf16[16,64,128]{2,1,0:T(8,128)(2,1)S(1)} %collective-permute-done.64.refs_7_), channel_id=1, source_target_pairs={{0,1},{1,0},{2,3},{3,2},{4,5},{5,4},{6,7},{7,6},{8,9},{9,8},{10,11... | collective-permute-start | bytes 786440 | tf_op jit(solution)/shard_map/ppermute | solution.py:62
  (17 other events, 126.9 us)

commit v11 on v10

--- a/solution.py
+++ b/solution.py
@@ -609,7 +609,7 @@
             across[step] = places.send(after(across[0], line[size - 1]), places.shift(1))
         else:
             across[step] = places.send(line[step], places.pair())
-    middle = run(1, [0], across) + run(0, near, line)
+    middle = [across[step] for step in near] if together else run(1, [0], across) + run(0, near, line)
     for step in far:
         across[step] = places.send(after(line[step], *middle), places.pair())
     late = run(0, far, line) + run(1, near, across)
@@ -658,7 +658,7 @@
         else:
             own, _ = gather_chips(places, windowed)
         half = correlate(own[0], swap_cores(places, own[0]), reflection, line, 0)
-        across = [own[1][step] if step in (0, line - 1) else after(own[1][step], half) for step in range(line)]
+        across = [own[1][step] if step == 0 else after(own[1][step], half) for step in range(line)]
         downgoing_spec = correlate(own[1], swap_cores(places, across), reflection, line, 1, half, last)
         if not last:
             spectrum_plus = window([downgoing_spec], forward, inverse, onset_times, base=start)

time: 279 us -> 270 us (0.968)
  waiting for transfers between devices: 132 us -> 125 us
    ppermute x73, waiting for transfers between devices: 132 us -> 125 us  [send(): return lax.ppermute(array, self.axis, pairs)]
  transfers between devices with their start and end apart: 73 -> 73, of which waited for: 39 -> 41; matrix products, arithmetic and copies ran while one was open for 1% -> 1% of each run, Pallas kernels for 13% -> 13%
where the time goes in v11:
time: 270 us
  waiting for transfers between devices  125 us (46%)
  Pallas kernels  83.3 us (31%)
  starting transfers between devices  54.8 us (20%)
  local copies, waits for them, and re-layouts  2.82 us (1%)
    ppermute x73, waiting for transfers between devices, send(): return lax.ppermute(array, self.axis, pairs)  125 us
    ppermute x73, starting transfers between devices, send(): return lax.ppermute(array, self.axis, pairs)  54.8 us
    pallas_call x4, Pallas kernels, correlate(): pl.pallas_call(functools.partial(correlate_kernel, line, flip, bool(more)...  30.3 us
    pallas_call x2, Pallas kernels, convolve(): pl.pallas_call(functools.partial(convolve_kernel, line), in_specs=[VMEM,...  23.4 us
    pallas_call x8, Pallas kernels, window_at(): pl.pallas_call(functools.partial(window_at_kernel, line, flip, step, begu...  19.3 us
  transfers between devices with their start and end apart: 73, of which 41 were waited for; matrix products, arithmetic and copies ran while one was open for 1% of the time, Pallas kernels for 13%

profile of v11, /device:TPU:0, one launch (start us, length us, event | category | flops | bytes accessed | tf_op | source)
XLA Modules:
  0.0 269.9 jit_solution(943016944262494495)
XLA Ops:
  0.6 1.6 copy-done.2
  3.2 1.9 first_analysis.1
  5.7 2.2 collective-permute-done.1
  8.2 3.0 %collective-permute-start.2 = (bf16[16,64,128]{2,1,0:T(8,128)(2,1)S(1)}, bf16[16,64,128]{2,1,0:T(8,128)(2,1)S(1)}, u32[]{:S(2)}, u32[]{:S(2)}) collective-permute-start(bf16[16,64,128]{2,1,0:T(8,128)(2,1)S(1)} %get-tuple-element.126), channel_id=1, source_target_pairs={{0,2},{1,3},{2,0},{3,1},{4,6},{5,7},{6,4},{7,5},{8,10},{9,11},{10,... | collective-permute-start | bytes 786440 | tf_op jit(solution)/shard_map/ppermute | solution.py:62
  11.2 1.6 collective-permute-start.7
  13.3 5.0 %collective-permute-done.2 = bf16[16,64,128]{2,1,0:T(8,128)(2,1)S(1)} collective-permute-done((bf16[16,64,128]{2,1,0:T(8,128)(2,1)S(1)}, bf16[16,64,128]{2,1,0:T(8,128)(2,1)S(1)}, u32[]{:S(2)}, u32[]{:S(2)}) %collective-permute-start.2) | collective-permute-done | bytes 262176 | tf_op jit(solution)/shard_map/ppermute | solution.py:62
  18.4 2.2 collective-permute-start.3
  22.3 1.5 collective-permute-done.5
  23.8 3.8 %collective-permute-done.3 = bf16[16,64,128]{2,1,0:T(8,128)(2,1)S(1)} collective-permute-done((bf16[16,64,128]{2,1,0:T(8,128)(2,1)S(1)}, bf16[16,64,128]{2,1,0:T(8,128)(2,1)S(1)}, u32[]{:S(2)}, u32[]{:S(2)}) %collective-permute-start.3) | collective-permute-done | bytes 262176 | tf_op jit(solution)/shard_map/ppermute | solution.py:62
  27.9 3.8 %collective-permute-start.6 = (bf16[16,64,128]{2,1,0:T(8,128)(2,1)S(1)}, bf16[16,64,128]{2,1,0:T(8,128)(2,1)S(1)}, u32[]{:S(2)}, u32[]{:S(2)}) collective-permute-start(bf16[16,64,128]{2,1,0:T(8,128)(2,1)S(1)} %get-tuple-element.125), channel_id=1, source_target_pairs={{0,12},{1,13},{2,14},{3,15},{4,0},{5,1},{6,2},{7,3},{8,4},{9,5},{1... | collective-permute-start | bytes 786440 | tf_op jit(solution)/shard_map/ppermute | solution.py:62
  31.7 7.0 %collective-permute-done.4 = bf16[16,64,128]{2,1,0:T(8,128)(2,1)S(1)} collective-permute-done((bf16[16,64,128]{2,1,0:T(8,128)(2,1)S(1)}, bf16[16,64,128]{2,1,0:T(8,128)(2,1)S(1)}, u32[]{:S(2)}, u32[]{:S(2)}) %collective-permute-start.4) | collective-permute-done | bytes 262176 | tf_op jit(solution)/shard_map/ppermute | solution.py:62
  40.1 11.7 %convolve.2 = (bf16[4,32,2,16,128]{4,3,2,1,0:T(8,128)(2,1)S(1)}, bf16[4,32,2,16,128]{4,3,2,1,0:T(8,128)(2,1)S(1)}, bf16[4,32,2,16,128]{4,3,2,1,0:T(8,128)(2,1)S(1)}, bf16[4,32,2,16,128]{4,3,2,1,0:T(8,128)(2,1)S(1)}) custom-call(bf16[32,2,16,128]{3,2,1,0:T(8,128)(2,1)S(1)} %bitcast.87, bf16[2,32,128,2048]{3,2,1,0:T(8,128)(2,1)} %refs_8_.7), custom_call_target="tpu_custom_call" | custom-call | flops 1073741824 | bytes 37748736 | tf_op jit(solution)/shard_map/convolve/pallas_call | solution.py:238
  52.4 2.1 collective-permute-done.10
  57.4 6.5 %collective-permute-done.11 = bf16[32,2,16,128]{3,2,1,0:T(8,128)(2,1)S(1)} collective-permute-done((bf16[32,2,16,128]{3,2,1,0:T(8,128)(2,1)S(1)}, bf16[32,2,16,128]{3,2,1,0:T(8,128)(2,1)S(1)}, u32[]{:S(2)}, u32[]{:S(2)}) %collective-permute-start.11) | collective-permute-done | bytes 262176 | tf_op jit(solution)/shard_map/ppermute | solution.py:62
  66.9 2.7 collective-permute-done.14
  69.6 3.2 %collective-permute-done.12 = bf16[32,2,16,128]{3,2,1,0:T(8,128)(2,1)S(1)} collective-permute-done((bf16[32,2,16,128]{3,2,1,0:T(8,128)(2,1)S(1)}, bf16[32,2,16,128]{3,2,1,0:T(8,128)(2,1)S(1)}, u32[]{:S(2)}, u32[]{:S(2)}) %collective-permute-start.12) | collective-permute-done | bytes 262176 | tf_op jit(solution)/shard_map/ppermute | solution.py:62
  73.2 1.8 collective-permute-start.13
  75.1 6.5 %collective-permute-done.15.refs_6_ = bf16[32,2,16,128]{3,2,1,0:T(8,128)(2,1)S(1)} collective-permute-done((bf16[32,2,16,128]{3,2,1,0:T(8,128)(2,1)S(1)}, bf16[32,2,16,128]{3,2,1,0:T(8,128)(2,1)S(1)}, u32[]{:S(2)}, u32[]{:S(2)}) %collective-permute-start.15) | collective-permute-done | bytes 262176 | tf_op jit(solution)/shard_map/ppermute | solution.py:62
  81.6 2.8 %collective-permute-done.13.refs_5_ = bf16[32,2,16,128]{3,2,1,0:T(8,128)(2,1)S(1)} collective-permute-done((bf16[32,2,16,128]{3,2,1,0:T(8,128)(2,1)S(1)}, bf16[32,2,16,128]{3,2,1,0:T(8,128)(2,1)S(1)}, u32[]{:S(2)}, u32[]{:S(2)}) %collective-permute-start.13) | collective-permute-done | bytes 262176 | tf_op jit(solution)/shard_map/ppermute | solution.py:62
  84.5 2.2 window.3.refs_0_
  87.0 1.4 collective-permute-start.18
  88.4 3.4 %collective-permute-start.19 = (bf16[32,2,16,128]{3,2,1,0:T(8,128)(2,1)S(1)}, bf16[32,2,16,128]{3,2,1,0:T(8,128)(2,1)S(1)}, u32[]{:S(2)}, u32[]{:S(2)}) collective-permute-start(bf16[32,2,16,128]{3,2,1,0:T(8,128)(2,1)S(1)} %window.3.refs_0_), channel_id=1, source_target_pairs={{0,12},{1,13},{2,14},{3,15},{4,0},{5,1},{6,2},{7,3},{8,4},{9,5},{1... | collective-permute-start | bytes 786440 | tf_op jit(solution)/shard_map/ppermute | solution.py:62
  91.8 6.1 %collective-permute-done.21.refs_1_ = bf16[32,2,16,128]{3,2,1,0:T(8,128)(2,1)S(1)} collective-permute-done((bf16[32,2,16,128]{3,2,1,0:T(8,128)(2,1)S(1)}, bf16[32,2,16,128]{3,2,1,0:T(8,128)(2,1)S(1)}, u32[]{:S(2)}, u32[]{:S(2)}) %collective-permute-start.21) | collective-permute-done | bytes 262176 | tf_op jit(solution)/shard_map/ppermute | solution.py:62
  99.3 3.2 %collective-permute-done.19.refs_3_ = bf16[32,2,16,128]{3,2,1,0:T(8,128)(2,1)S(1)} collective-permute-done((bf16[32,2,16,128]{3,2,1,0:T(8,128)(2,1)S(1)}, bf16[32,2,16,128]{3,2,1,0:T(8,128)(2,1)S(1)}, u32[]{:S(2)}, u32[]{:S(2)}) %collective-permute-start.19) | collective-permute-done | bytes 262176 | tf_op jit(solution)/shard_map/ppermute | solution.py:62
  102.5 3.5 %collective-permute-done.22.refs_2_ = bf16[32,2,16,128]{3,2,1,0:T(8,128)(2,1)S(1)} collective-permute-done((bf16[32,2,16,128]{3,2,1,0:T(8,128)(2,1)S(1)}, bf16[32,2,16,128]{3,2,1,0:T(8,128)(2,1)S(1)}, u32[]{:S(2)}, u32[]{:S(2)}) %collective-permute-start.22) | collective-permute-done | bytes 262176 | tf_op jit(solution)/shard_map/ppermute | solution.py:62
  108.1 7.5 %correlate0.2.refs_9_ = f32[32,2,16,128]{3,2,1,0:T(8,128)S(1)} custom-call(bf16[32,2,16,128]{3,2,1,0:T(8,128)(2,1)S(1)} %window.3.refs_0_, bf16[32,2,16,128]{3,2,1,0:T(8,128)(2,1)S(1)} %collective-permute-done.21.refs_1_, bf16[32,2,16,128]{3,2,1,0:T(8,128)(2,1)S(1)} %collective-permute-done.22.refs_2_, ...), custom_call_target="tpu_custom_call" | custom-call | flops 536870912 | bytes 18874368 | tf_op jit(solution)/shard_map/correlate0/pallas_call | solution.py:312
  115.7 1.6 collective-permute-done.20.refs_1_
  117.8 2.6 collective-permute-done.23.refs_2_
  120.4 1.5 collective-permute-done.31.refs_6_
  121.9 7.5 %correlate1.2.refs_3_ = f32[32,2,16,128]{3,2,1,0:T(8,128)S(1)} custom-call(bf16[32,2,16,128]{3,2,1,0:T(8,128)(2,1)S(1)} %collective-permute-done.18.refs_0_, bf16[32,2,16,128]{3,2,1,0:T(8,128)(2,1)S(1)} %collective-permute-done.20.refs_1_, bf16[32,2,16,128]{3,2,1,0:T(8,128)(2,1)S(1)} %collective-permute-done.23.refs_2_, ...), custom_call_target="tpu_custom_call" | custom-call | flops 536870912 | bytes 18874368 | tf_op jit(solution)/shard_map/correlate1/pallas_call | solution.py:312
  129.4 2.1 window.4.spec_ref
  131.6 11.7 %convolve.3 = (bf16[4,32,2,16,128]{4,3,2,1,0:T(8,128)(2,1)S(1)}, bf16[4,32,2,16,128]{4,3,2,1,0:T(8,128)(2,1)S(1)}, bf16[4,32,2,16,128]{4,3,2,1,0:T(8,128)(2,1)S(1)}, bf16[4,32,2,16,128]{4,3,2,1,0:T(8,128)(2,1)S(1)}) custom-call(bf16[32,2,16,128]{3,2,1,0:T(8,128)(2,1)S(1)} %window.4.spec_ref, bf16[2,32,128,2048]{3,2,1,0:T(8,128)(2,1)} %refs_8_.7), custom_call_target="tpu_custom_call" | custom-call | flops 1073741824 | bytes 37748736 | tf_op jit(solution)/shard_map/convolve/pallas_call | solution.py:238
  143.8 2.1 collective-permute-done.34
  148.3 7.1 %collective-permute-done.35 = bf16[32,2,16,128]{3,2,1,0:T(8,128)(2,1)S(1)} collective-permute-done((bf16[32,2,16,128]{3,2,1,0:T(8,128)(2,1)S(1)}, bf16[32,2,16,128]{3,2,1,0:T(8,128)(2,1)S(1)}, u32[]{:S(2)}, u32[]{:S(2)}) %collective-permute-start.35) | collective-permute-done | bytes 262176 | tf_op jit(solution)/shard_map/ppermute | solution.py:62
  155.6 1.6 collective-permute-done.40
  158.4 2.7 collective-permute-done.38
  161.0 3.2 %collective-permute-done.36 = bf16[32,2,16,128]{3,2,1,0:T(8,128)(2,1)S(1)} collective-permute-done((bf16[32,2,16,128]{3,2,1,0:T(8,128)(2,1)S(1)}, bf16[32,2,16,128]{3,2,1,0:T(8,128)(2,1)S(1)}, u32[]{:S(2)}, u32[]{:S(2)}) %collective-permute-start.36) | collective-permute-done | bytes 262176 | tf_op jit(solution)/shard_map/ppermute | solution.py:62
  164.7 2.0 collective-permute-start.37
  166.7 9.2 %collective-permute-done.39.refs_6_ = bf16[32,2,16,128]{3,2,1,0:T(8,128)(2,1)S(1)} collective-permute-done((bf16[32,2,16,128]{3,2,1,0:T(8,128)(2,1)S(1)}, bf16[32,2,16,128]{3,2,1,0:T(8,128)(2,1)S(1)}, u32[]{:S(2)}, u32[]{:S(2)}) %collective-permute-start.39) | collective-permute-done | bytes 262176 | tf_op jit(solution)/shard_map/ppermute | solution.py:62
  176.4 1.5 collective-permute-start.43
  177.9 3.8 %collective-permute-start.45 = (bf16[16,64,128]{2,1,0:T(8,128)(2,1)S(1)}, bf16[16,64,128]{2,1,0:T(8,128)(2,1)S(1)}, u32[]{:S(2)}, u32[]{:S(2)}) collective-permute-start(bf16[16,64,128]{2,1,0:T(8,128)(2,1)S(1)} %window.5.refs_4_), channel_id=1, source_target_pairs={{0,12},{1,13},{2,14},{3,15},{4,0},{5,1},{6,2},{7,3},{8,4},{9,5},{1... | collective-permute-start | bytes 786440 | tf_op jit(solution)/shard_map/ppermute | solution.py:62
  181.7 2.4 window_at.8
  184.1 4.1 %collective-permute-done.42.refs_4_ = bf16[16,64,128]{2,1,0:T(8,128)(2,1)S(1)} collective-permute-done((bf16[16,64,128]{2,1,0:T(8,128)(2,1)S(1)}, bf16[16,64,128]{2,1,0:T(8,128)(2,1)S(1)}, u32[]{:S(2)}, u32[]{:S(2)}) %collective-permute-start.42) | collective-permute-done | bytes 262176 | tf_op jit(solution)/shard_map/ppermute | solution.py:62
  188.2 4.1 %collective-permute-done.45.refs_4_ = bf16[16,64,128]{2,1,0:T(8,128)(2,1)S(1)} collective-permute-done((bf16[16,64,128]{2,1,0:T(8,128)(2,1)S(1)}, bf16[16,64,128]{2,1,0:T(8,128)(2,1)S(1)}, u32[]{:S(2)}, u32[]{:S(2)}) %collective-permute-start.45) | collective-permute-done | bytes 262176 | tf_op jit(solution)/shard_map/ppermute | solution.py:62
  193.4 2.4 window_at.9
  195.8 2.4 window_at.10
  198.2 2.4 window_at.11
  201.3 2.4 window_at.12
  204.2 1.7 collective-permute-start.46
  205.9 2.4 window_at.13
  208.3 2.4 window_at.14
  210.9 7.5 %correlate0.3.refs_9_ = f32[32,2,16,128]{3,2,1,0:T(8,128)S(1)} custom-call(bf16[32,2,16,128]{3,2,1,0:T(8,128)(2,1)S(1)} %get-tuple-element.78.refs_0_, bf16[32,2,16,128]{3,2,1,0:T(8,128)(2,1)S(1)} %get-tuple-element.85.refs_1_, bf16[32,2,16,128]{3,2,1,0:T(8,128)(2,1)S(1)} %get-tuple-element.92.refs_2_, ...), custom_call_target="tpu_custom_call" | custom-call | flops 536870912 | bytes 18874368 | tf_op jit(solution)/shard_map/correlate0/pallas_call | solution.py:312
  218.4 2.4 window_at.15
  223.3 7.7 %correlate1.3.refs_0_ = bf16[16,64,128]{2,1,0:T(8,128)(2,1)S(1)} custom-call(bf16[32,2,16,128]{3,2,1,0:T(8,128)(2,1)S(1)} %get-tuple-element.82.refs_0_, bf16[32,2,16,128]{3,2,1,0:T(8,128)(2,1)S(1)} %get-tuple-element.106.refs_1_, bf16[32,2,16,128]{3,2,1,0:T(8,128)(2,1)S(1)} %get-tuple-element.107.refs_2_, ...), custom_call_target="tpu_custom_call" | custom-call | flops 536870912 | bytes 18874368 | tf_op jit(solution)/shard_map/correlate1/pallas_call | solution.py:312
  231.4 3.1 %collective-permute-start.60 = (bf16[16,64,128]{2,1,0:T(8,128)(2,1)S(1)}, bf16[16,64,128]{2,1,0:T(8,128)(2,1)S(1)}, u32[]{:S(2)}, u32[]{:S(2)}) collective-permute-start(bf16[16,64,128]{2,1,0:T(8,128)(2,1)S(1)} %correlate1.3.refs_0_), channel_id=1, source_target_pairs={{0,12},{1,13},{2,14},{3,15},{4,0},{5,1},{6,2},{7,3},{8,4},{9,5},{1... | collective-permute-start | bytes 786440 | tf_op jit(solution)/shard_map/ppermute | solution.py:62
  235.0 6.2 %collective-permute-done.60.refs_3_ = bf16[16,64,128]{2,1,0:T(8,128)(2,1)S(1)} collective-permute-done((bf16[16,64,128]{2,1,0:T(8,128)(2,1)S(1)}, bf16[16,64,128]{2,1,0:T(8,128)(2,1)S(1)}, u32[]{:S(2)}, u32[]{:S(2)}) %collective-permute-start.60) | collective-permute-done | bytes 262176 | tf_op jit(solution)/shard_map/ppermute | solution.py:62
  241.2 1.4 collective-permute-done.59.refs_4_
  242.6 4.6 %collective-permute-done.58.refs_1_ = bf16[16,64,128]{2,1,0:T(8,128)(2,1)S(1)} collective-permute-done((bf16[16,64,128]{2,1,0:T(8,128)(2,1)S(1)}, bf16[16,64,128]{2,1,0:T(8,128)(2,1)S(1)}, u32[]{:S(2)}, u32[]{:S(2)}) %collective-permute-start.58) | collective-permute-done | bytes 262176 | tf_op jit(solution)/shard_map/ppermute | solution.py:62
  248.5 1.3 collective-permute-start.61
  249.8 4.7 %collective-permute-done.63.refs_7_ = bf16[16,64,128]{2,1,0:T(8,128)(2,1)S(1)} collective-permute-done((bf16[16,64,128]{2,1,0:T(8,128)(2,1)S(1)}, bf16[16,64,128]{2,1,0:T(8,128)(2,1)S(1)}, u32[]{:S(2)}, u32[]{:S(2)}) %collective-permute-start.63) | collective-permute-done | bytes 262176 | tf_op jit(solution)/shard_map/ppermute | solution.py:62
  254.6 3.4 %collective-permute-done.61.refs_2_ = bf16[16,64,128]{2,1,0:T(8,128)(2,1)S(1)} collective-permute-done((bf16[16,64,128]{2,1,0:T(8,128)(2,1)S(1)}, bf16[16,64,128]{2,1,0:T(8,128)(2,1)S(1)}, u32[]{:S(2)}, u32[]{:S(2)}) %collective-permute-start.61) | collective-permute-done | bytes 262176 | tf_op jit(solution)/shard_map/ppermute | solution.py:62
  260.0 1.4 merge.1
  261.4 3.4 %collective-permute-done.64.refs_6_ = bf16[16,64,128]{2,1,0:T(8,128)(2,1)S(1)} collective-permute-done((bf16[16,64,128]{2,1,0:T(8,128)(2,1)S(1)}, bf16[16,64,128]{2,1,0:T(8,128)(2,1)S(1)}, u32[]{:S(2)}, u32[]{:S(2)}) %collective-permute-start.64) | collective-permute-done | bytes 262176 | tf_op jit(solution)/shard_map/ppermute | solution.py:62
  267.5 2.3 field.1
  (136 shorter events, 33.9 us)
Async XLA Ops:
  5.1 2.8 %collective-permute-start.1 = (bf16[4,16,64,128]{3,2,1,0:T(8,128)(2,1)S(1)}, bf16[4,16,64,128]{3,2,1,0:T(8,128)(2,1)S(1)}, u32[]{:S(2)}, u32[]{:S(2)}) collective-permute-start(bf16[4,16,64,128]{3,2,1,0:T(8,128)(2,1)S(1)} %get-tuple-element.61), channel_id=1, source_target_pairs={{0,1},{1,0},{2,3},{3,2},{4,5},{5,4},{6,7},{7,6},{8,9},{9,8},{10,11... | collective-permute-start | bytes 3145736 | tf_op jit(solution)/shard_map/ppermute | solution.py:62
  5.6 7.7 %collective-permute-start = (bf16[4,16,64,128]{3,2,1,0:T(8,128)(2,1)S(1)}, bf16[4,16,64,128]{3,2,1,0:T(8,128)(2,1)S(1)}, u32[]{:S(2)}, u32[]{:S(2)}) collective-permute-start(bf16[4,16,64,128]{3,2,1,0:T(8,128)(2,1)S(1)} %get-tuple-element.59), channel_id=1, source_target_pairs={{0,1},{1,0},{2,3},{3,2},{4,5},{5,4},{6,7},{7,6},{8,9},{9,8},{10,11... | collective-permute-start | bytes 3145736 | tf_op jit(solution)/shard_map/ppermute | solution.py:62
  8.2 10.0 %collective-permute-start.2 = (bf16[16,64,128]{2,1,0:T(8,128)(2,1)S(1)}, bf16[16,64,128]{2,1,0:T(8,128)(2,1)S(1)}, u32[]{:S(2)}, u32[]{:S(2)}) collective-permute-start(bf16[16,64,128]{2,1,0:T(8,128)(2,1)S(1)} %get-tuple-element.126), channel_id=1, source_target_pairs={{0,2},{1,3},{2,0},{3,1},{4,6},{5,7},{6,4},{7,5},{8,10},{9,11},{10,... | collective-permute-start | bytes 786440 | tf_op jit(solution)/shard_map/ppermute | solution.py:62
  11.2 9.9 %collective-permute-start.7 = (bf16[16,64,128]{2,1,0:T(8,128)(2,1)S(1)}, bf16[16,64,128]{2,1,0:T(8,128)(2,1)S(1)}, u32[]{:S(2)}, u32[]{:S(2)}) collective-permute-start(bf16[16,64,128]{2,1,0:T(8,128)(2,1)S(1)} %get-tuple-element.127), channel_id=1, source_target_pairs={{0,4},{1,5},{2,6},{3,7},{4,8},{5,9},{6,10},{7,11},{8,12},{9,13},{1... | collective-permute-start | bytes 786440 | tf_op jit(solution)/shard_map/ppermute | solution.py:62
  12.7 11.0 %collective-permute-start.5 = (bf16[16,64,128]{2,1,0:T(8,128)(2,1)S(1)}, bf16[16,64,128]{2,1,0:T(8,128)(2,1)S(1)}, u32[]{:S(2)}, u32[]{:S(2)}) collective-permute-start(bf16[16,64,128]{2,1,0:T(8,128)(2,1)S(1)} %get-tuple-element.128), channel_id=1, source_target_pairs={{0,2},{1,3},{2,0},{3,1},{4,6},{5,7},{6,4},{7,5},{8,10},{9,11},{10,... | collective-permute-start | bytes 786440 | tf_op jit(solution)/shard_map/ppermute | solution.py:62
  18.4 9.2 %collective-permute-start.3 = (bf16[16,64,128]{2,1,0:T(8,128)(2,1)S(1)}, bf16[16,64,128]{2,1,0:T(8,128)(2,1)S(1)}, u32[]{:S(2)}, u32[]{:S(2)}) collective-permute-start(bf16[16,64,128]{2,1,0:T(8,128)(2,1)S(1)} %fusion.10), channel_id=1, source_target_pairs={{0,4},{1,5},{2,6},{3,7},{4,8},{5,9},{6,10},{7,11},{8,12},{9,13},{1... | collective-permute-start | bytes 786440 | tf_op jit(solution)/shard_map/ppermute | solution.py:62
  21.2 10.5 %collective-permute-start.8 = (bf16[16,64,128]{2,1,0:T(8,128)(2,1)S(1)}, bf16[16,64,128]{2,1,0:T(8,128)(2,1)S(1)}, u32[]{:S(2)}, u32[]{:S(2)}) collective-permute-start(bf16[16,64,128]{2,1,0:T(8,128)(2,1)S(1)} %fusion.8), channel_id=1, source_target_pairs={{0,2},{1,3},{2,0},{3,1},{4,6},{5,7},{6,4},{7,5},{8,10},{9,11},{10,... | collective-permute-start | bytes 786440 | tf_op jit(solution)/shard_map/ppermute | solution.py:62
  27.9 10.8 %collective-permute-start.4 = (bf16[16,64,128]{2,1,0:T(8,128)(2,1)S(1)}, bf16[16,64,128]{2,1,0:T(8,128)(2,1)S(1)}, u32[]{:S(2)}, u32[]{:S(2)}) collective-permute-start(bf16[16,64,128]{2,1,0:T(8,128)(2,1)S(1)} %get-tuple-element.124), channel_id=1, source_target_pairs={{0,4},{1,5},{2,6},{3,7},{4,8},{5,9},{6,10},{7,11},{8,12},{9,13},{1... | collective-permute-start | bytes 786440 | tf_op jit(solution)/shard_map/ppermute | solution.py:62
  27.9 11.8 %collective-permute-start.6 = (bf16[16,64,128]{2,1,0:T(8,128)(2,1)S(1)}, bf16[16,64,128]{2,1,0:T(8,128)(2,1)S(1)}, u32[]{:S(2)}, u32[]{:S(2)}) collective-permute-start(bf16[16,64,128]{2,1,0:T(8,128)(2,1)S(1)} %get-tuple-element.125), channel_id=1, source_target_pairs={{0,12},{1,13},{2,14},{3,15},{4,0},{5,1},{6,2},{7,3},{8,4},{9,5},{1... | collective-permute-start | bytes 786440 | tf_op jit(solution)/shard_map/ppermute | solution.py:62
  51.8 2.7 %collective-permute-start.10 = (bf16[4,32,2,16,128]{4,3,2,1,0:T(8,128)(2,1)S(1)}, bf16[4,32,2,16,128]{4,3,2,1,0:T(8,128)(2,1)S(1)}, u32[]{:S(2)}, u32[]{:S(2)}) collective-permute-start(bf16[4,32,2,16,128]{4,3,2,1,0:T(8,128)(2,1)S(1)} %get-tuple-element.66), channel_id=1, source_target_pairs={{0,1},{1,0},{2,3},{3,2},{4,5},{5,4},{6,7},{7,6},{8,9},{9,8},{10,11... | collective-permute-start | bytes 3145736 | tf_op jit(solution)/shard_map/ppermute | solution.py:62
  51.9 5.6 %collective-permute-start.9 = (bf16[4,32,2,16,128]{4,3,2,1,0:T(8,128)(2,1)S(1)}, bf16[4,32,2,16,128]{4,3,2,1,0:T(8,128)(2,1)S(1)}, u32[]{:S(2)}, u32[]{:S(2)}) collective-permute-start(bf16[4,32,2,16,128]{4,3,2,1,0:T(8,128)(2,1)S(1)} %get-tuple-element.64), channel_id=1, source_target_pairs={{0,1},{1,0},{2,3},{3,2},{4,5},{5,4},{6,7},{7,6},{8,9},{9,8},{10,11... | collective-permute-start | bytes 3145736 | tf_op jit(solution)/shard_map/ppermute | solution.py:62
  54.7 9.2 %collective-permute-start.11 = (bf16[32,2,16,128]{3,2,1,0:T(8,128)(2,1)S(1)}, bf16[32,2,16,128]{3,2,1,0:T(8,128)(2,1)S(1)}, u32[]{:S(2)}, u32[]{:S(2)}) collective-permute-start(bf16[32,2,16,128]{3,2,1,0:T(8,128)(2,1)S(1)} %get-tuple-element.121), channel_id=1, source_target_pairs={{0,2},{1,3},{2,0},{3,1},{4,6},{5,7},{6,4},{7,5},{8,10},{9,11},{10,... | collective-permute-start | bytes 786440 | tf_op jit(solution)/shard_map/ppermute | solution.py:62
  56.0 9.9 %collective-permute-start.16 = (bf16[32,2,16,128]{3,2,1,0:T(8,128)(2,1)S(1)}, bf16[32,2,16,128]{3,2,1,0:T(8,128)(2,1)S(1)}, u32[]{:S(2)}, u32[]{:S(2)}) collective-permute-start(bf16[32,2,16,128]{3,2,1,0:T(8,128)(2,1)S(1)} %get-tuple-element.119), channel_id=1, source_target_pairs={{0,4},{1,5},{2,6},{3,7},{4,8},{5,9},{6,10},{7,11},{8,12},{9,13},{1... | collective-permute-start | bytes 786440 | tf_op jit(solution)/shard_map/ppermute | solution.py:62
  56.9 12.6 %collective-permute-start.14 = (bf16[32,2,16,128]{3,2,1,0:T(8,128)(2,1)S(1)}, bf16[32,2,16,128]{3,2,1,0:T(8,128)(2,1)S(1)}, u32[]{:S(2)}, u32[]{:S(2)}) collective-permute-start(bf16[32,2,16,128]{3,2,1,0:T(8,128)(2,1)S(1)} %get-tuple-element.120), channel_id=1, source_target_pairs={{0,2},{1,3},{2,0},{3,1},{4,6},{5,7},{6,4},{7,5},{8,10},{9,11},{10,... | collective-permute-start | bytes 786440 | tf_op jit(solution)/shard_map/ppermute | solution.py:62
  64.1 8.7 %collective-permute-start.12 = (bf16[32,2,16,128]{3,2,1,0:T(8,128)(2,1)S(1)}, bf16[32,2,16,128]{3,2,1,0:T(8,128)(2,1)S(1)}, u32[]{:S(2)}, u32[]{:S(2)}) collective-permute-start(bf16[32,2,16,128]{3,2,1,0:T(8,128)(2,1)S(1)} %fusion.6), channel_id=1, source_target_pairs={{0,4},{1,5},{2,6},{3,7},{4,8},{5,9},{6,10},{7,11},{8,12},{9,13},{1... | collective-permute-start | bytes 786440 | tf_op jit(solution)/shard_map/ppermute | solution.py:62
  66.0 9.1 %collective-permute-start.17 = (bf16[32,2,16,128]{3,2,1,0:T(8,128)(2,1)S(1)}, bf16[32,2,16,128]{3,2,1,0:T(8,128)(2,1)S(1)}, u32[]{:S(2)}, u32[]{:S(2)}) collective-permute-start(bf16[32,2,16,128]{3,2,1,0:T(8,128)(2,1)S(1)} %fusion.4), channel_id=1, source_target_pairs={{0,2},{1,3},{2,0},{3,1},{4,6},{5,7},{6,4},{7,5},{8,10},{9,11},{10,... | collective-permute-start | bytes 786440 | tf_op jit(solution)/shard_map/ppermute | solution.py:62
  73.0 8.7 %collective-permute-start.15 = (bf16[32,2,16,128]{3,2,1,0:T(8,128)(2,1)S(1)}, bf16[32,2,16,128]{3,2,1,0:T(8,128)(2,1)S(1)}, u32[]{:S(2)}, u32[]{:S(2)}) collective-permute-start(bf16[32,2,16,128]{3,2,1,0:T(8,128)(2,1)S(1)} %get-tuple-element.122), channel_id=1, source_target_pairs={{0,12},{1,13},{2,14},{3,15},{4,0},{5,1},{6,2},{7,3},{8,4},{9,5},{1... | collective-permute-start | bytes 786440 | tf_op jit(solution)/shard_map/ppermute | solution.py:62
  73.2 11.2 %collective-permute-start.13 = (bf16[32,2,16,128]{3,2,1,0:T(8,128)(2,1)S(1)}, bf16[32,2,16,128]{3,2,1,0:T(8,128)(2,1)S(1)}, u32[]{:S(2)}, u32[]{:S(2)}) collective-permute-start(bf16[32,2,16,128]{3,2,1,0:T(8,128)(2,1)S(1)} %get-tuple-element.123), channel_id=1, source_target_pairs={{0,4},{1,5},{2,6},{3,7},{4,8},{5,9},{6,10},{7,11},{8,12},{9,13},{1... | collective-permute-start | bytes 786440 | tf_op jit(solution)/shard_map/ppermute | solution.py:62
  86.7 11.1 %collective-permute-start.21 = (bf16[32,2,16,128]{3,2,1,0:T(8,128)(2,1)S(1)}, bf16[32,2,16,128]{3,2,1,0:T(8,128)(2,1)S(1)}, u32[]{:S(2)}, u32[]{:S(2)}) collective-permute-start(bf16[32,2,16,128]{3,2,1,0:T(8,128)(2,1)S(1)} %window.3.refs_0_), channel_id=1, source_target_pairs={{0,4},{1,5},{2,6},{3,7},{4,8},{5,9},{6,10},{7,11},{8,12},{9,13},{1... | collective-permute-start | bytes 786440 | tf_op jit(solution)/shard_map/ppermute | solution.py:62
  87.0 10.8 %collective-permute-start.18 = (bf16[32,2,16,128]{3,2,1,0:T(8,128)(2,1)S(1)}, bf16[32,2,16,128]{3,2,1,0:T(8,128)(2,1)S(1)}, u32[]{:S(2)}, u32[]{:S(2)}) collective-permute-start(bf16[32,2,16,128]{3,2,1,0:T(8,128)(2,1)S(1)} %window.3.refs_0_), channel_id=1, source_target_pairs={{0,2},{1,3},{2,0},{3,1},{4,6},{5,7},{6,4},{7,5},{8,10},{9,11},{10,... | collective-permute-start | bytes 786440 | tf_op jit(solution)/shard_map/ppermute | solution.py:62
  88.4 14.1 %collective-permute-start.19 = (bf16[32,2,16,128]{3,2,1,0:T(8,128)(2,1)S(1)}, bf16[32,2,16,128]{3,2,1,0:T(8,128)(2,1)S(1)}, u32[]{:S(2)}, u32[]{:S(2)}) collective-permute-start(bf16[32,2,16,128]{3,2,1,0:T(8,128)(2,1)S(1)} %window.3.refs_0_), channel_id=1, source_target_pairs={{0,12},{1,13},{2,14},{3,15},{4,0},{5,1},{6,2},{7,3},{8,4},{9,5},{1... | collective-permute-start | bytes 786440 | tf_op jit(solution)/shard_map/ppermute | solution.py:62
  97.8 8.2 %collective-permute-start.22 = (bf16[32,2,16,128]{3,2,1,0:T(8,128)(2,1)S(1)}, bf16[32,2,16,128]{3,2,1,0:T(8,128)(2,1)S(1)}, u32[]{:S(2)}, u32[]{:S(2)}) collective-permute-start(bf16[32,2,16,128]{3,2,1,0:T(8,128)(2,1)S(1)} %collective-permute-done.21.refs_1_), channel_id=1, source_target_pairs={{0,4},{1,5},{2,6},{3,7},{4,8},{5,9},{6,10},{7,11},{8,12},{9,13},{1... | collective-permute-start | bytes 786440 | tf_op jit(solution)/shard_map/ppermute | solution.py:62
  98.8 8.3 %collective-permute-start.26 = (bf16[32,2,16,128]{3,2,1,0:T(8,128)(2,1)S(1)}, bf16[32,2,16,128]{3,2,1,0:T(8,128)(2,1)S(1)}, u32[]{:S(2)}, u32[]{:S(2)}) collective-permute-start(bf16[32,2,16,128]{3,2,1,0:T(8,128)(2,1)S(1)} %window.3.refs_0_), channel_id=1, source_target_pairs={{0,1},{1,0},{2,3},{3,2},{4,5},{5,4},{6,7},{7,6},{8,9},{9,8},{10,11... | collective-permute-start | bytes 786440 | tf_op jit(solution)/shard_map/ppermute | solution.py:62
  98.8 8.3 %collective-permute-start.27 = (bf16[32,2,16,128]{3,2,1,0:T(8,128)(2,1)S(1)}, bf16[32,2,16,128]{3,2,1,0:T(8,128)(2,1)S(1)}, u32[]{:S(2)}, u32[]{:S(2)}) collective-permute-start(bf16[32,2,16,128]{3,2,1,0:T(8,128)(2,1)S(1)} %collective-permute-done.21.refs_1_), channel_id=1, source_target_pairs={{0,1},{1,0},{2,3},{3,2},{4,5},{5,4},{6,7},{7,6},{8,9},{9,8},{10,11... | collective-permute-start | bytes 786440 | tf_op jit(solution)/shard_map/ppermute | solution.py:62
  102.5 5.6 %collective-permute-start.29 = (bf16[32,2,16,128]{3,2,1,0:T(8,128)(2,1)S(1)}, bf16[32,2,16,128]{3,2,1,0:T(8,128)(2,1)S(1)}, u32[]{:S(2)}, u32[]{:S(2)}) collective-permute-start(bf16[32,2,16,128]{3,2,1,0:T(8,128)(2,1)S(1)} %collective-permute-done.19.refs_3_), channel_id=1, source_target_pairs={{0,1},{1,0},{2,3},{3,2},{4,5},{5,4},{6,7},{7,6},{8,9},{9,8},{10,11... | collective-permute-start | bytes 786440 | tf_op jit(solution)/shard_map/ppermute | solution.py:62
  106.0 9.7 %collective-permute-start.24 = (bf16[32,2,16,128]{3,2,1,0:T(8,128)(2,1)S(1)}, bf16[32,2,16,128]{3,2,1,0:T(8,128)(2,1)S(1)}, u32[]{:S(2)}, u32[]{:S(2)}) collective-permute-start(bf16[32,2,16,128]{3,2,1,0:T(8,128)(2,1)S(1)} %collective-permute-done.19.refs_3_), channel_id=1, source_target_pairs={{0,2},{1,3},{2,0},{3,1},{4,6},{5,7},{6,4},{7,5},{8,10},{9,11},{10,... | collective-permute-start | bytes 786440 | tf_op jit(solution)/shard_map/ppermute | solution.py:62
  107.0 10.2 %collective-permute-start.20 = (bf16[32,2,16,128]{3,2,1,0:T(8,128)(2,1)S(1)}, bf16[32,2,16,128]{3,2,1,0:T(8,128)(2,1)S(1)}, u32[]{:S(2)}, u32[]{:S(2)}) collective-permute-start(bf16[32,2,16,128]{3,2,1,0:T(8,128)(2,1)S(1)} %collective-permute-done.18.refs_0_), channel_id=1, source_target_pairs={{0,4},{1,5},{2,6},{3,7},{4,8},{5,9},{6,10},{7,11},{8,12},{9,13},{1... | collective-permute-start | bytes 786440 | tf_op jit(solution)/shard_map/ppermute | solution.py:62
  107.1 13.3 %collective-permute-start.23 = (bf16[32,2,16,128]{3,2,1,0:T(8,128)(2,1)S(1)}, bf16[32,2,16,128]{3,2,1,0:T(8,128)(2,1)S(1)}, u32[]{:S(2)}, u32[]{:S(2)}) collective-permute-start(bf16[32,2,16,128]{3,2,1,0:T(8,128)(2,1)S(1)} %collective-permute-done.22.refs_2_), channel_id=1, source_target_pairs={{0,2},{1,3},{2,0},{3,1},{4,6},{5,7},{6,4},{7,5},{8,10},{9,11},{10,... | collective-permute-start | bytes 786440 | tf_op jit(solution)/shard_map/ppermute | solution.py:62
  108.1 12.2 %collective-permute-start.25 = (bf16[32,2,16,128]{3,2,1,0:T(8,128)(2,1)S(1)}, bf16[32,2,16,128]{3,2,1,0:T(8,128)(2,1)S(1)}, u32[]{:S(2)}, u32[]{:S(2)}) collective-permute-start(bf16[32,2,16,128]{3,2,1,0:T(8,128)(2,1)S(1)} %collective-permute-done.18.refs_0_), channel_id=1, source_target_pairs={{0,1},{1,0},{2,3},{3,2},{4,5},{5,4},{6,7},{7,6},{8,9},{9,8},{10,11... | collective-permute-start | bytes 786440 | tf_op jit(solution)/shard_map/ppermute | solution.py:62
  117.3 3.1 %collective-permute-start.30 = (bf16[32,2,16,128]{3,2,1,0:T(8,128)(2,1)S(1)}, bf16[32,2,16,128]{3,2,1,0:T(8,128)(2,1)S(1)}, u32[]{:S(2)}, u32[]{:S(2)}) collective-permute-start(bf16[32,2,16,128]{3,2,1,0:T(8,128)(2,1)S(1)} %collective-permute-done.20.refs_1_), channel_id=1, source_target_pairs={{0,1},{1,0},{2,3},{3,2},{4,5},{5,4},{6,7},{7,6},{8,9},{9,8},{10,11... | collective-permute-start | bytes 786440 | tf_op jit(solution)/shard_map/ppermute | solution.py:62
  117.3 3.1 %collective-permute-start.32 = (bf16[32,2,16,128]{3,2,1,0:T(8,128)(2,1)S(1)}, bf16[32,2,16,128]{3,2,1,0:T(8,128)(2,1)S(1)}, u32[]{:S(2)}, u32[]{:S(2)}) collective-permute-start(bf16[32,2,16,128]{3,2,1,0:T(8,128)(2,1)S(1)} %collective-permute-done.24.refs_3_), channel_id=1, source_target_pairs={{0,1},{1,0},{2,3},{3,2},{4,5},{5,4},{6,7},{7,6},{8,9},{9,8},{10,11... | collective-permute-start | bytes 786440 | tf_op jit(solution)/shard_map/ppermute | solution.py:62
  143.3 2.7 %collective-permute-start.34 = (bf16[4,32,2,16,128]{4,3,2,1,0:T(8,128)(2,1)S(1)}, bf16[4,32,2,16,128]{4,3,2,1,0:T(8,128)(2,1)S(1)}, u32[]{:S(2)}, u32[]{:S(2)}) collective-permute-start(bf16[4,32,2,16,128]{4,3,2,1,0:T(8,128)(2,1)S(1)} %get-tuple-element.76), channel_id=1, source_target_pairs={{0,1},{1,0},{2,3},{3,2},{4,5},{5,4},{6,7},{7,6},{8,9},{9,8},{10,11... | collective-permute-start | bytes 3145736 | tf_op jit(solution)/shard_map/ppermute | solution.py:62
  143.5 4.8 %collective-permute-start.33 = (bf16[4,32,2,16,128]{4,3,2,1,0:T(8,128)(2,1)S(1)}, bf16[4,32,2,16,128]{4,3,2,1,0:T(8,128)(2,1)S(1)}, u32[]{:S(2)}, u32[]{:S(2)}) collective-permute-start(bf16[4,32,2,16,128]{4,3,2,1,0:T(8,128)(2,1)S(1)} %get-tuple-element.74), channel_id=1, source_target_pairs={{0,1},{1,0},{2,3},{3,2},{4,5},{5,4},{6,7},{7,6},{8,9},{9,8},{10,11... | collective-permute-start | bytes 3145736 | tf_op jit(solution)/shard_map/ppermute | solution.py:62
  146.2 9.2 %collective-permute-start.35 = (bf16[32,2,16,128]{3,2,1,0:T(8,128)(2,1)S(1)}, bf16[32,2,16,128]{3,2,1,0:T(8,128)(2,1)S(1)}, u32[]{:S(2)}, u32[]{:S(2)}) collective-permute-start(bf16[32,2,16,128]{3,2,1,0:T(8,128)(2,1)S(1)} %get-tuple-element.116), channel_id=1, source_target_pairs={{0,2},{1,3},{2,0},{3,1},{4,6},{5,7},{6,4},{7,5},{8,10},{9,11},{10,... | collective-permute-start | bytes 786440 | tf_op jit(solution)/shard_map/ppermute | solution.py:62
  147.3 9.9 %collective-permute-start.40 = (bf16[32,2,16,128]{3,2,1,0:T(8,128)(2,1)S(1)}, bf16[32,2,16,128]{3,2,1,0:T(8,128)(2,1)S(1)}, u32[]{:S(2)}, u32[]{:S(2)}) collective-permute-start(bf16[32,2,16,128]{3,2,1,0:T(8,128)(2,1)S(1)} %get-tuple-element.114), channel_id=1, source_target_pairs={{0,4},{1,5},{2,6},{3,7},{4,8},{5,9},{6,10},{7,11},{8,12},{9,13},{1... | collective-permute-start | bytes 786440 | tf_op jit(solution)/shard_map/ppermute | solution.py:62
  147.3 13.7 %collective-permute-start.38 = (bf16[32,2,16,128]{3,2,1,0:T(8,128)(2,1)S(1)}, bf16[32,2,16,128]{3,2,1,0:T(8,128)(2,1)S(1)}, u32[]{:S(2)}, u32[]{:S(2)}) collective-permute-start(bf16[32,2,16,128]{3,2,1,0:T(8,128)(2,1)S(1)} %get-tuple-element.115), channel_id=1, source_target_pairs={{0,2},{1,3},{2,0},{3,1},{4,6},{5,7},{6,4},{7,5},{8,10},{9,11},{10,... | collective-permute-start | bytes 786440 | tf_op jit(solution)/shard_map/ppermute | solution.py:62
  155.5 8.7 %collective-permute-start.36 = (bf16[32,2,16,128]{3,2,1,0:T(8,128)(2,1)S(1)}, bf16[32,2,16,128]{3,2,1,0:T(8,128)(2,1)S(1)}, u32[]{:S(2)}, u32[]{:S(2)}) collective-permute-start(bf16[32,2,16,128]{3,2,1,0:T(8,128)(2,1)S(1)} %fusion.2), channel_id=1, source_target_pairs={{0,4},{1,5},{2,6},{3,7},{4,8},{5,9},{6,10},{7,11},{8,12},{9,13},{1... | collective-permute-start | bytes 786440 | tf_op jit(solution)/shard_map/ppermute | solution.py:62
  157.3 9.4 %collective-permute-start.41 = (bf16[32,2,16,128]{3,2,1,0:T(8,128)(2,1)S(1)}, bf16[32,2,16,128]{3,2,1,0:T(8,128)(2,1)S(1)}, u32[]{:S(2)}, u32[]{:S(2)}) collective-permute-start(bf16[32,2,16,128]{3,2,1,0:T(8,128)(2,1)S(1)} %fusion), channel_id=1, source_target_pairs={{0,2},{1,3},{2,0},{3,1},{4,6},{5,7},{6,4},{7,5},{8,10},{9,11},{10,... | collective-permute-start | bytes 786440 | tf_op jit(solution)/shard_map/ppermute | solution.py:62
  164.4 11.5 %collective-permute-start.39 = (bf16[32,2,16,128]{3,2,1,0:T(8,128)(2,1)S(1)}, bf16[32,2,16,128]{3,2,1,0:T(8,128)(2,1)S(1)}, u32[]{:S(2)}, u32[]{:S(2)}) collective-permute-start(bf16[32,2,16,128]{3,2,1,0:T(8,128)(2,1)S(1)} %get-tuple-element.117), channel_id=1, source_target_pairs={{0,12},{1,13},{2,14},{3,15},{4,0},{5,1},{6,2},{7,3},{8,4},{9,5},{1... | collective-permute-start | bytes 786440 | tf_op jit(solution)/shard_map/ppermute | solution.py:62
  164.7 11.3 %collective-permute-start.37 = (bf16[32,2,16,128]{3,2,1,0:T(8,128)(2,1)S(1)}, bf16[32,2,16,128]{3,2,1,0:T(8,128)(2,1)S(1)}, u32[]{:S(2)}, u32[]{:S(2)}) collective-permute-start(bf16[32,2,16,128]{3,2,1,0:T(8,128)(2,1)S(1)} %get-tuple-element.118), channel_id=1, source_target_pairs={{0,4},{1,5},{2,6},{3,7},{4,8},{5,9},{6,10},{7,11},{8,12},{9,13},{1... | collective-permute-start | bytes 786440 | tf_op jit(solution)/shard_map/ppermute | solution.py:62
  176.4 7.7 %collective-permute-start.43 = (bf16[16,64,128]{2,1,0:T(8,128)(2,1)S(1)}, bf16[16,64,128]{2,1,0:T(8,128)(2,1)S(1)}, u32[]{:S(2)}, u32[]{:S(2)}) collective-permute-start(bf16[16,64,128]{2,1,0:T(8,128)(2,1)S(1)} %window.5.refs_4_), channel_id=1, source_target_pairs={{0,2},{1,3},{2,0},{3,1},{4,6},{5,7},{6,4},{7,5},{8,10},{9,11},{10,... | collective-permute-start | bytes 786440 | tf_op jit(solution)/shard_map/ppermute | solution.py:62
  177.9 10.4 %collective-permute-start.42 = (bf16[16,64,128]{2,1,0:T(8,128)(2,1)S(1)}, bf16[16,64,128]{2,1,0:T(8,128)(2,1)S(1)}, u32[]{:S(2)}, u32[]{:S(2)}) collective-permute-start(bf16[16,64,128]{2,1,0:T(8,128)(2,1)S(1)} %window.5.refs_4_), channel_id=1, source_target_pairs={{0,4},{1,5},{2,6},{3,7},{4,8},{5,9},{6,10},{7,11},{8,12},{9,13},{1... | collective-permute-start | bytes 786440 | tf_op jit(solution)/shard_map/ppermute | solution.py:62
  177.9 14.4 %collective-permute-start.45 = (bf16[16,64,128]{2,1,0:T(8,128)(2,1)S(1)}, bf16[16,64,128]{2,1,0:T(8,128)(2,1)S(1)}, u32[]{:S(2)}, u32[]{:S(2)}) collective-permute-start(bf16[16,64,128]{2,1,0:T(8,128)(2,1)S(1)} %window.5.refs_4_), channel_id=1, source_target_pairs={{0,12},{1,13},{2,14},{3,15},{4,0},{5,1},{6,2},{7,3},{8,4},{9,5},{1... | collective-permute-start | bytes 786440 | tf_op jit(solution)/shard_map/ppermute | solution.py:62
  188.2 13.0 %collective-permute-start.44 = (bf16[16,64,128]{2,1,0:T(8,128)(2,1)S(1)}, bf16[16,64,128]{2,1,0:T(8,128)(2,1)S(1)}, u32[]{:S(2)}, u32[]{:S(2)}) collective-permute-start(bf16[16,64,128]{2,1,0:T(8,128)(2,1)S(1)} %collective-permute-done.42.refs_4_), channel_id=1, source_target_pairs={{0,4},{1,5},{2,6},{3,7},{4,8},{5,9},{6,10},{7,11},{8,12},{9,13},{1... | collective-permute-start | bytes 786440 | tf_op jit(solution)/shard_map/ppermute | solution.py:62
  192.3 11.4 %collective-permute-start.48 = (bf16[16,64,128]{2,1,0:T(8,128)(2,1)S(1)}, bf16[16,64,128]{2,1,0:T(8,128)(2,1)S(1)}, u32[]{:S(2)}, u32[]{:S(2)}) collective-permute-start(bf16[16,64,128]{2,1,0:T(8,128)(2,1)S(1)} %collective-permute-done.45.refs_4_), channel_id=1, source_target_pairs={{0,2},{1,3},{2,0},{3,1},{4,6},{5,7},{6,4},{7,5},{8,10},{9,11},{10,... | collective-permute-start | bytes 786440 | tf_op jit(solution)/shard_map/ppermute | solution.py:62
  192.8 11.4 %collective-permute-start.47 = (bf16[16,64,128]{2,1,0:T(8,128)(2,1)S(1)}, bf16[16,64,128]{2,1,0:T(8,128)(2,1)S(1)}, u32[]{:S(2)}, u32[]{:S(2)}) collective-permute-start(bf16[16,64,128]{2,1,0:T(8,128)(2,1)S(1)} %collective-permute-done.43.refs_4_), channel_id=1, source_target_pairs={{0,4},{1,5},{2,6},{3,7},{4,8},{5,9},{6,10},{7,11},{8,12},{9,13},{1... | collective-permute-start | bytes 786440 | tf_op jit(solution)/shard_map/ppermute | solution.py:62
  193.4 17.4 %collective-permute-start.50 = (bf16[32,2,16,128]{3,2,1,0:T(8,128)(2,1)S(1)}, bf16[32,2,16,128]{3,2,1,0:T(8,128)(2,1)S(1)}, u32[]{:S(2)}, u32[]{:S(2)}) collective-permute-start(bf16[32,2,16,128]{3,2,1,0:T(8,128)(2,1)S(1)} %get-tuple-element.78.refs_0_), channel_id=1, source_target_pairs={{0,1},{1,0},{2,3},{3,2},{4,5},{5,4},{6,7},{7,6},{8,9},{9,8},{10,11... | collective-permute-start | bytes 786440 | tf_op jit(solution)/shard_map/ppermute | solution.py:62
  200.6 10.2 %collective-permute-start.53 = (bf16[32,2,16,128]{3,2,1,0:T(8,128)(2,1)S(1)}, bf16[32,2,16,128]{3,2,1,0:T(8,128)(2,1)S(1)}, u32[]{:S(2)}, u32[]{:S(2)}) collective-permute-start(bf16[32,2,16,128]{3,2,1,0:T(8,128)(2,1)S(1)} %get-tuple-element.88.refs_3_), channel_id=1, source_target_pairs={{0,1},{1,0},{2,3},{3,2},{4,5},{5,4},{6,7},{7,6},{8,9},{9,8},{10,11... | collective-permute-start | bytes 786440 | tf_op jit(solution)/shard_map/ppermute | solution.py:62
  201.2 9.6 %collective-permute-start.51 = (bf16[32,2,16,128]{3,2,1,0:T(8,128)(2,1)S(1)}, bf16[32,2,16,128]{3,2,1,0:T(8,128)(2,1)S(1)}, u32[]{:S(2)}, u32[]{:S(2)}) collective-permute-start(bf16[32,2,16,128]{3,2,1,0:T(8,128)(2,1)S(1)} %get-tuple-element.85.refs_1_), channel_id=1, source_target_pairs={{0,1},{1,0},{2,3},{3,2},{4,5},{5,4},{6,7},{7,6},{8,9},{9,8},{10,11... | collective-permute-start | bytes 786440 | tf_op jit(solution)/shard_map/ppermute | solution.py:62
  203.7 7.1 %collective-permute-start.52 = (bf16[32,2,16,128]{3,2,1,0:T(8,128)(2,1)S(1)}, bf16[32,2,16,128]{3,2,1,0:T(8,128)(2,1)S(1)}, u32[]{:S(2)}, u32[]{:S(2)}) collective-permute-start(bf16[32,2,16,128]{3,2,1,0:T(8,128)(2,1)S(1)} %get-tuple-element.92.refs_2_), channel_id=1, source_target_pairs={{0,1},{1,0},{2,3},{3,2},{4,5},{5,4},{6,7},{7,6},{8,9},{9,8},{10,11... | collective-permute-start | bytes 786440 | tf_op jit(solution)/shard_map/ppermute | solution.py:62
  204.2 14.2 %collective-permute-start.46 = (bf16[16,64,128]{2,1,0:T(8,128)(2,1)S(1)}, bf16[16,64,128]{2,1,0:T(8,128)(2,1)S(1)}, u32[]{:S(2)}, u32[]{:S(2)}) collective-permute-start(bf16[16,64,128]{2,1,0:T(8,128)(2,1)S(1)} %collective-permute-done.44.refs_4_), channel_id=1, source_target_pairs={{0,2},{1,3},{2,0},{3,1},{4,6},{5,7},{6,4},{7,5},{8,10},{9,11},{10,... | collective-permute-start | bytes 786440 | tf_op jit(solution)/shard_map/ppermute | solution.py:62
  210.7 11.2 %collective-permute-start.49 = (bf16[32,2,16,128]{3,2,1,0:T(8,128)(2,1)S(1)}, bf16[32,2,16,128]{3,2,1,0:T(8,128)(2,1)S(1)}, u32[]{:S(2)}, u32[]{:S(2)}) collective-permute-start(bf16[32,2,16,128]{3,2,1,0:T(8,128)(2,1)S(1)} %get-tuple-element.82.refs_0_), channel_id=1, source_target_pairs={{0,1},{1,0},{2,3},{3,2},{4,5},{5,4},{6,7},{7,6},{8,9},{9,8},{10,11... | collective-permute-start | bytes 786440 | tf_op jit(solution)/shard_map/ppermute | solution.py:62
  231.0 28.5 %collective-permute-start.57 = (bf16[16,32,1024]{2,1,0:T(8,128)(2,1)S(1)}, bf16[16,32,1024]{2,1,0:T(8,128)(2,1)S(1)}, u32[]{:S(2)}, u32[]{:S(2)}) collective-permute-start(bf16[16,32,1024]{2,1,0:T(8,128)(2,1)S(1)} %get-tuple-element.109), channel_id=1, source_target_pairs={{0,1},{1,0},{2,3},{3,2},{4,5},{5,4},{6,7},{7,6},{8,9},{9,8},{10,11... | collective-permute-start | bytes 3145736 | tf_op jit(solution)/shard_map/ppermute | solution.py:62
  231.4 9.8 %collective-permute-start.60 = (bf16[16,64,128]{2,1,0:T(8,128)(2,1)S(1)}, bf16[16,64,128]{2,1,0:T(8,128)(2,1)S(1)}, u32[]{:S(2)}, u32[]{:S(2)}) collective-permute-start(bf16[16,64,128]{2,1,0:T(8,128)(2,1)S(1)} %correlate1.3.refs_0_), channel_id=1, source_target_pairs={{0,12},{1,13},{2,14},{3,15},{4,0},{5,1},{6,2},{7,3},{8,4},{9,5},{1... | collective-permute-start | bytes 786440 | tf_op jit(solution)/shard_map/ppermute | solution.py:62
  234.5 8.1 %collective-permute-start.59 = (bf16[16,64,128]{2,1,0:T(8,128)(2,1)S(1)}, bf16[16,64,128]{2,1,0:T(8,128)(2,1)S(1)}, u32[]{:S(2)}, u32[]{:S(2)}) collective-permute-start(bf16[16,64,128]{2,1,0:T(8,128)(2,1)S(1)} %correlate1.3.refs_0_), channel_id=1, source_target_pairs={{0,2},{1,3},{2,0},{3,1},{4,6},{5,7},{6,4},{7,5},{8,10},{9,11},{10,... | collective-permute-start | bytes 786440 | tf_op jit(solution)/shard_map/ppermute | solution.py:62
  235.0 12.2 %collective-permute-start.58 = (bf16[16,64,128]{2,1,0:T(8,128)(2,1)S(1)}, bf16[16,64,128]{2,1,0:T(8,128)(2,1)S(1)}, u32[]{:S(2)}, u32[]{:S(2)}) collective-permute-start(bf16[16,64,128]{2,1,0:T(8,128)(2,1)S(1)} %correlate1.3.refs_0_), channel_id=1, source_target_pairs={{0,4},{1,5},{2,6},{3,7},{4,8},{5,9},{6,10},{7,11},{8,12},{9,13},{1... | collective-permute-start | bytes 786440 | tf_op jit(solution)/shard_map/ppermute | solution.py:62
  242.6 12.0 %collective-permute-start.62 = (bf16[16,64,128]{2,1,0:T(8,128)(2,1)S(1)}, bf16[16,64,128]{2,1,0:T(8,128)(2,1)S(1)}, u32[]{:S(2)}, u32[]{:S(2)}) collective-permute-start(bf16[16,64,128]{2,1,0:T(8,128)(2,1)S(1)} %collective-permute-done.59.refs_4_), channel_id=1, source_target_pairs={{0,4},{1,5},{2,6},{3,7},{4,8},{5,9},{6,10},{7,11},{8,12},{9,13},{1... | collective-permute-start | bytes 786440 | tf_op jit(solution)/shard_map/ppermute | solution.py:62
  247.2 7.4 %collective-permute-start.63 = (bf16[16,64,128]{2,1,0:T(8,128)(2,1)S(1)}, bf16[16,64,128]{2,1,0:T(8,128)(2,1)S(1)}, u32[]{:S(2)}, u32[]{:S(2)}) collective-permute-start(bf16[16,64,128]{2,1,0:T(8,128)(2,1)S(1)} %collective-permute-done.60.refs_3_), channel_id=1, source_target_pairs={{0,2},{1,3},{2,0},{3,1},{4,6},{5,7},{6,4},{7,5},{8,10},{9,11},{10,... | collective-permute-start | bytes 786440 | tf_op jit(solution)/shard_map/ppermute | solution.py:62
  248.5 9.5 %collective-permute-start.61 = (bf16[16,64,128]{2,1,0:T(8,128)(2,1)S(1)}, bf16[16,64,128]{2,1,0:T(8,128)(2,1)S(1)}, u32[]{:S(2)}, u32[]{:S(2)}) collective-permute-start(bf16[16,64,128]{2,1,0:T(8,128)(2,1)S(1)} %collective-permute-done.58.refs_1_), channel_id=1, source_target_pairs={{0,4},{1,5},{2,6},{3,7},{4,8},{5,9},{6,10},{7,11},{8,12},{9,13},{1... | collective-permute-start | bytes 786440 | tf_op jit(solution)/shard_map/ppermute | solution.py:62
  258.0 6.8 %collective-permute-start.64 = (bf16[16,64,128]{2,1,0:T(8,128)(2,1)S(1)}, bf16[16,64,128]{2,1,0:T(8,128)(2,1)S(1)}, u32[]{:S(2)}, u32[]{:S(2)}) collective-permute-start(bf16[16,64,128]{2,1,0:T(8,128)(2,1)S(1)} %collective-permute-done.61.refs_2_), channel_id=1, source_target_pairs={{0,2},{1,3},{2,0},{3,1},{4,6},{5,7},{6,4},{7,5},{8,10},{9,11},{10,... | collective-permute-start | bytes 786440 | tf_op jit(solution)/shard_map/ppermute | solution.py:62
  259.0 5.9 %collective-permute-start.65 = (bf16[16,64,128]{2,1,0:T(8,128)(2,1)S(1)}, bf16[16,64,128]{2,1,0:T(8,128)(2,1)S(1)}, u32[]{:S(2)}, u32[]{:S(2)}) collective-permute-start(bf16[16,64,128]{2,1,0:T(8,128)(2,1)S(1)} %correlate1.3.refs_0_), channel_id=1, source_target_pairs={{0,1},{1,0},{2,3},{3,2},{4,5},{5,4},{6,7},{7,6},{8,9},{9,8},{10,11... | collective-permute-start | bytes 786440 | tf_op jit(solution)/shard_map/ppermute | solution.py:62
  259.0 6.4 %collective-permute-start.68 = (bf16[16,64,128]{2,1,0:T(8,128)(2,1)S(1)}, bf16[16,64,128]{2,1,0:T(8,128)(2,1)S(1)}, u32[]{:S(2)}, u32[]{:S(2)}) collective-permute-start(bf16[16,64,128]{2,1,0:T(8,128)(2,1)S(1)} %collective-permute-done.60.refs_3_), channel_id=1, source_target_pairs={{0,1},{1,0},{2,3},{3,2},{4,5},{5,4},{6,7},{7,6},{8,9},{9,8},{10,11... | collective-permute-start | bytes 786440 | tf_op jit(solution)/shard_map/ppermute | solution.py:62
  259.5 5.9 %collective-permute-start.69 = (bf16[16,64,128]{2,1,0:T(8,128)(2,1)S(1)}, bf16[16,64,128]{2,1,0:T(8,128)(2,1)S(1)}, u32[]{:S(2)}, u32[]{:S(2)}) collective-permute-start(bf16[16,64,128]{2,1,0:T(8,128)(2,1)S(1)} %collective-permute-done.59.refs_4_), channel_id=1, source_target_pairs={{0,1},{1,0},{2,3},{3,2},{4,5},{5,4},{6,7},{7,6},{8,9},{9,8},{10,11... | collective-permute-start | bytes 786440 | tf_op jit(solution)/shard_map/ppermute | solution.py:62
  259.5 6.4 %collective-permute-start.66 = (bf16[16,64,128]{2,1,0:T(8,128)(2,1)S(1)}, bf16[16,64,128]{2,1,0:T(8,128)(2,1)S(1)}, u32[]{:S(2)}, u32[]{:S(2)}) collective-permute-start(bf16[16,64,128]{2,1,0:T(8,128)(2,1)S(1)} %collective-permute-done.58.refs_1_), channel_id=1, source_target_pairs={{0,1},{1,0},{2,3},{3,2},{4,5},{5,4},{6,7},{7,6},{8,9},{9,8},{10,11... | collective-permute-start | bytes 786440 | tf_op jit(solution)/shard_map/ppermute | solution.py:62
  (17 other events, 119.0 us)

commit v12 on v11

--- a/solution.py
+++ b/solution.py
@@ -598,8 +598,6 @@
         line[step] = places.send(block, places.shift(step))
     across = {0: places.send(block, places.pair())}
     own = run(0, [0], line)
-    if together:
-        own = [line[size - 1]]
     for step in range(2, size // 2 + 1):
         line[step] = places.send(after(line[step - 1], across[0], *own), places.shift(1))
     for step in range(size - 2, size // 2, -1):

time: 270 us -> 270 us (level)
  no operation moved by 1% of the time
where the time goes in v12:
time: 270 us
  waiting for transfers between devices  125 us (46%)
  Pallas kernels  83.3 us (31%)
  starting transfers between devices  54.8 us (20%)
  local copies, waits for them, and re-layouts  2.82 us (1%)
    ppermute x73, waiting for transfers between devices, send(): return lax.ppermute(array, self.axis, pairs)  125 us
    ppermute x73, starting transfers between devices, send(): return lax.ppermute(array, self.axis, pairs)  54.8 us
    pallas_call x4, Pallas kernels, correlate(): pl.pallas_call(functools.partial(correlate_kernel, line, flip, bool(more)...  30.3 us
    pallas_call x2, Pallas kernels, convolve(): pl.pallas_call(functools.partial(convolve_kernel, line), in_specs=[VMEM,...  23.4 us
    pallas_call x8, Pallas kernels, window_at(): pl.pallas_call(functools.partial(window_at_kernel, line, flip, step, begu...  19.3 us
  transfers between devices with their start and end apart: 73, of which 41 were waited for; matrix products, arithmetic and copies ran while one was open for 1% of the time, Pallas kernels for 13%

profile of v12, /device:TPU:0, one launch (start us, length us, event | category | flops | bytes accessed | tf_op | source)
XLA Modules:
  0.0 269.9 jit_solution(943016944262494495)
XLA Ops:
  0.6 1.6 copy-done.2
  3.2 1.9 first_analysis.1
  5.7 2.2 collective-permute-done.1
  8.2 3.0 %collective-permute-start.2 = (bf16[16,64,128]{2,1,0:T(8,128)(2,1)S(1)}, bf16[16,64,128]{2,1,0:T(8,128)(2,1)S(1)}, u32[]{:S(2)}, u32[]{:S(2)}) collective-permute-start(bf16[16,64,128]{2,1,0:T(8,128)(2,1)S(1)} %get-tuple-element.126), channel_id=1, source_target_pairs={{0,2},{1,3},{2,0},{3,1},{4,6},{5,7},{6,4},{7,5},{8,10},{9,11},{10,... | collective-permute-start | bytes 786440 | tf_op jit(solution)/shard_map/ppermute | solution.py:62
  11.2 1.6 collective-permute-start.7
  13.3 5.0 %collective-permute-done.2 = bf16[16,64,128]{2,1,0:T(8,128)(2,1)S(1)} collective-permute-done((bf16[16,64,128]{2,1,0:T(8,128)(2,1)S(1)}, bf16[16,64,128]{2,1,0:T(8,128)(2,1)S(1)}, u32[]{:S(2)}, u32[]{:S(2)}) %collective-permute-start.2) | collective-permute-done | bytes 262176 | tf_op jit(solution)/shard_map/ppermute | solution.py:62
  18.4 2.2 collective-permute-start.3
  22.3 1.5 collective-permute-done.5
  23.8 3.8 %collective-permute-done.3 = bf16[16,64,128]{2,1,0:T(8,128)(2,1)S(1)} collective-permute-done((bf16[16,64,128]{2,1,0:T(8,128)(2,1)S(1)}, bf16[16,64,128]{2,1,0:T(8,128)(2,1)S(1)}, u32[]{:S(2)}, u32[]{:S(2)}) %collective-permute-start.3) | collective-permute-done | bytes 262176 | tf_op jit(solution)/shard_map/ppermute | solution.py:62
  27.9 3.8 %collective-permute-start.6 = (bf16[16,64,128]{2,1,0:T(8,128)(2,1)S(1)}, bf16[16,64,128]{2,1,0:T(8,128)(2,1)S(1)}, u32[]{:S(2)}, u32[]{:S(2)}) collective-permute-start(bf16[16,64,128]{2,1,0:T(8,128)(2,1)S(1)} %get-tuple-element.125), channel_id=1, source_target_pairs={{0,12},{1,13},{2,14},{3,15},{4,0},{5,1},{6,2},{7,3},{8,4},{9,5},{1... | collective-permute-start | bytes 786440 | tf_op jit(solution)/shard_map/ppermute | solution.py:62
  31.7 7.0 %collective-permute-done.4 = bf16[16,64,128]{2,1,0:T(8,128)(2,1)S(1)} collective-permute-done((bf16[16,64,128]{2,1,0:T(8,128)(2,1)S(1)}, bf16[16,64,128]{2,1,0:T(8,128)(2,1)S(1)}, u32[]{:S(2)}, u32[]{:S(2)}) %collective-permute-start.4) | collective-permute-done | bytes 262176 | tf_op jit(solution)/shard_map/ppermute | solution.py:62
  40.1 11.7 %convolve.2 = (bf16[4,32,2,16,128]{4,3,2,1,0:T(8,128)(2,1)S(1)}, bf16[4,32,2,16,128]{4,3,2,1,0:T(8,128)(2,1)S(1)}, bf16[4,32,2,16,128]{4,3,2,1,0:T(8,128)(2,1)S(1)}, bf16[4,32,2,16,128]{4,3,2,1,0:T(8,128)(2,1)S(1)}) custom-call(bf16[32,2,16,128]{3,2,1,0:T(8,128)(2,1)S(1)} %bitcast.87, bf16[2,32,128,2048]{3,2,1,0:T(8,128)(2,1)} %refs_8_.7), custom_call_target="tpu_custom_call" | custom-call | flops 1073741824 | bytes 37748736 | tf_op jit(solution)/shard_map/convolve/pallas_call | solution.py:238
  52.4 2.1 collective-permute-done.10
  57.4 6.5 %collective-permute-done.11 = bf16[32,2,16,128]{3,2,1,0:T(8,128)(2,1)S(1)} collective-permute-done((bf16[32,2,16,128]{3,2,1,0:T(8,128)(2,1)S(1)}, bf16[32,2,16,128]{3,2,1,0:T(8,128)(2,1)S(1)}, u32[]{:S(2)}, u32[]{:S(2)}) %collective-permute-start.11) | collective-permute-done | bytes 262176 | tf_op jit(solution)/shard_map/ppermute | solution.py:62
  66.9 2.7 collective-permute-done.14
  69.6 3.2 %collective-permute-done.12 = bf16[32,2,16,128]{3,2,1,0:T(8,128)(2,1)S(1)} collective-permute-done((bf16[32,2,16,128]{3,2,1,0:T(8,128)(2,1)S(1)}, bf16[32,2,16,128]{3,2,1,0:T(8,128)(2,1)S(1)}, u32[]{:S(2)}, u32[]{:S(2)}) %collective-permute-start.12) | collective-permute-done | bytes 262176 | tf_op jit(solution)/shard_map/ppermute | solution.py:62
  73.2 1.8 collective-permute-start.13
  75.1 6.5 %collective-permute-done.15.refs_6_ = bf16[32,2,16,128]{3,2,1,0:T(8,128)(2,1)S(1)} collective-permute-done((bf16[32,2,16,128]{3,2,1,0:T(8,128)(2,1)S(1)}, bf16[32,2,16,128]{3,2,1,0:T(8,128)(2,1)S(1)}, u32[]{:S(2)}, u32[]{:S(2)}) %collective-permute-start.15) | collective-permute-done | bytes 262176 | tf_op jit(solution)/shard_map/ppermute | solution.py:62
  81.6 2.8 %collective-permute-done.13.refs_5_ = bf16[32,2,16,128]{3,2,1,0:T(8,128)(2,1)S(1)} collective-permute-done((bf16[32,2,16,128]{3,2,1,0:T(8,128)(2,1)S(1)}, bf16[32,2,16,128]{3,2,1,0:T(8,128)(2,1)S(1)}, u32[]{:S(2)}, u32[]{:S(2)}) %collective-permute-start.13) | collective-permute-done | bytes 262176 | tf_op jit(solution)/shard_map/ppermute | solution.py:62
  84.5 2.2 window.3.refs_0_
  87.0 1.4 collective-permute-start.18
  88.4 3.4 %collective-permute-start.19 = (bf16[32,2,16,128]{3,2,1,0:T(8,128)(2,1)S(1)}, bf16[32,2,16,128]{3,2,1,0:T(8,128)(2,1)S(1)}, u32[]{:S(2)}, u32[]{:S(2)}) collective-permute-start(bf16[32,2,16,128]{3,2,1,0:T(8,128)(2,1)S(1)} %window.3.refs_0_), channel_id=1, source_target_pairs={{0,12},{1,13},{2,14},{3,15},{4,0},{5,1},{6,2},{7,3},{8,4},{9,5},{1... | collective-permute-start | bytes 786440 | tf_op jit(solution)/shard_map/ppermute | solution.py:62
  91.8 6.1 %collective-permute-done.21.refs_1_ = bf16[32,2,16,128]{3,2,1,0:T(8,128)(2,1)S(1)} collective-permute-done((bf16[32,2,16,128]{3,2,1,0:T(8,128)(2,1)S(1)}, bf16[32,2,16,128]{3,2,1,0:T(8,128)(2,1)S(1)}, u32[]{:S(2)}, u32[]{:S(2)}) %collective-permute-start.21) | collective-permute-done | bytes 262176 | tf_op jit(solution)/shard_map/ppermute | solution.py:62
  99.3 3.2 %collective-permute-done.19.refs_3_ = bf16[32,2,16,128]{3,2,1,0:T(8,128)(2,1)S(1)} collective-permute-done((bf16[32,2,16,128]{3,2,1,0:T(8,128)(2,1)S(1)}, bf16[32,2,16,128]{3,2,1,0:T(8,128)(2,1)S(1)}, u32[]{:S(2)}, u32[]{:S(2)}) %collective-permute-start.19) | collective-permute-done | bytes 262176 | tf_op jit(solution)/shard_map/ppermute | solution.py:62
  102.5 3.5 %collective-permute-done.22.refs_2_ = bf16[32,2,16,128]{3,2,1,0:T(8,128)(2,1)S(1)} collective-permute-done((bf16[32,2,16,128]{3,2,1,0:T(8,128)(2,1)S(1)}, bf16[32,2,16,128]{3,2,1,0:T(8,128)(2,1)S(1)}, u32[]{:S(2)}, u32[]{:S(2)}) %collective-permute-start.22) | collective-permute-done | bytes 262176 | tf_op jit(solution)/shard_map/ppermute | solution.py:62
  108.1 7.5 %correlate0.2.refs_9_ = f32[32,2,16,128]{3,2,1,0:T(8,128)S(1)} custom-call(bf16[32,2,16,128]{3,2,1,0:T(8,128)(2,1)S(1)} %window.3.refs_0_, bf16[32,2,16,128]{3,2,1,0:T(8,128)(2,1)S(1)} %collective-permute-done.21.refs_1_, bf16[32,2,16,128]{3,2,1,0:T(8,128)(2,1)S(1)} %collective-permute-done.22.refs_2_, ...), custom_call_target="tpu_custom_call" | custom-call | flops 536870912 | bytes 18874368 | tf_op jit(solution)/shard_map/correlate0/pallas_call | solution.py:312
  115.7 1.6 collective-permute-done.20.refs_1_
  117.8 2.6 collective-permute-done.23.refs_2_
  120.4 1.5 collective-permute-done.31.refs_6_
  121.9 7.5 %correlate1.2.refs_3_ = f32[32,2,16,128]{3,2,1,0:T(8,128)S(1)} custom-call(bf16[32,2,16,128]{3,2,1,0:T(8,128)(2,1)S(1)} %collective-permute-done.18.refs_0_, bf16[32,2,16,128]{3,2,1,0:T(8,128)(2,1)S(1)} %collective-permute-done.20.refs_1_, bf16[32,2,16,128]{3,2,1,0:T(8,128)(2,1)S(1)} %collective-permute-done.23.refs_2_, ...), custom_call_target="tpu_custom_call" | custom-call | flops 536870912 | bytes 18874368 | tf_op jit(solution)/shard_map/correlate1/pallas_call | solution.py:312
  129.4 2.1 window.4.spec_ref
  131.6 11.7 %convolve.3 = (bf16[4,32,2,16,128]{4,3,2,1,0:T(8,128)(2,1)S(1)}, bf16[4,32,2,16,128]{4,3,2,1,0:T(8,128)(2,1)S(1)}, bf16[4,32,2,16,128]{4,3,2,1,0:T(8,128)(2,1)S(1)}, bf16[4,32,2,16,128]{4,3,2,1,0:T(8,128)(2,1)S(1)}) custom-call(bf16[32,2,16,128]{3,2,1,0:T(8,128)(2,1)S(1)} %window.4.spec_ref, bf16[2,32,128,2048]{3,2,1,0:T(8,128)(2,1)} %refs_8_.7), custom_call_target="tpu_custom_call" | custom-call | flops 1073741824 | bytes 37748736 | tf_op jit(solution)/shard_map/convolve/pallas_call | solution.py:238
  143.8 2.1 collective-permute-done.34
  148.3 7.1 %collective-permute-done.35 = bf16[32,2,16,128]{3,2,1,0:T(8,128)(2,1)S(1)} collective-permute-done((bf16[32,2,16,128]{3,2,1,0:T(8,128)(2,1)S(1)}, bf16[32,2,16,128]{3,2,1,0:T(8,128)(2,1)S(1)}, u32[]{:S(2)}, u32[]{:S(2)}) %collective-permute-start.35) | collective-permute-done | bytes 262176 | tf_op jit(solution)/shard_map/ppermute | solution.py:62
  155.6 1.6 collective-permute-done.40
  158.4 2.7 collective-permute-done.38
  161.0 3.2 %collective-permute-done.36 = bf16[32,2,16,128]{3,2,1,0:T(8,128)(2,1)S(1)} collective-permute-done((bf16[32,2,16,128]{3,2,1,0:T(8,128)(2,1)S(1)}, bf16[32,2,16,128]{3,2,1,0:T(8,128)(2,1)S(1)}, u32[]{:S(2)}, u32[]{:S(2)}) %collective-permute-start.36) | collective-permute-done | bytes 262176 | tf_op jit(solution)/shard_map/ppermute | solution.py:62
  164.7 2.0 collective-permute-start.37
  166.7 9.2 %collective-permute-done.39.refs_6_ = bf16[32,2,16,128]{3,2,1,0:T(8,128)(2,1)S(1)} collective-permute-done((bf16[32,2,16,128]{3,2,1,0:T(8,128)(2,1)S(1)}, bf16[32,2,16,128]{3,2,1,0:T(8,128)(2,1)S(1)}, u32[]{:S(2)}, u32[]{:S(2)}) %collective-permute-start.39) | collective-permute-done | bytes 262176 | tf_op jit(solution)/shard_map/ppermute | solution.py:62
  176.4 1.5 collective-permute-start.43
  177.9 3.8 %collective-permute-start.45 = (bf16[16,64,128]{2,1,0:T(8,128)(2,1)S(1)}, bf16[16,64,128]{2,1,0:T(8,128)(2,1)S(1)}, u32[]{:S(2)}, u32[]{:S(2)}) collective-permute-start(bf16[16,64,128]{2,1,0:T(8,128)(2,1)S(1)} %window.5.refs_4_), channel_id=1, source_target_pairs={{0,12},{1,13},{2,14},{3,15},{4,0},{5,1},{6,2},{7,3},{8,4},{9,5},{1... | collective-permute-start | bytes 786440 | tf_op jit(solution)/shard_map/ppermute | solution.py:62
  181.7 2.4 window_at.8
  184.1 4.1 %collective-permute-done.42.refs_4_ = bf16[16,64,128]{2,1,0:T(8,128)(2,1)S(1)} collective-permute-done((bf16[16,64,128]{2,1,0:T(8,128)(2,1)S(1)}, bf16[16,64,128]{2,1,0:T(8,128)(2,1)S(1)}, u32[]{:S(2)}, u32[]{:S(2)}) %collective-permute-start.42) | collective-permute-done | bytes 262176 | tf_op jit(solution)/shard_map/ppermute | solution.py:62
  188.2 4.1 %collective-permute-done.45.refs_4_ = bf16[16,64,128]{2,1,0:T(8,128)(2,1)S(1)} collective-permute-done((bf16[16,64,128]{2,1,0:T(8,128)(2,1)S(1)}, bf16[16,64,128]{2,1,0:T(8,128)(2,1)S(1)}, u32[]{:S(2)}, u32[]{:S(2)}) %collective-permute-start.45) | collective-permute-done | bytes 262176 | tf_op jit(solution)/shard_map/ppermute | solution.py:62
  193.4 2.4 window_at.9
  195.8 2.4 window_at.10
  198.2 2.4 window_at.11
  201.3 2.4 window_at.12
  204.2 1.7 collective-permute-start.46
  205.9 2.4 window_at.13
  208.3 2.4 window_at.14
  210.9 7.5 %correlate0.3.refs_9_ = f32[32,2,16,128]{3,2,1,0:T(8,128)S(1)} custom-call(bf16[32,2,16,128]{3,2,1,0:T(8,128)(2,1)S(1)} %get-tuple-element.78.refs_0_, bf16[32,2,16,128]{3,2,1,0:T(8,128)(2,1)S(1)} %get-tuple-element.85.refs_1_, bf16[32,2,16,128]{3,2,1,0:T(8,128)(2,1)S(1)} %get-tuple-element.92.refs_2_, ...), custom_call_target="tpu_custom_call" | custom-call | flops 536870912 | bytes 18874368 | tf_op jit(solution)/shard_map/correlate0/pallas_call | solution.py:312
  218.4 2.4 window_at.15
  223.3 7.7 %correlate1.3.refs_0_ = bf16[16,64,128]{2,1,0:T(8,128)(2,1)S(1)} custom-call(bf16[32,2,16,128]{3,2,1,0:T(8,128)(2,1)S(1)} %get-tuple-element.82.refs_0_, bf16[32,2,16,128]{3,2,1,0:T(8,128)(2,1)S(1)} %get-tuple-element.106.refs_1_, bf16[32,2,16,128]{3,2,1,0:T(8,128)(2,1)S(1)} %get-tuple-element.107.refs_2_, ...), custom_call_target="tpu_custom_call" | custom-call | flops 536870912 | bytes 18874368 | tf_op jit(solution)/shard_map/correlate1/pallas_call | solution.py:312
  231.4 3.1 %collective-permute-start.61 = (bf16[16,64,128]{2,1,0:T(8,128)(2,1)S(1)}, bf16[16,64,128]{2,1,0:T(8,128)(2,1)S(1)}, u32[]{:S(2)}, u32[]{:S(2)}) collective-permute-start(bf16[16,64,128]{2,1,0:T(8,128)(2,1)S(1)} %correlate1.3.refs_0_), channel_id=1, source_target_pairs={{0,12},{1,13},{2,14},{3,15},{4,0},{5,1},{6,2},{7,3},{8,4},{9,5},{1... | collective-permute-start | bytes 786440 | tf_op jit(solution)/shard_map/ppermute | solution.py:62
  235.0 6.2 %collective-permute-done.61.refs_3_ = bf16[16,64,128]{2,1,0:T(8,128)(2,1)S(1)} collective-permute-done((bf16[16,64,128]{2,1,0:T(8,128)(2,1)S(1)}, bf16[16,64,128]{2,1,0:T(8,128)(2,1)S(1)}, u32[]{:S(2)}, u32[]{:S(2)}) %collective-permute-start.61) | collective-permute-done | bytes 262176 | tf_op jit(solution)/shard_map/ppermute | solution.py:62
  241.2 1.4 collective-permute-done.59.refs_4_
  242.6 4.6 %collective-permute-done.58.refs_1_ = bf16[16,64,128]{2,1,0:T(8,128)(2,1)S(1)} collective-permute-done((bf16[16,64,128]{2,1,0:T(8,128)(2,1)S(1)}, bf16[16,64,128]{2,1,0:T(8,128)(2,1)S(1)}, u32[]{:S(2)}, u32[]{:S(2)}) %collective-permute-start.58) | collective-permute-done | bytes 262176 | tf_op jit(solution)/shard_map/ppermute | solution.py:62
  248.5 1.3 collective-permute-start.60
  249.8 4.7 %collective-permute-done.63.refs_7_ = bf16[16,64,128]{2,1,0:T(8,128)(2,1)S(1)} collective-permute-done((bf16[16,64,128]{2,1,0:T(8,128)(2,1)S(1)}, bf16[16,64,128]{2,1,0:T(8,128)(2,1)S(1)}, u32[]{:S(2)}, u32[]{:S(2)}) %collective-permute-start.63) | collective-permute-done | bytes 262176 | tf_op jit(solution)/shard_map/ppermute | solution.py:62
  254.6 3.4 %collective-permute-done.60.refs_2_ = bf16[16,64,128]{2,1,0:T(8,128)(2,1)S(1)} collective-permute-done((bf16[16,64,128]{2,1,0:T(8,128)(2,1)S(1)}, bf16[16,64,128]{2,1,0:T(8,128)(2,1)S(1)}, u32[]{:S(2)}, u32[]{:S(2)}) %collective-permute-start.60) | collective-permute-done | bytes 262176 | tf_op jit(solution)/shard_map/ppermute | solution.py:62
  260.0 1.4 merge.1
  261.4 3.4 %collective-permute-done.64.refs_6_ = bf16[16,64,128]{2,1,0:T(8,128)(2,1)S(1)} collective-permute-done((bf16[16,64,128]{2,1,0:T(8,128)(2,1)S(1)}, bf16[16,64,128]{2,1,0:T(8,128)(2,1)S(1)}, u32[]{:S(2)}, u32[]{:S(2)}) %collective-permute-start.64) | collective-permute-done | bytes 262176 | tf_op jit(solution)/shard_map/ppermute | solution.py:62
  267.5 2.3 field.1
  (136 shorter events, 33.9 us)
Async XLA Ops:
  5.1 2.8 %collective-permute-start.1 = (bf16[4,16,64,128]{3,2,1,0:T(8,128)(2,1)S(1)}, bf16[4,16,64,128]{3,2,1,0:T(8,128)(2,1)S(1)}, u32[]{:S(2)}, u32[]{:S(2)}) collective-permute-start(bf16[4,16,64,128]{3,2,1,0:T(8,128)(2,1)S(1)} %get-tuple-element.61), channel_id=1, source_target_pairs={{0,1},{1,0},{2,3},{3,2},{4,5},{5,4},{6,7},{7,6},{8,9},{9,8},{10,11... | collective-permute-start | bytes 3145736 | tf_op jit(solution)/shard_map/ppermute | solution.py:62
  5.6 7.7 %collective-permute-start = (bf16[4,16,64,128]{3,2,1,0:T(8,128)(2,1)S(1)}, bf16[4,16,64,128]{3,2,1,0:T(8,128)(2,1)S(1)}, u32[]{:S(2)}, u32[]{:S(2)}) collective-permute-start(bf16[4,16,64,128]{3,2,1,0:T(8,128)(2,1)S(1)} %get-tuple-element.59), channel_id=1, source_target_pairs={{0,1},{1,0},{2,3},{3,2},{4,5},{5,4},{6,7},{7,6},{8,9},{9,8},{10,11... | collective-permute-start | bytes 3145736 | tf_op jit(solution)/shard_map/ppermute | solution.py:62
  8.2 10.0 %collective-permute-start.2 = (bf16[16,64,128]{2,1,0:T(8,128)(2,1)S(1)}, bf16[16,64,128]{2,1,0:T(8,128)(2,1)S(1)}, u32[]{:S(2)}, u32[]{:S(2)}) collective-permute-start(bf16[16,64,128]{2,1,0:T(8,128)(2,1)S(1)} %get-tuple-element.126), channel_id=1, source_target_pairs={{0,2},{1,3},{2,0},{3,1},{4,6},{5,7},{6,4},{7,5},{8,10},{9,11},{10,... | collective-permute-start | bytes 786440 | tf_op jit(solution)/shard_map/ppermute | solution.py:62
  11.2 9.9 %collective-permute-start.7 = (bf16[16,64,128]{2,1,0:T(8,128)(2,1)S(1)}, bf16[16,64,128]{2,1,0:T(8,128)(2,1)S(1)}, u32[]{:S(2)}, u32[]{:S(2)}) collective-permute-start(bf16[16,64,128]{2,1,0:T(8,128)(2,1)S(1)} %get-tuple-element.127), channel_id=1, source_target_pairs={{0,4},{1,5},{2,6},{3,7},{4,8},{5,9},{6,10},{7,11},{8,12},{9,13},{1... | collective-permute-start | bytes 786440 | tf_op jit(solution)/shard_map/ppermute | solution.py:62
  12.7 11.0 %collective-permute-start.5 = (bf16[16,64,128]{2,1,0:T(8,128)(2,1)S(1)}, bf16[16,64,128]{2,1,0:T(8,128)(2,1)S(1)}, u32[]{:S(2)}, u32[]{:S(2)}) collective-permute-start(bf16[16,64,128]{2,1,0:T(8,128)(2,1)S(1)} %get-tuple-element.128), channel_id=1, source_target_pairs={{0,2},{1,3},{2,0},{3,1},{4,6},{5,7},{6,4},{7,5},{8,10},{9,11},{10,... | collective-permute-start | bytes 786440 | tf_op jit(solution)/shard_map/ppermute | solution.py:62
  18.4 9.2 %collective-permute-start.3 = (bf16[16,64,128]{2,1,0:T(8,128)(2,1)S(1)}, bf16[16,64,128]{2,1,0:T(8,128)(2,1)S(1)}, u32[]{:S(2)}, u32[]{:S(2)}) collective-permute-start(bf16[16,64,128]{2,1,0:T(8,128)(2,1)S(1)} %fusion.10), channel_id=1, source_target_pairs={{0,4},{1,5},{2,6},{3,7},{4,8},{5,9},{6,10},{7,11},{8,12},{9,13},{1... | collective-permute-start | bytes 786440 | tf_op jit(solution)/shard_map/ppermute | solution.py:62
  21.2 10.5 %collective-permute-start.8 = (bf16[16,64,128]{2,1,0:T(8,128)(2,1)S(1)}, bf16[16,64,128]{2,1,0:T(8,128)(2,1)S(1)}, u32[]{:S(2)}, u32[]{:S(2)}) collective-permute-start(bf16[16,64,128]{2,1,0:T(8,128)(2,1)S(1)} %fusion.8), channel_id=1, source_target_pairs={{0,2},{1,3},{2,0},{3,1},{4,6},{5,7},{6,4},{7,5},{8,10},{9,11},{10,... | collective-permute-start | bytes 786440 | tf_op jit(solution)/shard_map/ppermute | solution.py:62
  27.9 10.8 %collective-permute-start.4 = (bf16[16,64,128]{2,1,0:T(8,128)(2,1)S(1)}, bf16[16,64,128]{2,1,0:T(8,128)(2,1)S(1)}, u32[]{:S(2)}, u32[]{:S(2)}) collective-permute-start(bf16[16,64,128]{2,1,0:T(8,128)(2,1)S(1)} %get-tuple-element.124), channel_id=1, source_target_pairs={{0,4},{1,5},{2,6},{3,7},{4,8},{5,9},{6,10},{7,11},{8,12},{9,13},{1... | collective-permute-start | bytes 786440 | tf_op jit(solution)/shard_map/ppermute | solution.py:62
  27.9 11.8 %collective-permute-start.6 = (bf16[16,64,128]{2,1,0:T(8,128)(2,1)S(1)}, bf16[16,64,128]{2,1,0:T(8,128)(2,1)S(1)}, u32[]{:S(2)}, u32[]{:S(2)}) collective-permute-start(bf16[16,64,128]{2,1,0:T(8,128)(2,1)S(1)} %get-tuple-element.125), channel_id=1, source_target_pairs={{0,12},{1,13},{2,14},{3,15},{4,0},{5,1},{6,2},{7,3},{8,4},{9,5},{1... | collective-permute-start | bytes 786440 | tf_op jit(solution)/shard_map/ppermute | solution.py:62
  51.8 2.7 %collective-permute-start.10 = (bf16[4,32,2,16,128]{4,3,2,1,0:T(8,128)(2,1)S(1)}, bf16[4,32,2,16,128]{4,3,2,1,0:T(8,128)(2,1)S(1)}, u32[]{:S(2)}, u32[]{:S(2)}) collective-permute-start(bf16[4,32,2,16,128]{4,3,2,1,0:T(8,128)(2,1)S(1)} %get-tuple-element.66), channel_id=1, source_target_pairs={{0,1},{1,0},{2,3},{3,2},{4,5},{5,4},{6,7},{7,6},{8,9},{9,8},{10,11... | collective-permute-start | bytes 3145736 | tf_op jit(solution)/shard_map/ppermute | solution.py:62
  51.9 5.6 %collective-permute-start.9 = (bf16[4,32,2,16,128]{4,3,2,1,0:T(8,128)(2,1)S(1)}, bf16[4,32,2,16,128]{4,3,2,1,0:T(8,128)(2,1)S(1)}, u32[]{:S(2)}, u32[]{:S(2)}) collective-permute-start(bf16[4,32,2,16,128]{4,3,2,1,0:T(8,128)(2,1)S(1)} %get-tuple-element.64), channel_id=1, source_target_pairs={{0,1},{1,0},{2,3},{3,2},{4,5},{5,4},{6,7},{7,6},{8,9},{9,8},{10,11... | collective-permute-start | bytes 3145736 | tf_op jit(solution)/shard_map/ppermute | solution.py:62
  54.7 9.2 %collective-permute-start.11 = (bf16[32,2,16,128]{3,2,1,0:T(8,128)(2,1)S(1)}, bf16[32,2,16,128]{3,2,1,0:T(8,128)(2,1)S(1)}, u32[]{:S(2)}, u32[]{:S(2)}) collective-permute-start(bf16[32,2,16,128]{3,2,1,0:T(8,128)(2,1)S(1)} %get-tuple-element.121), channel_id=1, source_target_pairs={{0,2},{1,3},{2,0},{3,1},{4,6},{5,7},{6,4},{7,5},{8,10},{9,11},{10,... | collective-permute-start | bytes 786440 | tf_op jit(solution)/shard_map/ppermute | solution.py:62
  56.0 9.9 %collective-permute-start.16 = (bf16[32,2,16,128]{3,2,1,0:T(8,128)(2,1)S(1)}, bf16[32,2,16,128]{3,2,1,0:T(8,128)(2,1)S(1)}, u32[]{:S(2)}, u32[]{:S(2)}) collective-permute-start(bf16[32,2,16,128]{3,2,1,0:T(8,128)(2,1)S(1)} %get-tuple-element.119), channel_id=1, source_target_pairs={{0,4},{1,5},{2,6},{3,7},{4,8},{5,9},{6,10},{7,11},{8,12},{9,13},{1... | collective-permute-start | bytes 786440 | tf_op jit(solution)/shard_map/ppermute | solution.py:62
  56.9 12.6 %collective-permute-start.14 = (bf16[32,2,16,128]{3,2,1,0:T(8,128)(2,1)S(1)}, bf16[32,2,16,128]{3,2,1,0:T(8,128)(2,1)S(1)}, u32[]{:S(2)}, u32[]{:S(2)}) collective-permute-start(bf16[32,2,16,128]{3,2,1,0:T(8,128)(2,1)S(1)} %get-tuple-element.120), channel_id=1, source_target_pairs={{0,2},{1,3},{2,0},{3,1},{4,6},{5,7},{6,4},{7,5},{8,10},{9,11},{10,... | collective-permute-start | bytes 786440 | tf_op jit(solution)/shard_map/ppermute | solution.py:62
  64.1 8.7 %collective-permute-start.12 = (bf16[32,2,16,128]{3,2,1,0:T(8,128)(2,1)S(1)}, bf16[32,2,16,128]{3,2,1,0:T(8,128)(2,1)S(1)}, u32[]{:S(2)}, u32[]{:S(2)}) collective-permute-start(bf16[32,2,16,128]{3,2,1,0:T(8,128)(2,1)S(1)} %fusion.6), channel_id=1, source_target_pairs={{0,4},{1,5},{2,6},{3,7},{4,8},{5,9},{6,10},{7,11},{8,12},{9,13},{1... | collective-permute-start | bytes 786440 | tf_op jit(solution)/shard_map/ppermute | solution.py:62
  66.0 9.1 %collective-permute-start.17 = (bf16[32,2,16,128]{3,2,1,0:T(8,128)(2,1)S(1)}, bf16[32,2,16,128]{3,2,1,0:T(8,128)(2,1)S(1)}, u32[]{:S(2)}, u32[]{:S(2)}) collective-permute-start(bf16[32,2,16,128]{3,2,1,0:T(8,128)(2,1)S(1)} %fusion.4), channel_id=1, source_target_pairs={{0,2},{1,3},{2,0},{3,1},{4,6},{5,7},{6,4},{7,5},{8,10},{9,11},{10,... | collective-permute-start | bytes 786440 | tf_op jit(solution)/shard_map/ppermute | solution.py:62
  73.0 8.7 %collective-permute-start.15 = (bf16[32,2,16,128]{3,2,1,0:T(8,128)(2,1)S(1)}, bf16[32,2,16,128]{3,2,1,0:T(8,128)(2,1)S(1)}, u32[]{:S(2)}, u32[]{:S(2)}) collective-permute-start(bf16[32,2,16,128]{3,2,1,0:T(8,128)(2,1)S(1)} %get-tuple-element.122), channel_id=1, source_target_pairs={{0,12},{1,13},{2,14},{3,15},{4,0},{5,1},{6,2},{7,3},{8,4},{9,5},{1... | collective-permute-start | bytes 786440 | tf_op jit(solution)/shard_map/ppermute | solution.py:62
  73.2 11.2 %collective-permute-start.13 = (bf16[32,2,16,128]{3,2,1,0:T(8,128)(2,1)S(1)}, bf16[32,2,16,128]{3,2,1,0:T(8,128)(2,1)S(1)}, u32[]{:S(2)}, u32[]{:S(2)}) collective-permute-start(bf16[32,2,16,128]{3,2,1,0:T(8,128)(2,1)S(1)} %get-tuple-element.123), channel_id=1, source_target_pairs={{0,4},{1,5},{2,6},{3,7},{4,8},{5,9},{6,10},{7,11},{8,12},{9,13},{1... | collective-permute-start | bytes 786440 | tf_op jit(solution)/shard_map/ppermute | solution.py:62
  86.7 11.1 %collective-permute-start.21 = (bf16[32,2,16,128]{3,2,1,0:T(8,128)(2,1)S(1)}, bf16[32,2,16,128]{3,2,1,0:T(8,128)(2,1)S(1)}, u32[]{:S(2)}, u32[]{:S(2)}) collective-permute-start(bf16[32,2,16,128]{3,2,1,0:T(8,128)(2,1)S(1)} %window.3.refs_0_), channel_id=1, source_target_pairs={{0,4},{1,5},{2,6},{3,7},{4,8},{5,9},{6,10},{7,11},{8,12},{9,13},{1... | collective-permute-start | bytes 786440 | tf_op jit(solution)/shard_map/ppermute | solution.py:62
  87.0 10.8 %collective-permute-start.18 = (bf16[32,2,16,128]{3,2,1,0:T(8,128)(2,1)S(1)}, bf16[32,2,16,128]{3,2,1,0:T(8,128)(2,1)S(1)}, u32[]{:S(2)}, u32[]{:S(2)}) collective-permute-start(bf16[32,2,16,128]{3,2,1,0:T(8,128)(2,1)S(1)} %window.3.refs_0_), channel_id=1, source_target_pairs={{0,2},{1,3},{2,0},{3,1},{4,6},{5,7},{6,4},{7,5},{8,10},{9,11},{10,... | collective-permute-start | bytes 786440 | tf_op jit(solution)/shard_map/ppermute | solution.py:62
  88.4 14.1 %collective-permute-start.19 = (bf16[32,2,16,128]{3,2,1,0:T(8,128)(2,1)S(1)}, bf16[32,2,16,128]{3,2,1,0:T(8,128)(2,1)S(1)}, u32[]{:S(2)}, u32[]{:S(2)}) collective-permute-start(bf16[32,2,16,128]{3,2,1,0:T(8,128)(2,1)S(1)} %window.3.refs_0_), channel_id=1, source_target_pairs={{0,12},{1,13},{2,14},{3,15},{4,0},{5,1},{6,2},{7,3},{8,4},{9,5},{1... | collective-permute-start | bytes 786440 | tf_op jit(solution)/shard_map/ppermute | solution.py:62
  97.8 8.2 %collective-permute-start.22 = (bf16[32,2,16,128]{3,2,1,0:T(8,128)(2,1)S(1)}, bf16[32,2,16,128]{3,2,1,0:T(8,128)(2,1)S(1)}, u32[]{:S(2)}, u32[]{:S(2)}) collective-permute-start(bf16[32,2,16,128]{3,2,1,0:T(8,128)(2,1)S(1)} %collective-permute-done.21.refs_1_), channel_id=1, source_target_pairs={{0,4},{1,5},{2,6},{3,7},{4,8},{5,9},{6,10},{7,11},{8,12},{9,13},{1... | collective-permute-start | bytes 786440 | tf_op jit(solution)/shard_map/ppermute | solution.py:62
  98.8 8.3 %collective-permute-start.26 = (bf16[32,2,16,128]{3,2,1,0:T(8,128)(2,1)S(1)}, bf16[32,2,16,128]{3,2,1,0:T(8,128)(2,1)S(1)}, u32[]{:S(2)}, u32[]{:S(2)}) collective-permute-start(bf16[32,2,16,128]{3,2,1,0:T(8,128)(2,1)S(1)} %window.3.refs_0_), channel_id=1, source_target_pairs={{0,1},{1,0},{2,3},{3,2},{4,5},{5,4},{6,7},{7,6},{8,9},{9,8},{10,11... | collective-permute-start | bytes 786440 | tf_op jit(solution)/shard_map/ppermute | solution.py:62
  98.8 8.3 %collective-permute-start.27 = (bf16[32,2,16,128]{3,2,1,0:T(8,128)(2,1)S(1)}, bf16[32,2,16,128]{3,2,1,0:T(8,128)(2,1)S(1)}, u32[]{:S(2)}, u32[]{:S(2)}) collective-permute-start(bf16[32,2,16,128]{3,2,1,0:T(8,128)(2,1)S(1)} %collective-permute-done.21.refs_1_), channel_id=1, source_target_pairs={{0,1},{1,0},{2,3},{3,2},{4,5},{5,4},{6,7},{7,6},{8,9},{9,8},{10,11... | collective-permute-start | bytes 786440 | tf_op jit(solution)/shard_map/ppermute | solution.py:62
  102.5 5.6 %collective-permute-start.29 = (bf16[32,2,16,128]{3,2,1,0:T(8,128)(2,1)S(1)}, bf16[32,2,16,128]{3,2,1,0:T(8,128)(2,1)S(1)}, u32[]{:S(2)}, u32[]{:S(2)}) collective-permute-start(bf16[32,2,16,128]{3,2,1,0:T(8,128)(2,1)S(1)} %collective-permute-done.19.refs_3_), channel_id=1, source_target_pairs={{0,1},{1,0},{2,3},{3,2},{4,5},{5,4},{6,7},{7,6},{8,9},{9,8},{10,11... | collective-permute-start | bytes 786440 | tf_op jit(solution)/shard_map/ppermute | solution.py:62
  106.0 9.7 %collective-permute-start.24 = (bf16[32,2,16,128]{3,2,1,0:T(8,128)(2,1)S(1)}, bf16[32,2,16,128]{3,2,1,0:T(8,128)(2,1)S(1)}, u32[]{:S(2)}, u32[]{:S(2)}) collective-permute-start(bf16[32,2,16,128]{3,2,1,0:T(8,128)(2,1)S(1)} %collective-permute-done.19.refs_3_), channel_id=1, source_target_pairs={{0,2},{1,3},{2,0},{3,1},{4,6},{5,7},{6,4},{7,5},{8,10},{9,11},{10,... | collective-permute-start | bytes 786440 | tf_op jit(solution)/shard_map/ppermute | solution.py:62
  107.0 10.2 %collective-permute-start.20 = (bf16[32,2,16,128]{3,2,1,0:T(8,128)(2,1)S(1)}, bf16[32,2,16,128]{3,2,1,0:T(8,128)(2,1)S(1)}, u32[]{:S(2)}, u32[]{:S(2)}) collective-permute-start(bf16[32,2,16,128]{3,2,1,0:T(8,128)(2,1)S(1)} %collective-permute-done.18.refs_0_), channel_id=1, source_target_pairs={{0,4},{1,5},{2,6},{3,7},{4,8},{5,9},{6,10},{7,11},{8,12},{9,13},{1... | collective-permute-start | bytes 786440 | tf_op jit(solution)/shard_map/ppermute | solution.py:62
  107.1 13.3 %collective-permute-start.23 = (bf16[32,2,16,128]{3,2,1,0:T(8,128)(2,1)S(1)}, bf16[32,2,16,128]{3,2,1,0:T(8,128)(2,1)S(1)}, u32[]{:S(2)}, u32[]{:S(2)}) collective-permute-start(bf16[32,2,16,128]{3,2,1,0:T(8,128)(2,1)S(1)} %collective-permute-done.22.refs_2_), channel_id=1, source_target_pairs={{0,2},{1,3},{2,0},{3,1},{4,6},{5,7},{6,4},{7,5},{8,10},{9,11},{10,... | collective-permute-start | bytes 786440 | tf_op jit(solution)/shard_map/ppermute | solution.py:62
  108.1 12.2 %collective-permute-start.25 = (bf16[32,2,16,128]{3,2,1,0:T(8,128)(2,1)S(1)}, bf16[32,2,16,128]{3,2,1,0:T(8,128)(2,1)S(1)}, u32[]{:S(2)}, u32[]{:S(2)}) collective-permute-start(bf16[32,2,16,128]{3,2,1,0:T(8,128)(2,1)S(1)} %collective-permute-done.18.refs_0_), channel_id=1, source_target_pairs={{0,1},{1,0},{2,3},{3,2},{4,5},{5,4},{6,7},{7,6},{8,9},{9,8},{10,11... | collective-permute-start | bytes 786440 | tf_op jit(solution)/shard_map/ppermute | solution.py:62
  117.3 3.1 %collective-permute-start.30 = (bf16[32,2,16,128]{3,2,1,0:T(8,128)(2,1)S(1)}, bf16[32,2,16,128]{3,2,1,0:T(8,128)(2,1)S(1)}, u32[]{:S(2)}, u32[]{:S(2)}) collective-permute-start(bf16[32,2,16,128]{3,2,1,0:T(8,128)(2,1)S(1)} %collective-permute-done.20.refs_1_), channel_id=1, source_target_pairs={{0,1},{1,0},{2,3},{3,2},{4,5},{5,4},{6,7},{7,6},{8,9},{9,8},{10,11... | collective-permute-start | bytes 786440 | tf_op jit(solution)/shard_map/ppermute | solution.py:62
  117.3 3.1 %collective-permute-start.32 = (bf16[32,2,16,128]{3,2,1,0:T(8,128)(2,1)S(1)}, bf16[32,2,16,128]{3,2,1,0:T(8,128)(2,1)S(1)}, u32[]{:S(2)}, u32[]{:S(2)}) collective-permute-start(bf16[32,2,16,128]{3,2,1,0:T(8,128)(2,1)S(1)} %collective-permute-done.24.refs_3_), channel_id=1, source_target_pairs={{0,1},{1,0},{2,3},{3,2},{4,5},{5,4},{6,7},{7,6},{8,9},{9,8},{10,11... | collective-permute-start | bytes 786440 | tf_op jit(solution)/shard_map/ppermute | solution.py:62
  143.3 2.7 %collective-permute-start.34 = (bf16[4,32,2,16,128]{4,3,2,1,0:T(8,128)(2,1)S(1)}, bf16[4,32,2,16,128]{4,3,2,1,0:T(8,128)(2,1)S(1)}, u32[]{:S(2)}, u32[]{:S(2)}) collective-permute-start(bf16[4,32,2,16,128]{4,3,2,1,0:T(8,128)(2,1)S(1)} %get-tuple-element.76), channel_id=1, source_target_pairs={{0,1},{1,0},{2,3},{3,2},{4,5},{5,4},{6,7},{7,6},{8,9},{9,8},{10,11... | collective-permute-start | bytes 3145736 | tf_op jit(solution)/shard_map/ppermute | solution.py:62
  143.5 4.8 %collective-permute-start.33 = (bf16[4,32,2,16,128]{4,3,2,1,0:T(8,128)(2,1)S(1)}, bf16[4,32,2,16,128]{4,3,2,1,0:T(8,128)(2,1)S(1)}, u32[]{:S(2)}, u32[]{:S(2)}) collective-permute-start(bf16[4,32,2,16,128]{4,3,2,1,0:T(8,128)(2,1)S(1)} %get-tuple-element.74), channel_id=1, source_target_pairs={{0,1},{1,0},{2,3},{3,2},{4,5},{5,4},{6,7},{7,6},{8,9},{9,8},{10,11... | collective-permute-start | bytes 3145736 | tf_op jit(solution)/shard_map/ppermute | solution.py:62
  146.2 9.2 %collective-permute-start.35 = (bf16[32,2,16,128]{3,2,1,0:T(8,128)(2,1)S(1)}, bf16[32,2,16,128]{3,2,1,0:T(8,128)(2,1)S(1)}, u32[]{:S(2)}, u32[]{:S(2)}) collective-permute-start(bf16[32,2,16,128]{3,2,1,0:T(8,128)(2,1)S(1)} %get-tuple-element.116), channel_id=1, source_target_pairs={{0,2},{1,3},{2,0},{3,1},{4,6},{5,7},{6,4},{7,5},{8,10},{9,11},{10,... | collective-permute-start | bytes 786440 | tf_op jit(solution)/shard_map/ppermute | solution.py:62
  147.3 9.9 %collective-permute-start.40 = (bf16[32,2,16,128]{3,2,1,0:T(8,128)(2,1)S(1)}, bf16[32,2,16,128]{3,2,1,0:T(8,128)(2,1)S(1)}, u32[]{:S(2)}, u32[]{:S(2)}) collective-permute-start(bf16[32,2,16,128]{3,2,1,0:T(8,128)(2,1)S(1)} %get-tuple-element.114), channel_id=1, source_target_pairs={{0,4},{1,5},{2,6},{3,7},{4,8},{5,9},{6,10},{7,11},{8,12},{9,13},{1... | collective-permute-start | bytes 786440 | tf_op jit(solution)/shard_map/ppermute | solution.py:62
  147.3 13.7 %collective-permute-start.38 = (bf16[32,2,16,128]{3,2,1,0:T(8,128)(2,1)S(1)}, bf16[32,2,16,128]{3,2,1,0:T(8,128)(2,1)S(1)}, u32[]{:S(2)}, u32[]{:S(2)}) collective-permute-start(bf16[32,2,16,128]{3,2,1,0:T(8,128)(2,1)S(1)} %get-tuple-element.115), channel_id=1, source_target_pairs={{0,2},{1,3},{2,0},{3,1},{4,6},{5,7},{6,4},{7,5},{8,10},{9,11},{10,... | collective-permute-start | bytes 786440 | tf_op jit(solution)/shard_map/ppermute | solution.py:62
  155.5 8.7 %collective-permute-start.36 = (bf16[32,2,16,128]{3,2,1,0:T(8,128)(2,1)S(1)}, bf16[32,2,16,128]{3,2,1,0:T(8,128)(2,1)S(1)}, u32[]{:S(2)}, u32[]{:S(2)}) collective-permute-start(bf16[32,2,16,128]{3,2,1,0:T(8,128)(2,1)S(1)} %fusion.2), channel_id=1, source_target_pairs={{0,4},{1,5},{2,6},{3,7},{4,8},{5,9},{6,10},{7,11},{8,12},{9,13},{1... | collective-permute-start | bytes 786440 | tf_op jit(solution)/shard_map/ppermute | solution.py:62
  157.3 9.4 %collective-permute-start.41 = (bf16[32,2,16,128]{3,2,1,0:T(8,128)(2,1)S(1)}, bf16[32,2,16,128]{3,2,1,0:T(8,128)(2,1)S(1)}, u32[]{:S(2)}, u32[]{:S(2)}) collective-permute-start(bf16[32,2,16,128]{3,2,1,0:T(8,128)(2,1)S(1)} %fusion), channel_id=1, source_target_pairs={{0,2},{1,3},{2,0},{3,1},{4,6},{5,7},{6,4},{7,5},{8,10},{9,11},{10,... | collective-permute-start | bytes 786440 | tf_op jit(solution)/shard_map/ppermute | solution.py:62
  164.4 11.5 %collective-permute-start.39 = (bf16[32,2,16,128]{3,2,1,0:T(8,128)(2,1)S(1)}, bf16[32,2,16,128]{3,2,1,0:T(8,128)(2,1)S(1)}, u32[]{:S(2)}, u32[]{:S(2)}) collective-permute-start(bf16[32,2,16,128]{3,2,1,0:T(8,128)(2,1)S(1)} %get-tuple-element.117), channel_id=1, source_target_pairs={{0,12},{1,13},{2,14},{3,15},{4,0},{5,1},{6,2},{7,3},{8,4},{9,5},{1... | collective-permute-start | bytes 786440 | tf_op jit(solution)/shard_map/ppermute | solution.py:62
  164.7 11.3 %collective-permute-start.37 = (bf16[32,2,16,128]{3,2,1,0:T(8,128)(2,1)S(1)}, bf16[32,2,16,128]{3,2,1,0:T(8,128)(2,1)S(1)}, u32[]{:S(2)}, u32[]{:S(2)}) collective-permute-start(bf16[32,2,16,128]{3,2,1,0:T(8,128)(2,1)S(1)} %get-tuple-element.118), channel_id=1, source_target_pairs={{0,4},{1,5},{2,6},{3,7},{4,8},{5,9},{6,10},{7,11},{8,12},{9,13},{1... | collective-permute-start | bytes 786440 | tf_op jit(solution)/shard_map/ppermute | solution.py:62
  176.4 7.7 %collective-permute-start.43 = (bf16[16,64,128]{2,1,0:T(8,128)(2,1)S(1)}, bf16[16,64,128]{2,1,0:T(8,128)(2,1)S(1)}, u32[]{:S(2)}, u32[]{:S(2)}) collective-permute-start(bf16[16,64,128]{2,1,0:T(8,128)(2,1)S(1)} %window.5.refs_4_), channel_id=1, source_target_pairs={{0,2},{1,3},{2,0},{3,1},{4,6},{5,7},{6,4},{7,5},{8,10},{9,11},{10,... | collective-permute-start | bytes 786440 | tf_op jit(solution)/shard_map/ppermute | solution.py:62
  177.9 10.4 %collective-permute-start.42 = (bf16[16,64,128]{2,1,0:T(8,128)(2,1)S(1)}, bf16[16,64,128]{2,1,0:T(8,128)(2,1)S(1)}, u32[]{:S(2)}, u32[]{:S(2)}) collective-permute-start(bf16[16,64,128]{2,1,0:T(8,128)(2,1)S(1)} %window.5.refs_4_), channel_id=1, source_target_pairs={{0,4},{1,5},{2,6},{3,7},{4,8},{5,9},{6,10},{7,11},{8,12},{9,13},{1... | collective-permute-start | bytes 786440 | tf_op jit(solution)/shard_map/ppermute | solution.py:62
  177.9 14.4 %collective-permute-start.45 = (bf16[16,64,128]{2,1,0:T(8,128)(2,1)S(1)}, bf16[16,64,128]{2,1,0:T(8,128)(2,1)S(1)}, u32[]{:S(2)}, u32[]{:S(2)}) collective-permute-start(bf16[16,64,128]{2,1,0:T(8,128)(2,1)S(1)} %window.5.refs_4_), channel_id=1, source_target_pairs={{0,12},{1,13},{2,14},{3,15},{4,0},{5,1},{6,2},{7,3},{8,4},{9,5},{1... | collective-permute-start | bytes 786440 | tf_op jit(solution)/shard_map/ppermute | solution.py:62
  188.2 13.0 %collective-permute-start.44 = (bf16[16,64,128]{2,1,0:T(8,128)(2,1)S(1)}, bf16[16,64,128]{2,1,0:T(8,128)(2,1)S(1)}, u32[]{:S(2)}, u32[]{:S(2)}) collective-permute-start(bf16[16,64,128]{2,1,0:T(8,128)(2,1)S(1)} %collective-permute-done.42.refs_4_), channel_id=1, source_target_pairs={{0,4},{1,5},{2,6},{3,7},{4,8},{5,9},{6,10},{7,11},{8,12},{9,13},{1... | collective-permute-start | bytes 786440 | tf_op jit(solution)/shard_map/ppermute | solution.py:62
  192.3 11.4 %collective-permute-start.48 = (bf16[16,64,128]{2,1,0:T(8,128)(2,1)S(1)}, bf16[16,64,128]{2,1,0:T(8,128)(2,1)S(1)}, u32[]{:S(2)}, u32[]{:S(2)}) collective-permute-start(bf16[16,64,128]{2,1,0:T(8,128)(2,1)S(1)} %collective-permute-done.45.refs_4_), channel_id=1, source_target_pairs={{0,2},{1,3},{2,0},{3,1},{4,6},{5,7},{6,4},{7,5},{8,10},{9,11},{10,... | collective-permute-start | bytes 786440 | tf_op jit(solution)/shard_map/ppermute | solution.py:62
  192.8 11.4 %collective-permute-start.47 = (bf16[16,64,128]{2,1,0:T(8,128)(2,1)S(1)}, bf16[16,64,128]{2,1,0:T(8,128)(2,1)S(1)}, u32[]{:S(2)}, u32[]{:S(2)}) collective-permute-start(bf16[16,64,128]{2,1,0:T(8,128)(2,1)S(1)} %collective-permute-done.43.refs_4_), channel_id=1, source_target_pairs={{0,4},{1,5},{2,6},{3,7},{4,8},{5,9},{6,10},{7,11},{8,12},{9,13},{1... | collective-permute-start | bytes 786440 | tf_op jit(solution)/shard_map/ppermute | solution.py:62
  193.4 17.4 %collective-permute-start.50 = (bf16[32,2,16,128]{3,2,1,0:T(8,128)(2,1)S(1)}, bf16[32,2,16,128]{3,2,1,0:T(8,128)(2,1)S(1)}, u32[]{:S(2)}, u32[]{:S(2)}) collective-permute-start(bf16[32,2,16,128]{3,2,1,0:T(8,128)(2,1)S(1)} %get-tuple-element.78.refs_0_), channel_id=1, source_target_pairs={{0,1},{1,0},{2,3},{3,2},{4,5},{5,4},{6,7},{7,6},{8,9},{9,8},{10,11... | collective-permute-start | bytes 786440 | tf_op jit(solution)/shard_map/ppermute | solution.py:62
  200.6 10.2 %collective-permute-start.53 = (bf16[32,2,16,128]{3,2,1,0:T(8,128)(2,1)S(1)}, bf16[32,2,16,128]{3,2,1,0:T(8,128)(2,1)S(1)}, u32[]{:S(2)}, u32[]{:S(2)}) collective-permute-start(bf16[32,2,16,128]{3,2,1,0:T(8,128)(2,1)S(1)} %get-tuple-element.88.refs_3_), channel_id=1, source_target_pairs={{0,1},{1,0},{2,3},{3,2},{4,5},{5,4},{6,7},{7,6},{8,9},{9,8},{10,11... | collective-permute-start | bytes 786440 | tf_op jit(solution)/shard_map/ppermute | solution.py:62
  201.2 9.6 %collective-permute-start.51 = (bf16[32,2,16,128]{3,2,1,0:T(8,128)(2,1)S(1)}, bf16[32,2,16,128]{3,2,1,0:T(8,128)(2,1)S(1)}, u32[]{:S(2)}, u32[]{:S(2)}) collective-permute-start(bf16[32,2,16,128]{3,2,1,0:T(8,128)(2,1)S(1)} %get-tuple-element.85.refs_1_), channel_id=1, source_target_pairs={{0,1},{1,0},{2,3},{3,2},{4,5},{5,4},{6,7},{7,6},{8,9},{9,8},{10,11... | collective-permute-start | bytes 786440 | tf_op jit(solution)/shard_map/ppermute | solution.py:62
  203.7 7.1 %collective-permute-start.52 = (bf16[32,2,16,128]{3,2,1,0:T(8,128)(2,1)S(1)}, bf16[32,2,16,128]{3,2,1,0:T(8,128)(2,1)S(1)}, u32[]{:S(2)}, u32[]{:S(2)}) collective-permute-start(bf16[32,2,16,128]{3,2,1,0:T(8,128)(2,1)S(1)} %get-tuple-element.92.refs_2_), channel_id=1, source_target_pairs={{0,1},{1,0},{2,3},{3,2},{4,5},{5,4},{6,7},{7,6},{8,9},{9,8},{10,11... | collective-permute-start | bytes 786440 | tf_op jit(solution)/shard_map/ppermute | solution.py:62
  204.2 14.2 %collective-permute-start.46 = (bf16[16,64,128]{2,1,0:T(8,128)(2,1)S(1)}, bf16[16,64,128]{2,1,0:T(8,128)(2,1)S(1)}, u32[]{:S(2)}, u32[]{:S(2)}) collective-permute-start(bf16[16,64,128]{2,1,0:T(8,128)(2,1)S(1)} %collective-permute-done.44.refs_4_), channel_id=1, source_target_pairs={{0,2},{1,3},{2,0},{3,1},{4,6},{5,7},{6,4},{7,5},{8,10},{9,11},{10,... | collective-permute-start | bytes 786440 | tf_op jit(solution)/shard_map/ppermute | solution.py:62
  210.7 11.2 %collective-permute-start.49 = (bf16[32,2,16,128]{3,2,1,0:T(8,128)(2,1)S(1)}, bf16[32,2,16,128]{3,2,1,0:T(8,128)(2,1)S(1)}, u32[]{:S(2)}, u32[]{:S(2)}) collective-permute-start(bf16[32,2,16,128]{3,2,1,0:T(8,128)(2,1)S(1)} %get-tuple-element.82.refs_0_), channel_id=1, source_target_pairs={{0,1},{1,0},{2,3},{3,2},{4,5},{5,4},{6,7},{7,6},{8,9},{9,8},{10,11... | collective-permute-start | bytes 786440 | tf_op jit(solution)/shard_map/ppermute | solution.py:62
  231.0 28.5 %collective-permute-start.57 = (bf16[16,32,1024]{2,1,0:T(8,128)(2,1)S(1)}, bf16[16,32,1024]{2,1,0:T(8,128)(2,1)S(1)}, u32[]{:S(2)}, u32[]{:S(2)}) collective-permute-start(bf16[16,32,1024]{2,1,0:T(8,128)(2,1)S(1)} %get-tuple-element.109), channel_id=1, source_target_pairs={{0,1},{1,0},{2,3},{3,2},{4,5},{5,4},{6,7},{7,6},{8,9},{9,8},{10,11... | collective-permute-start | bytes 3145736 | tf_op jit(solution)/shard_map/ppermute | solution.py:62
  231.4 9.8 %collective-permute-start.61 = (bf16[16,64,128]{2,1,0:T(8,128)(2,1)S(1)}, bf16[16,64,128]{2,1,0:T(8,128)(2,1)S(1)}, u32[]{:S(2)}, u32[]{:S(2)}) collective-permute-start(bf16[16,64,128]{2,1,0:T(8,128)(2,1)S(1)} %correlate1.3.refs_0_), channel_id=1, source_target_pairs={{0,12},{1,13},{2,14},{3,15},{4,0},{5,1},{6,2},{7,3},{8,4},{9,5},{1... | collective-permute-start | bytes 786440 | tf_op jit(solution)/shard_map/ppermute | solution.py:62
  234.5 8.1 %collective-permute-start.59 = (bf16[16,64,128]{2,1,0:T(8,128)(2,1)S(1)}, bf16[16,64,128]{2,1,0:T(8,128)(2,1)S(1)}, u32[]{:S(2)}, u32[]{:S(2)}) collective-permute-start(bf16[16,64,128]{2,1,0:T(8,128)(2,1)S(1)} %correlate1.3.refs_0_), channel_id=1, source_target_pairs={{0,2},{1,3},{2,0},{3,1},{4,6},{5,7},{6,4},{7,5},{8,10},{9,11},{10,... | collective-permute-start | bytes 786440 | tf_op jit(solution)/shard_map/ppermute | solution.py:62
  235.0 12.2 %collective-permute-start.58 = (bf16[16,64,128]{2,1,0:T(8,128)(2,1)S(1)}, bf16[16,64,128]{2,1,0:T(8,128)(2,1)S(1)}, u32[]{:S(2)}, u32[]{:S(2)}) collective-permute-start(bf16[16,64,128]{2,1,0:T(8,128)(2,1)S(1)} %correlate1.3.refs_0_), channel_id=1, source_target_pairs={{0,4},{1,5},{2,6},{3,7},{4,8},{5,9},{6,10},{7,11},{8,12},{9,13},{1... | collective-permute-start | bytes 786440 | tf_op jit(solution)/shard_map/ppermute | solution.py:62
  242.6 12.0 %collective-permute-start.62 = (bf16[16,64,128]{2,1,0:T(8,128)(2,1)S(1)}, bf16[16,64,128]{2,1,0:T(8,128)(2,1)S(1)}, u32[]{:S(2)}, u32[]{:S(2)}) collective-permute-start(bf16[16,64,128]{2,1,0:T(8,128)(2,1)S(1)} %collective-permute-done.59.refs_4_), channel_id=1, source_target_pairs={{0,4},{1,5},{2,6},{3,7},{4,8},{5,9},{6,10},{7,11},{8,12},{9,13},{1... | collective-permute-start | bytes 786440 | tf_op jit(solution)/shard_map/ppermute | solution.py:62
  247.2 7.4 %collective-permute-start.63 = (bf16[16,64,128]{2,1,0:T(8,128)(2,1)S(1)}, bf16[16,64,128]{2,1,0:T(8,128)(2,1)S(1)}, u32[]{:S(2)}, u32[]{:S(2)}) collective-permute-start(bf16[16,64,128]{2,1,0:T(8,128)(2,1)S(1)} %collective-permute-done.61.refs_3_), channel_id=1, source_target_pairs={{0,2},{1,3},{2,0},{3,1},{4,6},{5,7},{6,4},{7,5},{8,10},{9,11},{10,... | collective-permute-start | bytes 786440 | tf_op jit(solution)/shard_map/ppermute | solution.py:62
  248.5 9.5 %collective-permute-start.60 = (bf16[16,64,128]{2,1,0:T(8,128)(2,1)S(1)}, bf16[16,64,128]{2,1,0:T(8,128)(2,1)S(1)}, u32[]{:S(2)}, u32[]{:S(2)}) collective-permute-start(bf16[16,64,128]{2,1,0:T(8,128)(2,1)S(1)} %collective-permute-done.58.refs_1_), channel_id=1, source_target_pairs={{0,4},{1,5},{2,6},{3,7},{4,8},{5,9},{6,10},{7,11},{8,12},{9,13},{1... | collective-permute-start | bytes 786440 | tf_op jit(solution)/shard_map/ppermute | solution.py:62
  258.0 6.8 %collective-permute-start.64 = (bf16[16,64,128]{2,1,0:T(8,128)(2,1)S(1)}, bf16[16,64,128]{2,1,0:T(8,128)(2,1)S(1)}, u32[]{:S(2)}, u32[]{:S(2)}) collective-permute-start(bf16[16,64,128]{2,1,0:T(8,128)(2,1)S(1)} %collective-permute-done.60.refs_2_), channel_id=1, source_target_pairs={{0,2},{1,3},{2,0},{3,1},{4,6},{5,7},{6,4},{7,5},{8,10},{9,11},{10,... | collective-permute-start | bytes 786440 | tf_op jit(solution)/shard_map/ppermute | solution.py:62
  259.0 5.9 %collective-permute-start.65 = (bf16[16,64,128]{2,1,0:T(8,128)(2,1)S(1)}, bf16[16,64,128]{2,1,0:T(8,128)(2,1)S(1)}, u32[]{:S(2)}, u32[]{:S(2)}) collective-permute-start(bf16[16,64,128]{2,1,0:T(8,128)(2,1)S(1)} %correlate1.3.refs_0_), channel_id=1, source_target_pairs={{0,1},{1,0},{2,3},{3,2},{4,5},{5,4},{6,7},{7,6},{8,9},{9,8},{10,11... | collective-permute-start | bytes 786440 | tf_op jit(solution)/shard_map/ppermute | solution.py:62
  259.0 6.4 %collective-permute-start.68 = (bf16[16,64,128]{2,1,0:T(8,128)(2,1)S(1)}, bf16[16,64,128]{2,1,0:T(8,128)(2,1)S(1)}, u32[]{:S(2)}, u32[]{:S(2)}) collective-permute-start(bf16[16,64,128]{2,1,0:T(8,128)(2,1)S(1)} %collective-permute-done.61.refs_3_), channel_id=1, source_target_pairs={{0,1},{1,0},{2,3},{3,2},{4,5},{5,4},{6,7},{7,6},{8,9},{9,8},{10,11... | collective-permute-start | bytes 786440 | tf_op jit(solution)/shard_map/ppermute | solution.py:62
  259.5 5.9 %collective-permute-start.69 = (bf16[16,64,128]{2,1,0:T(8,128)(2,1)S(1)}, bf16[16,64,128]{2,1,0:T(8,128)(2,1)S(1)}, u32[]{:S(2)}, u32[]{:S(2)}) collective-permute-start(bf16[16,64,128]{2,1,0:T(8,128)(2,1)S(1)} %collective-permute-done.59.refs_4_), channel_id=1, source_target_pairs={{0,1},{1,0},{2,3},{3,2},{4,5},{5,4},{6,7},{7,6},{8,9},{9,8},{10,11... | collective-permute-start | bytes 786440 | tf_op jit(solution)/shard_map/ppermute | solution.py:62
  259.5 6.4 %collective-permute-start.66 = (bf16[16,64,128]{2,1,0:T(8,128)(2,1)S(1)}, bf16[16,64,128]{2,1,0:T(8,128)(2,1)S(1)}, u32[]{:S(2)}, u32[]{:S(2)}) collective-permute-start(bf16[16,64,128]{2,1,0:T(8,128)(2,1)S(1)} %collective-permute-done.58.refs_1_), channel_id=1, source_target_pairs={{0,1},{1,0},{2,3},{3,2},{4,5},{5,4},{6,7},{7,6},{8,9},{9,8},{10,11... | collective-permute-start | bytes 786440 | tf_op jit(solution)/shard_map/ppermute | solution.py:62
  (17 other events, 119.0 us)

commit v13 on v12

--- a/solution.py
+++ b/solution.py
@@ -574,7 +574,7 @@
         return sent
 
     ahead = pass_on(range(size // 2, 0, -1), 1)
-    behind = pass_on(range(size // 2 + 1, size), size - 1, *ahead[:1])
+    behind = pass_on(range(size // 2 + 1, size), size - 1, *beside)
     parts += ahead[-1:] + behind[-1:]
     across[0] = places.send(add(keep1[0], got1[0], *beside).astype(BF16), places.pair())
     return parts + [across[0]]

time: 270 us -> 282 us (1.044)
  waiting for transfers between devices: 125 us -> 132 us
  starting transfers between devices: 54.8 us -> 59.7 us
    ppermute x73, waiting for transfers between devices: 125 us -> 132 us  [send(): return lax.ppermute(array, self.axis, pairs)]
    ppermute x73, starting transfers between devices: 54.8 us -> 59.7 us  [send(): return lax.ppermute(array, self.axis, pairs)]
  transfers between devices with their start and end apart: 73 -> 73, of which waited for: 41 -> 40; matrix products, arithmetic and copies ran while one was open for 1% -> 1% of each run, Pallas kernels for 13% -> 13%
where the time goes in v13:
time: 282 us
  waiting for transfers between devices  132 us (47%)
  Pallas kernels  83.3 us (30%)
  starting transfers between devices  59.7 us (21%)
  local copies, waits for them, and re-layouts  2.82 us (1%)
    ppermute x73, waiting for transfers between devices, send(): return lax.ppermute(array, self.axis, pairs)  132 us
    ppermute x73, starting transfers between devices, send(): return lax.ppermute(array, self.axis, pairs)  59.7 us
    pallas_call x4, Pallas kernels, correlate(): pl.pallas_call(functools.partial(correlate_kernel, line, flip, bool(more)...  30.3 us
    pallas_call x2, Pallas kernels, convolve(): pl.pallas_call(functools.partial(convolve_kernel, line), in_specs=[VMEM,...  23.4 us
    pallas_call x8, Pallas kernels, window_at(): pl.pallas_call(functools.partial(window_at_kernel, line, flip, step, begu...  19.3 us
  transfers between devices with their start and end apart: 73, of which 40 were waited for; matrix products, arithmetic and copies ran while one was open for 1% of the time, Pallas kernels for 13%

profile of v13, /device:TPU:0, one launch (start us, length us, event | category | flops | bytes accessed | tf_op | source)
XLA Modules:
  0.0 281.8 jit_solution(2307027665674578259)
XLA Ops:
  0.6 1.6 copy-done.2
  3.2 1.9 first_analysis.1
  5.7 2.2 collective-permute-done.1
  8.2 3.0 %collective-permute-start.2 = (bf16[16,64,128]{2,1,0:T(8,128)(2,1)S(1)}, bf16[16,64,128]{2,1,0:T(8,128)(2,1)S(1)}, u32[]{:S(2)}, u32[]{:S(2)}) collective-permute-start(bf16[16,64,128]{2,1,0:T(8,128)(2,1)S(1)} %get-tuple-element.126), channel_id=1, source_target_pairs={{0,2},{1,3},{2,0},{3,1},{4,6},{5,7},{6,4},{7,5},{8,10},{9,11},{10,... | collective-permute-start | bytes 786440 | tf_op jit(solution)/shard_map/ppermute | solution.py:62
  11.2 1.6 collective-permute-start.6
  13.3 5.0 %collective-permute-done.2 = bf16[16,64,128]{2,1,0:T(8,128)(2,1)S(1)} collective-permute-done((bf16[16,64,128]{2,1,0:T(8,128)(2,1)S(1)}, bf16[16,64,128]{2,1,0:T(8,128)(2,1)S(1)}, u32[]{:S(2)}, u32[]{:S(2)}) %collective-permute-start.2) | collective-permute-done | bytes 262176 | tf_op jit(solution)/shard_map/ppermute | solution.py:62
  18.4 2.2 collective-permute-start.3
  22.3 1.5 collective-permute-done.5
  23.8 3.8 %collective-permute-done.3 = bf16[16,64,128]{2,1,0:T(8,128)(2,1)S(1)} collective-permute-done((bf16[16,64,128]{2,1,0:T(8,128)(2,1)S(1)}, bf16[16,64,128]{2,1,0:T(8,128)(2,1)S(1)}, u32[]{:S(2)}, u32[]{:S(2)}) %collective-permute-start.3) | collective-permute-done | bytes 262176 | tf_op jit(solution)/shard_map/ppermute | solution.py:62
  27.9 3.8 %collective-permute-start.7 = (bf16[16,64,128]{2,1,0:T(8,128)(2,1)S(1)}, bf16[16,64,128]{2,1,0:T(8,128)(2,1)S(1)}, u32[]{:S(2)}, u32[]{:S(2)}) collective-permute-start(bf16[16,64,128]{2,1,0:T(8,128)(2,1)S(1)} %get-tuple-element.125), channel_id=1, source_target_pairs={{0,12},{1,13},{2,14},{3,15},{4,0},{5,1},{6,2},{7,3},{8,4},{9,5},{1... | collective-permute-start | bytes 786440 | tf_op jit(solution)/shard_map/ppermute | solution.py:62
  31.7 7.0 %collective-permute-done.4 = bf16[16,64,128]{2,1,0:T(8,128)(2,1)S(1)} collective-permute-done((bf16[16,64,128]{2,1,0:T(8,128)(2,1)S(1)}, bf16[16,64,128]{2,1,0:T(8,128)(2,1)S(1)}, u32[]{:S(2)}, u32[]{:S(2)}) %collective-permute-start.4) | collective-permute-done | bytes 262176 | tf_op jit(solution)/shard_map/ppermute | solution.py:62
  40.1 11.7 %convolve.2 = (bf16[4,32,2,16,128]{4,3,2,1,0:T(8,128)(2,1)S(1)}, bf16[4,32,2,16,128]{4,3,2,1,0:T(8,128)(2,1)S(1)}, bf16[4,32,2,16,128]{4,3,2,1,0:T(8,128)(2,1)S(1)}, bf16[4,32,2,16,128]{4,3,2,1,0:T(8,128)(2,1)S(1)}) custom-call(bf16[32,2,16,128]{3,2,1,0:T(8,128)(2,1)S(1)} %bitcast.87, bf16[2,32,128,2048]{3,2,1,0:T(8,128)(2,1)} %refs_8_.7), custom_call_target="tpu_custom_call" | custom-call | flops 1073741824 | bytes 37748736 | tf_op jit(solution)/shard_map/convolve/pallas_call | solution.py:238
  52.4 2.1 collective-permute-done.10
  55.4 1.5 collective-permute-start.14
  57.4 7.5 %collective-permute-done.15 = bf16[32,2,16,128]{3,2,1,0:T(8,128)(2,1)S(1)} collective-permute-done((bf16[32,2,16,128]{3,2,1,0:T(8,128)(2,1)S(1)}, bf16[32,2,16,128]{3,2,1,0:T(8,128)(2,1)S(1)}, u32[]{:S(2)}, u32[]{:S(2)}) %collective-permute-start.15) | collective-permute-done | bytes 262176 | tf_op jit(solution)/shard_map/ppermute | solution.py:62
  65.0 4.1 %collective-permute-done.11 = bf16[32,2,16,128]{3,2,1,0:T(8,128)(2,1)S(1)} collective-permute-done((bf16[32,2,16,128]{3,2,1,0:T(8,128)(2,1)S(1)}, bf16[32,2,16,128]{3,2,1,0:T(8,128)(2,1)S(1)}, u32[]{:S(2)}, u32[]{:S(2)}) %collective-permute-start.11) | collective-permute-done | bytes 262176 | tf_op jit(solution)/shard_map/ppermute | solution.py:62
  69.3 2.4 collective-permute-start.12
  73.1 1.9 collective-permute-start.16
  74.9 5.6 %collective-permute-done.12 = bf16[32,2,16,128]{3,2,1,0:T(8,128)(2,1)S(1)} collective-permute-done((bf16[32,2,16,128]{3,2,1,0:T(8,128)(2,1)S(1)}, bf16[32,2,16,128]{3,2,1,0:T(8,128)(2,1)S(1)}, u32[]{:S(2)}, u32[]{:S(2)}) %collective-permute-start.12) | collective-permute-done | bytes 262176 | tf_op jit(solution)/shard_map/ppermute | solution.py:62
  81.2 4.9 %collective-permute-done.16.refs_6_ = bf16[32,2,16,128]{3,2,1,0:T(8,128)(2,1)S(1)} collective-permute-done((bf16[32,2,16,128]{3,2,1,0:T(8,128)(2,1)S(1)}, bf16[32,2,16,128]{3,2,1,0:T(8,128)(2,1)S(1)}, u32[]{:S(2)}, u32[]{:S(2)}) %collective-permute-start.16) | collective-permute-done | bytes 262176 | tf_op jit(solution)/shard_map/ppermute | solution.py:62
  86.0 3.6 %collective-permute-done.13.refs_5_ = bf16[32,2,16,128]{3,2,1,0:T(8,128)(2,1)S(1)} collective-permute-done((bf16[32,2,16,128]{3,2,1,0:T(8,128)(2,1)S(1)}, bf16[32,2,16,128]{3,2,1,0:T(8,128)(2,1)S(1)}, u32[]{:S(2)}, u32[]{:S(2)}) %collective-permute-start.13) | collective-permute-done | bytes 262176 | tf_op jit(solution)/shard_map/ppermute | solution.py:62
  89.7 2.2 window.3.refs_0_
  93.7 3.6 %collective-permute-start.19 = (bf16[32,2,16,128]{3,2,1,0:T(8,128)(2,1)S(1)}, bf16[32,2,16,128]{3,2,1,0:T(8,128)(2,1)S(1)}, u32[]{:S(2)}, u32[]{:S(2)}) collective-permute-start(bf16[32,2,16,128]{3,2,1,0:T(8,128)(2,1)S(1)} %window.3.refs_0_), channel_id=1, source_target_pairs={{0,12},{1,13},{2,14},{3,15},{4,0},{5,1},{6,2},{7,3},{8,4},{9,5},{1... | collective-permute-start | bytes 786440 | tf_op jit(solution)/shard_map/ppermute | solution.py:62
  97.3 5.7 %collective-permute-done.21.refs_1_ = bf16[32,2,16,128]{3,2,1,0:T(8,128)(2,1)S(1)} collective-permute-done((bf16[32,2,16,128]{3,2,1,0:T(8,128)(2,1)S(1)}, bf16[32,2,16,128]{3,2,1,0:T(8,128)(2,1)S(1)}, u32[]{:S(2)}, u32[]{:S(2)}) %collective-permute-start.21) | collective-permute-done | bytes 262176 | tf_op jit(solution)/shard_map/ppermute | solution.py:62
  103.6 4.0 %collective-permute-done.19.refs_3_ = bf16[32,2,16,128]{3,2,1,0:T(8,128)(2,1)S(1)} collective-permute-done((bf16[32,2,16,128]{3,2,1,0:T(8,128)(2,1)S(1)}, bf16[32,2,16,128]{3,2,1,0:T(8,128)(2,1)S(1)}, u32[]{:S(2)}, u32[]{:S(2)}) %collective-permute-start.19) | collective-permute-done | bytes 262176 | tf_op jit(solution)/shard_map/ppermute | solution.py:62
  107.6 3.7 %collective-permute-done.22.refs_2_ = bf16[32,2,16,128]{3,2,1,0:T(8,128)(2,1)S(1)} collective-permute-done((bf16[32,2,16,128]{3,2,1,0:T(8,128)(2,1)S(1)}, bf16[32,2,16,128]{3,2,1,0:T(8,128)(2,1)S(1)}, u32[]{:S(2)}, u32[]{:S(2)}) %collective-permute-start.22) | collective-permute-done | bytes 262176 | tf_op jit(solution)/shard_map/ppermute | solution.py:62
  113.4 7.5 %correlate0.2.refs_9_ = f32[32,2,16,128]{3,2,1,0:T(8,128)S(1)} custom-call(bf16[32,2,16,128]{3,2,1,0:T(8,128)(2,1)S(1)} %window.3.refs_0_, bf16[32,2,16,128]{3,2,1,0:T(8,128)(2,1)S(1)} %collective-permute-done.21.refs_1_, bf16[32,2,16,128]{3,2,1,0:T(8,128)(2,1)S(1)} %collective-permute-done.22.refs_2_, ...), custom_call_target="tpu_custom_call" | custom-call | flops 536870912 | bytes 18874368 | tf_op jit(solution)/shard_map/correlate0/pallas_call | solution.py:312
  121.0 2.1 collective-permute-done.20.refs_1_
  123.6 2.1 collective-permute-done.23.refs_2_
  127.2 7.5 %correlate1.2.refs_3_ = f32[32,2,16,128]{3,2,1,0:T(8,128)S(1)} custom-call(bf16[32,2,16,128]{3,2,1,0:T(8,128)(2,1)S(1)} %collective-permute-done.18.refs_0_, bf16[32,2,16,128]{3,2,1,0:T(8,128)(2,1)S(1)} %collective-permute-done.20.refs_1_, bf16[32,2,16,128]{3,2,1,0:T(8,128)(2,1)S(1)} %collective-permute-done.23.refs_2_, ...), custom_call_target="tpu_custom_call" | custom-call | flops 536870912 | bytes 18874368 | tf_op jit(solution)/shard_map/correlate1/pallas_call | solution.py:312
  134.7 2.2 window.4.spec_ref
  136.9 11.7 %convolve.3 = (bf16[4,32,2,16,128]{4,3,2,1,0:T(8,128)(2,1)S(1)}, bf16[4,32,2,16,128]{4,3,2,1,0:T(8,128)(2,1)S(1)}, bf16[4,32,2,16,128]{4,3,2,1,0:T(8,128)(2,1)S(1)}, bf16[4,32,2,16,128]{4,3,2,1,0:T(8,128)(2,1)S(1)}) custom-call(bf16[32,2,16,128]{3,2,1,0:T(8,128)(2,1)S(1)} %window.4.spec_ref, bf16[2,32,128,2048]{3,2,1,0:T(8,128)(2,1)} %refs_8_.7), custom_call_target="tpu_custom_call" | custom-call | flops 1073741824 | bytes 37748736 | tf_op jit(solution)/shard_map/convolve/pallas_call | solution.py:238
  149.2 2.1 collective-permute-done.34
  151.6 1.6 collective-permute-start.38
  153.7 8.0 %collective-permute-done.39 = bf16[32,2,16,128]{3,2,1,0:T(8,128)(2,1)S(1)} collective-permute-done((bf16[32,2,16,128]{3,2,1,0:T(8,128)(2,1)S(1)}, bf16[32,2,16,128]{3,2,1,0:T(8,128)(2,1)S(1)}, u32[]{:S(2)}, u32[]{:S(2)}) %collective-permute-start.39) | collective-permute-done | bytes 262176 | tf_op jit(solution)/shard_map/ppermute | solution.py:62
  161.7 3.9 %collective-permute-done.35 = bf16[32,2,16,128]{3,2,1,0:T(8,128)(2,1)S(1)} collective-permute-done((bf16[32,2,16,128]{3,2,1,0:T(8,128)(2,1)S(1)}, bf16[32,2,16,128]{3,2,1,0:T(8,128)(2,1)S(1)}, u32[]{:S(2)}, u32[]{:S(2)}) %collective-permute-start.35) | collective-permute-done | bytes 262176 | tf_op jit(solution)/shard_map/ppermute | solution.py:62
  166.0 1.6 collective-permute-start.41
  167.6 3.8 %collective-permute-start.40 = (bf16[32,2,16,128]{3,2,1,0:T(8,128)(2,1)S(1)}, bf16[32,2,16,128]{3,2,1,0:T(8,128)(2,1)S(1)}, u32[]{:S(2)}, u32[]{:S(2)}) collective-permute-start(bf16[32,2,16,128]{3,2,1,0:T(8,128)(2,1)S(1)} %get-tuple-element.114), channel_id=1, source_target_pairs={{0,12},{1,13},{2,14},{3,15},{4,0},{5,1},{6,2},{7,3},{8,4},{9,5},{1... | collective-permute-start | bytes 786440 | tf_op jit(solution)/shard_map/ppermute | solution.py:62
  171.4 5.6 %collective-permute-done.36 = bf16[32,2,16,128]{3,2,1,0:T(8,128)(2,1)S(1)} collective-permute-done((bf16[32,2,16,128]{3,2,1,0:T(8,128)(2,1)S(1)}, bf16[32,2,16,128]{3,2,1,0:T(8,128)(2,1)S(1)}, u32[]{:S(2)}, u32[]{:S(2)}) %collective-permute-start.36) | collective-permute-done | bytes 262176 | tf_op jit(solution)/shard_map/ppermute | solution.py:62
  177.2 4.4 %collective-permute-done.40.refs_6_ = bf16[32,2,16,128]{3,2,1,0:T(8,128)(2,1)S(1)} collective-permute-done((bf16[32,2,16,128]{3,2,1,0:T(8,128)(2,1)S(1)}, bf16[32,2,16,128]{3,2,1,0:T(8,128)(2,1)S(1)}, u32[]{:S(2)}, u32[]{:S(2)}) %collective-permute-start.40) | collective-permute-done | bytes 262176 | tf_op jit(solution)/shard_map/ppermute | solution.py:62
  181.7 5.8 %collective-permute-done.37.refs_5_ = bf16[32,2,16,128]{3,2,1,0:T(8,128)(2,1)S(1)} collective-permute-done((bf16[32,2,16,128]{3,2,1,0:T(8,128)(2,1)S(1)}, bf16[32,2,16,128]{3,2,1,0:T(8,128)(2,1)S(1)}, u32[]{:S(2)}, u32[]{:S(2)}) %collective-permute-start.37) | collective-permute-done | bytes 262176 | tf_op jit(solution)/shard_map/ppermute | solution.py:62
  187.9 1.7 collective-permute-start.43
  189.6 3.8 %collective-permute-start.45 = (bf16[16,64,128]{2,1,0:T(8,128)(2,1)S(1)}, bf16[16,64,128]{2,1,0:T(8,128)(2,1)S(1)}, u32[]{:S(2)}, u32[]{:S(2)}) collective-permute-start(bf16[16,64,128]{2,1,0:T(8,128)(2,1)S(1)} %window.5.refs_4_), channel_id=1, source_target_pairs={{0,12},{1,13},{2,14},{3,15},{4,0},{5,1},{6,2},{7,3},{8,4},{9,5},{1... | collective-permute-start | bytes 786440 | tf_op jit(solution)/shard_map/ppermute | solution.py:62
  193.4 2.4 window_at.8
  195.9 3.6 %collective-permute-done.42.refs_4_ = bf16[16,64,128]{2,1,0:T(8,128)(2,1)S(1)} collective-permute-done((bf16[16,64,128]{2,1,0:T(8,128)(2,1)S(1)}, bf16[16,64,128]{2,1,0:T(8,128)(2,1)S(1)}, u32[]{:S(2)}, u32[]{:S(2)}) %collective-permute-start.42) | collective-permute-done | bytes 262176 | tf_op jit(solution)/shard_map/ppermute | solution.py:62
  199.8 1.8 collective-permute-done.45.refs_4_
  201.7 1.5 collective-permute-start.48
  203.2 1.9 collective-permute-start.47
  205.1 2.4 window_at.9
  207.5 2.4 window_at.10
  210.0 2.4 window_at.11
  213.0 2.4 window_at.12
  216.0 2.0 collective-permute-start.46
  218.0 2.4 window_at.13
  220.4 2.4 window_at.14
  222.9 7.5 %correlate0.3.refs_9_ = f32[32,2,16,128]{3,2,1,0:T(8,128)S(1)} custom-call(bf16[32,2,16,128]{3,2,1,0:T(8,128)(2,1)S(1)} %get-tuple-element.78.refs_0_, bf16[32,2,16,128]{3,2,1,0:T(8,128)(2,1)S(1)} %get-tuple-element.85.refs_1_, bf16[32,2,16,128]{3,2,1,0:T(8,128)(2,1)S(1)} %get-tuple-element.92.refs_2_, ...), custom_call_target="tpu_custom_call" | custom-call | flops 536870912 | bytes 18874368 | tf_op jit(solution)/shard_map/correlate0/pallas_call | solution.py:312
  230.5 2.4 window_at.15
  235.4 7.7 %correlate1.3.refs_0_ = bf16[16,64,128]{2,1,0:T(8,128)(2,1)S(1)} custom-call(bf16[32,2,16,128]{3,2,1,0:T(8,128)(2,1)S(1)} %get-tuple-element.82.refs_0_, bf16[32,2,16,128]{3,2,1,0:T(8,128)(2,1)S(1)} %get-tuple-element.106.refs_1_, bf16[32,2,16,128]{3,2,1,0:T(8,128)(2,1)S(1)} %get-tuple-element.107.refs_2_, ...), custom_call_target="tpu_custom_call" | custom-call | flops 536870912 | bytes 18874368 | tf_op jit(solution)/shard_map/correlate1/pallas_call | solution.py:312
  245.5 6.3 %collective-permute-done.61.refs_3_ = bf16[16,64,128]{2,1,0:T(8,128)(2,1)S(1)} collective-permute-done((bf16[16,64,128]{2,1,0:T(8,128)(2,1)S(1)}, bf16[16,64,128]{2,1,0:T(8,128)(2,1)S(1)}, u32[]{:S(2)}, u32[]{:S(2)}) %collective-permute-start.61) | collective-permute-done | bytes 262176 | tf_op jit(solution)/shard_map/ppermute | solution.py:62
  253.6 5.5 %collective-permute-done.58.refs_1_ = bf16[16,64,128]{2,1,0:T(8,128)(2,1)S(1)} collective-permute-done((bf16[16,64,128]{2,1,0:T(8,128)(2,1)S(1)}, bf16[16,64,128]{2,1,0:T(8,128)(2,1)S(1)}, u32[]{:S(2)}, u32[]{:S(2)}) %collective-permute-start.58) | collective-permute-done | bytes 262176 | tf_op jit(solution)/shard_map/ppermute | solution.py:62
  260.2 5.6 %collective-permute-done.63.refs_7_ = bf16[16,64,128]{2,1,0:T(8,128)(2,1)S(1)} collective-permute-done((bf16[16,64,128]{2,1,0:T(8,128)(2,1)S(1)}, bf16[16,64,128]{2,1,0:T(8,128)(2,1)S(1)}, u32[]{:S(2)}, u32[]{:S(2)}) %collective-permute-start.63) | collective-permute-done | bytes 262176 | tf_op jit(solution)/shard_map/ppermute | solution.py:62
  265.9 3.7 %collective-permute-done.60.refs_2_ = bf16[16,64,128]{2,1,0:T(8,128)(2,1)S(1)} collective-permute-done((bf16[16,64,128]{2,1,0:T(8,128)(2,1)S(1)}, bf16[16,64,128]{2,1,0:T(8,128)(2,1)S(1)}, u32[]{:S(2)}, u32[]{:S(2)}) %collective-permute-start.60) | collective-permute-done | bytes 262176 | tf_op jit(solution)/shard_map/ppermute | solution.py:62
  272.6 4.1 %collective-permute-done.64.refs_6_ = bf16[16,64,128]{2,1,0:T(8,128)(2,1)S(1)} collective-permute-done((bf16[16,64,128]{2,1,0:T(8,128)(2,1)S(1)}, bf16[16,64,128]{2,1,0:T(8,128)(2,1)S(1)}, u32[]{:S(2)}, u32[]{:S(2)}) %collective-permute-start.64) | collective-permute-done | bytes 262176 | tf_op jit(solution)/shard_map/ppermute | solution.py:62
  279.4 2.3 field.1
  (136 shorter events, 33.9 us)
Async XLA Ops:
  5.1 2.8 collective-permute-start.1
  5.6 7.7 %collective-permute-start = (bf16[4,16,64,128]{3,2,1,0:T(8,128)(2,1)S(1)}, bf16[4,16,64,128]{3,2,1,0:T(8,128)(2,1)S(1)}, u32[]{:S(2)}, u32[]{:S(2)}) collective-permute-start(bf16[4,16,64,128]{3,2,1,0:T(8,128)(2,1)S(1)} %get-tuple-element.59), channel_id=1, source_target_pairs={{0,1},{1,0},{2,3},{3,2},{4,5},{5,4},{6,7},{7,6},{8,9},{9,8},{10,11... | collective-permute-start | bytes 3145736 | tf_op jit(solution)/shard_map/ppermute | solution.py:62
  8.2 10.0 %collective-permute-start.2 = (bf16[16,64,128]{2,1,0:T(8,128)(2,1)S(1)}, bf16[16,64,128]{2,1,0:T(8,128)(2,1)S(1)}, u32[]{:S(2)}, u32[]{:S(2)}) collective-permute-start(bf16[16,64,128]{2,1,0:T(8,128)(2,1)S(1)} %get-tuple-element.126), channel_id=1, source_target_pairs={{0,2},{1,3},{2,0},{3,1},{4,6},{5,7},{6,4},{7,5},{8,10},{9,11},{10,... | collective-permute-start | bytes 786440 | tf_op jit(solution)/shard_map/ppermute | solution.py:62
  11.2 9.9 %collective-permute-start.6 = (bf16[16,64,128]{2,1,0:T(8,128)(2,1)S(1)}, bf16[16,64,128]{2,1,0:T(8,128)(2,1)S(1)}, u32[]{:S(2)}, u32[]{:S(2)}) collective-permute-start(bf16[16,64,128]{2,1,0:T(8,128)(2,1)S(1)} %get-tuple-element.127), channel_id=1, source_target_pairs={{0,4},{1,5},{2,6},{3,7},{4,8},{5,9},{6,10},{7,11},{8,12},{9,13},{1... | collective-permute-start | bytes 786440 | tf_op jit(solution)/shard_map/ppermute | solution.py:62
  12.7 11.0 %collective-permute-start.5 = (bf16[16,64,128]{2,1,0:T(8,128)(2,1)S(1)}, bf16[16,64,128]{2,1,0:T(8,128)(2,1)S(1)}, u32[]{:S(2)}, u32[]{:S(2)}) collective-permute-start(bf16[16,64,128]{2,1,0:T(8,128)(2,1)S(1)} %get-tuple-element.128), channel_id=1, source_target_pairs={{0,2},{1,3},{2,0},{3,1},{4,6},{5,7},{6,4},{7,5},{8,10},{9,11},{10,... | collective-permute-start | bytes 786440 | tf_op jit(solution)/shard_map/ppermute | solution.py:62
  18.4 9.2 %collective-permute-start.3 = (bf16[16,64,128]{2,1,0:T(8,128)(2,1)S(1)}, bf16[16,64,128]{2,1,0:T(8,128)(2,1)S(1)}, u32[]{:S(2)}, u32[]{:S(2)}) collective-permute-start(bf16[16,64,128]{2,1,0:T(8,128)(2,1)S(1)} %fusion.10), channel_id=1, source_target_pairs={{0,4},{1,5},{2,6},{3,7},{4,8},{5,9},{6,10},{7,11},{8,12},{9,13},{1... | collective-permute-start | bytes 786440 | tf_op jit(solution)/shard_map/ppermute | solution.py:62
  21.2 10.5 %collective-permute-start.8 = (bf16[16,64,128]{2,1,0:T(8,128)(2,1)S(1)}, bf16[16,64,128]{2,1,0:T(8,128)(2,1)S(1)}, u32[]{:S(2)}, u32[]{:S(2)}) collective-permute-start(bf16[16,64,128]{2,1,0:T(8,128)(2,1)S(1)} %fusion.8), channel_id=1, source_target_pairs={{0,2},{1,3},{2,0},{3,1},{4,6},{5,7},{6,4},{7,5},{8,10},{9,11},{10,... | collective-permute-start | bytes 786440 | tf_op jit(solution)/shard_map/ppermute | solution.py:62
  27.9 10.8 %collective-permute-start.4 = (bf16[16,64,128]{2,1,0:T(8,128)(2,1)S(1)}, bf16[16,64,128]{2,1,0:T(8,128)(2,1)S(1)}, u32[]{:S(2)}, u32[]{:S(2)}) collective-permute-start(bf16[16,64,128]{2,1,0:T(8,128)(2,1)S(1)} %get-tuple-element.124), channel_id=1, source_target_pairs={{0,4},{1,5},{2,6},{3,7},{4,8},{5,9},{6,10},{7,11},{8,12},{9,13},{1... | collective-permute-start | bytes 786440 | tf_op jit(solution)/shard_map/ppermute | solution.py:62
  27.9 11.8 %collective-permute-start.7 = (bf16[16,64,128]{2,1,0:T(8,128)(2,1)S(1)}, bf16[16,64,128]{2,1,0:T(8,128)(2,1)S(1)}, u32[]{:S(2)}, u32[]{:S(2)}) collective-permute-start(bf16[16,64,128]{2,1,0:T(8,128)(2,1)S(1)} %get-tuple-element.125), channel_id=1, source_target_pairs={{0,12},{1,13},{2,14},{3,15},{4,0},{5,1},{6,2},{7,3},{8,4},{9,5},{1... | collective-permute-start | bytes 786440 | tf_op jit(solution)/shard_map/ppermute | solution.py:62
  51.8 2.7 collective-permute-start.10
  51.9 13.1 %collective-permute-start.9 = (bf16[4,32,2,16,128]{4,3,2,1,0:T(8,128)(2,1)S(1)}, bf16[4,32,2,16,128]{4,3,2,1,0:T(8,128)(2,1)S(1)}, u32[]{:S(2)}, u32[]{:S(2)}) collective-permute-start(bf16[4,32,2,16,128]{4,3,2,1,0:T(8,128)(2,1)S(1)} %get-tuple-element.64), channel_id=1, source_target_pairs={{0,1},{1,0},{2,3},{3,2},{4,5},{5,4},{6,7},{7,6},{8,9},{9,8},{10,11... | collective-permute-start | bytes 3145736 | tf_op jit(solution)/shard_map/ppermute | solution.py:62
  54.7 10.2 %collective-permute-start.15 = (bf16[32,2,16,128]{3,2,1,0:T(8,128)(2,1)S(1)}, bf16[32,2,16,128]{3,2,1,0:T(8,128)(2,1)S(1)}, u32[]{:S(2)}, u32[]{:S(2)}) collective-permute-start(bf16[32,2,16,128]{3,2,1,0:T(8,128)(2,1)S(1)} %get-tuple-element.121), channel_id=1, source_target_pairs={{0,4},{1,5},{2,6},{3,7},{4,8},{5,9},{6,10},{7,11},{8,12},{9,13},{1... | collective-permute-start | bytes 786440 | tf_op jit(solution)/shard_map/ppermute | solution.py:62
  55.4 9.5 %collective-permute-start.14 = (bf16[32,2,16,128]{3,2,1,0:T(8,128)(2,1)S(1)}, bf16[32,2,16,128]{3,2,1,0:T(8,128)(2,1)S(1)}, u32[]{:S(2)}, u32[]{:S(2)}) collective-permute-start(bf16[32,2,16,128]{3,2,1,0:T(8,128)(2,1)S(1)} %get-tuple-element.122), channel_id=1, source_target_pairs={{0,2},{1,3},{2,0},{3,1},{4,6},{5,7},{6,4},{7,5},{8,10},{9,11},{10,... | collective-permute-start | bytes 786440 | tf_op jit(solution)/shard_map/ppermute | solution.py:62
  56.9 12.2 %collective-permute-start.11 = (bf16[32,2,16,128]{3,2,1,0:T(8,128)(2,1)S(1)}, bf16[32,2,16,128]{3,2,1,0:T(8,128)(2,1)S(1)}, u32[]{:S(2)}, u32[]{:S(2)}) collective-permute-start(bf16[32,2,16,128]{3,2,1,0:T(8,128)(2,1)S(1)} %get-tuple-element.123), channel_id=1, source_target_pairs={{0,2},{1,3},{2,0},{3,1},{4,6},{5,7},{6,4},{7,5},{8,10},{9,11},{10,... | collective-permute-start | bytes 786440 | tf_op jit(solution)/shard_map/ppermute | solution.py:62
  69.3 11.1 %collective-permute-start.12 = (bf16[32,2,16,128]{3,2,1,0:T(8,128)(2,1)S(1)}, bf16[32,2,16,128]{3,2,1,0:T(8,128)(2,1)S(1)}, u32[]{:S(2)}, u32[]{:S(2)}) collective-permute-start(bf16[32,2,16,128]{3,2,1,0:T(8,128)(2,1)S(1)} %get-tuple-element.120), channel_id=1, source_target_pairs={{0,4},{1,5},{2,6},{3,7},{4,8},{5,9},{6,10},{7,11},{8,12},{9,13},{1... | collective-permute-start | bytes 786440 | tf_op jit(solution)/shard_map/ppermute | solution.py:62
  71.8 9.3 %collective-permute-start.17 = (bf16[32,2,16,128]{3,2,1,0:T(8,128)(2,1)S(1)}, bf16[32,2,16,128]{3,2,1,0:T(8,128)(2,1)S(1)}, u32[]{:S(2)}, u32[]{:S(2)}) collective-permute-start(bf16[32,2,16,128]{3,2,1,0:T(8,128)(2,1)S(1)} %fusion.4), channel_id=1, source_target_pairs={{0,2},{1,3},{2,0},{3,1},{4,6},{5,7},{6,4},{7,5},{8,10},{9,11},{10,... | collective-permute-start | bytes 786440 | tf_op jit(solution)/shard_map/ppermute | solution.py:62
  73.1 13.0 %collective-permute-start.16 = (bf16[32,2,16,128]{3,2,1,0:T(8,128)(2,1)S(1)}, bf16[32,2,16,128]{3,2,1,0:T(8,128)(2,1)S(1)}, u32[]{:S(2)}, u32[]{:S(2)}) collective-permute-start(bf16[32,2,16,128]{3,2,1,0:T(8,128)(2,1)S(1)} %get-tuple-element.119), channel_id=1, source_target_pairs={{0,12},{1,13},{2,14},{3,15},{4,0},{5,1},{6,2},{7,3},{8,4},{9,5},{1... | collective-permute-start | bytes 786440 | tf_op jit(solution)/shard_map/ppermute | solution.py:62
  80.6 9.1 %collective-permute-start.13 = (bf16[32,2,16,128]{3,2,1,0:T(8,128)(2,1)S(1)}, bf16[32,2,16,128]{3,2,1,0:T(8,128)(2,1)S(1)}, u32[]{:S(2)}, u32[]{:S(2)}) collective-permute-start(bf16[32,2,16,128]{3,2,1,0:T(8,128)(2,1)S(1)} %fusion.7), channel_id=1, source_target_pairs={{0,4},{1,5},{2,6},{3,7},{4,8},{5,9},{6,10},{7,11},{8,12},{9,13},{1... | collective-permute-start | bytes 786440 | tf_op jit(solution)/shard_map/ppermute | solution.py:62
  91.9 11.1 %collective-permute-start.21 = (bf16[32,2,16,128]{3,2,1,0:T(8,128)(2,1)S(1)}, bf16[32,2,16,128]{3,2,1,0:T(8,128)(2,1)S(1)}, u32[]{:S(2)}, u32[]{:S(2)}) collective-permute-start(bf16[32,2,16,128]{3,2,1,0:T(8,128)(2,1)S(1)} %window.3.refs_0_), channel_id=1, source_target_pairs={{0,4},{1,5},{2,6},{3,7},{4,8},{5,9},{6,10},{7,11},{8,12},{9,13},{1... | collective-permute-start | bytes 786440 | tf_op jit(solution)/shard_map/ppermute | solution.py:62
  92.5 10.6 %collective-permute-start.18 = (bf16[32,2,16,128]{3,2,1,0:T(8,128)(2,1)S(1)}, bf16[32,2,16,128]{3,2,1,0:T(8,128)(2,1)S(1)}, u32[]{:S(2)}, u32[]{:S(2)}) collective-permute-start(bf16[32,2,16,128]{3,2,1,0:T(8,128)(2,1)S(1)} %window.3.refs_0_), channel_id=1, source_target_pairs={{0,2},{1,3},{2,0},{3,1},{4,6},{5,7},{6,4},{7,5},{8,10},{9,11},{10,... | collective-permute-start | bytes 786440 | tf_op jit(solution)/shard_map/ppermute | solution.py:62
  93.7 13.9 %collective-permute-start.19 = (bf16[32,2,16,128]{3,2,1,0:T(8,128)(2,1)S(1)}, bf16[32,2,16,128]{3,2,1,0:T(8,128)(2,1)S(1)}, u32[]{:S(2)}, u32[]{:S(2)}) collective-permute-start(bf16[32,2,16,128]{3,2,1,0:T(8,128)(2,1)S(1)} %window.3.refs_0_), channel_id=1, source_target_pairs={{0,12},{1,13},{2,14},{3,15},{4,0},{5,1},{6,2},{7,3},{8,4},{9,5},{1... | collective-permute-start | bytes 786440 | tf_op jit(solution)/shard_map/ppermute | solution.py:62
  103.0 8.3 %collective-permute-start.22 = (bf16[32,2,16,128]{3,2,1,0:T(8,128)(2,1)S(1)}, bf16[32,2,16,128]{3,2,1,0:T(8,128)(2,1)S(1)}, u32[]{:S(2)}, u32[]{:S(2)}) collective-permute-start(bf16[32,2,16,128]{3,2,1,0:T(8,128)(2,1)S(1)} %collective-permute-done.21.refs_1_), channel_id=1, source_target_pairs={{0,4},{1,5},{2,6},{3,7},{4,8},{5,9},{6,10},{7,11},{8,12},{9,13},{1... | collective-permute-start | bytes 786440 | tf_op jit(solution)/shard_map/ppermute | solution.py:62
  103.0 9.8 %collective-permute-start.26 = (bf16[32,2,16,128]{3,2,1,0:T(8,128)(2,1)S(1)}, bf16[32,2,16,128]{3,2,1,0:T(8,128)(2,1)S(1)}, u32[]{:S(2)}, u32[]{:S(2)}) collective-permute-start(bf16[32,2,16,128]{3,2,1,0:T(8,128)(2,1)S(1)} %window.3.refs_0_), channel_id=1, source_target_pairs={{0,1},{1,0},{2,3},{3,2},{4,5},{5,4},{6,7},{7,6},{8,9},{9,8},{10,11... | collective-permute-start | bytes 786440 | tf_op jit(solution)/shard_map/ppermute | solution.py:62
  103.0 9.8 %collective-permute-start.27 = (bf16[32,2,16,128]{3,2,1,0:T(8,128)(2,1)S(1)}, bf16[32,2,16,128]{3,2,1,0:T(8,128)(2,1)S(1)}, u32[]{:S(2)}, u32[]{:S(2)}) collective-permute-start(bf16[32,2,16,128]{3,2,1,0:T(8,128)(2,1)S(1)} %collective-permute-done.21.refs_1_), channel_id=1, source_target_pairs={{0,1},{1,0},{2,3},{3,2},{4,5},{5,4},{6,7},{7,6},{8,9},{9,8},{10,11... | collective-permute-start | bytes 786440 | tf_op jit(solution)/shard_map/ppermute | solution.py:62
  107.6 5.9 %collective-permute-start.29 = (bf16[32,2,16,128]{3,2,1,0:T(8,128)(2,1)S(1)}, bf16[32,2,16,128]{3,2,1,0:T(8,128)(2,1)S(1)}, u32[]{:S(2)}, u32[]{:S(2)}) collective-permute-start(bf16[32,2,16,128]{3,2,1,0:T(8,128)(2,1)S(1)} %collective-permute-done.19.refs_3_), channel_id=1, source_target_pairs={{0,1},{1,0},{2,3},{3,2},{4,5},{5,4},{6,7},{7,6},{8,9},{9,8},{10,11... | collective-permute-start | bytes 786440 | tf_op jit(solution)/shard_map/ppermute | solution.py:62
  111.3 9.7 %collective-permute-start.24 = (bf16[32,2,16,128]{3,2,1,0:T(8,128)(2,1)S(1)}, bf16[32,2,16,128]{3,2,1,0:T(8,128)(2,1)S(1)}, u32[]{:S(2)}, u32[]{:S(2)}) collective-permute-start(bf16[32,2,16,128]{3,2,1,0:T(8,128)(2,1)S(1)} %collective-permute-done.19.refs_3_), channel_id=1, source_target_pairs={{0,2},{1,3},{2,0},{3,1},{4,6},{5,7},{6,4},{7,5},{8,10},{9,11},{10,... | collective-permute-start | bytes 786440 | tf_op jit(solution)/shard_map/ppermute | solution.py:62
  112.8 10.2 %collective-permute-start.20 = (bf16[32,2,16,128]{3,2,1,0:T(8,128)(2,1)S(1)}, bf16[32,2,16,128]{3,2,1,0:T(8,128)(2,1)S(1)}, u32[]{:S(2)}, u32[]{:S(2)}) collective-permute-start(bf16[32,2,16,128]{3,2,1,0:T(8,128)(2,1)S(1)} %collective-permute-done.18.refs_0_), channel_id=1, source_target_pairs={{0,4},{1,5},{2,6},{3,7},{4,8},{5,9},{6,10},{7,11},{8,12},{9,13},{1... | collective-permute-start | bytes 786440 | tf_op jit(solution)/shard_map/ppermute | solution.py:62
  112.8 12.8 %collective-permute-start.23 = (bf16[32,2,16,128]{3,2,1,0:T(8,128)(2,1)S(1)}, bf16[32,2,16,128]{3,2,1,0:T(8,128)(2,1)S(1)}, u32[]{:S(2)}, u32[]{:S(2)}) collective-permute-start(bf16[32,2,16,128]{3,2,1,0:T(8,128)(2,1)S(1)} %collective-permute-done.22.refs_2_), channel_id=1, source_target_pairs={{0,2},{1,3},{2,0},{3,1},{4,6},{5,7},{6,4},{7,5},{8,10},{9,11},{10,... | collective-permute-start | bytes 786440 | tf_op jit(solution)/shard_map/ppermute | solution.py:62
  113.4 12.2 %collective-permute-start.25 = (bf16[32,2,16,128]{3,2,1,0:T(8,128)(2,1)S(1)}, bf16[32,2,16,128]{3,2,1,0:T(8,128)(2,1)S(1)}, u32[]{:S(2)}, u32[]{:S(2)}) collective-permute-start(bf16[32,2,16,128]{3,2,1,0:T(8,128)(2,1)S(1)} %collective-permute-done.18.refs_0_), channel_id=1, source_target_pairs={{0,1},{1,0},{2,3},{3,2},{4,5},{5,4},{6,7},{7,6},{8,9},{9,8},{10,11... | collective-permute-start | bytes 786440 | tf_op jit(solution)/shard_map/ppermute | solution.py:62
  123.1 2.6 collective-permute-start.30
  123.1 2.6 collective-permute-start.32
  148.6 2.7 collective-permute-start.34
  148.8 12.9 %collective-permute-start.33 = (bf16[4,32,2,16,128]{4,3,2,1,0:T(8,128)(2,1)S(1)}, bf16[4,32,2,16,128]{4,3,2,1,0:T(8,128)(2,1)S(1)}, u32[]{:S(2)}, u32[]{:S(2)}) collective-permute-start(bf16[4,32,2,16,128]{4,3,2,1,0:T(8,128)(2,1)S(1)} %get-tuple-element.74), channel_id=1, source_target_pairs={{0,1},{1,0},{2,3},{3,2},{4,5},{5,4},{6,7},{7,6},{8,9},{9,8},{10,11... | collective-permute-start | bytes 3145736 | tf_op jit(solution)/shard_map/ppermute | solution.py:62
  151.5 10.2 %collective-permute-start.39 = (bf16[32,2,16,128]{3,2,1,0:T(8,128)(2,1)S(1)}, bf16[32,2,16,128]{3,2,1,0:T(8,128)(2,1)S(1)}, u32[]{:S(2)}, u32[]{:S(2)}) collective-permute-start(bf16[32,2,16,128]{3,2,1,0:T(8,128)(2,1)S(1)} %get-tuple-element.116), channel_id=1, source_target_pairs={{0,4},{1,5},{2,6},{3,7},{4,8},{5,9},{6,10},{7,11},{8,12},{9,13},{1... | collective-permute-start | bytes 786440 | tf_op jit(solution)/shard_map/ppermute | solution.py:62
  151.6 10.1 %collective-permute-start.38 = (bf16[32,2,16,128]{3,2,1,0:T(8,128)(2,1)S(1)}, bf16[32,2,16,128]{3,2,1,0:T(8,128)(2,1)S(1)}, u32[]{:S(2)}, u32[]{:S(2)}) collective-permute-start(bf16[32,2,16,128]{3,2,1,0:T(8,128)(2,1)S(1)} %get-tuple-element.117), channel_id=1, source_target_pairs={{0,2},{1,3},{2,0},{3,1},{4,6},{5,7},{6,4},{7,5},{8,10},{9,11},{10,... | collective-permute-start | bytes 786440 | tf_op jit(solution)/shard_map/ppermute | solution.py:62
  153.2 12.4 %collective-permute-start.35 = (bf16[32,2,16,128]{3,2,1,0:T(8,128)(2,1)S(1)}, bf16[32,2,16,128]{3,2,1,0:T(8,128)(2,1)S(1)}, u32[]{:S(2)}, u32[]{:S(2)}) collective-permute-start(bf16[32,2,16,128]{3,2,1,0:T(8,128)(2,1)S(1)} %get-tuple-element.118), channel_id=1, source_target_pairs={{0,2},{1,3},{2,0},{3,1},{4,6},{5,7},{6,4},{7,5},{8,10},{9,11},{10,... | collective-permute-start | bytes 786440 | tf_op jit(solution)/shard_map/ppermute | solution.py:62
  165.8 11.2 %collective-permute-start.36 = (bf16[32,2,16,128]{3,2,1,0:T(8,128)(2,1)S(1)}, bf16[32,2,16,128]{3,2,1,0:T(8,128)(2,1)S(1)}, u32[]{:S(2)}, u32[]{:S(2)}) collective-permute-start(bf16[32,2,16,128]{3,2,1,0:T(8,128)(2,1)S(1)} %get-tuple-element.115), channel_id=1, source_target_pairs={{0,4},{1,5},{2,6},{3,7},{4,8},{5,9},{6,10},{7,11},{8,12},{9,13},{1... | collective-permute-start | bytes 786440 | tf_op jit(solution)/shard_map/ppermute | solution.py:62
  166.0 11.2 %collective-permute-start.41 = (bf16[32,2,16,128]{3,2,1,0:T(8,128)(2,1)S(1)}, bf16[32,2,16,128]{3,2,1,0:T(8,128)(2,1)S(1)}, u32[]{:S(2)}, u32[]{:S(2)}) collective-permute-start(bf16[32,2,16,128]{3,2,1,0:T(8,128)(2,1)S(1)} %fusion), channel_id=1, source_target_pairs={{0,2},{1,3},{2,0},{3,1},{4,6},{5,7},{6,4},{7,5},{8,10},{9,11},{10,... | collective-permute-start | bytes 786440 | tf_op jit(solution)/shard_map/ppermute | solution.py:62
  167.6 14.1 %collective-permute-start.40 = (bf16[32,2,16,128]{3,2,1,0:T(8,128)(2,1)S(1)}, bf16[32,2,16,128]{3,2,1,0:T(8,128)(2,1)S(1)}, u32[]{:S(2)}, u32[]{:S(2)}) collective-permute-start(bf16[32,2,16,128]{3,2,1,0:T(8,128)(2,1)S(1)} %get-tuple-element.114), channel_id=1, source_target_pairs={{0,12},{1,13},{2,14},{3,15},{4,0},{5,1},{6,2},{7,3},{8,4},{9,5},{1... | collective-permute-start | bytes 786440 | tf_op jit(solution)/shard_map/ppermute | solution.py:62
  177.1 10.4 %collective-permute-start.37 = (bf16[32,2,16,128]{3,2,1,0:T(8,128)(2,1)S(1)}, bf16[32,2,16,128]{3,2,1,0:T(8,128)(2,1)S(1)}, u32[]{:S(2)}, u32[]{:S(2)}) collective-permute-start(bf16[32,2,16,128]{3,2,1,0:T(8,128)(2,1)S(1)} %fusion.3), channel_id=1, source_target_pairs={{0,4},{1,5},{2,6},{3,7},{4,8},{5,9},{6,10},{7,11},{8,12},{9,13},{1... | collective-permute-start | bytes 786440 | tf_op jit(solution)/shard_map/ppermute | solution.py:62
  187.9 8.0 %collective-permute-start.43 = (bf16[16,64,128]{2,1,0:T(8,128)(2,1)S(1)}, bf16[16,64,128]{2,1,0:T(8,128)(2,1)S(1)}, u32[]{:S(2)}, u32[]{:S(2)}) collective-permute-start(bf16[16,64,128]{2,1,0:T(8,128)(2,1)S(1)} %window.5.refs_4_), channel_id=1, source_target_pairs={{0,2},{1,3},{2,0},{3,1},{4,6},{5,7},{6,4},{7,5},{8,10},{9,11},{10,... | collective-permute-start | bytes 786440 | tf_op jit(solution)/shard_map/ppermute | solution.py:62
  189.6 9.8 %collective-permute-start.42 = (bf16[16,64,128]{2,1,0:T(8,128)(2,1)S(1)}, bf16[16,64,128]{2,1,0:T(8,128)(2,1)S(1)}, u32[]{:S(2)}, u32[]{:S(2)}) collective-permute-start(bf16[16,64,128]{2,1,0:T(8,128)(2,1)S(1)} %window.5.refs_4_), channel_id=1, source_target_pairs={{0,4},{1,5},{2,6},{3,7},{4,8},{5,9},{6,10},{7,11},{8,12},{9,13},{1... | collective-permute-start | bytes 786440 | tf_op jit(solution)/shard_map/ppermute | solution.py:62
  189.6 12.1 %collective-permute-start.45 = (bf16[16,64,128]{2,1,0:T(8,128)(2,1)S(1)}, bf16[16,64,128]{2,1,0:T(8,128)(2,1)S(1)}, u32[]{:S(2)}, u32[]{:S(2)}) collective-permute-start(bf16[16,64,128]{2,1,0:T(8,128)(2,1)S(1)} %window.5.refs_4_), channel_id=1, source_target_pairs={{0,12},{1,13},{2,14},{3,15},{4,0},{5,1},{6,2},{7,3},{8,4},{9,5},{1... | collective-permute-start | bytes 786440 | tf_op jit(solution)/shard_map/ppermute | solution.py:62
  199.5 13.5 %collective-permute-start.44 = (bf16[16,64,128]{2,1,0:T(8,128)(2,1)S(1)}, bf16[16,64,128]{2,1,0:T(8,128)(2,1)S(1)}, u32[]{:S(2)}, u32[]{:S(2)}) collective-permute-start(bf16[16,64,128]{2,1,0:T(8,128)(2,1)S(1)} %collective-permute-done.42.refs_4_), channel_id=1, source_target_pairs={{0,4},{1,5},{2,6},{3,7},{4,8},{5,9},{6,10},{7,11},{8,12},{9,13},{1... | collective-permute-start | bytes 786440 | tf_op jit(solution)/shard_map/ppermute | solution.py:62
  201.7 13.8 %collective-permute-start.48 = (bf16[16,64,128]{2,1,0:T(8,128)(2,1)S(1)}, bf16[16,64,128]{2,1,0:T(8,128)(2,1)S(1)}, u32[]{:S(2)}, u32[]{:S(2)}) collective-permute-start(bf16[16,64,128]{2,1,0:T(8,128)(2,1)S(1)} %collective-permute-done.45.refs_4_), channel_id=1, source_target_pairs={{0,2},{1,3},{2,0},{3,1},{4,6},{5,7},{6,4},{7,5},{8,10},{9,11},{10,... | collective-permute-start | bytes 786440 | tf_op jit(solution)/shard_map/ppermute | solution.py:62
  203.2 12.7 %collective-permute-start.47 = (bf16[16,64,128]{2,1,0:T(8,128)(2,1)S(1)}, bf16[16,64,128]{2,1,0:T(8,128)(2,1)S(1)}, u32[]{:S(2)}, u32[]{:S(2)}) collective-permute-start(bf16[16,64,128]{2,1,0:T(8,128)(2,1)S(1)} %collective-permute-done.43.refs_4_), channel_id=1, source_target_pairs={{0,4},{1,5},{2,6},{3,7},{4,8},{5,9},{6,10},{7,11},{8,12},{9,13},{1... | collective-permute-start | bytes 786440 | tf_op jit(solution)/shard_map/ppermute | solution.py:62
  205.1 17.7 %collective-permute-start.50 = (bf16[32,2,16,128]{3,2,1,0:T(8,128)(2,1)S(1)}, bf16[32,2,16,128]{3,2,1,0:T(8,128)(2,1)S(1)}, u32[]{:S(2)}, u32[]{:S(2)}) collective-permute-start(bf16[32,2,16,128]{3,2,1,0:T(8,128)(2,1)S(1)} %get-tuple-element.78.refs_0_), channel_id=1, source_target_pairs={{0,1},{1,0},{2,3},{3,2},{4,5},{5,4},{6,7},{7,6},{8,9},{9,8},{10,11... | collective-permute-start | bytes 786440 | tf_op jit(solution)/shard_map/ppermute | solution.py:62
  212.4 10.5 %collective-permute-start.53 = (bf16[32,2,16,128]{3,2,1,0:T(8,128)(2,1)S(1)}, bf16[32,2,16,128]{3,2,1,0:T(8,128)(2,1)S(1)}, u32[]{:S(2)}, u32[]{:S(2)}) collective-permute-start(bf16[32,2,16,128]{3,2,1,0:T(8,128)(2,1)S(1)} %get-tuple-element.88.refs_3_), channel_id=1, source_target_pairs={{0,1},{1,0},{2,3},{3,2},{4,5},{5,4},{6,7},{7,6},{8,9},{9,8},{10,11... | collective-permute-start | bytes 786440 | tf_op jit(solution)/shard_map/ppermute | solution.py:62
  213.0 10.0 %collective-permute-start.51 = (bf16[32,2,16,128]{3,2,1,0:T(8,128)(2,1)S(1)}, bf16[32,2,16,128]{3,2,1,0:T(8,128)(2,1)S(1)}, u32[]{:S(2)}, u32[]{:S(2)}) collective-permute-start(bf16[32,2,16,128]{3,2,1,0:T(8,128)(2,1)S(1)} %get-tuple-element.85.refs_1_), channel_id=1, source_target_pairs={{0,1},{1,0},{2,3},{3,2},{4,5},{5,4},{6,7},{7,6},{8,9},{9,8},{10,11... | collective-permute-start | bytes 786440 | tf_op jit(solution)/shard_map/ppermute | solution.py:62
  215.5 7.5 %collective-permute-start.52 = (bf16[32,2,16,128]{3,2,1,0:T(8,128)(2,1)S(1)}, bf16[32,2,16,128]{3,2,1,0:T(8,128)(2,1)S(1)}, u32[]{:S(2)}, u32[]{:S(2)}) collective-permute-start(bf16[32,2,16,128]{3,2,1,0:T(8,128)(2,1)S(1)} %get-tuple-element.92.refs_2_), channel_id=1, source_target_pairs={{0,1},{1,0},{2,3},{3,2},{4,5},{5,4},{6,7},{7,6},{8,9},{9,8},{10,11... | collective-permute-start | bytes 786440 | tf_op jit(solution)/shard_map/ppermute | solution.py:62
  216.0 14.5 %collective-permute-start.46 = (bf16[16,64,128]{2,1,0:T(8,128)(2,1)S(1)}, bf16[16,64,128]{2,1,0:T(8,128)(2,1)S(1)}, u32[]{:S(2)}, u32[]{:S(2)}) collective-permute-start(bf16[16,64,128]{2,1,0:T(8,128)(2,1)S(1)} %collective-permute-done.44.refs_4_), channel_id=1, source_target_pairs={{0,2},{1,3},{2,0},{3,1},{4,6},{5,7},{6,4},{7,5},{8,10},{9,11},{10,... | collective-permute-start | bytes 786440 | tf_op jit(solution)/shard_map/ppermute | solution.py:62
  222.8 11.2 %collective-permute-start.49 = (bf16[32,2,16,128]{3,2,1,0:T(8,128)(2,1)S(1)}, bf16[32,2,16,128]{3,2,1,0:T(8,128)(2,1)S(1)}, u32[]{:S(2)}, u32[]{:S(2)}) collective-permute-start(bf16[32,2,16,128]{3,2,1,0:T(8,128)(2,1)S(1)} %get-tuple-element.82.refs_0_), channel_id=1, source_target_pairs={{0,1},{1,0},{2,3},{3,2},{4,5},{5,4},{6,7},{7,6},{8,9},{9,8},{10,11... | collective-permute-start | bytes 786440 | tf_op jit(solution)/shard_map/ppermute | solution.py:62
  243.1 27.6 %collective-permute-start.57 = (bf16[16,32,1024]{2,1,0:T(8,128)(2,1)S(1)}, bf16[16,32,1024]{2,1,0:T(8,128)(2,1)S(1)}, u32[]{:S(2)}, u32[]{:S(2)}) collective-permute-start(bf16[16,32,1024]{2,1,0:T(8,128)(2,1)S(1)} %get-tuple-element.109), channel_id=1, source_target_pairs={{0,1},{1,0},{2,3},{3,2},{4,5},{5,4},{6,7},{7,6},{8,9},{9,8},{10,11... | collective-permute-start | bytes 3145736 | tf_op jit(solution)/shard_map/ppermute | solution.py:62
  243.5 8.3 %collective-permute-start.61 = (bf16[16,64,128]{2,1,0:T(8,128)(2,1)S(1)}, bf16[16,64,128]{2,1,0:T(8,128)(2,1)S(1)}, u32[]{:S(2)}, u32[]{:S(2)}) collective-permute-start(bf16[16,64,128]{2,1,0:T(8,128)(2,1)S(1)} %correlate1.3.refs_0_), channel_id=1, source_target_pairs={{0,12},{1,13},{2,14},{3,15},{4,0},{5,1},{6,2},{7,3},{8,4},{9,5},{1... | collective-permute-start | bytes 786440 | tf_op jit(solution)/shard_map/ppermute | solution.py:62
  244.4 8.1 %collective-permute-start.59 = (bf16[16,64,128]{2,1,0:T(8,128)(2,1)S(1)}, bf16[16,64,128]{2,1,0:T(8,128)(2,1)S(1)}, u32[]{:S(2)}, u32[]{:S(2)}) collective-permute-start(bf16[16,64,128]{2,1,0:T(8,128)(2,1)S(1)} %correlate1.3.refs_0_), channel_id=1, source_target_pairs={{0,2},{1,3},{2,0},{3,1},{4,6},{5,7},{6,4},{7,5},{8,10},{9,11},{10,... | collective-permute-start | bytes 786440 | tf_op jit(solution)/shard_map/ppermute | solution.py:62
  245.4 13.7 %collective-permute-start.58 = (bf16[16,64,128]{2,1,0:T(8,128)(2,1)S(1)}, bf16[16,64,128]{2,1,0:T(8,128)(2,1)S(1)}, u32[]{:S(2)}, u32[]{:S(2)}) collective-permute-start(bf16[16,64,128]{2,1,0:T(8,128)(2,1)S(1)} %correlate1.3.refs_0_), channel_id=1, source_target_pairs={{0,4},{1,5},{2,6},{3,7},{4,8},{5,9},{6,10},{7,11},{8,12},{9,13},{1... | collective-permute-start | bytes 786440 | tf_op jit(solution)/shard_map/ppermute | solution.py:62
  252.4 13.4 %collective-permute-start.62 = (bf16[16,64,128]{2,1,0:T(8,128)(2,1)S(1)}, bf16[16,64,128]{2,1,0:T(8,128)(2,1)S(1)}, u32[]{:S(2)}, u32[]{:S(2)}) collective-permute-start(bf16[16,64,128]{2,1,0:T(8,128)(2,1)S(1)} %collective-permute-done.59.refs_4_), channel_id=1, source_target_pairs={{0,4},{1,5},{2,6},{3,7},{4,8},{5,9},{6,10},{7,11},{8,12},{9,13},{1... | collective-permute-start | bytes 786440 | tf_op jit(solution)/shard_map/ppermute | solution.py:62
  259.1 6.7 %collective-permute-start.63 = (bf16[16,64,128]{2,1,0:T(8,128)(2,1)S(1)}, bf16[16,64,128]{2,1,0:T(8,128)(2,1)S(1)}, u32[]{:S(2)}, u32[]{:S(2)}) collective-permute-start(bf16[16,64,128]{2,1,0:T(8,128)(2,1)S(1)} %collective-permute-done.61.refs_3_), channel_id=1, source_target_pairs={{0,2},{1,3},{2,0},{3,1},{4,6},{5,7},{6,4},{7,5},{8,10},{9,11},{10,... | collective-permute-start | bytes 786440 | tf_op jit(solution)/shard_map/ppermute | solution.py:62
  259.7 9.8 %collective-permute-start.60 = (bf16[16,64,128]{2,1,0:T(8,128)(2,1)S(1)}, bf16[16,64,128]{2,1,0:T(8,128)(2,1)S(1)}, u32[]{:S(2)}, u32[]{:S(2)}) collective-permute-start(bf16[16,64,128]{2,1,0:T(8,128)(2,1)S(1)} %collective-permute-done.58.refs_1_), channel_id=1, source_target_pairs={{0,4},{1,5},{2,6},{3,7},{4,8},{5,9},{6,10},{7,11},{8,12},{9,13},{1... | collective-permute-start | bytes 786440 | tf_op jit(solution)/shard_map/ppermute | solution.py:62
  269.6 7.1 %collective-permute-start.64 = (bf16[16,64,128]{2,1,0:T(8,128)(2,1)S(1)}, bf16[16,64,128]{2,1,0:T(8,128)(2,1)S(1)}, u32[]{:S(2)}, u32[]{:S(2)}) collective-permute-start(bf16[16,64,128]{2,1,0:T(8,128)(2,1)S(1)} %collective-permute-done.60.refs_2_), channel_id=1, source_target_pairs={{0,2},{1,3},{2,0},{3,1},{4,6},{5,7},{6,4},{7,5},{8,10},{9,11},{10,... | collective-permute-start | bytes 786440 | tf_op jit(solution)/shard_map/ppermute | solution.py:62
  270.2 6.6 %collective-permute-start.65 = (bf16[16,64,128]{2,1,0:T(8,128)(2,1)S(1)}, bf16[16,64,128]{2,1,0:T(8,128)(2,1)S(1)}, u32[]{:S(2)}, u32[]{:S(2)}) collective-permute-start(bf16[16,64,128]{2,1,0:T(8,128)(2,1)S(1)} %correlate1.3.refs_0_), channel_id=1, source_target_pairs={{0,1},{1,0},{2,3},{3,2},{4,5},{5,4},{6,7},{7,6},{8,9},{9,8},{10,11... | collective-permute-start | bytes 786440 | tf_op jit(solution)/shard_map/ppermute | solution.py:62
  270.2 7.1 %collective-permute-start.68 = (bf16[16,64,128]{2,1,0:T(8,128)(2,1)S(1)}, bf16[16,64,128]{2,1,0:T(8,128)(2,1)S(1)}, u32[]{:S(2)}, u32[]{:S(2)}) collective-permute-start(bf16[16,64,128]{2,1,0:T(8,128)(2,1)S(1)} %collective-permute-done.61.refs_3_), channel_id=1, source_target_pairs={{0,1},{1,0},{2,3},{3,2},{4,5},{5,4},{6,7},{7,6},{8,9},{9,8},{10,11... | collective-permute-start | bytes 786440 | tf_op jit(solution)/shard_map/ppermute | solution.py:62
  270.7 6.6 %collective-permute-start.69 = (bf16[16,64,128]{2,1,0:T(8,128)(2,1)S(1)}, bf16[16,64,128]{2,1,0:T(8,128)(2,1)S(1)}, u32[]{:S(2)}, u32[]{:S(2)}) collective-permute-start(bf16[16,64,128]{2,1,0:T(8,128)(2,1)S(1)} %collective-permute-done.59.refs_4_), channel_id=1, source_target_pairs={{0,1},{1,0},{2,3},{3,2},{4,5},{5,4},{6,7},{7,6},{8,9},{9,8},{10,11... | collective-permute-start | bytes 786440 | tf_op jit(solution)/shard_map/ppermute | solution.py:62
  270.7 7.1 %collective-permute-start.66 = (bf16[16,64,128]{2,1,0:T(8,128)(2,1)S(1)}, bf16[16,64,128]{2,1,0:T(8,128)(2,1)S(1)}, u32[]{:S(2)}, u32[]{:S(2)}) collective-permute-start(bf16[16,64,128]{2,1,0:T(8,128)(2,1)S(1)} %collective-permute-done.58.refs_1_), channel_id=1, source_target_pairs={{0,1},{1,0},{2,3},{3,2},{4,5},{5,4},{6,7},{7,6},{8,9},{9,8},{10,11... | collective-permute-start | bytes 786440 | tf_op jit(solution)/shard_map/ppermute | solution.py:62
  (17 other events, 123.4 us)
